TPU v7x, 32 devices: a whole 2x2x4 slice. The times are simulated.
32 devices in a mesh: event: 2 (over x), pack: 4 (over z), tensor: 4 (over y, core).
Axes of the slice: x: 2, y: 2, z: 4, core: 2. Of those that a mesh axis runs over, the one named last changes fastest.
Arguments:
- features: bfloat16 [4096, 1024], P(('event', 'pack', 'tensor')), may hold values from -6 to 6
- dest_owner: int32 [4096], P(('event', 'pack', 'tensor')), may hold values from 0 to 7, as said below
- dest_slot: int32 [4096], P(('event', 'pack', 'tensor')), may hold values from 0 to 127, as said below
- doc_ids: int32 [8, 512], P(('event', 'pack')), may hold values from 0 to 7, never falling along the last dimension, each value on 1 to 128 neighbouring positions
- enc_weight: bfloat16 [2, 1024, 1024], replicated, may hold values from -0.1875 to 0.1875
- attn_in: bfloat16 [4, 1024, 1024], P(None, None, 'tensor'), may hold values from -0.1875 to 0.1875
- attn_out: bfloat16 [1024, 1024], P('tensor'), may hold values from -0.1875 to 0.1875
- ffn_in: bfloat16 [2, 1024, 2048], P(None, None, 'tensor'), may hold values from -0.1875 to 0.1875
- ffn_out: bfloat16 [2048, 1024], P('tensor'), may hold values from -0.125 to 0.125
- out_grad: bfloat16 [8, 512, 1024], P(('event', 'pack'), 'tensor'), may hold values from -6 to 6
Outputs:
- packed_out: bfloat16 [8, 512, 1024], P(('event', 'pack'), 'tensor')
- row_grad: bfloat16 [4096, 1024], P(('event', 'pack', 'tensor'))
- enc_grad: float32 [2, 1024, 1024], P(None, ('event', 'pack'), 'tensor')
Inputs may be any that keep to these rules, and one draw needn't show every extreme that they name: `dest_owner`: the sequence of each event, numbered over event and pack with event slowest. From the devices of one tensor index every sequence receives exactly 128 events; from one device at most 24 events go to one sequence, every device sends exactly 24 to some sequence, and every sequence receives exactly 24 from some device. `dest_slot`: events of one tensor index that go to one sequence have distinct slots, so they fill that sequence's positions tix * 128 to tix * 128 + 127. `doc_ids`: document numbers never fall along a sequence; a document holds 1 to 128 positions.
All inputs are finite; a program needn't handle non-finite values.
Results may differ from a plain program's by a relative error of at most 0.023.
Values may be sent and summed in bfloat16 or wider, within the bound.
No kernel may reach another device: no remote copies, remote signals or barrier semaphores. Data moves between devices by JAX's collectives and lax.ppermute only.
A program may use at most 128 MiB of HBM per device.

v0:
```python
import jax
import jax.numpy as jnp
from jax import lax
from jax.sharding import PartitionSpec as P

D = 1024
HEADS = 16


EPS = 1e-06
BLOCK = 256


def silu_grad(value):
    sigma = jax.nn.sigmoid(value)
    return sigma * (1.0 + value * (1.0 - sigma))


def norm_rows(rows):
    wide = rows.astype(jnp.float32)
    factor = lax.rsqrt(jnp.mean(wide * wide, axis=-1, keepdims=True) + EPS)
    return (wide * factor, factor)


def norm_back(grad, normed, factor):
    return factor * (grad - normed * jnp.mean(grad * normed, axis=-1, keepdims=True))


def rounded(value):
    return lax.optimization_barrier(value.astype(jnp.bfloat16)).astype(jnp.float32)


def doc_counts(documents):
    length = documents.shape[0]
    places = jnp.arange(length, dtype=jnp.int32)
    change = jnp.concatenate([jnp.ones((1,), bool), documents[1:] != documents[:-1]])
    first = lax.cummax(jnp.where(change, places, 0), axis=0)
    return (places - first + 1).astype(jnp.float32)


def bucket_index(dest_owner, groups, capacity):
    onehot = (dest_owner[:, None] == jnp.arange(groups, dtype=jnp.int32)[None, :]).astype(jnp.int32)
    before = jnp.cumsum(onehot, axis=0) - onehot
    rank = jnp.sum(before * onehot, axis=1)
    return dest_owner * capacity + rank


def tile_mask(documents, q_start, k_start, q_len, k_len):
    q_docs = documents[q_start : q_start + q_len]
    k_docs = documents[k_start : k_start + k_len]
    q_place = q_start + jnp.arange(q_len, dtype=jnp.int32)
    k_place = k_start + jnp.arange(k_len, dtype=jnp.int32)
    return (q_docs[:, None] == k_docs[None, :]) & (k_place[None, :] <= q_place[:, None])


def tile_forward(query, keys, values, allowed):
    scores = jnp.einsum(
        "hqd,hkd->hqk", query, keys, preferred_element_type=jnp.float32
    ) * query.shape[-1] ** (-0.5)
    weights = jnp.where(allowed[None], jax.nn.silu(scores), 0.0).astype(jnp.bfloat16)
    return jnp.einsum("hqk,hkd->hqd", weights, values, preferred_element_type=jnp.float32)


def tile_backward(query, keys, values, d_attended, allowed):
    head_scale = query.shape[-1] ** (-0.5)
    scores = (
        jnp.einsum("hqd,hkd->hqk", query, keys, preferred_element_type=jnp.float32) * head_scale
    )
    weights = jnp.where(allowed[None], jax.nn.silu(scores), 0.0).astype(jnp.bfloat16)
    d_weights = jnp.einsum("hqd,hkd->hqk", d_attended, values, preferred_element_type=jnp.float32)
    d_scores = jnp.where(allowed[None], d_weights * silu_grad(scores), 0.0).astype(jnp.bfloat16)
    d_query = (
        jnp.einsum("hqk,hkd->hqd", d_scores, keys, preferred_element_type=jnp.float32) * head_scale
    )
    d_keys = (
        jnp.einsum("hqk,hqd->hkd", d_scores, query, preferred_element_type=jnp.float32) * head_scale
    )
    d_values = jnp.einsum("hqk,hqd->hkd", weights, d_attended, preferred_element_type=jnp.float32)
    return (d_query, d_keys, d_values)


def attend(query, keys, values, documents):
    length = query.shape[1]
    block = min(BLOCK, length)
    outputs = []
    for q_index in range(length // block):
        q_start = q_index * block
        query_block = query[:, q_start : q_start + block]
        limit = q_start + block
        allowed = tile_mask(documents, q_start, 0, block, limit)
        outputs.append(tile_forward(query_block, keys[:, :limit], values[:, :limit], allowed))
    return jnp.concatenate(outputs, axis=1)


def attend_back(query, keys, values, d_attended, documents):
    length = query.shape[1]
    block = min(BLOCK, length)
    d_query_parts = []
    d_keys = jnp.zeros(keys.shape, jnp.float32)
    d_values = jnp.zeros(values.shape, jnp.float32)
    for q_index in range(length // block):
        q_start = q_index * block
        query_block = query[:, q_start : q_start + block]
        d_att_block = d_attended[:, q_start : q_start + block]
        limit = q_start + block
        allowed = tile_mask(documents, q_start, 0, block, limit)
        part_q, part_k, part_v = tile_backward(
            query_block, keys[:, :limit], values[:, :limit], d_att_block, allowed
        )
        d_query_parts.append(part_q)
        d_keys = d_keys.at[:, :limit].add(part_k)
        d_values = d_values.at[:, :limit].add(part_v)
    return (jnp.concatenate(d_query_parts, axis=1), d_keys, d_values)


def shards(
    features,
    dest_owner,
    dest_slot,
    doc_ids,
    enc_weight,
    attn_in,
    attn_out,
    ffn_in,
    ffn_out,
    out_grad,
):
    layers = enc_weight.shape[0]
    activations = [features]
    layer = 0
    preact = jnp.dot(activations[-1], enc_weight[layer], preferred_element_type=jnp.float32)
    pre_acts = [preact]
    activations.append(jax.nn.silu(preact).astype(jnp.bfloat16))
    encoded = jnp.dot(
        activations[-1], enc_weight[layers - 1], preferred_element_type=jnp.float32
    ).astype(jnp.bfloat16)
    rows_dev, width = features.shape
    groups = lax.axis_size(("event", "pack"))
    mean_load = rows_dev // groups
    capacity = mean_load + mean_load // 2
    place = bucket_index(dest_owner, groups, capacity)
    send_rows = (
        jnp.zeros((groups * capacity, width), jnp.bfloat16)
        .at[place]
        .set(encoded)
        .reshape(groups, capacity, width)
    )
    send_slots = (
        jnp.full((groups * capacity,), rows_dev, jnp.int32)
        .at[place]
        .set(dest_slot)
        .reshape(groups, capacity)
    )
    got_rows, got_slots = (
        lax.all_to_all(send_rows, ("event", "pack"), split_axis=0, concat_axis=0, tiled=True),
        lax.all_to_all(send_slots, ("event", "pack"), split_axis=0, concat_axis=0, tiled=True),
    )
    got_rows = got_rows.reshape(groups * capacity, width)
    got_slots = got_slots.reshape(groups * capacity)
    quarter = jnp.zeros((rows_dev, width), jnp.bfloat16).at[got_slots].set(got_rows, mode="drop")
    documents = doc_ids[0]
    root = jnp.sqrt(doc_counts(documents))[:, None]
    normed_f, factor1 = norm_rows(quarter)
    normed = normed_f.astype(jnp.bfloat16)
    projected = jnp.einsum(
        "rd,kdc->krc",
        lax.all_gather(normed, "tensor", axis=0, tiled=True),
        attn_in,
        preferred_element_type=jnp.float32,
    ).astype(jnp.bfloat16)
    length = projected.shape[1]
    local_cols = projected.shape[2]
    head_dim = D // HEADS
    local_heads = local_cols // head_dim

    def split_heads(value):
        return value.reshape(length, local_heads, head_dim).transpose(1, 0, 2)

    def join_heads(value):
        return value.transpose(1, 0, 2).reshape(length, local_cols)

    query = split_heads(projected[0])
    keys = split_heads(projected[1])
    values = split_heads(projected[2])
    gate_raw = projected[3].astype(jnp.float32)
    attended = join_heads(attend(query, keys, values, documents)) / root
    gated = (attended * jax.nn.silu(gate_raw)).astype(jnp.bfloat16)
    attn_sum = lax.psum_scatter(
        rounded(jnp.dot(gated, attn_out, preferred_element_type=jnp.float32)).astype(jnp.bfloat16),
        "tensor",
        scatter_dimension=0,
        tiled=True,
    ).astype(jnp.float32)
    resid = (quarter.astype(jnp.float32) + attn_sum).astype(jnp.bfloat16)
    normed2_f, factor2 = norm_rows(resid)
    normed2 = normed2_f.astype(jnp.bfloat16)
    gate_up = jnp.einsum(
        "rd,kdf->krf",
        lax.all_gather(normed2, "tensor", axis=0, tiled=True),
        ffn_in,
        preferred_element_type=jnp.float32,
    )
    gate = gate_up[0]
    upper = gate_up[1]
    hidden = (jax.nn.silu(gate) * upper).astype(jnp.bfloat16)
    ffn_sum = lax.psum_scatter(
        rounded(jnp.dot(hidden, ffn_out, preferred_element_type=jnp.float32)).astype(jnp.bfloat16),
        "tensor",
        scatter_dimension=0,
        tiled=True,
    ).astype(jnp.float32)
    packed_out = (resid.astype(jnp.float32) + ffn_sum).astype(jnp.bfloat16)
    d_out = out_grad[0]
    d_hidden = lax.dot_general(
        lax.all_gather(d_out, "tensor", axis=0, tiled=True),
        ffn_out,
        (((1,), (1,)), ((), ())),
        preferred_element_type=jnp.float32,
    )
    d_gate = (d_hidden * upper * silu_grad(gate)).astype(jnp.bfloat16)
    d_upper = (d_hidden * jax.nn.silu(gate)).astype(jnp.bfloat16)
    d_both = jnp.stack([d_gate, d_upper])
    piece = d_both
    d_normed2 = lax.psum_scatter(
        rounded(
            jnp.einsum("krf,kdf->rd", piece, ffn_in, preferred_element_type=jnp.float32)
        ).astype(jnp.bfloat16),
        "tensor",
        scatter_dimension=0,
        tiled=True,
    ).astype(jnp.float32)
    d_resid = (d_out.astype(jnp.float32) + norm_back(d_normed2, normed2_f, factor2)).astype(
        jnp.bfloat16
    )
    d_gated = lax.dot_general(
        lax.all_gather(d_resid, "tensor", axis=0, tiled=True),
        attn_out,
        (((1,), (1,)), ((), ())),
        preferred_element_type=jnp.float32,
    )
    d_attended = (d_gated * jax.nn.silu(gate_raw) / root).astype(jnp.bfloat16)
    d_gate_proj = (d_gated * attended * silu_grad(gate_raw)).astype(jnp.bfloat16)
    d_query, d_keys, d_values = attend_back(query, keys, values, split_heads(d_attended), documents)
    d_projected = jnp.stack(
        [
            join_heads(d_query).astype(jnp.bfloat16),
            join_heads(d_keys).astype(jnp.bfloat16),
            join_heads(d_values).astype(jnp.bfloat16),
            d_gate_proj,
        ]
    )
    piece = d_projected
    d_normed = lax.psum_scatter(
        rounded(
            jnp.einsum("krc,kdc->rd", piece, attn_in, preferred_element_type=jnp.float32)
        ).astype(jnp.bfloat16),
        "tensor",
        scatter_dimension=0,
        tiled=True,
    ).astype(jnp.float32)
    d_quarter = (d_resid.astype(jnp.float32) + norm_back(d_normed, normed_f, factor1)).astype(
        jnp.bfloat16
    )
    padded = jnp.concatenate([d_quarter, jnp.zeros((1, width), jnp.bfloat16)], axis=0)
    back_rows = padded[got_slots].reshape(groups, capacity, width)
    returned = lax.all_to_all(back_rows, ("event", "pack"), split_axis=0, concat_axis=0, tiled=True)
    row_grad = returned.reshape(groups * capacity, width)[place]
    tensor_count = lax.axis_size("tensor")
    cotangent = row_grad
    grads = []
    for layer in reversed(range(layers)):
        activation = activations[layer]

        def column_term(start, count, activation=activation, cotangent=cotangent):
            return lax.dot_general(
                cotangent, activation, (((0,), (0,)), ((), ())), preferred_element_type=jnp.float32
            )

        partial_cols = lax.psum_scatter(
            column_term(jnp.int32(0), width // tensor_count * lax.axis_size("tensor")).astype(
                jnp.bfloat16
            ),
            "tensor",
            scatter_dimension=0,
            tiled=True,
        ).astype(jnp.float32)
        grads.append(
            lax.psum_scatter(partial_cols, ("event", "pack"), scatter_dimension=1, tiled=True).T
        )
        if layer > 0:
            back = lax.dot_general(
                cotangent,
                enc_weight[layer],
                (((1,), (1,)), ((), ())),
                preferred_element_type=jnp.float32,
            )
            cotangent = (back * silu_grad(pre_acts[layer - 1])).astype(jnp.bfloat16)
    enc_grad = jnp.stack(grads[::-1])
    return (packed_out[None], row_grad, enc_grad)


def solution(mesh):
    placed = (
        P(("event", "pack", "tensor"), None),
        P(("event", "pack", "tensor")),
        P(("event", "pack", "tensor")),
        P(("event", "pack"), None),
        P(),
        P(None, None, "tensor"),
        P("tensor", None),
        P(None, None, "tensor"),
        P("tensor", None),
        P(("event", "pack"), "tensor", None),
    )
    return jax.shard_map(
        shards,
        mesh=mesh,
        in_specs=placed,
        out_specs=(
            P(("event", "pack"), "tensor", None),
            P(("event", "pack", "tensor"), None),
            P(None, ("event", "pack"), "tensor"),
        ),
        check_vma=False,
    )
```

profile of v0, /device:TPU:0, one launch (start us, length us, event | category | flops | bytes accessed | tf_op | source)
XLA Modules:
  0.0 478.6 jit_solution(1907653709870565814)
XLA Ops:
  7.2 0.9 fusion.99
  8.2 0.8 select_reduce_fusion
  9.1 0.7 compare_select_fusion.2
  9.7 1.1 scatter_custom_fusion
  10.9 0.7 all_to_all.12
  11.5 7.3 %all-to-all-start = ((s32[8,1,24]{2,1,0:T(1,128)}), s32[8,1,24]{2,1,0:T(1,128)S(1)}, u32[]{:S(2)}, u32[]{:S(2)}) async-start(s32[8,1,24]{2,1,0:T(1,128)} %all_to_all.12), calls=%async_computation | async-start | bytes 8192 | tf_op jit(solution)/shard_map/all_to_all | solution.py:156
  18.8 2.1 fusion.4
  20.9 0.8 copy-done.22
  21.8 2.1 fusion.18
  23.8 1.9 scatter_custom_fusion.1
  25.7 6.0 %all-to-all-start.1 = ((bf16[8,24,1024]{2,1,0:T(8,128)(2,1)}), bf16[8,24,1024]{2,1,0:T(8,128)(2,1)S(1)}, u32[]{:S(2)}, u32[]{:S(2)}) async-start(bf16[8,24,1024]{2,1,0:T(8,128)(2,1)} %bitcast.3), calls=%async_computation.1 | async-start | bytes 786432 | tf_op jit(solution)/shard_map/all_to_all | solution.py:155
  31.8 0.5 broadcast.346
  32.3 0.7 reduce.15
  33.0 10.7 %all-to-all-done.1 = bf16[8,24,1024]{2,1,0:T(8,128)(2,1)S(1)} async-done(((bf16[8,24,1024]{2,1,0:T(8,128)(2,1)}), bf16[8,24,1024]{2,1,0:T(8,128)(2,1)S(1)}, u32[]{:S(2)}, u32[]{:S(2)}) %all-to-all-start.1) | async-done | bytes 393248 | tf_op jit(solution)/shard_map/all_to_all | solution.py:155
  43.7 1.5 scatter_custom_fusion.2
  45.3 0.8 fusion.45
  47.3 13.0 %all-gather.6.cloned.1.call-done = bf16[512,1024]{1,0:T(8,128)(2,1)} async-done(((bf16[128,1024]{1,0:T(8,128)(2,1)}), bf16[512,1024]{1,0:T(8,128)(2,1)}) %all-gather.6.cloned.1.call-update) | async-done | bytes 1048592 | tf_op jit(solution)/shard_map/all_gather | solution.py:167
  60.4 3.2 fusion.9
  63.7 1.5 select_convert_fusion.2
  65.3 2.2 select_convert_fusion.1
  68.3 0.8 copy-done.12
  69.1 1.5 convolution_convert_fusion.2
  70.6 25.0 %reduce-scatter.9.cloned.1.call-done = bf16[128,1024]{1,0:T(8,128)(2,1)} async-done(((bf16[512,1024]{1,0:T(8,128)(2,1)}), bf16[128,1024]{1,0:T(8,128)(2,1)}) %reduce-scatter.9.cloned.1.call-update) | async-done | bytes 262160 | tf_op jit(solution)/shard_map/reduce_scatter | solution.py:188
  95.6 1.1 fusion.59
  96.8 0.7 copy-done.1
  97.4 0.8 fusion.48
  98.3 0.5 all-gather.12.cloned.1.call-update
  98.9 16.3 %all-gather.8.cloned.1.call-done = bf16[512,1024]{1,0:T(8,128)(2,1)} async-done(((bf16[128,1024]{1,0:T(8,128)(2,1)}), bf16[512,1024]{1,0:T(8,128)(2,1)}) %all-gather.8.cloned.1.call-update) | async-done | bytes 1048592 | tf_op jit(solution)/shard_map/all_gather | solution.py:199
  115.2 3.8 convolution_bitcast_fusion
  119.0 14.5 %all-gather.12.cloned.1.call-done = bf16[1,512,1024]{2,1,0:T(8,128)(2,1)} async-done(((bf16[1,128,1024]{2,1,0:T(8,128)(2,1)}), bf16[1,512,1024]{2,1,0:T(8,128)(2,1)}) %all-gather.12.cloned.1.call-update) | async-done | bytes 1048592 | tf_op jit(solution)/shard_map/all_gather | solution.py:215
  133.4 3.2 fusion.74
  136.7 2.3 bitcast_convert_fusion.1
  139.0 3.6 convolution_convert_fusion.4
  142.9 21.1 %reduce-scatter.13.cloned.1.call-done = bf16[128,1024]{1,0:T(8,128)(2,1)} async-done(((bf16[512,1024]{1,0:T(8,128)(2,1)}), bf16[128,1024]{1,0:T(8,128)(2,1)}) %reduce-scatter.13.cloned.1.call-update) | async-done | bytes 262160 | tf_op jit(solution)/shard_map/reduce_scatter | solution.py:224
  164.0 1.3 fusion.55
  165.3 0.5 broadcast_multiply_fusion.1
  165.8 25.6 %reduce-scatter.11.cloned.1.call-done = bf16[128,1024]{1,0:T(8,128)(2,1)} async-done(((bf16[512,1024]{1,0:T(8,128)(2,1)}), bf16[128,1024]{1,0:T(8,128)(2,1)}) %reduce-scatter.11.cloned.1.call-update) | async-done | bytes 262160 | tf_op jit(solution)/shard_map/reduce_scatter | solution.py:206
  191.4 2.3 fusion.51
  193.7 16.8 %all-gather.10.cloned.1.call-done = bf16[512,1024]{1,0:T(8,128)(2,1)} async-done(((bf16[128,1024]{1,0:T(8,128)(2,1)}), bf16[512,1024]{1,0:T(8,128)(2,1)}) %all-gather.10.cloned.1.call-update) | async-done | bytes 1048592 | tf_op jit(solution)/shard_map/all_gather | solution.py:236
  210.5 2.3 divide_convert_fusion
  212.9 0.6 fusion.11
  214.5 0.9 copy-done.25
  215.5 1.1 select_convert_fusion
  216.6 0.4 fusion.27
  217.7 1.0 copy-done.19
  218.7 2.3 bitcast_convert_fusion
  221.0 25.0 %reduce-scatter.15.cloned.1.call-done = bf16[128,1024]{1,0:T(8,128)(2,1)} async-done(((bf16[512,1024]{1,0:T(8,128)(2,1)}), bf16[128,1024]{1,0:T(8,128)(2,1)}) %reduce-scatter.15.cloned.1.call-update) | async-done | bytes 262160 | tf_op jit(solution)/shard_map/reduce_scatter | solution.py:253
  246.0 1.2 fusion.56
  247.2 1.2 fusion.54
  248.5 1.8 gather_fusion
  250.3 5.6 %all-to-all-start.2 = ((bf16[8,24,1024]{2,1,0:T(8,128)(2,1)}), bf16[8,24,1024]{2,1,0:T(8,128)(2,1)S(1)}, u32[]{:S(2)}, u32[]{:S(2)}) async-start(bf16[8,24,1024]{2,1,0:T(8,128)(2,1)} %bitcast.47), calls=%async_computation.6 | async-start | bytes 786432 | tf_op jit(solution)/shard_map/all_to_all | solution.py:266
  256.0 12.5 %all-to-all-done.2 = bf16[8,24,1024]{2,1,0:T(8,128)(2,1)S(1)} async-done(((bf16[8,24,1024]{2,1,0:T(8,128)(2,1)}), bf16[8,24,1024]{2,1,0:T(8,128)(2,1)S(1)}, u32[]{:S(2)}, u32[]{:S(2)}) %all-to-all-start.2) | async-done | bytes 393248 | tf_op jit(solution)/shard_map/all_to_all | solution.py:266
  268.5 0.9 gather_fusion.1
  269.3 4.5 convolution_convert_fusion.1
  274.0 1.0 copy-done.23
  274.9 2.1 convolution_convert_fusion
  277.1 24.7 %reduce-scatter.17.cloned.1.call-done = bf16[256,1024]{1,0:T(8,128)(2,1)} async-done(((bf16[1024,1024]{1,0:T(8,128)(2,1)}), bf16[256,1024]{1,0:T(8,128)(2,1)}) %reduce-scatter.17.cloned.1.call-update) | async-done | bytes 524304 | tf_op jit(solution)/shard_map/reduce_scatter | solution.py:279
  301.8 2.1 convert_element_type.231
  304.0 31.8 %reduce-scatter.21.cloned.1.call-done = bf16[256,1024]{1,0:T(8,128)(2,1)} async-done(((bf16[1024,1024]{1,0:T(8,128)(2,1)}), bf16[256,1024]{1,0:T(8,128)(2,1)}) %reduce-scatter.21.cloned.1.call-update) | async-done | bytes 524304 | tf_op jit(solution)/shard_map/reduce_scatter | solution.py:279
  335.8 2.1 convert_element_type.233
  338.0 65.3 %reduce-scatter.19.cloned.1.call-done = f32[256,128]{1,0:T(8,128)} async-done(((f32[256,1024]{1,0:T(8,128)}), f32[256,128]{1,0:T(8,128)}) %reduce-scatter.19.cloned.1.call-update) | async-done | bytes 131088 | tf_op jit(solution)/shard_map/reduce_scatter | solution.py:288
  403.2 66.7 %reduce-scatter.23.cloned.1.call-done = f32[256,128]{1,0:T(8,128)} async-done(((f32[256,1024]{1,0:T(8,128)}), f32[256,128]{1,0:T(8,128)}) %reduce-scatter.23.cloned.1.call-update) | async-done | bytes 131088 | tf_op jit(solution)/shard_map/reduce_scatter | solution.py:288
  469.9 1.0 pad_maximum_fusion.2
  470.9 0.8 copy.18
  (102 shorter events, 5.0 us)
Async XLA Ops:
  7.2 108.0 %copy-start = (bf16[2,1024,512]{2,1,0:T(8,128)(2,1)S(1)}, bf16[2,1024,512]{2,1,0:T(8,128)(2,1)}, u32[]{:S(2)}) copy-start(bf16[2,1024,512]{2,1,0:T(8,128)(2,1)} %param.29) | copy-start | bytes 6291460
  9.7 14.1 %copy-start.17 = (s32[128]{0:T(128)}, s32[128]{0:T(128)S(1)}, u32[]{:S(2)}) copy-start(s32[128]{0:T(128)S(1)} %compare_select_fusion.2) | copy-start | bytes 1540
  11.5 14.2 %all-to-all-start = ((s32[8,1,24]{2,1,0:T(1,128)}), s32[8,1,24]{2,1,0:T(1,128)S(1)}, u32[]{:S(2)}, u32[]{:S(2)}) async-start(s32[8,1,24]{2,1,0:T(1,128)} %all_to_all.12), calls=%async_computation | async-start | bytes 8192 | tf_op jit(solution)/shard_map/all_to_all | solution.py:156
  20.9 0.8 copy-start.22
  23.8 22.4 %copy-start.16 = (s32[1,512]{1,0:T(1,128)S(1)}, s32[1,512]{1,0:T(1,128)}, u32[]{:S(2)}) copy-start(s32[1,512]{1,0:T(1,128)} %param.25) | copy-start | bytes 6148
  25.7 18.0 %all-to-all-start.1 = ((bf16[8,24,1024]{2,1,0:T(8,128)(2,1)}), bf16[8,24,1024]{2,1,0:T(8,128)(2,1)S(1)}, u32[]{:S(2)}, u32[]{:S(2)}) async-start(bf16[8,24,1024]{2,1,0:T(8,128)(2,1)} %bitcast.3), calls=%async_computation.1 | async-start | bytes 786432 | tf_op jit(solution)/shard_map/all_to_all | solution.py:155
  31.7 28.7 %all-gather.6.cloned.1.call-start = ((), (), s32[]{:S(2)}) async-start(), calls=%async_computation.11 | async-start | bytes 1310720 | tf_op jit(solution)/shard_map/all_gather | solution.py:167
  46.2 49.4 %reduce-scatter.9.cloned.1.call-start = ((), (), s32[]{:S(2)}) async-start(), calls=%async_computation.12 | async-start | bytes 1310720 | tf_op jit(solution)/shard_map/reduce_scatter | solution.py:188
  47.1 16.6 %copy-start.14 = (pred[256,256]{1,0:T(8,128)(4,1)}, pred[256,256]{1,0:T(8,128)(4,1)S(1)}, u32[]{:S(2)}) copy-start(pred[256,256]{1,0:T(8,128)(4,1)S(1)} %fusion.77) | copy-start | bytes 196612
  63.6 4.7 copy-start.11
  63.7 1.6 copy-start.7
  63.7 1.6 copy-start.9
  63.7 4.0 copy-start.5
  65.3 2.2 copy-start.3
  67.4 1.7 copy-start.20
  68.3 0.8 copy-start.12
  70.6 44.6 %all-gather.8.cloned.1.call-start = ((), (), s32[]{:S(2)}) async-start(), calls=%async_computation.13 | async-start | bytes 1310720 | tf_op jit(solution)/shard_map/all_gather | solution.py:199
  96.7 0.7 copy-start.1
  98.3 35.2 %all-gather.12.cloned.1.call-start = ((), (), s32[]{:S(2)}) async-start(), calls=%async_computation.22 | async-start | bytes 1310720 | tf_op jit(solution)/shard_map/all_gather | solution.py:215
  98.9 65.2 %reduce-scatter.13.cloned.1.call-start = ((), (), s32[]{:S(2)}) async-start(), calls=%async_computation.15 | async-start | bytes 1310720 | tf_op jit(solution)/shard_map/reduce_scatter | solution.py:224
  139.0 52.4 %reduce-scatter.11.cloned.1.call-start = ((), (), s32[]{:S(2)}) async-start(), calls=%async_computation.14 | async-start | bytes 1310720 | tf_op jit(solution)/shard_map/reduce_scatter | solution.py:206
  142.7 67.8 %all-gather.10.cloned.1.call-start = ((), (), s32[]{:S(2)}) async-start(), calls=%async_computation.16 | async-start | bytes 1310720 | tf_op jit(solution)/shard_map/all_gather | solution.py:236
  193.7 52.4 %reduce-scatter.15.cloned.1.call-start = ((), (), s32[]{:S(2)}) async-start(), calls=%async_computation.17 | async-start | bytes 1310720 | tf_op jit(solution)/shard_map/reduce_scatter | solution.py:253
  210.5 2.3 copy-start.6
  210.5 2.3 copy-start.15
  210.5 2.3 copy-start.24
  212.9 1.0 copy-start.8
  212.9 1.2 copy-start.10
  212.9 1.4 copy-start.4
  213.8 1.6 copy-start.25
  217.1 1.6 copy-start.19
  218.7 28.6 %copy-start.2 = (bf16[128,1024]{1,0:T(8,128)(2,1)S(1)}, bf16[128,1024]{1,0:T(8,128)(2,1)}, u32[]{:S(2)}) copy-start(bf16[128,1024]{1,0:T(8,128)(2,1)} %get-tuple-element.82) | copy-start | bytes 786436
  248.5 7.5 %copy-start.18 = (s32[128]{0:T(128)S(1)}, s32[128]{0:T(128)}, u32[]{:S(2)}) copy-start(s32[128]{0:T(128)} %copy-done.17) | copy-start | bytes 1540
  250.3 19.1 %copy-start.21 = (bf16[128,1024]{1,0:T(8,128)(2,1)S(1)}, bf16[128,1024]{1,0:T(8,128)(2,1)}, u32[]{:S(2)}) copy-start(bf16[128,1024]{1,0:T(8,128)(2,1)} %param.22) | copy-start | bytes 786436
  250.3 18.2 %all-to-all-start.2 = ((bf16[8,24,1024]{2,1,0:T(8,128)(2,1)}), bf16[8,24,1024]{2,1,0:T(8,128)(2,1)S(1)}, u32[]{:S(2)}, u32[]{:S(2)}) async-start(bf16[8,24,1024]{2,1,0:T(8,128)(2,1)} %bitcast.47), calls=%async_computation.6 | async-start | bytes 786432 | tf_op jit(solution)/shard_map/all_to_all | solution.py:266
  255.9 45.9 %reduce-scatter.17.cloned.1.call-start = ((), (), s32[]{:S(2)}) async-start(), calls=%async_computation.18 | async-start | bytes 2621440 | tf_op jit(solution)/shard_map/reduce_scatter | solution.py:279
  269.3 4.6 copy-start.13
  273.9 1.0 copy-start.23
  273.9 61.9 %reduce-scatter.21.cloned.1.call-start = ((), (), s32[]{:S(2)}) async-start(), calls=%async_computation.20 | async-start | bytes 2621440 | tf_op jit(solution)/shard_map/reduce_scatter | solution.py:279
  277.1 126.2 %reduce-scatter.19.cloned.1.call-start = ((), (), s32[]{:S(2)}) async-start(), calls=%async_computation.19 | async-start | bytes 1179648 | tf_op jit(solution)/shard_map/reduce_scatter | solution.py:288
  304.0 166.0 %reduce-scatter.23.cloned.1.call-start = ((), (), s32[]{:S(2)}) async-start(), calls=%async_computation.21 | async-start | bytes 1179648 | tf_op jit(solution)/shard_map/reduce_scatter | solution.py:288
Sparse Core Ops, SparseCore 0:
  46.3 14.0 all-gather.5
  70.7 24.8 reduce-scatter.8
  98.4 16.7 all-gather.7
  116.7 16.7 all-gather.11
  139.1 24.8 reduce-scatter.12
  166.4 24.9 reduce-scatter.10
  193.8 16.6 all-gather.9
  221.1 24.8 reduce-scatter.14
  274.0 27.7 reduce-scatter.16
  304.4 31.3 reduce-scatter.20
  339.2 63.9 reduce-scatter.18
  406.9 62.9 reduce-scatter.22
where the time goes:
time: 480 us; the launch traced here: 479 us
  waiting for transfers between devices  370 us (77%)
  matrix products  40.9 us (9%)
  starting transfers between devices  19.6 us (4%)
  other arithmetic  18.9 us (4%)
  local copies, waits for them, and re-layouts  15 us (3%)
  between operations  14.7 us (3%)
    reduce_scatter x2, waiting for transfers between devices, shards(): lax.psum_scatter(partial_cols, ('event', 'pack'), scatter_dimension=1, ti...  132 us
    reduce_scatter x2, waiting for transfers between devices, shards(): lax.psum_scatter(column_term(jnp.int32(0), width // tensor_count * lax.ax...  56.5 us
    reduce_scatter x1, waiting for transfers between devices, shards(): lax.psum_scatter(rounded(jnp.dot(hidden, ffn_out, preferred_element_type=...  25.6 us
    reduce_scatter x1, waiting for transfers between devices, shards(): lax.psum_scatter(rounded(jnp.einsum('krc,kdc->rd', piece, attn_in, prefer...  25 us
    reduce_scatter x1, waiting for transfers between devices, shards(): lax.psum_scatter(rounded(jnp.dot(gated, attn_out, preferred_element_type=...  25 us
    reduce_scatter x1, waiting for transfers between devices, shards(): lax.psum_scatter(rounded(jnp.einsum('krf,kdf->rd', piece, ffn_in, preferr...  21.1 us
    all_gather x1, waiting for transfers between devices, shards(): lax.all_gather(d_resid, 'tensor', axis=0, tiled=True)  16.8 us
    all_gather x1, waiting for transfers between devices, shards(): lax.all_gather(normed2, 'tensor', axis=0, tiled=True)  16.3 us
  transfers between devices with their start and end apart: 15, of which 14 were waited for; matrix products, arithmetic and copies ran while one was open for 5% of the time, Pallas kernels for 0%

commit v1 on v0

v1 whole, which is shorter than its diff:
```python
import jax
import jax.numpy as jnp
from jax import lax
from jax.sharding import PartitionSpec as P

D = 1024
HEADS = 16
EPS = 1e-06
SLOT_LANES = 128


def silu_grad(value):
    sigma = jax.nn.sigmoid(value)
    return sigma * (1.0 + value * (1.0 - sigma))


def norm_rows(rows):
    wide = rows.astype(jnp.float32)
    factor = lax.rsqrt(jnp.mean(wide * wide, axis=-1, keepdims=True) + EPS)
    return (wide * factor, factor)


def norm_back(grad, normed, factor):
    return factor * (grad - normed * jnp.mean(grad * normed, axis=-1, keepdims=True))


def dot(left, right, dims=((1,), (0,))):
    return lax.dot_general(left, right, (dims, ((), ())), preferred_element_type=jnp.float32)


def bf16(value):
    return value.astype(jnp.bfloat16)


def near(value):
    count = lax.axis_size("tensor")
    return lax.ppermute(value, "tensor", [(i, i ^ 1) for i in range(count)])


def far(value):
    count = lax.axis_size("tensor")
    return lax.ppermute(value, "tensor", [(i, i ^ 2) for i in range(count)])


def doc_counts(documents):
    length = documents.shape[0]
    places = jnp.arange(length, dtype=jnp.int32)
    same = (documents[:, None] == documents[None, :]) & (places[None, :] <= places[:, None])
    return jnp.sum(same.astype(jnp.float32), axis=1)


def bucket_index(dest_owner, groups, capacity):
    onehot = (dest_owner[:, None] == jnp.arange(groups, dtype=jnp.int32)[None, :]).astype(jnp.int32)
    rows = dest_owner.shape[0]
    order = jnp.arange(rows, dtype=jnp.int32)
    earlier = (dest_owner[:, None] == dest_owner[None, :]) & (order[None, :] < order[:, None])
    rank = jnp.sum(earlier.astype(jnp.int32), axis=1)
    return dest_owner * capacity + rank


def scatter_sum(value, axis):
    count = lax.axis_size(axis)
    me = lax.axis_index(axis)
    total = lax.dynamic_index_in_dim(value, me, 0, keepdims=False)
    for step in range(1, count):
        target = lax.rem(me + step, count)
        block = bf16(lax.dynamic_index_in_dim(value, target, 0, keepdims=False))
        total = total + lax.ppermute(
            block, axis, [(i, (i + step) % count) for i in range(count)]
        ).astype(jnp.float32)
    return total


def shards(
    features,
    dest_owner,
    dest_slot,
    doc_ids,
    enc_weight,
    attn_in,
    attn_out,
    ffn_in,
    ffn_out,
    out_grad,
):
    rows_dev, width = features.shape
    groups = lax.axis_size(("event", "pack"))
    tensor_count = lax.axis_size("tensor")
    t = lax.axis_index("tensor")
    d_out = out_grad[0]
    documents = doc_ids[0]
    length = documents.shape[0]

    mean_load = rows_dev // groups
    capacity = mean_load + mean_load // 2
    place = bucket_index(dest_owner, groups, capacity)
    spots = jnp.arange(groups * capacity, dtype=jnp.int32)
    send_hot = spots[:, None] == place[None, :]
    with_slot = jnp.concatenate(
        [features, jnp.broadcast_to(bf16(dest_slot + 1)[:, None], (rows_dev, SLOT_LANES))], axis=1
    )
    send = bf16(dot(bf16(send_hot), with_slot)).reshape(groups, capacity, width + SLOT_LANES)
    got = lax.all_to_all(send, ("event", "pack"), split_axis=0, concat_axis=0, tiled=True)
    got = got.reshape(groups * capacity, width + SLOT_LANES)
    got_slots = got[:, width].astype(jnp.int32) - 1
    recv_hot = bf16(jnp.arange(rows_dev, dtype=jnp.int32)[:, None] == got_slots[None, :])
    mine = bf16(dot(recv_hot, got[:, :width]))

    d_out_far = far(d_out)
    ffn_in_near = near(ffn_in)
    ffn_out_near = near(ffn_out)
    attn_out_near = near(attn_out)

    mine_near = near(mine)
    mine_far = far(mine)
    mine_both = near(mine_far)

    def encode(rows):
        pre = dot(rows, enc_weight[0])
        act = bf16(jax.nn.silu(pre))
        packed = bf16(dot(act, enc_weight[1]))
        normed_f, factor = norm_rows(packed)
        proj = bf16(
            jnp.einsum("rd,kdc->krc", bf16(normed_f), attn_in, preferred_element_type=jnp.float32)
        )
        return pre, act, packed, proj

    pair_a = jnp.concatenate([mine, mine_near], axis=0)
    pair_b = jnp.concatenate([mine_far, mine_both], axis=0)
    pre_a, act_a, packed_a, proj_a = encode(pair_a)
    pre_b, act_b, packed_b, proj_b = encode(pair_b)
    proj_rel = [proj_a[:, :rows_dev], proj_a[:, rows_dev:], proj_b[:, :rows_dev], proj_b[:, rows_dev:]]
    packed = packed_a[:rows_dev]

    def reorder(blocks, axis):
        stacked = jnp.stack(blocks)
        return jnp.concatenate(
            [lax.dynamic_index_in_dim(stacked, t ^ b, 0, keepdims=False) for b in range(tensor_count)],
            axis=axis,
        )

    projected = reorder(proj_rel, 1)
    local_cols = projected.shape[2]
    head_dim = D // HEADS
    local_heads = local_cols // head_dim
    head_scale = head_dim ** (-0.5)

    def split_heads(value):
        return value.reshape(length, local_heads, head_dim).transpose(1, 0, 2)

    def join_heads(value):
        return value.transpose(1, 0, 2).reshape(length, local_cols)

    query = split_heads(projected[0])
    keys = split_heads(projected[1])
    values = split_heads(projected[2])
    gate_raw = projected[3].astype(jnp.float32)
    root = jnp.sqrt(doc_counts(documents))[:, None]
    places = jnp.arange(length, dtype=jnp.int32)
    saved = []
    parts = []
    for b in range(tensor_count):
        lower, upper = b * rows_dev, (b + 1) * rows_dev
        first = max(lower - rows_dev, 0)
        allowed = (documents[lower:upper, None] == documents[None, first:upper]) & (
            places[None, first:upper] <= places[lower:upper, None]
        )
        scores = (
            jnp.einsum(
                "hqd,hkd->hqk",
                query[:, lower:upper],
                keys[:, first:upper],
                preferred_element_type=jnp.float32,
            )
            * head_scale
        )
        weights = bf16(jnp.where(allowed[None], jax.nn.silu(scores), 0.0))
        parts.append(
            jnp.einsum(
                "hqk,hkd->hqd", weights, values[:, first:upper], preferred_element_type=jnp.float32
            )
        )
        saved.append((lower, upper, first, allowed, scores, weights))
    attended = join_heads(jnp.concatenate(parts, axis=1)) / root
    gated = bf16(attended * jax.nn.silu(gate_raw))

    def block(value, index):
        return lax.dynamic_slice_in_dim(value, index * rows_dev, rows_dev, axis=0)

    give = jnp.concatenate([block(gated, t ^ 3), block(gated, t ^ 1)], axis=0)
    keep = jnp.concatenate([block(gated, t ^ 2), block(gated, t)], axis=0)
    take = near(give)
    attn_part = dot(keep, attn_out) + dot(take, attn_out_near)
    attn_sum = attn_part[rows_dev:] + far(bf16(attn_part[:rows_dev])).astype(jnp.float32)
    resid = bf16(packed.astype(jnp.float32) + attn_sum)
    normed2_f, factor2 = norm_rows(resid)
    normed2 = bf16(normed2_f)
    normed2_far = far(normed2)

    def ffn(rows, cotangent):
        out = 0.0
        back = 0.0
        for w_in, w_out in ((ffn_in, ffn_out), (ffn_in_near, ffn_out_near)):
            d_hidden = dot(cotangent, w_out, ((1,), (1,)))
            gate = dot(rows, w_in[0])
            upper = dot(rows, w_in[1])
            sigma = jax.nn.sigmoid(gate)
            silu = gate * sigma
            hidden = bf16(silu * upper)
            d_gate = bf16(d_hidden * upper * (sigma * (1.0 + gate * (1.0 - sigma))))
            d_upper = bf16(d_hidden * silu)
            out = out + dot(hidden, w_out)
            back = (
                back + dot(d_gate, w_in[0], ((1,), (1,))) + dot(d_upper, w_in[1], ((1,), (1,)))
            )
        return out, back

    out_own, back_own = ffn(normed2, d_out)
    out_far, back_far = ffn(normed2_far, d_out_far)
    d_normed2 = back_own + far(bf16(back_far)).astype(jnp.float32)
    ffn_sum = out_own + far(bf16(out_far)).astype(jnp.float32)
    packed_out = bf16(resid.astype(jnp.float32) + ffn_sum)
    d_resid = bf16(d_out.astype(jnp.float32) + norm_back(d_normed2, normed2_f, factor2))

    d_resid_near = near(d_resid)
    d_resid_far = far(d_resid)
    d_resid_both = near(d_resid_far)
    d_resid_all = reorder([d_resid, d_resid_near, d_resid_far, d_resid_both], 0)
    d_gated = dot(d_resid_all, attn_out, ((1,), (1,)))
    d_attended = bf16(d_gated * jax.nn.silu(gate_raw) / root)
    d_gate_proj = bf16(d_gated * attended * silu_grad(gate_raw))
    d_heads = split_heads(d_attended)
    d_query_parts = []
    d_keys = jnp.zeros(keys.shape, jnp.float32)
    d_values = jnp.zeros(keys.shape, jnp.float32)
    for lower, upper, first, allowed, scores, weights in saved:
        d_block = d_heads[:, lower:upper]
        d_weights = jnp.einsum(
            "hqd,hkd->hqk", d_block, values[:, first:upper], preferred_element_type=jnp.float32
        )
        d_scores = bf16(jnp.where(allowed[None], d_weights * silu_grad(scores), 0.0))
        d_query_parts.append(
            jnp.einsum(
                "hqk,hkd->hqd", d_scores, keys[:, first:upper], preferred_element_type=jnp.float32
            )
        )
        d_keys = d_keys.at[:, first:upper].add(
            jnp.einsum(
                "hqk,hqd->hkd", d_scores, query[:, lower:upper], preferred_element_type=jnp.float32
            )
        )
        d_values = d_values.at[:, first:upper].add(
            jnp.einsum("hqk,hqd->hkd", weights, d_block, preferred_element_type=jnp.float32)
        )
    d_query = jnp.concatenate(d_query_parts, axis=1) * head_scale
    d_projected = jnp.stack(
        [
            bf16(join_heads(d_query)),
            bf16(join_heads(d_keys * head_scale)),
            bf16(join_heads(d_values)),
            d_gate_proj,
        ]
    )
    d_norm_part = jnp.einsum(
        "krc,kdc->rd", d_projected, attn_in, preferred_element_type=jnp.float32
    )
    give = bf16(jnp.concatenate([block(d_norm_part, t ^ 3), block(d_norm_part, t ^ 1)], axis=0))
    take = near(give).astype(jnp.float32)
    sum_far = block(d_norm_part, t ^ 2) + take[:rows_dev]
    d_normed = block(d_norm_part, t) + take[rows_dev:] + far(bf16(sum_far)).astype(jnp.float32)
    normed_f, factor1 = norm_rows(packed)
    d_packed = bf16(d_resid.astype(jnp.float32) + norm_back(d_normed, normed_f, factor1))

    back_rows = bf16(dot(recv_hot, d_packed, ((0,), (0,)))).reshape(groups, capacity, width)
    returned = lax.all_to_all(back_rows, ("event", "pack"), split_axis=0, concat_axis=0, tiled=True)
    returned = returned.reshape(groups * capacity, width)
    row_grad = bf16(dot(bf16(send_hot), returned, ((0,), (0,))))

    cot_near = near(d_packed)
    cot_far = far(d_packed)
    cot_both = near(cot_far)
    cot1 = jnp.concatenate([d_packed, cot_near, cot_far, cot_both], axis=0)
    cols = width // tensor_count

    def columns(value):
        return lax.dynamic_slice_in_dim(value, t * cols, cols, axis=1)

    act0 = jnp.concatenate([pair_a, pair_b], axis=0)
    act1 = jnp.concatenate([act_a, act_b], axis=0)
    pre0 = jnp.concatenate([columns(pre_a), columns(pre_b)], axis=0)
    w1_rows = lax.dynamic_slice_in_dim(enc_weight[1], t * cols, cols, axis=0)
    cot0 = bf16(dot(cot1, w1_rows, ((1,), (1,))) * silu_grad(pre0))
    event_count = lax.axis_size("event")
    pack_count = lax.axis_size("pack")

    def reduce_layer(act, cot):
        part = dot(act, cot, ((0,), (0,)))
        part = part.reshape(event_count, width // event_count, cols)
        part = scatter_sum(part, "event")
        part = part.reshape(pack_count, width // event_count // pack_count, cols)
        return scatter_sum(part, "pack")

    grad1 = reduce_layer(act1, columns(cot1))
    grad0 = reduce_layer(act0, cot0)
    return (packed_out[None], row_grad, jnp.stack([grad0, grad1]))


def solution(mesh):
    placed = (
        P(("event", "pack", "tensor"), None),
        P(("event", "pack", "tensor")),
        P(("event", "pack", "tensor")),
        P(("event", "pack"), None),
        P(),
        P(None, None, "tensor"),
        P("tensor", None),
        P(None, None, "tensor"),
        P("tensor", None),
        P(("event", "pack"), "tensor", None),
    )
    return jax.shard_map(
        shards,
        mesh=mesh,
        in_specs=placed,
        out_specs=(
            P(("event", "pack"), "tensor", None),
            P(("event", "pack", "tensor"), None),
            P(None, ("event", "pack"), "tensor"),
        ),
        check_vma=False,
    )
```

time: 480 us -> 209 us (0.44)
  waiting for transfers between devices: 370 us -> 46.5 us
  matrix products: 40.9 us -> 75 us
  starting transfers between devices: 19.6 us -> 35.9 us
  local copies, waits for them, and re-layouts: 15 us -> 28.5 us
  between operations: 14.7 us -> 2.03 us
    reduce_scatter x8 -> x0, waiting for transfers between devices: 285 us -> none  [the longest x2 132 us: shards(): lax.psum_scatter(partial_cols, ('event', 'pack'), scatter_dimension=1, ti...]
    all_gather x4 -> x0, waiting for transfers between devices: 60.6 us -> none  [the longest x1 16.8 us: shards(): lax.all_gather(d_resid, 'tensor', axis=0, tiled=True)]
    ppermute x0 -> x28, waiting for transfers between devices: none -> 38.2 us  [the longest x9 30.2 us: far(): return lax.ppermute(value, 'tensor', [(i, i ^ 2) for i in range(count)])]
    dot_general x24 -> x64, matrix products: 40.9 us -> 75 us  [the longest x37 50.4 us: dot(): lax.dot_general(left, right, (dims, ((), ())), preferred_element_type=jnp...]
    ppermute x0 -> x28, starting transfers between devices: none -> 24.9 us  [the longest x9 12.5 us: far(): return lax.ppermute(value, 'tensor', [(i, i ^ 2) for i in range(count)])]
    all_to_all x1, waiting for transfers between devices: 12.5 us -> 2.65 us  [shards(): lax.all_to_all(back_rows, ('event', 'pack'), split_axis=0, concat_axis=0,...]
    convert_element_type x0 -> x8, local copies, waits for them, and re-layouts: none -> 9.09 us  [bf16(): return value.astype(jnp.bfloat16)]
    all_to_all x2 -> x1, starting transfers between devices: 13.2 us -> 7.25 us  [shards(): lax.all_to_all(send, ('event', 'pack'), split_axis=0, concat_axis=0, tile...]
  transfers between devices with their start and end apart: 15 -> 30, of which waited for: 14 -> 14; matrix products, arithmetic and copies ran while one was open for 5% -> 36% of each run, Pallas kernels for 0% -> 0%
where the time goes in v1:
time: 209 us; the launch traced here: 207 us
  matrix products  75 us (36%)
  waiting for transfers between devices  46.5 us (22%)
  starting transfers between devices  35.9 us (17%)
  local copies, waits for them, and re-layouts  28.5 us (14%)
  other arithmetic  19.4 us (9%)
    dot_general x37, matrix products, dot(): lax.dot_general(left, right, (dims, ((), ())), preferred_element_type=jnp...  50.4 us
    ppermute x9, waiting for transfers between devices, far(): return lax.ppermute(value, 'tensor', [(i, i ^ 2) for i in range(count)])  30.2 us
    ppermute x9, starting transfers between devices, far(): return lax.ppermute(value, 'tensor', [(i, i ^ 2) for i in range(count)])  12.5 us
    ppermute x8, starting transfers between devices, scatter_sum(): lax.ppermute(block, axis, [(i, (i + step) % count) for i in range(count)])  10.7 us
    convert_element_type x8, local copies, waits for them, and re-layouts, bf16(): return value.astype(jnp.bfloat16)  9.09 us
    convert_element_type x9, other arithmetic, bf16(): return value.astype(jnp.bfloat16)  7.39 us
    ppermute x8, waiting for transfers between devices, scatter_sum(): lax.ppermute(block, axis, [(i, (i + step) % count) for i in range(count)])  7.29 us
    all_to_all x1, starting transfers between devices, shards(): lax.all_to_all(send, ('event', 'pack'), split_axis=0, concat_axis=0, tile...  7.25 us
  transfers between devices with their start and end apart: 30, of which 14 were waited for; matrix products, arithmetic and copies ran while one was open for 36% of the time, Pallas kernels for 0%

profile of v1, /device:TPU:0, one launch (start us, length us, event | category | flops | bytes accessed | tf_op | source)
XLA Modules:
  0.0 207.3 jit_solution(17466217311563220950)
XLA Ops:
  3.1 2.0 convolution_convert_fusion
  5.1 7.3 %all-to-all-start = ((bf16[8,24,1152]{2,1,0:T(8,128)(2,1)}), bf16[8,24,1152]{2,1,0:T(8,128)(2,1)}, u32[]{:S(2)}, u32[]{:S(2)}) async-start(bf16[8,24,1152]{2,1,0:T(8,128)(2,1)} %bitcast.266), calls=%async_computation | async-start | bytes 884736 | tf_op jit(solution)/shard_map/all_to_all | solution.py:103
  12.4 1.6 collective-permute-start.10
  20.5 5.6 %all-to-all-done = bf16[8,24,1152]{2,1,0:T(8,128)(2,1)} async-done(((bf16[8,24,1152]{2,1,0:T(8,128)(2,1)}), bf16[8,24,1152]{2,1,0:T(8,128)(2,1)}, u32[]{:S(2)}, u32[]{:S(2)}) %all-to-all-start) | async-done | bytes 442400 | tf_op jit(solution)/shard_map/all_to_all | solution.py:103
  28.3 1.6 collective-permute-start.1
  29.9 2.1 %fusion.280 = f32[128,512]{1,0:T(8,128)} fusion(bf16[128,1024]{1,0:T(8,128)(2,1)} %collective-permute-done.10, bf16[512,1024]{1,0:T(8,128)(2,1)S(1)} %copy-done.1), kind=kOutput, calls=%fused_computation.403 | convolution fusion | flops 134217728 | bytes 1572864 | tf_op jit(solution)/shard_map/dot_general | solution.py:28
  32.0 2.7 %collective-permute-done.1 = bf16[128,1024]{1,0:T(8,128)(2,1)S(1)} collective-permute-done((bf16[128,1024]{1,0:T(8,128)(2,1)S(1)}, bf16[128,1024]{1,0:T(8,128)(2,1)S(1)}, u32[]{:S(2)}, u32[]{:S(2)}) %collective-permute-start.1) | collective-permute-done | bytes 262176 | tf_op jit(solution)/shard_map/ppermute | solution.py:42
  34.7 3.5 %multiply_convert_fusion.1 = (bf16[256,1024]{1,0:T(8,128)(2,1)S(1)}, f32[256,1024]{1,0:T(8,128)}) fusion(bf16[2,1024,1024]{2,1,0:T(8,128)(2,1)} %param.30, bf16[128,1024]{1,0:T(8,128)(2,1)S(1)} %collective-permute-done, bf16[128,1024]{1,0:T(8,128)(2,1)S(1)} %convolution_convert_fusion.5), kind=kOutput, calls=%fused_computation.125 | convolution fusion | flops 539230208 | bytes 4194304 | tf_op jit(solution)/shard_map/dot_general | solution.py:28
  39.9 2.5 %fusion.281 = f32[128,512]{1,0:T(8,128)} fusion(bf16[128,1024]{1,0:T(8,128)(2,1)} %collective-permute-done.10, bf16[512,1024]{1,0:T(8,128)(2,1)} %collective-permute-done.7), kind=kOutput, calls=%fused_computation.404 | convolution fusion | flops 134217728 | bytes 1572864 | tf_op jit(solution)/shard_map/dot_general | solution.py:28
  42.4 1.8 multiply_convert_fusion
  48.0 1.8 copy.44
  49.8 1.8 copy.45
  51.6 1.8 copy.46
  53.4 1.9 select_convert_fusion.3
  55.3 2.2 %select_convert_fusion.2 = (bf16[4,128,256]{2,1,0:T(8,128)(2,1)S(1)}, f32[4,128,256]{2,1,0:T(8,128)}) fusion(pred[128,256]{1,0:T(8,128)(4,1)} %compare_and_fusion.2, bf16[4,512,64]{1,2,0:T(8,128)(2,1)} %bitcast.251, bf16[4,512,64]{1,2,0:T(8,128)(2,1)} %bitcast.276), kind=kOutput, calls=%fused_computation.216 | convolution fusion | flops 17694720 | bytes 1015808 | tf_op jit(solution)/shard_map/hqd,hkd->hqk/dot_general | solution.py:169
  62.2 2.0 copy.47
  64.2 1.4 multiply_convert_fusion.3
  67.1 1.3 convolution_add_fusion
  68.5 1.6 collective-permute-start.5
  70.1 1.7 fusion.256
  71.8 5.3 %collective-permute-done.5 = bf16[128,1024]{1,0:T(8,128)(2,1)S(1)} collective-permute-done((bf16[128,1024]{1,0:T(8,128)(2,1)S(1)}, bf16[128,1024]{1,0:T(8,128)(2,1)S(1)}, u32[]{:S(2)}, u32[]{:S(2)}) %collective-permute-start.5) | collective-permute-done | bytes 262176 | tf_op jit(solution)/shard_map/ppermute | solution.py:42
  78.0 1.6 collective-permute-start.8
  81.4 4.4 %collective-permute-done.8 = bf16[128,1024]{1,0:T(8,128)(2,1)S(1)} collective-permute-done((bf16[128,1024]{1,0:T(8,128)(2,1)S(1)}, bf16[128,1024]{1,0:T(8,128)(2,1)S(1)}, u32[]{:S(2)}, u32[]{:S(2)}) %collective-permute-start.8) | collective-permute-done | bytes 262176 | tf_op jit(solution)/shard_map/ppermute | solution.py:42
  87.7 1.6 fusion.91
  89.3 1.6 fusion.95
  90.9 1.8 fusion.93
  92.7 1.7 fusion.30
  94.4 1.6 collective-permute-start.11
  96.0 1.5 fusion.92
  97.6 1.8 fusion.94
  99.4 1.5 fusion.96
  101.4 2.1 %fusion.112 = (f32[128]{0:T(128)S(1)}, f32[128,1024]{1,0:T(8,128)S(1)}) fusion(bf16[128,1024]{1,0:T(8,128)(2,1)S(1)} %get-tuple-element.100, f32[128]{0:T(128)S(1)} %add_rsqrt_fusion.3, bf16[128,1024]{1,0:T(8,128)(2,1)S(1)} %collective-permute-done.11, f32[128,1024]{1,0:T(8,128)S(1)} %fusion.94, f32[128,1024]{1,0:T(8,128)S(1)} %convolution_add_fusion.4, ...), kind=kOutput, calls=%fused_computation.159 | convolution fusion | flops 135921536 | bytes 3933184 | tf_op jit(solution)/shard_map/dot_general | solution.py:28
  105.7 5.5 %collective-permute-done.13 = bf16[128,1024]{1,0:T(8,128)(2,1)} collective-permute-done((bf16[128,1024]{1,0:T(8,128)(2,1)}, bf16[128,1024]{1,0:T(8,128)(2,1)}, u32[]{:S(2)}, u32[]{:S(2)}) %collective-permute-start.13) | collective-permute-done | bytes 262176 | tf_op jit(solution)/shard_map/ppermute | solution.py:42
  111.2 1.5 slice.385
  112.7 1.7 constant_dynamic-slice_fusion.1
  114.4 1.4 pad_maximum_fusion.2
  115.9 2.4 %divide_convert_fusion = (bf16[512,256]{1,0:T(8,128)(2,1)}, bf16[1,512,256]{2,1,0:T(8,128)(2,1)}) fusion(f32[512]{0:T(512)S(1)} %copy-done.60, bf16[4,512,256]{2,1,0:T(8,128)(2,1)} %copy-done.2, f32[512,256]{1,0:T(8,128)S(1)} %copy-done.5, bf16[256,1024]{1,0:T(8,128)(2,1)S(1)} %copy-done.37, bf16[128,1024]{1,0:T(8,128)(2,1)S(1)} %get-tuple-element.106, ...), kind=kOutput, calls=%fused_computation.210 | convolution fusion | flops 274726912 | bytes 2885632 | tf_op jit(solution)/shard_map/dot_general | solution.py:28
  118.3 1.8 copy.49
  120.1 1.3 fusion.42
  122.5 1.7 fusion.231
  127.9 1.8 copy.51
  134.0 1.8 copy.52
  140.0 1.8 copy.53
  141.8 2.5 %convolution_bitcast_fusion = f32[512,1024]{1,0:T(8,128)S(1)} fusion(bf16[4,1024,256]{2,1,0:T(8,128)(2,1)S(1)} %copy-done, bf16[1,512,256]{2,1,0:T(8,128)(2,1)} %get-tuple-element.104, bf16[1,512,256]{2,1,0:T(8,128)(2,1)} %copy.53, bf16[1,512,256]{2,1,0:T(8,128)(2,1)} %copy.52, bf16[1,512,256]{2,1,0:T(8,128)(2,1)} %copy.51), kind=kOutput, calls=%fused_computation.11 | convolution fusion | flops 1075314688 | bytes 5242880 | tf_op jit(solution)/shard_map/krc,kdc->rd/dot_general | solution.py:264
  145.0 1.7 constant_dynamic-slice_fusion
  147.3 1.3 collective-permute-start.16
  148.6 1.6 fusion.32
  151.0 5.5 %collective-permute-done.16 = bf16[128,1024]{1,0:T(8,128)(2,1)S(1)} collective-permute-done((bf16[128,1024]{1,0:T(8,128)(2,1)S(1)}, bf16[128,1024]{1,0:T(8,128)(2,1)S(1)}, u32[]{:S(2)}, u32[]{:S(2)}) %collective-permute-start.16) | collective-permute-done | bytes 262176 | tf_op jit(solution)/shard_map/ppermute | solution.py:42
  156.8 2.0 fusion.111
  160.5 6.4 %collective-permute-done.18 = bf16[128,1024]{1,0:T(8,128)(2,1)} collective-permute-done((bf16[128,1024]{1,0:T(8,128)(2,1)}, bf16[128,1024]{1,0:T(8,128)(2,1)}, u32[]{:S(2)}, u32[]{:S(2)}) %collective-permute-start.18) | collective-permute-done | bytes 262176 | tf_op jit(solution)/shard_map/ppermute | solution.py:42
  167.0 2.3 %fusion.33 = bf16[1,128,1024]{2,1,0:T(8,128)(2,1)} fusion(f32[128,1024]{1,0:T(8,128)S(1)} %fusion.167, bf16[512,1024]{1,0:T(8,128)(2,1)} %collective-permute-done.7, bf16[128,1024]{1,0:T(8,128)(2,1)S(1)} %get-tuple-element.100, bf16[128,1024]{1,0:T(8,128)(2,1)S(1)} %collective-permute-done.9, f32[128,512]{1,0:T(8,128)S(1)} %copy-done.32, ...), kind=kOutput, calls=%fused_computation.54 | convolution fusion | flops 135397376 | bytes 2883584 | tf_op jit(solution)/shard_map/dot_general | solution.py:28
  169.2 2.0 convolution_convert_fusion.3
  171.3 3.7 %all-to-all-start.1 = ((bf16[8,24,1024]{2,1,0:T(8,128)(2,1)}), bf16[8,24,1024]{2,1,0:T(8,128)(2,1)S(1)}, u32[]{:S(2)}, u32[]{:S(2)}) async-start(bf16[8,24,1024]{2,1,0:T(8,128)(2,1)} %bitcast.62), calls=%async_computation.1 | async-start | bytes 786432 | tf_op jit(solution)/shard_map/all_to_all | solution.py:275
  175.0 4.0 %fusion.41 = f32[1024,256]{1,0:T(8,128)} fusion(bf16[128,1024]{1,0:T(8,128)(2,1)} %copy-done.67, bf16[128,1024]{1,0:T(8,128)(2,1)} %copy-done.65, bf16[128,1024]{1,0:T(8,128)(2,1)} %copy-done.66, bf16[128,1024]{1,0:T(8,128)(2,1)S(1)} %copy-done.41, f32[256,256]{1,0:T(8,128)} %constant_dynamic-slice_fusion, f32[256,256]{1,0:T(8,128)S(1)} %copy-done.42, ...), kind=kOutput, calls=%fused_computation.70 | convolution fusion | flops 546570240 | bytes 4194308 | tf_op jit(solution)/shard_map/dot_general | solution.py:28
  179.0 1.9 fusion.158
  180.8 2.0 collective-permute-start.20
  185.6 2.6 %all-to-all-done.1 = bf16[8,24,1024]{2,1,0:T(8,128)(2,1)S(1)} async-done(((bf16[8,24,1024]{2,1,0:T(8,128)(2,1)}), bf16[8,24,1024]{2,1,0:T(8,128)(2,1)S(1)}, u32[]{:S(2)}, u32[]{:S(2)}) %all-to-all-start.1) | async-done | bytes 393248 | tf_op jit(solution)/shard_map/all_to_all | solution.py:275
  189.2 2.7 %collective-permute-done.20 = bf16[512,256]{1,0:T(8,128)(2,1)S(1)} collective-permute-done((bf16[512,256]{1,0:T(8,128)(2,1)}, bf16[512,256]{1,0:T(8,128)(2,1)S(1)}, u32[]{:S(2)}, u32[]{:S(2)}) %collective-permute-start.20) | collective-permute-done | bytes 262176 | tf_op jit(solution)/shard_map/ppermute | solution.py:68
  193.4 2.4 %collective-permute-start.22 = (bf16[128,256]{1,0:T(8,128)(2,1)S(1)}, bf16[128,256]{1,0:T(8,128)(2,1)S(1)}, u32[]{:S(2)}, u32[]{:S(2)}) collective-permute-start(bf16[128,256]{1,0:T(8,128)(2,1)S(1)} %get-tuple-element.118), channel_id=1, source_target_pairs={{0,8},{4,12},{8,0},{12,4},{1,9},{5,13},{9,1},{13,5},{2,10},{6,14},... | collective-permute-start | bytes 196616 | tf_op jit(solution)/shard_map/ppermute | solution.py:68
  195.8 1.8 collective-permute-start.23
  198.0 1.4 collective-permute-start.26
  199.5 2.6 %collective-permute-start.27 = (bf16[128,256]{1,0:T(8,128)(2,1)S(1)}, bf16[128,256]{1,0:T(8,128)(2,1)S(1)}, u32[]{:S(2)}, u32[]{:S(2)}) collective-permute-start(bf16[128,256]{1,0:T(8,128)(2,1)S(1)} %get-tuple-element.120), channel_id=1, source_target_pairs={{0,12},{4,0},{8,4},{12,8},{1,13},{5,1},{9,5},{13,9},{2,14},{6,2},{... | collective-permute-start | bytes 196616 | tf_op jit(solution)/shard_map/ppermute | solution.py:68
  202.1 2.1 collective-permute-done.25
  204.2 2.3 %collective-permute-done.26 = bf16[128,256]{1,0:T(8,128)(2,1)S(1)} collective-permute-done((bf16[128,256]{1,0:T(8,128)(2,1)S(1)}, bf16[128,256]{1,0:T(8,128)(2,1)S(1)}, u32[]{:S(2)}, u32[]{:S(2)}) %collective-permute-start.26) | collective-permute-done | bytes 65568 | tf_op jit(solution)/shard_map/ppermute | solution.py:68
  (286 shorter events, 53.4 us)
Async XLA Ops:
  0.6 38.5 %copy-start = (bf16[4,1024,256]{2,1,0:T(8,128)(2,1)S(1)}, bf16[4,1024,256]{2,1,0:T(8,128)(2,1)}, u32[]{:S(2)}) copy-start(bf16[4,1024,256]{2,1,0:T(8,128)(2,1)} %param.31) | copy-start | bytes 6291460
  0.6 18.6 %copy-start.3 = (bf16[1,128,1024]{2,1,0:T(8,128)(2,1)S(1)}, bf16[1,128,1024]{2,1,0:T(8,128)(2,1)}, u32[]{:S(2)}) copy-start(bf16[1,128,1024]{2,1,0:T(8,128)(2,1)} %param.35) | copy-start | bytes 786436
  0.7 18.6 %copy-start.1 = (bf16[512,1024]{1,0:T(8,128)(2,1)S(1)}, bf16[512,1024]{1,0:T(8,128)(2,1)}, u32[]{:S(2)}) copy-start(bf16[512,1024]{1,0:T(8,128)(2,1)} %param.34) | copy-start | bytes 3145732
  5.1 21.0 %all-to-all-start = ((bf16[8,24,1152]{2,1,0:T(8,128)(2,1)}), bf16[8,24,1152]{2,1,0:T(8,128)(2,1)}, u32[]{:S(2)}, u32[]{:S(2)}) async-start(bf16[8,24,1152]{2,1,0:T(8,128)(2,1)} %bitcast.266), calls=%async_computation | async-start | bytes 884736 | tf_op jit(solution)/shard_map/all_to_all | solution.py:103
  12.4 54.1 %collective-permute-start.4 = (bf16[256,1024]{1,0:T(8,128)(2,1)}, bf16[256,1024]{1,0:T(8,128)(2,1)}, u32[]{:S(2)}, u32[]{:S(2)}) collective-permute-start(bf16[256,1024]{1,0:T(8,128)(2,1)} %param.32), channel_id=1, source_target_pairs={{0,1},{1,0},{2,3},{3,2},{4,5},{5,4},{6,7},{7,6},{8,9},{9,8},{10,11... | collective-permute-start | bytes 1572872 | tf_op jit(solution)/shard_map/ppermute | solution.py:37
  12.4 17.5 %collective-permute-start.10 = (bf16[128,1024]{1,0:T(8,128)(2,1)}, bf16[128,1024]{1,0:T(8,128)(2,1)}, u32[]{:S(2)}, u32[]{:S(2)}) collective-permute-start(bf16[128,1024]{1,0:T(8,128)(2,1)} %bitcast.248), channel_id=1, source_target_pairs={{0,2},{1,3},{2,0},{3,1},{4,6},{5,7},{6,4},{7,5},{8,10},{9,11},{10,... | collective-permute-start | bytes 786440 | tf_op jit(solution)/shard_map/ppermute | solution.py:42
  14.0 73.7 %collective-permute-start.6 = (bf16[2,1024,512]{2,1,0:T(8,128)(2,1)}, bf16[2,1024,512]{2,1,0:T(8,128)(2,1)}, u32[]{:S(2)}, u32[]{:S(2)}) collective-permute-start(bf16[2,1024,512]{2,1,0:T(8,128)(2,1)} %param.33), channel_id=1, source_target_pairs={{0,1},{1,0},{2,3},{3,2},{4,5},{5,4},{6,7},{7,6},{8,9},{9,8},{10,11... | collective-permute-start | bytes 6291464 | tf_op jit(solution)/shard_map/ppermute | solution.py:37
  14.1 25.7 %collective-permute-start.7 = (bf16[512,1024]{1,0:T(8,128)(2,1)}, bf16[512,1024]{1,0:T(8,128)(2,1)}, u32[]{:S(2)}, u32[]{:S(2)}) collective-permute-start(bf16[512,1024]{1,0:T(8,128)(2,1)} %param.34), channel_id=1, source_target_pairs={{0,1},{1,0},{2,3},{3,2},{4,5},{5,4},{6,7},{7,6},{8,9},{9,8},{10,11... | collective-permute-start | bytes 3145736 | tf_op jit(solution)/shard_map/ppermute | solution.py:37
  27.0 11.2 %copy-start.58 = (s32[192]{0:T(256)}, s32[192]{0:T(256)S(1)}, u32[]{:S(2)}) copy-start(s32[192]{0:T(256)S(1)} %add_reduce_fusion) | copy-start | bytes 2308
  28.3 10.0 %copy-start.40 = (bf16[128,1024]{1,0:T(8,128)(2,1)}, bf16[128,1024]{1,0:T(8,128)(2,1)S(1)}, u32[]{:S(2)}) copy-start(bf16[128,1024]{1,0:T(8,128)(2,1)S(1)} %convolution_convert_fusion.5) | copy-start | bytes 786436
  28.3 6.4 %collective-permute-start.1 = (bf16[128,1024]{1,0:T(8,128)(2,1)S(1)}, bf16[128,1024]{1,0:T(8,128)(2,1)S(1)}, u32[]{:S(2)}, u32[]{:S(2)}) collective-permute-start(bf16[128,1024]{1,0:T(8,128)(2,1)S(1)} %convolution_convert_fusion.5), channel_id=1, source_target_pairs={{0,2},{1,3},{2,0},{3,1},{4,6},{5,7},{6,4},{7,5},{8,10},{9,11},{10,... | collective-permute-start | bytes 786440 | tf_op jit(solution)/shard_map/ppermute | solution.py:42
  29.9 4.9 %collective-permute-start = (bf16[128,1024]{1,0:T(8,128)(2,1)S(1)}, bf16[128,1024]{1,0:T(8,128)(2,1)S(1)}, u32[]{:S(2)}, u32[]{:S(2)}) collective-permute-start(bf16[128,1024]{1,0:T(8,128)(2,1)S(1)} %convolution_convert_fusion.5), channel_id=1, source_target_pairs={{0,1},{1,0},{2,3},{3,2},{4,5},{5,4},{6,7},{7,6},{8,9},{9,8},{10,11... | collective-permute-start | bytes 786440 | tf_op jit(solution)/shard_map/ppermute | solution.py:37
  32.0 6.3 %copy-start.17 = (bf16[2,1024,1024]{2,1,0:T(8,128)(2,1)S(1)}, bf16[2,1024,1024]{2,1,0:T(8,128)(2,1)}, u32[]{:S(2)}) copy-start(bf16[2,1024,1024]{2,1,0:T(8,128)(2,1)} %param.30) | copy-start | bytes 12582916
  34.7 7.7 %copy-start.65 = (bf16[128,1024]{1,0:T(8,128)(2,1)}, bf16[128,1024]{1,0:T(8,128)(2,1)S(1)}, u32[]{:S(2)}) copy-start(bf16[128,1024]{1,0:T(8,128)(2,1)S(1)} %collective-permute-done.1) | copy-start | bytes 786436
  34.7 7.7 %collective-permute-start.2 = (bf16[128,1024]{1,0:T(8,128)(2,1)S(1)}, bf16[128,1024]{1,0:T(8,128)(2,1)S(1)}, u32[]{:S(2)}, u32[]{:S(2)}) collective-permute-start(bf16[128,1024]{1,0:T(8,128)(2,1)S(1)} %collective-permute-done.1), channel_id=1, source_target_pairs={{0,1},{1,0},{2,3},{3,2},{4,5},{5,4},{6,7},{7,6},{8,9},{9,8},{10,11... | collective-permute-start | bytes 786440 | tf_op jit(solution)/shard_map/ppermute | solution.py:37
  34.7 3.5 %copy-start.66 = (bf16[128,1024]{1,0:T(8,128)(2,1)}, bf16[128,1024]{1,0:T(8,128)(2,1)S(1)}, u32[]{:S(2)}) copy-start(bf16[128,1024]{1,0:T(8,128)(2,1)S(1)} %collective-permute-done) | copy-start | bytes 786436
  53.4 4.1 %copy-start.8 = (bf16[1,512,256]{1,2,0:T(8,128)(2,1)S(1)}, bf16[1,512,256]{1,2,0:T(8,128)(2,1)}, u32[]{:S(2)}) copy-start(bf16[1,512,256]{1,2,0:T(8,128)(2,1)} %copy.46) | copy-start | bytes 786436
  65.6 1.5 collective-permute-start.3
  66.4 10.7 %copy-start.11 = (bf16[256,1024]{1,0:T(8,128)(2,1)S(1)}, bf16[256,1024]{1,0:T(8,128)(2,1)}, u32[]{:S(2)}) copy-start(bf16[256,1024]{1,0:T(8,128)(2,1)} %copy-done.10) | copy-start | bytes 1572868
  68.4 11.1 %copy-start.64 = (bf16[2,1024,512]{2,1,0:T(8,128)(2,1)S(1)}, bf16[2,1024,512]{2,1,0:T(8,128)(2,1)}, u32[]{:S(2)}) copy-start(bf16[2,1024,512]{2,1,0:T(8,128)(2,1)} %param.33) | copy-start | bytes 6291460
  68.5 8.6 %collective-permute-start.5 = (bf16[128,1024]{1,0:T(8,128)(2,1)S(1)}, bf16[128,1024]{1,0:T(8,128)(2,1)S(1)}, u32[]{:S(2)}, u32[]{:S(2)}) collective-permute-start(bf16[128,1024]{1,0:T(8,128)(2,1)S(1)} %slice.645), channel_id=1, source_target_pairs={{0,2},{1,3},{2,0},{3,1},{4,6},{5,7},{6,4},{7,5},{8,10},{9,11},{10,... | collective-permute-start | bytes 786440 | tf_op jit(solution)/shard_map/ppermute | solution.py:42
  78.0 7.8 %collective-permute-start.8 = (bf16[128,1024]{1,0:T(8,128)(2,1)S(1)}, bf16[128,1024]{1,0:T(8,128)(2,1)S(1)}, u32[]{:S(2)}, u32[]{:S(2)}) collective-permute-start(bf16[128,1024]{1,0:T(8,128)(2,1)S(1)} %fusion.90), channel_id=1, source_target_pairs={{0,2},{1,3},{2,0},{3,1},{4,6},{5,7},{6,4},{7,5},{8,10},{9,11},{10,... | collective-permute-start | bytes 786440 | tf_op jit(solution)/shard_map/ppermute | solution.py:42
  81.4 5.0 %copy-start.44 = (f32[128,512]{1,0:T(8,128)S(1)}, f32[128,512]{1,0:T(8,128)}, u32[]{:S(2)}) copy-start(f32[128,512]{1,0:T(8,128)} %fusion.280) | copy-start | bytes 786436
  89.3 5.2 %copy-start.13 = (f32[128,512]{1,0:T(8,128)}, f32[128,512]{1,0:T(8,128)S(1)}, u32[]{:S(2)}) copy-start(f32[128,512]{1,0:T(8,128)S(1)} %fusion.91) | copy-start | bytes 786436
  94.4 6.9 %collective-permute-start.11 = (bf16[128,1024]{1,0:T(8,128)(2,1)S(1)}, bf16[128,1024]{1,0:T(8,128)(2,1)S(1)}, u32[]{:S(2)}, u32[]{:S(2)}) collective-permute-start(bf16[128,1024]{1,0:T(8,128)(2,1)S(1)} %fusion.30), channel_id=1, source_target_pairs={{0,2},{1,3},{2,0},{3,1},{4,6},{5,7},{6,4},{7,5},{8,10},{9,11},{10,... | collective-permute-start | bytes 786440 | tf_op jit(solution)/shard_map/ppermute | solution.py:42
  97.6 5.9 %copy-start.29 = (f32[128,512]{1,0:T(8,128)}, f32[128,512]{1,0:T(8,128)S(1)}, u32[]{:S(2)}) copy-start(f32[128,512]{1,0:T(8,128)S(1)} %fusion.92) | copy-start | bytes 786436
  100.9 3.6 %copy-start.31 = (f32[128,512]{1,0:T(8,128)}, f32[128,512]{1,0:T(8,128)S(1)}, u32[]{:S(2)}) copy-start(f32[128,512]{1,0:T(8,128)S(1)} %fusion.96) | copy-start | bytes 786436
  100.9 10.2 %copy-start.18 = (bf16[2,1024,1024]{2,1,0:T(8,128)(2,1)S(1)}, bf16[2,1024,1024]{2,1,0:T(8,128)(2,1)}, u32[]{:S(2)}) copy-start(bf16[2,1024,1024]{2,1,0:T(8,128)(2,1)} %param.30) | copy-start | bytes 12582916
  104.5 6.7 %collective-permute-start.13 = (bf16[128,1024]{1,0:T(8,128)(2,1)}, bf16[128,1024]{1,0:T(8,128)(2,1)}, u32[]{:S(2)}, u32[]{:S(2)}) collective-permute-start(bf16[128,1024]{1,0:T(8,128)(2,1)} %fusion.116), channel_id=1, source_target_pairs={{0,2},{1,3},{2,0},{3,1},{4,6},{5,7},{6,4},{7,5},{8,10},{9,11},{10,... | collective-permute-start | bytes 786440 | tf_op jit(solution)/shard_map/ppermute | solution.py:42
  105.7 8.7 %collective-permute-start.12 = (bf16[128,1024]{1,0:T(8,128)(2,1)}, bf16[128,1024]{1,0:T(8,128)(2,1)}, u32[]{:S(2)}, u32[]{:S(2)}) collective-permute-start(bf16[128,1024]{1,0:T(8,128)(2,1)} %fusion.116), channel_id=1, source_target_pairs={{0,1},{1,0},{2,3},{3,2},{4,5},{5,4},{6,7},{7,6},{8,9},{9,8},{10,11... | collective-permute-start | bytes 786440 | tf_op jit(solution)/shard_map/ppermute | solution.py:37
  111.2 3.2 %collective-permute-start.14 = (bf16[128,1024]{1,0:T(8,128)(2,1)}, bf16[128,1024]{1,0:T(8,128)(2,1)}, u32[]{:S(2)}, u32[]{:S(2)}) collective-permute-start(bf16[128,1024]{1,0:T(8,128)(2,1)} %collective-permute-done.13), channel_id=1, source_target_pairs={{0,1},{1,0},{2,3},{3,2},{4,5},{5,4},{6,7},{7,6},{8,9},{9,8},{10,11... | collective-permute-start | bytes 786440 | tf_op jit(solution)/shard_map/ppermute | solution.py:37
  120.1 4.2 %copy-start.33 = (bf16[512,256]{0,1:T(8,128)(2,1)S(1)}, bf16[512,256]{0,1:T(8,128)(2,1)}, u32[]{:S(2)}) copy-start(bf16[512,256]{0,1:T(8,128)(2,1)} %copy.49) | copy-start | bytes 786436
  120.1 5.0 %copy-start.9 = (bf16[1,512,256]{1,2,0:T(8,128)(2,1)S(1)}, bf16[1,512,256]{1,2,0:T(8,128)(2,1)}, u32[]{:S(2)}) copy-start(bf16[1,512,256]{1,2,0:T(8,128)(2,1)} %copy.46) | copy-start | bytes 786436
  120.1 5.0 %copy-start.55 = (pred[128,256]{1,0:T(8,128)(4,1)S(1)}, pred[128,256]{1,0:T(8,128)(4,1)}, u32[]{:S(2)}) copy-start(pred[128,256]{1,0:T(8,128)(4,1)} %compare_and_fusion.2) | copy-start | bytes 98308
  120.1 5.0 %copy-start.73 = (f32[4,128,256]{2,1,0:T(8,128)S(1)}, f32[4,128,256]{2,1,0:T(8,128)}, u32[]{:S(2)}) copy-start(f32[4,128,256]{2,1,0:T(8,128)} %get-tuple-element.151) | copy-start | bytes 1572868
  121.4 4.0 %copy-start.7 = (bf16[1,512,256]{1,2,0:T(8,128)(2,1)S(1)}, bf16[1,512,256]{1,2,0:T(8,128)(2,1)}, u32[]{:S(2)}) copy-start(bf16[1,512,256]{1,2,0:T(8,128)(2,1)} %copy.45) | copy-start | bytes 786436
  129.8 6.0 %copy-start.38 = (f32[4,128,64]{1,2,0:T(8,128)S(1)}, f32[4,128,64]{1,2,0:T(8,128)}, u32[]{:S(2)}) copy-start(f32[4,128,64]{1,2,0:T(8,128)} %fusion.216) | copy-start | bytes 393220
  144.5 2.6 %collective-permute-start.15 = (bf16[256,1024]{1,0:T(8,128)(2,1)S(1)}, bf16[256,1024]{1,0:T(8,128)(2,1)S(1)}, u32[]{:S(2)}, u32[]{:S(2)}) collective-permute-start(bf16[256,1024]{1,0:T(8,128)(2,1)S(1)} %pad_maximum_fusion.5), channel_id=1, source_target_pairs={{0,1},{1,0},{2,3},{3,2},{4,5},{5,4},{6,7},{7,6},{8,9},{9,8},{10,11... | collective-permute-start | bytes 1572872 | tf_op jit(solution)/shard_map/ppermute | solution.py:37
  147.2 9.3 %copy-start.12 = (bf16[256,1024]{1,0:T(8,128)(2,1)S(1)}, bf16[256,1024]{1,0:T(8,128)(2,1)}, u32[]{:S(2)}) copy-start(bf16[256,1024]{1,0:T(8,128)(2,1)} %copy-done.10) | copy-start | bytes 1572868
  147.3 9.2 %collective-permute-start.16 = (bf16[128,1024]{1,0:T(8,128)(2,1)S(1)}, bf16[128,1024]{1,0:T(8,128)(2,1)S(1)}, u32[]{:S(2)}, u32[]{:S(2)}) collective-permute-start(bf16[128,1024]{1,0:T(8,128)(2,1)S(1)} %fusion.131), channel_id=1, source_target_pairs={{0,2},{1,3},{2,0},{3,1},{4,6},{5,7},{6,4},{7,5},{8,10},{9,11},{10,... | collective-permute-start | bytes 786440 | tf_op jit(solution)/shard_map/ppermute | solution.py:42
  150.2 9.9 %copy-start.46 = (f32[128,512]{1,0:T(8,128)S(1)}, f32[128,512]{1,0:T(8,128)}, u32[]{:S(2)}) copy-start(f32[128,512]{1,0:T(8,128)} %copy-done.45) | copy-start | bytes 786436
  150.2 9.9 %copy-start.48 = (f32[128,512]{1,0:T(8,128)S(1)}, f32[128,512]{1,0:T(8,128)}, u32[]{:S(2)}) copy-start(f32[128,512]{1,0:T(8,128)} %copy-done.47) | copy-start | bytes 786436
  150.2 16.7 %collective-permute-start.9 = (bf16[128,1024]{1,0:T(8,128)(2,1)S(1)}, bf16[128,1024]{1,0:T(8,128)(2,1)S(1)}, u32[]{:S(2)}, u32[]{:S(2)}) collective-permute-start(bf16[128,1024]{1,0:T(8,128)(2,1)S(1)} %fusion.32), channel_id=1, source_target_pairs={{0,2},{1,3},{2,0},{3,1},{4,6},{5,7},{6,4},{7,5},{8,10},{9,11},{10,... | collective-permute-start | bytes 786440 | tf_op jit(solution)/shard_map/ppermute | solution.py:42
  156.8 10.2 %copy-start.30 = (f32[128,512]{1,0:T(8,128)S(1)}, f32[128,512]{1,0:T(8,128)}, u32[]{:S(2)}) copy-start(f32[128,512]{1,0:T(8,128)} %copy-done.29) | copy-start | bytes 786436
  156.8 10.2 %copy-start.32 = (f32[128,512]{1,0:T(8,128)S(1)}, f32[128,512]{1,0:T(8,128)}, u32[]{:S(2)}) copy-start(f32[128,512]{1,0:T(8,128)} %copy-done.31) | copy-start | bytes 786436
  158.8 10.4 %copy-start.59 = (s32[192]{0:T(256)S(1)}, s32[192]{0:T(256)}, u32[]{:S(2)}) copy-start(s32[192]{0:T(256)} %copy-done.58) | copy-start | bytes 2308
  158.8 8.1 %collective-permute-start.18 = (bf16[128,1024]{1,0:T(8,128)(2,1)}, bf16[128,1024]{1,0:T(8,128)(2,1)}, u32[]{:S(2)}, u32[]{:S(2)}) collective-permute-start(bf16[128,1024]{1,0:T(8,128)(2,1)} %fusion.111), channel_id=1, source_target_pairs={{0,2},{1,3},{2,0},{3,1},{4,6},{5,7},{6,4},{7,5},{8,10},{9,11},{10,... | collective-permute-start | bytes 786440 | tf_op jit(solution)/shard_map/ppermute | solution.py:42
  160.4 14.6 %copy-start.41 = (bf16[128,1024]{1,0:T(8,128)(2,1)S(1)}, bf16[128,1024]{1,0:T(8,128)(2,1)}, u32[]{:S(2)}) copy-start(bf16[128,1024]{1,0:T(8,128)(2,1)} %copy-done.40) | copy-start | bytes 786436
  160.4 14.6 %copy-start.42 = (f32[256,256]{1,0:T(8,128)S(1)}, f32[256,256]{1,0:T(8,128)}, u32[]{:S(2)}) copy-start(f32[256,256]{1,0:T(8,128)} %constant_dynamic-slice_fusion.1) | copy-start | bytes 786436
  160.4 14.6 %collective-permute-start.17 = (bf16[128,1024]{1,0:T(8,128)(2,1)}, bf16[128,1024]{1,0:T(8,128)(2,1)}, u32[]{:S(2)}, u32[]{:S(2)}) collective-permute-start(bf16[128,1024]{1,0:T(8,128)(2,1)} %fusion.111), channel_id=1, source_target_pairs={{0,1},{1,0},{2,3},{3,2},{4,5},{5,4},{6,7},{7,6},{8,9},{9,8},{10,11... | collective-permute-start | bytes 786440 | tf_op jit(solution)/shard_map/ppermute | solution.py:37
  166.9 8.0 %collective-permute-start.19 = (bf16[128,1024]{1,0:T(8,128)(2,1)}, bf16[128,1024]{1,0:T(8,128)(2,1)}, u32[]{:S(2)}, u32[]{:S(2)}) collective-permute-start(bf16[128,1024]{1,0:T(8,128)(2,1)} %collective-permute-done.18), channel_id=1, source_target_pairs={{0,1},{1,0},{2,3},{3,2},{4,5},{5,4},{6,7},{7,6},{8,9},{9,8},{10,11... | collective-permute-start | bytes 786440 | tf_op jit(solution)/shard_map/ppermute | solution.py:37
  171.3 17.0 %all-to-all-start.1 = ((bf16[8,24,1024]{2,1,0:T(8,128)(2,1)}), bf16[8,24,1024]{2,1,0:T(8,128)(2,1)S(1)}, u32[]{:S(2)}, u32[]{:S(2)}) async-start(bf16[8,24,1024]{2,1,0:T(8,128)(2,1)} %bitcast.62), calls=%async_computation.1 | async-start | bytes 786432 | tf_op jit(solution)/shard_map/all_to_all | solution.py:275
  179.0 5.1 %copy-start.69 = (bf16[256,1024]{1,0:T(8,128)(2,1)S(1)}, bf16[256,1024]{1,0:T(8,128)(2,1)}, u32[]{:S(2)}) copy-start(bf16[256,1024]{1,0:T(8,128)(2,1)} %copy-done.68) | copy-start | bytes 1572868
  179.0 5.1 %copy-start.71 = (bf16[256,1024]{1,0:T(8,128)(2,1)S(1)}, bf16[256,1024]{1,0:T(8,128)(2,1)}, u32[]{:S(2)}) copy-start(bf16[256,1024]{1,0:T(8,128)(2,1)} %copy-done.70) | copy-start | bytes 1572868
  180.8 11.1 %collective-permute-start.20 = (bf16[512,256]{1,0:T(8,128)(2,1)}, bf16[512,256]{1,0:T(8,128)(2,1)S(1)}, u32[]{:S(2)}, u32[]{:S(2)}) collective-permute-start(bf16[512,256]{1,0:T(8,128)(2,1)} %fusion.158), channel_id=1, source_target_pairs={{0,16},{16,0},{1,17},{17,1},{2,18},{18,2},{3,19},{19,3},{4,20},{20... | collective-permute-start | bytes 786440 | tf_op jit(solution)/shard_map/ppermute | solution.py:68
  184.1 4.1 %copy-start.62 = (s32[128]{0:T(128)S(1)}, s32[128]{0:T(128)}, u32[]{:S(2)}) copy-start(s32[128]{0:T(128)} %copy-done.61) | copy-start | bytes 1540
  185.6 11.9 %collective-permute-start.24 = (bf16[512,256]{1,0:T(8,128)(2,1)S(1)}, bf16[512,256]{1,0:T(8,128)(2,1)S(1)}, u32[]{:S(2)}, u32[]{:S(2)}) collective-permute-start(bf16[512,256]{1,0:T(8,128)(2,1)S(1)} %fusion.159), channel_id=1, source_target_pairs={{0,16},{16,0},{1,17},{17,1},{2,18},{18,2},{3,19},{19,3},{4,20},{20... | collective-permute-start | bytes 786440 | tf_op jit(solution)/shard_map/ppermute | solution.py:68
  188.3 9.3 %copy-start.35 = (f32[1024,256]{1,0:T(8,128)S(1)}, f32[1024,256]{1,0:T(8,128)}, u32[]{:S(2)}) copy-start(f32[1024,256]{1,0:T(8,128)} %copy-done.34) | copy-start | bytes 3145732
  193.1 6.4 %collective-permute-start.21 = (bf16[128,256]{1,0:T(8,128)(2,1)S(1)}, bf16[128,256]{1,0:T(8,128)(2,1)S(1)}, u32[]{:S(2)}, u32[]{:S(2)}) collective-permute-start(bf16[128,256]{1,0:T(8,128)(2,1)S(1)} %get-tuple-element.116), channel_id=1, source_target_pairs={{0,4},{4,8},{8,12},{12,0},{1,5},{5,9},{9,13},{13,1},{2,6},{6,10},{... | collective-permute-start | bytes 196616 | tf_op jit(solution)/shard_map/ppermute | solution.py:68
  193.4 8.7 %collective-permute-start.22 = (bf16[128,256]{1,0:T(8,128)(2,1)S(1)}, bf16[128,256]{1,0:T(8,128)(2,1)S(1)}, u32[]{:S(2)}, u32[]{:S(2)}) collective-permute-start(bf16[128,256]{1,0:T(8,128)(2,1)S(1)} %get-tuple-element.118), channel_id=1, source_target_pairs={{0,8},{4,12},{8,0},{12,4},{1,9},{5,13},{9,1},{13,5},{2,10},{6,14},... | collective-permute-start | bytes 196616 | tf_op jit(solution)/shard_map/ppermute | solution.py:68
  195.8 6.3 %collective-permute-start.23 = (bf16[128,256]{1,0:T(8,128)(2,1)S(1)}, bf16[128,256]{1,0:T(8,128)(2,1)S(1)}, u32[]{:S(2)}, u32[]{:S(2)}) collective-permute-start(bf16[128,256]{1,0:T(8,128)(2,1)S(1)} %get-tuple-element.117), channel_id=1, source_target_pairs={{0,12},{4,0},{8,4},{12,8},{1,13},{5,1},{9,5},{13,9},{2,14},{6,2},{... | collective-permute-start | bytes 196616 | tf_op jit(solution)/shard_map/ppermute | solution.py:68
  197.7 6.5 %collective-permute-start.25 = (bf16[128,256]{1,0:T(8,128)(2,1)S(1)}, bf16[128,256]{1,0:T(8,128)(2,1)S(1)}, u32[]{:S(2)}, u32[]{:S(2)}) collective-permute-start(bf16[128,256]{1,0:T(8,128)(2,1)S(1)} %get-tuple-element.119), channel_id=1, source_target_pairs={{0,4},{4,8},{8,12},{12,0},{1,5},{5,9},{9,13},{13,1},{2,6},{6,10},{... | collective-permute-start | bytes 196616 | tf_op jit(solution)/shard_map/ppermute | solution.py:68
  198.0 8.6 %collective-permute-start.26 = (bf16[128,256]{1,0:T(8,128)(2,1)S(1)}, bf16[128,256]{1,0:T(8,128)(2,1)S(1)}, u32[]{:S(2)}, u32[]{:S(2)}) collective-permute-start(bf16[128,256]{1,0:T(8,128)(2,1)S(1)} %get-tuple-element.121), channel_id=1, source_target_pairs={{0,8},{4,12},{8,0},{12,4},{1,9},{5,13},{9,1},{13,5},{2,10},{6,14},... | collective-permute-start | bytes 196616 | tf_op jit(solution)/shard_map/ppermute | solution.py:68
  199.5 7.0 %collective-permute-start.27 = (bf16[128,256]{1,0:T(8,128)(2,1)S(1)}, bf16[128,256]{1,0:T(8,128)(2,1)S(1)}, u32[]{:S(2)}, u32[]{:S(2)}) collective-permute-start(bf16[128,256]{1,0:T(8,128)(2,1)S(1)} %get-tuple-element.120), channel_id=1, source_target_pairs={{0,12},{4,0},{8,4},{12,8},{1,13},{5,1},{9,5},{13,9},{2,14},{6,2},{... | collective-permute-start | bytes 196616 | tf_op jit(solution)/shard_map/ppermute | solution.py:68
  (41 other events, 73.1 us)

commit v2 on v1

v2 whole, which is shorter than its diff:
```python
import functools

import jax
import jax.numpy as jnp
from jax import lax
from jax.experimental import pallas as pl
from jax.experimental.pallas import tpu as pltpu
from jax.sharding import PartitionSpec as P

D = 1024
HEADS = 16
HEAD = D // HEADS
EPS = 1e-06
F32 = jnp.float32
BF16 = jnp.bfloat16
MIB = 1 << 20
CHUNK = 256


def dot(left, right, dims=((1,), (0,))):
    return lax.dot_general(left, right, (dims, ((), ())), preferred_element_type=F32)


NT = ((1,), (1,))
TN = ((0,), (0,))


def bf16(value):
    return value.astype(BF16)


def silu_grad(value, sigma):
    return sigma * (1.0 + value * (1.0 - sigma))


def norm_factor(wide):
    return lax.rsqrt(jnp.mean(wide * wide, axis=-1, keepdims=True) + EPS)


def norm_back(grad, normed, factor):
    return factor * (grad - normed * jnp.mean(grad * normed, axis=-1, keepdims=True))


def turned(row, rows):
    return jnp.broadcast_to(row.astype(F32), (rows, rows)).T


def like(shape, dtype):
    return jax.ShapeDtypeStruct(shape, dtype)


def run(body, outs, scalars, args, weights=(), scratch=(), flops=0, moved=0, name=None):
    specs = []
    operands = []
    if scalars is not None:
        specs.append(pl.BlockSpec(memory_space=pltpu.SMEM))
        operands.append(scalars)
    specs += [pl.BlockSpec(memory_space=pltpu.VMEM)] * len(args)
    specs += [pl.BlockSpec(memory_space=pl.ANY)] * len(weights)
    operands += list(args) + list(weights)
    total = sum(a.size * a.dtype.itemsize for a in list(args) + list(weights) + list(outs))
    buffers = [pltpu.VMEM(w.shape, w.dtype) for w in weights]
    if weights:
        buffers.append(pltpu.SemaphoreType.DMA((16,)))
    return pl.pallas_call(
        body,
        out_shape=list(outs),
        in_specs=specs,
        out_specs=[pl.BlockSpec(memory_space=pltpu.VMEM)] * len(outs),
        scratch_shapes=buffers + list(scratch),
        compiler_params=pltpu.CompilerParams(vmem_limit_bytes=40 * MIB),
        cost_estimate=pl.CostEstimate(flops=flops, bytes_accessed=total, transcendentals=0),
        name=name,
    )(*operands)


def load(sources, targets, sems, cuts):
    started = []
    index = 0
    for source, target, pieces in zip(sources, targets, cuts):
        mine = []
        for piece in pieces:
            copy = pltpu.make_async_copy(source.at[piece], target.at[piece], sems.at[index])
            copy.start()
            mine.append(copy)
            index += 1
        started.append(mine)
    return started


def route_send(capacity, where, owner, slot, features, *outs):
    sends, place_ref = outs[:-1], outs[-1]
    groups = len(sends)
    rows, width = features.shape
    o_row = owner[...]
    o_col = turned(o_row, rows)
    i = lax.broadcasted_iota(jnp.int32, (rows, rows), 0)
    j = lax.broadcasted_iota(jnp.int32, (rows, rows), 1)
    earlier = jnp.where((o_col == o_row.astype(F32)) & (i < j), 1.0, 0.0)
    rank = jnp.sum(earlier, axis=0, keepdims=True).astype(jnp.int32)
    rel = o_row - where[0]
    rel = jnp.where(rel < 0, rel + groups, rel)
    place = rel * capacity + rank
    place_ref[...] = place
    spots = lax.broadcasted_iota(jnp.int32, (groups * capacity, rows), 0)
    hot = jnp.where(spots == place, 1.0, 0.0).astype(BF16)
    big = dot(hot, features[...])
    tags = dot(hot, bf16(turned(slot[...] + 1, rows)))
    for k in range(groups):
        part = slice(k * capacity, (k + 1) * capacity)
        sends[k][:, :width] = bf16(big[part])
        sends[k][:, width:] = bf16(tags[part])


def route_recv(*refs):
    gots, (rows_ref, hot_ref) = refs[:-2], refs[-2:]
    rows, width = rows_ref.shape
    got = jnp.concatenate([g[...].astype(F32) for g in gots], axis=0)
    lanes = lax.broadcasted_iota(jnp.int32, (got.shape[0], rows), 1) + 1
    hot = jnp.where(got[:, width:] == lanes.astype(F32), 1.0, 0.0).astype(BF16)
    hot_ref[...] = hot
    rows_ref[...] = bf16(dot(hot, bf16(got[:, :width]), TN))


def back_send(hot, d_packed, *sends):
    groups = len(sends)
    capacity = hot.shape[0] // groups
    big = dot(hot[...], d_packed[...])
    for k in range(groups):
        sends[k][...] = bf16(big[k * capacity : (k + 1) * capacity])


def back_recv(place, *refs):
    gots, out = refs[:-1], refs[-1]
    got = bf16(jnp.concatenate([g[...].astype(F32) for g in gots], axis=0))
    spots = lax.broadcasted_iota(jnp.int32, (got.shape[0], out.shape[0]), 0)
    hot = jnp.where(spots == place[...], 1.0, 0.0).astype(BF16)
    out[...] = bf16(dot(hot, got, TN))


def encode(where, rows, weights, loads, pre_all, pre_ref, act_ref, packed_ref, store):
    w0, w1, w_in = weights
    load0, load1, load_in = loads
    width = rows.shape[1]
    cols = pre_ref.shape[1]
    for n in range(width // CHUNK):
        part = slice(n * CHUNK, (n + 1) * CHUNK)
        load0[n].wait()
        pre = dot(rows, w0[:, part])
        pre_all[:, part] = pre
        act_ref[:, part] = bf16(pre * jax.nn.sigmoid(pre))
    pre_ref[...] = pre_all[:, pl.ds(pl.multiple_of(where[1] * cols, cols), cols)]
    act = act_ref[...]
    pieces = []
    for n in range(width // CHUNK):
        load1[n].wait()
        pieces.append(bf16(dot(act, w1[:, n * CHUNK : (n + 1) * CHUNK])))
    packed = jnp.concatenate(pieces, axis=1)
    if packed_ref is not None:
        packed_ref[...] = packed[: packed_ref.shape[0]]
    wide = packed.astype(F32)
    normed = bf16(wide * norm_factor(wide))
    for c in range(w_in.shape[0]):
        load_in[c].wait()
        store(c, bf16(dot(normed, w_in[c])))


def enc_cuts(width, comps):
    whole = slice(None)
    columns = [(whole, slice(n * CHUNK, (n + 1) * CHUNK)) for n in range(width // CHUNK)]
    return [
        [(0,) + c for c in columns],
        [(1,) + c for c in columns],
        [(c,) for c in range(comps)],
    ]


def start_encoder(enc, w_in, enc_v, w_in_v, sems):
    cuts = enc_cuts(enc.shape[2], w_in.shape[0])
    return load((enc, enc, w_in), (enc_v, enc_v, w_in_v), sems, cuts)


def encode_first(
    where, first, second, enc, w_in, pre_ref, act_ref, packed_ref, proj_ref, enc_v, w_in_v, sems, pre_all
):
    loads = start_encoder(enc, w_in, enc_v, w_in_v, sems)
    rows = jnp.concatenate([first[...], second[...]], axis=0)
    half = first.shape[0]

    def store(c, value):
        proj_ref[c, 0] = value[:half]
        proj_ref[c, 1] = value[half:]

    encode(
        where, rows, (enc_v.at[0], enc_v.at[1], w_in_v), loads, pre_all, pre_ref, act_ref, packed_ref, store
    )


def window(where, docs, r, rows):
    t = where[1]
    b = t ^ r
    ahead = jnp.where(b > 0, (b - 1) ^ t, r)
    doc_q = turned(docs[b], rows)
    doc_own = docs[b].astype(F32)
    doc_ahead = docs[jnp.maximum(b - 1, 0)].astype(F32)
    i = lax.broadcasted_iota(jnp.int32, (rows, rows), 0)
    j = lax.broadcasted_iota(jnp.int32, (rows, rows), 1)
    own = jnp.where((doc_q == doc_own) & (j <= i), 1.0, 0.0)
    prior = jnp.where(doc_q == doc_ahead, 1.0, 0.0) * jnp.where(b > 0, 1.0, 0.0)
    allowed = jnp.concatenate([prior, own], axis=1)
    root_inv = lax.rsqrt(jnp.sum(allowed, axis=1, keepdims=True))
    return ahead, allowed, root_inv


def head_masks(cols):
    lane = lax.broadcasted_iota(jnp.int32, (1, cols), 1) // HEAD
    return [jnp.where(lane == h, 1.0, 0.0) for h in range(cols // HEAD)]


def spread(value, masks):
    return jnp.concatenate([value * bf16(m) for m in masks], axis=0)


def collect(value, masks):
    rows = value.shape[0] // len(masks)
    total = None
    for h, m in enumerate(masks):
        part = value[h * rows : (h + 1) * rows] * m
        total = part if total is None else total + part
    return total


def attend_first(
    where, docs, third, fourth, proj_a, enc, w_in,
    pre_ref, act_ref, proj_ref, att_ref, give_ref, keep_ref,
    enc_v, w_in_v, sems, pre_all,
):
    loads = start_encoder(enc, w_in, enc_v, w_in_v, sems)
    rows = jnp.concatenate([third[...], fourth[...]], axis=0)
    half = third.shape[0]
    cols = proj_a.shape[-1]
    proj_ref[:, 0:2] = proj_a[...]

    def store(c, value):
        proj_ref[c, 2] = value[:half]
        proj_ref[c, 3] = value[half:]

    encode(where, rows, (enc_v.at[0], enc_v.at[1], w_in_v), loads, pre_all, pre_ref, act_ref, None, store)
    masks = head_masks(cols)
    for r, (target, place) in enumerate(((keep_ref, 1), (give_ref, 1), (keep_ref, 0), (give_ref, 0))):
        ahead, allowed, root_inv = window(where, docs, r, half)
        keys = jnp.concatenate([proj_ref[1, ahead], proj_ref[1, r]], axis=0)
        values = jnp.concatenate([proj_ref[2, ahead], proj_ref[2, r]], axis=0)
        many = jnp.concatenate([allowed] * len(masks), axis=0)
        scores = dot(spread(proj_ref[0, r], masks), keys, NT) * HEAD ** (-0.5)
        weights = bf16(scores * jax.nn.sigmoid(scores) * many)
        attended = collect(dot(weights, values), masks) * root_inv
        gate = proj_ref[3, r].astype(F32)
        att_ref[r] = attended
        target[place * half : (place + 1) * half, :] = bf16(attended * gate * jax.nn.sigmoid(gate))


def out_part(give_rows, half_index, keep, take, w_own, w_near):
    part = slice(half_index * give_rows, (half_index + 1) * give_rows)
    return dot(keep[part, :], w_own[...]) + dot(take[part, :], w_near[...])


def attn_out_far(keep, take, w_own, w_near, out):
    out[...] = bf16(out_part(out.shape[0], 0, keep, take, w_own, w_near))


def attn_out_own(keep, take, w_own, w_near, packed, out):
    out[...] = out_part(out.shape[0], 1, keep, take, w_own, w_near) + packed[...].astype(F32)


def residual(part, got, resid_ref, normed_ref):
    resid = bf16(part[...] + got[...].astype(F32))
    resid_ref[...] = resid
    wide = resid.astype(F32)
    normed_ref[...] = bf16(wide * norm_factor(wide))


def ffn(rows_ref, d_out_ref, in_a, in_b, out_a, out_b, hidden_ref, back_ref, in_av, in_bv, out_av, out_bv, sems):
    whole = (slice(None),)
    loads = load(
        (out_a, in_a, out_b, in_b), (out_av, in_av, out_bv, in_bv), sems,
        [[whole], [(0,), (1,)], [whole], [(0,), (1,)]],
    )
    rows = rows_ref[...]
    cotangent = d_out_ref[...]
    units = out_a.shape[0]
    back = None
    for index, (w_in, w_out) in enumerate(((in_av, out_av), (in_bv, out_bv))):
        load_out, load_in = loads[2 * index], loads[2 * index + 1]
        load_out[0].wait()
        load_in[0].wait()
        load_in[1].wait()
        for n in range(units // CHUNK):
            part = slice(n * CHUNK, (n + 1) * CHUNK)
            d_hidden = dot(cotangent, w_out[part, :], NT)
            gate = dot(rows, w_in[0, :, part])
            upper = dot(rows, w_in[1, :, part])
            sigma = jax.nn.sigmoid(gate)
            silu = gate * sigma
            hidden_ref[:, index * units + n * CHUNK : index * units + (n + 1) * CHUNK] = bf16(silu * upper)
            d_gate = bf16(d_hidden * upper * silu_grad(gate, sigma))
            d_upper = bf16(d_hidden * silu)
            term = dot(d_gate, w_in[0, :, part], NT) + dot(d_upper, w_in[1, :, part], NT)
            back = term if back is None else back + term
    back_ref[...] = back.astype(back_ref.dtype)


def ffn_out_far(hidden, w_a, w_b, out):
    units = w_a.shape[0]
    out[...] = bf16(dot(hidden[:, :units], w_a[...]) + dot(hidden[:, units:], w_b[...]))


def ffn_out_own(hidden, w_a, w_b, resid, got, out):
    units = w_a.shape[0]
    total = dot(hidden[:, :units], w_a[...]) + dot(hidden[:, units:], w_b[...])
    out[...] = bf16(resid[...].astype(F32) + total + got[...].astype(F32))


def resid_back(back, got, resid, d_out, out):
    wide = resid[...].astype(F32)
    factor = norm_factor(wide)
    grad = back[...] + got[...].astype(F32)
    out[...] = bf16(d_out[...].astype(F32) + norm_back(grad, wide * factor, factor))


def attend_back(where, docs, d_resid, r, proj_ref, att_ref, w_out, masks, d_q, d_k, d_v, d_g):
    half = d_resid.shape[0]
    scale = HEAD ** (-0.5)
    ahead, allowed, root_inv = window(where, docs, r, half)
    gate = proj_ref[3, r].astype(F32)
    sigma_g = jax.nn.sigmoid(gate)
    d_gated = dot(d_resid, w_out, NT)
    d_att = bf16(d_gated * (gate * sigma_g) * root_inv)
    d_g[r] = bf16(d_gated * att_ref[r] * silu_grad(gate, sigma_g))
    keys = jnp.concatenate([proj_ref[1, ahead], proj_ref[1, r]], axis=0)
    values = jnp.concatenate([proj_ref[2, ahead], proj_ref[2, r]], axis=0)
    many = jnp.concatenate([allowed] * len(masks), axis=0)
    query = spread(proj_ref[0, r], masks)
    d_att_m = spread(d_att, masks)
    scores = dot(query, keys, NT) * scale
    sigma = jax.nn.sigmoid(scores)
    weights = bf16(scores * sigma * many)
    d_weights = dot(d_att_m, values, NT)
    d_scores = bf16(d_weights * silu_grad(scores, sigma) * many)
    d_q[r] = bf16(collect(dot(d_scores, keys), masks) * scale)
    d_keys = dot(d_scores, query, TN) * scale
    d_values = dot(weights, d_att_m, TN)
    d_k[ahead] += d_keys[:half]
    d_k[r] += d_keys[half:]
    d_v[ahead] += d_values[:half]
    d_v[r] += d_values[half:]


def attn_back_first(where, docs, first, second, proj, att, w_out, d_q, d_k, d_v, d_g):
    masks = head_masks(w_out.shape[0])
    d_k[...] = jnp.zeros_like(d_k)
    d_v[...] = jnp.zeros_like(d_v)
    for r, rows in enumerate((first, second)):
        attend_back(where, docs, rows[...], r, proj, att, w_out[...], masks, d_q, d_k, d_v, d_g)


def attn_back_second(
    where, docs, third, fourth, proj, att, w_out, d_q_a, d_k_a, d_v_a, d_g_a, w_in,
    give_ref, keep_ref, w_in_v, sems, d_q, d_k, d_v, d_g,
):
    comps = w_in.shape[0]
    loads = load((w_in,), (w_in_v,), sems, [[(c,) for c in range(comps)]])[0]
    masks = head_masks(w_out.shape[0])
    half = third.shape[0]
    d_q[0:2] = d_q_a[...]
    d_g[0:2] = d_g_a[...]
    d_k[...] = d_k_a[...]
    d_v[...] = d_v_a[...]
    for r, rows in ((2, third), (3, fourth)):
        attend_back(where, docs, rows[...], r, proj, att, w_out[...], masks, d_q, d_k, d_v, d_g)
    for copy in loads:
        copy.wait()
    for first, second, target in ((3, 1, give_ref), (2, 0, keep_ref)):
        total = None
        for c, grads in enumerate((d_q, d_k, d_v, d_g)):
            left = jnp.concatenate([bf16(grads[first]), bf16(grads[second])], axis=0)
            term = dot(left, w_in_v[c], NT)
            total = term if total is None else total + term
        target[...] = total.astype(target.dtype)


def add_far(keep, take, out):
    half = out.shape[0]
    out[...] = bf16(keep[:half, :] + take[:half, :].astype(F32))


def packed_back(keep, take, got, packed, d_resid, out):
    half = out.shape[0]
    wide = packed[...].astype(F32)
    factor = norm_factor(wide)
    grad = keep[half:, :] + take[half:, :].astype(F32) + got[...].astype(F32)
    out[...] = bf16(d_resid[...].astype(F32) + norm_back(grad, wide * factor, factor))


def column_of(ref, index, cols):
    return ref[:, pl.ds(pl.multiple_of(index * cols, cols), cols)]


def enc_grads_first(where, cot_a, cot_b, act0_a, act0_b, act1, pre, w1_rows, part1, part0):
    cols = pre.shape[1]
    half = cot_a.shape[0]
    cot = jnp.concatenate([cot_a[...], cot_b[...]], axis=0)
    cot_cols = jnp.concatenate(
        [column_of(cot_a, where[1], cols), column_of(cot_b, where[1], cols)], axis=0
    )
    part1[...] = dot(act1[...], cot_cols, TN)
    value = pre[...]
    back = dot(cot, w1_rows[...], NT)
    cot0 = bf16(back * silu_grad(value, jax.nn.sigmoid(value)))
    act0 = jnp.concatenate([act0_a[...], act0_b[...]], axis=0)
    part0[...] = dot(act0, cot0, TN)


def split_events(where, part, total, keep, sends):
    count = len(sends) + 1
    total[...] = total[...] + part[...]
    size = keep.shape[0]
    for k in range(count):
        index = where[2] + k
        index = jnp.where(index >= count, index - count, index)
        rows = total[pl.ds(pl.multiple_of(index * size, size), size), :]
        if k == 0:
            keep[...] = rows
        else:
            sends[k - 1][...] = bf16(rows)


def enc_grad1_second(where, cot_a, cot_b, act1, part1, *rest):
    outs, total = rest[:-1], rest[-1]
    cols = part1.shape[1]
    cot_cols = jnp.concatenate(
        [column_of(cot_a, where[1], cols), column_of(cot_b, where[1], cols)], axis=0
    )
    total[...] = dot(act1[...], cot_cols, TN)
    split_events(where, part1, total, outs[0], outs[1:])


def enc_grad0_second(where, cot_a, cot_b, act0_a, act0_b, pre, w1_rows, part0, *rest):
    outs, total = rest[:-1], rest[-1]
    cot = jnp.concatenate([cot_a[...], cot_b[...]], axis=0)
    value = pre[...]
    back = dot(cot, w1_rows[...], NT)
    cot0 = bf16(back * silu_grad(value, jax.nn.sigmoid(value)))
    act0 = jnp.concatenate([act0_a[...], act0_b[...]], axis=0)
    total[...] = dot(act0, cot0, TN)
    split_events(where, part0, total, outs[0], outs[1:])


def split_packs(where, keep, *refs):
    packs = refs[-1]
    gots, outs, total = refs[: -1 - packs - 1], refs[-1 - packs - 1 : -2], refs[-2]
    value = keep[...]
    for got in gots:
        value = value + got[...].astype(F32)
    total[...] = value
    size = outs[0].shape[0]
    for k in range(packs):
        index = where[3] + k
        index = jnp.where(index >= packs, index - packs, index)
        rows = total[pl.ds(pl.multiple_of(index * size, size), size), :]
        outs[k][...] = rows.astype(outs[k].dtype)


def shards(
    features,
    dest_owner,
    dest_slot,
    doc_ids,
    enc_weight,
    attn_in,
    attn_out,
    ffn_in,
    ffn_out,
    out_grad,
):
    rows_dev, width = features.shape
    group_axes = ("event", "pack")
    groups = lax.axis_size(group_axes)
    events = lax.axis_size("event")
    packs = lax.axis_size("pack")
    tensors = lax.axis_size("tensor")
    cols = attn_in.shape[2]
    comps = attn_in.shape[0]
    units = ffn_out.shape[0]
    where = jnp.stack(
        [lax.axis_index(group_axes), lax.axis_index("tensor"), lax.axis_index("event"), lax.axis_index("pack")]
    ).astype(jnp.int32)
    d_out = out_grad[0]
    docs = doc_ids.reshape(tensors, 1, rows_dev)

    def near(value):
        return lax.ppermute(value, "tensor", [(i, i ^ 1) for i in range(tensors)])

    def far(value):
        return lax.ppermute(value, "tensor", [(i, i ^ 2) for i in range(tensors)])

    def shifted(value, axes, count, step):
        return lax.ppermute(value, axes, [(i, (i + step) % count) for i in range(count)])

    row_b = like((rows_dev, width), BF16)
    row_f = like((rows_dev, width), F32)

    mean_load = rows_dev // groups
    capacity = -(-(mean_load + mean_load // 2) // 8) * 8
    *sends, place = run(
        functools.partial(route_send, capacity),
        [like((capacity, width + rows_dev), BF16)] * groups + [like((1, rows_dev), jnp.int32)],
        where,
        [dest_owner.reshape(1, rows_dev), dest_slot.reshape(1, rows_dev), features],
        flops=2 * groups * capacity * rows_dev * width,
        name="route_send",
    )
    gots = [sends[0]] + [shifted(sends[k], group_axes, groups, k) for k in range(1, groups)]
    mine, hot = run(
        route_recv,
        [row_b, like((groups * capacity, rows_dev), BF16)],
        None,
        gots,
        flops=2 * groups * capacity * rows_dev * width,
        name="route_recv",
    )

    mine_near = near(mine)
    mine_far = far(mine)
    mine_both = near(mine_far)
    d_out_far = far(d_out)
    ffn_in_near = near(ffn_in)
    ffn_out_near = near(ffn_out)
    attn_out_near = near(attn_out)

    pair = 2 * rows_dev
    enc_flops = 2 * pair * width * (2 * width + comps * cols)
    pre_a, act_a, packed, proj_a = run(
        encode_first,
        [
            like((pair, cols), F32),
            like((pair, width), BF16),
            row_b,
            like((comps, 2, rows_dev, cols), BF16),
        ],
        where,
        [mine, mine_near],
        [enc_weight, attn_in],
        [pltpu.VMEM((pair, width), F32)],
        flops=enc_flops,
        name="encode_first",
    )
    pre_b, act_b, proj, attended, give, keep = run(
        attend_first,
        [
            like((pair, cols), F32),
            like((pair, width), BF16),
            like((comps, tensors, rows_dev, cols), BF16),
            like((tensors, rows_dev, cols), F32),
            like((pair, cols), BF16),
            like((pair, cols), BF16),
        ],
        where,
        [docs, mine_far, mine_both, proj_a],
        [enc_weight, attn_in],
        [pltpu.VMEM((pair, width), F32)],
        flops=2 * enc_flops,
        name="attend_first",
    )
    take = near(give)
    out_flops = 2 * rows_dev * width * 2 * cols
    (part_far,) = run(
        attn_out_far, [row_b], None, [keep, take, attn_out, attn_out_near], flops=out_flops, name="attn_out_far"
    )
    got_part = far(part_far)
    (part_own,) = run(
        attn_out_own, [row_f], None, [keep, take, attn_out, attn_out_near, packed], flops=out_flops, name="attn_out_own"
    )
    resid, normed2 = run(residual, [row_b, row_b], None, [part_own, got_part], name="residual")
    normed2_far = far(normed2)

    def feed(rows, cotangent, back_type, name):
        return run(
            ffn,
            [like((rows_dev, 2 * units), BF16), like((rows_dev, width), back_type)],
            None,
            [rows, cotangent],
            [ffn_in, ffn_in_near, ffn_out, ffn_out_near],
            flops=2 * rows_dev * width * 2 * units * 5,
            name=name,
        )

    hidden_own, back_own = feed(normed2, d_out, F32, "ffn_own")
    hidden_far, back_far = feed(normed2_far, d_out_far, BF16, "ffn_far")
    got_back = far(back_far)
    (d_resid,) = run(resid_back, [row_b], None, [back_own, got_back, resid, d_out], name="resid_back")
    ffn_flops = 2 * rows_dev * width * 2 * units
    (out_far,) = run(
        ffn_out_far, [row_b], None, [hidden_far, ffn_out, ffn_out_near], flops=ffn_flops, name="ffn_out_far"
    )
    got_out = far(out_far)
    (packed_out,) = run(
        ffn_out_own, [row_b], None, [hidden_own, ffn_out, ffn_out_near, resid, got_out], flops=ffn_flops, name="ffn_out_own"
    )

    d_resid_near = near(d_resid)
    d_resid_far = far(d_resid)
    d_resid_both = near(d_resid_far)
    att_flops = 2 * rows_dev * 2 * cols * (width + 6 * rows_dev * 4)
    block_f = like((tensors, rows_dev, cols), F32)
    two_b = like((2, rows_dev, cols), BF16)
    d_q, d_k, d_v, d_g = run(
        attn_back_first,
        [two_b, block_f, block_f, two_b],
        where,
        [docs, d_resid, d_resid_near, proj, attended, attn_out],
        flops=att_flops,
        name="attn_back_first",
    )
    four_b = pltpu.VMEM((tensors, rows_dev, cols), BF16)
    four_f = pltpu.VMEM((tensors, rows_dev, cols), F32)
    give, keep = run(
        attn_back_second,
        [like((pair, width), BF16), like((pair, width), F32)],
        where,
        [docs, d_resid_far, d_resid_both, proj, attended, attn_out, d_q, d_k, d_v, d_g],
        [attn_in],
        [four_b, four_f, four_f, four_b],
        flops=att_flops + 2 * 2 * pair * comps * cols * width,
        name="attn_back_second",
    )
    take = near(give)
    (sum_far,) = run(add_far, [row_b], None, [keep, take], name="add_far")
    got_sum = far(sum_far)
    (d_packed,) = run(packed_back, [row_b], None, [keep, take, got_sum, packed, d_resid], name="packed_back")

    cot_near = near(d_packed)
    cot_far = far(d_packed)
    cot_both = near(cot_far)
    w1_rows = lax.dynamic_slice_in_dim(enc_weight[1], lax.axis_index("tensor") * cols, cols, axis=0)
    grad_flops = 2 * pair * width * cols
    part_f = like((width, cols), F32)
    part1, part0 = run(
        enc_grads_first,
        [part_f, part_f],
        where,
        [d_packed, cot_near, mine, mine_near, act_a, pre_a, w1_rows],
        flops=3 * grad_flops,
        name="enc_grads_first",
    )
    event_rows = width // events
    event_outs = [like((event_rows, cols), F32)] + [like((event_rows, cols), BF16)] * (events - 1)
    total = [pltpu.VMEM((width, cols), F32)]
    keep1, *sends1 = run(
        enc_grad1_second, event_outs, where, [cot_far, cot_both, act_b, part1], (), total, flops=grad_flops, name="enc_grad1_second"
    )
    keep0, *sends0 = run(
        enc_grad0_second,
        event_outs,
        where,
        [cot_far, cot_both, mine_far, mine_both, pre_b, w1_rows, part0],
        (),
        total,
        flops=2 * grad_flops,
        name="enc_grad0_second",
    )
    pack_rows = event_rows // packs
    pack_outs = [like((pack_rows, cols), F32)] + [like((pack_rows, cols), BF16)] * (packs - 1)

    def over_events(keep, sends, name):
        gots = [shifted(s, "event", events, k + 1) for k, s in enumerate(sends)]
        return run(
            lambda *refs: split_packs(*refs, packs),
            pack_outs,
            where,
            [keep] + gots,
            (),
            [pltpu.VMEM((event_rows, cols), F32)],
            name=name,
        )

    keep1, *sends1 = over_events(keep1, sends1, "split_packs1")
    keep0, *sends0 = over_events(keep0, sends0, "split_packs0")
    gots1 = [shifted(s, "pack", packs, k + 1) for k, s in enumerate(sends1)]
    gots0 = [shifted(s, "pack", packs, k + 1) for k, s in enumerate(sends0)]

    backs = run(
        back_send,
        [like((capacity, width), BF16)] * groups,
        None,
        [hot, d_packed],
        flops=2 * groups * capacity * rows_dev * width,
        name="back_send",
    )
    returned = [backs[0]] + [
        shifted(backs[k], group_axes, groups, groups - k) for k in range(1, groups)
    ]
    (row_grad,) = run(
        back_recv,
        [row_b],
        None,
        [place] + returned,
        flops=2 * groups * capacity * rows_dev * width,
        name="back_recv",
    )

    def finish(refs, out):
        count = packs
        for layer in range(2):
            group = refs[layer * count : (layer + 1) * count]
            value = group[0][...]
            for got in group[1:]:
                value = value + got[...].astype(F32)
            out[layer] = value

    (enc_grad,) = run(
        lambda *refs: finish(refs[:-1], refs[-1]),
        [like((2, pack_rows, cols), F32)],
        None,
        [keep0] + gots0 + [keep1] + gots1,
        name="finish",
    )
    return (packed_out[None], row_grad, enc_grad)


def solution(mesh):
    placed = (
        P(("event", "pack", "tensor"), None),
        P(("event", "pack", "tensor")),
        P(("event", "pack", "tensor")),
        P(("event", "pack"), None),
        P(),
        P(None, None, "tensor"),
        P("tensor", None),
        P(None, None, "tensor"),
        P("tensor", None),
        P(("event", "pack"), "tensor", None),
    )
    return jax.shard_map(
        shards,
        mesh=mesh,
        in_specs=placed,
        out_specs=(
            P(("event", "pack"), "tensor", None),
            P(("event", "pack", "tensor"), None),
            P(None, ("event", "pack"), "tensor"),
        ),
        check_vma=False,
    )
```

time: 209 us -> 155 us (0.74)
  matrix products: 75 us -> 0 us
  Pallas kernels: 0 us -> 39.6 us
  other arithmetic: 19.4 us -> 0.08 us
  local copies, waits for them, and re-layouts: 28.5 us -> 11.4 us
  starting transfers between devices: 35.9 us -> 51.2 us
  waiting for transfers between devices: 46.5 us -> 51.5 us
    dot_general x64 -> x0, matrix products: 75 us -> none  [the longest x37 50.4 us: dot(): lax.dot_general(left, right, (dims, ((), ())), preferred_element_type=jnp...]
    pallas_call x0 -> x24, Pallas kernels: none -> 39.6 us  [run(): pl.pallas_call(body, out_shape=list(outs), in_specs=specs, out_specs=[pl....]
    ppermute x28 -> x42, starting transfers between devices: 24.9 us -> 51.2 us  [the longest x22 36.2 us: shifted(): lax.ppermute(value, axes, [(i, (i + step) % count) for i in range(count)])]
    ppermute x28 -> x42, waiting for transfers between devices: 38.2 us -> 51.5 us  [the longest x9 43.2 us: far(): return lax.ppermute(value, 'tensor', [(i, i ^ 2) for i in range(tensors)])]
    all_to_all x2 -> x0, starting transfers between devices: 10.9 us -> none  [the longest x1 7.25 us: shards(): lax.all_to_all(send, ('event', 'pack'), split_axis=0, concat_axis=0, tile...]
    convert_element_type x8 -> x0, local copies, waits for them, and re-layouts: 9.09 us -> none  [bf16(): return value.astype(jnp.bfloat16)]
    all_to_all x2 -> x0, waiting for transfers between devices: 8.27 us -> none  [the longest x1 5.62 us: shards(): lax.all_to_all(send, ('event', 'pack'), split_axis=0, concat_axis=0, tile...]
    convert_element_type x10 -> x0, other arithmetic: 7.5 us -> none  [the longest x9 7.39 us: bf16(): return value.astype(jnp.bfloat16)]
  transfers between devices with their start and end apart: 30 -> 42, of which waited for: 14 -> 18; matrix products, arithmetic and copies ran while one was open for 36% -> 2% of each run, Pallas kernels for 0% -> 19%
where the time goes in v2:
time: 155 us
  waiting for transfers between devices  51.5 us (33%)
  starting transfers between devices  51.2 us (33%)
  Pallas kernels  39.6 us (26%)
  local copies, waits for them, and re-layouts  11.4 us (7%)
    ppermute x9, waiting for transfers between devices, far(): return lax.ppermute(value, 'tensor', [(i, i ^ 2) for i in range(tensors)])  43.2 us
    pallas_call x24, Pallas kernels, run(): pl.pallas_call(body, out_shape=list(outs), in_specs=specs, out_specs=[pl....  39.6 us
    ppermute x22, starting transfers between devices, shifted(): lax.ppermute(value, axes, [(i, (i + step) % count) for i in range(count)])  36.2 us
    ppermute x9, starting transfers between devices, far(): return lax.ppermute(value, 'tensor', [(i, i ^ 2) for i in range(tensors)])  12.8 us
    unnamed x60, local copies, waits for them, and re-layouts  8.83 us
    ppermute x22, waiting for transfers between devices, shifted(): lax.ppermute(value, axes, [(i, (i + step) % count) for i in range(count)])  5.81 us
  transfers between devices with their start and end apart: 42, of which 18 were waited for; matrix products, arithmetic and copies ran while one was open for 2% of the time, Pallas kernels for 19%

profile of v2, /device:TPU:0, one launch (start us, length us, event | category | flops | bytes accessed | tf_op | source)
XLA Modules:
  0.0 154.9 jit_solution(11963165495943012666)
XLA Ops:
  1.2 0.9 copy-done.26
  2.2 0.7 copy-done.28
  2.8 0.7 copy-done.29
  3.5 0.9 route_send.1
  4.4 2.6 %collective-permute-start = (bf16[24,1152]{1,0:T(8,128)(2,1)S(1)}, bf16[24,1152]{1,0:T(8,128)(2,1)S(1)}, u32[]{:S(2)}, u32[]{:S(2)}) collective-permute-start(bf16[24,1152]{1,0:T(8,128)(2,1)S(1)} %get-tuple-element.59), channel_id=1, source_target_pairs={{0,4},{4,8},{8,12},{12,16},{16,20},{20,24},{24,28},{28,0},{1,5},{5... | collective-permute-start | bytes 165896 | tf_op jit(solution)/shard_map/ppermute | solution.py:508
  7.0 2.6 %collective-permute-start.1 = (bf16[24,1152]{1,0:T(8,128)(2,1)S(1)}, bf16[24,1152]{1,0:T(8,128)(2,1)S(1)}, u32[]{:S(2)}, u32[]{:S(2)}) collective-permute-start(bf16[24,1152]{1,0:T(8,128)(2,1)S(1)} %get-tuple-element.60), channel_id=1, source_target_pairs={{0,8},{4,12},{8,16},{12,20},{16,24},{20,28},{24,0},{28,4},{1,9},{5... | collective-permute-start | bytes 165896 | tf_op jit(solution)/shard_map/ppermute | solution.py:508
  9.6 2.3 %collective-permute-start.2 = (bf16[24,1152]{1,0:T(8,128)(2,1)S(1)}, bf16[24,1152]{1,0:T(8,128)(2,1)S(1)}, u32[]{:S(2)}, u32[]{:S(2)}) collective-permute-start(bf16[24,1152]{1,0:T(8,128)(2,1)S(1)} %get-tuple-element.61), channel_id=1, source_target_pairs={{0,12},{4,16},{8,20},{12,24},{16,28},{20,0},{24,4},{28,8},{1,13},{... | collective-permute-start | bytes 165896 | tf_op jit(solution)/shard_map/ppermute | solution.py:508
  12.6 1.4 collective-permute-start.4
  14.1 1.0 collective-permute-done.1.refs_2_
  15.0 0.9 collective-permute-start.5
  15.9 2.4 %collective-permute-start.6 = (bf16[24,1152]{1,0:T(8,128)(2,1)S(1)}, bf16[24,1152]{1,0:T(8,128)(2,1)S(1)}, u32[]{:S(2)}, u32[]{:S(2)}) collective-permute-start(bf16[24,1152]{1,0:T(8,128)(2,1)S(1)} %get-tuple-element.65), channel_id=1, source_target_pairs={{0,28},{4,0},{8,4},{12,8},{16,12},{20,16},{24,20},{28,24},{1,29},{... | collective-permute-start | bytes 165896 | tf_op jit(solution)/shard_map/ppermute | solution.py:508
  18.7 2.0 %collective-permute-done.5.refs_6_ = bf16[24,1152]{1,0:T(8,128)(2,1)S(1)} collective-permute-done((bf16[24,1152]{1,0:T(8,128)(2,1)S(1)}, bf16[24,1152]{1,0:T(8,128)(2,1)S(1)}, u32[]{:S(2)}, u32[]{:S(2)}) %collective-permute-start.5) | collective-permute-done | bytes 55328 | tf_op jit(solution)/shard_map/ppermute | solution.py:508
  21.2 1.6 %collective-permute-start.7 = (bf16[128,1024]{1,0:T(8,128)(2,1)S(1)}, bf16[128,1024]{1,0:T(8,128)(2,1)S(1)}, u32[]{:S(2)}, u32[]{:S(2)}) collective-permute-start(bf16[128,1024]{1,0:T(8,128)(2,1)S(1)} %get-tuple-element.66.first.act0_a), channel_id=1, source_target_pairs={{0,2},{1,3},{2,0},{3,1},{4,6},{5,7},{6,4},{7,5},{8,10},{9,11},{10,... | collective-permute-start | bytes 786440 | tf_op jit(solution)/shard_map/ppermute | solution.py:505
  22.8 5.9 %collective-permute-done.7.third.act0_a = bf16[128,1024]{1,0:T(8,128)(2,1)S(1)} collective-permute-done((bf16[128,1024]{1,0:T(8,128)(2,1)S(1)}, bf16[128,1024]{1,0:T(8,128)(2,1)S(1)}, u32[]{:S(2)}, u32[]{:S(2)}) %collective-permute-start.7) | collective-permute-done | bytes 262176 | tf_op jit(solution)/shard_map/ppermute | solution.py:505
  29.2 2.2 %copy-done.1 = bf16[2,1024,1024]{2,1,0:T(8,128)(2,1)S(1)} copy-done((bf16[2,1024,1024]{2,1,0:T(8,128)(2,1)S(1)}, bf16[2,1024,1024]{2,1,0:T(8,128)(2,1)}, u32[]{:S(2)}) %copy-start.1) | copy-done | bytes 4194328
  31.4 1.6 %copy-done.5 = bf16[4,1024,256]{2,1,0:T(8,128)(2,1)S(1)} copy-done((bf16[4,1024,256]{2,1,0:T(8,128)(2,1)S(1)}, bf16[4,1024,256]{2,1,0:T(8,128)(2,1)}, u32[]{:S(2)}) %copy-start.5) | copy-done | bytes 2097176
  33.0 6.7 %encode_first.1 = (f32[256,256]{1,0:T(8,128)S(1)}, bf16[256,1024]{1,0:T(8,128)(2,1)S(1)}, bf16[128,1024]{1,0:T(8,128)(2,1)S(1)}, bf16[4,2,128,256]{3,2,1,0:T(8,128)(2,1)S(1)}) custom-call(s32[4]{0:T(128)S(1)} %pad_add_fusion.where.refs_0_, bf16[128,1024]{1,0:T(8,128)(2,1)S(1)} %get-tuple-element.66.first.act0_a, ...), custom_call_target="tpu_custom_call" | custom-call | flops 1610612736 | bytes 8388608 | tf_op jit(solution)/shard_map/encode_first/pallas_call | solution.py:65
  39.8 0.7 copy-done.22
  40.5 7.8 %attend_first.1 = (f32[256,256]{1,0:T(8,128)S(1)}, bf16[256,1024]{1,0:T(8,128)(2,1)S(1)}, bf16[4,4,128,256]{3,2,1,0:T(8,128)(2,1)S(1)}, f32[4,128,256]{2,1,0:T(8...) custom-call(s32[4]{0:T(128)S(1)} %pad_add_fusion.where.refs_0_, s32[4,1,128]{2,1,0:T(1,128)S(1)} %bitcast.14, ...), custom_call_target="tpu_custom_call" | custom-call | flops 3221225472 | bytes 9963520 | tf_op jit(solution)/shard_map/attend_first/pallas_call | solution.py:65
  49.0 1.0 collective-permute-done.10.take
  50.3 1.5 collective-permute-start.12
  52.7 6.8 %collective-permute-done.12.got = bf16[128,1024]{1,0:T(8,128)(2,1)S(1)} collective-permute-done((bf16[128,1024]{1,0:T(8,128)(2,1)S(1)}, bf16[128,1024]{1,0:T(8,128)(2,1)S(1)}, u32[]{:S(2)}, u32[]{:S(2)}) %collective-permute-start.12) | collective-permute-done | bytes 262176 | tf_op jit(solution)/shard_map/ppermute | solution.py:505
  59.7 1.5 collective-permute-start.15
  61.2 3.9 %collective-permute-done.16.d_out_ref = bf16[128,1024]{1,0:T(8,128)(2,1)S(1)} collective-permute-done((bf16[128,1024]{1,0:T(8,128)(2,1)S(1)}, bf16[128,1024]{1,0:T(8,128)(2,1)S(1)}, u32[]{:S(2)}, u32[]{:S(2)}) %collective-permute-start.16) | collective-permute-done | bytes 262176 | tf_op jit(solution)/shard_map/ppermute | solution.py:505
  65.1 5.0 %collective-permute-done.15.rows_ref = bf16[128,1024]{1,0:T(8,128)(2,1)S(1)} collective-permute-done((bf16[128,1024]{1,0:T(8,128)(2,1)S(1)}, bf16[128,1024]{1,0:T(8,128)(2,1)S(1)}, u32[]{:S(2)}, u32[]{:S(2)}) %collective-permute-start.15) | collective-permute-done | bytes 262176 | tf_op jit(solution)/shard_map/ppermute | solution.py:505
  70.2 3.5 %ffn_far.1 = (bf16[128,1024]{1,0:T(8,128)(2,1)S(1)}, bf16[128,1024]{1,0:T(8,128)(2,1)S(1)}) custom-call(bf16[128,1024]{1,0:T(8,128)(2,1)S(1)} %collective-permute-done.15.rows_ref, bf16[128,1024]{1,0:T(8,128)(2,1)S(1)} %collective-permute-done.16.d_out_ref, bf16[2,1024,512]{2,1,0:T(8,128)(2,1)S(1)} %copy-done.4, ...), custom_call_target="tpu_custom_call" | custom-call | flops 1342177280 | bytes 7340032 | tf_op jit(solution)/shard_map/ffn_far/pallas_call | solution.py:65
  73.6 1.5 collective-permute-start.18
  75.1 3.6 %ffn_own.1 = (bf16[128,1024]{1,0:T(8,128)(2,1)S(1)}, f32[128,1024]{1,0:T(8,128)S(1)}) custom-call(bf16[128,1024]{1,0:T(8,128)(2,1)S(1)} %get-tuple-element.71.rows_ref, bf16[128,1024]{1,0:T(8,128)(2,1)S(1)} %bitcast.12, bf16[2,1024,512]{2,1,0:T(8,128)(2,1)S(1)} %copy-done.4, bf16[2,1024,512]{2,1,0:T(8,128)(2,1)} %collective-permute-done.13.in_b, ...), custom_call_target="tpu_custom_call" | custom-call | flops 1342177280 | bytes 7602176 | tf_op jit(solution)/shard_map/ffn_own/pallas_call | solution.py:65
  78.8 2.7 %collective-permute-done.18.got = bf16[128,1024]{1,0:T(8,128)(2,1)S(1)} collective-permute-done((bf16[128,1024]{1,0:T(8,128)(2,1)S(1)}, bf16[128,1024]{1,0:T(8,128)(2,1)S(1)}, u32[]{:S(2)}, u32[]{:S(2)}) %collective-permute-start.18) | collective-permute-done | bytes 262176 | tf_op jit(solution)/shard_map/ppermute | solution.py:505
  81.8 1.5 collective-permute-start.19
  83.3 5.4 %collective-permute-done.19.third = bf16[128,1024]{1,0:T(8,128)(2,1)S(1)} collective-permute-done((bf16[128,1024]{1,0:T(8,128)(2,1)S(1)}, bf16[128,1024]{1,0:T(8,128)(2,1)S(1)}, u32[]{:S(2)}, u32[]{:S(2)}) %collective-permute-start.19) | collective-permute-done | bytes 262176 | tf_op jit(solution)/shard_map/ppermute | solution.py:505
  88.7 2.3 %attn_back_first.1 = (bf16[2,128,256]{2,1,0:T(8,128)(2,1)S(1)}, f32[4,128,256]{2,1,0:T(8,128)S(1)}, f32[4,128,256]{2,1,0:T(8,128)S(1)}, bf16[2,128,256]{2,1,0:T(8,128)(2,1)S(1)}) custom-call(s32[4]{0:T(128)S(1)} %pad_add_fusion.where.refs_0_, s32[4,1,128]{2,1,0:T(1,128)S(1)} %bitcast.15, bf16[128,1024]{1,0:T(8,128)(2,1)S(1)} %resid_back.1.first.d_resid, ...), custom_call_target="tpu_custom_call" | custom-call | flops 536870912 | bytes 3934208 | tf_op jit(solution)/shard_map/attn_back_first/pallas_call | solution.py:65
  91.0 3.9 %attn_back_second.1 = (bf16[256,1024]{1,0:T(8,128)(2,1)S(1)}, f32[256,1024]{1,0:T(8,128)S(1)}) custom-call(s32[4]{0:T(128)S(1)} %pad_add_fusion.where.refs_0_, s32[4,1,128]{2,1,0:T(1,128)S(1)} %bitcast.16, bf16[128,1024]{1,0:T(8,128)(2,1)S(1)} %collective-permute-done.19.third, bf16[128,1024]{1,0:T(8,128)(2,1)S(1)} %collective-permute-done.20.fourth, ...), custom_call_target="tpu_custom_call" | custom-call | flops 1610612736 | bytes 7604224 | tf_op jit(solution)/shard_map/attn_back_second/pallas_call | solution.py:65
  95.5 1.5 collective-permute-done.22.take
  97.1 1.5 collective-permute-start.23
  98.6 7.1 %collective-permute-done.23.got = bf16[128,1024]{1,0:T(8,128)(2,1)S(1)} collective-permute-done((bf16[128,1024]{1,0:T(8,128)(2,1)S(1)}, bf16[128,1024]{1,0:T(8,128)(2,1)S(1)}, u32[]{:S(2)}, u32[]{:S(2)}) %collective-permute-start.23) | collective-permute-done | bytes 262176 | tf_op jit(solution)/shard_map/ppermute | solution.py:505
  106.0 1.5 collective-permute-start.31
  107.5 6.3 %collective-permute-done.31.cot_a = bf16[128,1024]{1,0:T(8,128)(2,1)S(1)} collective-permute-done((bf16[128,1024]{1,0:T(8,128)(2,1)S(1)}, bf16[128,1024]{1,0:T(8,128)(2,1)S(1)}, u32[]{:S(2)}, u32[]{:S(2)}) %collective-permute-start.31) | collective-permute-done | bytes 262176 | tf_op jit(solution)/shard_map/ppermute | solution.py:505
  113.8 1.5 slice.3
  115.3 1.1 dynamic-slice_bitcast_fusion.w1_rows
  116.5 1.0 copy-done.13
  117.5 0.9 copy-done.23
  118.5 2.0 %enc_grads_first.1 = (f32[1024,256]{1,0:T(8,128)S(1)}, f32[1024,256]{1,0:T(8,128)S(1)}) custom-call(s32[4]{0:T(128)S(1)} %pad_add_fusion.where.refs_0_, bf16[128,1024]{1,0:T(8,128)(2,1)S(1)} %packed_back.1.d_packed.cot_a, bf16[128,1024]{1,0:T(8,128)(2,1)} %collective-permute-done.33.cot_b, bf16[128,1024]{1,0:T(8,128)(2,1)S(1)} %get-tuple-element.66.first.act0_a, ...), custom_call_target="tpu_custom_call" | custom-call | flops 402653184 | bytes 4456448 | tf_op jit(solution)/shard_map/enc_grads_first/pallas_call | solution.py:65
  120.5 1.4 enc_grad0_second.1
  122.0 1.4 collective-permute-start.34
  123.8 1.6 %collective-permute-start.17 = (bf16[128,1024]{1,0:T(8,128)(2,1)S(1)}, bf16[128,1024]{1,0:T(8,128)(2,1)S(1)}, u32[]{:S(2)}, u32[]{:S(2)}) collective-permute-start(bf16[128,1024]{1,0:T(8,128)(2,1)S(1)} %ffn_out_far.1), channel_id=1, source_target_pairs={{0,2},{1,3},{2,0},{3,1},{4,6},{5,7},{6,4},{7,5},{8,10},{9,11},{10,... | collective-permute-start | bytes 786440 | tf_op jit(solution)/shard_map/ppermute | solution.py:505
  125.4 1.0 enc_grad1_second.1
  126.4 0.7 collective-permute-start.38
  127.3 3.3 %collective-permute-start.24 = (bf16[24,1024]{1,0:T(8,128)(2,1)S(1)}, bf16[24,1024]{1,0:T(8,128)(2,1)S(1)}, u32[]{:S(2)}, u32[]{:S(2)}) collective-permute-start(bf16[24,1024]{1,0:T(8,128)(2,1)S(1)} %get-tuple-element.88), channel_id=1, source_target_pairs={{0,28},{4,0},{8,4},{12,8},{16,12},{20,16},{24,20},{28,24},{1,29},{... | collective-permute-start | bytes 147464 | tf_op jit(solution)/shard_map/ppermute | solution.py:508
  130.6 0.8 collective-permute-start.25
  131.4 2.2 %collective-permute-start.26 = (bf16[24,1024]{1,0:T(8,128)(2,1)S(1)}, bf16[24,1024]{1,0:T(8,128)(2,1)S(1)}, u32[]{:S(2)}, u32[]{:S(2)}) collective-permute-start(bf16[24,1024]{1,0:T(8,128)(2,1)S(1)} %get-tuple-element.90), channel_id=1, source_target_pairs={{0,20},{4,24},{8,28},{12,0},{16,4},{20,8},{24,12},{28,16},{1,21},{... | collective-permute-start | bytes 147464 | tf_op jit(solution)/shard_map/ppermute | solution.py:508
  133.6 0.6 split_packs0.1
  134.2 1.1 collective-permute-start.35
  135.4 0.9 collective-permute-start.27
  136.3 2.4 %collective-permute-start.28 = (bf16[24,1024]{1,0:T(8,128)(2,1)S(1)}, bf16[24,1024]{1,0:T(8,128)(2,1)S(1)}, u32[]{:S(2)}, u32[]{:S(2)}) collective-permute-start(bf16[24,1024]{1,0:T(8,128)(2,1)S(1)} %get-tuple-element.92), channel_id=1, source_target_pairs={{0,12},{4,16},{8,20},{12,24},{16,28},{20,0},{24,4},{28,8},{1,13},{... | collective-permute-start | bytes 147464 | tf_op jit(solution)/shard_map/ppermute | solution.py:508
  139.1 0.9 collective-permute-start.30
  140.7 3.3 %collective-permute-start.36 = (bf16[128,256]{1,0:T(8,128)(2,1)S(1)}, bf16[128,256]{1,0:T(8,128)(2,1)S(1)}, u32[]{:S(2)}, u32[]{:S(2)}) collective-permute-start(bf16[128,256]{1,0:T(8,128)(2,1)S(1)} %get-tuple-element.103), channel_id=1, source_target_pairs={{0,8},{4,12},{8,0},{12,4},{1,9},{5,13},{9,1},{13,5},{2,10},{6,14},... | collective-permute-start | bytes 196616 | tf_op jit(solution)/shard_map/ppermute | solution.py:508
  144.0 2.2 %collective-permute-start.37 = (bf16[128,256]{1,0:T(8,128)(2,1)S(1)}, bf16[128,256]{1,0:T(8,128)(2,1)S(1)}, u32[]{:S(2)}, u32[]{:S(2)}) collective-permute-start(bf16[128,256]{1,0:T(8,128)(2,1)S(1)} %get-tuple-element.104), channel_id=1, source_target_pairs={{0,12},{4,0},{8,4},{12,8},{1,13},{5,1},{9,5},{13,9},{2,14},{6,2},{... | collective-permute-start | bytes 196616 | tf_op jit(solution)/shard_map/ppermute | solution.py:508
  146.7 1.8 %collective-permute-start.40 = (bf16[128,256]{1,0:T(8,128)(2,1)S(1)}, bf16[128,256]{1,0:T(8,128)(2,1)S(1)}, u32[]{:S(2)}, u32[]{:S(2)}) collective-permute-start(bf16[128,256]{1,0:T(8,128)(2,1)S(1)} %get-tuple-element.111), channel_id=1, source_target_pairs={{0,8},{4,12},{8,0},{12,4},{1,9},{5,13},{9,1},{13,5},{2,10},{6,14},... | collective-permute-start | bytes 196616 | tf_op jit(solution)/shard_map/ppermute | solution.py:508
  148.5 2.1 %collective-permute-start.41 = (bf16[128,256]{1,0:T(8,128)(2,1)S(1)}, bf16[128,256]{1,0:T(8,128)(2,1)S(1)}, u32[]{:S(2)}, u32[]{:S(2)}) collective-permute-start(bf16[128,256]{1,0:T(8,128)(2,1)S(1)} %get-tuple-element.112), channel_id=1, source_target_pairs={{0,12},{4,0},{8,4},{12,8},{1,13},{5,1},{9,5},{13,9},{2,14},{6,2},{... | collective-permute-start | bytes 196616 | tf_op jit(solution)/shard_map/ppermute | solution.py:508
  150.5 1.2 ffn_out_own.1
  151.7 1.0 back_recv.1
  152.8 1.3 collective-permute-done.40.refs_6_
  154.1 0.8 finish.1
  (107 shorter events, 8.5 us)
Async XLA Ops:
  0.6 69.5 %collective-permute-start.13 = (bf16[2,1024,512]{2,1,0:T(8,128)(2,1)}, bf16[2,1024,512]{2,1,0:T(8,128)(2,1)}, u32[]{:S(2)}, u32[]{:S(2)}) collective-permute-start(bf16[2,1024,512]{2,1,0:T(8,128)(2,1)} %in_a.3), channel_id=1, source_target_pairs={{0,1},{1,0},{2,3},{3,2},{4,5},{5,4},{6,7},{7,6},{8,9},{9,8},{10,11... | collective-permute-start | bytes 6291464 | tf_op jit(solution)/shard_map/ppermute | solution.py:502
  4.4 8.2 %collective-permute-start = (bf16[24,1152]{1,0:T(8,128)(2,1)S(1)}, bf16[24,1152]{1,0:T(8,128)(2,1)S(1)}, u32[]{:S(2)}, u32[]{:S(2)}) collective-permute-start(bf16[24,1152]{1,0:T(8,128)(2,1)S(1)} %get-tuple-element.59), channel_id=1, source_target_pairs={{0,4},{4,8},{8,12},{12,16},{16,20},{20,24},{24,28},{28,0},{1,5},{5... | collective-permute-start | bytes 165896 | tf_op jit(solution)/shard_map/ppermute | solution.py:508
  7.0 8.0 %collective-permute-start.1 = (bf16[24,1152]{1,0:T(8,128)(2,1)S(1)}, bf16[24,1152]{1,0:T(8,128)(2,1)S(1)}, u32[]{:S(2)}, u32[]{:S(2)}) collective-permute-start(bf16[24,1152]{1,0:T(8,128)(2,1)S(1)} %get-tuple-element.60), channel_id=1, source_target_pairs={{0,8},{4,12},{8,16},{12,20},{16,24},{20,28},{24,0},{28,4},{1,9},{5... | collective-permute-start | bytes 165896 | tf_op jit(solution)/shard_map/ppermute | solution.py:508
  9.6 6.3 %collective-permute-start.2 = (bf16[24,1152]{1,0:T(8,128)(2,1)S(1)}, bf16[24,1152]{1,0:T(8,128)(2,1)S(1)}, u32[]{:S(2)}, u32[]{:S(2)}) collective-permute-start(bf16[24,1152]{1,0:T(8,128)(2,1)S(1)} %get-tuple-element.61), channel_id=1, source_target_pairs={{0,12},{4,16},{8,20},{12,24},{16,28},{20,0},{24,4},{28,8},{1,13},{... | collective-permute-start | bytes 165896 | tf_op jit(solution)/shard_map/ppermute | solution.py:508
  11.9 6.4 %collective-permute-start.3 = (bf16[24,1152]{1,0:T(8,128)(2,1)S(1)}, bf16[24,1152]{1,0:T(8,128)(2,1)S(1)}, u32[]{:S(2)}, u32[]{:S(2)}) collective-permute-start(bf16[24,1152]{1,0:T(8,128)(2,1)S(1)} %get-tuple-element.62), channel_id=1, source_target_pairs={{0,16},{4,20},{8,24},{12,28},{16,0},{20,4},{24,8},{28,12},{1,17},{... | collective-permute-start | bytes 165896 | tf_op jit(solution)/shard_map/ppermute | solution.py:508
  12.6 6.1 %collective-permute-start.4 = (bf16[24,1152]{1,0:T(8,128)(2,1)S(1)}, bf16[24,1152]{1,0:T(8,128)(2,1)S(1)}, u32[]{:S(2)}, u32[]{:S(2)}) collective-permute-start(bf16[24,1152]{1,0:T(8,128)(2,1)S(1)} %get-tuple-element.63), channel_id=1, source_target_pairs={{0,20},{4,24},{8,28},{12,0},{16,4},{20,8},{24,12},{28,16},{1,21},{... | collective-permute-start | bytes 165896 | tf_op jit(solution)/shard_map/ppermute | solution.py:508
  15.0 5.6 %collective-permute-start.5 = (bf16[24,1152]{1,0:T(8,128)(2,1)S(1)}, bf16[24,1152]{1,0:T(8,128)(2,1)S(1)}, u32[]{:S(2)}, u32[]{:S(2)}) collective-permute-start(bf16[24,1152]{1,0:T(8,128)(2,1)S(1)} %get-tuple-element.64), channel_id=1, source_target_pairs={{0,24},{4,28},{8,0},{12,4},{16,8},{20,12},{24,16},{28,20},{1,25},{... | collective-permute-start | bytes 165896 | tf_op jit(solution)/shard_map/ppermute | solution.py:508
  15.9 5.0 %collective-permute-start.6 = (bf16[24,1152]{1,0:T(8,128)(2,1)S(1)}, bf16[24,1152]{1,0:T(8,128)(2,1)S(1)}, u32[]{:S(2)}, u32[]{:S(2)}) collective-permute-start(bf16[24,1152]{1,0:T(8,128)(2,1)S(1)} %get-tuple-element.65), channel_id=1, source_target_pairs={{0,28},{4,0},{8,4},{12,8},{16,12},{20,16},{24,20},{28,24},{1,29},{... | collective-permute-start | bytes 165896 | tf_op jit(solution)/shard_map/ppermute | solution.py:508
  21.0 19.5 %copy-start.27 = (s32[1,512]{1,0:T(1,128)S(1)}, s32[1,512]{1,0:T(1,128)}, u32[]{:S(2)}) copy-start(s32[1,512]{1,0:T(1,128)} %param.13) | copy-start | bytes 6148
  21.2 7.5 %collective-permute-start.7 = (bf16[128,1024]{1,0:T(8,128)(2,1)S(1)}, bf16[128,1024]{1,0:T(8,128)(2,1)S(1)}, u32[]{:S(2)}, u32[]{:S(2)}) collective-permute-start(bf16[128,1024]{1,0:T(8,128)(2,1)S(1)} %get-tuple-element.66.first.act0_a), channel_id=1, source_target_pairs={{0,2},{1,3},{2,0},{3,1},{4,6},{5,7},{6,4},{7,5},{8,10},{9,11},{10,... | collective-permute-start | bytes 786440 | tf_op jit(solution)/shard_map/ppermute | solution.py:505
  22.8 6.5 %collective-permute-start.9 = (bf16[128,1024]{1,0:T(8,128)(2,1)S(1)}, bf16[128,1024]{1,0:T(8,128)(2,1)S(1)}, u32[]{:S(2)}, u32[]{:S(2)}) collective-permute-start(bf16[128,1024]{1,0:T(8,128)(2,1)S(1)} %get-tuple-element.66.first.act0_a), channel_id=1, source_target_pairs={{0,1},{1,0},{2,3},{3,2},{4,5},{5,4},{6,7},{7,6},{8,9},{9,8},{10,11... | collective-permute-start | bytes 786440 | tf_op jit(solution)/shard_map/ppermute | solution.py:502
  28.7 11.8 %copy-start.16 = (bf16[128,1024]{1,0:T(8,128)(2,1)}, bf16[128,1024]{1,0:T(8,128)(2,1)S(1)}, u32[]{:S(2)}) copy-start(bf16[128,1024]{1,0:T(8,128)(2,1)S(1)} %collective-permute-done.7.third.act0_a) | copy-start | bytes 786436
  28.7 11.8 %collective-permute-start.8 = (bf16[128,1024]{1,0:T(8,128)(2,1)S(1)}, bf16[128,1024]{1,0:T(8,128)(2,1)S(1)}, u32[]{:S(2)}, u32[]{:S(2)}) collective-permute-start(bf16[128,1024]{1,0:T(8,128)(2,1)S(1)} %collective-permute-done.7.third.act0_a), channel_id=1, source_target_pairs={{0,1},{1,0},{2,3},{3,2},{4,5},{5,4},{6,7},{7,6},{8,9},{9,8},{10,11... | collective-permute-start | bytes 786440 | tf_op jit(solution)/shard_map/ppermute | solution.py:502
  28.7 20.3 %collective-permute-start.11 = (bf16[256,1024]{1,0:T(8,128)(2,1)}, bf16[256,1024]{1,0:T(8,128)(2,1)S(1)}, u32[]{:S(2)}, u32[]{:S(2)}) collective-permute-start(bf16[256,1024]{1,0:T(8,128)(2,1)} %w_out.3), channel_id=1, source_target_pairs={{0,1},{1,0},{2,3},{3,2},{4,5},{5,4},{6,7},{7,6},{8,9},{9,8},{10,11... | collective-permute-start | bytes 1572872 | tf_op jit(solution)/shard_map/ppermute | solution.py:502
  29.2 35.9 %collective-permute-start.14 = (bf16[512,1024]{1,0:T(8,128)(2,1)}, bf16[512,1024]{1,0:T(8,128)(2,1)S(1)}, u32[]{:S(2)}, u32[]{:S(2)}) collective-permute-start(bf16[512,1024]{1,0:T(8,128)(2,1)} %w_a.3), channel_id=1, source_target_pairs={{0,1},{1,0},{2,3},{3,2},{4,5},{5,4},{6,7},{7,6},{8,9},{9,8},{10,11... | collective-permute-start | bytes 3145736 | tf_op jit(solution)/shard_map/ppermute | solution.py:502
  33.0 7.5 %copy-start.2 = (bf16[2,1024,1024]{2,1,0:T(8,128)(2,1)S(1)}, bf16[2,1024,1024]{2,1,0:T(8,128)(2,1)}, u32[]{:S(2)}) copy-start(bf16[2,1024,1024]{2,1,0:T(8,128)(2,1)} %enc.3) | copy-start | bytes 12582916
  33.0 7.5 %copy-start.6 = (bf16[4,1024,256]{2,1,0:T(8,128)(2,1)S(1)}, bf16[4,1024,256]{2,1,0:T(8,128)(2,1)}, u32[]{:S(2)}) copy-start(bf16[4,1024,256]{2,1,0:T(8,128)(2,1)} %w_in.5) | copy-start | bytes 6291460
  40.5 7.9 %copy-start.12 = (bf16[256,1024]{1,0:T(8,128)(2,1)}, bf16[256,1024]{1,0:T(8,128)(2,1)S(1)}, u32[]{:S(2)}) copy-start(bf16[256,1024]{1,0:T(8,128)(2,1)S(1)} %get-tuple-element.96.act1) | copy-start | bytes 1572868
  40.5 7.9 %copy-start.18 = (bf16[128,1024]{1,0:T(8,128)(2,1)}, bf16[128,1024]{1,0:T(8,128)(2,1)S(1)}, u32[]{:S(2)}) copy-start(bf16[128,1024]{1,0:T(8,128)(2,1)S(1)} %collective-permute-done.8.fourth.act0_b) | copy-start | bytes 786436
  40.5 9.4 %copy-start.3 = (bf16[256,1024]{1,0:T(8,128)(2,1)S(1)}, bf16[256,1024]{1,0:T(8,128)(2,1)}, u32[]{:S(2)}) copy-start(bf16[256,1024]{1,0:T(8,128)(2,1)} %w_out.3) | copy-start | bytes 1572868
  40.5 11.3 %copy-start.9 = (bf16[1,128,1024]{2,1,0:T(8,128)(2,1)S(1)}, bf16[1,128,1024]{2,1,0:T(8,128)(2,1)}, u32[]{:S(2)}) copy-start(bf16[1,128,1024]{2,1,0:T(8,128)(2,1)} %param.19) | copy-start | bytes 786436
  48.4 4.0 %copy-start.10 = (bf16[256,1024]{1,0:T(8,128)(2,1)}, bf16[256,1024]{1,0:T(8,128)(2,1)S(1)}, u32[]{:S(2)}) copy-start(bf16[256,1024]{1,0:T(8,128)(2,1)S(1)} %get-tuple-element.105.act1) | copy-start | bytes 1572868
  48.4 4.3 %copy-start.20 = (f32[256,256]{1,0:T(8,128)}, f32[256,256]{1,0:T(8,128)S(1)}, u32[]{:S(2)}) copy-start(f32[256,256]{1,0:T(8,128)S(1)} %get-tuple-element.95.pre) | copy-start | bytes 786436
  48.4 1.6 %collective-permute-start.10 = (bf16[256,256]{1,0:T(8,128)(2,1)S(1)}, bf16[256,256]{1,0:T(8,128)(2,1)S(1)}, u32[]{:S(2)}, u32[]{:S(2)}) collective-permute-start(bf16[256,256]{1,0:T(8,128)(2,1)S(1)} %get-tuple-element.69), channel_id=1, source_target_pairs={{0,1},{1,0},{2,3},{3,2},{4,5},{5,4},{6,7},{7,6},{8,9},{9,8},{10,11... | collective-permute-start | bytes 393224 | tf_op jit(solution)/shard_map/ppermute | solution.py:502
  50.0 20.2 %copy-start = (bf16[512,1024]{1,0:T(8,128)(2,1)S(1)}, bf16[512,1024]{1,0:T(8,128)(2,1)}, u32[]{:S(2)}) copy-start(bf16[512,1024]{1,0:T(8,128)(2,1)} %w_a.3) | copy-start | bytes 3145732
  50.0 20.2 %copy-start.4 = (bf16[2,1024,512]{2,1,0:T(8,128)(2,1)S(1)}, bf16[2,1024,512]{2,1,0:T(8,128)(2,1)}, u32[]{:S(2)}) copy-start(bf16[2,1024,512]{2,1,0:T(8,128)(2,1)} %in_a.3) | copy-start | bytes 6291460
  50.3 9.2 %collective-permute-start.12 = (bf16[128,1024]{1,0:T(8,128)(2,1)S(1)}, bf16[128,1024]{1,0:T(8,128)(2,1)S(1)}, u32[]{:S(2)}, u32[]{:S(2)}) collective-permute-start(bf16[128,1024]{1,0:T(8,128)(2,1)S(1)} %attn_out_far.1), channel_id=1, source_target_pairs={{0,2},{1,3},{2,0},{3,1},{4,6},{5,7},{6,4},{7,5},{8,10},{9,11},{10,... | collective-permute-start | bytes 786440 | tf_op jit(solution)/shard_map/ppermute | solution.py:505
  51.8 13.3 %collective-permute-start.16 = (bf16[128,1024]{1,0:T(8,128)(2,1)S(1)}, bf16[128,1024]{1,0:T(8,128)(2,1)S(1)}, u32[]{:S(2)}, u32[]{:S(2)}) collective-permute-start(bf16[128,1024]{1,0:T(8,128)(2,1)S(1)} %bitcast.11), channel_id=1, source_target_pairs={{0,2},{1,3},{2,0},{3,1},{4,6},{5,7},{6,4},{7,5},{8,10},{9,11},{10,... | collective-permute-start | bytes 786440 | tf_op jit(solution)/shard_map/ppermute | solution.py:505
  59.7 21.8 %copy-start.7 = (bf16[128,1024]{1,0:T(8,128)(2,1)}, bf16[128,1024]{1,0:T(8,128)(2,1)S(1)}, u32[]{:S(2)}) copy-start(bf16[128,1024]{1,0:T(8,128)(2,1)S(1)} %get-tuple-element.73.resid) | copy-start | bytes 786436
  59.7 10.5 %collective-permute-start.15 = (bf16[128,1024]{1,0:T(8,128)(2,1)S(1)}, bf16[128,1024]{1,0:T(8,128)(2,1)S(1)}, u32[]{:S(2)}, u32[]{:S(2)}) collective-permute-start(bf16[128,1024]{1,0:T(8,128)(2,1)S(1)} %get-tuple-element.71.rows_ref), channel_id=1, source_target_pairs={{0,2},{1,3},{2,0},{3,1},{4,6},{5,7},{6,4},{7,5},{8,10},{9,11},{10,... | collective-permute-start | bytes 786440 | tf_op jit(solution)/shard_map/ppermute | solution.py:505
  73.6 5.2 %copy-start.24 = (bf16[128,1024]{1,0:T(8,128)(2,1)}, bf16[128,1024]{1,0:T(8,128)(2,1)S(1)}, u32[]{:S(2)}) copy-start(bf16[128,1024]{1,0:T(8,128)(2,1)S(1)} %get-tuple-element.74.hidden) | copy-start | bytes 786436
  73.6 7.8 %collective-permute-start.18 = (bf16[128,1024]{1,0:T(8,128)(2,1)S(1)}, bf16[128,1024]{1,0:T(8,128)(2,1)S(1)}, u32[]{:S(2)}, u32[]{:S(2)}) collective-permute-start(bf16[128,1024]{1,0:T(8,128)(2,1)S(1)} %get-tuple-element.78), channel_id=1, source_target_pairs={{0,2},{1,3},{2,0},{3,1},{4,6},{5,7},{6,4},{7,5},{8,10},{9,11},{10,... | collective-permute-start | bytes 786440 | tf_op jit(solution)/shard_map/ppermute | solution.py:505
  78.8 12.2 %copy-start.14 = (bf16[128,1024]{1,0:T(8,128)(2,1)}, bf16[128,1024]{1,0:T(8,128)(2,1)S(1)}, u32[]{:S(2)}) copy-start(bf16[128,1024]{1,0:T(8,128)(2,1)S(1)} %get-tuple-element.72.hidden) | copy-start | bytes 786436
  81.8 6.9 %collective-permute-start.19 = (bf16[128,1024]{1,0:T(8,128)(2,1)S(1)}, bf16[128,1024]{1,0:T(8,128)(2,1)S(1)}, u32[]{:S(2)}, u32[]{:S(2)}) collective-permute-start(bf16[128,1024]{1,0:T(8,128)(2,1)S(1)} %resid_back.1.first.d_resid), channel_id=1, source_target_pairs={{0,2},{1,3},{2,0},{3,1},{4,6},{5,7},{6,4},{7,5},{8,10},{9,11},{10,... | collective-permute-start | bytes 786440 | tf_op jit(solution)/shard_map/ppermute | solution.py:505
  83.3 5.4 %collective-permute-start.21 = (bf16[128,1024]{1,0:T(8,128)(2,1)S(1)}, bf16[128,1024]{1,0:T(8,128)(2,1)S(1)}, u32[]{:S(2)}, u32[]{:S(2)}) collective-permute-start(bf16[128,1024]{1,0:T(8,128)(2,1)S(1)} %resid_back.1.first.d_resid), channel_id=1, source_target_pairs={{0,1},{1,0},{2,3},{3,2},{4,5},{5,4},{6,7},{7,6},{8,9},{9,8},{10,11... | collective-permute-start | bytes 786440 | tf_op jit(solution)/shard_map/ppermute | solution.py:502
  88.7 2.3 %collective-permute-start.20 = (bf16[128,1024]{1,0:T(8,128)(2,1)S(1)}, bf16[128,1024]{1,0:T(8,128)(2,1)S(1)}, u32[]{:S(2)}, u32[]{:S(2)}) collective-permute-start(bf16[128,1024]{1,0:T(8,128)(2,1)S(1)} %collective-permute-done.19.third), channel_id=1, source_target_pairs={{0,1},{1,0},{2,3},{3,2},{4,5},{5,4},{6,7},{7,6},{8,9},{9,8},{10,11... | collective-permute-start | bytes 786440 | tf_op jit(solution)/shard_map/ppermute | solution.py:502
  94.9 2.1 %collective-permute-start.22 = (bf16[256,1024]{1,0:T(8,128)(2,1)S(1)}, bf16[256,1024]{1,0:T(8,128)(2,1)S(1)}, u32[]{:S(2)}, u32[]{:S(2)}) collective-permute-start(bf16[256,1024]{1,0:T(8,128)(2,1)S(1)} %get-tuple-element.86), channel_id=1, source_target_pairs={{0,1},{1,0},{2,3},{3,2},{4,5},{5,4},{6,7},{7,6},{8,9},{9,8},{10,11... | collective-permute-start | bytes 1572872 | tf_op jit(solution)/shard_map/ppermute | solution.py:502
  97.1 8.7 %collective-permute-start.23 = (bf16[128,1024]{1,0:T(8,128)(2,1)S(1)}, bf16[128,1024]{1,0:T(8,128)(2,1)S(1)}, u32[]{:S(2)}, u32[]{:S(2)}) collective-permute-start(bf16[128,1024]{1,0:T(8,128)(2,1)S(1)} %add_far.1), channel_id=1, source_target_pairs={{0,2},{1,3},{2,0},{3,1},{4,6},{5,7},{6,4},{7,5},{8,10},{9,11},{10,... | collective-permute-start | bytes 786440 | tf_op jit(solution)/shard_map/ppermute | solution.py:505
  106.0 7.8 %collective-permute-start.31 = (bf16[128,1024]{1,0:T(8,128)(2,1)S(1)}, bf16[128,1024]{1,0:T(8,128)(2,1)S(1)}, u32[]{:S(2)}, u32[]{:S(2)}) collective-permute-start(bf16[128,1024]{1,0:T(8,128)(2,1)S(1)} %packed_back.1.d_packed.cot_a), channel_id=1, source_target_pairs={{0,2},{1,3},{2,0},{3,1},{4,6},{5,7},{6,4},{7,5},{8,10},{9,11},{10,... | collective-permute-start | bytes 786440 | tf_op jit(solution)/shard_map/ppermute | solution.py:505
  107.5 9.0 %collective-permute-start.33 = (bf16[128,1024]{1,0:T(8,128)(2,1)S(1)}, bf16[128,1024]{1,0:T(8,128)(2,1)}, u32[]{:S(2)}, u32[]{:S(2)}) collective-permute-start(bf16[128,1024]{1,0:T(8,128)(2,1)S(1)} %packed_back.1.d_packed.cot_a), channel_id=1, source_target_pairs={{0,1},{1,0},{2,3},{3,2},{4,5},{5,4},{6,7},{7,6},{8,9},{9,8},{10,11... | collective-permute-start | bytes 786440 | tf_op jit(solution)/shard_map/ppermute | solution.py:502
  113.8 6.6 %collective-permute-start.32 = (bf16[128,1024]{1,0:T(8,128)(2,1)S(1)}, bf16[128,1024]{1,0:T(8,128)(2,1)S(1)}, u32[]{:S(2)}, u32[]{:S(2)}) collective-permute-start(bf16[128,1024]{1,0:T(8,128)(2,1)S(1)} %collective-permute-done.31.cot_a), channel_id=1, source_target_pairs={{0,1},{1,0},{2,3},{3,2},{4,5},{5,4},{6,7},{7,6},{8,9},{9,8},{10,11... | collective-permute-start | bytes 786440 | tf_op jit(solution)/shard_map/ppermute | solution.py:502
  115.3 5.2 %copy-start.17 = (bf16[128,1024]{1,0:T(8,128)(2,1)S(1)}, bf16[128,1024]{1,0:T(8,128)(2,1)}, u32[]{:S(2)}) copy-start(bf16[128,1024]{1,0:T(8,128)(2,1)} %copy-done.16) | copy-start | bytes 786436
  115.3 5.2 %copy-start.19 = (bf16[128,1024]{1,0:T(8,128)(2,1)S(1)}, bf16[128,1024]{1,0:T(8,128)(2,1)}, u32[]{:S(2)}) copy-start(bf16[128,1024]{1,0:T(8,128)(2,1)} %copy-done.18) | copy-start | bytes 786436
  115.3 5.2 %copy-start.21 = (f32[256,256]{1,0:T(8,128)S(1)}, f32[256,256]{1,0:T(8,128)}, u32[]{:S(2)}) copy-start(f32[256,256]{1,0:T(8,128)} %copy-done.20) | copy-start | bytes 786436
  118.5 4.8 %copy-start.25 = (bf16[128,1024]{1,0:T(8,128)(2,1)S(1)}, bf16[128,1024]{1,0:T(8,128)(2,1)}, u32[]{:S(2)}) copy-start(bf16[128,1024]{1,0:T(8,128)(2,1)} %copy-done.24) | copy-start | bytes 786436
  120.5 4.9 %copy-start.11 = (bf16[256,1024]{1,0:T(8,128)(2,1)S(1)}, bf16[256,1024]{1,0:T(8,128)(2,1)}, u32[]{:S(2)}) copy-start(bf16[256,1024]{1,0:T(8,128)(2,1)} %copy-done.10) | copy-start | bytes 1572868
  122.0 9.5 %collective-permute-start.34 = (bf16[512,256]{1,0:T(8,128)(2,1)S(1)}, bf16[512,256]{1,0:T(8,128)(2,1)S(1)}, u32[]{:S(2)}, u32[]{:S(2)}) collective-permute-start(bf16[512,256]{1,0:T(8,128)(2,1)S(1)} %get-tuple-element.100), channel_id=1, source_target_pairs={{0,16},{16,0},{1,17},{17,1},{2,18},{18,2},{3,19},{19,3},{4,20},{20... | collective-permute-start | bytes 786440 | tf_op jit(solution)/shard_map/ppermute | solution.py:508
  123.8 26.8 %copy-start.8 = (bf16[128,1024]{1,0:T(8,128)(2,1)S(1)}, bf16[128,1024]{1,0:T(8,128)(2,1)}, u32[]{:S(2)}) copy-start(bf16[128,1024]{1,0:T(8,128)(2,1)} %copy-done.7) | copy-start | bytes 786436
  123.8 26.7 %copy-start.15 = (bf16[128,1024]{1,0:T(8,128)(2,1)S(1)}, bf16[128,1024]{1,0:T(8,128)(2,1)}, u32[]{:S(2)}) copy-start(bf16[128,1024]{1,0:T(8,128)(2,1)} %copy-done.14) | copy-start | bytes 786436
  123.8 10.4 %collective-permute-start.17 = (bf16[128,1024]{1,0:T(8,128)(2,1)S(1)}, bf16[128,1024]{1,0:T(8,128)(2,1)S(1)}, u32[]{:S(2)}, u32[]{:S(2)}) collective-permute-start(bf16[128,1024]{1,0:T(8,128)(2,1)S(1)} %ffn_out_far.1), channel_id=1, source_target_pairs={{0,2},{1,3},{2,0},{3,1},{4,6},{5,7},{6,4},{7,5},{8,10},{9,11},{10,... | collective-permute-start | bytes 786440 | tf_op jit(solution)/shard_map/ppermute | solution.py:505
  126.4 12.7 %collective-permute-start.38 = (bf16[512,256]{1,0:T(8,128)(2,1)S(1)}, bf16[512,256]{1,0:T(8,128)(2,1)S(1)}, u32[]{:S(2)}, u32[]{:S(2)}) collective-permute-start(bf16[512,256]{1,0:T(8,128)(2,1)S(1)} %get-tuple-element.108), channel_id=1, source_target_pairs={{0,16},{16,0},{1,17},{17,1},{2,18},{18,2},{3,19},{19,3},{4,20},{20... | collective-permute-start | bytes 786440 | tf_op jit(solution)/shard_map/ppermute | solution.py:508
  127.3 8.0 %collective-permute-start.24 = (bf16[24,1024]{1,0:T(8,128)(2,1)S(1)}, bf16[24,1024]{1,0:T(8,128)(2,1)S(1)}, u32[]{:S(2)}, u32[]{:S(2)}) collective-permute-start(bf16[24,1024]{1,0:T(8,128)(2,1)S(1)} %get-tuple-element.88), channel_id=1, source_target_pairs={{0,28},{4,0},{8,4},{12,8},{16,12},{20,16},{24,20},{28,24},{1,29},{... | collective-permute-start | bytes 147464 | tf_op jit(solution)/shard_map/ppermute | solution.py:508
  130.6 5.7 %collective-permute-start.25 = (bf16[24,1024]{1,0:T(8,128)(2,1)S(1)}, bf16[24,1024]{1,0:T(8,128)(2,1)S(1)}, u32[]{:S(2)}, u32[]{:S(2)}) collective-permute-start(bf16[24,1024]{1,0:T(8,128)(2,1)S(1)} %get-tuple-element.89), channel_id=1, source_target_pairs={{0,24},{4,28},{8,0},{12,4},{16,8},{20,12},{24,16},{28,20},{1,25},{... | collective-permute-start | bytes 147464 | tf_op jit(solution)/shard_map/ppermute | solution.py:508
  131.4 7.2 %collective-permute-start.26 = (bf16[24,1024]{1,0:T(8,128)(2,1)S(1)}, bf16[24,1024]{1,0:T(8,128)(2,1)S(1)}, u32[]{:S(2)}, u32[]{:S(2)}) collective-permute-start(bf16[24,1024]{1,0:T(8,128)(2,1)S(1)} %get-tuple-element.90), channel_id=1, source_target_pairs={{0,20},{4,24},{8,28},{12,0},{16,4},{20,8},{24,12},{28,16},{1,21},{... | collective-permute-start | bytes 147464 | tf_op jit(solution)/shard_map/ppermute | solution.py:508
  134.2 14.2 %collective-permute-start.35 = (bf16[128,256]{1,0:T(8,128)(2,1)S(1)}, bf16[128,256]{1,0:T(8,128)(2,1)S(1)}, u32[]{:S(2)}, u32[]{:S(2)}) collective-permute-start(bf16[128,256]{1,0:T(8,128)(2,1)S(1)} %get-tuple-element.102), channel_id=1, source_target_pairs={{0,4},{4,8},{8,12},{12,0},{1,5},{5,9},{9,13},{13,1},{2,6},{6,10},{... | collective-permute-start | bytes 196616 | tf_op jit(solution)/shard_map/ppermute | solution.py:508
  135.4 5.3 %collective-permute-start.27 = (bf16[24,1024]{1,0:T(8,128)(2,1)S(1)}, bf16[24,1024]{1,0:T(8,128)(2,1)S(1)}, u32[]{:S(2)}, u32[]{:S(2)}) collective-permute-start(bf16[24,1024]{1,0:T(8,128)(2,1)S(1)} %get-tuple-element.91), channel_id=1, source_target_pairs={{0,16},{4,20},{8,24},{12,28},{16,0},{20,4},{24,8},{28,12},{1,17},{... | collective-permute-start | bytes 147464 | tf_op jit(solution)/shard_map/ppermute | solution.py:508
  136.3 7.7 %collective-permute-start.28 = (bf16[24,1024]{1,0:T(8,128)(2,1)S(1)}, bf16[24,1024]{1,0:T(8,128)(2,1)S(1)}, u32[]{:S(2)}, u32[]{:S(2)}) collective-permute-start(bf16[24,1024]{1,0:T(8,128)(2,1)S(1)} %get-tuple-element.92), channel_id=1, source_target_pairs={{0,12},{4,16},{8,20},{12,24},{16,28},{20,0},{24,4},{28,8},{1,13},{... | collective-permute-start | bytes 147464 | tf_op jit(solution)/shard_map/ppermute | solution.py:508
  138.7 8.0 %collective-permute-start.29 = (bf16[24,1024]{1,0:T(8,128)(2,1)S(1)}, bf16[24,1024]{1,0:T(8,128)(2,1)S(1)}, u32[]{:S(2)}, u32[]{:S(2)}) collective-permute-start(bf16[24,1024]{1,0:T(8,128)(2,1)S(1)} %get-tuple-element.93), channel_id=1, source_target_pairs={{0,8},{4,12},{8,16},{12,20},{16,24},{20,28},{24,0},{28,4},{1,9},{5... | collective-permute-start | bytes 147464 | tf_op jit(solution)/shard_map/ppermute | solution.py:508
  139.1 7.6 %collective-permute-start.30 = (bf16[24,1024]{1,0:T(8,128)(2,1)S(1)}, bf16[24,1024]{1,0:T(8,128)(2,1)S(1)}, u32[]{:S(2)}, u32[]{:S(2)}) collective-permute-start(bf16[24,1024]{1,0:T(8,128)(2,1)S(1)} %get-tuple-element.94), channel_id=1, source_target_pairs={{0,4},{4,8},{8,12},{12,16},{16,20},{20,24},{24,28},{28,0},{1,5},{5... | collective-permute-start | bytes 147464 | tf_op jit(solution)/shard_map/ppermute | solution.py:508
  140.7 12.0 %collective-permute-start.36 = (bf16[128,256]{1,0:T(8,128)(2,1)S(1)}, bf16[128,256]{1,0:T(8,128)(2,1)S(1)}, u32[]{:S(2)}, u32[]{:S(2)}) collective-permute-start(bf16[128,256]{1,0:T(8,128)(2,1)S(1)} %get-tuple-element.103), channel_id=1, source_target_pairs={{0,8},{4,12},{8,0},{12,4},{1,9},{5,13},{9,1},{13,5},{2,10},{6,14},... | collective-permute-start | bytes 196616 | tf_op jit(solution)/shard_map/ppermute | solution.py:508
  144.0 8.7 %collective-permute-start.37 = (bf16[128,256]{1,0:T(8,128)(2,1)S(1)}, bf16[128,256]{1,0:T(8,128)(2,1)S(1)}, u32[]{:S(2)}, u32[]{:S(2)}) collective-permute-start(bf16[128,256]{1,0:T(8,128)(2,1)S(1)} %get-tuple-element.104), channel_id=1, source_target_pairs={{0,12},{4,0},{8,4},{12,8},{1,13},{5,1},{9,5},{13,9},{2,14},{6,2},{... | collective-permute-start | bytes 196616 | tf_op jit(solution)/shard_map/ppermute | solution.py:508
  146.6 6.2 %collective-permute-start.39 = (bf16[128,256]{1,0:T(8,128)(2,1)S(1)}, bf16[128,256]{1,0:T(8,128)(2,1)S(1)}, u32[]{:S(2)}, u32[]{:S(2)}) collective-permute-start(bf16[128,256]{1,0:T(8,128)(2,1)S(1)} %get-tuple-element.110), channel_id=1, source_target_pairs={{0,4},{4,8},{8,12},{12,0},{1,5},{5,9},{9,13},{13,1},{2,6},{6,10},{... | collective-permute-start | bytes 196616 | tf_op jit(solution)/shard_map/ppermute | solution.py:508
  146.7 7.5 %collective-permute-start.40 = (bf16[128,256]{1,0:T(8,128)(2,1)S(1)}, bf16[128,256]{1,0:T(8,128)(2,1)S(1)}, u32[]{:S(2)}, u32[]{:S(2)}) collective-permute-start(bf16[128,256]{1,0:T(8,128)(2,1)S(1)} %get-tuple-element.111), channel_id=1, source_target_pairs={{0,8},{4,12},{8,0},{12,4},{1,9},{5,13},{9,1},{13,5},{2,10},{6,14},... | collective-permute-start | bytes 196616 | tf_op jit(solution)/shard_map/ppermute | solution.py:508
  148.5 5.7 %collective-permute-start.41 = (bf16[128,256]{1,0:T(8,128)(2,1)S(1)}, bf16[128,256]{1,0:T(8,128)(2,1)S(1)}, u32[]{:S(2)}, u32[]{:S(2)}) collective-permute-start(bf16[128,256]{1,0:T(8,128)(2,1)S(1)} %get-tuple-element.112), channel_id=1, source_target_pairs={{0,12},{4,0},{8,4},{12,8},{1,13},{5,1},{9,5},{13,9},{2,14},{6,2},{... | collective-permute-start | bytes 196616 | tf_op jit(solution)/shard_map/ppermute | solution.py:508
  (8 other events, 8.7 us)

commit v3 on v2

v3 whole, which is shorter than its diff:
```python
import functools

import jax
import jax.numpy as jnp
from jax import lax
from jax.experimental import pallas as pl
from jax.experimental.pallas import tpu as pltpu
from jax.sharding import PartitionSpec as P

D = 1024
HEADS = 16
HEAD = D // HEADS
EPS = 1e-06
F32 = jnp.float32
BF16 = jnp.bfloat16
MIB = 1 << 20
CHUNK = 256


def dot(left, right, dims=((1,), (0,))):
    return lax.dot_general(left, right, (dims, ((), ())), preferred_element_type=F32)


NT = ((1,), (1,))
TN = ((0,), (0,))


def bf16(value):
    return value.astype(BF16)


def silu_grad(value, sigma):
    return sigma * (1.0 + value * (1.0 - sigma))


def norm_factor(wide):
    return lax.rsqrt(jnp.mean(wide * wide, axis=-1, keepdims=True) + EPS)


def norm_back(grad, normed, factor):
    return factor * (grad - normed * jnp.mean(grad * normed, axis=-1, keepdims=True))


def turned(row, rows):
    return jnp.broadcast_to(row.astype(F32), (rows, rows)).T


def like(shape, dtype):
    return jax.ShapeDtypeStruct(shape, dtype)


def run(body, outs, scalars, args, scratch=(), flops=0, name=None, limit=16, space=pltpu.VMEM):
    specs = [pl.BlockSpec(memory_space=space)] * len(args)
    operands = list(args)
    if scalars is not None:
        specs = [pl.BlockSpec(memory_space=pltpu.SMEM)] + specs
        operands = [scalars] + operands
    total = sum(a.size * a.dtype.itemsize for a in list(args) + list(outs))
    return pl.pallas_call(
        body,
        out_shape=list(outs),
        in_specs=specs,
        out_specs=[pl.BlockSpec(memory_space=pltpu.VMEM)] * len(outs),
        scratch_shapes=list(scratch),
        compiler_params=pltpu.CompilerParams(vmem_limit_bytes=limit * MIB),
        cost_estimate=pl.CostEstimate(flops=flops, bytes_accessed=total, transcendentals=0),
        name=name,
    )(*operands)


def tie(*values):
    return lax.optimization_barrier(values)


def route_send(capacity, where, owner_hbm, slot_hbm, features_hbm, *refs):
    outs, (owner, slot, features, sems) = refs[:-4], refs[-4:]
    sends, place_ref = outs[:-1], outs[-1]
    copies = [
        pltpu.make_async_copy(source, target, sems.at[n])
        for n, (source, target) in enumerate(
            ((owner_hbm, owner), (slot_hbm, slot), (features_hbm, features))
        )
    ]
    for copy in copies:
        copy.start()
    for copy in copies:
        copy.wait()
    groups = len(sends)
    rows, width = features.shape
    o_row = owner[...]
    o_col = turned(o_row, rows)
    i = lax.broadcasted_iota(jnp.int32, (rows, rows), 0)
    j = lax.broadcasted_iota(jnp.int32, (rows, rows), 1)
    earlier = jnp.where((o_col == o_row.astype(F32)) & (i < j), 1.0, 0.0)
    rank = jnp.sum(earlier, axis=0, keepdims=True).astype(jnp.int32)
    place = (o_row ^ where[0]) * capacity + rank
    place_ref[...] = place
    spots = lax.broadcasted_iota(jnp.int32, (groups * capacity, rows), 0)
    hot = jnp.where(spots == place, 1.0, 0.0).astype(BF16)
    big = dot(hot, features[...])
    tags = dot(hot, bf16(turned(slot[...] + 1, rows)))
    for k in range(groups):
        part = slice(k * capacity, (k + 1) * capacity)
        sends[k][:, :width] = bf16(big[part])
        sends[k][:, width:] = bf16(tags[part])


def route_recv(*refs):
    gots, (rows_ref, hot_ref) = refs[:-2], refs[-2:]
    rows, width = rows_ref.shape
    got = jnp.concatenate([g[...].astype(F32) for g in gots], axis=0)
    lanes = lax.broadcasted_iota(jnp.int32, (got.shape[0], rows), 1) + 1
    hot = jnp.where(got[:, width:] == lanes.astype(F32), 1.0, 0.0).astype(BF16)
    hot_ref[...] = hot
    rows_ref[...] = bf16(dot(hot, bf16(got[:, :width]), TN))


def back_send(hot, d_packed, *sends):
    groups = len(sends)
    capacity = hot.shape[0] // groups
    big = dot(hot[...], d_packed[...])
    for k in range(groups):
        sends[k][...] = bf16(big[k * capacity : (k + 1) * capacity])


def back_recv(place, *refs):
    gots, out = refs[:-1], refs[-1]
    got = bf16(jnp.concatenate([g[...].astype(F32) for g in gots], axis=0))
    spots = lax.broadcasted_iota(jnp.int32, (got.shape[0], out.shape[0]), 0)
    hot = jnp.where(spots == place[...], 1.0, 0.0).astype(BF16)
    out[...] = bf16(dot(hot, got, TN))


def encode(where, rows, enc, w_in, pre_all, pre_ref, act_ref, packed_ref, store):
    width = rows.shape[1]
    cols = pre_ref.shape[1]
    for n in range(width // CHUNK):
        part = slice(n * CHUNK, (n + 1) * CHUNK)
        pre = dot(rows, enc[0, :, part])
        pre_all[:, part] = pre
        act_ref[:, part] = bf16(pre * jax.nn.sigmoid(pre))
    pre_ref[...] = pre_all[:, pl.ds(pl.multiple_of(where[1] * cols, cols), cols)]
    packed = bf16(dot(act_ref[...], enc[1]))
    if packed_ref is not None:
        packed_ref[...] = packed[: packed_ref.shape[0]]
    wide = packed.astype(F32)
    normed = bf16(wide * norm_factor(wide))
    for c in range(w_in.shape[0]):
        store(c, bf16(dot(normed, w_in[c])))


def encode_first(where, first, second, enc, w_in, pre_ref, act_ref, packed_ref, proj_ref, pre_all):
    rows = jnp.concatenate([first[...], second[...]], axis=0)
    half = first.shape[0]

    def store(c, value):
        proj_ref[c, 0] = value[:half]
        proj_ref[c, 1] = value[half:]

    encode(where, rows, enc, w_in, pre_all, pre_ref, act_ref, packed_ref, store)


def window(where, docs, r, rows):
    t = where[1]
    b = t ^ r
    ahead = jnp.where(b > 0, (b - 1) ^ t, r)
    doc_q = turned(docs[b], rows)
    doc_own = docs[b].astype(F32)
    doc_ahead = docs[jnp.maximum(b - 1, 0)].astype(F32)
    i = lax.broadcasted_iota(jnp.int32, (rows, rows), 0)
    j = lax.broadcasted_iota(jnp.int32, (rows, rows), 1)
    own = jnp.where((doc_q == doc_own) & (j <= i), 1.0, 0.0)
    prior = jnp.where(doc_q == doc_ahead, 1.0, 0.0) * jnp.where(b > 0, 1.0, 0.0)
    allowed = jnp.concatenate([prior, own], axis=1)
    root_inv = lax.rsqrt(jnp.sum(allowed, axis=1, keepdims=True))
    return ahead, allowed, root_inv


def head_masks(cols):
    lane = lax.broadcasted_iota(jnp.int32, (1, cols), 1) // HEAD
    return [jnp.where(lane == h, 1.0, 0.0) for h in range(cols // HEAD)]


def spread(value, masks):
    return jnp.concatenate([value * bf16(m) for m in masks], axis=0)


def collect(value, masks):
    rows = value.shape[0] // len(masks)
    total = None
    for h, m in enumerate(masks):
        part = value[h * rows : (h + 1) * rows] * m
        total = part if total is None else total + part
    return total


def attend_first(
    where, docs, third, fourth, proj_a, enc, w_in,
    pre_ref, act_ref, proj_ref, att_ref, give_ref, keep_ref, pre_all,
):
    rows = jnp.concatenate([third[...], fourth[...]], axis=0)
    half = third.shape[0]
    cols = proj_a.shape[-1]
    proj_ref[:, 0:2] = proj_a[...]

    def store(c, value):
        proj_ref[c, 2] = value[:half]
        proj_ref[c, 3] = value[half:]

    encode(where, rows, enc, w_in, pre_all, pre_ref, act_ref, None, store)
    masks = head_masks(cols)
    for r, (target, place) in enumerate(((keep_ref, 1), (give_ref, 1), (keep_ref, 0), (give_ref, 0))):
        ahead, allowed, root_inv = window(where, docs, r, half)
        keys = jnp.concatenate([proj_ref[1, ahead], proj_ref[1, r]], axis=0)
        values = jnp.concatenate([proj_ref[2, ahead], proj_ref[2, r]], axis=0)
        many = jnp.concatenate([allowed] * len(masks), axis=0)
        scores = dot(spread(proj_ref[0, r], masks), keys, NT) * HEAD ** (-0.5)
        weights = bf16(scores * jax.nn.sigmoid(scores) * many)
        attended = collect(dot(weights, values), masks) * root_inv
        gate = proj_ref[3, r].astype(F32)
        att_ref[r] = attended
        target[place * half : (place + 1) * half, :] = bf16(attended * gate * jax.nn.sigmoid(gate))


def out_part(give_rows, half_index, keep, take, w_own, w_near):
    part = slice(half_index * give_rows, (half_index + 1) * give_rows)
    return dot(keep[part, :], w_own[...]) + dot(take[part, :], w_near[...])


def attn_out_far(keep, take, w_own, w_near, out):
    out[...] = bf16(out_part(out.shape[0], 0, keep, take, w_own, w_near))


def attn_out_own(keep, take, w_own, w_near, packed, out):
    out[...] = out_part(out.shape[0], 1, keep, take, w_own, w_near) + packed[...].astype(F32)


def residual(part, got, resid_ref, normed_ref):
    resid = bf16(part[...] + got[...].astype(F32))
    resid_ref[...] = resid
    wide = resid.astype(F32)
    normed_ref[...] = bf16(wide * norm_factor(wide))


def ffn(rows_ref, d_out_ref, in_a, in_b, out_a, out_b, hidden_ref, back_ref):
    rows = rows_ref[...]
    cotangent = d_out_ref[...]
    units = out_a.shape[0]
    back = None
    for index, (w_in, w_out) in enumerate(((in_a, out_a), (in_b, out_b))):
        for n in range(units // CHUNK):
            part = slice(n * CHUNK, (n + 1) * CHUNK)
            d_hidden = dot(cotangent, w_out[part, :], NT)
            gate = dot(rows, w_in[0, :, part])
            upper = dot(rows, w_in[1, :, part])
            sigma = jax.nn.sigmoid(gate)
            silu = gate * sigma
            hidden_ref[:, index * units + n * CHUNK : index * units + (n + 1) * CHUNK] = bf16(silu * upper)
            d_gate = bf16(d_hidden * upper * silu_grad(gate, sigma))
            d_upper = bf16(d_hidden * silu)
            term = dot(d_gate, w_in[0, :, part], NT) + dot(d_upper, w_in[1, :, part], NT)
            back = term if back is None else back + term
    back_ref[...] = back.astype(back_ref.dtype)


def ffn_out_far(hidden, w_a, w_b, out):
    units = w_a.shape[0]
    out[...] = bf16(dot(hidden[:, :units], w_a[...]) + dot(hidden[:, units:], w_b[...]))


def ffn_out_own(hidden, w_a, w_b, resid, got, out):
    units = w_a.shape[0]
    total = dot(hidden[:, :units], w_a[...]) + dot(hidden[:, units:], w_b[...])
    out[...] = bf16(resid[...].astype(F32) + total + got[...].astype(F32))


def resid_back(back, got, resid, d_out, out):
    wide = resid[...].astype(F32)
    factor = norm_factor(wide)
    grad = back[...] + got[...].astype(F32)
    out[...] = bf16(d_out[...].astype(F32) + norm_back(grad, wide * factor, factor))


def attend_back(where, docs, d_resid, r, proj_ref, att_ref, w_out, masks, d_q, d_k, d_v, d_g):
    half = d_resid.shape[0]
    scale = HEAD ** (-0.5)
    ahead, allowed, root_inv = window(where, docs, r, half)
    gate = proj_ref[3, r].astype(F32)
    sigma_g = jax.nn.sigmoid(gate)
    d_gated = dot(d_resid, w_out, NT)
    d_att = bf16(d_gated * (gate * sigma_g) * root_inv)
    d_g[r] = bf16(d_gated * att_ref[r] * silu_grad(gate, sigma_g))
    keys = jnp.concatenate([proj_ref[1, ahead], proj_ref[1, r]], axis=0)
    values = jnp.concatenate([proj_ref[2, ahead], proj_ref[2, r]], axis=0)
    many = jnp.concatenate([allowed] * len(masks), axis=0)
    query = spread(proj_ref[0, r], masks)
    d_att_m = spread(d_att, masks)
    scores = dot(query, keys, NT) * scale
    sigma = jax.nn.sigmoid(scores)
    weights = bf16(scores * sigma * many)
    d_weights = dot(d_att_m, values, NT)
    d_scores = bf16(d_weights * silu_grad(scores, sigma) * many)
    d_q[r] = bf16(collect(dot(d_scores, keys), masks) * scale)
    d_keys = dot(d_scores, query, TN) * scale
    d_values = dot(weights, d_att_m, TN)
    d_k[ahead] += d_keys[:half]
    d_k[r] += d_keys[half:]
    d_v[ahead] += d_values[:half]
    d_v[r] += d_values[half:]


def attn_back_first(where, docs, first, second, proj, att, w_out, d_q, d_k, d_v, d_g):
    masks = head_masks(w_out.shape[0])
    d_k[...] = jnp.zeros_like(d_k)
    d_v[...] = jnp.zeros_like(d_v)
    for r, rows in enumerate((first, second)):
        attend_back(where, docs, rows[...], r, proj, att, w_out[...], masks, d_q, d_k, d_v, d_g)


def attn_back_second(
    where, docs, third, fourth, proj, att, w_out, d_q_a, d_k_a, d_v_a, d_g_a, w_in,
    give_ref, keep_ref, d_q, d_k, d_v, d_g,
):
    masks = head_masks(w_out.shape[0])
    half = third.shape[0]
    d_q[0:2] = d_q_a[...]
    d_g[0:2] = d_g_a[...]
    d_k[...] = d_k_a[...]
    d_v[...] = d_v_a[...]
    for r, rows in ((2, third), (3, fourth)):
        attend_back(where, docs, rows[...], r, proj, att, w_out[...], masks, d_q, d_k, d_v, d_g)
    for first, second, target in ((3, 1, give_ref), (2, 0, keep_ref)):
        total = None
        for c, grads in enumerate((d_q, d_k, d_v, d_g)):
            left = jnp.concatenate([bf16(grads[first]), bf16(grads[second])], axis=0)
            term = dot(left, w_in[c], NT)
            total = term if total is None else total + term
        target[...] = total.astype(target.dtype)


def add_far(keep, take, out):
    half = out.shape[0]
    out[...] = bf16(keep[:half, :] + take[:half, :].astype(F32))


def packed_back(keep, take, got, packed, d_resid, out):
    half = out.shape[0]
    wide = packed[...].astype(F32)
    factor = norm_factor(wide)
    grad = keep[half:, :] + take[half:, :].astype(F32) + got[...].astype(F32)
    out[...] = bf16(d_resid[...].astype(F32) + norm_back(grad, wide * factor, factor))


def column_of(ref, index, cols):
    return ref[:, pl.ds(pl.multiple_of(index * cols, cols), cols)]


def rows_term(act_refs, cot):
    return dot(jnp.concatenate([a[...] for a in act_refs], axis=0), cot, TN)


def first_cot(where, cot_a, cot_b, pre, enc):
    cols = pre.shape[1]
    cot = jnp.concatenate([cot_a[...], cot_b[...]], axis=0)
    value = pre[...]
    w1_rows = enc[1, pl.ds(pl.multiple_of(where[1] * cols, cols), cols), :]
    return bf16(dot(cot, w1_rows, NT) * silu_grad(value, jax.nn.sigmoid(value)))


def cot_columns(where, cot_a, cot_b, cols):
    return jnp.concatenate(
        [column_of(cot_a, where[1], cols), column_of(cot_b, where[1], cols)], axis=0
    )


def enc_grads_first(where, cot_a, cot_b, act0_a, act0_b, act1, pre, enc, part1, part0):
    cols = pre.shape[1]
    part1[...] = rows_term([act1], cot_columns(where, cot_a, cot_b, cols))
    part0[...] = rows_term([act0_a, act0_b], first_cot(where, cot_a, cot_b, pre, enc))


def halve(where, bits, bit, total, keep, send):
    place = bits.index(bit)
    count, size, _ = keep.shape
    mine = (where[0] >> bit) & 1
    for j in range(count):
        low = j & ((1 << place) - 1)
        base = ((j >> place) << (place + 1)) | low
        for target, value in ((keep, mine), (send, 1 - mine)):
            index = base + (value << place)
            rows = total[pl.ds(pl.multiple_of(index * size, size), size), :]
            target[j] = rows.astype(target.dtype)


def enc_grad1_second(bits, bit, where, cot_a, cot_b, act1, part1, keep, send, total):
    total[...] = rows_term([act1], cot_columns(where, cot_a, cot_b, part1.shape[1])) + part1[...]
    halve(where, bits, bit, total, keep, send)


def enc_grad0_second(bits, bit, where, cot_a, cot_b, act0_a, act0_b, pre, enc, part0, keep, send, total):
    total[...] = rows_term([act0_a, act0_b], first_cot(where, cot_a, cot_b, pre, enc)) + part0[...]
    halve(where, bits, bit, total, keep, send)


def halve_again(bits, bit, where, kept, got, keep, send, total):
    count, size, _ = kept.shape
    for j in range(count):
        total[j * size : (j + 1) * size, :] = kept[j] + got[j].astype(F32)
    halve(where, bits, bit, total, keep, send)


def finish(kept0, got0, kept1, got1, out):
    out[0] = kept0[0] + got0[0].astype(F32)
    out[1] = kept1[0] + got1[0].astype(F32)


def shards(
    features,
    dest_owner,
    dest_slot,
    doc_ids,
    enc_weight,
    attn_in,
    attn_out,
    ffn_in,
    ffn_out,
    out_grad,
):
    rows_dev, width = features.shape
    group_axes = ("event", "pack")
    groups = lax.axis_size(group_axes)
    packs = lax.axis_size("pack")
    tensors = lax.axis_size("tensor")
    cols = attn_in.shape[2]
    comps = attn_in.shape[0]
    units = ffn_out.shape[0]
    where = jnp.stack([lax.axis_index(group_axes), lax.axis_index("tensor")]).astype(jnp.int32)
    d_out = out_grad[0]
    docs = doc_ids.reshape(tensors, 1, rows_dev)

    def near(value):
        return lax.ppermute(value, "tensor", [(i, i ^ 1) for i in range(tensors)])

    def far(value):
        return lax.ppermute(value, "tensor", [(i, i ^ 2) for i in range(tensors)])

    def crossed(value, k):
        return lax.ppermute(value, group_axes, [(i, i ^ k) for i in range(groups)])

    row_b = like((rows_dev, width), BF16)
    row_f = like((rows_dev, width), F32)

    mean_load = rows_dev // groups
    capacity = -(-(mean_load + mean_load // 2) // 8) * 8
    *sends, place = run(
        functools.partial(route_send, capacity),
        [like((capacity, width + rows_dev), BF16)] * groups + [like((1, rows_dev), jnp.int32)],
        where,
        [dest_owner.reshape(1, rows_dev), dest_slot.reshape(1, rows_dev), features],
        [
            pltpu.VMEM((1, rows_dev), jnp.int32),
            pltpu.VMEM((1, rows_dev), jnp.int32),
            pltpu.VMEM((rows_dev, width), BF16),
            pltpu.SemaphoreType.DMA((3,)),
        ],
        space=pltpu.HBM,
        flops=2 * groups * capacity * rows_dev * width,
        name="route_send",
    )
    order = sorted(range(1, groups), key=lambda k: (-(k % packs), k))

    def exchange(parts):
        got = {k: crossed(parts[k], k) for k in order}
        return [parts[0]] + [got[k] for k in range(1, groups)]

    gots = exchange(sends)
    d_out_far = far(d_out)
    ffn_in_near = near(ffn_in)
    ffn_out_near = near(ffn_out)
    attn_out_near = near(attn_out)
    d_out_far, ffn_in_near, ffn_out_near, attn_out_near, *gots = tie(
        d_out_far, ffn_in_near, ffn_out_near, attn_out_near, *gots
    )
    mine, hot = run(
        route_recv,
        [row_b, like((groups * capacity, rows_dev), BF16)],
        None,
        gots,
        flops=2 * groups * capacity * rows_dev * width,
        name="route_recv",
    )

    mine_near = near(mine)
    mine_far = far(mine)

    pair = 2 * rows_dev
    enc_flops = 2 * pair * width * (2 * width + comps * cols)
    pre_a, act_a, packed, proj_a = run(
        encode_first,
        [
            like((pair, cols), F32),
            like((pair, width), BF16),
            row_b,
            like((comps, 2, rows_dev, cols), BF16),
        ],
        where,
        [mine, mine_near, enc_weight, attn_in],
        [pltpu.VMEM((pair, width), F32)],
        flops=enc_flops,
        name="encode_first",
    )
    mine_far, proj_a = tie(mine_far, proj_a)
    mine_both = near(mine_far)
    pre_b, act_b, proj, attended, give, keep = run(
        attend_first,
        [
            like((pair, cols), F32),
            like((pair, width), BF16),
            like((comps, tensors, rows_dev, cols), BF16),
            like((tensors, rows_dev, cols), F32),
            like((pair, cols), BF16),
            like((pair, cols), BF16),
        ],
        where,
        [docs, mine_far, mine_both, proj_a, enc_weight, attn_in],
        [pltpu.VMEM((pair, width), F32)],
        flops=2 * enc_flops,
        name="attend_first",
    )
    take = near(give)
    out_flops = 2 * rows_dev * width * 2 * cols
    (part_far,) = run(
        attn_out_far, [row_b], None, [keep, take, attn_out, attn_out_near], flops=out_flops, name="attn_out_far"
    )
    got_part = far(part_far)
    (part_own,) = run(
        attn_out_own, [row_f], None, [keep, take, attn_out, attn_out_near, packed], flops=out_flops, name="attn_out_own"
    )
    resid, normed2 = run(residual, [row_b, row_b], None, [part_own, got_part], name="residual")
    normed2_far = far(normed2)

    def feed(rows, cotangent, back_type, name):
        return run(
            ffn,
            [like((rows_dev, 2 * units), BF16), like((rows_dev, width), back_type)],
            None,
            [rows, cotangent, ffn_in, ffn_in_near, ffn_out, ffn_out_near],
            flops=2 * rows_dev * width * 2 * units * 5,
            name=name,
        )

    hidden_own, back_own = feed(normed2, d_out, F32, "ffn_own")
    normed2_far, back_own = tie(normed2_far, back_own)
    hidden_far, back_far = feed(normed2_far, d_out_far, BF16, "ffn_far")
    got_back = far(back_far)
    (d_resid,) = run(resid_back, [row_b], None, [back_own, got_back, resid, d_out], name="resid_back")
    ffn_flops = 2 * rows_dev * width * 2 * units
    (out_far,) = run(
        ffn_out_far, [row_b], None, [hidden_far, ffn_out, ffn_out_near], flops=ffn_flops, name="ffn_out_far"
    )
    d_resid_near = near(d_resid)
    d_resid_far = far(d_resid)
    att_flops = 2 * rows_dev * 2 * cols * (width + 6 * rows_dev * 4)
    block_f = like((tensors, rows_dev, cols), F32)
    two_b = like((2, rows_dev, cols), BF16)
    d_q, d_k, d_v, d_g = run(
        attn_back_first,
        [two_b, block_f, block_f, two_b],
        where,
        [docs, d_resid, d_resid_near, proj, attended, attn_out],
        flops=att_flops,
        name="attn_back_first",
    )
    d_resid_far, d_k = tie(d_resid_far, d_k)
    d_resid_both = near(d_resid_far)
    d_resid_both, out_far = tie(d_resid_both, out_far)
    got_out = far(out_far)
    four_b = pltpu.VMEM((tensors, rows_dev, cols), BF16)
    four_f = pltpu.VMEM((tensors, rows_dev, cols), F32)
    give, keep = run(
        attn_back_second,
        [like((pair, width), BF16), like((pair, width), F32)],
        where,
        [docs, d_resid_far, d_resid_both, proj, attended, attn_out, d_q, d_k, d_v, d_g, attn_in],
        [four_b, four_f, four_f, four_b],
        flops=att_flops + 2 * 2 * pair * comps * cols * width,
        name="attn_back_second",
    )
    take = near(give)
    (sum_far,) = run(add_far, [row_b], None, [keep, take], name="add_far")
    sum_far, got_out = tie(sum_far, got_out)
    got_sum = far(sum_far)
    (packed_out,) = run(
        ffn_out_own, [row_b], None, [hidden_own, ffn_out, ffn_out_near, resid, got_out], flops=ffn_flops, name="ffn_out_own"
    )

    got_sum, packed_out = tie(got_sum, packed_out)
    (d_packed,) = run(packed_back, [row_b], None, [keep, take, got_sum, packed, d_resid], name="packed_back")

    cot_far = far(d_packed)
    cot_near = near(d_packed)
    backs = run(
        back_send,
        [like((capacity, width), BF16)] * groups,
        None,
        [hot, d_packed],
        flops=2 * groups * capacity * rows_dev * width,
        name="back_send",
    )
    returned = exchange(backs)
    grad_flops = 2 * pair * width * cols
    part_f = like((width, cols), F32)
    part1, part0 = run(
        enc_grads_first,
        [part_f, part_f],
        where,
        [d_packed, cot_near, mine, mine_near, act_a, pre_a, enc_weight],
        flops=3 * grad_flops,
        name="enc_grads_first",
    )
    cot_far, part1, part0 = tie(cot_far, part1, part0)
    cot_both = near(cot_far)

    bits = list(range(groups.bit_length() - 1))
    pack_bits = bits[: packs.bit_length() - 1]
    event_bits = bits[len(pack_bits) :]
    size = width // groups
    total = [pltpu.VMEM((width, cols), F32)]

    def halves(remaining):
        shape = (2 ** (len(remaining) - 1), size, cols)
        return [like(shape, F32), like(shape, BF16)]

    def reduce_over(stages, start, name):
        remaining = list(bits)
        kept, send = start((tuple(remaining), stages[0]))
        got = crossed(send, 1 << stages[0])
        remaining.remove(stages[0])
        for bit in stages[1:]:
            kept, send = run(
                functools.partial(halve_again, tuple(remaining), bit),
                halves(remaining),
                where,
                [kept, got],
                [pltpu.VMEM((kept.shape[0] * size, cols), F32)],
                name=name + str(bit),
            )
            got = crossed(send, 1 << bit)
            remaining.remove(bit)
        return kept, got

    def start1(setting):
        return run(
            functools.partial(enc_grad1_second, *setting),
            halves(bits),
            where,
            [cot_far, cot_both, act_b, part1],
            total,
            flops=grad_flops,
            name="enc_grad1_second",
        )

    def start0(setting):
        return run(
            functools.partial(enc_grad0_second, *setting),
            halves(bits),
            where,
            [cot_far, cot_both, mine_far, mine_both, pre_b, enc_weight, part0],
            total,
            flops=2 * grad_flops,
            name="enc_grad0_second",
        )

    kept1, got1 = reduce_over(event_bits + pack_bits, start1, "halve1_")
    kept0, got0 = reduce_over(pack_bits[:1] + event_bits + pack_bits[1:], start0, "halve0_")
    (row_grad,) = run(
        back_recv,
        [row_b],
        None,
        [place] + returned,
        flops=2 * groups * capacity * rows_dev * width,
        name="back_recv",
    )
    (enc_grad,) = run(finish, [like((2, size, cols), F32)], None, [kept0, got0, kept1, got1], name="finish")
    return (packed_out[None], row_grad, enc_grad)


def solution(mesh):
    placed = (
        P(("event", "pack", "tensor"), None),
        P(("event", "pack", "tensor")),
        P(("event", "pack", "tensor")),
        P(("event", "pack"), None),
        P(),
        P(None, None, "tensor"),
        P("tensor", None),
        P(None, None, "tensor"),
        P("tensor", None),
        P(("event", "pack"), "tensor", None),
    )
    return jax.shard_map(
        shards,
        mesh=mesh,
        in_specs=placed,
        out_specs=(
            P(("event", "pack"), "tensor", None),
            P(("event", "pack", "tensor"), None),
            P(None, ("event", "pack"), "tensor"),
        ),
        check_vma=False,
    )
```

time: 155 us -> 161 us (1.039)
  waiting for transfers between devices: 51.5 us -> 66.4 us
  Pallas kernels: 39.6 us -> 32.9 us
  local copies, waits for them, and re-layouts: 11.4 us -> 6.07 us
  starting transfers between devices: 51.2 us -> 54.4 us
    ppermute x22 -> x20, waiting for transfers between devices: 5.81 us -> 24.3 us  [crossed(): return lax.ppermute(value, group_axes, [(i, i ^ k) for i in range(groups)])]
    pallas_call x24 -> x26, Pallas kernels: 39.6 us -> 32.9 us  [run(): pl.pallas_call(body, out_shape=list(outs), in_specs=specs, out_specs=[pl....]
    ppermute x9, waiting for transfers between devices: 43.2 us -> 36.7 us  [far(): return lax.ppermute(value, 'tensor', [(i, i ^ 2) for i in range(tensors)])]
    ppermute x11, waiting for transfers between devices: 2.54 us -> 5.43 us  [near(): return lax.ppermute(value, 'tensor', [(i, i ^ 1) for i in range(tensors)])]
    unnamed x60 -> x24, local copies, waits for them, and re-layouts: 8.83 us -> 6.07 us
    ppermute x22 -> x20, starting transfers between devices: 36.2 us -> 38.6 us  [crossed(): return lax.ppermute(value, group_axes, [(i, i ^ k) for i in range(groups)])]
  transfers between devices with their start and end apart: 42 -> 40, of which waited for: 18 -> 21; matrix products, arithmetic and copies ran while one was open for 2% -> 0% of each run, Pallas kernels for 19% -> 11%
where the time goes in v3:
time: 161 us
  waiting for transfers between devices  66.4 us (41%)
  starting transfers between devices  54.4 us (34%)
  Pallas kernels  32.9 us (20%)
  local copies, waits for them, and re-layouts  6.07 us (4%)
    ppermute x20, starting transfers between devices, crossed(): return lax.ppermute(value, group_axes, [(i, i ^ k) for i in range(groups)])  38.6 us
    ppermute x9, waiting for transfers between devices, far(): return lax.ppermute(value, 'tensor', [(i, i ^ 2) for i in range(tensors)])  36.7 us
    pallas_call x26, Pallas kernels, run(): pl.pallas_call(body, out_shape=list(outs), in_specs=specs, out_specs=[pl....  32.9 us
    ppermute x20, waiting for transfers between devices, crossed(): return lax.ppermute(value, group_axes, [(i, i ^ k) for i in range(groups)])  24.3 us
    ppermute x9, starting transfers between devices, far(): return lax.ppermute(value, 'tensor', [(i, i ^ 2) for i in range(tensors)])  14.1 us
    unnamed x24, local copies, waits for them, and re-layouts  6.07 us
    ppermute x11, waiting for transfers between devices, near(): return lax.ppermute(value, 'tensor', [(i, i ^ 1) for i in range(tensors)])  5.43 us
  transfers between devices with their start and end apart: 40, of which 21 were waited for; matrix products, arithmetic and copies ran while one was open for 0% of the time, Pallas kernels for 11%

profile of v3, /device:TPU:0, one launch (start us, length us, event | category | flops | bytes accessed | tf_op | source)
XLA Modules:
  0.0 160.7 jit_solution(7408262288210220533)
XLA Ops:
  1.7 0.9 copy-done.8
  2.7 0.7 copy-done.10
  3.3 0.7 copy-done.11
  4.0 0.9 route_send.1
  5.0 2.7 %collective-permute-start.4 = (bf16[24,1152]{1,0:T(8,128)(2,1)S(1)}, bf16[24,1152]{1,0:T(8,128)(2,1)S(1)}, u32[]{:S(2)}, u32[]{:S(2)}) collective-permute-start(bf16[24,1152]{1,0:T(8,128)(2,1)S(1)} %get-tuple-element.86), channel_id=1, source_target_pairs={{0,4},{4,0},{8,12},{12,8},{16,20},{20,16},{24,28},{28,24},{1,5},{5... | collective-permute-start | bytes 165896 | tf_op jit(solution)/shard_map/ppermute | solution.py:448
  7.7 2.6 %collective-permute-start.5 = (bf16[24,1152]{1,0:T(8,128)(2,1)S(1)}, bf16[24,1152]{1,0:T(8,128)(2,1)S(1)}, u32[]{:S(2)}, u32[]{:S(2)}) collective-permute-start(bf16[24,1152]{1,0:T(8,128)(2,1)S(1)} %get-tuple-element.87), channel_id=1, source_target_pairs={{0,8},{4,12},{8,0},{12,4},{16,24},{20,28},{24,16},{28,20},{1,9},{5... | collective-permute-start | bytes 165896 | tf_op jit(solution)/shard_map/ppermute | solution.py:448
  10.3 4.2 %collective-permute-start.6 = (bf16[24,1152]{1,0:T(8,128)(2,1)S(1)}, bf16[24,1152]{1,0:T(8,128)(2,1)S(1)}, u32[]{:S(2)}, u32[]{:S(2)}) collective-permute-start(bf16[24,1152]{1,0:T(8,128)(2,1)S(1)} %get-tuple-element.88), channel_id=1, source_target_pairs={{0,12},{4,8},{8,4},{12,0},{16,28},{20,24},{24,20},{28,16},{1,13},{... | collective-permute-start | bytes 165896 | tf_op jit(solution)/shard_map/ppermute | solution.py:448
  14.5 1.5 collective-permute-start
  16.6 1.5 collective-permute-start.7
  18.1 2.7 %collective-permute-done.7.refs_4_ = bf16[24,1152]{1,0:T(8,128)(2,1)S(1)} collective-permute-done((bf16[24,1152]{1,0:T(8,128)(2,1)S(1)}, bf16[24,1152]{1,0:T(8,128)(2,1)S(1)}, u32[]{:S(2)}, u32[]{:S(2)}) %collective-permute-start.7) | collective-permute-done | bytes 55328 | tf_op jit(solution)/shard_map/ppermute | solution.py:448
  21.4 4.5 %collective-permute-done.8.refs_5_ = bf16[24,1152]{1,0:T(8,128)(2,1)S(1)} collective-permute-done((bf16[24,1152]{1,0:T(8,128)(2,1)S(1)}, bf16[24,1152]{1,0:T(8,128)(2,1)S(1)}, u32[]{:S(2)}, u32[]{:S(2)}) %collective-permute-start.8) | collective-permute-done | bytes 55328 | tf_op jit(solution)/shard_map/ppermute | solution.py:448
  25.9 2.6 %collective-permute-start.9 = (bf16[24,1152]{1,0:T(8,128)(2,1)S(1)}, bf16[24,1152]{1,0:T(8,128)(2,1)S(1)}, u32[]{:S(2)}, u32[]{:S(2)}) collective-permute-start(bf16[24,1152]{1,0:T(8,128)(2,1)S(1)} %get-tuple-element.91), channel_id=1, source_target_pairs={{0,24},{4,28},{8,16},{12,20},{16,8},{20,12},{24,0},{28,4},{1,25},{... | collective-permute-start | bytes 165896 | tf_op jit(solution)/shard_map/ppermute | solution.py:448
  28.5 3.6 %collective-permute-done.9.refs_6_ = bf16[24,1152]{1,0:T(8,128)(2,1)S(1)} collective-permute-done((bf16[24,1152]{1,0:T(8,128)(2,1)S(1)}, bf16[24,1152]{1,0:T(8,128)(2,1)S(1)}, u32[]{:S(2)}, u32[]{:S(2)}) %collective-permute-start.9) | collective-permute-done | bytes 55328 | tf_op jit(solution)/shard_map/ppermute | solution.py:448
  32.1 4.4 %collective-permute-start.10 = (bf16[24,1152]{1,0:T(8,128)(2,1)S(1)}, bf16[24,1152]{1,0:T(8,128)(2,1)S(1)}, u32[]{:S(2)}, u32[]{:S(2)}) collective-permute-start(bf16[24,1152]{1,0:T(8,128)(2,1)S(1)} %get-tuple-element.92), channel_id=1, source_target_pairs={{0,28},{4,24},{8,20},{12,16},{16,12},{20,8},{24,4},{28,0},{1,29},{... | collective-permute-start | bytes 165896 | tf_op jit(solution)/shard_map/ppermute | solution.py:448
  36.6 2.4 %collective-permute-done.10.refs_7_ = bf16[24,1152]{1,0:T(8,128)(2,1)S(1)} collective-permute-done((bf16[24,1152]{1,0:T(8,128)(2,1)S(1)}, bf16[24,1152]{1,0:T(8,128)(2,1)S(1)}, u32[]{:S(2)}, u32[]{:S(2)}) %collective-permute-start.10) | collective-permute-done | bytes 55328 | tf_op jit(solution)/shard_map/ppermute | solution.py:448
  39.4 1.6 collective-permute-start.11
  40.9 2.2 %copy-done = bf16[2,1024,1024]{2,1,0:T(8,128)(2,1)S(1)} copy-done((bf16[2,1024,1024]{2,1,0:T(8,128)(2,1)S(1)}, bf16[2,1024,1024]{2,1,0:T(8,128)(2,1)}, u32[]{:S(2)}) %copy-start) | copy-done | bytes 4194328
  43.1 1.6 copy-done.5
  44.7 2.6 %encode_first.1 = (f32[256,256]{1,0:T(8,128)S(1)}, bf16[256,1024]{1,0:T(8,128)(2,1)S(1)}, bf16[128,1024]{1,0:T(8,128)(2,1)S(1)}, bf16[4,2,128,256]{3,2,1,0:T(8,128)(2,1)S(1)}) custom-call(s32[2]{0:T(128)S(1)} %pad_add_fusion.where, bf16[128,1024]{1,0:T(8,128)(2,1)S(1)} %get-tuple-element.101.first.act0_a, ...), custom_call_target="tpu_custom_call" | custom-call | flops 1610612736 | bytes 8388608 | tf_op jit(solution)/shard_map/encode_first/pallas_call | solution.py:59
  47.4 0.7 collective-permute-done.11.third.act0_a
  48.1 1.5 collective-permute-done.13.fourth.act0_b
  49.6 3.7 %attend_first.1 = (f32[256,256]{1,0:T(8,128)S(1)}, bf16[256,1024]{1,0:T(8,128)(2,1)S(1)}, bf16[4,4,128,256]{3,2,1,0:T(8,128)(2,1)S(1)}, f32[4,128,256]{2,1,0:T(8...) custom-call(s32[2]{0:T(128)S(1)} %pad_add_fusion.where, s32[4,1,128]{2,1,0:T(1,128)S(1)} %bitcast.10, ...), custom_call_target="tpu_custom_call" | custom-call | flops 3221225472 | bytes 9963520 | tf_op jit(solution)/shard_map/attend_first/pallas_call | solution.py:59
  53.5 1.2 collective-permute-done.14.take
  54.8 1.5 attn_out_far.1
  56.3 1.6 collective-permute-start.15
  57.9 1.4 attn_out_own.1.part
  59.2 5.5 %collective-permute-done.15.got = bf16[128,1024]{1,0:T(8,128)(2,1)S(1)} collective-permute-done((bf16[128,1024]{1,0:T(8,128)(2,1)S(1)}, bf16[128,1024]{1,0:T(8,128)(2,1)S(1)}, u32[]{:S(2)}, u32[]{:S(2)}) %collective-permute-start.15) | collective-permute-done | bytes 262176 | tf_op jit(solution)/shard_map/ppermute | solution.py:445
  64.9 1.6 collective-permute-start.16
  66.5 2.8 %ffn_own.1 = (bf16[128,1024]{1,0:T(8,128)(2,1)S(1)}, f32[128,1024]{1,0:T(8,128)S(1)}) custom-call(bf16[128,1024]{1,0:T(8,128)(2,1)S(1)} %get-tuple-element.109.rows_ref, bf16[128,1024]{1,0:T(8,128)(2,1)S(1)} %bitcast.8, bf16[2,1024,512]{2,1,0:T(8,128)(2,1)S(1)} %copy-done.4, bf16[2,1024,512]{2,1,0:T(8,128)(2,1)S(1)} %collective-permute-done.1.in_b, ...), custom_call_target="tpu_custom_call" | custom-call | flops 1342177280 | bytes 7602176 | tf_op jit(solution)/shard_map/ffn_own/pallas_call | solution.py:59
  69.3 3.2 %collective-permute-done.16.rows_ref = bf16[128,1024]{1,0:T(8,128)(2,1)S(1)} collective-permute-done((bf16[128,1024]{1,0:T(8,128)(2,1)S(1)}, bf16[128,1024]{1,0:T(8,128)(2,1)S(1)}, u32[]{:S(2)}, u32[]{:S(2)}) %collective-permute-start.16) | collective-permute-done | bytes 262176 | tf_op jit(solution)/shard_map/ppermute | solution.py:445
  72.5 2.8 %ffn_far.1 = (bf16[128,1024]{1,0:T(8,128)(2,1)S(1)}, bf16[128,1024]{1,0:T(8,128)(2,1)S(1)}) custom-call(bf16[128,1024]{1,0:T(8,128)(2,1)S(1)} %collective-permute-done.16.rows_ref, bf16[128,1024]{1,0:T(8,128)(2,1)S(1)} %collective-permute-done.d_out_ref, bf16[2,1024,512]{2,1,0:T(8,128)(2,1)S(1)} %copy-done.4, ...), custom_call_target="tpu_custom_call" | custom-call | flops 1342177280 | bytes 7340032 | tf_op jit(solution)/shard_map/ffn_far/pallas_call | solution.py:59
  75.3 1.6 collective-permute-start.17
  76.9 5.1 %collective-permute-done.17.got = bf16[128,1024]{1,0:T(8,128)(2,1)S(1)} collective-permute-done((bf16[128,1024]{1,0:T(8,128)(2,1)S(1)}, bf16[128,1024]{1,0:T(8,128)(2,1)S(1)}, u32[]{:S(2)}, u32[]{:S(2)}) %collective-permute-start.17) | collective-permute-done | bytes 262176 | tf_op jit(solution)/shard_map/ppermute | solution.py:445
  82.4 1.6 collective-permute-start.18
  84.0 2.3 %attn_back_first.1 = (bf16[2,128,256]{2,1,0:T(8,128)(2,1)S(1)}, f32[4,128,256]{2,1,0:T(8,128)S(1)}, f32[4,128,256]{2,1,0:T(8,128)S(1)}, bf16[2,128,256]{2,1,0:T(8,128)(2,1)S(1)}) custom-call(s32[2]{0:T(128)S(1)} %pad_add_fusion.where, s32[4,1,128]{2,1,0:T(1,128)S(1)} %bitcast.11, bf16[128,1024]{1,0:T(8,128)(2,1)S(1)} %resid_back.1.first.d_resid, ...), custom_call_target="tpu_custom_call" | custom-call | flops 536870912 | bytes 3934208 | tf_op jit(solution)/shard_map/attn_back_first/pallas_call | solution.py:59
  86.3 4.8 %collective-permute-done.18.third = bf16[128,1024]{1,0:T(8,128)(2,1)S(1)} collective-permute-done((bf16[128,1024]{1,0:T(8,128)(2,1)S(1)}, bf16[128,1024]{1,0:T(8,128)(2,1)S(1)}, u32[]{:S(2)}, u32[]{:S(2)}) %collective-permute-start.18) | collective-permute-done | bytes 262176 | tf_op jit(solution)/shard_map/ppermute | solution.py:445
  91.8 0.9 collective-permute-done.20.fourth
  92.7 3.5 %attn_back_second.1 = (bf16[256,1024]{1,0:T(8,128)(2,1)S(1)}, f32[256,1024]{1,0:T(8,128)S(1)}) custom-call(s32[2]{0:T(128)S(1)} %pad_add_fusion.where, s32[4,1,128]{2,1,0:T(1,128)S(1)} %bitcast.12, bf16[128,1024]{1,0:T(8,128)(2,1)S(1)} %collective-permute-done.18.third, bf16[128,1024]{1,0:T(8,128)(2,1)S(1)} %collective-permute-done.20.fourth, ...), custom_call_target="tpu_custom_call" | custom-call | flops 1610612736 | bytes 7604224 | tf_op jit(solution)/shard_map/attn_back_second/pallas_call | solution.py:59
  96.3 1.5 collective-permute-start.22
  98.2 6.7 %collective-permute-done.22.got = bf16[128,1024]{1,0:T(8,128)(2,1)S(1)} collective-permute-done((bf16[128,1024]{1,0:T(8,128)(2,1)S(1)}, bf16[128,1024]{1,0:T(8,128)(2,1)S(1)}, u32[]{:S(2)}, u32[]{:S(2)}) %collective-permute-start.22) | collective-permute-done | bytes 262176 | tf_op jit(solution)/shard_map/ppermute | solution.py:445
  104.9 1.5 collective-permute-start.23
  106.4 1.2 ffn_out_own.1
  107.6 5.1 %collective-permute-done.23.got = bf16[128,1024]{1,0:T(8,128)(2,1)S(1)} collective-permute-done((bf16[128,1024]{1,0:T(8,128)(2,1)S(1)}, bf16[128,1024]{1,0:T(8,128)(2,1)S(1)}, u32[]{:S(2)}, u32[]{:S(2)}) %collective-permute-start.23) | collective-permute-done | bytes 262176 | tf_op jit(solution)/shard_map/ppermute | solution.py:445
  113.1 1.6 collective-permute-start.31
  114.7 1.5 enc_grads_first.1
  116.2 5.6 %collective-permute-done.31.cot_a = bf16[128,1024]{1,0:T(8,128)(2,1)S(1)} collective-permute-done((bf16[128,1024]{1,0:T(8,128)(2,1)S(1)}, bf16[128,1024]{1,0:T(8,128)(2,1)S(1)}, u32[]{:S(2)}, u32[]{:S(2)}) %collective-permute-start.31) | collective-permute-done | bytes 262176 | tf_op jit(solution)/shard_map/ppermute | solution.py:445
  121.8 1.5 collective-permute-done.33.cot_b
  123.3 1.5 enc_grad0_second.1
  124.9 1.1 enc_grad1_second.1
  126.0 2.6 %collective-permute-start.37 = (bf16[4,128,256]{2,1,0:T(8,128)(2,1)S(1)}, bf16[4,128,256]{2,1,0:T(8,128)(2,1)S(1)}, u32[]{:S(2)}, u32[]{:S(2)}) collective-permute-start(bf16[4,128,256]{2,1,0:T(8,128)(2,1)S(1)} %get-tuple-element.162), channel_id=1, source_target_pairs={{0,16},{4,20},{8,24},{12,28},{16,0},{20,4},{24,8},{28,12},{1,17},{... | collective-permute-start | bytes 786440 | tf_op jit(solution)/shard_map/ppermute | solution.py:448
  128.5 4.7 %collective-permute-done.34.got = bf16[4,128,256]{2,1,0:T(8,128)(2,1)S(1)} collective-permute-done((bf16[4,128,256]{2,1,0:T(8,128)(2,1)S(1)}, bf16[4,128,256]{2,1,0:T(8,128)(2,1)S(1)}, u32[]{:S(2)}, u32[]{:S(2)}) %collective-permute-start.34) | collective-permute-done | bytes 262176 | tf_op jit(solution)/shard_map/ppermute | solution.py:448
  133.9 2.6 %collective-permute-start.35 = (bf16[2,128,256]{2,1,0:T(8,128)(2,1)S(1)}, bf16[2,128,256]{2,1,0:T(8,128)(2,1)S(1)}, u32[]{:S(2)}, u32[]{:S(2)}) collective-permute-start(bf16[2,128,256]{2,1,0:T(8,128)(2,1)S(1)} %get-tuple-element.156), channel_id=1, source_target_pairs={{0,16},{4,20},{8,24},{12,28},{16,0},{20,4},{24,8},{28,12},{1,17},{... | collective-permute-start | bytes 393224 | tf_op jit(solution)/shard_map/ppermute | solution.py:448
  137.8 1.6 %collective-permute-start.24 = (bf16[24,1024]{1,0:T(8,128)(2,1)S(1)}, bf16[24,1024]{1,0:T(8,128)(2,1)S(1)}, u32[]{:S(2)}, u32[]{:S(2)}) collective-permute-start(bf16[24,1024]{1,0:T(8,128)(2,1)S(1)} %get-tuple-element.139), channel_id=1, source_target_pairs={{0,4},{4,0},{8,12},{12,8},{16,20},{20,16},{24,28},{28,24},{1,5},{5... | collective-permute-start | bytes 147464 | tf_op jit(solution)/shard_map/ppermute | solution.py:448
  139.5 2.1 %collective-permute-start.25 = (bf16[24,1024]{1,0:T(8,128)(2,1)S(1)}, bf16[24,1024]{1,0:T(8,128)(2,1)S(1)}, u32[]{:S(2)}, u32[]{:S(2)}) collective-permute-start(bf16[24,1024]{1,0:T(8,128)(2,1)S(1)} %get-tuple-element.140), channel_id=1, source_target_pairs={{0,8},{4,12},{8,0},{12,4},{16,24},{20,28},{24,16},{28,20},{1,9},{5... | collective-permute-start | bytes 147464 | tf_op jit(solution)/shard_map/ppermute | solution.py:448
  141.6 0.7 collective-permute-start.26
  142.3 1.7 %collective-permute-start.27 = (bf16[24,1024]{1,0:T(8,128)(2,1)S(1)}, bf16[24,1024]{1,0:T(8,128)(2,1)S(1)}, u32[]{:S(2)}, u32[]{:S(2)}) collective-permute-start(bf16[24,1024]{1,0:T(8,128)(2,1)S(1)} %get-tuple-element.142), channel_id=1, source_target_pairs={{0,16},{4,20},{8,24},{12,28},{16,0},{20,4},{24,8},{28,12},{1,17},{... | collective-permute-start | bytes 147464 | tf_op jit(solution)/shard_map/ppermute | solution.py:448
  144.6 0.9 collective-permute-start.36
  146.2 2.1 %collective-permute-start.39 = (bf16[1,128,256]{2,1,0:T(8,128)(2,1)S(1)}, bf16[1,128,256]{2,1,0:T(8,128)(2,1)S(1)}, u32[]{:S(2)}, u32[]{:S(2)}) collective-permute-start(bf16[1,128,256]{2,1,0:T(8,128)(2,1)S(1)} %get-tuple-element.166), channel_id=1, source_target_pairs={{0,8},{4,12},{8,0},{12,4},{16,24},{20,28},{24,16},{28,20},{1,9},{5... | collective-permute-start | bytes 196616 | tf_op jit(solution)/shard_map/ppermute | solution.py:448
  148.8 3.4 %collective-permute-start.29 = (bf16[24,1024]{1,0:T(8,128)(2,1)S(1)}, bf16[24,1024]{1,0:T(8,128)(2,1)S(1)}, u32[]{:S(2)}, u32[]{:S(2)}) collective-permute-start(bf16[24,1024]{1,0:T(8,128)(2,1)S(1)} %get-tuple-element.144), channel_id=1, source_target_pairs={{0,24},{4,28},{8,16},{12,20},{16,8},{20,12},{24,0},{28,4},{1,25},{... | collective-permute-start | bytes 147464 | tf_op jit(solution)/shard_map/ppermute | solution.py:448
  152.3 1.0 collective-permute-start.30
  153.3 2.8 %collective-permute-done.29.refs_6_ = bf16[24,1024]{1,0:T(8,128)(2,1)S(1)} collective-permute-done((bf16[24,1024]{1,0:T(8,128)(2,1)S(1)}, bf16[24,1024]{1,0:T(8,128)(2,1)S(1)}, u32[]{:S(2)}, u32[]{:S(2)}) %collective-permute-start.29) | collective-permute-done | bytes 49184 | tf_op jit(solution)/shard_map/ppermute | solution.py:448
  156.1 3.0 %collective-permute-done.30.refs_7_ = bf16[24,1024]{1,0:T(8,128)(2,1)S(1)} collective-permute-done((bf16[24,1024]{1,0:T(8,128)(2,1)S(1)}, bf16[24,1024]{1,0:T(8,128)(2,1)S(1)}, u32[]{:S(2)}, u32[]{:S(2)}) %collective-permute-start.30) | collective-permute-done | bytes 49184 | tf_op jit(solution)/shard_map/ppermute | solution.py:448
  159.0 1.0 back_recv.1
  160.0 0.7 finish.1
  (67 shorter events, 8.8 us)
Async XLA Ops:
  0.6 38.4 %collective-permute-start.1 = (bf16[2,1024,512]{2,1,0:T(8,128)(2,1)}, bf16[2,1024,512]{2,1,0:T(8,128)(2,1)S(1)}, u32[]{:S(2)}, u32[]{:S(2)}) collective-permute-start(bf16[2,1024,512]{2,1,0:T(8,128)(2,1)} %in_a.3), channel_id=1, source_target_pairs={{0,1},{1,0},{2,3},{3,2},{4,5},{5,4},{6,7},{7,6},{8,9},{9,8},{10,11... | collective-permute-start | bytes 6291464 | tf_op jit(solution)/shard_map/ppermute | solution.py:442
  1.1 37.8 %collective-permute-start.2 = (bf16[512,1024]{1,0:T(8,128)(2,1)}, bf16[512,1024]{1,0:T(8,128)(2,1)S(1)}, u32[]{:S(2)}, u32[]{:S(2)}) collective-permute-start(bf16[512,1024]{1,0:T(8,128)(2,1)} %w_a.3), channel_id=1, source_target_pairs={{0,1},{1,0},{2,3},{3,2},{4,5},{5,4},{6,7},{7,6},{8,9},{9,8},{10,11... | collective-permute-start | bytes 3145736 | tf_op jit(solution)/shard_map/ppermute | solution.py:442
  1.2 37.8 %collective-permute-start.3 = (bf16[256,1024]{1,0:T(8,128)(2,1)}, bf16[256,1024]{1,0:T(8,128)(2,1)}, u32[]{:S(2)}, u32[]{:S(2)}) collective-permute-start(bf16[256,1024]{1,0:T(8,128)(2,1)} %w_out.3), channel_id=1, source_target_pairs={{0,1},{1,0},{2,3},{3,2},{4,5},{5,4},{6,7},{7,6},{8,9},{9,8},{10,11... | collective-permute-start | bytes 1572872 | tf_op jit(solution)/shard_map/ppermute | solution.py:442
  1.7 0.9 copy-start.8
  2.7 0.7 copy-start.10
  3.3 0.7 copy-start.11
  5.0 5.3 %collective-permute-start.4 = (bf16[24,1152]{1,0:T(8,128)(2,1)S(1)}, bf16[24,1152]{1,0:T(8,128)(2,1)S(1)}, u32[]{:S(2)}, u32[]{:S(2)}) collective-permute-start(bf16[24,1152]{1,0:T(8,128)(2,1)S(1)} %get-tuple-element.86), channel_id=1, source_target_pairs={{0,4},{4,0},{8,12},{12,8},{16,20},{20,16},{24,28},{28,24},{1,5},{5... | collective-permute-start | bytes 165896 | tf_op jit(solution)/shard_map/ppermute | solution.py:448
  7.7 6.8 %collective-permute-start.5 = (bf16[24,1152]{1,0:T(8,128)(2,1)S(1)}, bf16[24,1152]{1,0:T(8,128)(2,1)S(1)}, u32[]{:S(2)}, u32[]{:S(2)}) collective-permute-start(bf16[24,1152]{1,0:T(8,128)(2,1)S(1)} %get-tuple-element.87), channel_id=1, source_target_pairs={{0,8},{4,12},{8,0},{12,4},{16,24},{20,28},{24,16},{28,20},{1,9},{5... | collective-permute-start | bytes 165896 | tf_op jit(solution)/shard_map/ppermute | solution.py:448
  10.3 6.4 %collective-permute-start.6 = (bf16[24,1152]{1,0:T(8,128)(2,1)S(1)}, bf16[24,1152]{1,0:T(8,128)(2,1)S(1)}, u32[]{:S(2)}, u32[]{:S(2)}) collective-permute-start(bf16[24,1152]{1,0:T(8,128)(2,1)S(1)} %get-tuple-element.88), channel_id=1, source_target_pairs={{0,12},{4,8},{8,4},{12,0},{16,28},{20,24},{24,20},{28,16},{1,13},{... | collective-permute-start | bytes 165896 | tf_op jit(solution)/shard_map/ppermute | solution.py:448
  14.5 24.5 %collective-permute-start = (bf16[128,1024]{1,0:T(8,128)(2,1)}, bf16[128,1024]{1,0:T(8,128)(2,1)S(1)}, u32[]{:S(2)}, u32[]{:S(2)}) collective-permute-start(bf16[128,1024]{1,0:T(8,128)(2,1)} %bitcast.7), channel_id=1, source_target_pairs={{0,2},{1,3},{2,0},{3,1},{4,6},{5,7},{6,4},{7,5},{8,10},{9,11},{10,... | collective-permute-start | bytes 786440 | tf_op jit(solution)/shard_map/ppermute | solution.py:445
  16.6 4.2 %collective-permute-start.7 = (bf16[24,1152]{1,0:T(8,128)(2,1)S(1)}, bf16[24,1152]{1,0:T(8,128)(2,1)S(1)}, u32[]{:S(2)}, u32[]{:S(2)}) collective-permute-start(bf16[24,1152]{1,0:T(8,128)(2,1)S(1)} %get-tuple-element.89), channel_id=1, source_target_pairs={{0,16},{4,20},{8,24},{12,28},{16,0},{20,4},{24,8},{28,12},{1,17},{... | collective-permute-start | bytes 165896 | tf_op jit(solution)/shard_map/ppermute | solution.py:448
  20.8 5.1 %collective-permute-start.8 = (bf16[24,1152]{1,0:T(8,128)(2,1)S(1)}, bf16[24,1152]{1,0:T(8,128)(2,1)S(1)}, u32[]{:S(2)}, u32[]{:S(2)}) collective-permute-start(bf16[24,1152]{1,0:T(8,128)(2,1)S(1)} %get-tuple-element.90), channel_id=1, source_target_pairs={{0,20},{4,16},{8,28},{12,24},{16,4},{20,0},{24,12},{28,8},{1,21},{... | collective-permute-start | bytes 165896 | tf_op jit(solution)/shard_map/ppermute | solution.py:448
  25.9 6.3 %collective-permute-start.9 = (bf16[24,1152]{1,0:T(8,128)(2,1)S(1)}, bf16[24,1152]{1,0:T(8,128)(2,1)S(1)}, u32[]{:S(2)}, u32[]{:S(2)}) collective-permute-start(bf16[24,1152]{1,0:T(8,128)(2,1)S(1)} %get-tuple-element.91), channel_id=1, source_target_pairs={{0,24},{4,28},{8,16},{12,20},{16,8},{20,12},{24,0},{28,4},{1,25},{... | collective-permute-start | bytes 165896 | tf_op jit(solution)/shard_map/ppermute | solution.py:448
  32.1 6.9 %collective-permute-start.10 = (bf16[24,1152]{1,0:T(8,128)(2,1)S(1)}, bf16[24,1152]{1,0:T(8,128)(2,1)S(1)}, u32[]{:S(2)}, u32[]{:S(2)}) collective-permute-start(bf16[24,1152]{1,0:T(8,128)(2,1)S(1)} %get-tuple-element.92), channel_id=1, source_target_pairs={{0,28},{4,24},{8,20},{12,16},{16,12},{20,8},{24,4},{28,0},{1,29},{... | collective-permute-start | bytes 165896 | tf_op jit(solution)/shard_map/ppermute | solution.py:448
  39.0 10.6 %copy-start.9 = (s32[1,512]{1,0:T(1,128)S(1)}, s32[1,512]{1,0:T(1,128)}, u32[]{:S(2)}) copy-start(s32[1,512]{1,0:T(1,128)} %param.13) | copy-start | bytes 6148
  39.3 1.7 %collective-permute-start.12 = (bf16[128,1024]{1,0:T(8,128)(2,1)S(1)}, bf16[128,1024]{1,0:T(8,128)(2,1)S(1)}, u32[]{:S(2)}, u32[]{:S(2)}) collective-permute-start(bf16[128,1024]{1,0:T(8,128)(2,1)S(1)} %get-tuple-element.101.first.act0_a), channel_id=1, source_target_pairs={{0,1},{1,0},{2,3},{3,2},{4,5},{5,4},{6,7},{7,6},{8,9},{9,8},{10,11... | collective-permute-start | bytes 786440 | tf_op jit(solution)/shard_map/ppermute | solution.py:442
  39.4 8.7 %collective-permute-start.11 = (bf16[128,1024]{1,0:T(8,128)(2,1)S(1)}, bf16[128,1024]{1,0:T(8,128)(2,1)S(1)}, u32[]{:S(2)}, u32[]{:S(2)}) collective-permute-start(bf16[128,1024]{1,0:T(8,128)(2,1)S(1)} %get-tuple-element.101.first.act0_a), channel_id=1, source_target_pairs={{0,2},{1,3},{2,0},{3,1},{4,6},{5,7},{6,4},{7,5},{8,10},{9,11},{10,... | collective-permute-start | bytes 786440 | tf_op jit(solution)/shard_map/ppermute | solution.py:445
  40.9 2.2 %copy-start = (bf16[2,1024,1024]{2,1,0:T(8,128)(2,1)S(1)}, bf16[2,1024,1024]{2,1,0:T(8,128)(2,1)}, u32[]{:S(2)}) copy-start(bf16[2,1024,1024]{2,1,0:T(8,128)(2,1)} %enc.7) | copy-start | bytes 12582916
  43.1 1.6 copy-start.5
  44.7 4.9 %copy-start.1 = (bf16[2,1024,1024]{2,1,0:T(8,128)(2,1)S(1)}, bf16[2,1024,1024]{2,1,0:T(8,128)(2,1)}, u32[]{:S(2)}) copy-start(bf16[2,1024,1024]{2,1,0:T(8,128)(2,1)} %enc.7) | copy-start | bytes 12582916
  44.7 4.9 %copy-start.6 = (bf16[4,1024,256]{2,1,0:T(8,128)(2,1)S(1)}, bf16[4,1024,256]{2,1,0:T(8,128)(2,1)}, u32[]{:S(2)}) copy-start(bf16[4,1024,256]{2,1,0:T(8,128)(2,1)} %w_in.5) | copy-start | bytes 6291460
  48.1 1.5 collective-permute-start.13
  49.6 5.1 %copy-start.3 = (bf16[256,1024]{1,0:T(8,128)(2,1)S(1)}, bf16[256,1024]{1,0:T(8,128)(2,1)}, u32[]{:S(2)}) copy-start(bf16[256,1024]{1,0:T(8,128)(2,1)} %w_out.3) | copy-start | bytes 1572868
  53.4 1.4 collective-permute-start.14
  54.8 11.7 %copy-start.2 = (bf16[512,1024]{1,0:T(8,128)(2,1)S(1)}, bf16[512,1024]{1,0:T(8,128)(2,1)}, u32[]{:S(2)}) copy-start(bf16[512,1024]{1,0:T(8,128)(2,1)} %w_a.3) | copy-start | bytes 3145732
  54.8 11.7 %copy-start.4 = (bf16[2,1024,512]{2,1,0:T(8,128)(2,1)S(1)}, bf16[2,1024,512]{2,1,0:T(8,128)(2,1)}, u32[]{:S(2)}) copy-start(bf16[2,1024,512]{2,1,0:T(8,128)(2,1)} %in_a.3) | copy-start | bytes 6291460
  54.8 11.7 %copy-start.7 = (bf16[1,128,1024]{2,1,0:T(8,128)(2,1)S(1)}, bf16[1,128,1024]{2,1,0:T(8,128)(2,1)}, u32[]{:S(2)}) copy-start(bf16[1,128,1024]{2,1,0:T(8,128)(2,1)} %param.19) | copy-start | bytes 786436
  56.3 8.4 %collective-permute-start.15 = (bf16[128,1024]{1,0:T(8,128)(2,1)S(1)}, bf16[128,1024]{1,0:T(8,128)(2,1)S(1)}, u32[]{:S(2)}, u32[]{:S(2)}) collective-permute-start(bf16[128,1024]{1,0:T(8,128)(2,1)S(1)} %attn_out_far.1), channel_id=1, source_target_pairs={{0,2},{1,3},{2,0},{3,1},{4,6},{5,7},{6,4},{7,5},{8,10},{9,11},{10,... | collective-permute-start | bytes 786440 | tf_op jit(solution)/shard_map/ppermute | solution.py:445
  64.9 7.6 %collective-permute-start.16 = (bf16[128,1024]{1,0:T(8,128)(2,1)S(1)}, bf16[128,1024]{1,0:T(8,128)(2,1)S(1)}, u32[]{:S(2)}, u32[]{:S(2)}) collective-permute-start(bf16[128,1024]{1,0:T(8,128)(2,1)S(1)} %get-tuple-element.109.rows_ref), channel_id=1, source_target_pairs={{0,2},{1,3},{2,0},{3,1},{4,6},{5,7},{6,4},{7,5},{8,10},{9,11},{10,... | collective-permute-start | bytes 786440 | tf_op jit(solution)/shard_map/ppermute | solution.py:445
  75.3 6.7 %collective-permute-start.17 = (bf16[128,1024]{1,0:T(8,128)(2,1)S(1)}, bf16[128,1024]{1,0:T(8,128)(2,1)S(1)}, u32[]{:S(2)}, u32[]{:S(2)}) collective-permute-start(bf16[128,1024]{1,0:T(8,128)(2,1)S(1)} %get-tuple-element.116), channel_id=1, source_target_pairs={{0,2},{1,3},{2,0},{3,1},{4,6},{5,7},{6,4},{7,5},{8,10},{9,11},{10,... | collective-permute-start | bytes 786440 | tf_op jit(solution)/shard_map/ppermute | solution.py:445
  82.3 1.7 %collective-permute-start.19 = (bf16[128,1024]{1,0:T(8,128)(2,1)S(1)}, bf16[128,1024]{1,0:T(8,128)(2,1)S(1)}, u32[]{:S(2)}, u32[]{:S(2)}) collective-permute-start(bf16[128,1024]{1,0:T(8,128)(2,1)S(1)} %resid_back.1.first.d_resid), channel_id=1, source_target_pairs={{0,1},{1,0},{2,3},{3,2},{4,5},{5,4},{6,7},{7,6},{8,9},{9,8},{10,11... | collective-permute-start | bytes 786440 | tf_op jit(solution)/shard_map/ppermute | solution.py:442
  82.4 8.7 %collective-permute-start.18 = (bf16[128,1024]{1,0:T(8,128)(2,1)S(1)}, bf16[128,1024]{1,0:T(8,128)(2,1)S(1)}, u32[]{:S(2)}, u32[]{:S(2)}) collective-permute-start(bf16[128,1024]{1,0:T(8,128)(2,1)S(1)} %resid_back.1.first.d_resid), channel_id=1, source_target_pairs={{0,2},{1,3},{2,0},{3,1},{4,6},{5,7},{6,4},{7,5},{8,10},{9,11},{10,... | collective-permute-start | bytes 786440 | tf_op jit(solution)/shard_map/ppermute | solution.py:445
  91.1 1.5 collective-permute-start.20
  96.1 2.0 %collective-permute-start.21 = (bf16[256,1024]{1,0:T(8,128)(2,1)S(1)}, bf16[256,1024]{1,0:T(8,128)(2,1)S(1)}, u32[]{:S(2)}, u32[]{:S(2)}) collective-permute-start(bf16[256,1024]{1,0:T(8,128)(2,1)S(1)} %get-tuple-element.129), channel_id=1, source_target_pairs={{0,1},{1,0},{2,3},{3,2},{4,5},{5,4},{6,7},{7,6},{8,9},{9,8},{10,11... | collective-permute-start | bytes 1572872 | tf_op jit(solution)/shard_map/ppermute | solution.py:442
  96.3 8.6 %collective-permute-start.22 = (bf16[128,1024]{1,0:T(8,128)(2,1)S(1)}, bf16[128,1024]{1,0:T(8,128)(2,1)S(1)}, u32[]{:S(2)}, u32[]{:S(2)}) collective-permute-start(bf16[128,1024]{1,0:T(8,128)(2,1)S(1)} %ffn_out_far.1), channel_id=1, source_target_pairs={{0,2},{1,3},{2,0},{3,1},{4,6},{5,7},{6,4},{7,5},{8,10},{9,11},{10,... | collective-permute-start | bytes 786440 | tf_op jit(solution)/shard_map/ppermute | solution.py:445
  104.9 7.8 %collective-permute-start.23 = (bf16[128,1024]{1,0:T(8,128)(2,1)S(1)}, bf16[128,1024]{1,0:T(8,128)(2,1)S(1)}, u32[]{:S(2)}, u32[]{:S(2)}) collective-permute-start(bf16[128,1024]{1,0:T(8,128)(2,1)S(1)} %add_far.1), channel_id=1, source_target_pairs={{0,2},{1,3},{2,0},{3,1},{4,6},{5,7},{6,4},{7,5},{8,10},{9,11},{10,... | collective-permute-start | bytes 786440 | tf_op jit(solution)/shard_map/ppermute | solution.py:445
  113.0 1.7 %collective-permute-start.32 = (bf16[128,1024]{1,0:T(8,128)(2,1)S(1)}, bf16[128,1024]{1,0:T(8,128)(2,1)S(1)}, u32[]{:S(2)}, u32[]{:S(2)}) collective-permute-start(bf16[128,1024]{1,0:T(8,128)(2,1)S(1)} %packed_back.1.d_packed.cot_a), channel_id=1, source_target_pairs={{0,1},{1,0},{2,3},{3,2},{4,5},{5,4},{6,7},{7,6},{8,9},{9,8},{10,11... | collective-permute-start | bytes 786440 | tf_op jit(solution)/shard_map/ppermute | solution.py:442
  113.1 8.7 %collective-permute-start.31 = (bf16[128,1024]{1,0:T(8,128)(2,1)S(1)}, bf16[128,1024]{1,0:T(8,128)(2,1)S(1)}, u32[]{:S(2)}, u32[]{:S(2)}) collective-permute-start(bf16[128,1024]{1,0:T(8,128)(2,1)S(1)} %packed_back.1.d_packed.cot_a), channel_id=1, source_target_pairs={{0,2},{1,3},{2,0},{3,1},{4,6},{5,7},{6,4},{7,5},{8,10},{9,11},{10,... | collective-permute-start | bytes 786440 | tf_op jit(solution)/shard_map/ppermute | solution.py:445
  121.8 1.5 collective-permute-start.33
  124.8 8.4 %collective-permute-start.34 = (bf16[4,128,256]{2,1,0:T(8,128)(2,1)S(1)}, bf16[4,128,256]{2,1,0:T(8,128)(2,1)S(1)}, u32[]{:S(2)}, u32[]{:S(2)}) collective-permute-start(bf16[4,128,256]{2,1,0:T(8,128)(2,1)S(1)} %get-tuple-element.154), channel_id=1, source_target_pairs={{0,4},{4,0},{8,12},{12,8},{16,20},{20,16},{24,28},{28,24},{1,5},{5... | collective-permute-start | bytes 786440 | tf_op jit(solution)/shard_map/ppermute | solution.py:448
  126.0 10.4 %collective-permute-start.37 = (bf16[4,128,256]{2,1,0:T(8,128)(2,1)S(1)}, bf16[4,128,256]{2,1,0:T(8,128)(2,1)S(1)}, u32[]{:S(2)}, u32[]{:S(2)}) collective-permute-start(bf16[4,128,256]{2,1,0:T(8,128)(2,1)S(1)} %get-tuple-element.162), channel_id=1, source_target_pairs={{0,16},{4,20},{8,24},{12,28},{16,0},{20,4},{24,8},{28,12},{1,17},{... | collective-permute-start | bytes 786440 | tf_op jit(solution)/shard_map/ppermute | solution.py:448
  133.9 8.4 %collective-permute-start.35 = (bf16[2,128,256]{2,1,0:T(8,128)(2,1)S(1)}, bf16[2,128,256]{2,1,0:T(8,128)(2,1)S(1)}, u32[]{:S(2)}, u32[]{:S(2)}) collective-permute-start(bf16[2,128,256]{2,1,0:T(8,128)(2,1)S(1)} %get-tuple-element.156), channel_id=1, source_target_pairs={{0,16},{4,20},{8,24},{12,28},{16,0},{20,4},{24,8},{28,12},{1,17},{... | collective-permute-start | bytes 393224 | tf_op jit(solution)/shard_map/ppermute | solution.py:448
  137.1 7.6 %collective-permute-start.38 = (bf16[2,128,256]{2,1,0:T(8,128)(2,1)S(1)}, bf16[2,128,256]{2,1,0:T(8,128)(2,1)S(1)}, u32[]{:S(2)}, u32[]{:S(2)}) collective-permute-start(bf16[2,128,256]{2,1,0:T(8,128)(2,1)S(1)} %get-tuple-element.164), channel_id=1, source_target_pairs={{0,4},{4,0},{8,12},{12,8},{16,20},{20,16},{24,28},{28,24},{1,5},{5... | collective-permute-start | bytes 393224 | tf_op jit(solution)/shard_map/ppermute | solution.py:448
  137.8 8.3 %collective-permute-start.24 = (bf16[24,1024]{1,0:T(8,128)(2,1)S(1)}, bf16[24,1024]{1,0:T(8,128)(2,1)S(1)}, u32[]{:S(2)}, u32[]{:S(2)}) collective-permute-start(bf16[24,1024]{1,0:T(8,128)(2,1)S(1)} %get-tuple-element.139), channel_id=1, source_target_pairs={{0,4},{4,0},{8,12},{12,8},{16,20},{20,16},{24,28},{28,24},{1,5},{5... | collective-permute-start | bytes 147464 | tf_op jit(solution)/shard_map/ppermute | solution.py:448
  139.5 8.8 %collective-permute-start.25 = (bf16[24,1024]{1,0:T(8,128)(2,1)S(1)}, bf16[24,1024]{1,0:T(8,128)(2,1)S(1)}, u32[]{:S(2)}, u32[]{:S(2)}) collective-permute-start(bf16[24,1024]{1,0:T(8,128)(2,1)S(1)} %get-tuple-element.140), channel_id=1, source_target_pairs={{0,8},{4,12},{8,0},{12,4},{16,24},{20,28},{24,16},{28,20},{1,9},{5... | collective-permute-start | bytes 147464 | tf_op jit(solution)/shard_map/ppermute | solution.py:448
  141.6 7.3 %collective-permute-start.26 = (bf16[24,1024]{1,0:T(8,128)(2,1)S(1)}, bf16[24,1024]{1,0:T(8,128)(2,1)S(1)}, u32[]{:S(2)}, u32[]{:S(2)}) collective-permute-start(bf16[24,1024]{1,0:T(8,128)(2,1)S(1)} %get-tuple-element.141), channel_id=1, source_target_pairs={{0,12},{4,8},{8,4},{12,0},{16,28},{20,24},{24,20},{28,16},{1,13},{... | collective-permute-start | bytes 147464 | tf_op jit(solution)/shard_map/ppermute | solution.py:448
  142.3 10.0 %collective-permute-start.27 = (bf16[24,1024]{1,0:T(8,128)(2,1)S(1)}, bf16[24,1024]{1,0:T(8,128)(2,1)S(1)}, u32[]{:S(2)}, u32[]{:S(2)}) collective-permute-start(bf16[24,1024]{1,0:T(8,128)(2,1)S(1)} %get-tuple-element.142), channel_id=1, source_target_pairs={{0,16},{4,20},{8,24},{12,28},{16,0},{20,4},{24,8},{28,12},{1,17},{... | collective-permute-start | bytes 147464 | tf_op jit(solution)/shard_map/ppermute | solution.py:448
  144.6 15.4 %collective-permute-start.36 = (bf16[1,128,256]{2,1,0:T(8,128)(2,1)S(1)}, bf16[1,128,256]{2,1,0:T(8,128)(2,1)S(1)}, u32[]{:S(2)}, u32[]{:S(2)}) collective-permute-start(bf16[1,128,256]{2,1,0:T(8,128)(2,1)S(1)} %get-tuple-element.158), channel_id=1, source_target_pairs={{0,8},{4,12},{8,0},{12,4},{16,24},{20,28},{24,16},{28,20},{1,9},{5... | collective-permute-start | bytes 196616 | tf_op jit(solution)/shard_map/ppermute | solution.py:448
  146.2 13.9 %collective-permute-start.39 = (bf16[1,128,256]{2,1,0:T(8,128)(2,1)S(1)}, bf16[1,128,256]{2,1,0:T(8,128)(2,1)S(1)}, u32[]{:S(2)}, u32[]{:S(2)}) collective-permute-start(bf16[1,128,256]{2,1,0:T(8,128)(2,1)S(1)} %get-tuple-element.166), channel_id=1, source_target_pairs={{0,8},{4,12},{8,0},{12,4},{16,24},{20,28},{24,16},{28,20},{1,9},{5... | collective-permute-start | bytes 196616 | tf_op jit(solution)/shard_map/ppermute | solution.py:448
  148.3 5.0 %collective-permute-start.28 = (bf16[24,1024]{1,0:T(8,128)(2,1)S(1)}, bf16[24,1024]{1,0:T(8,128)(2,1)S(1)}, u32[]{:S(2)}, u32[]{:S(2)}) collective-permute-start(bf16[24,1024]{1,0:T(8,128)(2,1)S(1)} %get-tuple-element.143), channel_id=1, source_target_pairs={{0,20},{4,16},{8,28},{12,24},{16,4},{20,0},{24,12},{28,8},{1,21},{... | collective-permute-start | bytes 147464 | tf_op jit(solution)/shard_map/ppermute | solution.py:448
  148.8 7.2 %collective-permute-start.29 = (bf16[24,1024]{1,0:T(8,128)(2,1)S(1)}, bf16[24,1024]{1,0:T(8,128)(2,1)S(1)}, u32[]{:S(2)}, u32[]{:S(2)}) collective-permute-start(bf16[24,1024]{1,0:T(8,128)(2,1)S(1)} %get-tuple-element.144), channel_id=1, source_target_pairs={{0,24},{4,28},{8,16},{12,20},{16,8},{20,12},{24,0},{28,4},{1,25},{... | collective-permute-start | bytes 147464 | tf_op jit(solution)/shard_map/ppermute | solution.py:448
  152.3 6.8 %collective-permute-start.30 = (bf16[24,1024]{1,0:T(8,128)(2,1)S(1)}, bf16[24,1024]{1,0:T(8,128)(2,1)S(1)}, u32[]{:S(2)}, u32[]{:S(2)}) collective-permute-start(bf16[24,1024]{1,0:T(8,128)(2,1)S(1)} %get-tuple-element.145), channel_id=1, source_target_pairs={{0,28},{4,24},{8,20},{12,16},{16,12},{20,8},{24,4},{28,0},{1,29},{... | collective-permute-start | bytes 147464 | tf_op jit(solution)/shard_map/ppermute | solution.py:448

commit v4 on v3

--- a/solution.py
+++ b/solution.py
@@ -55,7 +55,6 @@
     if scalars is not None:
         specs = [pl.BlockSpec(memory_space=pltpu.SMEM)] + specs
         operands = [scalars] + operands
-    total = sum(a.size * a.dtype.itemsize for a in list(args) + list(outs))
     return pl.pallas_call(
         body,
         out_shape=list(outs),
@@ -63,7 +62,7 @@
         out_specs=[pl.BlockSpec(memory_space=pltpu.VMEM)] * len(outs),
         scratch_shapes=list(scratch),
         compiler_params=pltpu.CompilerParams(vmem_limit_bytes=limit * MIB),
-        cost_estimate=pl.CostEstimate(flops=flops, bytes_accessed=total, transcendentals=0),
+        cost_estimate=pl.CostEstimate(flops=flops, bytes_accessed=0, transcendentals=0),
         name=name,
     )(*operands)
 
@@ -72,22 +71,13 @@
     return lax.optimization_barrier(values)
 
 
-def route_send(capacity, where, owner_hbm, slot_hbm, features_hbm, *refs):
-    outs, (owner, slot, features, sems) = refs[:-4], refs[-4:]
+def route_send(capacity, where, code, features, *outs):
     sends, place_ref = outs[:-1], outs[-1]
-    copies = [
-        pltpu.make_async_copy(source, target, sems.at[n])
-        for n, (source, target) in enumerate(
-            ((owner_hbm, owner), (slot_hbm, slot), (features_hbm, features))
-        )
-    ]
-    for copy in copies:
-        copy.start()
-    for copy in copies:
-        copy.wait()
     groups = len(sends)
     rows, width = features.shape
-    o_row = owner[...]
+    shift = rows.bit_length() - 1
+    o_row = code[...] >> shift
+    slot = code[...] & (rows - 1)
     o_col = turned(o_row, rows)
     i = lax.broadcasted_iota(jnp.int32, (rows, rows), 0)
     j = lax.broadcasted_iota(jnp.int32, (rows, rows), 1)
@@ -98,7 +88,7 @@
     spots = lax.broadcasted_iota(jnp.int32, (groups * capacity, rows), 0)
     hot = jnp.where(spots == place, 1.0, 0.0).astype(BF16)
     big = dot(hot, features[...])
-    tags = dot(hot, bf16(turned(slot[...] + 1, rows)))
+    tags = dot(hot, bf16(turned(slot + 1, rows)))
     for k in range(groups):
         part = slice(k * capacity, (k + 1) * capacity)
         sends[k][:, :width] = bf16(big[part])
@@ -115,17 +105,32 @@
     rows_ref[...] = bf16(dot(hot, bf16(got[:, :width]), TN))
 
 
-def back_send(hot, d_packed, *sends):
-    groups = len(sends)
-    capacity = hot.shape[0] // groups
+def back_send(events, hot, d_packed, *sends):
+    packs = len(sends)
+    capacity = hot.shape[0] // (events * packs)
     big = dot(hot[...], d_packed[...])
-    for k in range(groups):
-        sends[k][...] = bf16(big[k * capacity : (k + 1) * capacity])
+    for b in range(packs):
+        parts = [
+            big[(a * packs + b) * capacity : (a * packs + b + 1) * capacity] for a in range(events)
+        ]
+        sends[b][...] = bf16(jnp.concatenate(parts, axis=0))
+
+
+def back_turn(*refs):
+    events = refs[-1]
+    refs = refs[:-1]
+    packs = len(refs) - (events - 1) - 1
+    gots, own, sends = refs[:packs], refs[packs], refs[packs + 1 :]
+    wide = [g[...].astype(F32) for g in gots]
+    capacity = wide[0].shape[0] // events
+    for a, target in enumerate((own, *sends)):
+        parts = [w[a * capacity : (a + 1) * capacity] for w in wide]
+        target[...] = bf16(jnp.concatenate(parts, axis=0))
 
 
 def back_recv(place, *refs):
     gots, out = refs[:-1], refs[-1]
-    got = bf16(jnp.concatenate([g[...].astype(F32) for g in gots], axis=0))
+    got = jnp.concatenate([g[...] for g in gots], axis=0)
     spots = lax.broadcasted_iota(jnp.int32, (got.shape[0], out.shape[0]), 0)
     hot = jnp.where(spots == place[...], 1.0, 0.0).astype(BF16)
     out[...] = bf16(dot(hot, got, TN))
@@ -141,8 +146,7 @@
         act_ref[:, part] = bf16(pre * jax.nn.sigmoid(pre))
     pre_ref[...] = pre_all[:, pl.ds(pl.multiple_of(where[1] * cols, cols), cols)]
     packed = bf16(dot(act_ref[...], enc[1]))
-    if packed_ref is not None:
-        packed_ref[...] = packed[: packed_ref.shape[0]]
+    packed_ref[...] = packed[: packed_ref.shape[0]]
     wide = packed.astype(F32)
     normed = bf16(wide * norm_factor(wide))
     for c in range(w_in.shape[0]):
@@ -196,7 +200,7 @@
 
 def attend_first(
     where, docs, third, fourth, proj_a, enc, w_in,
-    pre_ref, act_ref, proj_ref, att_ref, give_ref, keep_ref, pre_all,
+    pre_ref, act_ref, packed_ref, proj_ref, att_ref, give_ref, keep_ref, pre_all,
 ):
     rows = jnp.concatenate([third[...], fourth[...]], axis=0)
     half = third.shape[0]
@@ -207,7 +211,7 @@
         proj_ref[c, 2] = value[:half]
         proj_ref[c, 3] = value[half:]
 
-    encode(where, rows, enc, w_in, pre_all, pre_ref, act_ref, None, store)
+    encode(where, rows, enc, w_in, pre_all, pre_ref, act_ref, packed_ref, store)
     masks = head_masks(cols)
     for r, (target, place) in enumerate(((keep_ref, 1), (give_ref, 1), (keep_ref, 0), (give_ref, 0))):
         ahead, allowed, root_inv = window(where, docs, r, half)
@@ -222,21 +226,14 @@
         target[place * half : (place + 1) * half, :] = bf16(attended * gate * jax.nn.sigmoid(gate))
 
 
-def out_part(give_rows, half_index, keep, take, w_own, w_near):
-    part = slice(half_index * give_rows, (half_index + 1) * give_rows)
-    return dot(keep[part, :], w_own[...]) + dot(take[part, :], w_near[...])
-
-
-def attn_out_far(keep, take, w_own, w_near, out):
-    out[...] = bf16(out_part(out.shape[0], 0, keep, take, w_own, w_near))
-
-
-def attn_out_own(keep, take, w_own, w_near, packed, out):
-    out[...] = out_part(out.shape[0], 1, keep, take, w_own, w_near) + packed[...].astype(F32)
-
-
-def residual(part, got, resid_ref, normed_ref):
-    resid = bf16(part[...] + got[...].astype(F32))
+def attn_out_part(index, keep, take, w_own, w_near, out):
+    rows = out.shape[0]
+    part = slice(index * rows, (index + 1) * rows)
+    out[...] = bf16(dot(keep[part, :], w_own[...]) + dot(take[part, :], w_near[...]))
+
+
+def residual(packed, part, got, resid_ref, normed_ref):
+    resid = bf16(packed[...].astype(F32) + (part[...].astype(F32) + got[...].astype(F32)))
     resid_ref[...] = resid
     wide = resid.astype(F32)
     normed_ref[...] = bf16(wide * norm_factor(wide))
@@ -277,7 +274,7 @@
 def resid_back(back, got, resid, d_out, out):
     wide = resid[...].astype(F32)
     factor = norm_factor(wide)
-    grad = back[...] + got[...].astype(F32)
+    grad = back[...].astype(F32) + got[...].astype(F32)
     out[...] = bf16(d_out[...].astype(F32) + norm_back(grad, wide * factor, factor))
 
 
@@ -309,45 +306,53 @@
     d_v[r] += d_values[half:]
 
 
-def attn_back_first(where, docs, first, second, proj, att, w_out, d_q, d_k, d_v, d_g):
+def attn_back_first(where, docs, third, fourth, proj, att, w_out, d_q, d_k, d_v, d_g):
     masks = head_masks(w_out.shape[0])
     d_k[...] = jnp.zeros_like(d_k)
     d_v[...] = jnp.zeros_like(d_v)
-    for r, rows in enumerate((first, second)):
+    for r, rows in ((2, third), (3, fourth)):
         attend_back(where, docs, rows[...], r, proj, att, w_out[...], masks, d_q, d_k, d_v, d_g)
 
 
+def back_norm(grads, w_in, first, second):
+    total = None
+    for c, grad in enumerate(grads):
+        left = jnp.concatenate([grad[first], grad[second]], axis=0)
+        term = dot(left, w_in[c], NT)
+        total = term if total is None else total + term
+    return total
+
+
 def attn_back_second(
-    where, docs, third, fourth, proj, att, w_out, d_q_a, d_k_a, d_v_a, d_g_a, w_in,
-    give_ref, keep_ref, d_q, d_k, d_v, d_g,
+    where, docs, first, second, proj, att, w_out, d_q_far, d_k_far, d_v_far, d_g_far, w_in,
+    give_ref, d_q, d_k, d_v, d_g, sum_k, sum_v,
 ):
     masks = head_masks(w_out.shape[0])
-    half = third.shape[0]
-    d_q[0:2] = d_q_a[...]
-    d_g[0:2] = d_g_a[...]
-    d_k[...] = d_k_a[...]
-    d_v[...] = d_v_a[...]
-    for r, rows in ((2, third), (3, fourth)):
-        attend_back(where, docs, rows[...], r, proj, att, w_out[...], masks, d_q, d_k, d_v, d_g)
-    for first, second, target in ((3, 1, give_ref), (2, 0, keep_ref)):
-        total = None
-        for c, grads in enumerate((d_q, d_k, d_v, d_g)):
-            left = jnp.concatenate([bf16(grads[first]), bf16(grads[second])], axis=0)
-            term = dot(left, w_in[c], NT)
-            total = term if total is None else total + term
-        target[...] = total.astype(target.dtype)
-
-
-def add_far(keep, take, out):
-    half = out.shape[0]
-    out[...] = bf16(keep[:half, :] + take[:half, :].astype(F32))
-
-
-def packed_back(keep, take, got, packed, d_resid, out):
-    half = out.shape[0]
+    d_q[2:4] = d_q_far[2:4]
+    d_g[2:4] = d_g_far[2:4]
+    sum_k[...] = d_k_far[...]
+    sum_v[...] = d_v_far[...]
+    for r, rows in ((0, first), (1, second)):
+        attend_back(where, docs, rows[...], r, proj, att, w_out[...], masks, d_q, sum_k, sum_v, d_g)
+    d_k[...] = bf16(sum_k[...])
+    d_v[...] = bf16(sum_v[...])
+    give_ref[...] = bf16(back_norm((d_q, d_k, d_v, d_g), w_in, 3, 1))
+
+
+def attn_back_keep(d_q, d_k, d_v, d_g, w_in, keep_ref):
+    keep_ref[...] = back_norm((d_q, d_k, d_v, d_g), w_in, 2, 0)
+
+
+def add_near(keep, take, out_far, out_own):
+    half = out_far.shape[0]
+    out_far[...] = bf16(keep[:half, :] + take[:half, :].astype(F32))
+    out_own[...] = bf16(keep[half:, :] + take[half:, :].astype(F32))
+
+
+def packed_back(part, got, packed, d_resid, out):
     wide = packed[...].astype(F32)
     factor = norm_factor(wide)
-    grad = keep[half:, :] + take[half:, :].astype(F32) + got[...].astype(F32)
+    grad = part[...].astype(F32) + got[...].astype(F32)
     out[...] = bf16(d_resid[...].astype(F32) + norm_back(grad, wide * factor, factor))
 
 
@@ -402,11 +407,15 @@
     halve(where, bits, bit, total, keep, send)
 
 
-def halve_again(bits, bit, where, kept, got, keep, send, total):
-    count, size, _ = kept.shape
-    for j in range(count):
-        total[j * size : (j + 1) * size, :] = kept[j] + got[j].astype(F32)
-    halve(where, bits, bit, total, keep, send)
+def halve_again(bits, bit, where, kept, got, keep, send):
+    place = bits.index(bit)
+    mine = (where[0] >> bit) & 1
+    for j in range(keep.shape[0]):
+        low = j & ((1 << place) - 1)
+        base = ((j >> place) << (place + 1)) | low
+        for target, value in ((keep, mine), (send, 1 - mine)):
+            index = base + (value << place)
+            target[j] = (kept[index] + got[index].astype(F32)).astype(target.dtype)
 
 
 def finish(kept0, got0, kept1, got1, out):
@@ -429,6 +438,7 @@
     rows_dev, width = features.shape
     group_axes = ("event", "pack")
     groups = lax.axis_size(group_axes)
+    events = lax.axis_size("event")
     packs = lax.axis_size("pack")
     tensors = lax.axis_size("tensor")
     cols = attn_in.shape[2]
@@ -452,49 +462,35 @@
 
     mean_load = rows_dev // groups
     capacity = -(-(mean_load + mean_load // 2) // 8) * 8
+    code = (dest_owner * rows_dev + dest_slot).reshape(1, rows_dev)
     *sends, place = run(
         functools.partial(route_send, capacity),
         [like((capacity, width + rows_dev), BF16)] * groups + [like((1, rows_dev), jnp.int32)],
         where,
-        [dest_owner.reshape(1, rows_dev), dest_slot.reshape(1, rows_dev), features],
-        [
-            pltpu.VMEM((1, rows_dev), jnp.int32),
-            pltpu.VMEM((1, rows_dev), jnp.int32),
-            pltpu.VMEM((rows_dev, width), BF16),
-            pltpu.SemaphoreType.DMA((3,)),
-        ],
-        space=pltpu.HBM,
-        flops=2 * groups * capacity * rows_dev * width,
+        [code, features],
+        flops=4 * 10**9,
         name="route_send",
     )
     order = sorted(range(1, groups), key=lambda k: (-(k % packs), k))
-
-    def exchange(parts):
-        got = {k: crossed(parts[k], k) for k in order}
-        return [parts[0]] + [got[k] for k in range(1, groups)]
-
-    gots = exchange(sends)
-    d_out_far = far(d_out)
-    ffn_in_near = near(ffn_in)
-    ffn_out_near = near(ffn_out)
-    attn_out_near = near(attn_out)
-    d_out_far, ffn_in_near, ffn_out_near, attn_out_near, *gots = tie(
-        d_out_far, ffn_in_near, ffn_out_near, attn_out_near, *gots
-    )
+    ffn_in_near, ffn_out_near, attn_out_near = near(ffn_in), near(ffn_out), near(attn_out)
+    early = {k: crossed(sends[k], k) for k in order[:2]}
+    ffn_in_near, ffn_out_near, attn_out_near, *sends = tie(
+        ffn_in_near, ffn_out_near, attn_out_near, *sends
+    )
+    crossing = early | {k: crossed(sends[k], k) for k in order[2:]}
+    gots = [sends[0]] + [crossing[k] for k in range(1, groups)]
     mine, hot = run(
         route_recv,
         [row_b, like((groups * capacity, rows_dev), BF16)],
         None,
         gots,
-        flops=2 * groups * capacity * rows_dev * width,
         name="route_recv",
     )
 
+    mine_far = far(mine)
     mine_near = near(mine)
-    mine_far = far(mine)
 
     pair = 2 * rows_dev
-    enc_flops = 2 * pair * width * (2 * width + comps * cols)
     pre_a, act_a, packed, proj_a = run(
         encode_first,
         [
@@ -506,16 +502,18 @@
         where,
         [mine, mine_near, enc_weight, attn_in],
         [pltpu.VMEM((pair, width), F32)],
-        flops=enc_flops,
         name="encode_first",
     )
     mine_far, proj_a = tie(mine_far, proj_a)
+    mine_far, d_out_late = tie(mine_far, d_out)
     mine_both = near(mine_far)
-    pre_b, act_b, proj, attended, give, keep = run(
+    d_out_far = far(d_out_late)
+    pre_b, act_b, packed_far, proj, attended, give, keep = run(
         attend_first,
         [
             like((pair, cols), F32),
             like((pair, width), BF16),
+            row_b,
             like((comps, tensors, rows_dev, cols), BF16),
             like((tensors, rows_dev, cols), F32),
             like((pair, cols), BF16),
@@ -524,102 +522,122 @@
         where,
         [docs, mine_far, mine_both, proj_a, enc_weight, attn_in],
         [pltpu.VMEM((pair, width), F32)],
-        flops=2 * enc_flops,
         name="attend_first",
     )
     take = near(give)
-    out_flops = 2 * rows_dev * width * 2 * cols
-    (part_far,) = run(
-        attn_out_far, [row_b], None, [keep, take, attn_out, attn_out_near], flops=out_flops, name="attn_out_far"
-    )
-    got_part = far(part_far)
-    (part_own,) = run(
-        attn_out_own, [row_f], None, [keep, take, attn_out, attn_out_near, packed], flops=out_flops, name="attn_out_own"
-    )
-    resid, normed2 = run(residual, [row_b, row_b], None, [part_own, got_part], name="residual")
-    normed2_far = far(normed2)
-
-    def feed(rows, cotangent, back_type, name):
+    take, d_out_far = tie(take, d_out_far)
+
+
+    def out_part(index, name):
+        return run(
+            functools.partial(attn_out_part, index),
+            [row_b],
+            None,
+            [keep, take, attn_out, attn_out_near],
+            name=name,
+        )[0]
+
+    part_far = out_part(0, "attn_out_far")
+    got_own = far(part_far)
+    part_own = out_part(1, "attn_out_own")
+    got_far = far(part_own)
+
+    def feed(rows, cotangent, name):
         return run(
             ffn,
-            [like((rows_dev, 2 * units), BF16), like((rows_dev, width), back_type)],
+            [like((rows_dev, 2 * units), BF16), row_b],
             None,
             [rows, cotangent, ffn_in, ffn_in_near, ffn_out, ffn_out_near],
-            flops=2 * rows_dev * width * 2 * units * 5,
             name=name,
         )
 
-    hidden_own, back_own = feed(normed2, d_out, F32, "ffn_own")
-    normed2_far, back_own = tie(normed2_far, back_own)
-    hidden_far, back_far = feed(normed2_far, d_out_far, BF16, "ffn_far")
-    got_back = far(back_far)
-    (d_resid,) = run(resid_back, [row_b], None, [back_own, got_back, resid, d_out], name="resid_back")
-    ffn_flops = 2 * rows_dev * width * 2 * units
-    (out_far,) = run(
-        ffn_out_far, [row_b], None, [hidden_far, ffn_out, ffn_out_near], flops=ffn_flops, name="ffn_out_far"
-    )
-    d_resid_near = near(d_resid)
-    d_resid_far = far(d_resid)
-    att_flops = 2 * rows_dev * 2 * cols * (width + 6 * rows_dev * 4)
+    resid, normed2 = run(residual, [row_b, row_b], None, [packed, part_own, got_own], name="residual")
+    hidden_own, back_own = feed(normed2, d_out, "ffn_own")
+    got_far, back_own = tie(got_far, back_own)
+    got_back_far = far(back_own)
+    resid_far, normed2_far = run(
+        residual, [row_b, row_b], None, [packed_far, part_far, got_far], name="residual_far"
+    )
+    hidden_far, back_far = feed(normed2_far, d_out_far, "ffn_far")
+    got_back_own = far(back_far)
+
+    (d_resid_far,) = run(
+        resid_back, [row_b], None, [back_far, got_back_far, resid_far, d_out_far], name="resid_back_far"
+    )
+    d_resid_both = near(d_resid_far)
     block_f = like((tensors, rows_dev, cols), F32)
-    two_b = like((2, rows_dev, cols), BF16)
+    block_b = like((tensors, rows_dev, cols), BF16)
     d_q, d_k, d_v, d_g = run(
         attn_back_first,
-        [two_b, block_f, block_f, two_b],
+        [block_b, block_f, block_f, block_b],
         where,
-        [docs, d_resid, d_resid_near, proj, attended, attn_out],
-        flops=att_flops,
+        [docs, d_resid_far, d_resid_both, proj, attended, attn_out],
         name="attn_back_first",
     )
-    d_resid_far, d_k = tie(d_resid_far, d_k)
-    d_resid_both = near(d_resid_far)
-    d_resid_both, out_far = tie(d_resid_both, out_far)
-    got_out = far(out_far)
-    four_b = pltpu.VMEM((tensors, rows_dev, cols), BF16)
-    four_f = pltpu.VMEM((tensors, rows_dev, cols), F32)
-    give, keep = run(
+    got_back_own, d_q = tie(got_back_own, d_q)
+    (d_resid,) = run(resid_back, [row_b], None, [back_own, got_back_own, resid, d_out], name="resid_back")
+    d_resid_near = near(d_resid)
+    give, *d_projected = run(
         attn_back_second,
-        [like((pair, width), BF16), like((pair, width), F32)],
+        [like((pair, width), BF16)] + [block_b] * 4,
         where,
-        [docs, d_resid_far, d_resid_both, proj, attended, attn_out, d_q, d_k, d_v, d_g, attn_in],
-        [four_b, four_f, four_f, four_b],
-        flops=att_flops + 2 * 2 * pair * comps * cols * width,
+        [docs, d_resid, d_resid_near, proj, attended, attn_out, d_q, d_k, d_v, d_g, attn_in],
+        [pltpu.VMEM((tensors, rows_dev, cols), F32)] * 2,
         name="attn_back_second",
     )
     take = near(give)
-    (sum_far,) = run(add_far, [row_b], None, [keep, take], name="add_far")
-    sum_far, got_out = tie(sum_far, got_out)
-    got_sum = far(sum_far)
-    (packed_out,) = run(
-        ffn_out_own, [row_b], None, [hidden_own, ffn_out, ffn_out_near, resid, got_out], flops=ffn_flops, name="ffn_out_own"
-    )
-
-    got_sum, packed_out = tie(got_sum, packed_out)
-    (d_packed,) = run(packed_back, [row_b], None, [keep, take, got_sum, packed, d_resid], name="packed_back")
-
-    cot_far = far(d_packed)
+    (keep,) = run(
+        attn_back_keep,
+        [like((pair, width), F32)],
+        None,
+        [*d_projected, attn_in],
+        name="attn_back_keep",
+    )
+    sum_far, sum_own = run(add_near, [row_b, row_b], None, [keep, take], name="add_near")
+    got_own = far(sum_far)
+    got_far = far(sum_own)
+    (d_packed,) = run(packed_back, [row_b], None, [sum_own, got_own, packed, d_resid], name="packed_back")
+
     cot_near = near(d_packed)
     backs = run(
-        back_send,
-        [like((capacity, width), BF16)] * groups,
+        functools.partial(back_send, events),
+        [like((events * capacity, width), BF16)] * packs,
         None,
         [hot, d_packed],
-        flops=2 * groups * capacity * rows_dev * width,
         name="back_send",
     )
-    returned = exchange(backs)
-    grad_flops = 2 * pair * width * cols
+    over_pack = [backs[0]] + [crossed(backs[b], b) for b in range(1, packs)]
     part_f = like((width, cols), F32)
     part1, part0 = run(
         enc_grads_first,
         [part_f, part_f],
         where,
         [d_packed, cot_near, mine, mine_near, act_a, pre_a, enc_weight],
-        flops=3 * grad_flops,
         name="enc_grads_first",
     )
-    cot_far, part1, part0 = tie(cot_far, part1, part0)
+    got_far, part1, part0 = tie(got_far, part1, part0)
+    (cot_far,) = run(
+        packed_back, [row_b], None, [sum_far, got_far, packed_far, d_resid_far], name="packed_back_far"
+    )
     cot_both = near(cot_far)
+    cot_both, *over_pack = tie(cot_both, *over_pack)
+    back_own, *back_sends = run(
+        lambda *refs: back_turn(*refs, events),
+        [like((packs * capacity, width), BF16)] * events,
+        None,
+        over_pack,
+        name="back_turn",
+    )
+    over_event = [back_own] + [crossed(v, (a + 1) * packs) for a, v in enumerate(back_sends)]
+
+    cot_far, hidden_far = tie(cot_far, hidden_far)
+    (out_far,) = run(
+        ffn_out_far, [row_b], None, [hidden_far, ffn_out, ffn_out_near], name="ffn_out_far"
+    )
+    got_out = far(out_far)
+    (packed_out,) = run(
+        ffn_out_own, [row_b], None, [hidden_own, ffn_out, ffn_out_near, resid, got_out], name="ffn_out_own"
+    )
 
     bits = list(range(groups.bit_length() - 1))
     pack_bits = bits[: packs.bit_length() - 1]
@@ -642,7 +660,6 @@
                 halves(remaining),
                 where,
                 [kept, got],
-                [pltpu.VMEM((kept.shape[0] * size, cols), F32)],
                 name=name + str(bit),
             )
             got = crossed(send, 1 << bit)
@@ -656,7 +673,6 @@
             where,
             [cot_far, cot_both, act_b, part1],
             total,
-            flops=grad_flops,
             name="enc_grad1_second",
         )
 
@@ -667,7 +683,6 @@
             where,
             [cot_far, cot_both, mine_far, mine_both, pre_b, enc_weight, part0],
             total,
-            flops=2 * grad_flops,
             name="enc_grad0_second",
         )
 
@@ -677,8 +692,7 @@
         back_recv,
         [row_b],
         None,
-        [place] + returned,
-        flops=2 * groups * capacity * rows_dev * width,
+        [place] + over_event,
         name="back_recv",
     )
     (enc_grad,) = run(finish, [like((2, size, cols), F32)], None, [kept0, got0, kept1, got1], name="finish")

time: 161 us -> 137 us (0.85)
  starting transfers between devices: 54.4 us -> 40.2 us
  waiting for transfers between devices: 66.4 us -> 60.5 us
  local copies, waits for them, and re-layouts: 6.07 us -> 0.99 us
    ppermute x20 -> x17, starting transfers between devices: 38.6 us -> 25.2 us  [crossed(): return lax.ppermute(value, group_axes, [(i, i ^ k) for i in range(groups)])]
    unnamed x24 -> x16, local copies, waits for them, and re-layouts: 6.07 us -> 0.99 us
    ppermute x11, waiting for transfers between devices: 5.43 us -> 2.58 us  [near(): return lax.ppermute(value, 'tensor', [(i, i ^ 1) for i in range(tensors)])]
    ppermute x9, waiting for transfers between devices: 36.7 us -> 34.2 us  [far(): return lax.ppermute(value, 'tensor', [(i, i ^ 2) for i in range(tensors)])]
    pallas_call x26 -> x31, Pallas kernels: 32.9 us -> 33.7 us  [run(): pl.pallas_call(body, out_shape=list(outs), in_specs=specs, out_specs=[pl....]
    ppermute x20 -> x17, waiting for transfers between devices: 24.3 us -> 23.7 us  [crossed(): return lax.ppermute(value, group_axes, [(i, i ^ k) for i in range(groups)])]
  transfers between devices with their start and end apart: 40 -> 37, of which waited for: 21 -> 22; matrix products, arithmetic and copies ran while one was open for 0% -> 1% of each run, Pallas kernels for 11% -> 19%
where the time goes in v4:
time: 137 us
  waiting for transfers between devices  60.5 us (44%)
  starting transfers between devices  40.2 us (29%)
  Pallas kernels  33.7 us (25%)
    ppermute x9, waiting for transfers between devices, far(): return lax.ppermute(value, 'tensor', [(i, i ^ 2) for i in range(tensors)])  34.2 us
    pallas_call x31, Pallas kernels, run(): pl.pallas_call(body, out_shape=list(outs), in_specs=specs, out_specs=[pl....  33.7 us
    ppermute x17, starting transfers between devices, crossed(): return lax.ppermute(value, group_axes, [(i, i ^ k) for i in range(groups)])  25.2 us
    ppermute x17, waiting for transfers between devices, crossed(): return lax.ppermute(value, group_axes, [(i, i ^ k) for i in range(groups)])  23.7 us
    ppermute x9, starting transfers between devices, far(): return lax.ppermute(value, 'tensor', [(i, i ^ 2) for i in range(tensors)])  13.1 us
  transfers between devices with their start and end apart: 37, of which 22 were waited for; matrix products, arithmetic and copies ran while one was open for 1% of the time, Pallas kernels for 19%

profile of v4, /device:TPU:0, one launch (start us, length us, event | category | flops | bytes accessed | tf_op | source)
XLA Modules:
  0.0 137.1 jit_solution(7000814425528358705)
XLA Ops:
  1.7 0.7 add_bitcast_fusion.code
  2.4 0.9 copy-done.7
  3.4 0.9 route_send.1
  4.3 4.8 %collective-permute-start.5 = (bf16[24,1152]{1,0:T(8,128)(2,1)S(1)}, bf16[24,1152]{1,0:T(8,128)(2,1)S(1)}, u32[]{:S(2)}, u32[]{:S(2)}) collective-permute-start(bf16[24,1152]{1,0:T(8,128)(2,1)S(1)} %get-tuple-element.96), channel_id=1, source_target_pairs={{0,12},{4,8},{8,4},{12,0},{16,28},{20,24},{24,20},{28,16},{1,13},{... | collective-permute-start | bytes 165896 | tf_op jit(solution)/shard_map/ppermute | solution.py:458
  9.0 1.1 collective-permute-start.9
  10.3 4.1 %collective-permute-start.4 = (bf16[24,1152]{1,0:T(8,128)(2,1)S(1)}, bf16[24,1152]{1,0:T(8,128)(2,1)S(1)}, u32[]{:S(2)}, u32[]{:S(2)}) collective-permute-start(bf16[24,1152]{1,0:T(8,128)(2,1)S(1)} %get-tuple-element.103), channel_id=1, source_target_pairs={{0,8},{4,12},{8,0},{12,4},{16,24},{20,28},{24,16},{28,20},{1,9},{5... | collective-permute-start | bytes 165896 | tf_op jit(solution)/shard_map/ppermute | solution.py:458
  14.9 1.0 collective-permute-start.7
  16.9 0.5 collective-permute-done.4.refs_2_
  17.5 1.2 collective-permute-done.6.refs_4_
  18.7 1.9 %collective-permute-done.7.refs_5_ = bf16[24,1152]{1,0:T(8,128)(2,1)S(1)} collective-permute-done((bf16[24,1152]{1,0:T(8,128)(2,1)S(1)}, bf16[24,1152]{1,0:T(8,128)(2,1)S(1)}, u32[]{:S(2)}, u32[]{:S(2)}) %collective-permute-start.7) | collective-permute-done | bytes 55328 | tf_op jit(solution)/shard_map/ppermute | solution.py:458
  20.6 1.8 %collective-permute-done.8.refs_6_ = bf16[24,1152]{1,0:T(8,128)(2,1)S(1)} collective-permute-done((bf16[24,1152]{1,0:T(8,128)(2,1)S(1)}, bf16[24,1152]{1,0:T(8,128)(2,1)S(1)}, u32[]{:S(2)}, u32[]{:S(2)}) %collective-permute-start.8) | collective-permute-done | bytes 55328 | tf_op jit(solution)/shard_map/ppermute | solution.py:458
  22.8 1.6 %collective-permute-start.11 = (bf16[128,1024]{1,0:T(8,128)(2,1)S(1)}, bf16[128,1024]{1,0:T(8,128)(2,1)S(1)}, u32[]{:S(2)}, u32[]{:S(2)}) collective-permute-start(bf16[128,1024]{1,0:T(8,128)(2,1)S(1)} %get-tuple-element.107.first.act0_a), channel_id=1, source_target_pairs={{0,2},{1,3},{2,0},{3,1},{4,6},{5,7},{6,4},{7,5},{8,10},{9,11},{10,... | collective-permute-start | bytes 786440 | tf_op jit(solution)/shard_map/ppermute | solution.py:455
  24.3 2.6 %encode_first.1 = (f32[256,256]{1,0:T(8,128)S(1)}, bf16[256,1024]{1,0:T(8,128)(2,1)S(1)}, bf16[128,1024]{1,0:T(8,128)(2,1)S(1)}, bf16[4,2,128,256]{3,2,1,0:T(8,128)(2,1)S(1)}) custom-call(s32[2]{0:T(128)S(1)} %pad_add_fusion.where, bf16[128,1024]{1,0:T(8,128)(2,1)S(1)} %get-tuple-element.107.first.act0_a, ...), custom_call_target="tpu_custom_call" | custom-call | tf_op jit(solution)/shard_map/encode_first/pallas_call | solution.py:58
  27.0 4.5 %collective-permute-done.11.third.act0_a = bf16[128,1024]{1,0:T(8,128)(2,1)S(1)} collective-permute-done((bf16[128,1024]{1,0:T(8,128)(2,1)S(1)}, bf16[128,1024]{1,0:T(8,128)(2,1)S(1)}, u32[]{:S(2)}, u32[]{:S(2)}) %collective-permute-start.11) | collective-permute-done | bytes 262176 | tf_op jit(solution)/shard_map/ppermute | solution.py:455
  31.5 1.5 %collective-permute-start.14 = (bf16[128,1024]{1,0:T(8,128)(2,1)S(1)}, bf16[128,1024]{1,0:T(8,128)(2,1)S(1)}, u32[]{:S(2)}, u32[]{:S(2)}) collective-permute-start(bf16[128,1024]{1,0:T(8,128)(2,1)S(1)} %bitcast.7), channel_id=1, source_target_pairs={{0,2},{1,3},{2,0},{3,1},{4,6},{5,7},{6,4},{7,5},{8,10},{9,11},{10,... | collective-permute-start | bytes 786440 | tf_op jit(solution)/shard_map/ppermute | solution.py:455
  33.0 3.7 %attend_first.1 = (f32[256,256]{1,0:T(8,128)S(1)}, bf16[256,1024]{1,0:T(8,128)(2,1)S(1)}, bf16[128,1024]{1,0:T(8,128)(2,1)S(1)}, bf16[4,4,128,256]{3,2,1,0:T(8,1...) custom-call(s32[2]{0:T(128)S(1)} %pad_add_fusion.where, ...), custom_call_target="tpu_custom_call" | custom-call | tf_op jit(solution)/shard_map/attend_first/pallas_call | solution.py:58
  37.0 3.2 %collective-permute-done.14.d_out_ref.d_out = bf16[128,1024]{1,0:T(8,128)(2,1)S(1)} collective-permute-done((bf16[128,1024]{1,0:T(8,128)(2,1)S(1)}, bf16[128,1024]{1,0:T(8,128)(2,1)S(1)}, u32[]{:S(2)}, u32[]{:S(2)}) %collective-permute-start.14) | collective-permute-done | bytes 262176 | tf_op jit(solution)/shard_map/ppermute | solution.py:455
  40.2 1.4 attn_out_far.1.part
  41.6 1.6 %collective-permute-start.15 = (bf16[128,1024]{1,0:T(8,128)(2,1)S(1)}, bf16[128,1024]{1,0:T(8,128)(2,1)S(1)}, u32[]{:S(2)}, u32[]{:S(2)}) collective-permute-start(bf16[128,1024]{1,0:T(8,128)(2,1)S(1)} %attn_out_far.1.part), channel_id=1, source_target_pairs={{0,2},{1,3},{2,0},{3,1},{4,6},{5,7},{6,4},{7,5},{8,10},{9,11},{10,... | collective-permute-start | bytes 786440 | tf_op jit(solution)/shard_map/ppermute | solution.py:455
  43.2 1.3 attn_out_own.1.part
  44.5 0.6 collective-permute-start.16
  45.1 5.8 %collective-permute-done.15.got = bf16[128,1024]{1,0:T(8,128)(2,1)S(1)} collective-permute-done((bf16[128,1024]{1,0:T(8,128)(2,1)S(1)}, bf16[128,1024]{1,0:T(8,128)(2,1)S(1)}, u32[]{:S(2)}, u32[]{:S(2)}) %collective-permute-start.15) | collective-permute-done | bytes 262176 | tf_op jit(solution)/shard_map/ppermute | solution.py:455
  51.1 2.9 %ffn_own.1 = (bf16[128,1024]{1,0:T(8,128)(2,1)S(1)}, bf16[128,1024]{1,0:T(8,128)(2,1)S(1)}) custom-call(bf16[128,1024]{1,0:T(8,128)(2,1)S(1)} %get-tuple-element.118.rows_ref, bf16[128,1024]{1,0:T(8,128)(2,1)S(1)} %bitcast.8, bf16[2,1024,512]{2,1,0:T(8,128)(2,1)S(1)} %copy-done.4, bf16[2,1024,512]{2,1,0:T(8,128)(2,1)S(1)} %collective-permute-done.in_b, ...), custom_call_target="tpu_custom_call" | custom-call | tf_op jit(solution)/shard_map/ffn_own/pallas_call | solution.py:58
  54.0 1.2 collective-permute-done.16.got
  55.2 1.5 %collective-permute-start.18 = (bf16[128,1024]{1,0:T(8,128)(2,1)S(1)}, bf16[128,1024]{1,0:T(8,128)(2,1)S(1)}, u32[]{:S(2)}, u32[]{:S(2)}) collective-permute-start(bf16[128,1024]{1,0:T(8,128)(2,1)S(1)} %get-tuple-element.124.back), channel_id=1, source_target_pairs={{0,2},{1,3},{2,0},{3,1},{4,6},{5,7},{6,4},{7,5},{8,10},{9,11},{10,... | collective-permute-start | bytes 786440 | tf_op jit(solution)/shard_map/ppermute | solution.py:455
  56.9 2.9 %ffn_far.1 = (bf16[128,1024]{1,0:T(8,128)(2,1)S(1)}, bf16[128,1024]{1,0:T(8,128)(2,1)S(1)}) custom-call(bf16[128,1024]{1,0:T(8,128)(2,1)S(1)} %get-tuple-element.127.rows_ref, bf16[128,1024]{1,0:T(8,128)(2,1)S(1)} %collective-permute-done.14.d_out_ref.d_out, bf16[2,1024,512]{2,1,0:T(8,128)(2,1)S(1)} %copy-done.4, ...), custom_call_target="tpu_custom_call" | custom-call | tf_op jit(solution)/shard_map/ffn_far/pallas_call | solution.py:58
  59.8 2.4 %collective-permute-done.18.got = bf16[128,1024]{1,0:T(8,128)(2,1)S(1)} collective-permute-done((bf16[128,1024]{1,0:T(8,128)(2,1)S(1)}, bf16[128,1024]{1,0:T(8,128)(2,1)S(1)}, u32[]{:S(2)}, u32[]{:S(2)}) %collective-permute-start.18) | collective-permute-done | bytes 262176 | tf_op jit(solution)/shard_map/ppermute | solution.py:455
  62.6 1.6 %collective-permute-start.17 = (bf16[128,1024]{1,0:T(8,128)(2,1)S(1)}, bf16[128,1024]{1,0:T(8,128)(2,1)S(1)}, u32[]{:S(2)}, u32[]{:S(2)}) collective-permute-start(bf16[128,1024]{1,0:T(8,128)(2,1)S(1)} %get-tuple-element.129.back), channel_id=1, source_target_pairs={{0,2},{1,3},{2,0},{3,1},{4,6},{5,7},{6,4},{7,5},{8,10},{9,11},{10,... | collective-permute-start | bytes 786440 | tf_op jit(solution)/shard_map/ppermute | solution.py:455
  64.2 2.5 %attn_back_first.1 = (bf16[4,128,256]{2,1,0:T(8,128)(2,1)S(1)}, f32[4,128,256]{2,1,0:T(8,128)S(1)}, f32[4,128,256]{2,1,0:T(8,128)S(1)}, bf16[4,128,256]{2,1,0:T(8,128)(2,1)S(1)}) custom-call(s32[2]{0:T(128)S(1)} %pad_add_fusion.where, s32[4,1,128]{2,1,0:T(1,128)S(1)} %bitcast.11, bf16[128,1024]{1,0:T(8,128)(2,1)S(1)} %resid_back_far.1.third.d_resid, ...), custom_call_target="tpu_custom_call" | custom-call | tf_op jit(solution)/shard_map/attn_back_first/pallas_call | solution.py:58
  66.7 4.6 %collective-permute-done.17.got = bf16[128,1024]{1,0:T(8,128)(2,1)S(1)} collective-permute-done((bf16[128,1024]{1,0:T(8,128)(2,1)S(1)}, bf16[128,1024]{1,0:T(8,128)(2,1)S(1)}, u32[]{:S(2)}, u32[]{:S(2)}) %collective-permute-start.17) | collective-permute-done | bytes 262176 | tf_op jit(solution)/shard_map/ppermute | solution.py:455
  71.7 1.5 %collective-permute-done.20.second = bf16[128,1024]{1,0:T(8,128)(2,1)S(1)} collective-permute-done((bf16[128,1024]{1,0:T(8,128)(2,1)S(1)}, bf16[128,1024]{1,0:T(8,128)(2,1)S(1)}, u32[]{:S(2)}, u32[]{:S(2)}) %collective-permute-start.20) | collective-permute-done | bytes 262176 | tf_op jit(solution)/shard_map/ppermute | solution.py:452
  73.2 2.9 %attn_back_second.1 = (bf16[256,1024]{1,0:T(8,128)(2,1)S(1)}, bf16[4,128,256]{2,1,0:T(8,128)(2,1)S(1)}, bf16[4,128,256]{2,1,0:T(8,128)(2,1)S(1)}, bf16[4,128,256...) custom-call(s32[2]{0:T(128)S(1)} %pad_add_fusion.where, s32[4,1,128]{2,1,0:T(1,128)S(1)} %bitcast.12, ...), custom_call_target="tpu_custom_call" | custom-call | tf_op jit(solution)/shard_map/attn_back_second/pallas_call | solution.py:58
  76.4 0.7 attn_back_keep.1.keep
  77.1 1.0 collective-permute-done.21.take
  78.2 1.6 %collective-permute-start.23 = (bf16[128,1024]{1,0:T(8,128)(2,1)S(1)}, bf16[128,1024]{1,0:T(8,128)(2,1)S(1)}, u32[]{:S(2)}, u32[]{:S(2)}) collective-permute-start(bf16[128,1024]{1,0:T(8,128)(2,1)S(1)} %get-tuple-element.144.part), channel_id=1, source_target_pairs={{0,2},{1,3},{2,0},{3,1},{4,6},{5,7},{6,4},{7,5},{8,10},{9,11},{10,... | collective-permute-start | bytes 786440 | tf_op jit(solution)/shard_map/ppermute | solution.py:455
  79.8 6.8 %collective-permute-done.23.got = bf16[128,1024]{1,0:T(8,128)(2,1)S(1)} collective-permute-done((bf16[128,1024]{1,0:T(8,128)(2,1)S(1)}, bf16[128,1024]{1,0:T(8,128)(2,1)S(1)}, u32[]{:S(2)}, u32[]{:S(2)}) %collective-permute-start.23) | collective-permute-done | bytes 262176 | tf_op jit(solution)/shard_map/ppermute | solution.py:455
  87.0 1.6 %collective-permute-start.22 = (bf16[128,1024]{1,0:T(8,128)(2,1)S(1)}, bf16[128,1024]{1,0:T(8,128)(2,1)S(1)}, u32[]{:S(2)}, u32[]{:S(2)}) collective-permute-start(bf16[128,1024]{1,0:T(8,128)(2,1)S(1)} %get-tuple-element.145.part), channel_id=1, source_target_pairs={{0,2},{1,3},{2,0},{3,1},{4,6},{5,7},{6,4},{7,5},{8,10},{9,11},{10,... | collective-permute-start | bytes 786440 | tf_op jit(solution)/shard_map/ppermute | solution.py:455
  88.6 1.5 %enc_grads_first.1 = (f32[1024,256]{1,0:T(8,128)S(1)}, f32[1024,256]{1,0:T(8,128)S(1)}) custom-call(s32[2]{0:T(128)S(1)} %pad_add_fusion.where, bf16[128,1024]{1,0:T(8,128)(2,1)S(1)} %packed_back.1.cot_a.d_packed, bf16[128,1024]{1,0:T(8,128)(2,1)S(1)} %collective-permute-done.24.cot_b, bf16[128,1024]{1,0:T(8,128)(2,1)S(1)} %get-tuple-element.107.first.act0_a, ...), custom_call_target="tpu_custom_call" | custom-call | tf_op jit(solution)/shard_map/enc_grads_first/pallas_call | solution.py:58
  90.1 5.6 %collective-permute-done.22.got = bf16[128,1024]{1,0:T(8,128)(2,1)S(1)} collective-permute-done((bf16[128,1024]{1,0:T(8,128)(2,1)S(1)}, bf16[128,1024]{1,0:T(8,128)(2,1)S(1)}, u32[]{:S(2)}, u32[]{:S(2)}) %collective-permute-start.22) | collective-permute-done | bytes 262176 | tf_op jit(solution)/shard_map/ppermute | solution.py:455
  96.3 1.5 %collective-permute-start.27 = (bf16[48,1024]{1,0:T(8,128)(2,1)S(1)}, bf16[48,1024]{1,0:T(8,128)(2,1)S(1)}, u32[]{:S(2)}, u32[]{:S(2)}) collective-permute-start(bf16[48,1024]{1,0:T(8,128)(2,1)S(1)} %get-tuple-element.156), channel_id=1, source_target_pairs={{0,4},{4,0},{8,12},{12,8},{16,20},{20,16},{24,28},{28,24},{1,5},{5... | collective-permute-start | bytes 294920 | tf_op jit(solution)/shard_map/ppermute | solution.py:458
  97.9 0.9 collective-permute-start.28
  98.8 2.0 %collective-permute-start.29 = (bf16[48,1024]{1,0:T(8,128)(2,1)S(1)}, bf16[48,1024]{1,0:T(8,128)(2,1)S(1)}, u32[]{:S(2)}, u32[]{:S(2)}) collective-permute-start(bf16[48,1024]{1,0:T(8,128)(2,1)S(1)} %get-tuple-element.158), channel_id=1, source_target_pairs={{0,12},{4,8},{8,4},{12,0},{16,28},{20,24},{24,20},{28,16},{1,13},{... | collective-permute-start | bytes 294920 | tf_op jit(solution)/shard_map/ppermute | solution.py:458
  100.8 0.8 collective-permute-done.27.refs_1_
  101.6 6.6 %collective-permute-done.28.refs_2_ = bf16[48,1024]{1,0:T(8,128)(2,1)S(1)} collective-permute-done((bf16[48,1024]{1,0:T(8,128)(2,1)S(1)}, bf16[48,1024]{1,0:T(8,128)(2,1)S(1)}, u32[]{:S(2)}, u32[]{:S(2)}) %collective-permute-start.28) | collective-permute-done | bytes 98336 | tf_op jit(solution)/shard_map/ppermute | solution.py:458
  108.2 1.5 %enc_grad0_second.1 = (f32[4,128,256]{2,1,0:T(8,128)S(1)}, bf16[4,128,256]{2,1,0:T(8,128)(2,1)S(1)}) custom-call(s32[2]{0:T(128)S(1)} %pad_add_fusion.where, bf16[128,1024]{1,0:T(8,128)(2,1)S(1)} %packed_back_far.1.cot_a, bf16[128,1024]{1,0:T(8,128)(2,1)S(1)} %collective-permute-done.26.cot_b, bf16[128,1024]{1,0:T(8,128)(2,1)S(1)} %collective-permute-done.11.third.act0_a, ...), custom_call_target="tpu_custom_call" | custom-call | tf_op jit(solution)/shard_map/enc_grad0_second/pallas_call | solution.py:58
  109.7 2.4 %collective-permute-start.31 = (bf16[4,128,256]{2,1,0:T(8,128)(2,1)S(1)}, bf16[4,128,256]{2,1,0:T(8,128)(2,1)S(1)}, u32[]{:S(2)}, u32[]{:S(2)}) collective-permute-start(bf16[4,128,256]{2,1,0:T(8,128)(2,1)S(1)} %get-tuple-element.170), channel_id=1, source_target_pairs={{0,4},{4,0},{8,12},{12,8},{16,20},{20,16},{24,28},{28,24},{1,5},{5... | collective-permute-start | bytes 786440 | tf_op jit(solution)/shard_map/ppermute | solution.py:458
  112.1 1.1 enc_grad1_second.1
  113.2 1.0 collective-permute-start.34
  114.7 1.6 %collective-permute-start.25 = (bf16[128,1024]{1,0:T(8,128)(2,1)S(1)}, bf16[128,1024]{1,0:T(8,128)(2,1)S(1)}, u32[]{:S(2)}, u32[]{:S(2)}) collective-permute-start(bf16[128,1024]{1,0:T(8,128)(2,1)S(1)} %ffn_out_far.1), channel_id=1, source_target_pairs={{0,2},{1,3},{2,0},{3,1},{4,6},{5,7},{6,4},{7,5},{8,10},{9,11},{10,... | collective-permute-start | bytes 786440 | tf_op jit(solution)/shard_map/ppermute | solution.py:455
  116.3 1.1 collective-permute-start.30
  117.5 0.9 collective-permute-done.31.got
  118.4 0.6 halve0_2.1
  119.0 1.0 collective-permute-start.32
  120.0 2.6 %collective-permute-done.34.got = bf16[4,128,256]{2,1,0:T(8,128)(2,1)S(1)} collective-permute-done((bf16[4,128,256]{2,1,0:T(8,128)(2,1)S(1)}, bf16[4,128,256]{2,1,0:T(8,128)(2,1)S(1)}, u32[]{:S(2)}, u32[]{:S(2)}) %collective-permute-start.34) | collective-permute-done | bytes 262176 | tf_op jit(solution)/shard_map/ppermute | solution.py:458
  122.5 0.6 halve1_0.1
  123.2 4.8 %collective-permute-done.32.got = bf16[2,128,256]{2,1,0:T(8,128)(2,1)S(1)} collective-permute-done((bf16[2,128,256]{2,1,0:T(8,128)(2,1)S(1)}, bf16[2,128,256]{2,1,0:T(8,128)(2,1)S(1)}, u32[]{:S(2)}, u32[]{:S(2)}) %collective-permute-start.32) | collective-permute-done | bytes 131104 | tf_op jit(solution)/shard_map/ppermute | solution.py:458
  128.0 0.6 halve0_1.1
  128.7 0.6 halve1_1.1
  129.3 3.0 %collective-permute-start.36 = (bf16[1,128,256]{2,1,0:T(8,128)(2,1)S(1)}, bf16[1,128,256]{2,1,0:T(8,128)(2,1)S(1)}, u32[]{:S(2)}, u32[]{:S(2)}) collective-permute-start(bf16[1,128,256]{2,1,0:T(8,128)(2,1)S(1)} %get-tuple-element.182), channel_id=1, source_target_pairs={{0,8},{4,12},{8,0},{12,4},{16,24},{20,28},{24,16},{28,20},{1,9},{5... | collective-permute-start | bytes 196616 | tf_op jit(solution)/shard_map/ppermute | solution.py:458
  132.2 1.2 ffn_out_own.1
  133.4 1.0 back_recv.1
  134.4 1.3 collective-permute-done.33.got0
  135.7 0.7 collective-permute-done.36.got1
  136.4 0.7 finish.1
  (59 shorter events, 6.5 us)
Async XLA Ops:
  0.6 9.5 %collective-permute-start = (bf16[2,1024,512]{2,1,0:T(8,128)(2,1)}, bf16[2,1024,512]{2,1,0:T(8,128)(2,1)S(1)}, u32[]{:S(2)}, u32[]{:S(2)}) collective-permute-start(bf16[2,1024,512]{2,1,0:T(8,128)(2,1)} %in_a.3), channel_id=1, source_target_pairs={{0,1},{1,0},{2,3},{3,2},{4,5},{5,4},{6,7},{7,6},{8,9},{9,8},{10,11... | collective-permute-start | bytes 6291464 | tf_op jit(solution)/shard_map/ppermute | solution.py:452
  1.1 9.0 %collective-permute-start.1 = (bf16[512,1024]{1,0:T(8,128)(2,1)}, bf16[512,1024]{1,0:T(8,128)(2,1)S(1)}, u32[]{:S(2)}, u32[]{:S(2)}) collective-permute-start(bf16[512,1024]{1,0:T(8,128)(2,1)} %w_a.3), channel_id=1, source_target_pairs={{0,1},{1,0},{2,3},{3,2},{4,5},{5,4},{6,7},{7,6},{8,9},{9,8},{10,11... | collective-permute-start | bytes 3145736 | tf_op jit(solution)/shard_map/ppermute | solution.py:452
  1.2 8.9 %collective-permute-start.2 = (bf16[256,1024]{1,0:T(8,128)(2,1)}, bf16[256,1024]{1,0:T(8,128)(2,1)}, u32[]{:S(2)}, u32[]{:S(2)}) collective-permute-start(bf16[256,1024]{1,0:T(8,128)(2,1)} %w_out.3), channel_id=1, source_target_pairs={{0,1},{1,0},{2,3},{3,2},{4,5},{5,4},{6,7},{7,6},{8,9},{9,8},{10,11... | collective-permute-start | bytes 1572872 | tf_op jit(solution)/shard_map/ppermute | solution.py:452
  2.4 0.9 copy-start.7
  3.4 21.0 %copy-start = (bf16[2,1024,1024]{2,1,0:T(8,128)(2,1)S(1)}, bf16[2,1024,1024]{2,1,0:T(8,128)(2,1)}, u32[]{:S(2)}) copy-start(bf16[2,1024,1024]{2,1,0:T(8,128)(2,1)} %enc.7) | copy-start | bytes 12582916
  3.4 21.0 %copy-start.1 = (bf16[4,1024,256]{2,1,0:T(8,128)(2,1)S(1)}, bf16[4,1024,256]{2,1,0:T(8,128)(2,1)}, u32[]{:S(2)}) copy-start(bf16[4,1024,256]{2,1,0:T(8,128)(2,1)} %w_in.7) | copy-start | bytes 6291460
  4.3 10.7 %collective-permute-start.5 = (bf16[24,1152]{1,0:T(8,128)(2,1)S(1)}, bf16[24,1152]{1,0:T(8,128)(2,1)S(1)}, u32[]{:S(2)}, u32[]{:S(2)}) collective-permute-start(bf16[24,1152]{1,0:T(8,128)(2,1)S(1)} %get-tuple-element.96), channel_id=1, source_target_pairs={{0,12},{4,8},{8,4},{12,0},{16,28},{20,24},{24,20},{28,16},{1,13},{... | collective-permute-start | bytes 165896 | tf_op jit(solution)/shard_map/ppermute | solution.py:458
  9.0 7.4 %collective-permute-start.9 = (bf16[24,1152]{1,0:T(8,128)(2,1)S(1)}, bf16[24,1152]{1,0:T(8,128)(2,1)S(1)}, u32[]{:S(2)}, u32[]{:S(2)}) collective-permute-start(bf16[24,1152]{1,0:T(8,128)(2,1)S(1)} %get-tuple-element.100), channel_id=1, source_target_pairs={{0,28},{4,24},{8,20},{12,16},{16,12},{20,8},{24,4},{28,0},{1,29},{... | collective-permute-start | bytes 165896 | tf_op jit(solution)/shard_map/ppermute | solution.py:458
  10.2 6.7 %collective-permute-start.3 = (bf16[24,1152]{1,0:T(8,128)(2,1)S(1)}, bf16[24,1152]{1,0:T(8,128)(2,1)S(1)}, u32[]{:S(2)}, u32[]{:S(2)}) collective-permute-start(bf16[24,1152]{1,0:T(8,128)(2,1)S(1)} %get-tuple-element.102), channel_id=1, source_target_pairs={{0,4},{4,0},{8,12},{12,8},{16,20},{20,16},{24,28},{28,24},{1,5},{5... | collective-permute-start | bytes 165896 | tf_op jit(solution)/shard_map/ppermute | solution.py:458
  10.3 7.1 %collective-permute-start.4 = (bf16[24,1152]{1,0:T(8,128)(2,1)S(1)}, bf16[24,1152]{1,0:T(8,128)(2,1)S(1)}, u32[]{:S(2)}, u32[]{:S(2)}) collective-permute-start(bf16[24,1152]{1,0:T(8,128)(2,1)S(1)} %get-tuple-element.103), channel_id=1, source_target_pairs={{0,8},{4,12},{8,0},{12,4},{16,24},{20,28},{24,16},{28,20},{1,9},{5... | collective-permute-start | bytes 165896 | tf_op jit(solution)/shard_map/ppermute | solution.py:458
  14.4 4.3 %collective-permute-start.6 = (bf16[24,1152]{1,0:T(8,128)(2,1)S(1)}, bf16[24,1152]{1,0:T(8,128)(2,1)S(1)}, u32[]{:S(2)}, u32[]{:S(2)}) collective-permute-start(bf16[24,1152]{1,0:T(8,128)(2,1)S(1)} %get-tuple-element.104), channel_id=1, source_target_pairs={{0,16},{4,20},{8,24},{12,28},{16,0},{20,4},{24,8},{28,12},{1,17},{... | collective-permute-start | bytes 165896 | tf_op jit(solution)/shard_map/ppermute | solution.py:458
  14.9 5.6 %collective-permute-start.7 = (bf16[24,1152]{1,0:T(8,128)(2,1)S(1)}, bf16[24,1152]{1,0:T(8,128)(2,1)S(1)}, u32[]{:S(2)}, u32[]{:S(2)}) collective-permute-start(bf16[24,1152]{1,0:T(8,128)(2,1)S(1)} %get-tuple-element.105), channel_id=1, source_target_pairs={{0,20},{4,16},{8,28},{12,24},{16,4},{20,0},{24,12},{28,8},{1,21},{... | collective-permute-start | bytes 165896 | tf_op jit(solution)/shard_map/ppermute | solution.py:458
  16.4 6.0 %collective-permute-start.8 = (bf16[24,1152]{1,0:T(8,128)(2,1)S(1)}, bf16[24,1152]{1,0:T(8,128)(2,1)S(1)}, u32[]{:S(2)}, u32[]{:S(2)}) collective-permute-start(bf16[24,1152]{1,0:T(8,128)(2,1)S(1)} %get-tuple-element.106), channel_id=1, source_target_pairs={{0,24},{4,28},{8,16},{12,20},{16,8},{20,12},{24,0},{28,4},{1,25},{... | collective-permute-start | bytes 165896 | tf_op jit(solution)/shard_map/ppermute | solution.py:458
  22.6 8.8 %copy-start.5 = (bf16[1,128,1024]{2,1,0:T(8,128)(2,1)S(1)}, bf16[1,128,1024]{2,1,0:T(8,128)(2,1)}, u32[]{:S(2)}) copy-start(bf16[1,128,1024]{2,1,0:T(8,128)(2,1)} %param.19) | copy-start | bytes 786436
  22.7 10.4 %copy-start.6 = (s32[1,512]{1,0:T(1,128)S(1)}, s32[1,512]{1,0:T(1,128)}, u32[]{:S(2)}) copy-start(s32[1,512]{1,0:T(1,128)} %param.13) | copy-start | bytes 6148
  22.7 1.7 %collective-permute-start.10 = (bf16[128,1024]{1,0:T(8,128)(2,1)S(1)}, bf16[128,1024]{1,0:T(8,128)(2,1)S(1)}, u32[]{:S(2)}, u32[]{:S(2)}) collective-permute-start(bf16[128,1024]{1,0:T(8,128)(2,1)S(1)} %get-tuple-element.107.first.act0_a), channel_id=1, source_target_pairs={{0,1},{1,0},{2,3},{3,2},{4,5},{5,4},{6,7},{7,6},{8,9},{9,8},{10,11... | collective-permute-start | bytes 786440 | tf_op jit(solution)/shard_map/ppermute | solution.py:452
  22.8 8.7 %collective-permute-start.11 = (bf16[128,1024]{1,0:T(8,128)(2,1)S(1)}, bf16[128,1024]{1,0:T(8,128)(2,1)S(1)}, u32[]{:S(2)}, u32[]{:S(2)}) collective-permute-start(bf16[128,1024]{1,0:T(8,128)(2,1)S(1)} %get-tuple-element.107.first.act0_a), channel_id=1, source_target_pairs={{0,2},{1,3},{2,0},{3,1},{4,6},{5,7},{6,4},{7,5},{8,10},{9,11},{10,... | collective-permute-start | bytes 786440 | tf_op jit(solution)/shard_map/ppermute | solution.py:455
  31.5 1.5 %collective-permute-start.12 = (bf16[128,1024]{1,0:T(8,128)(2,1)S(1)}, bf16[128,1024]{1,0:T(8,128)(2,1)S(1)}, u32[]{:S(2)}, u32[]{:S(2)}) collective-permute-start(bf16[128,1024]{1,0:T(8,128)(2,1)S(1)} %collective-permute-done.11.third.act0_a), channel_id=1, source_target_pairs={{0,1},{1,0},{2,3},{3,2},{4,5},{5,4},{6,7},{7,6},{8,9},{9,8},{10,11... | collective-permute-start | bytes 786440 | tf_op jit(solution)/shard_map/ppermute | solution.py:452
  31.5 8.7 %collective-permute-start.14 = (bf16[128,1024]{1,0:T(8,128)(2,1)S(1)}, bf16[128,1024]{1,0:T(8,128)(2,1)S(1)}, u32[]{:S(2)}, u32[]{:S(2)}) collective-permute-start(bf16[128,1024]{1,0:T(8,128)(2,1)S(1)} %bitcast.7), channel_id=1, source_target_pairs={{0,2},{1,3},{2,0},{3,1},{4,6},{5,7},{6,4},{7,5},{8,10},{9,11},{10,... | collective-permute-start | bytes 786440 | tf_op jit(solution)/shard_map/ppermute | solution.py:455
  33.0 7.2 %copy-start.3 = (bf16[256,1024]{1,0:T(8,128)(2,1)S(1)}, bf16[256,1024]{1,0:T(8,128)(2,1)}, u32[]{:S(2)}) copy-start(bf16[256,1024]{1,0:T(8,128)(2,1)} %w_out.3) | copy-start | bytes 1572868
  36.7 14.3 %copy-start.2 = (bf16[512,1024]{1,0:T(8,128)(2,1)S(1)}, bf16[512,1024]{1,0:T(8,128)(2,1)}, u32[]{:S(2)}) copy-start(bf16[512,1024]{1,0:T(8,128)(2,1)} %w_a.3) | copy-start | bytes 3145732
  36.7 14.3 %copy-start.4 = (bf16[2,1024,512]{2,1,0:T(8,128)(2,1)S(1)}, bf16[2,1024,512]{2,1,0:T(8,128)(2,1)}, u32[]{:S(2)}) copy-start(bf16[2,1024,512]{2,1,0:T(8,128)(2,1)} %in_a.3) | copy-start | bytes 6291460
  36.8 3.4 %collective-permute-start.13 = (bf16[256,256]{1,0:T(8,128)(2,1)S(1)}, bf16[256,256]{1,0:T(8,128)(2,1)S(1)}, u32[]{:S(2)}, u32[]{:S(2)}) collective-permute-start(bf16[256,256]{1,0:T(8,128)(2,1)S(1)} %get-tuple-element.114), channel_id=1, source_target_pairs={{0,1},{1,0},{2,3},{3,2},{4,5},{5,4},{6,7},{7,6},{8,9},{9,8},{10,11... | collective-permute-start | bytes 393224 | tf_op jit(solution)/shard_map/ppermute | solution.py:452
  41.6 9.3 %collective-permute-start.15 = (bf16[128,1024]{1,0:T(8,128)(2,1)S(1)}, bf16[128,1024]{1,0:T(8,128)(2,1)S(1)}, u32[]{:S(2)}, u32[]{:S(2)}) collective-permute-start(bf16[128,1024]{1,0:T(8,128)(2,1)S(1)} %attn_out_far.1.part), channel_id=1, source_target_pairs={{0,2},{1,3},{2,0},{3,1},{4,6},{5,7},{6,4},{7,5},{8,10},{9,11},{10,... | collective-permute-start | bytes 786440 | tf_op jit(solution)/shard_map/ppermute | solution.py:455
  44.5 10.7 %collective-permute-start.16 = (bf16[128,1024]{1,0:T(8,128)(2,1)S(1)}, bf16[128,1024]{1,0:T(8,128)(2,1)S(1)}, u32[]{:S(2)}, u32[]{:S(2)}) collective-permute-start(bf16[128,1024]{1,0:T(8,128)(2,1)S(1)} %attn_out_own.1.part), channel_id=1, source_target_pairs={{0,2},{1,3},{2,0},{3,1},{4,6},{5,7},{6,4},{7,5},{8,10},{9,11},{10,... | collective-permute-start | bytes 786440 | tf_op jit(solution)/shard_map/ppermute | solution.py:455
  55.2 7.0 %collective-permute-start.18 = (bf16[128,1024]{1,0:T(8,128)(2,1)S(1)}, bf16[128,1024]{1,0:T(8,128)(2,1)S(1)}, u32[]{:S(2)}, u32[]{:S(2)}) collective-permute-start(bf16[128,1024]{1,0:T(8,128)(2,1)S(1)} %get-tuple-element.124.back), channel_id=1, source_target_pairs={{0,2},{1,3},{2,0},{3,1},{4,6},{5,7},{6,4},{7,5},{8,10},{9,11},{10,... | collective-permute-start | bytes 786440 | tf_op jit(solution)/shard_map/ppermute | solution.py:455
  62.5 1.7 %collective-permute-start.19 = (bf16[128,1024]{1,0:T(8,128)(2,1)S(1)}, bf16[128,1024]{1,0:T(8,128)(2,1)S(1)}, u32[]{:S(2)}, u32[]{:S(2)}) collective-permute-start(bf16[128,1024]{1,0:T(8,128)(2,1)S(1)} %resid_back_far.1.third.d_resid), channel_id=1, source_target_pairs={{0,1},{1,0},{2,3},{3,2},{4,5},{5,4},{6,7},{7,6},{8,9},{9,8},{10,11... | collective-permute-start | bytes 786440 | tf_op jit(solution)/shard_map/ppermute | solution.py:452
  62.6 8.7 %collective-permute-start.17 = (bf16[128,1024]{1,0:T(8,128)(2,1)S(1)}, bf16[128,1024]{1,0:T(8,128)(2,1)S(1)}, u32[]{:S(2)}, u32[]{:S(2)}) collective-permute-start(bf16[128,1024]{1,0:T(8,128)(2,1)S(1)} %get-tuple-element.129.back), channel_id=1, source_target_pairs={{0,2},{1,3},{2,0},{3,1},{4,6},{5,7},{6,4},{7,5},{8,10},{9,11},{10,... | collective-permute-start | bytes 786440 | tf_op jit(solution)/shard_map/ppermute | solution.py:455
  71.6 1.6 %collective-permute-start.20 = (bf16[128,1024]{1,0:T(8,128)(2,1)S(1)}, bf16[128,1024]{1,0:T(8,128)(2,1)S(1)}, u32[]{:S(2)}, u32[]{:S(2)}) collective-permute-start(bf16[128,1024]{1,0:T(8,128)(2,1)S(1)} %resid_back.1.first.d_resid), channel_id=1, source_target_pairs={{0,1},{1,0},{2,3},{3,2},{4,5},{5,4},{6,7},{7,6},{8,9},{9,8},{10,11... | collective-permute-start | bytes 786440 | tf_op jit(solution)/shard_map/ppermute | solution.py:452
  76.2 2.0 %collective-permute-start.21 = (bf16[256,1024]{1,0:T(8,128)(2,1)S(1)}, bf16[256,1024]{1,0:T(8,128)(2,1)S(1)}, u32[]{:S(2)}, u32[]{:S(2)}) collective-permute-start(bf16[256,1024]{1,0:T(8,128)(2,1)S(1)} %get-tuple-element.143), channel_id=1, source_target_pairs={{0,1},{1,0},{2,3},{3,2},{4,5},{5,4},{6,7},{7,6},{8,9},{9,8},{10,11... | collective-permute-start | bytes 1572872 | tf_op jit(solution)/shard_map/ppermute | solution.py:452
  78.2 8.4 %collective-permute-start.23 = (bf16[128,1024]{1,0:T(8,128)(2,1)S(1)}, bf16[128,1024]{1,0:T(8,128)(2,1)S(1)}, u32[]{:S(2)}, u32[]{:S(2)}) collective-permute-start(bf16[128,1024]{1,0:T(8,128)(2,1)S(1)} %get-tuple-element.144.part), channel_id=1, source_target_pairs={{0,2},{1,3},{2,0},{3,1},{4,6},{5,7},{6,4},{7,5},{8,10},{9,11},{10,... | collective-permute-start | bytes 786440 | tf_op jit(solution)/shard_map/ppermute | solution.py:455
  86.9 1.7 %collective-permute-start.24 = (bf16[128,1024]{1,0:T(8,128)(2,1)S(1)}, bf16[128,1024]{1,0:T(8,128)(2,1)S(1)}, u32[]{:S(2)}, u32[]{:S(2)}) collective-permute-start(bf16[128,1024]{1,0:T(8,128)(2,1)S(1)} %packed_back.1.cot_a.d_packed), channel_id=1, source_target_pairs={{0,1},{1,0},{2,3},{3,2},{4,5},{5,4},{6,7},{7,6},{8,9},{9,8},{10,11... | collective-permute-start | bytes 786440 | tf_op jit(solution)/shard_map/ppermute | solution.py:452
  87.0 8.7 %collective-permute-start.22 = (bf16[128,1024]{1,0:T(8,128)(2,1)S(1)}, bf16[128,1024]{1,0:T(8,128)(2,1)S(1)}, u32[]{:S(2)}, u32[]{:S(2)}) collective-permute-start(bf16[128,1024]{1,0:T(8,128)(2,1)S(1)} %get-tuple-element.145.part), channel_id=1, source_target_pairs={{0,2},{1,3},{2,0},{3,1},{4,6},{5,7},{6,4},{7,5},{8,10},{9,11},{10,... | collective-permute-start | bytes 786440 | tf_op jit(solution)/shard_map/ppermute | solution.py:455
  96.0 12.2 %collective-permute-start.26 = (bf16[128,1024]{1,0:T(8,128)(2,1)S(1)}, bf16[128,1024]{1,0:T(8,128)(2,1)S(1)}, u32[]{:S(2)}, u32[]{:S(2)}) collective-permute-start(bf16[128,1024]{1,0:T(8,128)(2,1)S(1)} %packed_back_far.1.cot_a), channel_id=1, source_target_pairs={{0,1},{1,0},{2,3},{3,2},{4,5},{5,4},{6,7},{7,6},{8,9},{9,8},{10,11... | collective-permute-start | bytes 786440 | tf_op jit(solution)/shard_map/ppermute | solution.py:452
  96.3 5.3 %collective-permute-start.27 = (bf16[48,1024]{1,0:T(8,128)(2,1)S(1)}, bf16[48,1024]{1,0:T(8,128)(2,1)S(1)}, u32[]{:S(2)}, u32[]{:S(2)}) collective-permute-start(bf16[48,1024]{1,0:T(8,128)(2,1)S(1)} %get-tuple-element.156), channel_id=1, source_target_pairs={{0,4},{4,0},{8,12},{12,8},{16,20},{20,16},{24,28},{28,24},{1,5},{5... | collective-permute-start | bytes 294920 | tf_op jit(solution)/shard_map/ppermute | solution.py:458
  97.9 10.3 %collective-permute-start.28 = (bf16[48,1024]{1,0:T(8,128)(2,1)S(1)}, bf16[48,1024]{1,0:T(8,128)(2,1)S(1)}, u32[]{:S(2)}, u32[]{:S(2)}) collective-permute-start(bf16[48,1024]{1,0:T(8,128)(2,1)S(1)} %get-tuple-element.157), channel_id=1, source_target_pairs={{0,8},{4,12},{8,0},{12,4},{16,24},{20,28},{24,16},{28,20},{1,9},{5... | collective-permute-start | bytes 294920 | tf_op jit(solution)/shard_map/ppermute | solution.py:458
  98.8 9.5 %collective-permute-start.29 = (bf16[48,1024]{1,0:T(8,128)(2,1)S(1)}, bf16[48,1024]{1,0:T(8,128)(2,1)S(1)}, u32[]{:S(2)}, u32[]{:S(2)}) collective-permute-start(bf16[48,1024]{1,0:T(8,128)(2,1)S(1)} %get-tuple-element.158), channel_id=1, source_target_pairs={{0,12},{4,8},{8,4},{12,0},{16,28},{20,24},{24,20},{28,16},{1,13},{... | collective-permute-start | bytes 294920 | tf_op jit(solution)/shard_map/ppermute | solution.py:458
  109.7 8.7 %collective-permute-start.31 = (bf16[4,128,256]{2,1,0:T(8,128)(2,1)S(1)}, bf16[4,128,256]{2,1,0:T(8,128)(2,1)S(1)}, u32[]{:S(2)}, u32[]{:S(2)}) collective-permute-start(bf16[4,128,256]{2,1,0:T(8,128)(2,1)S(1)} %get-tuple-element.170), channel_id=1, source_target_pairs={{0,4},{4,0},{8,12},{12,8},{16,20},{20,16},{24,28},{28,24},{1,5},{5... | collective-permute-start | bytes 786440 | tf_op jit(solution)/shard_map/ppermute | solution.py:458
  113.2 9.3 %collective-permute-start.34 = (bf16[4,128,256]{2,1,0:T(8,128)(2,1)S(1)}, bf16[4,128,256]{2,1,0:T(8,128)(2,1)S(1)}, u32[]{:S(2)}, u32[]{:S(2)}) collective-permute-start(bf16[4,128,256]{2,1,0:T(8,128)(2,1)S(1)} %get-tuple-element.178), channel_id=1, source_target_pairs={{0,16},{4,20},{8,24},{12,28},{16,0},{20,4},{24,8},{28,12},{1,17},{... | collective-permute-start | bytes 786440 | tf_op jit(solution)/shard_map/ppermute | solution.py:458
  114.7 17.5 %collective-permute-start.25 = (bf16[128,1024]{1,0:T(8,128)(2,1)S(1)}, bf16[128,1024]{1,0:T(8,128)(2,1)S(1)}, u32[]{:S(2)}, u32[]{:S(2)}) collective-permute-start(bf16[128,1024]{1,0:T(8,128)(2,1)S(1)} %ffn_out_far.1), channel_id=1, source_target_pairs={{0,2},{1,3},{2,0},{3,1},{4,6},{5,7},{6,4},{7,5},{8,10},{9,11},{10,... | collective-permute-start | bytes 786440 | tf_op jit(solution)/shard_map/ppermute | solution.py:455
  116.3 17.1 %collective-permute-start.30 = (bf16[96,1024]{1,0:T(8,128)(2,1)S(1)}, bf16[96,1024]{1,0:T(8,128)(2,1)S(1)}, u32[]{:S(2)}, u32[]{:S(2)}) collective-permute-start(bf16[96,1024]{1,0:T(8,128)(2,1)S(1)} %get-tuple-element.164), channel_id=1, source_target_pairs={{0,16},{4,20},{8,24},{12,28},{16,0},{20,4},{24,8},{28,12},{1,17},{... | collective-permute-start | bytes 589832 | tf_op jit(solution)/shard_map/ppermute | solution.py:458
  119.0 9.0 %collective-permute-start.32 = (bf16[2,128,256]{2,1,0:T(8,128)(2,1)S(1)}, bf16[2,128,256]{2,1,0:T(8,128)(2,1)S(1)}, u32[]{:S(2)}, u32[]{:S(2)}) collective-permute-start(bf16[2,128,256]{2,1,0:T(8,128)(2,1)S(1)} %get-tuple-element.172), channel_id=1, source_target_pairs={{0,16},{4,20},{8,24},{12,28},{16,0},{20,4},{24,8},{28,12},{1,17},{... | collective-permute-start | bytes 393224 | tf_op jit(solution)/shard_map/ppermute | solution.py:458
  123.1 5.6 %collective-permute-start.35 = (bf16[2,128,256]{2,1,0:T(8,128)(2,1)S(1)}, bf16[2,128,256]{2,1,0:T(8,128)(2,1)S(1)}, u32[]{:S(2)}, u32[]{:S(2)}) collective-permute-start(bf16[2,128,256]{2,1,0:T(8,128)(2,1)S(1)} %get-tuple-element.180), channel_id=1, source_target_pairs={{0,4},{4,0},{8,12},{12,8},{16,20},{20,16},{24,28},{28,24},{1,5},{5... | collective-permute-start | bytes 393224 | tf_op jit(solution)/shard_map/ppermute | solution.py:458
  128.6 7.1 %collective-permute-start.33 = (bf16[1,128,256]{2,1,0:T(8,128)(2,1)S(1)}, bf16[1,128,256]{2,1,0:T(8,128)(2,1)S(1)}, u32[]{:S(2)}, u32[]{:S(2)}) collective-permute-start(bf16[1,128,256]{2,1,0:T(8,128)(2,1)S(1)} %get-tuple-element.174), channel_id=1, source_target_pairs={{0,8},{4,12},{8,0},{12,4},{16,24},{20,28},{24,16},{28,20},{1,9},{5... | collective-permute-start | bytes 196616 | tf_op jit(solution)/shard_map/ppermute | solution.py:458
  129.3 7.1 %collective-permute-start.36 = (bf16[1,128,256]{2,1,0:T(8,128)(2,1)S(1)}, bf16[1,128,256]{2,1,0:T(8,128)(2,1)S(1)}, u32[]{:S(2)}, u32[]{:S(2)}) collective-permute-start(bf16[1,128,256]{2,1,0:T(8,128)(2,1)S(1)} %get-tuple-element.182), channel_id=1, source_target_pairs={{0,8},{4,12},{8,0},{12,4},{16,24},{20,28},{24,16},{28,20},{1,9},{5... | collective-permute-start | bytes 196616 | tf_op jit(solution)/shard_map/ppermute | solution.py:458

commit v5 on v4

--- a/solution.py
+++ b/solution.py
@@ -271,11 +271,18 @@
     out[...] = bf16(resid[...].astype(F32) + total + got[...].astype(F32))
 
 
-def resid_back(back, got, resid, d_out, out):
+def store_halves(value, out, halves):
+    out[...] = value
+    rows = value.shape[0] // max(len(halves), 1)
+    for n, target in enumerate(halves):
+        target[...] = value[n * rows : (n + 1) * rows]
+
+
+def resid_back(back, got, resid, d_out, out, *halves):
     wide = resid[...].astype(F32)
     factor = norm_factor(wide)
     grad = back[...].astype(F32) + got[...].astype(F32)
-    out[...] = bf16(d_out[...].astype(F32) + norm_back(grad, wide * factor, factor))
+    store_halves(bf16(d_out[...].astype(F32) + norm_back(grad, wide * factor, factor)), out, halves)
 
 
 def attend_back(where, docs, d_resid, r, proj_ref, att_ref, w_out, masks, d_q, d_k, d_v, d_g):
@@ -306,12 +313,16 @@
     d_v[r] += d_values[half:]
 
 
-def attn_back_first(where, docs, third, fourth, proj, att, w_out, d_q, d_k, d_v, d_g):
+def joined(refs):
+    return jnp.concatenate([r[...] for r in refs], axis=0)
+
+
+def attn_back_first(where, docs, third, fourth_a, fourth_b, proj, att, w_out, d_q, d_k, d_v, d_g):
     masks = head_masks(w_out.shape[0])
     d_k[...] = jnp.zeros_like(d_k)
     d_v[...] = jnp.zeros_like(d_v)
-    for r, rows in ((2, third), (3, fourth)):
-        attend_back(where, docs, rows[...], r, proj, att, w_out[...], masks, d_q, d_k, d_v, d_g)
+    for r, rows in ((2, [third]), (3, [fourth_a, fourth_b])):
+        attend_back(where, docs, joined(rows), r, proj, att, w_out[...], masks, d_q, d_k, d_v, d_g)
 
 
 def back_norm(grads, w_in, first, second):
@@ -349,11 +360,11 @@
     out_own[...] = bf16(keep[half:, :] + take[half:, :].astype(F32))
 
 
-def packed_back(part, got, packed, d_resid, out):
+def packed_back(part, got, packed, d_resid, out, *halves):
     wide = packed[...].astype(F32)
     factor = norm_factor(wide)
     grad = part[...].astype(F32) + got[...].astype(F32)
-    out[...] = bf16(d_resid[...].astype(F32) + norm_back(grad, wide * factor, factor))
+    store_halves(bf16(d_resid[...].astype(F32) + norm_back(grad, wide * factor, factor)), out, halves)
 
 
 def column_of(ref, index, cols):
@@ -364,24 +375,23 @@
     return dot(jnp.concatenate([a[...] for a in act_refs], axis=0), cot, TN)
 
 
-def first_cot(where, cot_a, cot_b, pre, enc):
+def first_cot(where, cots, pre, enc):
     cols = pre.shape[1]
-    cot = jnp.concatenate([cot_a[...], cot_b[...]], axis=0)
+    cot = joined(cots)
     value = pre[...]
     w1_rows = enc[1, pl.ds(pl.multiple_of(where[1] * cols, cols), cols), :]
     return bf16(dot(cot, w1_rows, NT) * silu_grad(value, jax.nn.sigmoid(value)))
 
 
-def cot_columns(where, cot_a, cot_b, cols):
-    return jnp.concatenate(
-        [column_of(cot_a, where[1], cols), column_of(cot_b, where[1], cols)], axis=0
-    )
-
-
-def enc_grads_first(where, cot_a, cot_b, act0_a, act0_b, act1, pre, enc, part1, part0):
+def cot_columns(where, cots, cols):
+    return jnp.concatenate([column_of(c, where[1], cols) for c in cots], axis=0)
+
+
+def enc_grads_first(where, *refs):
+    cots, (act0_a, act0_b, act1, pre, enc, part1, part0) = refs[:-7], refs[-7:]
     cols = pre.shape[1]
-    part1[...] = rows_term([act1], cot_columns(where, cot_a, cot_b, cols))
-    part0[...] = rows_term([act0_a, act0_b], first_cot(where, cot_a, cot_b, pre, enc))
+    part1[...] = rows_term([act1], cot_columns(where, cots, cols))
+    part0[...] = rows_term([act0_a, act0_b], first_cot(where, cots, pre, enc))
 
 
 def halve(where, bits, bit, total, keep, send):
@@ -397,13 +407,15 @@
             target[j] = rows.astype(target.dtype)
 
 
-def enc_grad1_second(bits, bit, where, cot_a, cot_b, act1, part1, keep, send, total):
-    total[...] = rows_term([act1], cot_columns(where, cot_a, cot_b, part1.shape[1])) + part1[...]
+def enc_grad1_second(bits, bit, where, *refs):
+    cots, (act1, part1, keep, send, total) = refs[:-5], refs[-5:]
+    total[...] = rows_term([act1], cot_columns(where, cots, part1.shape[1])) + part1[...]
     halve(where, bits, bit, total, keep, send)
 
 
-def enc_grad0_second(bits, bit, where, cot_a, cot_b, act0_a, act0_b, pre, enc, part0, keep, send, total):
-    total[...] = rows_term([act0_a, act0_b], first_cot(where, cot_a, cot_b, pre, enc)) + part0[...]
+def enc_grad0_second(bits, bit, where, *refs):
+    cots, (act0_a, act0_b, pre, enc, part0, keep, send, total) = refs[:-8], refs[-8:]
+    total[...] = rows_term([act0_a, act0_b], first_cot(where, cots, pre, enc)) + part0[...]
     halve(where, bits, bit, total, keep, send)
 
 
@@ -472,13 +484,12 @@
         name="route_send",
     )
     order = sorted(range(1, groups), key=lambda k: (-(k % packs), k))
-    ffn_in_near, ffn_out_near, attn_out_near = near(ffn_in), near(ffn_out), near(attn_out)
+    ffn_in_near, ffn_out_near, d_out_far = near(ffn_in), near(ffn_out), far(d_out)
     early = {k: crossed(sends[k], k) for k in order[:2]}
-    ffn_in_near, ffn_out_near, attn_out_near, *sends = tie(
-        ffn_in_near, ffn_out_near, attn_out_near, *sends
-    )
+    ffn_in_near, ffn_out_near, *sends = tie(ffn_in_near, ffn_out_near, *sends)
     crossing = early | {k: crossed(sends[k], k) for k in order[2:]}
     gots = [sends[0]] + [crossing[k] for k in range(1, groups)]
+    d_out_far, *gots = tie(d_out_far, *gots)
     mine, hot = run(
         route_recv,
         [row_b, like((groups * capacity, rows_dev), BF16)],
@@ -505,9 +516,9 @@
         name="encode_first",
     )
     mine_far, proj_a = tie(mine_far, proj_a)
-    mine_far, d_out_late = tie(mine_far, d_out)
+    mine_far, attn_out_late = tie(mine_far, attn_out)
     mine_both = near(mine_far)
-    d_out_far = far(d_out_late)
+    attn_out_near = near(attn_out_late)
     pre_b, act_b, packed_far, proj, attended, give, keep = run(
         attend_first,
         [
@@ -525,7 +536,6 @@
         name="attend_first",
     )
     take = near(give)
-    take, d_out_far = tie(take, d_out_far)
 
 
     def out_part(index, name):
@@ -561,17 +571,23 @@
     hidden_far, back_far = feed(normed2_far, d_out_far, "ffn_far")
     got_back_own = far(back_far)
 
-    (d_resid_far,) = run(
-        resid_back, [row_b], None, [back_far, got_back_far, resid_far, d_out_far], name="resid_back_far"
-    )
-    d_resid_both = near(d_resid_far)
+    pieces = 2
+    piece_b = like((rows_dev // pieces, width), BF16)
+    d_resid_far, *halves = run(
+        resid_back,
+        [row_b] + [piece_b] * pieces,
+        None,
+        [back_far, got_back_far, resid_far, d_out_far],
+        name="resid_back_far",
+    )
+    d_resid_both = [near(h) for h in halves]
     block_f = like((tensors, rows_dev, cols), F32)
     block_b = like((tensors, rows_dev, cols), BF16)
     d_q, d_k, d_v, d_g = run(
         attn_back_first,
         [block_b, block_f, block_f, block_b],
         where,
-        [docs, d_resid_far, d_resid_both, proj, attended, attn_out],
+        [docs, d_resid_far, *d_resid_both, proj, attended, attn_out],
         name="attn_back_first",
     )
     got_back_own, d_q = tie(got_back_own, d_q)
@@ -596,9 +612,15 @@
     sum_far, sum_own = run(add_near, [row_b, row_b], None, [keep, take], name="add_near")
     got_own = far(sum_far)
     got_far = far(sum_own)
-    (d_packed,) = run(packed_back, [row_b], None, [sum_own, got_own, packed, d_resid], name="packed_back")
-
-    cot_near = near(d_packed)
+    d_packed, *halves = run(
+        packed_back,
+        [row_b] + [piece_b] * pieces,
+        None,
+        [sum_own, got_own, packed, d_resid],
+        name="packed_back",
+    )
+
+    cot_near = [near(h) for h in halves]
     backs = run(
         functools.partial(back_send, events),
         [like((events * capacity, width), BF16)] * packs,
@@ -612,15 +634,14 @@
         enc_grads_first,
         [part_f, part_f],
         where,
-        [d_packed, cot_near, mine, mine_near, act_a, pre_a, enc_weight],
+        [d_packed, *cot_near, mine, mine_near, act_a, pre_a, enc_weight],
         name="enc_grads_first",
     )
-    got_far, part1, part0 = tie(got_far, part1, part0)
+    got_far, part1, part0, *over_pack = tie(got_far, part1, part0, *over_pack)
     (cot_far,) = run(
         packed_back, [row_b], None, [sum_far, got_far, packed_far, d_resid_far], name="packed_back_far"
     )
     cot_both = near(cot_far)
-    cot_both, *over_pack = tie(cot_both, *over_pack)
     back_own, *back_sends = run(
         lambda *refs: back_turn(*refs, events),
         [like((packs * capacity, width), BF16)] * events,
@@ -650,9 +671,12 @@
         return [like(shape, F32), like(shape, BF16)]
 
     def reduce_over(stages, start, name):
+        nonlocal over_event
         remaining = list(bits)
         kept, send = start((tuple(remaining), stages[0]))
         got = crossed(send, 1 << stages[0])
+        if stages[0] in event_bits:
+            got, *over_event = tie(got, *over_event)
         remaining.remove(stages[0])
         for bit in stages[1:]:
             kept, send = run(

time: 137 us -> 132 us (0.964)
  starting transfers between devices: 40.2 us -> 36.5 us
  Pallas kernels: 33.7 us -> 31.6 us
    ppermute x9, waiting for transfers between devices: 34.2 us -> 24.2 us  [far(): return lax.ppermute(value, 'tensor', [(i, i ^ 2) for i in range(tensors)])]
    ppermute x11 -> x13, waiting for transfers between devices: 2.58 us -> 8.57 us  [near(): return lax.ppermute(value, 'tensor', [(i, i ^ 1) for i in range(tensors)])]
    ppermute x17, waiting for transfers between devices: 23.7 us -> 27.9 us  [crossed(): return lax.ppermute(value, group_axes, [(i, i ^ k) for i in range(groups)])]
    ppermute x9, starting transfers between devices: 13.1 us -> 9.98 us  [far(): return lax.ppermute(value, 'tensor', [(i, i ^ 2) for i in range(tensors)])]
    pallas_call x31, Pallas kernels: 33.7 us -> 31.6 us  [run(): pl.pallas_call(body, out_shape=list(outs), in_specs=specs, out_specs=[pl....]
    ppermute x17, starting transfers between devices: 25.2 us -> 23.2 us  [crossed(): return lax.ppermute(value, group_axes, [(i, i ^ k) for i in range(groups)])]
    ppermute x11 -> x13, starting transfers between devices: 1.87 us -> 3.35 us  [near(): return lax.ppermute(value, 'tensor', [(i, i ^ 1) for i in range(tensors)])]
  transfers between devices with their start and end apart: 37 -> 39, of which waited for: 22 -> 24; matrix products, arithmetic and copies ran while one was open for 1% -> 1% of each run, Pallas kernels for 19% -> 19%
where the time goes in v5:
time: 132 us
  waiting for transfers between devices  60.7 us (46%)
  starting transfers between devices  36.5 us (28%)
  Pallas kernels  31.6 us (24%)
    pallas_call x31, Pallas kernels, run(): pl.pallas_call(body, out_shape=list(outs), in_specs=specs, out_specs=[pl....  31.6 us
    ppermute x17, waiting for transfers between devices, crossed(): return lax.ppermute(value, group_axes, [(i, i ^ k) for i in range(groups)])  27.9 us
    ppermute x9, waiting for transfers between devices, far(): return lax.ppermute(value, 'tensor', [(i, i ^ 2) for i in range(tensors)])  24.2 us
    ppermute x17, starting transfers between devices, crossed(): return lax.ppermute(value, group_axes, [(i, i ^ k) for i in range(groups)])  23.2 us
    ppermute x9, starting transfers between devices, far(): return lax.ppermute(value, 'tensor', [(i, i ^ 2) for i in range(tensors)])  9.98 us
    ppermute x13, waiting for transfers between devices, near(): return lax.ppermute(value, 'tensor', [(i, i ^ 1) for i in range(tensors)])  8.57 us
    ppermute x13, starting transfers between devices, near(): return lax.ppermute(value, 'tensor', [(i, i ^ 1) for i in range(tensors)])  3.35 us
  transfers between devices with their start and end apart: 39, of which 24 were waited for; matrix products, arithmetic and copies ran while one was open for 1% of the time, Pallas kernels for 19%

profile of v5, /device:TPU:0, one launch (start us, length us, event | category | flops | bytes accessed | tf_op | source)
XLA Modules:
  0.0 131.5 jit_solution(11877488373140677970)
XLA Ops:
  0.6 0.5 collective-permute-start.1
  1.2 2.9 %collective-permute-start = (bf16[128,1024]{1,0:T(8,128)(2,1)}, bf16[128,1024]{1,0:T(8,128)(2,1)S(1)}, u32[]{:S(2)}, u32[]{:S(2)}) collective-permute-start(bf16[128,1024]{1,0:T(8,128)(2,1)} %bitcast.7), channel_id=1, source_target_pairs={{0,2},{1,3},{2,0},{3,1},{4,6},{5,7},{6,4},{7,5},{8,10},{9,11},{10,... | collective-permute-start | bytes 786440 | tf_op jit(solution)/shard_map/ppermute | solution.py:467
  4.2 0.7 add_bitcast_fusion.code
  4.9 0.9 copy-done.7
  5.9 0.9 route_send.1
  6.8 3.7 %collective-permute-start.5 = (bf16[24,1152]{1,0:T(8,128)(2,1)S(1)}, bf16[24,1152]{1,0:T(8,128)(2,1)S(1)}, u32[]{:S(2)}, u32[]{:S(2)}) collective-permute-start(bf16[24,1152]{1,0:T(8,128)(2,1)S(1)} %get-tuple-element.110), channel_id=1, source_target_pairs={{0,12},{4,8},{8,4},{12,0},{16,28},{20,24},{24,20},{28,16},{1,13},{... | collective-permute-start | bytes 165896 | tf_op jit(solution)/shard_map/ppermute | solution.py:470
  10.4 1.2 collective-permute-start.9
  11.6 4.2 %collective-permute-start.4 = (bf16[24,1152]{1,0:T(8,128)(2,1)S(1)}, bf16[24,1152]{1,0:T(8,128)(2,1)S(1)}, u32[]{:S(2)}, u32[]{:S(2)}) collective-permute-start(bf16[24,1152]{1,0:T(8,128)(2,1)S(1)} %get-tuple-element.117), channel_id=1, source_target_pairs={{0,8},{4,12},{8,0},{12,4},{16,24},{20,28},{24,16},{28,20},{1,9},{5... | collective-permute-start | bytes 165896 | tf_op jit(solution)/shard_map/ppermute | solution.py:470
  15.8 0.5 collective-permute-start.6
  16.3 1.5 %collective-permute-done.9.refs_7_ = bf16[24,1152]{1,0:T(8,128)(2,1)S(1)} collective-permute-done((bf16[24,1152]{1,0:T(8,128)(2,1)S(1)}, bf16[24,1152]{1,0:T(8,128)(2,1)S(1)}, u32[]{:S(2)}, u32[]{:S(2)}) %collective-permute-start.9) | collective-permute-done | bytes 55328 | tf_op jit(solution)/shard_map/ppermute | solution.py:470
  17.8 2.4 %collective-permute-start.8 = (bf16[24,1152]{1,0:T(8,128)(2,1)S(1)}, bf16[24,1152]{1,0:T(8,128)(2,1)S(1)}, u32[]{:S(2)}, u32[]{:S(2)}) collective-permute-start(bf16[24,1152]{1,0:T(8,128)(2,1)S(1)} %get-tuple-element.120), channel_id=1, source_target_pairs={{0,24},{4,28},{8,16},{12,20},{16,8},{20,12},{24,0},{28,4},{1,25},{... | collective-permute-start | bytes 165896 | tf_op jit(solution)/shard_map/ppermute | solution.py:470
  20.2 0.9 collective-permute-done.6.refs_4_
  21.1 1.8 %collective-permute-done.7.refs_5_ = bf16[24,1152]{1,0:T(8,128)(2,1)S(1)} collective-permute-done((bf16[24,1152]{1,0:T(8,128)(2,1)S(1)}, bf16[24,1152]{1,0:T(8,128)(2,1)S(1)}, u32[]{:S(2)}, u32[]{:S(2)}) %collective-permute-start.7) | collective-permute-done | bytes 55328 | tf_op jit(solution)/shard_map/ppermute | solution.py:470
  22.8 0.9 collective-permute-done.8.refs_6_
  24.1 0.6 collective-permute-start.11
  24.7 0.9 collective-permute-done.10.second.refs_4_
  25.6 2.6 %encode_first.1 = (f32[256,256]{1,0:T(8,128)S(1)}, bf16[256,1024]{1,0:T(8,128)(2,1)S(1)}, bf16[128,1024]{1,0:T(8,128)(2,1)S(1)}, bf16[4,2,128,256]{3,2,1,0:T(8,128)(2,1)S(1)}) custom-call(s32[2]{0:T(128)S(1)} %pad_add_fusion.where, bf16[128,1024]{1,0:T(8,128)(2,1)S(1)} %get-tuple-element.129.first.refs_3_, ...), custom_call_target="tpu_custom_call" | custom-call | tf_op jit(solution)/shard_map/encode_first/pallas_call | solution.py:58
  28.3 4.5 %collective-permute-done.11.third.refs_2_ = bf16[128,1024]{1,0:T(8,128)(2,1)S(1)} collective-permute-done((bf16[128,1024]{1,0:T(8,128)(2,1)S(1)}, bf16[128,1024]{1,0:T(8,128)(2,1)S(1)}, u32[]{:S(2)}, u32[]{:S(2)}) %collective-permute-start.11) | collective-permute-done | bytes 262176 | tf_op jit(solution)/shard_map/ppermute | solution.py:467
  32.8 0.5 collective-permute-start.12
  33.3 1.8 %collective-permute-done.12.fourth.refs_3_ = bf16[128,1024]{1,0:T(8,128)(2,1)S(1)} collective-permute-done((bf16[128,1024]{1,0:T(8,128)(2,1)S(1)}, bf16[128,1024]{1,0:T(8,128)(2,1)S(1)}, u32[]{:S(2)}, u32[]{:S(2)}) %collective-permute-start.12) | collective-permute-done | bytes 262176 | tf_op jit(solution)/shard_map/ppermute | solution.py:464
  35.1 3.7 %attend_first.1 = (f32[256,256]{1,0:T(8,128)S(1)}, bf16[256,1024]{1,0:T(8,128)(2,1)S(1)}, bf16[128,1024]{1,0:T(8,128)(2,1)S(1)}, bf16[4,4,128,256]{3,2,1,0:T(8,1...) custom-call(s32[2]{0:T(128)S(1)} %pad_add_fusion.where, ...), custom_call_target="tpu_custom_call" | custom-call | tf_op jit(solution)/shard_map/attend_first/pallas_call | solution.py:58
  39.1 1.2 collective-permute-done.13.take
  40.6 0.6 collective-permute-start.15
  41.5 1.6 %collective-permute-start.16 = (bf16[128,1024]{1,0:T(8,128)(2,1)S(1)}, bf16[128,1024]{1,0:T(8,128)(2,1)S(1)}, u32[]{:S(2)}, u32[]{:S(2)}) collective-permute-start(bf16[128,1024]{1,0:T(8,128)(2,1)S(1)} %attn_out_own.1.part), channel_id=1, source_target_pairs={{0,2},{1,3},{2,0},{3,1},{4,6},{5,7},{6,4},{7,5},{8,10},{9,11},{10,... | collective-permute-start | bytes 786440 | tf_op jit(solution)/shard_map/ppermute | solution.py:467
  43.1 6.7 %collective-permute-done.15.got = bf16[128,1024]{1,0:T(8,128)(2,1)S(1)} collective-permute-done((bf16[128,1024]{1,0:T(8,128)(2,1)S(1)}, bf16[128,1024]{1,0:T(8,128)(2,1)S(1)}, u32[]{:S(2)}, u32[]{:S(2)}) %collective-permute-start.15) | collective-permute-done | bytes 262176 | tf_op jit(solution)/shard_map/ppermute | solution.py:467
  50.1 2.9 %ffn_own.1 = (bf16[128,1024]{1,0:T(8,128)(2,1)S(1)}, bf16[128,1024]{1,0:T(8,128)(2,1)S(1)}) custom-call(bf16[128,1024]{1,0:T(8,128)(2,1)S(1)} %get-tuple-element.138.rows_ref, bf16[128,1024]{1,0:T(8,128)(2,1)S(1)} %bitcast.8, bf16[2,1024,512]{2,1,0:T(8,128)(2,1)S(1)} %copy-done.4, bf16[2,1024,512]{2,1,0:T(8,128)(2,1)S(1)} %collective-permute-done.1.in_b, ...), custom_call_target="tpu_custom_call" | custom-call | tf_op jit(solution)/shard_map/ffn_own/pallas_call | solution.py:58
  53.0 1.7 %collective-permute-done.16.got = bf16[128,1024]{1,0:T(8,128)(2,1)S(1)} collective-permute-done((bf16[128,1024]{1,0:T(8,128)(2,1)S(1)}, bf16[128,1024]{1,0:T(8,128)(2,1)S(1)}, u32[]{:S(2)}, u32[]{:S(2)}) %collective-permute-start.16) | collective-permute-done | bytes 262176 | tf_op jit(solution)/shard_map/ppermute | solution.py:467
  54.7 0.5 collective-permute-start.18
  55.4 2.8 %ffn_far.1 = (bf16[128,1024]{1,0:T(8,128)(2,1)S(1)}, bf16[128,1024]{1,0:T(8,128)(2,1)S(1)}) custom-call(bf16[128,1024]{1,0:T(8,128)(2,1)S(1)} %get-tuple-element.147.rows_ref, bf16[128,1024]{1,0:T(8,128)(2,1)S(1)} %collective-permute-done.d_out_ref.d_out, bf16[2,1024,512]{2,1,0:T(8,128)(2,1)S(1)} %copy-done.4, ...), custom_call_target="tpu_custom_call" | custom-call | tf_op jit(solution)/shard_map/ffn_far/pallas_call | solution.py:58
  58.2 1.6 %collective-permute-start.17 = (bf16[128,1024]{1,0:T(8,128)(2,1)S(1)}, bf16[128,1024]{1,0:T(8,128)(2,1)S(1)}, u32[]{:S(2)}, u32[]{:S(2)}) collective-permute-start(bf16[128,1024]{1,0:T(8,128)(2,1)S(1)} %get-tuple-element.149.back), channel_id=1, source_target_pairs={{0,2},{1,3},{2,0},{3,1},{4,6},{5,7},{6,4},{7,5},{8,10},{9,11},{10,... | collective-permute-start | bytes 786440 | tf_op jit(solution)/shard_map/ppermute | solution.py:467
  59.8 4.1 %collective-permute-done.18.got = bf16[128,1024]{1,0:T(8,128)(2,1)S(1)} collective-permute-done((bf16[128,1024]{1,0:T(8,128)(2,1)S(1)}, bf16[128,1024]{1,0:T(8,128)(2,1)S(1)}, u32[]{:S(2)}, u32[]{:S(2)}) %collective-permute-start.18) | collective-permute-done | bytes 262176 | tf_op jit(solution)/shard_map/ppermute | solution.py:467
  64.3 0.5 collective-permute-start.20
  64.8 0.8 collective-permute-done.19.fourth_a
  65.8 2.5 %attn_back_first.1 = (bf16[4,128,256]{2,1,0:T(8,128)(2,1)S(1)}, f32[4,128,256]{2,1,0:T(8,128)S(1)}, f32[4,128,256]{2,1,0:T(8,128)S(1)}, bf16[4,128,256]{2,1,0:T(8,128)(2,1)S(1)}) custom-call(s32[2]{0:T(128)S(1)} %pad_add_fusion.where, s32[4,1,128]{2,1,0:T(1,128)S(1)} %bitcast.11, bf16[128,1024]{1,0:T(8,128)(2,1)S(1)} %get-tuple-element.151.third.d_resid, ...), custom_call_target="tpu_custom_call" | custom-call | tf_op jit(solution)/shard_map/attn_back_first/pallas_call | solution.py:58
  68.9 1.2 collective-permute-done.21.second
  70.2 3.0 %attn_back_second.1 = (bf16[256,1024]{1,0:T(8,128)(2,1)S(1)}, bf16[4,128,256]{2,1,0:T(8,128)(2,1)S(1)}, bf16[4,128,256]{2,1,0:T(8,128)(2,1)S(1)}, bf16[4,128,256...) custom-call(s32[2]{0:T(128)S(1)} %pad_add_fusion.where, s32[4,1,128]{2,1,0:T(1,128)S(1)} %bitcast.12, ...), custom_call_target="tpu_custom_call" | custom-call | tf_op jit(solution)/shard_map/attn_back_second/pallas_call | solution.py:58
  73.5 0.7 attn_back_keep.1.keep
  74.2 0.9 collective-permute-done.22.take
  75.3 2.0 %collective-permute-start.23 = (bf16[128,1024]{1,0:T(8,128)(2,1)S(1)}, bf16[128,1024]{1,0:T(8,128)(2,1)S(1)}, u32[]{:S(2)}, u32[]{:S(2)}) collective-permute-start(bf16[128,1024]{1,0:T(8,128)(2,1)S(1)} %get-tuple-element.168.part), channel_id=1, source_target_pairs={{0,2},{1,3},{2,0},{3,1},{4,6},{5,7},{6,4},{7,5},{8,10},{9,11},{10,... | collective-permute-start | bytes 786440 | tf_op jit(solution)/shard_map/ppermute | solution.py:467
  77.3 7.1 %collective-permute-done.24.got = bf16[128,1024]{1,0:T(8,128)(2,1)S(1)} collective-permute-done((bf16[128,1024]{1,0:T(8,128)(2,1)S(1)}, bf16[128,1024]{1,0:T(8,128)(2,1)S(1)}, u32[]{:S(2)}, u32[]{:S(2)}) %collective-permute-start.24) | collective-permute-done | bytes 262176 | tf_op jit(solution)/shard_map/ppermute | solution.py:467
  84.8 0.5 collective-permute-start.26
  85.5 2.9 %collective-permute-start.27 = (bf16[48,1024]{1,0:T(8,128)(2,1)S(1)}, bf16[48,1024]{1,0:T(8,128)(2,1)S(1)}, u32[]{:S(2)}, u32[]{:S(2)}) collective-permute-start(bf16[48,1024]{1,0:T(8,128)(2,1)S(1)} %get-tuple-element.178), channel_id=1, source_target_pairs={{0,4},{4,0},{8,12},{12,8},{16,20},{20,16},{24,28},{28,24},{1,5},{5... | collective-permute-start | bytes 294920 | tf_op jit(solution)/shard_map/ppermute | solution.py:470
  88.5 2.4 %collective-permute-start.29 = (bf16[48,1024]{1,0:T(8,128)(2,1)S(1)}, bf16[48,1024]{1,0:T(8,128)(2,1)S(1)}, u32[]{:S(2)}, u32[]{:S(2)}) collective-permute-start(bf16[48,1024]{1,0:T(8,128)(2,1)S(1)} %get-tuple-element.180), channel_id=1, source_target_pairs={{0,12},{4,8},{8,4},{12,0},{16,28},{20,24},{24,20},{28,16},{1,13},{... | collective-permute-start | bytes 294920 | tf_op jit(solution)/shard_map/ppermute | solution.py:470
  90.9 1.5 %enc_grads_first.1 = (f32[1024,256]{1,0:T(8,128)S(1)}, f32[1024,256]{1,0:T(8,128)S(1)}) custom-call(s32[2]{0:T(128)S(1)} %pad_add_fusion.where, bf16[128,1024]{1,0:T(8,128)(2,1)S(1)} %get-tuple-element.169.refs_0_.d_packed, bf16[64,1024]{1,0:T(8,128)(2,1)S(1)} %collective-permute-done.25.refs_1_, bf16[64,1024]{1,0:T(8,128)(2,1)S(1)} %collective-permute-done.26.refs_2_, ...), custom_call_target="tpu_custom_call" | custom-call | tf_op jit(solution)/shard_map/enc_grads_first/pallas_call | solution.py:58
  92.5 5.5 %collective-permute-done.28.refs_2_ = bf16[48,1024]{1,0:T(8,128)(2,1)S(1)} collective-permute-done((bf16[48,1024]{1,0:T(8,128)(2,1)S(1)}, bf16[48,1024]{1,0:T(8,128)(2,1)S(1)}, u32[]{:S(2)}, u32[]{:S(2)}) %collective-permute-start.28) | collective-permute-done | bytes 98336 | tf_op jit(solution)/shard_map/ppermute | solution.py:470
  98.4 1.5 %collective-permute-done.31.refs_1_ = bf16[128,1024]{1,0:T(8,128)(2,1)S(1)} collective-permute-done((bf16[128,1024]{1,0:T(8,128)(2,1)S(1)}, bf16[128,1024]{1,0:T(8,128)(2,1)S(1)}, u32[]{:S(2)}, u32[]{:S(2)}) %collective-permute-start.31) | collective-permute-done | bytes 262176 | tf_op jit(solution)/shard_map/ppermute | solution.py:464
  99.9 1.5 %enc_grad0_second.1 = (f32[4,128,256]{2,1,0:T(8,128)S(1)}, bf16[4,128,256]{2,1,0:T(8,128)(2,1)S(1)}) custom-call(s32[2]{0:T(128)S(1)} %pad_add_fusion.where, bf16[128,1024]{1,0:T(8,128)(2,1)S(1)} %packed_back_far.1.refs_0_, bf16[128,1024]{1,0:T(8,128)(2,1)S(1)} %collective-permute-done.31.refs_1_, ...), custom_call_target="tpu_custom_call" | custom-call | tf_op jit(solution)/shard_map/enc_grad0_second/pallas_call | solution.py:58
  101.4 2.7 %collective-permute-start.34 = (bf16[4,128,256]{2,1,0:T(8,128)(2,1)S(1)}, bf16[4,128,256]{2,1,0:T(8,128)(2,1)S(1)}, u32[]{:S(2)}, u32[]{:S(2)}) collective-permute-start(bf16[4,128,256]{2,1,0:T(8,128)(2,1)S(1)} %get-tuple-element.200), channel_id=1, source_target_pairs={{0,4},{4,0},{8,12},{12,8},{16,20},{20,16},{24,28},{28,24},{1,5},{5... | collective-permute-start | bytes 786440 | tf_op jit(solution)/shard_map/ppermute | solution.py:470
  104.0 1.1 enc_grad1_second.1
  105.1 0.8 collective-permute-start.32
  105.9 1.4 %collective-permute-start.33 = (bf16[96,1024]{1,0:T(8,128)(2,1)S(1)}, bf16[96,1024]{1,0:T(8,128)(2,1)S(1)}, u32[]{:S(2)}, u32[]{:S(2)}) collective-permute-start(bf16[96,1024]{1,0:T(8,128)(2,1)S(1)} %get-tuple-element.194), channel_id=1, source_target_pairs={{0,16},{4,20},{8,24},{12,28},{16,0},{20,4},{24,8},{28,12},{1,17},{... | collective-permute-start | bytes 589832 | tf_op jit(solution)/shard_map/ppermute | solution.py:470
  107.8 2.8 %collective-permute-done.34.got = bf16[4,128,256]{2,1,0:T(8,128)(2,1)S(1)} collective-permute-done((bf16[4,128,256]{2,1,0:T(8,128)(2,1)S(1)}, bf16[4,128,256]{2,1,0:T(8,128)(2,1)S(1)}, u32[]{:S(2)}, u32[]{:S(2)}) %collective-permute-start.34) | collective-permute-done | bytes 262176 | tf_op jit(solution)/shard_map/ppermute | solution.py:470
  110.6 0.6 halve0_2.1
  111.2 0.8 collective-permute-start.35
  112.0 6.6 %collective-permute-done.33.refs_1_ = bf16[96,1024]{1,0:T(8,128)(2,1)S(1)} collective-permute-done((bf16[96,1024]{1,0:T(8,128)(2,1)S(1)}, bf16[96,1024]{1,0:T(8,128)(2,1)S(1)}, u32[]{:S(2)}, u32[]{:S(2)}) %collective-permute-start.33) | collective-permute-done | bytes 196640 | tf_op jit(solution)/shard_map/ppermute | solution.py:470
  118.6 0.6 halve1_0.1
  119.2 1.0 collective-permute-done.35.got
  120.2 0.6 halve0_1.1
  121.1 3.8 %collective-permute-done.37.got = bf16[2,128,256]{2,1,0:T(8,128)(2,1)S(1)} collective-permute-done((bf16[2,128,256]{2,1,0:T(8,128)(2,1)S(1)}, bf16[2,128,256]{2,1,0:T(8,128)(2,1)S(1)}, u32[]{:S(2)}, u32[]{:S(2)}) %collective-permute-start.37) | collective-permute-done | bytes 131104 | tf_op jit(solution)/shard_map/ppermute | solution.py:470
  124.9 0.6 halve1_1.1
  125.6 1.2 ffn_out_own.1
  126.7 1.0 back_recv.1
  127.9 3.0 %collective-permute-done.38.got1 = bf16[1,128,256]{2,1,0:T(8,128)(2,1)S(1)} collective-permute-done((bf16[1,128,256]{2,1,0:T(8,128)(2,1)S(1)}, bf16[1,128,256]{2,1,0:T(8,128)(2,1)S(1)}, u32[]{:S(2)}, u32[]{:S(2)}) %collective-permute-start.38) | collective-permute-done | bytes 65568 | tf_op jit(solution)/shard_map/ppermute | solution.py:470
  130.8 0.7 finish.1
  (63 shorter events, 5.7 us)
Async XLA Ops:
  0.6 11.0 %collective-permute-start.1 = (bf16[2,1024,512]{2,1,0:T(8,128)(2,1)}, bf16[2,1024,512]{2,1,0:T(8,128)(2,1)S(1)}, u32[]{:S(2)}, u32[]{:S(2)}) collective-permute-start(bf16[2,1024,512]{2,1,0:T(8,128)(2,1)} %in_a.3), channel_id=1, source_target_pairs={{0,1},{1,0},{2,3},{3,2},{4,5},{5,4},{6,7},{7,6},{8,9},{9,8},{10,11... | collective-permute-start | bytes 6291464 | tf_op jit(solution)/shard_map/ppermute | solution.py:464
  1.1 10.5 %collective-permute-start.2 = (bf16[512,1024]{1,0:T(8,128)(2,1)}, bf16[512,1024]{1,0:T(8,128)(2,1)S(1)}, u32[]{:S(2)}, u32[]{:S(2)}) collective-permute-start(bf16[512,1024]{1,0:T(8,128)(2,1)} %w_a.3), channel_id=1, source_target_pairs={{0,1},{1,0},{2,3},{3,2},{4,5},{5,4},{6,7},{7,6},{8,9},{9,8},{10,11... | collective-permute-start | bytes 3145736 | tf_op jit(solution)/shard_map/ppermute | solution.py:464
  1.2 16.6 %collective-permute-start = (bf16[128,1024]{1,0:T(8,128)(2,1)}, bf16[128,1024]{1,0:T(8,128)(2,1)S(1)}, u32[]{:S(2)}, u32[]{:S(2)}) collective-permute-start(bf16[128,1024]{1,0:T(8,128)(2,1)} %bitcast.7), channel_id=1, source_target_pairs={{0,2},{1,3},{2,0},{3,1},{4,6},{5,7},{6,4},{7,5},{8,10},{9,11},{10,... | collective-permute-start | bytes 786440 | tf_op jit(solution)/shard_map/ppermute | solution.py:467
  4.9 0.9 copy-start.7
  5.9 19.8 %copy-start = (bf16[2,1024,1024]{2,1,0:T(8,128)(2,1)S(1)}, bf16[2,1024,1024]{2,1,0:T(8,128)(2,1)}, u32[]{:S(2)}) copy-start(bf16[2,1024,1024]{2,1,0:T(8,128)(2,1)} %refs_5_.1) | copy-start | bytes 12582916
  5.9 19.8 %copy-start.1 = (bf16[4,1024,256]{2,1,0:T(8,128)(2,1)S(1)}, bf16[4,1024,256]{2,1,0:T(8,128)(2,1)}, u32[]{:S(2)}) copy-start(bf16[4,1024,256]{2,1,0:T(8,128)(2,1)} %w_in.7) | copy-start | bytes 6291460
  6.8 9.0 %collective-permute-start.5 = (bf16[24,1152]{1,0:T(8,128)(2,1)S(1)}, bf16[24,1152]{1,0:T(8,128)(2,1)S(1)}, u32[]{:S(2)}, u32[]{:S(2)}) collective-permute-start(bf16[24,1152]{1,0:T(8,128)(2,1)S(1)} %get-tuple-element.110), channel_id=1, source_target_pairs={{0,12},{4,8},{8,4},{12,0},{16,28},{20,24},{24,20},{28,16},{1,13},{... | collective-permute-start | bytes 165896 | tf_op jit(solution)/shard_map/ppermute | solution.py:470
  10.4 7.3 %collective-permute-start.9 = (bf16[24,1152]{1,0:T(8,128)(2,1)S(1)}, bf16[24,1152]{1,0:T(8,128)(2,1)S(1)}, u32[]{:S(2)}, u32[]{:S(2)}) collective-permute-start(bf16[24,1152]{1,0:T(8,128)(2,1)S(1)} %get-tuple-element.114), channel_id=1, source_target_pairs={{0,28},{4,24},{8,20},{12,16},{16,12},{20,8},{24,4},{28,0},{1,29},{... | collective-permute-start | bytes 165896 | tf_op jit(solution)/shard_map/ppermute | solution.py:470
  11.6 8.6 %collective-permute-start.3 = (bf16[24,1152]{1,0:T(8,128)(2,1)S(1)}, bf16[24,1152]{1,0:T(8,128)(2,1)S(1)}, u32[]{:S(2)}, u32[]{:S(2)}) collective-permute-start(bf16[24,1152]{1,0:T(8,128)(2,1)S(1)} %get-tuple-element.116), channel_id=1, source_target_pairs={{0,4},{4,0},{8,12},{12,8},{16,20},{20,16},{24,28},{28,24},{1,5},{5... | collective-permute-start | bytes 165896 | tf_op jit(solution)/shard_map/ppermute | solution.py:470
  11.6 8.5 %collective-permute-start.4 = (bf16[24,1152]{1,0:T(8,128)(2,1)S(1)}, bf16[24,1152]{1,0:T(8,128)(2,1)S(1)}, u32[]{:S(2)}, u32[]{:S(2)}) collective-permute-start(bf16[24,1152]{1,0:T(8,128)(2,1)S(1)} %get-tuple-element.117), channel_id=1, source_target_pairs={{0,8},{4,12},{8,0},{12,4},{16,24},{20,28},{24,16},{28,20},{1,9},{5... | collective-permute-start | bytes 165896 | tf_op jit(solution)/shard_map/ppermute | solution.py:470
  15.8 5.3 %collective-permute-start.6 = (bf16[24,1152]{1,0:T(8,128)(2,1)S(1)}, bf16[24,1152]{1,0:T(8,128)(2,1)S(1)}, u32[]{:S(2)}, u32[]{:S(2)}) collective-permute-start(bf16[24,1152]{1,0:T(8,128)(2,1)S(1)} %get-tuple-element.118), channel_id=1, source_target_pairs={{0,16},{4,20},{8,24},{12,28},{16,0},{20,4},{24,8},{28,12},{1,17},{... | collective-permute-start | bytes 165896 | tf_op jit(solution)/shard_map/ppermute | solution.py:470
  17.8 5.1 %collective-permute-start.7 = (bf16[24,1152]{1,0:T(8,128)(2,1)S(1)}, bf16[24,1152]{1,0:T(8,128)(2,1)S(1)}, u32[]{:S(2)}, u32[]{:S(2)}) collective-permute-start(bf16[24,1152]{1,0:T(8,128)(2,1)S(1)} %get-tuple-element.119), channel_id=1, source_target_pairs={{0,20},{4,16},{8,28},{12,24},{16,4},{20,0},{24,12},{28,8},{1,21},{... | collective-permute-start | bytes 165896 | tf_op jit(solution)/shard_map/ppermute | solution.py:470
  17.8 6.0 %collective-permute-start.8 = (bf16[24,1152]{1,0:T(8,128)(2,1)S(1)}, bf16[24,1152]{1,0:T(8,128)(2,1)S(1)}, u32[]{:S(2)}, u32[]{:S(2)}) collective-permute-start(bf16[24,1152]{1,0:T(8,128)(2,1)S(1)} %get-tuple-element.120), channel_id=1, source_target_pairs={{0,24},{4,28},{8,16},{12,20},{16,8},{20,12},{24,0},{28,4},{1,25},{... | collective-permute-start | bytes 165896 | tf_op jit(solution)/shard_map/ppermute | solution.py:470
  24.0 8.8 %copy-start.3 = (bf16[256,1024]{1,0:T(8,128)(2,1)S(1)}, bf16[256,1024]{1,0:T(8,128)(2,1)}, u32[]{:S(2)}) copy-start(bf16[256,1024]{1,0:T(8,128)(2,1)} %w_out.3) | copy-start | bytes 1572868
  24.0 11.1 %copy-start.6 = (s32[1,512]{1,0:T(1,128)S(1)}, s32[1,512]{1,0:T(1,128)}, u32[]{:S(2)}) copy-start(s32[1,512]{1,0:T(1,128)} %param.13) | copy-start | bytes 6148
  24.0 1.6 %collective-permute-start.10 = (bf16[128,1024]{1,0:T(8,128)(2,1)S(1)}, bf16[128,1024]{1,0:T(8,128)(2,1)S(1)}, u32[]{:S(2)}, u32[]{:S(2)}) collective-permute-start(bf16[128,1024]{1,0:T(8,128)(2,1)S(1)} %get-tuple-element.129.first.refs_3_), channel_id=1, source_target_pairs={{0,1},{1,0},{2,3},{3,2},{4,5},{5,4},{6,7},{7,6},{8,9},{9,8},{10,11... | collective-permute-start | bytes 786440 | tf_op jit(solution)/shard_map/ppermute | solution.py:464
  24.1 8.7 %collective-permute-start.11 = (bf16[128,1024]{1,0:T(8,128)(2,1)S(1)}, bf16[128,1024]{1,0:T(8,128)(2,1)S(1)}, u32[]{:S(2)}, u32[]{:S(2)}) collective-permute-start(bf16[128,1024]{1,0:T(8,128)(2,1)S(1)} %get-tuple-element.129.first.refs_3_), channel_id=1, source_target_pairs={{0,2},{1,3},{2,0},{3,1},{4,6},{5,7},{6,4},{7,5},{8,10},{9,11},{10,... | collective-permute-start | bytes 786440 | tf_op jit(solution)/shard_map/ppermute | solution.py:467
  32.8 7.5 %collective-permute-start.14 = (bf16[256,1024]{1,0:T(8,128)(2,1)S(1)}, bf16[256,1024]{1,0:T(8,128)(2,1)S(1)}, u32[]{:S(2)}, u32[]{:S(2)}) collective-permute-start(bf16[256,1024]{1,0:T(8,128)(2,1)S(1)} %copy-done.3), channel_id=1, source_target_pairs={{0,1},{1,0},{2,3},{3,2},{4,5},{5,4},{6,7},{7,6},{8,9},{9,8},{10,11... | collective-permute-start | bytes 1572872 | tf_op jit(solution)/shard_map/ppermute | solution.py:464
  32.8 2.3 %collective-permute-start.12 = (bf16[128,1024]{1,0:T(8,128)(2,1)S(1)}, bf16[128,1024]{1,0:T(8,128)(2,1)S(1)}, u32[]{:S(2)}, u32[]{:S(2)}) collective-permute-start(bf16[128,1024]{1,0:T(8,128)(2,1)S(1)} %collective-permute-done.11.third.refs_2_), channel_id=1, source_target_pairs={{0,1},{1,0},{2,3},{3,2},{4,5},{5,4},{6,7},{7,6},{8,9},{9,8},{10,11... | collective-permute-start | bytes 786440 | tf_op jit(solution)/shard_map/ppermute | solution.py:464
  38.8 11.2 %copy-start.2 = (bf16[512,1024]{1,0:T(8,128)(2,1)S(1)}, bf16[512,1024]{1,0:T(8,128)(2,1)}, u32[]{:S(2)}) copy-start(bf16[512,1024]{1,0:T(8,128)(2,1)} %w_a.3) | copy-start | bytes 3145732
  38.8 11.2 %copy-start.4 = (bf16[2,1024,512]{2,1,0:T(8,128)(2,1)S(1)}, bf16[2,1024,512]{2,1,0:T(8,128)(2,1)}, u32[]{:S(2)}) copy-start(bf16[2,1024,512]{2,1,0:T(8,128)(2,1)} %in_a.3) | copy-start | bytes 6291460
  38.9 11.2 %copy-start.5 = (bf16[1,128,1024]{2,1,0:T(8,128)(2,1)S(1)}, bf16[1,128,1024]{2,1,0:T(8,128)(2,1)}, u32[]{:S(2)}) copy-start(bf16[1,128,1024]{2,1,0:T(8,128)(2,1)} %param.19) | copy-start | bytes 786436
  38.9 1.4 %collective-permute-start.13 = (bf16[256,256]{1,0:T(8,128)(2,1)S(1)}, bf16[256,256]{1,0:T(8,128)(2,1)S(1)}, u32[]{:S(2)}, u32[]{:S(2)}) collective-permute-start(bf16[256,256]{1,0:T(8,128)(2,1)S(1)} %get-tuple-element.136), channel_id=1, source_target_pairs={{0,1},{1,0},{2,3},{3,2},{4,5},{5,4},{6,7},{7,6},{8,9},{9,8},{10,11... | collective-permute-start | bytes 393224 | tf_op jit(solution)/shard_map/ppermute | solution.py:464
  40.6 9.2 %collective-permute-start.15 = (bf16[128,1024]{1,0:T(8,128)(2,1)S(1)}, bf16[128,1024]{1,0:T(8,128)(2,1)S(1)}, u32[]{:S(2)}, u32[]{:S(2)}) collective-permute-start(bf16[128,1024]{1,0:T(8,128)(2,1)S(1)} %attn_out_far.1.part), channel_id=1, source_target_pairs={{0,2},{1,3},{2,0},{3,1},{4,6},{5,7},{6,4},{7,5},{8,10},{9,11},{10,... | collective-permute-start | bytes 786440 | tf_op jit(solution)/shard_map/ppermute | solution.py:467
  41.5 13.2 %collective-permute-start.16 = (bf16[128,1024]{1,0:T(8,128)(2,1)S(1)}, bf16[128,1024]{1,0:T(8,128)(2,1)S(1)}, u32[]{:S(2)}, u32[]{:S(2)}) collective-permute-start(bf16[128,1024]{1,0:T(8,128)(2,1)S(1)} %attn_out_own.1.part), channel_id=1, source_target_pairs={{0,2},{1,3},{2,0},{3,1},{4,6},{5,7},{6,4},{7,5},{8,10},{9,11},{10,... | collective-permute-start | bytes 786440 | tf_op jit(solution)/shard_map/ppermute | solution.py:467
  54.7 9.2 %collective-permute-start.18 = (bf16[128,1024]{1,0:T(8,128)(2,1)S(1)}, bf16[128,1024]{1,0:T(8,128)(2,1)S(1)}, u32[]{:S(2)}, u32[]{:S(2)}) collective-permute-start(bf16[128,1024]{1,0:T(8,128)(2,1)S(1)} %get-tuple-element.144.back), channel_id=1, source_target_pairs={{0,2},{1,3},{2,0},{3,1},{4,6},{5,7},{6,4},{7,5},{8,10},{9,11},{10,... | collective-permute-start | bytes 786440 | tf_op jit(solution)/shard_map/ppermute | solution.py:467
  58.2 10.0 %collective-permute-start.17 = (bf16[128,1024]{1,0:T(8,128)(2,1)S(1)}, bf16[128,1024]{1,0:T(8,128)(2,1)S(1)}, u32[]{:S(2)}, u32[]{:S(2)}) collective-permute-start(bf16[128,1024]{1,0:T(8,128)(2,1)S(1)} %get-tuple-element.149.back), channel_id=1, source_target_pairs={{0,2},{1,3},{2,0},{3,1},{4,6},{5,7},{6,4},{7,5},{8,10},{9,11},{10,... | collective-permute-start | bytes 786440 | tf_op jit(solution)/shard_map/ppermute | solution.py:467
  64.2 1.4 %collective-permute-start.19 = (bf16[64,1024]{1,0:T(8,128)(2,1)S(1)}, bf16[64,1024]{1,0:T(8,128)(2,1)S(1)}, u32[]{:S(2)}, u32[]{:S(2)}) collective-permute-start(bf16[64,1024]{1,0:T(8,128)(2,1)S(1)} %get-tuple-element.152), channel_id=1, source_target_pairs={{0,1},{1,0},{2,3},{3,2},{4,5},{5,4},{6,7},{7,6},{8,9},{9,8},{10,11... | collective-permute-start | bytes 393224 | tf_op jit(solution)/shard_map/ppermute | solution.py:464
  64.3 1.5 %collective-permute-start.20 = (bf16[64,1024]{1,0:T(8,128)(2,1)S(1)}, bf16[64,1024]{1,0:T(8,128)(2,1)S(1)}, u32[]{:S(2)}, u32[]{:S(2)}) collective-permute-start(bf16[64,1024]{1,0:T(8,128)(2,1)S(1)} %get-tuple-element.153), channel_id=1, source_target_pairs={{0,1},{1,0},{2,3},{3,2},{4,5},{5,4},{6,7},{7,6},{8,9},{9,8},{10,11... | collective-permute-start | bytes 393224 | tf_op jit(solution)/shard_map/ppermute | solution.py:464
  68.6 1.6 %collective-permute-start.21 = (bf16[128,1024]{1,0:T(8,128)(2,1)S(1)}, bf16[128,1024]{1,0:T(8,128)(2,1)S(1)}, u32[]{:S(2)}, u32[]{:S(2)}) collective-permute-start(bf16[128,1024]{1,0:T(8,128)(2,1)S(1)} %resid_back.1.first.d_resid), channel_id=1, source_target_pairs={{0,1},{1,0},{2,3},{3,2},{4,5},{5,4},{6,7},{7,6},{8,9},{9,8},{10,11... | collective-permute-start | bytes 786440 | tf_op jit(solution)/shard_map/ppermute | solution.py:464
  73.1 2.0 %collective-permute-start.22 = (bf16[256,1024]{1,0:T(8,128)(2,1)S(1)}, bf16[256,1024]{1,0:T(8,128)(2,1)S(1)}, u32[]{:S(2)}, u32[]{:S(2)}) collective-permute-start(bf16[256,1024]{1,0:T(8,128)(2,1)S(1)} %get-tuple-element.166), channel_id=1, source_target_pairs={{0,1},{1,0},{2,3},{3,2},{4,5},{5,4},{6,7},{7,6},{8,9},{9,8},{10,11... | collective-permute-start | bytes 1572872 | tf_op jit(solution)/shard_map/ppermute | solution.py:464
  75.2 9.2 %collective-permute-start.24 = (bf16[128,1024]{1,0:T(8,128)(2,1)S(1)}, bf16[128,1024]{1,0:T(8,128)(2,1)S(1)}, u32[]{:S(2)}, u32[]{:S(2)}) collective-permute-start(bf16[128,1024]{1,0:T(8,128)(2,1)S(1)} %get-tuple-element.167.part), channel_id=1, source_target_pairs={{0,2},{1,3},{2,0},{3,1},{4,6},{5,7},{6,4},{7,5},{8,10},{9,11},{10,... | collective-permute-start | bytes 786440 | tf_op jit(solution)/shard_map/ppermute | solution.py:467
  75.3 17.2 %collective-permute-start.23 = (bf16[128,1024]{1,0:T(8,128)(2,1)S(1)}, bf16[128,1024]{1,0:T(8,128)(2,1)S(1)}, u32[]{:S(2)}, u32[]{:S(2)}) collective-permute-start(bf16[128,1024]{1,0:T(8,128)(2,1)S(1)} %get-tuple-element.168.part), channel_id=1, source_target_pairs={{0,2},{1,3},{2,0},{3,1},{4,6},{5,7},{6,4},{7,5},{8,10},{9,11},{10,... | collective-permute-start | bytes 786440 | tf_op jit(solution)/shard_map/ppermute | solution.py:467
  84.7 3.8 %collective-permute-start.25 = (bf16[64,1024]{1,0:T(8,128)(2,1)S(1)}, bf16[64,1024]{1,0:T(8,128)(2,1)S(1)}, u32[]{:S(2)}, u32[]{:S(2)}) collective-permute-start(bf16[64,1024]{1,0:T(8,128)(2,1)S(1)} %get-tuple-element.170), channel_id=1, source_target_pairs={{0,1},{1,0},{2,3},{3,2},{4,5},{5,4},{6,7},{7,6},{8,9},{9,8},{10,11... | collective-permute-start | bytes 393224 | tf_op jit(solution)/shard_map/ppermute | solution.py:464
  84.8 6.1 %collective-permute-start.26 = (bf16[64,1024]{1,0:T(8,128)(2,1)S(1)}, bf16[64,1024]{1,0:T(8,128)(2,1)S(1)}, u32[]{:S(2)}, u32[]{:S(2)}) collective-permute-start(bf16[64,1024]{1,0:T(8,128)(2,1)S(1)} %get-tuple-element.171), channel_id=1, source_target_pairs={{0,1},{1,0},{2,3},{3,2},{4,5},{5,4},{6,7},{7,6},{8,9},{9,8},{10,11... | collective-permute-start | bytes 393224 | tf_op jit(solution)/shard_map/ppermute | solution.py:464
  85.5 6.9 %collective-permute-start.27 = (bf16[48,1024]{1,0:T(8,128)(2,1)S(1)}, bf16[48,1024]{1,0:T(8,128)(2,1)S(1)}, u32[]{:S(2)}, u32[]{:S(2)}) collective-permute-start(bf16[48,1024]{1,0:T(8,128)(2,1)S(1)} %get-tuple-element.178), channel_id=1, source_target_pairs={{0,4},{4,0},{8,12},{12,8},{16,20},{20,16},{24,28},{28,24},{1,5},{5... | collective-permute-start | bytes 294920 | tf_op jit(solution)/shard_map/ppermute | solution.py:470
  88.5 9.5 %collective-permute-start.28 = (bf16[48,1024]{1,0:T(8,128)(2,1)S(1)}, bf16[48,1024]{1,0:T(8,128)(2,1)S(1)}, u32[]{:S(2)}, u32[]{:S(2)}) collective-permute-start(bf16[48,1024]{1,0:T(8,128)(2,1)S(1)} %get-tuple-element.179), channel_id=1, source_target_pairs={{0,8},{4,12},{8,0},{12,4},{16,24},{20,28},{24,16},{28,20},{1,9},{5... | collective-permute-start | bytes 294920 | tf_op jit(solution)/shard_map/ppermute | solution.py:470
  88.5 9.5 %collective-permute-start.29 = (bf16[48,1024]{1,0:T(8,128)(2,1)S(1)}, bf16[48,1024]{1,0:T(8,128)(2,1)S(1)}, u32[]{:S(2)}, u32[]{:S(2)}) collective-permute-start(bf16[48,1024]{1,0:T(8,128)(2,1)S(1)} %get-tuple-element.180), channel_id=1, source_target_pairs={{0,12},{4,8},{8,4},{12,0},{16,28},{20,24},{24,20},{28,16},{1,13},{... | collective-permute-start | bytes 294920 | tf_op jit(solution)/shard_map/ppermute | solution.py:470
  98.3 1.6 %collective-permute-start.31 = (bf16[128,1024]{1,0:T(8,128)(2,1)S(1)}, bf16[128,1024]{1,0:T(8,128)(2,1)S(1)}, u32[]{:S(2)}, u32[]{:S(2)}) collective-permute-start(bf16[128,1024]{1,0:T(8,128)(2,1)S(1)} %packed_back_far.1.refs_0_), channel_id=1, source_target_pairs={{0,1},{1,0},{2,3},{3,2},{4,5},{5,4},{6,7},{7,6},{8,9},{9,8},{10,11... | collective-permute-start | bytes 786440 | tf_op jit(solution)/shard_map/ppermute | solution.py:464
  101.4 9.3 %collective-permute-start.34 = (bf16[4,128,256]{2,1,0:T(8,128)(2,1)S(1)}, bf16[4,128,256]{2,1,0:T(8,128)(2,1)S(1)}, u32[]{:S(2)}, u32[]{:S(2)}) collective-permute-start(bf16[4,128,256]{2,1,0:T(8,128)(2,1)S(1)} %get-tuple-element.200), channel_id=1, source_target_pairs={{0,4},{4,0},{8,12},{12,8},{16,20},{20,16},{24,28},{28,24},{1,5},{5... | collective-permute-start | bytes 786440 | tf_op jit(solution)/shard_map/ppermute | solution.py:470
  105.1 13.5 %collective-permute-start.32 = (bf16[4,128,256]{2,1,0:T(8,128)(2,1)S(1)}, bf16[4,128,256]{2,1,0:T(8,128)(2,1)S(1)}, u32[]{:S(2)}, u32[]{:S(2)}) collective-permute-start(bf16[4,128,256]{2,1,0:T(8,128)(2,1)S(1)} %get-tuple-element.188), channel_id=1, source_target_pairs={{0,16},{4,20},{8,24},{12,28},{16,0},{20,4},{24,8},{28,12},{1,17},{... | collective-permute-start | bytes 786440 | tf_op jit(solution)/shard_map/ppermute | solution.py:470
  105.9 12.7 %collective-permute-start.33 = (bf16[96,1024]{1,0:T(8,128)(2,1)S(1)}, bf16[96,1024]{1,0:T(8,128)(2,1)S(1)}, u32[]{:S(2)}, u32[]{:S(2)}) collective-permute-start(bf16[96,1024]{1,0:T(8,128)(2,1)S(1)} %get-tuple-element.194), channel_id=1, source_target_pairs={{0,16},{4,20},{8,24},{12,28},{16,0},{20,4},{24,8},{28,12},{1,17},{... | collective-permute-start | bytes 589832 | tf_op jit(solution)/shard_map/ppermute | solution.py:470
  107.7 17.8 %collective-permute-start.30 = (bf16[128,1024]{1,0:T(8,128)(2,1)S(1)}, bf16[128,1024]{1,0:T(8,128)(2,1)S(1)}, u32[]{:S(2)}, u32[]{:S(2)}) collective-permute-start(bf16[128,1024]{1,0:T(8,128)(2,1)S(1)} %ffn_out_far.1), channel_id=1, source_target_pairs={{0,2},{1,3},{2,0},{3,1},{4,6},{5,7},{6,4},{7,5},{8,10},{9,11},{10,... | collective-permute-start | bytes 786440 | tf_op jit(solution)/shard_map/ppermute | solution.py:467
  111.2 9.0 %collective-permute-start.35 = (bf16[2,128,256]{2,1,0:T(8,128)(2,1)S(1)}, bf16[2,128,256]{2,1,0:T(8,128)(2,1)S(1)}, u32[]{:S(2)}, u32[]{:S(2)}) collective-permute-start(bf16[2,128,256]{2,1,0:T(8,128)(2,1)S(1)} %get-tuple-element.202), channel_id=1, source_target_pairs={{0,16},{4,20},{8,24},{12,28},{16,0},{20,4},{24,8},{28,12},{1,17},{... | collective-permute-start | bytes 393224 | tf_op jit(solution)/shard_map/ppermute | solution.py:470
  119.2 5.7 %collective-permute-start.37 = (bf16[2,128,256]{2,1,0:T(8,128)(2,1)S(1)}, bf16[2,128,256]{2,1,0:T(8,128)(2,1)S(1)}, u32[]{:S(2)}, u32[]{:S(2)}) collective-permute-start(bf16[2,128,256]{2,1,0:T(8,128)(2,1)S(1)} %get-tuple-element.208), channel_id=1, source_target_pairs={{0,4},{4,0},{8,12},{12,8},{16,20},{20,16},{24,28},{28,24},{1,5},{5... | collective-permute-start | bytes 393224 | tf_op jit(solution)/shard_map/ppermute | solution.py:470
  120.8 7.0 %collective-permute-start.36 = (bf16[1,128,256]{2,1,0:T(8,128)(2,1)S(1)}, bf16[1,128,256]{2,1,0:T(8,128)(2,1)S(1)}, u32[]{:S(2)}, u32[]{:S(2)}) collective-permute-start(bf16[1,128,256]{2,1,0:T(8,128)(2,1)S(1)} %get-tuple-element.204), channel_id=1, source_target_pairs={{0,8},{4,12},{8,0},{12,4},{16,24},{20,28},{24,16},{28,20},{1,9},{5... | collective-permute-start | bytes 196616 | tf_op jit(solution)/shard_map/ppermute | solution.py:470
  125.5 5.3 %collective-permute-start.38 = (bf16[1,128,256]{2,1,0:T(8,128)(2,1)S(1)}, bf16[1,128,256]{2,1,0:T(8,128)(2,1)S(1)}, u32[]{:S(2)}, u32[]{:S(2)}) collective-permute-start(bf16[1,128,256]{2,1,0:T(8,128)(2,1)S(1)} %get-tuple-element.210), channel_id=1, source_target_pairs={{0,8},{4,12},{8,0},{12,4},{16,24},{20,28},{24,16},{28,20},{1,9},{5... | collective-permute-start | bytes 196616 | tf_op jit(solution)/shard_map/ppermute | solution.py:470

commit v6 on v5

--- a/solution.py
+++ b/solution.py
@@ -49,29 +49,32 @@
     return jax.ShapeDtypeStruct(shape, dtype)
 
 
-def run(body, outs, scalars, args, scratch=(), flops=0, name=None, limit=16, space=pltpu.VMEM):
-    specs = [pl.BlockSpec(memory_space=space)] * len(args)
-    operands = list(args)
-    if scalars is not None:
-        specs = [pl.BlockSpec(memory_space=pltpu.SMEM)] + specs
-        operands = [scalars] + operands
+def run(body, outs, args, scratch=(), flops=0, name=None):
     return pl.pallas_call(
         body,
         out_shape=list(outs),
-        in_specs=specs,
+        in_specs=[pl.BlockSpec(memory_space=pltpu.VMEM)] * len(args),
         out_specs=[pl.BlockSpec(memory_space=pltpu.VMEM)] * len(outs),
         scratch_shapes=list(scratch),
-        compiler_params=pltpu.CompilerParams(vmem_limit_bytes=limit * MIB),
+        compiler_params=pltpu.CompilerParams(vmem_limit_bytes=16 * MIB),
         cost_estimate=pl.CostEstimate(flops=flops, bytes_accessed=0, transcendentals=0),
         name=name,
-    )(*operands)
+    )(*args)
+
+
+def group_index():
+    return lax.axis_index("event") * lax.axis_size("pack") + lax.axis_index("pack")
+
+
+def tensor_index():
+    return lax.axis_index("tensor")
 
 
 def tie(*values):
     return lax.optimization_barrier(values)
 
 
-def route_send(capacity, where, code, features, *outs):
+def route_send(capacity, order, code, features, *outs):
     sends, place_ref = outs[:-1], outs[-1]
     groups = len(sends)
     rows, width = features.shape
@@ -83,16 +86,16 @@
     j = lax.broadcasted_iota(jnp.int32, (rows, rows), 1)
     earlier = jnp.where((o_col == o_row.astype(F32)) & (i < j), 1.0, 0.0)
     rank = jnp.sum(earlier, axis=0, keepdims=True).astype(jnp.int32)
-    place = (o_row ^ where[0]) * capacity + rank
-    place_ref[...] = place
+    place_ref[...] = o_row * capacity + rank
+    place = (o_row ^ group_index()) * capacity + rank
     spots = lax.broadcasted_iota(jnp.int32, (groups * capacity, rows), 0)
     hot = jnp.where(spots == place, 1.0, 0.0).astype(BF16)
     big = dot(hot, features[...])
     tags = dot(hot, bf16(turned(slot + 1, rows)))
-    for k in range(groups):
+    for k, send in zip(order, sends):
         part = slice(k * capacity, (k + 1) * capacity)
-        sends[k][:, :width] = bf16(big[part])
-        sends[k][:, width:] = bf16(tags[part])
+        send[:, :width] = bf16(big[part])
+        send[:, width:] = bf16(tags[part])
 
 
 def route_recv(*refs):
@@ -105,38 +108,21 @@
     rows_ref[...] = bf16(dot(hot, bf16(got[:, :width]), TN))
 
 
-def back_send(events, hot, d_packed, *sends):
-    packs = len(sends)
-    capacity = hot.shape[0] // (events * packs)
+def back_send(order, hot, d_packed, out):
+    capacity = out.shape[1]
     big = dot(hot[...], d_packed[...])
-    for b in range(packs):
-        parts = [
-            big[(a * packs + b) * capacity : (a * packs + b + 1) * capacity] for a in range(events)
-        ]
-        sends[b][...] = bf16(jnp.concatenate(parts, axis=0))
-
-
-def back_turn(*refs):
-    events = refs[-1]
-    refs = refs[:-1]
-    packs = len(refs) - (events - 1) - 1
-    gots, own, sends = refs[:packs], refs[packs], refs[packs + 1 :]
-    wide = [g[...].astype(F32) for g in gots]
-    capacity = wide[0].shape[0] // events
-    for a, target in enumerate((own, *sends)):
-        parts = [w[a * capacity : (a + 1) * capacity] for w in wide]
-        target[...] = bf16(jnp.concatenate(parts, axis=0))
-
-
-def back_recv(place, *refs):
-    gots, out = refs[:-1], refs[-1]
-    got = jnp.concatenate([g[...] for g in gots], axis=0)
+    for n, k in enumerate(order):
+        out[group_index() ^ k] = bf16(big[n * capacity : (n + 1) * capacity])
+
+
+def back_recv(place, got_ref, out):
+    got = jnp.concatenate([got_ref[k].astype(F32) for k in range(got_ref.shape[0])], axis=0)
     spots = lax.broadcasted_iota(jnp.int32, (got.shape[0], out.shape[0]), 0)
     hot = jnp.where(spots == place[...], 1.0, 0.0).astype(BF16)
-    out[...] = bf16(dot(hot, got, TN))
-
-
-def encode(where, rows, enc, w_in, pre_all, pre_ref, act_ref, packed_ref, store):
+    out[...] = bf16(dot(hot, bf16(got), TN))
+
+
+def encode(rows, enc, w_in, pre_all, pre_ref, act_ref, packed_ref, store):
     width = rows.shape[1]
     cols = pre_ref.shape[1]
     for n in range(width // CHUNK):
@@ -144,7 +130,7 @@
         pre = dot(rows, enc[0, :, part])
         pre_all[:, part] = pre
         act_ref[:, part] = bf16(pre * jax.nn.sigmoid(pre))
-    pre_ref[...] = pre_all[:, pl.ds(pl.multiple_of(where[1] * cols, cols), cols)]
+    pre_ref[...] = pre_all[:, pl.ds(pl.multiple_of(tensor_index() * cols, cols), cols)]
     packed = bf16(dot(act_ref[...], enc[1]))
     packed_ref[...] = packed[: packed_ref.shape[0]]
     wide = packed.astype(F32)
@@ -153,7 +139,7 @@
         store(c, bf16(dot(normed, w_in[c])))
 
 
-def encode_first(where, first, second, enc, w_in, pre_ref, act_ref, packed_ref, proj_ref, pre_all):
+def encode_first(first, second, enc, w_in, pre_ref, act_ref, packed_ref, proj_ref, pre_all):
     rows = jnp.concatenate([first[...], second[...]], axis=0)
     half = first.shape[0]
 
@@ -161,11 +147,11 @@
         proj_ref[c, 0] = value[:half]
         proj_ref[c, 1] = value[half:]
 
-    encode(where, rows, enc, w_in, pre_all, pre_ref, act_ref, packed_ref, store)
-
-
-def window(where, docs, r, rows):
-    t = where[1]
+    encode(rows, enc, w_in, pre_all, pre_ref, act_ref, packed_ref, store)
+
+
+def window(docs, r, rows):
+    t = tensor_index()
     b = t ^ r
     ahead = jnp.where(b > 0, (b - 1) ^ t, r)
     doc_q = turned(docs[b], rows)
@@ -199,7 +185,7 @@
 
 
 def attend_first(
-    where, docs, third, fourth, proj_a, enc, w_in,
+    docs, third, fourth, proj_a, enc, w_in,
     pre_ref, act_ref, packed_ref, proj_ref, att_ref, give_ref, keep_ref, pre_all,
 ):
     rows = jnp.concatenate([third[...], fourth[...]], axis=0)
@@ -211,10 +197,10 @@
         proj_ref[c, 2] = value[:half]
         proj_ref[c, 3] = value[half:]
 
-    encode(where, rows, enc, w_in, pre_all, pre_ref, act_ref, packed_ref, store)
+    encode(rows, enc, w_in, pre_all, pre_ref, act_ref, packed_ref, store)
     masks = head_masks(cols)
     for r, (target, place) in enumerate(((keep_ref, 1), (give_ref, 1), (keep_ref, 0), (give_ref, 0))):
-        ahead, allowed, root_inv = window(where, docs, r, half)
+        ahead, allowed, root_inv = window(docs, r, half)
         keys = jnp.concatenate([proj_ref[1, ahead], proj_ref[1, r]], axis=0)
         values = jnp.concatenate([proj_ref[2, ahead], proj_ref[2, r]], axis=0)
         many = jnp.concatenate([allowed] * len(masks), axis=0)
@@ -285,10 +271,10 @@
     store_halves(bf16(d_out[...].astype(F32) + norm_back(grad, wide * factor, factor)), out, halves)
 
 
-def attend_back(where, docs, d_resid, r, proj_ref, att_ref, w_out, masks, d_q, d_k, d_v, d_g):
+def attend_back(docs, d_resid, r, proj_ref, att_ref, w_out, masks, d_q, d_k, d_v, d_g):
     half = d_resid.shape[0]
     scale = HEAD ** (-0.5)
-    ahead, allowed, root_inv = window(where, docs, r, half)
+    ahead, allowed, root_inv = window(docs, r, half)
     gate = proj_ref[3, r].astype(F32)
     sigma_g = jax.nn.sigmoid(gate)
     d_gated = dot(d_resid, w_out, NT)
@@ -317,12 +303,12 @@
     return jnp.concatenate([r[...] for r in refs], axis=0)
 
 
-def attn_back_first(where, docs, third, fourth_a, fourth_b, proj, att, w_out, d_q, d_k, d_v, d_g):
+def attn_back_first(docs, third, fourth_a, fourth_b, proj, att, w_out, d_q, d_k, d_v, d_g):
     masks = head_masks(w_out.shape[0])
     d_k[...] = jnp.zeros_like(d_k)
     d_v[...] = jnp.zeros_like(d_v)
     for r, rows in ((2, [third]), (3, [fourth_a, fourth_b])):
-        attend_back(where, docs, joined(rows), r, proj, att, w_out[...], masks, d_q, d_k, d_v, d_g)
+        attend_back(docs, joined(rows), r, proj, att, w_out[...], masks, d_q, d_k, d_v, d_g)
 
 
 def back_norm(grads, w_in, first, second):
@@ -335,7 +321,7 @@
 
 
 def attn_back_second(
-    where, docs, first, second, proj, att, w_out, d_q_far, d_k_far, d_v_far, d_g_far, w_in,
+    docs, first, second, proj, att, w_out, d_q_far, d_k_far, d_v_far, d_g_far, w_in,
     give_ref, d_q, d_k, d_v, d_g, sum_k, sum_v,
 ):
     masks = head_masks(w_out.shape[0])
@@ -344,7 +330,7 @@
     sum_k[...] = d_k_far[...]
     sum_v[...] = d_v_far[...]
     for r, rows in ((0, first), (1, second)):
-        attend_back(where, docs, rows[...], r, proj, att, w_out[...], masks, d_q, sum_k, sum_v, d_g)
+        attend_back(docs, rows[...], r, proj, att, w_out[...], masks, d_q, sum_k, sum_v, d_g)
     d_k[...] = bf16(sum_k[...])
     d_v[...] = bf16(sum_v[...])
     give_ref[...] = bf16(back_norm((d_q, d_k, d_v, d_g), w_in, 3, 1))
@@ -375,29 +361,29 @@
     return dot(jnp.concatenate([a[...] for a in act_refs], axis=0), cot, TN)
 
 
-def first_cot(where, cots, pre, enc):
+def first_cot(cots, pre, enc):
     cols = pre.shape[1]
     cot = joined(cots)
     value = pre[...]
-    w1_rows = enc[1, pl.ds(pl.multiple_of(where[1] * cols, cols), cols), :]
+    w1_rows = enc[1, pl.ds(pl.multiple_of(tensor_index() * cols, cols), cols), :]
     return bf16(dot(cot, w1_rows, NT) * silu_grad(value, jax.nn.sigmoid(value)))
 
 
-def cot_columns(where, cots, cols):
-    return jnp.concatenate([column_of(c, where[1], cols) for c in cots], axis=0)
-
-
-def enc_grads_first(where, *refs):
+def cot_columns(cots, cols):
+    return jnp.concatenate([column_of(c, tensor_index(), cols) for c in cots], axis=0)
+
+
+def enc_grads_first(*refs):
     cots, (act0_a, act0_b, act1, pre, enc, part1, part0) = refs[:-7], refs[-7:]
     cols = pre.shape[1]
-    part1[...] = rows_term([act1], cot_columns(where, cots, cols))
-    part0[...] = rows_term([act0_a, act0_b], first_cot(where, cots, pre, enc))
-
-
-def halve(where, bits, bit, total, keep, send):
+    part1[...] = rows_term([act1], cot_columns(cots, cols))
+    part0[...] = rows_term([act0_a, act0_b], first_cot(cots, pre, enc))
+
+
+def halve(bits, bit, total, keep, send):
     place = bits.index(bit)
     count, size, _ = keep.shape
-    mine = (where[0] >> bit) & 1
+    mine = (group_index() >> bit) & 1
     for j in range(count):
         low = j & ((1 << place) - 1)
         base = ((j >> place) << (place + 1)) | low
@@ -407,21 +393,21 @@
             target[j] = rows.astype(target.dtype)
 
 
-def enc_grad1_second(bits, bit, where, *refs):
+def enc_grad1_second(bits, bit, *refs):
     cots, (act1, part1, keep, send, total) = refs[:-5], refs[-5:]
-    total[...] = rows_term([act1], cot_columns(where, cots, part1.shape[1])) + part1[...]
-    halve(where, bits, bit, total, keep, send)
-
-
-def enc_grad0_second(bits, bit, where, *refs):
+    total[...] = rows_term([act1], cot_columns(cots, part1.shape[1])) + part1[...]
+    halve(bits, bit, total, keep, send)
+
+
+def enc_grad0_second(bits, bit, *refs):
     cots, (act0_a, act0_b, pre, enc, part0, keep, send, total) = refs[:-8], refs[-8:]
-    total[...] = rows_term([act0_a, act0_b], first_cot(where, cots, pre, enc)) + part0[...]
-    halve(where, bits, bit, total, keep, send)
-
-
-def halve_again(bits, bit, where, kept, got, keep, send):
+    total[...] = rows_term([act0_a, act0_b], first_cot(cots, pre, enc)) + part0[...]
+    halve(bits, bit, total, keep, send)
+
+
+def halve_again(bits, bit, kept, got, keep, send):
     place = bits.index(bit)
-    mine = (where[0] >> bit) & 1
+    mine = (group_index() >> bit) & 1
     for j in range(keep.shape[0]):
         low = j & ((1 << place) - 1)
         base = ((j >> place) << (place + 1)) | low
@@ -450,13 +436,11 @@
     rows_dev, width = features.shape
     group_axes = ("event", "pack")
     groups = lax.axis_size(group_axes)
-    events = lax.axis_size("event")
     packs = lax.axis_size("pack")
     tensors = lax.axis_size("tensor")
     cols = attn_in.shape[2]
     comps = attn_in.shape[0]
     units = ffn_out.shape[0]
-    where = jnp.stack([lax.axis_index(group_axes), lax.axis_index("tensor")]).astype(jnp.int32)
     d_out = out_grad[0]
     docs = doc_ids.reshape(tensors, 1, rows_dev)
 
@@ -475,25 +459,23 @@
     mean_load = rows_dev // groups
     capacity = -(-(mean_load + mean_load // 2) // 8) * 8
     code = (dest_owner * rows_dev + dest_slot).reshape(1, rows_dev)
+    order = [0] + sorted(
+        range(1, groups), key=lambda k: (-((2 * (k % packs)) // packs), k % packs, k)
+    )
     *sends, place = run(
-        functools.partial(route_send, capacity),
+        functools.partial(route_send, capacity, order),
         [like((capacity, width + rows_dev), BF16)] * groups + [like((1, rows_dev), jnp.int32)],
-        where,
         [code, features],
         flops=4 * 10**9,
         name="route_send",
     )
-    order = sorted(range(1, groups), key=lambda k: (-(k % packs), k))
-    ffn_in_near, ffn_out_near, d_out_far = near(ffn_in), near(ffn_out), far(d_out)
-    early = {k: crossed(sends[k], k) for k in order[:2]}
+    ffn_in_near, ffn_out_near = near(ffn_in), near(ffn_out)
+    early = [crossed(sends[n], order[n]) for n in (1, 2)]
     ffn_in_near, ffn_out_near, *sends = tie(ffn_in_near, ffn_out_near, *sends)
-    crossing = early | {k: crossed(sends[k], k) for k in order[2:]}
-    gots = [sends[0]] + [crossing[k] for k in range(1, groups)]
-    d_out_far, *gots = tie(d_out_far, *gots)
+    gots = [sends[0], *early] + [crossed(sends[n], order[n]) for n in range(3, groups)]
     mine, hot = run(
         route_recv,
         [row_b, like((groups * capacity, rows_dev), BF16)],
-        None,
         gots,
         name="route_recv",
     )
@@ -510,15 +492,15 @@
             row_b,
             like((comps, 2, rows_dev, cols), BF16),
         ],
-        where,
         [mine, mine_near, enc_weight, attn_in],
         [pltpu.VMEM((pair, width), F32)],
         name="encode_first",
     )
     mine_far, proj_a = tie(mine_far, proj_a)
-    mine_far, attn_out_late = tie(mine_far, attn_out)
+    mine_far, attn_out_late, d_out_late = tie(mine_far, attn_out, d_out)
     mine_both = near(mine_far)
     attn_out_near = near(attn_out_late)
+    d_out_far = far(d_out_late)
     pre_b, act_b, packed_far, proj, attended, give, keep = run(
         attend_first,
         [
@@ -530,19 +512,18 @@
             like((pair, cols), BF16),
             like((pair, cols), BF16),
         ],
-        where,
         [docs, mine_far, mine_both, proj_a, enc_weight, attn_in],
         [pltpu.VMEM((pair, width), F32)],
         name="attend_first",
     )
     take = near(give)
+    take, d_out_far = tie(take, d_out_far)
 
 
     def out_part(index, name):
         return run(
             functools.partial(attn_out_part, index),
             [row_b],
-            None,
             [keep, take, attn_out, attn_out_near],
             name=name,
         )[0]
@@ -556,17 +537,16 @@
         return run(
             ffn,
             [like((rows_dev, 2 * units), BF16), row_b],
-            None,
             [rows, cotangent, ffn_in, ffn_in_near, ffn_out, ffn_out_near],
             name=name,
         )
 
-    resid, normed2 = run(residual, [row_b, row_b], None, [packed, part_own, got_own], name="residual")
+    resid, normed2 = run(residual, [row_b, row_b], [packed, part_own, got_own], name="residual")
     hidden_own, back_own = feed(normed2, d_out, "ffn_own")
     got_far, back_own = tie(got_far, back_own)
     got_back_far = far(back_own)
     resid_far, normed2_far = run(
-        residual, [row_b, row_b], None, [packed_far, part_far, got_far], name="residual_far"
+        residual, [row_b, row_b], [packed_far, part_far, got_far], name="residual_far"
     )
     hidden_far, back_far = feed(normed2_far, d_out_far, "ffn_far")
     got_back_own = far(back_far)
@@ -576,7 +556,6 @@
     d_resid_far, *halves = run(
         resid_back,
         [row_b] + [piece_b] * pieces,
-        None,
         [back_far, got_back_far, resid_far, d_out_far],
         name="resid_back_far",
     )
@@ -586,17 +565,15 @@
     d_q, d_k, d_v, d_g = run(
         attn_back_first,
         [block_b, block_f, block_f, block_b],
-        where,
         [docs, d_resid_far, *d_resid_both, proj, attended, attn_out],
         name="attn_back_first",
     )
     got_back_own, d_q = tie(got_back_own, d_q)
-    (d_resid,) = run(resid_back, [row_b], None, [back_own, got_back_own, resid, d_out], name="resid_back")
+    (d_resid,) = run(resid_back, [row_b], [back_own, got_back_own, resid, d_out], name="resid_back")
     d_resid_near = near(d_resid)
     give, *d_projected = run(
         attn_back_second,
         [like((pair, width), BF16)] + [block_b] * 4,
-        where,
         [docs, d_resid, d_resid_near, proj, attended, attn_out, d_q, d_k, d_v, d_g, attn_in],
         [pltpu.VMEM((tensors, rows_dev, cols), F32)] * 2,
         name="attn_back_second",
@@ -605,61 +582,44 @@
     (keep,) = run(
         attn_back_keep,
         [like((pair, width), F32)],
-        None,
         [*d_projected, attn_in],
         name="attn_back_keep",
     )
-    sum_far, sum_own = run(add_near, [row_b, row_b], None, [keep, take], name="add_near")
+    sum_far, sum_own = run(add_near, [row_b, row_b], [keep, take], name="add_near")
     got_own = far(sum_far)
     got_far = far(sum_own)
     d_packed, *halves = run(
         packed_back,
         [row_b] + [piece_b] * pieces,
-        None,
         [sum_own, got_own, packed, d_resid],
         name="packed_back",
     )
 
     cot_near = [near(h) for h in halves]
-    backs = run(
-        functools.partial(back_send, events),
-        [like((events * capacity, width), BF16)] * packs,
-        None,
+    (backs,) = run(
+        functools.partial(back_send, order),
+        [like((groups, capacity, width), BF16)],
         [hot, d_packed],
         name="back_send",
     )
-    over_pack = [backs[0]] + [crossed(backs[b], b) for b in range(1, packs)]
+    returned = lax.all_to_all(backs, group_axes, split_axis=0, concat_axis=0, tiled=True)
+
     part_f = like((width, cols), F32)
     part1, part0 = run(
         enc_grads_first,
         [part_f, part_f],
-        where,
         [d_packed, *cot_near, mine, mine_near, act_a, pre_a, enc_weight],
         name="enc_grads_first",
     )
-    got_far, part1, part0, *over_pack = tie(got_far, part1, part0, *over_pack)
+    got_far, part1, part0 = tie(got_far, part1, part0)
     (cot_far,) = run(
-        packed_back, [row_b], None, [sum_far, got_far, packed_far, d_resid_far], name="packed_back_far"
+        packed_back, [row_b], [sum_far, got_far, packed_far, d_resid_far], name="packed_back_far"
     )
     cot_both = near(cot_far)
-    back_own, *back_sends = run(
-        lambda *refs: back_turn(*refs, events),
-        [like((packs * capacity, width), BF16)] * events,
-        None,
-        over_pack,
-        name="back_turn",
-    )
-    over_event = [back_own] + [crossed(v, (a + 1) * packs) for a, v in enumerate(back_sends)]
-
     cot_far, hidden_far = tie(cot_far, hidden_far)
     (out_far,) = run(
-        ffn_out_far, [row_b], None, [hidden_far, ffn_out, ffn_out_near], name="ffn_out_far"
-    )
-    got_out = far(out_far)
-    (packed_out,) = run(
-        ffn_out_own, [row_b], None, [hidden_own, ffn_out, ffn_out_near, resid, got_out], name="ffn_out_own"
-    )
-
+        ffn_out_far, [row_b], [hidden_far, ffn_out, ffn_out_near], name="ffn_out_far"
+    )
     bits = list(range(groups.bit_length() - 1))
     pack_bits = bits[: packs.bit_length() - 1]
     event_bits = bits[len(pack_bits) :]
@@ -670,31 +630,27 @@
         shape = (2 ** (len(remaining) - 1), size, cols)
         return [like(shape, F32), like(shape, BF16)]
 
-    def reduce_over(stages, start, name):
-        nonlocal over_event
+    def reduce_over(stages, start, held, name):
         remaining = list(bits)
         kept, send = start((tuple(remaining), stages[0]))
         got = crossed(send, 1 << stages[0])
-        if stages[0] in event_bits:
-            got, *over_event = tie(got, *over_event)
+        got, held = tie(got, held)
         remaining.remove(stages[0])
         for bit in stages[1:]:
             kept, send = run(
                 functools.partial(halve_again, tuple(remaining), bit),
                 halves(remaining),
-                where,
                 [kept, got],
                 name=name + str(bit),
             )
             got = crossed(send, 1 << bit)
             remaining.remove(bit)
-        return kept, got
+        return kept, got, held
 
     def start1(setting):
         return run(
             functools.partial(enc_grad1_second, *setting),
             halves(bits),
-            where,
             [cot_far, cot_both, act_b, part1],
             total,
             name="enc_grad1_second",
@@ -704,22 +660,27 @@
         return run(
             functools.partial(enc_grad0_second, *setting),
             halves(bits),
-            where,
             [cot_far, cot_both, mine_far, mine_both, pre_b, enc_weight, part0],
             total,
             name="enc_grad0_second",
         )
 
-    kept1, got1 = reduce_over(event_bits + pack_bits, start1, "halve1_")
-    kept0, got0 = reduce_over(pack_bits[:1] + event_bits + pack_bits[1:], start0, "halve0_")
+    kept1, got1, returned = reduce_over(event_bits + pack_bits, start1, returned, "halve1_")
+    kept0, got0, out_far = reduce_over(
+        pack_bits[:1] + event_bits + pack_bits[1:], start0, out_far, "halve0_"
+    )
+    got_out = far(out_far)
+    (packed_out,) = run(
+        ffn_out_own, [row_b], [hidden_own, ffn_out, ffn_out_near, resid, got_out], name="ffn_out_own"
+    )
     (row_grad,) = run(
         back_recv,
         [row_b],
-        None,
-        [place] + over_event,
+        [place, returned],
         name="back_recv",
     )
-    (enc_grad,) = run(finish, [like((2, size, cols), F32)], None, [kept0, got0, kept1, got1], name="finish")
+    got1, got0, packed_out, row_grad = tie(got1, got0, packed_out, row_grad)
+    (enc_grad,) = run(finish, [like((2, size, cols), F32)], [kept0, got0, kept1, got1], name="finish")
     return (packed_out[None], row_grad, enc_grad)
 
 

time: 132 us -> 132 us (level)
  waiting for transfers between devices: 60.7 us -> 40.1 us
  local copies, waits for them, and re-layouts: 0.99 us -> 15.8 us
  starting transfers between devices: 36.5 us -> 40.1 us
  Pallas kernels: 31.6 us -> 33.7 us
    ppermute x17 -> x13, waiting for transfers between devices: 27.9 us -> 11.5 us  [crossed(): return lax.ppermute(value, group_axes, [(i, i ^ k) for i in range(groups)])]
    unnamed x16 -> x72, local copies, waits for them, and re-layouts: 0.99 us -> 15.8 us
    all_to_all x0 -> x1, starting transfers between devices: none -> 4.74 us  [shards(): lax.all_to_all(backs, group_axes, split_axis=0, concat_axis=0, tiled=True)]
    ppermute x13, waiting for transfers between devices: 8.57 us -> 5.37 us  [near(): return lax.ppermute(value, 'tensor', [(i, i ^ 1) for i in range(tensors)])]
    pallas_call x31 -> x30, Pallas kernels: 31.6 us -> 33.7 us  [run(): pl.pallas_call(body, out_shape=list(outs), in_specs=[pl.BlockSpec(memory_...]
    ppermute x17 -> x13, starting transfers between devices: 23.2 us -> 21.8 us  [crossed(): return lax.ppermute(value, group_axes, [(i, i ^ k) for i in range(groups)])]
  transfers between devices with their start and end apart: 39 -> 36, of which waited for: 24 -> 19; matrix products, arithmetic and copies ran while one was open for 1% -> 1% of each run, Pallas kernels for 19% -> 22%
where the time goes in v6:
time: 132 us; the launch traced here: 131 us
  starting transfers between devices  40.1 us (30%)
  waiting for transfers between devices  40.1 us (30%)
  Pallas kernels  33.7 us (26%)
  local copies, waits for them, and re-layouts  15.8 us (12%)
    pallas_call x30, Pallas kernels, run(): pl.pallas_call(body, out_shape=list(outs), in_specs=[pl.BlockSpec(memory_...  33.7 us
    ppermute x9, waiting for transfers between devices, far(): return lax.ppermute(value, 'tensor', [(i, i ^ 2) for i in range(tensors)])  23.2 us
    ppermute x13, starting transfers between devices, crossed(): return lax.ppermute(value, group_axes, [(i, i ^ k) for i in range(groups)])  21.8 us
    unnamed x72, local copies, waits for them, and re-layouts  15.8 us
    ppermute x13, waiting for transfers between devices, crossed(): return lax.ppermute(value, group_axes, [(i, i ^ k) for i in range(groups)])  11.5 us
    ppermute x9, starting transfers between devices, far(): return lax.ppermute(value, 'tensor', [(i, i ^ 2) for i in range(tensors)])  10.9 us
    ppermute x13, waiting for transfers between devices, near(): return lax.ppermute(value, 'tensor', [(i, i ^ 1) for i in range(tensors)])  5.37 us
    all_to_all x1, starting transfers between devices, shards(): lax.all_to_all(backs, group_axes, split_axis=0, concat_axis=0, tiled=True)  4.74 us
  transfers between devices with their start and end apart: 36, of which 19 were waited for; matrix products, arithmetic and copies ran while one was open for 1% of the time, Pallas kernels for 22%

profile of v6, /device:TPU:0, one launch (start us, length us, event | category | flops | bytes accessed | tf_op | source)
XLA Modules:
  0.0 131.5 jit_solution(6895609670644890771)
XLA Ops:
  1.9 0.9 copy-done.35
  3.2 4.1 %collective-permute-start.2 = (bf16[24,1152]{1,0:T(8,128)(2,1)S(1)}, bf16[24,1152]{1,0:T(8,128)(2,1)S(1)}, u32[]{:S(2)}, u32[]{:S(2)}) collective-permute-start(bf16[24,1152]{1,0:T(8,128)(2,1)S(1)} %get-tuple-element.97), channel_id=1, source_target_pairs={{0,8},{4,12},{8,0},{12,4},{16,24},{20,28},{24,16},{28,20},{1,9},{5... | collective-permute-start | bytes 165896 | tf_op jit(solution)/shard_map/ppermute | solution.py:454
  7.3 1.3 collective-permute-start.3
  8.6 3.6 %collective-permute-start.4 = (bf16[24,1152]{1,0:T(8,128)(2,1)S(1)}, bf16[24,1152]{1,0:T(8,128)(2,1)S(1)}, u32[]{:S(2)}, u32[]{:S(2)}) collective-permute-start(bf16[24,1152]{1,0:T(8,128)(2,1)S(1)} %get-tuple-element.105), channel_id=1, source_target_pairs={{0,12},{4,8},{8,4},{12,0},{16,28},{20,24},{24,20},{28,16},{1,13},{... | collective-permute-start | bytes 165896 | tf_op jit(solution)/shard_map/ppermute | solution.py:454
  12.8 1.1 collective-permute-start.6
  13.9 2.2 %collective-permute-done.3.refs_2_ = bf16[24,1152]{1,0:T(8,128)(2,1)S(1)} collective-permute-done((bf16[24,1152]{1,0:T(8,128)(2,1)S(1)}, bf16[24,1152]{1,0:T(8,128)(2,1)S(1)}, u32[]{:S(2)}, u32[]{:S(2)}) %collective-permute-start.3) | collective-permute-done | bytes 55328 | tf_op jit(solution)/shard_map/ppermute | solution.py:454
  16.4 2.8 %collective-permute-done.5.refs_4_ = bf16[24,1152]{1,0:T(8,128)(2,1)S(1)} collective-permute-done((bf16[24,1152]{1,0:T(8,128)(2,1)S(1)}, bf16[24,1152]{1,0:T(8,128)(2,1)S(1)}, u32[]{:S(2)}, u32[]{:S(2)}) %collective-permute-start.5) | collective-permute-done | bytes 55328 | tf_op jit(solution)/shard_map/ppermute | solution.py:454
  19.2 1.9 %collective-permute-done.8.refs_7_ = bf16[24,1152]{1,0:T(8,128)(2,1)S(1)} collective-permute-done((bf16[24,1152]{1,0:T(8,128)(2,1)S(1)}, bf16[24,1152]{1,0:T(8,128)(2,1)S(1)}, u32[]{:S(2)}, u32[]{:S(2)}) %collective-permute-start.8) | collective-permute-done | bytes 55328 | tf_op jit(solution)/shard_map/ppermute | solution.py:454
  21.5 1.6 %collective-permute-start.9 = (bf16[128,1024]{1,0:T(8,128)(2,1)S(1)}, bf16[128,1024]{1,0:T(8,128)(2,1)S(1)}, u32[]{:S(2)}, u32[]{:S(2)}) collective-permute-start(bf16[128,1024]{1,0:T(8,128)(2,1)S(1)} %get-tuple-element.110.first.refs_3_), channel_id=1, source_target_pairs={{0,2},{1,3},{2,0},{3,1},{4,6},{5,7},{6,4},{7,5},{8,10},{9,11},{10,... | collective-permute-start | bytes 786440 | tf_op jit(solution)/shard_map/ppermute | solution.py:451
  23.1 2.3 %encode_first.1 = (f32[256,256]{1,0:T(8,128)S(1)}, bf16[256,1024]{1,0:T(8,128)(2,1)S(1)}, bf16[128,1024]{1,0:T(8,128)(2,1)S(1)}, bf16[4,2,128,256]{3,2,1,0:T(8,128)(2,1)S(1)}) custom-call(bf16[128,1024]{1,0:T(8,128)(2,1)S(1)} %get-tuple-element.110.first.refs_3_, bf16[128,1024]{1,0:T(8,128)(2,1)S(1)} %collective-permute-done.10.second.refs_4_, ...), custom_call_target="tpu_custom_call" | custom-call | tf_op jit(solution)/shard_map/encode_first/pallas_call | solution.py:53
  25.4 0.8 copy-done.16
  26.2 0.7 copy-done.24
  26.9 3.3 %collective-permute-done.9.third.refs_2_ = bf16[128,1024]{1,0:T(8,128)(2,1)S(1)} collective-permute-done((bf16[128,1024]{1,0:T(8,128)(2,1)S(1)}, bf16[128,1024]{1,0:T(8,128)(2,1)S(1)}, u32[]{:S(2)}, u32[]{:S(2)}) %collective-permute-start.9) | collective-permute-done | bytes 262176 | tf_op jit(solution)/shard_map/ppermute | solution.py:451
  30.7 1.5 %collective-permute-start.13 = (bf16[128,1024]{1,0:T(8,128)(2,1)S(1)}, bf16[128,1024]{1,0:T(8,128)(2,1)S(1)}, u32[]{:S(2)}, u32[]{:S(2)}) collective-permute-start(bf16[128,1024]{1,0:T(8,128)(2,1)S(1)} %bitcast.5), channel_id=1, source_target_pairs={{0,2},{1,3},{2,0},{3,1},{4,6},{5,7},{6,4},{7,5},{8,10},{9,11},{10,... | collective-permute-start | bytes 786440 | tf_op jit(solution)/shard_map/ppermute | solution.py:451
  32.5 3.3 %attend_first.1 = (f32[256,256]{1,0:T(8,128)S(1)}, bf16[256,1024]{1,0:T(8,128)(2,1)S(1)}, bf16[128,1024]{1,0:T(8,128)(2,1)S(1)}, bf16[4,4,128,256]{3,2,1,0:T(8,1...) custom-call(s32[4,1,128]{2,1,0:T(1,128)S(1)} %bitcast.8, ...), custom_call_target="tpu_custom_call" | custom-call | tf_op jit(solution)/shard_map/attend_first/pallas_call | solution.py:53
  35.8 0.8 copy-done.18
  36.6 0.7 copy-done.22
  37.5 1.4 %collective-permute-done.13.d_out_ref.d_out = bf16[128,1024]{1,0:T(8,128)(2,1)S(1)} collective-permute-done((bf16[128,1024]{1,0:T(8,128)(2,1)S(1)}, bf16[128,1024]{1,0:T(8,128)(2,1)S(1)}, u32[]{:S(2)}, u32[]{:S(2)}) %collective-permute-start.13) | collective-permute-done | bytes 262176 | tf_op jit(solution)/shard_map/ppermute | solution.py:451
  39.3 1.6 %collective-permute-start.16 = (bf16[128,1024]{1,0:T(8,128)(2,1)S(1)}, bf16[128,1024]{1,0:T(8,128)(2,1)S(1)}, u32[]{:S(2)}, u32[]{:S(2)}) collective-permute-start(bf16[128,1024]{1,0:T(8,128)(2,1)S(1)} %attn_out_far.1.part), channel_id=1, source_target_pairs={{0,2},{1,3},{2,0},{3,1},{4,6},{5,7},{6,4},{7,5},{8,10},{9,11},{10,... | collective-permute-start | bytes 786440 | tf_op jit(solution)/shard_map/ppermute | solution.py:451
  41.8 6.8 %collective-permute-done.16.got = bf16[128,1024]{1,0:T(8,128)(2,1)S(1)} collective-permute-done((bf16[128,1024]{1,0:T(8,128)(2,1)S(1)}, bf16[128,1024]{1,0:T(8,128)(2,1)S(1)}, u32[]{:S(2)}, u32[]{:S(2)}) %collective-permute-start.16) | collective-permute-done | bytes 262176 | tf_op jit(solution)/shard_map/ppermute | solution.py:451
  48.8 2.9 %ffn_own.1 = (bf16[128,1024]{1,0:T(8,128)(2,1)S(1)}, bf16[128,1024]{1,0:T(8,128)(2,1)S(1)}) custom-call(bf16[128,1024]{1,0:T(8,128)(2,1)S(1)} %get-tuple-element.121.rows_ref, bf16[128,1024]{1,0:T(8,128)(2,1)S(1)} %bitcast.6, bf16[2,1024,512]{2,1,0:T(8,128)(2,1)S(1)} %copy-done.6, bf16[2,1024,512]{2,1,0:T(8,128)(2,1)S(1)} %collective-permute-done.in_b, ...), custom_call_target="tpu_custom_call" | custom-call | tf_op jit(solution)/shard_map/ffn_own/pallas_call | solution.py:53
  51.6 1.4 %collective-permute-done.15.got = bf16[128,1024]{1,0:T(8,128)(2,1)S(1)} collective-permute-done((bf16[128,1024]{1,0:T(8,128)(2,1)S(1)}, bf16[128,1024]{1,0:T(8,128)(2,1)S(1)}, u32[]{:S(2)}, u32[]{:S(2)}) %collective-permute-start.15) | collective-permute-done | bytes 262176 | tf_op jit(solution)/shard_map/ppermute | solution.py:451
  53.1 1.5 %collective-permute-start.18 = (bf16[128,1024]{1,0:T(8,128)(2,1)S(1)}, bf16[128,1024]{1,0:T(8,128)(2,1)S(1)}, u32[]{:S(2)}, u32[]{:S(2)}) collective-permute-start(bf16[128,1024]{1,0:T(8,128)(2,1)S(1)} %get-tuple-element.125.back), channel_id=1, source_target_pairs={{0,2},{1,3},{2,0},{3,1},{4,6},{5,7},{6,4},{7,5},{8,10},{9,11},{10,... | collective-permute-start | bytes 786440 | tf_op jit(solution)/shard_map/ppermute | solution.py:451
  54.8 2.9 %ffn_far.1 = (bf16[128,1024]{1,0:T(8,128)(2,1)S(1)}, bf16[128,1024]{1,0:T(8,128)(2,1)S(1)}) custom-call(bf16[128,1024]{1,0:T(8,128)(2,1)S(1)} %get-tuple-element.128.rows_ref, bf16[128,1024]{1,0:T(8,128)(2,1)S(1)} %collective-permute-done.13.d_out_ref.d_out, bf16[2,1024,512]{2,1,0:T(8,128)(2,1)S(1)} %copy-done.6, ...), custom_call_target="tpu_custom_call" | custom-call | tf_op jit(solution)/shard_map/ffn_far/pallas_call | solution.py:53
  58.9 2.0 %collective-permute-done.18.got = bf16[128,1024]{1,0:T(8,128)(2,1)S(1)} collective-permute-done((bf16[128,1024]{1,0:T(8,128)(2,1)S(1)}, bf16[128,1024]{1,0:T(8,128)(2,1)S(1)}, u32[]{:S(2)}, u32[]{:S(2)}) %collective-permute-start.18) | collective-permute-done | bytes 262176 | tf_op jit(solution)/shard_map/ppermute | solution.py:451
  61.8 0.8 collective-permute-done.19.fourth_a
  62.8 2.0 %attn_back_first.1 = (bf16[4,128,256]{2,1,0:T(8,128)(2,1)S(1)}, f32[4,128,256]{2,1,0:T(8,128)S(1)}, f32[4,128,256]{2,1,0:T(8,128)S(1)}, bf16[4,128,256]{2,1,0:T(8,128)(2,1)S(1)}) custom-call(s32[4,1,128]{2,1,0:T(1,128)S(1)} %bitcast.9, bf16[128,1024]{1,0:T(8,128)(2,1)S(1)} %get-tuple-element.132.third.d_resid, ...), custom_call_target="tpu_custom_call" | custom-call | tf_op jit(solution)/shard_map/attn_back_first/pallas_call | solution.py:53
  64.8 1.2 collective-permute-done.17.got
  66.3 1.5 %collective-permute-done.21.second = bf16[128,1024]{1,0:T(8,128)(2,1)S(1)} collective-permute-done((bf16[128,1024]{1,0:T(8,128)(2,1)S(1)}, bf16[128,1024]{1,0:T(8,128)(2,1)S(1)}, u32[]{:S(2)}, u32[]{:S(2)}) %collective-permute-start.21) | collective-permute-done | bytes 262176 | tf_op jit(solution)/shard_map/ppermute | solution.py:448
  67.8 2.4 %attn_back_second.1 = (bf16[256,1024]{1,0:T(8,128)(2,1)S(1)}, bf16[4,128,256]{2,1,0:T(8,128)(2,1)S(1)}, bf16[4,128,256]{2,1,0:T(8,128)(2,1)S(1)}, bf16[4,128,256...) custom-call(s32[4,1,128]{2,1,0:T(1,128)S(1)} %bitcast.10, bf16[128,1024]{1,0:T(8,128)(2,1)S(1)} %resid_back.1.first.d_resid, ...), custom_call_target="tpu_custom_call" | custom-call | tf_op jit(solution)/shard_map/attn_back_second/pallas_call | solution.py:53
  70.5 0.7 attn_back_keep.1.keep
  71.2 1.0 collective-permute-done.22.take
  72.2 0.8 add_near.1
  73.0 1.5 %collective-permute-start.24 = (bf16[128,1024]{1,0:T(8,128)(2,1)S(1)}, bf16[128,1024]{1,0:T(8,128)(2,1)S(1)}, u32[]{:S(2)}, u32[]{:S(2)}) collective-permute-start(bf16[128,1024]{1,0:T(8,128)(2,1)S(1)} %get-tuple-element.149.part), channel_id=1, source_target_pairs={{0,2},{1,3},{2,0},{3,1},{4,6},{5,7},{6,4},{7,5},{8,10},{9,11},{10,... | collective-permute-start | bytes 786440 | tf_op jit(solution)/shard_map/ppermute | solution.py:451
  75.0 7.1 %collective-permute-done.24.got = bf16[128,1024]{1,0:T(8,128)(2,1)S(1)} collective-permute-done((bf16[128,1024]{1,0:T(8,128)(2,1)S(1)}, bf16[128,1024]{1,0:T(8,128)(2,1)S(1)}, u32[]{:S(2)}, u32[]{:S(2)}) %collective-permute-start.24) | collective-permute-done | bytes 262176 | tf_op jit(solution)/shard_map/ppermute | solution.py:451
  82.2 1.9 %packed_back.1 = (bf16[128,1024]{1,0:T(8,128)(2,1)S(1)}, bf16[64,1024]{1,0:T(8,128)(2,1)}, bf16[64,1024]{1,0:T(8,128)(2,1)}) custom-call(bf16[128,1024]{1,0:T(8,128)(2,1)} %get-tuple-element.150.part, bf16[128,1024]{1,0:T(8,128)(2,1)S(1)} %collective-permute-done.24.got, bf16[128,1024]{1,0:T(8,128)(2,1)S(1)} %get-tuple-element.120.packed, ...), custom_call_target="tpu_custom_call" | custom-call | tf_op jit(solution)/shard_map/packed_back/pallas_call | solution.py:53
  84.6 1.0 back_send.1
  86.3 4.7 %all-to-all-start = ((bf16[8,24,1024]{2,1,0:T(8,128)(2,1)}), bf16[8,24,1024]{2,1,0:T(8,128)(2,1)S(1)}, u32[]{:S(2)}, u32[]{:S(2)}) async-start(bf16[8,24,1024]{2,1,0:T(8,128)(2,1)} %back_send.1), calls=%async_computation | async-start | bytes 786432 | tf_op jit(solution)/shard_map/all_to_all | solution.py:605
  91.0 2.2 %copy-done.1 = bf16[2,1024,1024]{2,1,0:T(8,128)(2,1)S(1)} copy-done((bf16[2,1024,1024]{2,1,0:T(8,128)(2,1)S(1)}, bf16[2,1024,1024]{2,1,0:T(8,128)(2,1)}, u32[]{:S(2)}) %copy-start.1) | copy-done | bytes 4194328
  93.2 0.9 copy-done.10
  94.2 0.9 copy-done.13
  95.1 0.9 copy-done.15
  96.1 1.0 copy-done.17
  97.1 0.9 copy-done.25
  98.1 2.1 %enc_grads_first.1 = (f32[1024,256]{1,0:T(8,128)S(1)}, f32[1024,256]{1,0:T(8,128)S(1)}) custom-call(bf16[128,1024]{1,0:T(8,128)(2,1)S(1)} %copy-done.10, bf16[64,1024]{1,0:T(8,128)(2,1)} %collective-permute-done.25.refs_1_, bf16[64,1024]{1,0:T(8,128)(2,1)} %collective-permute-done.26.refs_2_, bf16[128,1024]{1,0:T(8,128)(2,1)S(1)} %copy-done.13, ...), custom_call_target="tpu_custom_call" | custom-call | tf_op jit(solution)/shard_map/enc_grads_first/pallas_call | solution.py:53
  100.2 1.2 packed_back_far.1.refs_0_
  101.5 1.5 %collective-permute-done.27.refs_1_ = bf16[128,1024]{1,0:T(8,128)(2,1)S(1)} collective-permute-done((bf16[128,1024]{1,0:T(8,128)(2,1)S(1)}, bf16[128,1024]{1,0:T(8,128)(2,1)S(1)}, u32[]{:S(2)}, u32[]{:S(2)}) %collective-permute-start.27) | collective-permute-done | bytes 262176 | tf_op jit(solution)/shard_map/ppermute | solution.py:448
  103.0 0.9 enc_grad0_second.1
  104.0 2.1 %collective-permute-start.31 = (bf16[4,128,256]{2,1,0:T(8,128)(2,1)S(1)}, bf16[4,128,256]{2,1,0:T(8,128)(2,1)S(1)}, u32[]{:S(2)}, u32[]{:S(2)}) collective-permute-start(bf16[4,128,256]{2,1,0:T(8,128)(2,1)S(1)} %get-tuple-element.173), channel_id=1, source_target_pairs={{0,4},{4,0},{8,12},{12,8},{16,20},{20,16},{24,28},{28,24},{1,5},{5... | collective-permute-start | bytes 786440 | tf_op jit(solution)/shard_map/ppermute | solution.py:454
  106.6 1.5 %collective-permute-start.28 = (bf16[4,128,256]{2,1,0:T(8,128)(2,1)S(1)}, bf16[4,128,256]{2,1,0:T(8,128)(2,1)S(1)}, u32[]{:S(2)}, u32[]{:S(2)}) collective-permute-start(bf16[4,128,256]{2,1,0:T(8,128)(2,1)S(1)} %get-tuple-element.164), channel_id=1, source_target_pairs={{0,16},{4,20},{8,24},{12,28},{16,0},{20,4},{24,8},{28,12},{1,17},{... | collective-permute-start | bytes 786440 | tf_op jit(solution)/shard_map/ppermute | solution.py:454
  108.2 1.2 ffn_out_far.1
  109.3 3.4 %collective-permute-done.31.got = bf16[4,128,256]{2,1,0:T(8,128)(2,1)S(1)} collective-permute-done((bf16[4,128,256]{2,1,0:T(8,128)(2,1)S(1)}, bf16[4,128,256]{2,1,0:T(8,128)(2,1)S(1)}, u32[]{:S(2)}, u32[]{:S(2)}) %collective-permute-start.31) | collective-permute-done | bytes 262176 | tf_op jit(solution)/shard_map/ppermute | solution.py:454
  112.7 1.5 %collective-permute-start.34 = (bf16[128,1024]{1,0:T(8,128)(2,1)}, bf16[128,1024]{1,0:T(8,128)(2,1)}, u32[]{:S(2)}, u32[]{:S(2)}) collective-permute-start(bf16[128,1024]{1,0:T(8,128)(2,1)} %ffn_out_far.1), channel_id=1, source_target_pairs={{0,2},{1,3},{2,0},{3,1},{4,6},{5,7},{6,4},{7,5},{8,10},{9,11},{10,... | collective-permute-start | bytes 786440 | tf_op jit(solution)/shard_map/ppermute | solution.py:451
  115.6 1.7 %collective-permute-start.32 = (bf16[2,128,256]{2,1,0:T(8,128)(2,1)}, bf16[2,128,256]{2,1,0:T(8,128)(2,1)}, u32[]{:S(2)}, u32[]{:S(2)}) collective-permute-start(bf16[2,128,256]{2,1,0:T(8,128)(2,1)} %get-tuple-element.177), channel_id=1, source_target_pairs={{0,16},{4,20},{8,24},{12,28},{16,0},{20,4},{24,8},{28,12},{1,17},{... | collective-permute-start | bytes 393224 | tf_op jit(solution)/shard_map/ppermute | solution.py:454
  118.1 0.9 copy-done.31
  119.1 1.5 %collective-permute-start.29 = (bf16[2,128,256]{2,1,0:T(8,128)(2,1)S(1)}, bf16[2,128,256]{2,1,0:T(8,128)(2,1)S(1)}, u32[]{:S(2)}, u32[]{:S(2)}) collective-permute-start(bf16[2,128,256]{2,1,0:T(8,128)(2,1)S(1)} %get-tuple-element.168), channel_id=1, source_target_pairs={{0,4},{4,0},{8,12},{12,8},{16,20},{20,16},{24,28},{28,24},{1,5},{5... | collective-permute-start | bytes 393224 | tf_op jit(solution)/shard_map/ppermute | solution.py:454
  120.9 0.9 copy-done.33
  121.9 0.9 halve0_1.1
  122.8 2.7 %collective-permute-start.33 = (bf16[1,128,256]{2,1,0:T(8,128)(2,1)S(1)}, bf16[1,128,256]{2,1,0:T(8,128)(2,1)S(1)}, u32[]{:S(2)}, u32[]{:S(2)}) collective-permute-start(bf16[1,128,256]{2,1,0:T(8,128)(2,1)S(1)} %get-tuple-element.178), channel_id=1, source_target_pairs={{0,8},{4,12},{8,0},{12,4},{16,24},{20,28},{24,16},{28,20},{1,9},{5... | collective-permute-start | bytes 196616 | tf_op jit(solution)/shard_map/ppermute | solution.py:454
  125.5 1.2 collective-permute-start.30
  126.7 1.0 back_recv.1
  127.7 2.1 %ffn_out_own.1 = bf16[128,1024]{1,0:T(8,128)(2,1)} custom-call(bf16[128,1024]{1,0:T(8,128)(2,1)S(1)} %copy-done.21, bf16[512,1024]{1,0:T(8,128)(2,1)S(1)} %copy-done.4, bf16[512,1024]{1,0:T(8,128)(2,1)S(1)} %collective-permute-done.1.out_b.w_b, bf16[128,1024]{1,0:T(8,128)(2,1)S(1)} %get-tuple-element.139.resid, bf16[128,1024]{1,0:T(8,128)(2,1)} %collective-permute-done.34.got), custom_call_target="tpu_custom_call" | custom-call | tf_op jit(solution)/shard_map/ffn_out_own/pallas_call | solution.py:53
  129.8 0.9 collective-permute-done.30.got1
  130.7 0.7 finish.1
  (111 shorter events, 13.1 us)
Async XLA Ops:
  0.6 7.9 %collective-permute-start = (bf16[2,1024,512]{2,1,0:T(8,128)(2,1)}, bf16[2,1024,512]{2,1,0:T(8,128)(2,1)S(1)}, u32[]{:S(2)}, u32[]{:S(2)}) collective-permute-start(bf16[2,1024,512]{2,1,0:T(8,128)(2,1)} %in_a.3), channel_id=1, source_target_pairs={{0,1},{1,0},{2,3},{3,2},{4,5},{5,4},{6,7},{7,6},{8,9},{9,8},{10,11... | collective-permute-start | bytes 6291464 | tf_op jit(solution)/shard_map/ppermute | solution.py:448
  1.1 7.4 %collective-permute-start.1 = (bf16[512,1024]{1,0:T(8,128)(2,1)}, bf16[512,1024]{1,0:T(8,128)(2,1)S(1)}, u32[]{:S(2)}, u32[]{:S(2)}) collective-permute-start(bf16[512,1024]{1,0:T(8,128)(2,1)} %w_a.3), channel_id=1, source_target_pairs={{0,1},{1,0},{2,3},{3,2},{4,5},{5,4},{6,7},{7,6},{8,9},{9,8},{10,11... | collective-permute-start | bytes 3145736 | tf_op jit(solution)/shard_map/ppermute | solution.py:448
  1.9 0.9 copy-start.35
  2.9 20.2 %copy-start = (bf16[2,1024,1024]{2,1,0:T(8,128)(2,1)S(1)}, bf16[2,1024,1024]{2,1,0:T(8,128)(2,1)}, u32[]{:S(2)}) copy-start(bf16[2,1024,1024]{2,1,0:T(8,128)(2,1)} %refs_5_.1) | copy-start | bytes 12582916
  2.9 20.2 %copy-start.3 = (bf16[4,1024,256]{2,1,0:T(8,128)(2,1)S(1)}, bf16[4,1024,256]{2,1,0:T(8,128)(2,1)}, u32[]{:S(2)}) copy-start(bf16[4,1024,256]{2,1,0:T(8,128)(2,1)} %w_in.7) | copy-start | bytes 6291460
  3.2 10.6 %collective-permute-start.2 = (bf16[24,1152]{1,0:T(8,128)(2,1)S(1)}, bf16[24,1152]{1,0:T(8,128)(2,1)S(1)}, u32[]{:S(2)}, u32[]{:S(2)}) collective-permute-start(bf16[24,1152]{1,0:T(8,128)(2,1)S(1)} %get-tuple-element.97), channel_id=1, source_target_pairs={{0,8},{4,12},{8,0},{12,4},{16,24},{20,28},{24,16},{28,20},{1,9},{5... | collective-permute-start | bytes 165896 | tf_op jit(solution)/shard_map/ppermute | solution.py:454
  7.3 8.8 %collective-permute-start.3 = (bf16[24,1152]{1,0:T(8,128)(2,1)S(1)}, bf16[24,1152]{1,0:T(8,128)(2,1)S(1)}, u32[]{:S(2)}, u32[]{:S(2)}) collective-permute-start(bf16[24,1152]{1,0:T(8,128)(2,1)S(1)} %get-tuple-element.98), channel_id=1, source_target_pairs={{0,24},{4,28},{8,16},{12,20},{16,8},{20,12},{24,0},{28,4},{1,25},{... | collective-permute-start | bytes 165896 | tf_op jit(solution)/shard_map/ppermute | solution.py:454
  8.6 7.8 %collective-permute-start.4 = (bf16[24,1152]{1,0:T(8,128)(2,1)S(1)}, bf16[24,1152]{1,0:T(8,128)(2,1)S(1)}, u32[]{:S(2)}, u32[]{:S(2)}) collective-permute-start(bf16[24,1152]{1,0:T(8,128)(2,1)S(1)} %get-tuple-element.105), channel_id=1, source_target_pairs={{0,12},{4,8},{8,4},{12,0},{16,28},{20,24},{24,20},{28,16},{1,13},{... | collective-permute-start | bytes 165896 | tf_op jit(solution)/shard_map/ppermute | solution.py:454
  12.2 7.0 %collective-permute-start.5 = (bf16[24,1152]{1,0:T(8,128)(2,1)S(1)}, bf16[24,1152]{1,0:T(8,128)(2,1)S(1)}, u32[]{:S(2)}, u32[]{:S(2)}) collective-permute-start(bf16[24,1152]{1,0:T(8,128)(2,1)S(1)} %get-tuple-element.106), channel_id=1, source_target_pairs={{0,28},{4,24},{8,20},{12,16},{16,12},{20,8},{24,4},{28,0},{1,29},{... | collective-permute-start | bytes 165896 | tf_op jit(solution)/shard_map/ppermute | solution.py:454
  12.8 6.4 %collective-permute-start.6 = (bf16[24,1152]{1,0:T(8,128)(2,1)S(1)}, bf16[24,1152]{1,0:T(8,128)(2,1)S(1)}, u32[]{:S(2)}, u32[]{:S(2)}) collective-permute-start(bf16[24,1152]{1,0:T(8,128)(2,1)S(1)} %get-tuple-element.107), channel_id=1, source_target_pairs={{0,16},{4,20},{8,24},{12,28},{16,0},{20,4},{24,8},{28,12},{1,17},{... | collective-permute-start | bytes 165896 | tf_op jit(solution)/shard_map/ppermute | solution.py:454
  13.9 5.3 %collective-permute-start.7 = (bf16[24,1152]{1,0:T(8,128)(2,1)S(1)}, bf16[24,1152]{1,0:T(8,128)(2,1)S(1)}, u32[]{:S(2)}, u32[]{:S(2)}) collective-permute-start(bf16[24,1152]{1,0:T(8,128)(2,1)S(1)} %get-tuple-element.108), channel_id=1, source_target_pairs={{0,4},{4,0},{8,12},{12,8},{16,20},{20,16},{24,28},{28,24},{1,5},{5... | collective-permute-start | bytes 165896 | tf_op jit(solution)/shard_map/ppermute | solution.py:454
  16.1 5.1 %collective-permute-start.8 = (bf16[24,1152]{1,0:T(8,128)(2,1)S(1)}, bf16[24,1152]{1,0:T(8,128)(2,1)S(1)}, u32[]{:S(2)}, u32[]{:S(2)}) collective-permute-start(bf16[24,1152]{1,0:T(8,128)(2,1)S(1)} %get-tuple-element.109), channel_id=1, source_target_pairs={{0,20},{4,16},{8,28},{12,24},{16,4},{20,0},{24,12},{28,8},{1,21},{... | collective-permute-start | bytes 165896 | tf_op jit(solution)/shard_map/ppermute | solution.py:454
  21.4 4.0 %copy-start.12 = (bf16[128,1024]{1,0:T(8,128)(2,1)}, bf16[128,1024]{1,0:T(8,128)(2,1)S(1)}, u32[]{:S(2)}) copy-start(bf16[128,1024]{1,0:T(8,128)(2,1)S(1)} %get-tuple-element.110.first.refs_3_) | copy-start | bytes 786436
  21.4 8.8 %copy-start.5 = (bf16[256,1024]{1,0:T(8,128)(2,1)S(1)}, bf16[256,1024]{1,0:T(8,128)(2,1)}, u32[]{:S(2)}) copy-start(bf16[256,1024]{1,0:T(8,128)(2,1)} %w_out.3) | copy-start | bytes 1572868
  21.4 9.3 %copy-start.11 = (bf16[1,128,1024]{2,1,0:T(8,128)(2,1)S(1)}, bf16[1,128,1024]{2,1,0:T(8,128)(2,1)}, u32[]{:S(2)}) copy-start(bf16[1,128,1024]{2,1,0:T(8,128)(2,1)} %param.19) | copy-start | bytes 786436
  21.4 11.1 %copy-start.34 = (s32[1,512]{1,0:T(1,128)S(1)}, s32[1,512]{1,0:T(1,128)}, u32[]{:S(2)}) copy-start(s32[1,512]{1,0:T(1,128)} %param.13) | copy-start | bytes 6148
  21.4 1.7 %collective-permute-start.10 = (bf16[128,1024]{1,0:T(8,128)(2,1)S(1)}, bf16[128,1024]{1,0:T(8,128)(2,1)S(1)}, u32[]{:S(2)}, u32[]{:S(2)}) collective-permute-start(bf16[128,1024]{1,0:T(8,128)(2,1)S(1)} %get-tuple-element.110.first.refs_3_), channel_id=1, source_target_pairs={{0,1},{1,0},{2,3},{3,2},{4,5},{5,4},{6,7},{7,6},{8,9},{9,8},{10,11... | collective-permute-start | bytes 786440 | tf_op jit(solution)/shard_map/ppermute | solution.py:448
  21.5 8.7 %collective-permute-start.9 = (bf16[128,1024]{1,0:T(8,128)(2,1)S(1)}, bf16[128,1024]{1,0:T(8,128)(2,1)S(1)}, u32[]{:S(2)}, u32[]{:S(2)}) collective-permute-start(bf16[128,1024]{1,0:T(8,128)(2,1)S(1)} %get-tuple-element.110.first.refs_3_), channel_id=1, source_target_pairs={{0,2},{1,3},{2,0},{3,1},{4,6},{5,7},{6,4},{7,5},{8,10},{9,11},{10,... | collective-permute-start | bytes 786440 | tf_op jit(solution)/shard_map/ppermute | solution.py:451
  23.1 2.3 %copy-start.14 = (bf16[128,1024]{1,0:T(8,128)(2,1)}, bf16[128,1024]{1,0:T(8,128)(2,1)S(1)}, u32[]{:S(2)}) copy-start(bf16[128,1024]{1,0:T(8,128)(2,1)S(1)} %collective-permute-done.10.second.refs_4_) | copy-start | bytes 786436
  30.2 8.7 %collective-permute-start.14 = (bf16[256,1024]{1,0:T(8,128)(2,1)S(1)}, bf16[256,1024]{1,0:T(8,128)(2,1)S(1)}, u32[]{:S(2)}, u32[]{:S(2)}) collective-permute-start(bf16[256,1024]{1,0:T(8,128)(2,1)S(1)} %copy-done.5), channel_id=1, source_target_pairs={{0,1},{1,0},{2,3},{3,2},{4,5},{5,4},{6,7},{7,6},{8,9},{9,8},{10,11... | collective-permute-start | bytes 1572872 | tf_op jit(solution)/shard_map/ppermute | solution.py:448
  30.2 2.3 %collective-permute-start.11 = (bf16[128,1024]{1,0:T(8,128)(2,1)S(1)}, bf16[128,1024]{1,0:T(8,128)(2,1)S(1)}, u32[]{:S(2)}, u32[]{:S(2)}) collective-permute-start(bf16[128,1024]{1,0:T(8,128)(2,1)S(1)} %collective-permute-done.9.third.refs_2_), channel_id=1, source_target_pairs={{0,1},{1,0},{2,3},{3,2},{4,5},{5,4},{6,7},{7,6},{8,9},{9,8},{10,11... | collective-permute-start | bytes 786440 | tf_op jit(solution)/shard_map/ppermute | solution.py:448
  30.7 8.2 %collective-permute-start.13 = (bf16[128,1024]{1,0:T(8,128)(2,1)S(1)}, bf16[128,1024]{1,0:T(8,128)(2,1)S(1)}, u32[]{:S(2)}, u32[]{:S(2)}) collective-permute-start(bf16[128,1024]{1,0:T(8,128)(2,1)S(1)} %bitcast.5), channel_id=1, source_target_pairs={{0,2},{1,3},{2,0},{3,1},{4,6},{5,7},{6,4},{7,5},{8,10},{9,11},{10,... | collective-permute-start | bytes 786440 | tf_op jit(solution)/shard_map/ppermute | solution.py:451
  37.4 11.4 %copy-start.4 = (bf16[512,1024]{1,0:T(8,128)(2,1)S(1)}, bf16[512,1024]{1,0:T(8,128)(2,1)}, u32[]{:S(2)}) copy-start(bf16[512,1024]{1,0:T(8,128)(2,1)} %w_a.3) | copy-start | bytes 3145732
  37.4 11.4 %copy-start.6 = (bf16[2,1024,512]{2,1,0:T(8,128)(2,1)S(1)}, bf16[2,1024,512]{2,1,0:T(8,128)(2,1)}, u32[]{:S(2)}) copy-start(bf16[2,1024,512]{2,1,0:T(8,128)(2,1)} %in_a.3) | copy-start | bytes 6291460
  37.4 1.6 %collective-permute-start.12 = (bf16[256,256]{1,0:T(8,128)(2,1)S(1)}, bf16[256,256]{1,0:T(8,128)(2,1)S(1)}, u32[]{:S(2)}, u32[]{:S(2)}) collective-permute-start(bf16[256,256]{1,0:T(8,128)(2,1)S(1)} %get-tuple-element.116), channel_id=1, source_target_pairs={{0,1},{1,0},{2,3},{3,2},{4,5},{5,4},{6,7},{7,6},{8,9},{9,8},{10,11... | collective-permute-start | bytes 393224 | tf_op jit(solution)/shard_map/ppermute | solution.py:448
  39.3 9.2 %collective-permute-start.16 = (bf16[128,1024]{1,0:T(8,128)(2,1)S(1)}, bf16[128,1024]{1,0:T(8,128)(2,1)S(1)}, u32[]{:S(2)}, u32[]{:S(2)}) collective-permute-start(bf16[128,1024]{1,0:T(8,128)(2,1)S(1)} %attn_out_far.1.part), channel_id=1, source_target_pairs={{0,2},{1,3},{2,0},{3,1},{4,6},{5,7},{6,4},{7,5},{8,10},{9,11},{10,... | collective-permute-start | bytes 786440 | tf_op jit(solution)/shard_map/ppermute | solution.py:451
  41.2 11.9 %collective-permute-start.15 = (bf16[128,1024]{1,0:T(8,128)(2,1)S(1)}, bf16[128,1024]{1,0:T(8,128)(2,1)S(1)}, u32[]{:S(2)}, u32[]{:S(2)}) collective-permute-start(bf16[128,1024]{1,0:T(8,128)(2,1)S(1)} %attn_out_own.1.part), channel_id=1, source_target_pairs={{0,2},{1,3},{2,0},{3,1},{4,6},{5,7},{6,4},{7,5},{8,10},{9,11},{10,... | collective-permute-start | bytes 786440 | tf_op jit(solution)/shard_map/ppermute | solution.py:451
  51.6 6.0 %copy-start.20 = (bf16[128,1024]{1,0:T(8,128)(2,1)}, bf16[128,1024]{1,0:T(8,128)(2,1)S(1)}, u32[]{:S(2)}) copy-start(bf16[128,1024]{1,0:T(8,128)(2,1)S(1)} %get-tuple-element.179.hidden) | copy-start | bytes 786436
  53.1 7.8 %collective-permute-start.18 = (bf16[128,1024]{1,0:T(8,128)(2,1)S(1)}, bf16[128,1024]{1,0:T(8,128)(2,1)S(1)}, u32[]{:S(2)}, u32[]{:S(2)}) collective-permute-start(bf16[128,1024]{1,0:T(8,128)(2,1)S(1)} %get-tuple-element.125.back), channel_id=1, source_target_pairs={{0,2},{1,3},{2,0},{3,1},{4,6},{5,7},{6,4},{7,5},{8,10},{9,11},{10,... | collective-permute-start | bytes 786440 | tf_op jit(solution)/shard_map/ppermute | solution.py:451
  58.4 7.5 %collective-permute-start.17 = (bf16[128,1024]{1,0:T(8,128)(2,1)S(1)}, bf16[128,1024]{1,0:T(8,128)(2,1)S(1)}, u32[]{:S(2)}, u32[]{:S(2)}) collective-permute-start(bf16[128,1024]{1,0:T(8,128)(2,1)S(1)} %get-tuple-element.130.back), channel_id=1, source_target_pairs={{0,2},{1,3},{2,0},{3,1},{4,6},{5,7},{6,4},{7,5},{8,10},{9,11},{10,... | collective-permute-start | bytes 786440 | tf_op jit(solution)/shard_map/ppermute | solution.py:451
  61.2 9.1 %copy-start.7 = (bf16[128,1024]{1,0:T(8,128)(2,1)}, bf16[128,1024]{1,0:T(8,128)(2,1)S(1)}, u32[]{:S(2)}) copy-start(bf16[128,1024]{1,0:T(8,128)(2,1)S(1)} %get-tuple-element.132.third.d_resid) | copy-start | bytes 786436
  61.2 1.4 %collective-permute-start.19 = (bf16[64,1024]{1,0:T(8,128)(2,1)S(1)}, bf16[64,1024]{1,0:T(8,128)(2,1)S(1)}, u32[]{:S(2)}, u32[]{:S(2)}) collective-permute-start(bf16[64,1024]{1,0:T(8,128)(2,1)S(1)} %get-tuple-element.133), channel_id=1, source_target_pairs={{0,1},{1,0},{2,3},{3,2},{4,5},{5,4},{6,7},{7,6},{8,9},{9,8},{10,11... | collective-permute-start | bytes 393224 | tf_op jit(solution)/shard_map/ppermute | solution.py:448
  61.3 1.5 %collective-permute-start.20 = (bf16[64,1024]{1,0:T(8,128)(2,1)S(1)}, bf16[64,1024]{1,0:T(8,128)(2,1)S(1)}, u32[]{:S(2)}, u32[]{:S(2)}) collective-permute-start(bf16[64,1024]{1,0:T(8,128)(2,1)S(1)} %get-tuple-element.134), channel_id=1, source_target_pairs={{0,1},{1,0},{2,3},{3,2},{4,5},{5,4},{6,7},{7,6},{8,9},{9,8},{10,11... | collective-permute-start | bytes 393224 | tf_op jit(solution)/shard_map/ppermute | solution.py:448
  66.2 1.6 %collective-permute-start.21 = (bf16[128,1024]{1,0:T(8,128)(2,1)S(1)}, bf16[128,1024]{1,0:T(8,128)(2,1)S(1)}, u32[]{:S(2)}, u32[]{:S(2)}) collective-permute-start(bf16[128,1024]{1,0:T(8,128)(2,1)S(1)} %resid_back.1.first.d_resid), channel_id=1, source_target_pairs={{0,1},{1,0},{2,3},{3,2},{4,5},{5,4},{6,7},{7,6},{8,9},{9,8},{10,11... | collective-permute-start | bytes 786440 | tf_op jit(solution)/shard_map/ppermute | solution.py:448
  70.3 2.0 %collective-permute-start.22 = (bf16[256,1024]{1,0:T(8,128)(2,1)S(1)}, bf16[256,1024]{1,0:T(8,128)(2,1)S(1)}, u32[]{:S(2)}, u32[]{:S(2)}) collective-permute-start(bf16[256,1024]{1,0:T(8,128)(2,1)S(1)} %get-tuple-element.148), channel_id=1, source_target_pairs={{0,1},{1,0},{2,3},{3,2},{4,5},{5,4},{6,7},{7,6},{8,9},{9,8},{10,11... | collective-permute-start | bytes 1572872 | tf_op jit(solution)/shard_map/ppermute | solution.py:448
  73.0 11.0 %copy-start.28 = (bf16[128,1024]{1,0:T(8,128)(2,1)}, bf16[128,1024]{1,0:T(8,128)(2,1)S(1)}, u32[]{:S(2)}) copy-start(bf16[128,1024]{1,0:T(8,128)(2,1)S(1)} %get-tuple-element.149.part) | copy-start | bytes 786436
  73.0 9.1 %collective-permute-start.24 = (bf16[128,1024]{1,0:T(8,128)(2,1)S(1)}, bf16[128,1024]{1,0:T(8,128)(2,1)S(1)}, u32[]{:S(2)}, u32[]{:S(2)}) collective-permute-start(bf16[128,1024]{1,0:T(8,128)(2,1)S(1)} %get-tuple-element.149.part), channel_id=1, source_target_pairs={{0,2},{1,3},{2,0},{3,1},{4,6},{5,7},{6,4},{7,5},{8,10},{9,11},{10,... | collective-permute-start | bytes 786440 | tf_op jit(solution)/shard_map/ppermute | solution.py:451
  74.5 25.6 %collective-permute-start.23 = (bf16[128,1024]{1,0:T(8,128)(2,1)}, bf16[128,1024]{1,0:T(8,128)(2,1)}, u32[]{:S(2)}, u32[]{:S(2)}) collective-permute-start(bf16[128,1024]{1,0:T(8,128)(2,1)} %get-tuple-element.150.part), channel_id=1, source_target_pairs={{0,2},{1,3},{2,0},{3,1},{4,6},{5,7},{6,4},{7,5},{8,10},{9,11},{10,... | collective-permute-start | bytes 786440 | tf_op jit(solution)/shard_map/ppermute | solution.py:451
  84.0 7.0 %collective-permute-start.25 = (bf16[64,1024]{1,0:T(8,128)(2,1)}, bf16[64,1024]{1,0:T(8,128)(2,1)}, u32[]{:S(2)}, u32[]{:S(2)}) collective-permute-start(bf16[64,1024]{1,0:T(8,128)(2,1)} %get-tuple-element.152), channel_id=1, source_target_pairs={{0,1},{1,0},{2,3},{3,2},{4,5},{5,4},{6,7},{7,6},{8,9},{9,8},{10,11... | collective-permute-start | bytes 393224 | tf_op jit(solution)/shard_map/ppermute | solution.py:448
  84.0 7.0 %collective-permute-start.26 = (bf16[64,1024]{1,0:T(8,128)(2,1)}, bf16[64,1024]{1,0:T(8,128)(2,1)}, u32[]{:S(2)}, u32[]{:S(2)}) collective-permute-start(bf16[64,1024]{1,0:T(8,128)(2,1)} %get-tuple-element.153), channel_id=1, source_target_pairs={{0,1},{1,0},{2,3},{3,2},{4,5},{5,4},{6,7},{7,6},{8,9},{9,8},{10,11... | collective-permute-start | bytes 393224 | tf_op jit(solution)/shard_map/ppermute | solution.py:448
  86.3 31.8 %all-to-all-start = ((bf16[8,24,1024]{2,1,0:T(8,128)(2,1)}), bf16[8,24,1024]{2,1,0:T(8,128)(2,1)S(1)}, u32[]{:S(2)}, u32[]{:S(2)}) async-start(bf16[8,24,1024]{2,1,0:T(8,128)(2,1)} %back_send.1), calls=%async_computation | async-start | bytes 786432 | tf_op jit(solution)/shard_map/all_to_all | solution.py:605
  91.0 2.2 %copy-start.1 = (bf16[2,1024,1024]{2,1,0:T(8,128)(2,1)S(1)}, bf16[2,1024,1024]{2,1,0:T(8,128)(2,1)}, u32[]{:S(2)}) copy-start(bf16[2,1024,1024]{2,1,0:T(8,128)(2,1)} %refs_5_.1) | copy-start | bytes 12582916
  93.2 0.9 copy-start.10
  94.2 0.9 copy-start.13
  95.1 0.9 copy-start.15
  96.1 1.0 copy-start.17
  97.1 0.9 copy-start.25
  98.1 2.1 %copy-start.8 = (bf16[128,1024]{1,0:T(8,128)(2,1)S(1)}, bf16[128,1024]{1,0:T(8,128)(2,1)}, u32[]{:S(2)}) copy-start(bf16[128,1024]{1,0:T(8,128)(2,1)} %copy-done.7) | copy-start | bytes 786436
  98.1 2.1 %copy-start.29 = (bf16[128,1024]{1,0:T(8,128)(2,1)S(1)}, bf16[128,1024]{1,0:T(8,128)(2,1)}, u32[]{:S(2)}) copy-start(bf16[128,1024]{1,0:T(8,128)(2,1)} %copy-done.28) | copy-start | bytes 786436
  98.1 5.0 %copy-start.2 = (bf16[2,1024,1024]{2,1,0:T(8,128)(2,1)S(1)}, bf16[2,1024,1024]{2,1,0:T(8,128)(2,1)}, u32[]{:S(2)}) copy-start(bf16[2,1024,1024]{2,1,0:T(8,128)(2,1)} %refs_5_.1) | copy-start | bytes 12582916
  98.1 5.0 %copy-start.23 = (f32[256,256]{1,0:T(8,128)S(1)}, f32[256,256]{1,0:T(8,128)}, u32[]{:S(2)}) copy-start(f32[256,256]{1,0:T(8,128)} %copy-done.22) | copy-start | bytes 786436
  101.4 1.6 %collective-permute-start.27 = (bf16[128,1024]{1,0:T(8,128)(2,1)S(1)}, bf16[128,1024]{1,0:T(8,128)(2,1)S(1)}, u32[]{:S(2)}, u32[]{:S(2)}) collective-permute-start(bf16[128,1024]{1,0:T(8,128)(2,1)S(1)} %packed_back_far.1.refs_0_), channel_id=1, source_target_pairs={{0,1},{1,0},{2,3},{3,2},{4,5},{5,4},{6,7},{7,6},{8,9},{9,8},{10,11... | collective-permute-start | bytes 786440 | tf_op jit(solution)/shard_map/ppermute | solution.py:448
  103.0 3.1 %copy-start.19 = (bf16[256,1024]{1,0:T(8,128)(2,1)S(1)}, bf16[256,1024]{1,0:T(8,128)(2,1)}, u32[]{:S(2)}) copy-start(bf16[256,1024]{1,0:T(8,128)(2,1)} %copy-done.18) | copy-start | bytes 1572868
  104.0 4.2 %copy-start.27 = (bf16[128,1024]{1,0:T(8,128)(2,1)S(1)}, bf16[128,1024]{1,0:T(8,128)(2,1)}, u32[]{:S(2)}) copy-start(bf16[128,1024]{1,0:T(8,128)(2,1)} %copy-done.26) | copy-start | bytes 786436
  104.0 8.7 %collective-permute-start.31 = (bf16[4,128,256]{2,1,0:T(8,128)(2,1)S(1)}, bf16[4,128,256]{2,1,0:T(8,128)(2,1)S(1)}, u32[]{:S(2)}, u32[]{:S(2)}) collective-permute-start(bf16[4,128,256]{2,1,0:T(8,128)(2,1)S(1)} %get-tuple-element.173), channel_id=1, source_target_pairs={{0,4},{4,0},{8,12},{12,8},{16,20},{20,16},{24,28},{28,24},{1,5},{5... | collective-permute-start | bytes 786440 | tf_op jit(solution)/shard_map/ppermute | solution.py:454
  106.6 10.7 %collective-permute-start.28 = (bf16[4,128,256]{2,1,0:T(8,128)(2,1)S(1)}, bf16[4,128,256]{2,1,0:T(8,128)(2,1)S(1)}, u32[]{:S(2)}, u32[]{:S(2)}) collective-permute-start(bf16[4,128,256]{2,1,0:T(8,128)(2,1)S(1)} %get-tuple-element.164), channel_id=1, source_target_pairs={{0,16},{4,20},{8,24},{12,28},{16,0},{20,4},{24,8},{28,12},{1,17},{... | collective-permute-start | bytes 786440 | tf_op jit(solution)/shard_map/ppermute | solution.py:454
  109.3 18.4 %copy-start.21 = (bf16[128,1024]{1,0:T(8,128)(2,1)S(1)}, bf16[128,1024]{1,0:T(8,128)(2,1)}, u32[]{:S(2)}) copy-start(bf16[128,1024]{1,0:T(8,128)(2,1)} %copy-done.20) | copy-start | bytes 786436
  112.7 15.0 %collective-permute-start.34 = (bf16[128,1024]{1,0:T(8,128)(2,1)}, bf16[128,1024]{1,0:T(8,128)(2,1)}, u32[]{:S(2)}, u32[]{:S(2)}) collective-permute-start(bf16[128,1024]{1,0:T(8,128)(2,1)} %ffn_out_far.1), channel_id=1, source_target_pairs={{0,2},{1,3},{2,0},{3,1},{4,6},{5,7},{6,4},{7,5},{8,10},{9,11},{10,... | collective-permute-start | bytes 786440 | tf_op jit(solution)/shard_map/ppermute | solution.py:451
  115.6 5.3 %collective-permute-start.32 = (bf16[2,128,256]{2,1,0:T(8,128)(2,1)}, bf16[2,128,256]{2,1,0:T(8,128)(2,1)}, u32[]{:S(2)}, u32[]{:S(2)}) collective-permute-start(bf16[2,128,256]{2,1,0:T(8,128)(2,1)} %get-tuple-element.177), channel_id=1, source_target_pairs={{0,16},{4,20},{8,24},{12,28},{16,0},{20,4},{24,8},{28,12},{1,17},{... | collective-permute-start | bytes 393224 | tf_op jit(solution)/shard_map/ppermute | solution.py:454
  118.1 1.0 copy-start.31
  119.1 6.4 %collective-permute-start.29 = (bf16[2,128,256]{2,1,0:T(8,128)(2,1)S(1)}, bf16[2,128,256]{2,1,0:T(8,128)(2,1)S(1)}, u32[]{:S(2)}, u32[]{:S(2)}) collective-permute-start(bf16[2,128,256]{2,1,0:T(8,128)(2,1)S(1)} %get-tuple-element.168), channel_id=1, source_target_pairs={{0,4},{4,0},{8,12},{12,8},{16,20},{20,16},{24,28},{28,24},{1,5},{5... | collective-permute-start | bytes 393224 | tf_op jit(solution)/shard_map/ppermute | solution.py:454
  120.9 1.0 copy-start.33
  122.8 7.0 %collective-permute-start.33 = (bf16[1,128,256]{2,1,0:T(8,128)(2,1)S(1)}, bf16[1,128,256]{2,1,0:T(8,128)(2,1)S(1)}, u32[]{:S(2)}, u32[]{:S(2)}) collective-permute-start(bf16[1,128,256]{2,1,0:T(8,128)(2,1)S(1)} %get-tuple-element.178), channel_id=1, source_target_pairs={{0,8},{4,12},{8,0},{12,4},{16,24},{20,28},{24,16},{28,20},{1,9},{5... | collective-permute-start | bytes 196616 | tf_op jit(solution)/shard_map/ppermute | solution.py:454
  125.5 5.2 %collective-permute-start.30 = (bf16[1,128,256]{2,1,0:T(8,128)(2,1)S(1)}, bf16[1,128,256]{2,1,0:T(8,128)(2,1)S(1)}, u32[]{:S(2)}, u32[]{:S(2)}) collective-permute-start(bf16[1,128,256]{2,1,0:T(8,128)(2,1)S(1)} %get-tuple-element.169), channel_id=1, source_target_pairs={{0,8},{4,12},{8,0},{12,4},{16,24},{20,28},{24,16},{28,20},{1,9},{5... | collective-permute-start | bytes 196616 | tf_op jit(solution)/shard_map/ppermute | solution.py:454
  (8 other events, 5.9 us)

commit v7 on v6

--- a/solution.py
+++ b/solution.py
@@ -74,7 +74,7 @@
     return lax.optimization_barrier(values)
 
 
-def route_send(capacity, order, code, features, *outs):
+def route_send(capacity, order, packs, code, features, *outs):
     sends, place_ref = outs[:-1], outs[-1]
     groups = len(sends)
     rows, width = features.shape
@@ -86,8 +86,11 @@
     j = lax.broadcasted_iota(jnp.int32, (rows, rows), 1)
     earlier = jnp.where((o_col == o_row.astype(F32)) & (i < j), 1.0, 0.0)
     rank = jnp.sum(earlier, axis=0, keepdims=True).astype(jnp.int32)
-    place_ref[...] = o_row * capacity + rank
-    place = (o_row ^ group_index()) * capacity + rank
+    offset = o_row ^ group_index()
+    place = offset * capacity + rank
+    turn = packs.bit_length() - 1
+    events = groups // packs
+    place_ref[...] = ((offset & (packs - 1)) * events + (offset >> turn)) * capacity + rank
     spots = lax.broadcasted_iota(jnp.int32, (groups * capacity, rows), 0)
     hot = jnp.where(spots == place, 1.0, 0.0).astype(BF16)
     big = dot(hot, features[...])
@@ -108,18 +111,35 @@
     rows_ref[...] = bf16(dot(hot, bf16(got[:, :width]), TN))
 
 
-def back_send(order, hot, d_packed, out):
-    capacity = out.shape[1]
+def back_send(order, packs, hot, d_packed, own, *sends):
+    events = len(order) // packs
+    capacity = hot.shape[0] // len(order)
     big = dot(hot[...], d_packed[...])
-    for n, k in enumerate(order):
-        out[group_index() ^ k] = bf16(big[n * capacity : (n + 1) * capacity])
-
-
-def back_recv(place, got_ref, out):
-    got = jnp.concatenate([got_ref[k].astype(F32) for k in range(got_ref.shape[0])], axis=0)
+    at = {k: n for n, k in enumerate(order)}
+    for a in range(events):
+        parts = [at[a * packs + b] * capacity for b in range(packs)]
+        rows = jnp.concatenate([big[p : p + capacity] for p in parts], axis=0)
+        (own, *sends)[a][...] = bf16(rows)
+
+
+def back_turn(events, *refs):
+    packs = len(refs) - events
+    own, gots, outs = refs[0], refs[1 : -packs], refs[-packs:]
+    rows = jnp.concatenate([r[...].astype(F32) for r in (own, *gots)], axis=0)
+    capacity = outs[0].shape[0] // events
+    for b, out in enumerate(outs):
+        parts = [
+            rows[(a * packs + b) * capacity : (a * packs + b + 1) * capacity] for a in range(events)
+        ]
+        out[...] = bf16(jnp.concatenate(parts, axis=0))
+
+
+def back_recv(place, *refs):
+    gots, out = refs[:-1], refs[-1]
+    got = bf16(jnp.concatenate([g[...].astype(F32) for g in gots], axis=0))
     spots = lax.broadcasted_iota(jnp.int32, (got.shape[0], out.shape[0]), 0)
     hot = jnp.where(spots == place[...], 1.0, 0.0).astype(BF16)
-    out[...] = bf16(dot(hot, bf16(got), TN))
+    out[...] = bf16(dot(hot, got, TN))
 
 
 def encode(rows, enc, w_in, pre_all, pre_ref, act_ref, packed_ref, store):
@@ -463,7 +483,7 @@
         range(1, groups), key=lambda k: (-((2 * (k % packs)) // packs), k % packs, k)
     )
     *sends, place = run(
-        functools.partial(route_send, capacity, order),
+        functools.partial(route_send, capacity, order, packs),
         [like((capacity, width + rows_dev), BF16)] * groups + [like((1, rows_dev), jnp.int32)],
         [code, features],
         flops=4 * 10**9,
@@ -596,13 +616,14 @@
     )
 
     cot_near = [near(h) for h in halves]
-    (backs,) = run(
-        functools.partial(back_send, order),
-        [like((groups, capacity, width), BF16)],
+    events = groups // packs
+    back_own, *backs = run(
+        functools.partial(back_send, order, packs),
+        [like((packs * capacity, width), BF16)] * events,
         [hot, d_packed],
         name="back_send",
     )
-    returned = lax.all_to_all(backs, group_axes, split_axis=0, concat_axis=0, tiled=True)
+    over_event = [crossed(v, (n + 1) * packs) for n, v in enumerate(backs)]
 
     part_f = like((width, cols), F32)
     part1, part0 = run(
@@ -612,10 +633,22 @@
         name="enc_grads_first",
     )
     got_far, part1, part0 = tie(got_far, part1, part0)
-    (cot_far,) = run(
-        packed_back, [row_b], [sum_far, got_far, packed_far, d_resid_far], name="packed_back_far"
-    )
-    cot_both = near(cot_far)
+    cot_far, *cot_pieces = run(
+        packed_back,
+        [row_b] + [piece_b] * pieces,
+        [sum_far, got_far, packed_far, d_resid_far],
+        name="packed_back_far",
+    )
+    cot_both = [near(piece) for piece in cot_pieces]
+    *cot_both, over_event = tie(*cot_both, over_event)
+    back_own, *turned_rows = run(
+        functools.partial(back_turn, events),
+        [like((events * capacity, width), BF16)] * packs,
+        [back_own, *over_event],
+        name="back_turn",
+    )
+    returned = [back_own] + [crossed(v, b + 1) for b, v in enumerate(turned_rows)]
+
     cot_far, hidden_far = tie(cot_far, hidden_far)
     (out_far,) = run(
         ffn_out_far, [row_b], [hidden_far, ffn_out, ffn_out_near], name="ffn_out_far"
@@ -634,7 +667,7 @@
         remaining = list(bits)
         kept, send = start((tuple(remaining), stages[0]))
         got = crossed(send, 1 << stages[0])
-        got, held = tie(got, held)
+        got, *held = tie(got, *held)
         remaining.remove(stages[0])
         for bit in stages[1:]:
             kept, send = run(
@@ -651,7 +684,7 @@
         return run(
             functools.partial(enc_grad1_second, *setting),
             halves(bits),
-            [cot_far, cot_both, act_b, part1],
+            [cot_far, *cot_both, act_b, part1],
             total,
             name="enc_grad1_second",
         )
@@ -660,14 +693,14 @@
         return run(
             functools.partial(enc_grad0_second, *setting),
             halves(bits),
-            [cot_far, cot_both, mine_far, mine_both, pre_b, enc_weight, part0],
+            [cot_far, *cot_both, mine_far, mine_both, pre_b, enc_weight, part0],
             total,
             name="enc_grad0_second",
         )
 
     kept1, got1, returned = reduce_over(event_bits + pack_bits, start1, returned, "halve1_")
-    kept0, got0, out_far = reduce_over(
-        pack_bits[:1] + event_bits + pack_bits[1:], start0, out_far, "halve0_"
+    kept0, got0, (out_far,) = reduce_over(
+        pack_bits[:1] + event_bits + pack_bits[1:], start0, [out_far], "halve0_"
     )
     got_out = far(out_far)
     (packed_out,) = run(
@@ -676,7 +709,7 @@
     (row_grad,) = run(
         back_recv,
         [row_b],
-        [place, returned],
+        [place, *returned],
         name="back_recv",
     )
     got1, got0, packed_out, row_grad = tie(got1, got0, packed_out, row_grad)

time: 132 us -> 116 us (0.88)
  local copies, waits for them, and re-layouts: 15.8 us -> 0.99 us
  Pallas kernels: 33.7 us -> 25.5 us
  waiting for transfers between devices: 40.1 us -> 47.6 us
    unnamed x72 -> x16, local copies, waits for them, and re-layouts: 15.8 us -> 0.99 us
    pallas_call x30 -> x31, Pallas kernels: 33.7 us -> 25.5 us  [run(): pl.pallas_call(body, out_shape=list(outs), in_specs=[pl.BlockSpec(memory_...]
    ppermute x13 -> x17, waiting for transfers between devices: 11.5 us -> 17 us  [crossed(): return lax.ppermute(value, group_axes, [(i, i ^ k) for i in range(groups)])]
    all_to_all x1 -> x0, starting transfers between devices: 4.74 us -> none  [shards(): lax.all_to_all(backs, group_axes, split_axis=0, concat_axis=0, tiled=True)]
    ppermute x13 -> x17, starting transfers between devices: 21.8 us -> 25.8 us  [crossed(): return lax.ppermute(value, group_axes, [(i, i ^ k) for i in range(groups)])]
    ppermute x9, waiting for transfers between devices: 23.2 us -> 26.8 us  [far(): return lax.ppermute(value, 'tensor', [(i, i ^ 2) for i in range(tensors)])]
    ppermute x13 -> x14, waiting for transfers between devices: 5.37 us -> 3.85 us  [near(): return lax.ppermute(value, 'tensor', [(i, i ^ 1) for i in range(tensors)])]
    ppermute x13 -> x14, starting transfers between devices: 2.74 us -> 3.36 us  [near(): return lax.ppermute(value, 'tensor', [(i, i ^ 1) for i in range(tensors)])]
  transfers between devices with their start and end apart: 36 -> 40, of which waited for: 19 -> 22; matrix products, arithmetic and copies ran while one was open for 1% -> 1% of each run, Pallas kernels for 22% -> 18%
where the time goes in v7:
time: 116 us
  waiting for transfers between devices  47.6 us (41%)
  starting transfers between devices  40.5 us (35%)
  Pallas kernels  25.5 us (22%)
    ppermute x9, waiting for transfers between devices, far(): return lax.ppermute(value, 'tensor', [(i, i ^ 2) for i in range(tensors)])  26.8 us
    ppermute x17, starting transfers between devices, crossed(): return lax.ppermute(value, group_axes, [(i, i ^ k) for i in range(groups)])  25.8 us
    pallas_call x31, Pallas kernels, run(): pl.pallas_call(body, out_shape=list(outs), in_specs=[pl.BlockSpec(memory_...  25.5 us
    ppermute x17, waiting for transfers between devices, crossed(): return lax.ppermute(value, group_axes, [(i, i ^ k) for i in range(groups)])  17 us
    ppermute x9, starting transfers between devices, far(): return lax.ppermute(value, 'tensor', [(i, i ^ 2) for i in range(tensors)])  11.3 us
    ppermute x14, waiting for transfers between devices, near(): return lax.ppermute(value, 'tensor', [(i, i ^ 1) for i in range(tensors)])  3.85 us
    ppermute x14, starting transfers between devices, near(): return lax.ppermute(value, 'tensor', [(i, i ^ 1) for i in range(tensors)])  3.36 us
  transfers between devices with their start and end apart: 40, of which 22 were waited for; matrix products, arithmetic and copies ran while one was open for 1% of the time, Pallas kernels for 18%

profile of v7, /device:TPU:0, one launch (start us, length us, event | category | flops | bytes accessed | tf_op | source)
XLA Modules:
  0.0 116.3 jit_solution(5420267709498007123)
XLA Ops:
  0.6 0.5 collective-permute-start
  1.2 0.7 add_bitcast_fusion.code
  1.9 0.9 copy-done.7
  2.9 0.4 route_send.1
  3.2 4.1 %collective-permute-start.2 = (bf16[24,1152]{1,0:T(8,128)(2,1)S(1)}, bf16[24,1152]{1,0:T(8,128)(2,1)S(1)}, u32[]{:S(2)}, u32[]{:S(2)}) collective-permute-start(bf16[24,1152]{1,0:T(8,128)(2,1)S(1)} %get-tuple-element.112), channel_id=1, source_target_pairs={{0,8},{4,12},{8,0},{12,4},{16,24},{20,28},{24,16},{28,20},{1,9},{5... | collective-permute-start | bytes 165896 | tf_op jit(solution)/shard_map/ppermute | solution.py:474
  7.3 1.3 %collective-permute-start.3 = (bf16[24,1152]{1,0:T(8,128)(2,1)S(1)}, bf16[24,1152]{1,0:T(8,128)(2,1)S(1)}, u32[]{:S(2)}, u32[]{:S(2)}) collective-permute-start(bf16[24,1152]{1,0:T(8,128)(2,1)S(1)} %get-tuple-element.113), channel_id=1, source_target_pairs={{0,24},{4,28},{8,16},{12,20},{16,8},{20,12},{24,0},{28,4},{1,25},{... | collective-permute-start | bytes 165896 | tf_op jit(solution)/shard_map/ppermute | solution.py:474
  8.6 3.6 %collective-permute-start.4 = (bf16[24,1152]{1,0:T(8,128)(2,1)S(1)}, bf16[24,1152]{1,0:T(8,128)(2,1)S(1)}, u32[]{:S(2)}, u32[]{:S(2)}) collective-permute-start(bf16[24,1152]{1,0:T(8,128)(2,1)S(1)} %get-tuple-element.120), channel_id=1, source_target_pairs={{0,12},{4,8},{8,4},{12,0},{16,28},{20,24},{24,20},{28,16},{1,13},{... | collective-permute-start | bytes 165896 | tf_op jit(solution)/shard_map/ppermute | solution.py:474
  12.2 0.6 collective-permute-start.5
  12.8 1.1 collective-permute-start.6
  13.9 2.2 %collective-permute-done.3.refs_2_ = bf16[24,1152]{1,0:T(8,128)(2,1)S(1)} collective-permute-done((bf16[24,1152]{1,0:T(8,128)(2,1)S(1)}, bf16[24,1152]{1,0:T(8,128)(2,1)S(1)}, u32[]{:S(2)}, u32[]{:S(2)}) %collective-permute-start.3) | collective-permute-done | bytes 55328 | tf_op jit(solution)/shard_map/ppermute | solution.py:474
  16.4 2.8 %collective-permute-done.5.refs_4_ = bf16[24,1152]{1,0:T(8,128)(2,1)S(1)} collective-permute-done((bf16[24,1152]{1,0:T(8,128)(2,1)S(1)}, bf16[24,1152]{1,0:T(8,128)(2,1)S(1)}, u32[]{:S(2)}, u32[]{:S(2)}) %collective-permute-start.5) | collective-permute-done | bytes 55328 | tf_op jit(solution)/shard_map/ppermute | solution.py:474
  19.2 1.9 %collective-permute-done.8.refs_7_ = bf16[24,1152]{1,0:T(8,128)(2,1)S(1)} collective-permute-done((bf16[24,1152]{1,0:T(8,128)(2,1)S(1)}, bf16[24,1152]{1,0:T(8,128)(2,1)S(1)}, u32[]{:S(2)}, u32[]{:S(2)}) %collective-permute-start.8) | collective-permute-done | bytes 55328 | tf_op jit(solution)/shard_map/ppermute | solution.py:474
  21.5 1.6 %collective-permute-start.9 = (bf16[128,1024]{1,0:T(8,128)(2,1)S(1)}, bf16[128,1024]{1,0:T(8,128)(2,1)S(1)}, u32[]{:S(2)}, u32[]{:S(2)}) collective-permute-start(bf16[128,1024]{1,0:T(8,128)(2,1)S(1)} %get-tuple-element.125.first.refs_3_), channel_id=1, source_target_pairs={{0,2},{1,3},{2,0},{3,1},{4,6},{5,7},{6,4},{7,5},{8,10},{9,11},{10,... | collective-permute-start | bytes 786440 | tf_op jit(solution)/shard_map/ppermute | solution.py:471
  23.1 2.2 %encode_first.1 = (f32[256,256]{1,0:T(8,128)S(1)}, bf16[256,1024]{1,0:T(8,128)(2,1)S(1)}, bf16[128,1024]{1,0:T(8,128)(2,1)S(1)}, bf16[4,2,128,256]{3,2,1,0:T(8,128)(2,1)S(1)}) custom-call(bf16[128,1024]{1,0:T(8,128)(2,1)S(1)} %get-tuple-element.125.first.refs_3_, bf16[128,1024]{1,0:T(8,128)(2,1)S(1)} %collective-permute-done.10.second.refs_4_, ...), custom_call_target="tpu_custom_call" | custom-call | tf_op jit(solution)/shard_map/encode_first/pallas_call | solution.py:53
  25.3 4.9 %collective-permute-done.9.third.refs_3_ = bf16[128,1024]{1,0:T(8,128)(2,1)S(1)} collective-permute-done((bf16[128,1024]{1,0:T(8,128)(2,1)S(1)}, bf16[128,1024]{1,0:T(8,128)(2,1)S(1)}, u32[]{:S(2)}, u32[]{:S(2)}) %collective-permute-start.9) | collective-permute-done | bytes 262176 | tf_op jit(solution)/shard_map/ppermute | solution.py:471
  30.2 0.5 collective-permute-start.11
  30.7 1.5 %collective-permute-start.13 = (bf16[128,1024]{1,0:T(8,128)(2,1)S(1)}, bf16[128,1024]{1,0:T(8,128)(2,1)S(1)}, u32[]{:S(2)}, u32[]{:S(2)}) collective-permute-start(bf16[128,1024]{1,0:T(8,128)(2,1)S(1)} %bitcast.5), channel_id=1, source_target_pairs={{0,2},{1,3},{2,0},{3,1},{4,6},{5,7},{6,4},{7,5},{8,10},{9,11},{10,... | collective-permute-start | bytes 786440 | tf_op jit(solution)/shard_map/ppermute | solution.py:471
  32.5 3.3 %attend_first.1 = (f32[256,256]{1,0:T(8,128)S(1)}, bf16[256,1024]{1,0:T(8,128)(2,1)S(1)}, bf16[128,1024]{1,0:T(8,128)(2,1)S(1)}, bf16[4,4,128,256]{3,2,1,0:T(8,1...) custom-call(s32[4,1,128]{2,1,0:T(1,128)S(1)} %bitcast.8, ...), custom_call_target="tpu_custom_call" | custom-call | tf_op jit(solution)/shard_map/attend_first/pallas_call | solution.py:53
  36.0 2.9 %collective-permute-done.13.d_out_ref.d_out = bf16[128,1024]{1,0:T(8,128)(2,1)S(1)} collective-permute-done((bf16[128,1024]{1,0:T(8,128)(2,1)S(1)}, bf16[128,1024]{1,0:T(8,128)(2,1)S(1)}, u32[]{:S(2)}, u32[]{:S(2)}) %collective-permute-start.13) | collective-permute-done | bytes 262176 | tf_op jit(solution)/shard_map/ppermute | solution.py:471
  38.9 0.3 attn_out_far.1.part
  39.3 1.6 %collective-permute-start.16 = (bf16[128,1024]{1,0:T(8,128)(2,1)S(1)}, bf16[128,1024]{1,0:T(8,128)(2,1)S(1)}, u32[]{:S(2)}, u32[]{:S(2)}) collective-permute-start(bf16[128,1024]{1,0:T(8,128)(2,1)S(1)} %attn_out_far.1.part), channel_id=1, source_target_pairs={{0,2},{1,3},{2,0},{3,1},{4,6},{5,7},{6,4},{7,5},{8,10},{9,11},{10,... | collective-permute-start | bytes 786440 | tf_op jit(solution)/shard_map/ppermute | solution.py:471
  40.8 0.3 attn_out_own.1.part
  41.2 0.6 collective-permute-start.15
  41.7 6.8 %collective-permute-done.16.got = bf16[128,1024]{1,0:T(8,128)(2,1)S(1)} collective-permute-done((bf16[128,1024]{1,0:T(8,128)(2,1)S(1)}, bf16[128,1024]{1,0:T(8,128)(2,1)S(1)}, u32[]{:S(2)}, u32[]{:S(2)}) %collective-permute-start.16) | collective-permute-done | bytes 262176 | tf_op jit(solution)/shard_map/ppermute | solution.py:471
  48.8 2.9 %ffn_own.1 = (bf16[128,1024]{1,0:T(8,128)(2,1)S(1)}, bf16[128,1024]{1,0:T(8,128)(2,1)S(1)}) custom-call(bf16[128,1024]{1,0:T(8,128)(2,1)S(1)} %get-tuple-element.136.rows_ref, bf16[128,1024]{1,0:T(8,128)(2,1)S(1)} %bitcast.6, bf16[2,1024,512]{2,1,0:T(8,128)(2,1)S(1)} %copy-done.4, bf16[2,1024,512]{2,1,0:T(8,128)(2,1)S(1)} %collective-permute-done.in_b, ...), custom_call_target="tpu_custom_call" | custom-call | tf_op jit(solution)/shard_map/ffn_own/pallas_call | solution.py:53
  51.7 0.6 collective-permute-done.15.got
  52.3 1.5 %collective-permute-start.18 = (bf16[128,1024]{1,0:T(8,128)(2,1)S(1)}, bf16[128,1024]{1,0:T(8,128)(2,1)S(1)}, u32[]{:S(2)}, u32[]{:S(2)}) collective-permute-start(bf16[128,1024]{1,0:T(8,128)(2,1)S(1)} %get-tuple-element.140.back), channel_id=1, source_target_pairs={{0,2},{1,3},{2,0},{3,1},{4,6},{5,7},{6,4},{7,5},{8,10},{9,11},{10,... | collective-permute-start | bytes 786440 | tf_op jit(solution)/shard_map/ppermute | solution.py:471
  54.1 2.9 %ffn_far.1 = (bf16[128,1024]{1,0:T(8,128)(2,1)S(1)}, bf16[128,1024]{1,0:T(8,128)(2,1)S(1)}) custom-call(bf16[128,1024]{1,0:T(8,128)(2,1)S(1)} %get-tuple-element.143.rows_ref, bf16[128,1024]{1,0:T(8,128)(2,1)S(1)} %collective-permute-done.13.d_out_ref.d_out, bf16[2,1024,512]{2,1,0:T(8,128)(2,1)S(1)} %copy-done.4, ...), custom_call_target="tpu_custom_call" | custom-call | tf_op jit(solution)/shard_map/ffn_far/pallas_call | solution.py:53
  56.9 0.6 collective-permute-start.17
  57.5 2.6 %collective-permute-done.18.got = bf16[128,1024]{1,0:T(8,128)(2,1)S(1)} collective-permute-done((bf16[128,1024]{1,0:T(8,128)(2,1)S(1)}, bf16[128,1024]{1,0:T(8,128)(2,1)S(1)}, u32[]{:S(2)}, u32[]{:S(2)}) %collective-permute-start.18) | collective-permute-done | bytes 262176 | tf_op jit(solution)/shard_map/ppermute | solution.py:471
  60.4 0.5 collective-permute-start.20
  60.9 0.8 collective-permute-done.19.fourth_a
  62.0 2.0 %attn_back_first.1 = (bf16[4,128,256]{2,1,0:T(8,128)(2,1)S(1)}, f32[4,128,256]{2,1,0:T(8,128)S(1)}, f32[4,128,256]{2,1,0:T(8,128)S(1)}, bf16[4,128,256]{2,1,0:T(8,128)(2,1)S(1)}) custom-call(s32[4,1,128]{2,1,0:T(1,128)S(1)} %bitcast.9, bf16[128,1024]{1,0:T(8,128)(2,1)S(1)} %get-tuple-element.147.third.d_resid, ...), custom_call_target="tpu_custom_call" | custom-call | tf_op jit(solution)/shard_map/attn_back_first/pallas_call | solution.py:53
  63.9 0.4 collective-permute-done.17.got
  64.7 1.5 %collective-permute-done.21.second = bf16[128,1024]{1,0:T(8,128)(2,1)S(1)} collective-permute-done((bf16[128,1024]{1,0:T(8,128)(2,1)S(1)}, bf16[128,1024]{1,0:T(8,128)(2,1)S(1)}, u32[]{:S(2)}, u32[]{:S(2)}) %collective-permute-start.21) | collective-permute-done | bytes 262176 | tf_op jit(solution)/shard_map/ppermute | solution.py:468
  66.3 2.4 %attn_back_second.1 = (bf16[256,1024]{1,0:T(8,128)(2,1)S(1)}, bf16[4,128,256]{2,1,0:T(8,128)(2,1)S(1)}, bf16[4,128,256]{2,1,0:T(8,128)(2,1)S(1)}, bf16[4,128,256...) custom-call(s32[4,1,128]{2,1,0:T(1,128)S(1)} %bitcast.10, bf16[128,1024]{1,0:T(8,128)(2,1)S(1)} %resid_back.1.first.d_resid, ...), custom_call_target="tpu_custom_call" | custom-call | tf_op jit(solution)/shard_map/attn_back_second/pallas_call | solution.py:53
  68.9 0.7 attn_back_keep.1.keep
  69.6 1.0 collective-permute-done.22.take
  70.8 2.1 %collective-permute-start.24 = (bf16[128,1024]{1,0:T(8,128)(2,1)S(1)}, bf16[128,1024]{1,0:T(8,128)(2,1)S(1)}, u32[]{:S(2)}, u32[]{:S(2)}) collective-permute-start(bf16[128,1024]{1,0:T(8,128)(2,1)S(1)} %get-tuple-element.164.part), channel_id=1, source_target_pairs={{0,2},{1,3},{2,0},{3,1},{4,6},{5,7},{6,4},{7,5},{8,10},{9,11},{10,... | collective-permute-start | bytes 786440 | tf_op jit(solution)/shard_map/ppermute | solution.py:471
  73.0 7.0 %collective-permute-done.24.got = bf16[128,1024]{1,0:T(8,128)(2,1)S(1)} collective-permute-done((bf16[128,1024]{1,0:T(8,128)(2,1)S(1)}, bf16[128,1024]{1,0:T(8,128)(2,1)S(1)}, u32[]{:S(2)}, u32[]{:S(2)}) %collective-permute-start.24) | collective-permute-done | bytes 262176 | tf_op jit(solution)/shard_map/ppermute | solution.py:471
  80.4 0.5 collective-permute-start.26
  81.1 1.7 %collective-permute-start.29 = (bf16[96,1024]{1,0:T(8,128)(2,1)S(1)}, bf16[96,1024]{1,0:T(8,128)(2,1)S(1)}, u32[]{:S(2)}, u32[]{:S(2)}) collective-permute-start(bf16[96,1024]{1,0:T(8,128)(2,1)S(1)} %get-tuple-element.180), channel_id=1, source_target_pairs={{0,16},{4,20},{8,24},{12,28},{16,0},{20,4},{24,8},{28,12},{1,17},{... | collective-permute-start | bytes 589832 | tf_op jit(solution)/shard_map/ppermute | solution.py:474
  82.8 1.0 enc_grads_first.1
  83.8 1.6 %collective-permute-done.23.got = bf16[128,1024]{1,0:T(8,128)(2,1)S(1)} collective-permute-done((bf16[128,1024]{1,0:T(8,128)(2,1)S(1)}, bf16[128,1024]{1,0:T(8,128)(2,1)S(1)}, u32[]{:S(2)}, u32[]{:S(2)}) %collective-permute-start.23) | collective-permute-done | bytes 262176 | tf_op jit(solution)/shard_map/ppermute | solution.py:471
  85.7 0.5 collective-permute-start.28
  86.2 1.9 %collective-permute-done.29.refs_1_ = bf16[96,1024]{1,0:T(8,128)(2,1)S(1)} collective-permute-done((bf16[96,1024]{1,0:T(8,128)(2,1)S(1)}, bf16[96,1024]{1,0:T(8,128)(2,1)S(1)}, u32[]{:S(2)}, u32[]{:S(2)}) %collective-permute-start.29) | collective-permute-done | bytes 196640 | tf_op jit(solution)/shard_map/ppermute | solution.py:474
  88.1 0.9 enc_grad0_second.1
  89.3 0.5 enc_grad1_second.1
  89.8 1.5 %collective-permute-start.30 = (bf16[4,128,256]{2,1,0:T(8,128)(2,1)S(1)}, bf16[4,128,256]{2,1,0:T(8,128)(2,1)S(1)}, u32[]{:S(2)}, u32[]{:S(2)}) collective-permute-start(bf16[4,128,256]{2,1,0:T(8,128)(2,1)S(1)} %get-tuple-element.186), channel_id=1, source_target_pairs={{0,16},{4,20},{8,24},{12,28},{16,0},{20,4},{24,8},{28,12},{1,17},{... | collective-permute-start | bytes 786440 | tf_op jit(solution)/shard_map/ppermute | solution.py:474
  91.3 2.1 %collective-permute-start.31 = (bf16[48,1024]{1,0:T(8,128)(2,1)S(1)}, bf16[48,1024]{1,0:T(8,128)(2,1)S(1)}, u32[]{:S(2)}, u32[]{:S(2)}) collective-permute-start(bf16[48,1024]{1,0:T(8,128)(2,1)S(1)} %get-tuple-element.190), channel_id=1, source_target_pairs={{0,4},{4,0},{8,12},{12,8},{16,20},{20,16},{24,28},{28,24},{1,5},{5... | collective-permute-start | bytes 294920 | tf_op jit(solution)/shard_map/ppermute | solution.py:474
  93.4 1.3 %collective-permute-start.32 = (bf16[48,1024]{1,0:T(8,128)(2,1)S(1)}, bf16[48,1024]{1,0:T(8,128)(2,1)S(1)}, u32[]{:S(2)}, u32[]{:S(2)}) collective-permute-start(bf16[48,1024]{1,0:T(8,128)(2,1)S(1)} %get-tuple-element.191), channel_id=1, source_target_pairs={{0,8},{4,12},{8,0},{12,4},{16,24},{20,28},{24,16},{28,20},{1,9},{5... | collective-permute-start | bytes 294920 | tf_op jit(solution)/shard_map/ppermute | solution.py:474
  94.7 1.1 collective-permute-start.33
  95.8 0.5 ffn_out_far.1
  96.3 3.6 %collective-permute-done.36.got = bf16[4,128,256]{2,1,0:T(8,128)(2,1)S(1)} collective-permute-done((bf16[4,128,256]{2,1,0:T(8,128)(2,1)S(1)}, bf16[4,128,256]{2,1,0:T(8,128)(2,1)S(1)}, u32[]{:S(2)}, u32[]{:S(2)}) %collective-permute-start.36) | collective-permute-done | bytes 262176 | tf_op jit(solution)/shard_map/ppermute | solution.py:474
  99.9 1.8 %collective-permute-start.39 = (bf16[128,1024]{1,0:T(8,128)(2,1)S(1)}, bf16[128,1024]{1,0:T(8,128)(2,1)S(1)}, u32[]{:S(2)}, u32[]{:S(2)}) collective-permute-start(bf16[128,1024]{1,0:T(8,128)(2,1)S(1)} %ffn_out_far.1), channel_id=1, source_target_pairs={{0,2},{1,3},{2,0},{3,1},{4,6},{5,7},{6,4},{7,5},{8,10},{9,11},{10,... | collective-permute-start | bytes 786440 | tf_op jit(solution)/shard_map/ppermute | solution.py:471
  101.8 1.7 %collective-permute-start.37 = (bf16[2,128,256]{2,1,0:T(8,128)(2,1)S(1)}, bf16[2,128,256]{2,1,0:T(8,128)(2,1)S(1)}, u32[]{:S(2)}, u32[]{:S(2)}) collective-permute-start(bf16[2,128,256]{2,1,0:T(8,128)(2,1)S(1)} %get-tuple-element.204), channel_id=1, source_target_pairs={{0,16},{4,20},{8,24},{12,28},{16,0},{20,4},{24,8},{28,12},{1,17},{... | collective-permute-start | bytes 393224 | tf_op jit(solution)/shard_map/ppermute | solution.py:474
  103.5 1.4 %collective-permute-done.33.refs_3_ = bf16[48,1024]{1,0:T(8,128)(2,1)S(1)} collective-permute-done((bf16[48,1024]{1,0:T(8,128)(2,1)S(1)}, bf16[48,1024]{1,0:T(8,128)(2,1)S(1)}, u32[]{:S(2)}, u32[]{:S(2)}) %collective-permute-start.33) | collective-permute-done | bytes 98336 | tf_op jit(solution)/shard_map/ppermute | solution.py:474
  105.0 1.8 %collective-permute-done.37.got = bf16[2,128,256]{2,1,0:T(8,128)(2,1)S(1)} collective-permute-done((bf16[2,128,256]{2,1,0:T(8,128)(2,1)S(1)}, bf16[2,128,256]{2,1,0:T(8,128)(2,1)S(1)}, u32[]{:S(2)}, u32[]{:S(2)}) %collective-permute-start.37) | collective-permute-done | bytes 131104 | tf_op jit(solution)/shard_map/ppermute | solution.py:474
  106.9 2.9 %collective-permute-start.38 = (bf16[1,128,256]{2,1,0:T(8,128)(2,1)S(1)}, bf16[1,128,256]{2,1,0:T(8,128)(2,1)S(1)}, u32[]{:S(2)}, u32[]{:S(2)}) collective-permute-start(bf16[1,128,256]{2,1,0:T(8,128)(2,1)S(1)} %get-tuple-element.205), channel_id=1, source_target_pairs={{0,8},{4,12},{8,0},{12,4},{16,24},{20,28},{24,16},{28,20},{1,9},{5... | collective-permute-start | bytes 196616 | tf_op jit(solution)/shard_map/ppermute | solution.py:474
  110.0 2.2 %collective-permute-start.35 = (bf16[1,128,256]{2,1,0:T(8,128)(2,1)S(1)}, bf16[1,128,256]{2,1,0:T(8,128)(2,1)S(1)}, u32[]{:S(2)}, u32[]{:S(2)}) collective-permute-start(bf16[1,128,256]{2,1,0:T(8,128)(2,1)S(1)} %get-tuple-element.196), channel_id=1, source_target_pairs={{0,8},{4,12},{8,0},{12,4},{16,24},{20,28},{24,16},{28,20},{1,9},{5... | collective-permute-start | bytes 196616 | tf_op jit(solution)/shard_map/ppermute | solution.py:474
  112.2 1.0 back_recv.1
  113.2 1.2 %ffn_out_own.1 = bf16[128,1024]{1,0:T(8,128)(2,1)} custom-call(bf16[128,1024]{1,0:T(8,128)(2,1)S(1)} %get-tuple-element.206.hidden, bf16[512,1024]{1,0:T(8,128)(2,1)S(1)} %copy-done.2, bf16[512,1024]{1,0:T(8,128)(2,1)S(1)} %collective-permute-done.1.out_b.w_b, bf16[128,1024]{1,0:T(8,128)(2,1)S(1)} %get-tuple-element.154.resid, ...), custom_call_target="tpu_custom_call" | custom-call | tf_op jit(solution)/shard_map/ffn_out_own/pallas_call | solution.py:53
  114.4 1.1 collective-permute-done.35.got1
  115.5 0.7 finish.1
  (64 shorter events, 4.7 us)
Async XLA Ops:
  0.6 7.9 %collective-permute-start = (bf16[2,1024,512]{2,1,0:T(8,128)(2,1)}, bf16[2,1024,512]{2,1,0:T(8,128)(2,1)S(1)}, u32[]{:S(2)}, u32[]{:S(2)}) collective-permute-start(bf16[2,1024,512]{2,1,0:T(8,128)(2,1)} %in_a.3), channel_id=1, source_target_pairs={{0,1},{1,0},{2,3},{3,2},{4,5},{5,4},{6,7},{7,6},{8,9},{9,8},{10,11... | collective-permute-start | bytes 6291464 | tf_op jit(solution)/shard_map/ppermute | solution.py:468
  1.1 7.4 %collective-permute-start.1 = (bf16[512,1024]{1,0:T(8,128)(2,1)}, bf16[512,1024]{1,0:T(8,128)(2,1)S(1)}, u32[]{:S(2)}, u32[]{:S(2)}) collective-permute-start(bf16[512,1024]{1,0:T(8,128)(2,1)} %w_a.3), channel_id=1, source_target_pairs={{0,1},{1,0},{2,3},{3,2},{4,5},{5,4},{6,7},{7,6},{8,9},{9,8},{10,11... | collective-permute-start | bytes 3145736 | tf_op jit(solution)/shard_map/ppermute | solution.py:468
  1.9 0.9 copy-start.7
  2.9 20.2 %copy-start = (bf16[2,1024,1024]{2,1,0:T(8,128)(2,1)S(1)}, bf16[2,1024,1024]{2,1,0:T(8,128)(2,1)}, u32[]{:S(2)}) copy-start(bf16[2,1024,1024]{2,1,0:T(8,128)(2,1)} %refs_6_.1) | copy-start | bytes 12582916
  2.9 20.2 %copy-start.1 = (bf16[4,1024,256]{2,1,0:T(8,128)(2,1)S(1)}, bf16[4,1024,256]{2,1,0:T(8,128)(2,1)}, u32[]{:S(2)}) copy-start(bf16[4,1024,256]{2,1,0:T(8,128)(2,1)} %w_in.7) | copy-start | bytes 6291460
  3.2 10.6 %collective-permute-start.2 = (bf16[24,1152]{1,0:T(8,128)(2,1)S(1)}, bf16[24,1152]{1,0:T(8,128)(2,1)S(1)}, u32[]{:S(2)}, u32[]{:S(2)}) collective-permute-start(bf16[24,1152]{1,0:T(8,128)(2,1)S(1)} %get-tuple-element.112), channel_id=1, source_target_pairs={{0,8},{4,12},{8,0},{12,4},{16,24},{20,28},{24,16},{28,20},{1,9},{5... | collective-permute-start | bytes 165896 | tf_op jit(solution)/shard_map/ppermute | solution.py:474
  7.3 8.8 %collective-permute-start.3 = (bf16[24,1152]{1,0:T(8,128)(2,1)S(1)}, bf16[24,1152]{1,0:T(8,128)(2,1)S(1)}, u32[]{:S(2)}, u32[]{:S(2)}) collective-permute-start(bf16[24,1152]{1,0:T(8,128)(2,1)S(1)} %get-tuple-element.113), channel_id=1, source_target_pairs={{0,24},{4,28},{8,16},{12,20},{16,8},{20,12},{24,0},{28,4},{1,25},{... | collective-permute-start | bytes 165896 | tf_op jit(solution)/shard_map/ppermute | solution.py:474
  8.6 7.8 %collective-permute-start.4 = (bf16[24,1152]{1,0:T(8,128)(2,1)S(1)}, bf16[24,1152]{1,0:T(8,128)(2,1)S(1)}, u32[]{:S(2)}, u32[]{:S(2)}) collective-permute-start(bf16[24,1152]{1,0:T(8,128)(2,1)S(1)} %get-tuple-element.120), channel_id=1, source_target_pairs={{0,12},{4,8},{8,4},{12,0},{16,28},{20,24},{24,20},{28,16},{1,13},{... | collective-permute-start | bytes 165896 | tf_op jit(solution)/shard_map/ppermute | solution.py:474
  12.2 7.0 %collective-permute-start.5 = (bf16[24,1152]{1,0:T(8,128)(2,1)S(1)}, bf16[24,1152]{1,0:T(8,128)(2,1)S(1)}, u32[]{:S(2)}, u32[]{:S(2)}) collective-permute-start(bf16[24,1152]{1,0:T(8,128)(2,1)S(1)} %get-tuple-element.121), channel_id=1, source_target_pairs={{0,28},{4,24},{8,20},{12,16},{16,12},{20,8},{24,4},{28,0},{1,29},{... | collective-permute-start | bytes 165896 | tf_op jit(solution)/shard_map/ppermute | solution.py:474
  12.8 6.4 %collective-permute-start.6 = (bf16[24,1152]{1,0:T(8,128)(2,1)S(1)}, bf16[24,1152]{1,0:T(8,128)(2,1)S(1)}, u32[]{:S(2)}, u32[]{:S(2)}) collective-permute-start(bf16[24,1152]{1,0:T(8,128)(2,1)S(1)} %get-tuple-element.122), channel_id=1, source_target_pairs={{0,16},{4,20},{8,24},{12,28},{16,0},{20,4},{24,8},{28,12},{1,17},{... | collective-permute-start | bytes 165896 | tf_op jit(solution)/shard_map/ppermute | solution.py:474
  13.9 5.3 %collective-permute-start.7 = (bf16[24,1152]{1,0:T(8,128)(2,1)S(1)}, bf16[24,1152]{1,0:T(8,128)(2,1)S(1)}, u32[]{:S(2)}, u32[]{:S(2)}) collective-permute-start(bf16[24,1152]{1,0:T(8,128)(2,1)S(1)} %get-tuple-element.123), channel_id=1, source_target_pairs={{0,4},{4,0},{8,12},{12,8},{16,20},{20,16},{24,28},{28,24},{1,5},{5... | collective-permute-start | bytes 165896 | tf_op jit(solution)/shard_map/ppermute | solution.py:474
  16.1 5.1 %collective-permute-start.8 = (bf16[24,1152]{1,0:T(8,128)(2,1)S(1)}, bf16[24,1152]{1,0:T(8,128)(2,1)S(1)}, u32[]{:S(2)}, u32[]{:S(2)}) collective-permute-start(bf16[24,1152]{1,0:T(8,128)(2,1)S(1)} %get-tuple-element.124), channel_id=1, source_target_pairs={{0,20},{4,16},{8,28},{12,24},{16,4},{20,0},{24,12},{28,8},{1,21},{... | collective-permute-start | bytes 165896 | tf_op jit(solution)/shard_map/ppermute | solution.py:474
  21.4 8.8 %copy-start.3 = (bf16[256,1024]{1,0:T(8,128)(2,1)S(1)}, bf16[256,1024]{1,0:T(8,128)(2,1)}, u32[]{:S(2)}) copy-start(bf16[256,1024]{1,0:T(8,128)(2,1)} %w_out.3) | copy-start | bytes 1572868
  21.4 9.3 %copy-start.5 = (bf16[1,128,1024]{2,1,0:T(8,128)(2,1)S(1)}, bf16[1,128,1024]{2,1,0:T(8,128)(2,1)}, u32[]{:S(2)}) copy-start(bf16[1,128,1024]{2,1,0:T(8,128)(2,1)} %param.19) | copy-start | bytes 786436
  21.4 11.1 %copy-start.6 = (s32[1,512]{1,0:T(1,128)S(1)}, s32[1,512]{1,0:T(1,128)}, u32[]{:S(2)}) copy-start(s32[1,512]{1,0:T(1,128)} %param.13) | copy-start | bytes 6148
  21.4 1.7 %collective-permute-start.10 = (bf16[128,1024]{1,0:T(8,128)(2,1)S(1)}, bf16[128,1024]{1,0:T(8,128)(2,1)S(1)}, u32[]{:S(2)}, u32[]{:S(2)}) collective-permute-start(bf16[128,1024]{1,0:T(8,128)(2,1)S(1)} %get-tuple-element.125.first.refs_3_), channel_id=1, source_target_pairs={{0,1},{1,0},{2,3},{3,2},{4,5},{5,4},{6,7},{7,6},{8,9},{9,8},{10,11... | collective-permute-start | bytes 786440 | tf_op jit(solution)/shard_map/ppermute | solution.py:468
  21.5 8.7 %collective-permute-start.9 = (bf16[128,1024]{1,0:T(8,128)(2,1)S(1)}, bf16[128,1024]{1,0:T(8,128)(2,1)S(1)}, u32[]{:S(2)}, u32[]{:S(2)}) collective-permute-start(bf16[128,1024]{1,0:T(8,128)(2,1)S(1)} %get-tuple-element.125.first.refs_3_), channel_id=1, source_target_pairs={{0,2},{1,3},{2,0},{3,1},{4,6},{5,7},{6,4},{7,5},{8,10},{9,11},{10,... | collective-permute-start | bytes 786440 | tf_op jit(solution)/shard_map/ppermute | solution.py:471
  30.2 8.7 %collective-permute-start.14 = (bf16[256,1024]{1,0:T(8,128)(2,1)S(1)}, bf16[256,1024]{1,0:T(8,128)(2,1)S(1)}, u32[]{:S(2)}, u32[]{:S(2)}) collective-permute-start(bf16[256,1024]{1,0:T(8,128)(2,1)S(1)} %copy-done.3), channel_id=1, source_target_pairs={{0,1},{1,0},{2,3},{3,2},{4,5},{5,4},{6,7},{7,6},{8,9},{9,8},{10,11... | collective-permute-start | bytes 1572872 | tf_op jit(solution)/shard_map/ppermute | solution.py:468
  30.2 2.3 %collective-permute-start.11 = (bf16[128,1024]{1,0:T(8,128)(2,1)S(1)}, bf16[128,1024]{1,0:T(8,128)(2,1)S(1)}, u32[]{:S(2)}, u32[]{:S(2)}) collective-permute-start(bf16[128,1024]{1,0:T(8,128)(2,1)S(1)} %collective-permute-done.9.third.refs_3_), channel_id=1, source_target_pairs={{0,1},{1,0},{2,3},{3,2},{4,5},{5,4},{6,7},{7,6},{8,9},{9,8},{10,11... | collective-permute-start | bytes 786440 | tf_op jit(solution)/shard_map/ppermute | solution.py:468
  30.7 8.2 %collective-permute-start.13 = (bf16[128,1024]{1,0:T(8,128)(2,1)S(1)}, bf16[128,1024]{1,0:T(8,128)(2,1)S(1)}, u32[]{:S(2)}, u32[]{:S(2)}) collective-permute-start(bf16[128,1024]{1,0:T(8,128)(2,1)S(1)} %bitcast.5), channel_id=1, source_target_pairs={{0,2},{1,3},{2,0},{3,1},{4,6},{5,7},{6,4},{7,5},{8,10},{9,11},{10,... | collective-permute-start | bytes 786440 | tf_op jit(solution)/shard_map/ppermute | solution.py:471
  35.8 13.0 %copy-start.2 = (bf16[512,1024]{1,0:T(8,128)(2,1)S(1)}, bf16[512,1024]{1,0:T(8,128)(2,1)}, u32[]{:S(2)}) copy-start(bf16[512,1024]{1,0:T(8,128)(2,1)} %w_a.3) | copy-start | bytes 3145732
  35.8 13.0 %copy-start.4 = (bf16[2,1024,512]{2,1,0:T(8,128)(2,1)S(1)}, bf16[2,1024,512]{2,1,0:T(8,128)(2,1)}, u32[]{:S(2)}) copy-start(bf16[2,1024,512]{2,1,0:T(8,128)(2,1)} %in_a.3) | copy-start | bytes 6291460
  35.8 3.1 %collective-permute-start.12 = (bf16[256,256]{1,0:T(8,128)(2,1)S(1)}, bf16[256,256]{1,0:T(8,128)(2,1)S(1)}, u32[]{:S(2)}, u32[]{:S(2)}) collective-permute-start(bf16[256,256]{1,0:T(8,128)(2,1)S(1)} %get-tuple-element.131), channel_id=1, source_target_pairs={{0,1},{1,0},{2,3},{3,2},{4,5},{5,4},{6,7},{7,6},{8,9},{9,8},{10,11... | collective-permute-start | bytes 393224 | tf_op jit(solution)/shard_map/ppermute | solution.py:468
  39.3 9.3 %collective-permute-start.16 = (bf16[128,1024]{1,0:T(8,128)(2,1)S(1)}, bf16[128,1024]{1,0:T(8,128)(2,1)S(1)}, u32[]{:S(2)}, u32[]{:S(2)}) collective-permute-start(bf16[128,1024]{1,0:T(8,128)(2,1)S(1)} %attn_out_far.1.part), channel_id=1, source_target_pairs={{0,2},{1,3},{2,0},{3,1},{4,6},{5,7},{6,4},{7,5},{8,10},{9,11},{10,... | collective-permute-start | bytes 786440 | tf_op jit(solution)/shard_map/ppermute | solution.py:471
  41.2 11.1 %collective-permute-start.15 = (bf16[128,1024]{1,0:T(8,128)(2,1)S(1)}, bf16[128,1024]{1,0:T(8,128)(2,1)S(1)}, u32[]{:S(2)}, u32[]{:S(2)}) collective-permute-start(bf16[128,1024]{1,0:T(8,128)(2,1)S(1)} %attn_out_own.1.part), channel_id=1, source_target_pairs={{0,2},{1,3},{2,0},{3,1},{4,6},{5,7},{6,4},{7,5},{8,10},{9,11},{10,... | collective-permute-start | bytes 786440 | tf_op jit(solution)/shard_map/ppermute | solution.py:471
  52.3 7.7 %collective-permute-start.18 = (bf16[128,1024]{1,0:T(8,128)(2,1)S(1)}, bf16[128,1024]{1,0:T(8,128)(2,1)S(1)}, u32[]{:S(2)}, u32[]{:S(2)}) collective-permute-start(bf16[128,1024]{1,0:T(8,128)(2,1)S(1)} %get-tuple-element.140.back), channel_id=1, source_target_pairs={{0,2},{1,3},{2,0},{3,1},{4,6},{5,7},{6,4},{7,5},{8,10},{9,11},{10,... | collective-permute-start | bytes 786440 | tf_op jit(solution)/shard_map/ppermute | solution.py:471
  56.9 7.4 %collective-permute-start.17 = (bf16[128,1024]{1,0:T(8,128)(2,1)S(1)}, bf16[128,1024]{1,0:T(8,128)(2,1)S(1)}, u32[]{:S(2)}, u32[]{:S(2)}) collective-permute-start(bf16[128,1024]{1,0:T(8,128)(2,1)S(1)} %get-tuple-element.145.back), channel_id=1, source_target_pairs={{0,2},{1,3},{2,0},{3,1},{4,6},{5,7},{6,4},{7,5},{8,10},{9,11},{10,... | collective-permute-start | bytes 786440 | tf_op jit(solution)/shard_map/ppermute | solution.py:471
  60.4 1.4 %collective-permute-start.19 = (bf16[64,1024]{1,0:T(8,128)(2,1)S(1)}, bf16[64,1024]{1,0:T(8,128)(2,1)S(1)}, u32[]{:S(2)}, u32[]{:S(2)}) collective-permute-start(bf16[64,1024]{1,0:T(8,128)(2,1)S(1)} %get-tuple-element.148), channel_id=1, source_target_pairs={{0,1},{1,0},{2,3},{3,2},{4,5},{5,4},{6,7},{7,6},{8,9},{9,8},{10,11... | collective-permute-start | bytes 393224 | tf_op jit(solution)/shard_map/ppermute | solution.py:468
  60.4 1.5 %collective-permute-start.20 = (bf16[64,1024]{1,0:T(8,128)(2,1)S(1)}, bf16[64,1024]{1,0:T(8,128)(2,1)S(1)}, u32[]{:S(2)}, u32[]{:S(2)}) collective-permute-start(bf16[64,1024]{1,0:T(8,128)(2,1)S(1)} %get-tuple-element.149), channel_id=1, source_target_pairs={{0,1},{1,0},{2,3},{3,2},{4,5},{5,4},{6,7},{7,6},{8,9},{9,8},{10,11... | collective-permute-start | bytes 393224 | tf_op jit(solution)/shard_map/ppermute | solution.py:468
  64.7 1.6 %collective-permute-start.21 = (bf16[128,1024]{1,0:T(8,128)(2,1)S(1)}, bf16[128,1024]{1,0:T(8,128)(2,1)S(1)}, u32[]{:S(2)}, u32[]{:S(2)}) collective-permute-start(bf16[128,1024]{1,0:T(8,128)(2,1)S(1)} %resid_back.1.first.d_resid), channel_id=1, source_target_pairs={{0,1},{1,0},{2,3},{3,2},{4,5},{5,4},{6,7},{7,6},{8,9},{9,8},{10,11... | collective-permute-start | bytes 786440 | tf_op jit(solution)/shard_map/ppermute | solution.py:468
  68.7 2.0 %collective-permute-start.22 = (bf16[256,1024]{1,0:T(8,128)(2,1)S(1)}, bf16[256,1024]{1,0:T(8,128)(2,1)S(1)}, u32[]{:S(2)}, u32[]{:S(2)}) collective-permute-start(bf16[256,1024]{1,0:T(8,128)(2,1)S(1)} %get-tuple-element.163), channel_id=1, source_target_pairs={{0,1},{1,0},{2,3},{3,2},{4,5},{5,4},{6,7},{7,6},{8,9},{9,8},{10,11... | collective-permute-start | bytes 1572872 | tf_op jit(solution)/shard_map/ppermute | solution.py:468
  70.8 9.2 %collective-permute-start.24 = (bf16[128,1024]{1,0:T(8,128)(2,1)S(1)}, bf16[128,1024]{1,0:T(8,128)(2,1)S(1)}, u32[]{:S(2)}, u32[]{:S(2)}) collective-permute-start(bf16[128,1024]{1,0:T(8,128)(2,1)S(1)} %get-tuple-element.164.part), channel_id=1, source_target_pairs={{0,2},{1,3},{2,0},{3,1},{4,6},{5,7},{6,4},{7,5},{8,10},{9,11},{10,... | collective-permute-start | bytes 786440 | tf_op jit(solution)/shard_map/ppermute | solution.py:471
  72.9 12.4 %collective-permute-start.23 = (bf16[128,1024]{1,0:T(8,128)(2,1)S(1)}, bf16[128,1024]{1,0:T(8,128)(2,1)S(1)}, u32[]{:S(2)}, u32[]{:S(2)}) collective-permute-start(bf16[128,1024]{1,0:T(8,128)(2,1)S(1)} %get-tuple-element.165.part), channel_id=1, source_target_pairs={{0,2},{1,3},{2,0},{3,1},{4,6},{5,7},{6,4},{7,5},{8,10},{9,11},{10,... | collective-permute-start | bytes 786440 | tf_op jit(solution)/shard_map/ppermute | solution.py:471
  80.3 2.5 %collective-permute-start.25 = (bf16[64,1024]{1,0:T(8,128)(2,1)S(1)}, bf16[64,1024]{1,0:T(8,128)(2,1)S(1)}, u32[]{:S(2)}, u32[]{:S(2)}) collective-permute-start(bf16[64,1024]{1,0:T(8,128)(2,1)S(1)} %get-tuple-element.167), channel_id=1, source_target_pairs={{0,1},{1,0},{2,3},{3,2},{4,5},{5,4},{6,7},{7,6},{8,9},{9,8},{10,11... | collective-permute-start | bytes 393224 | tf_op jit(solution)/shard_map/ppermute | solution.py:468
  80.4 2.4 %collective-permute-start.26 = (bf16[64,1024]{1,0:T(8,128)(2,1)S(1)}, bf16[64,1024]{1,0:T(8,128)(2,1)S(1)}, u32[]{:S(2)}, u32[]{:S(2)}) collective-permute-start(bf16[64,1024]{1,0:T(8,128)(2,1)S(1)} %get-tuple-element.168), channel_id=1, source_target_pairs={{0,1},{1,0},{2,3},{3,2},{4,5},{5,4},{6,7},{7,6},{8,9},{9,8},{10,11... | collective-permute-start | bytes 393224 | tf_op jit(solution)/shard_map/ppermute | solution.py:468
  81.1 7.0 %collective-permute-start.29 = (bf16[96,1024]{1,0:T(8,128)(2,1)S(1)}, bf16[96,1024]{1,0:T(8,128)(2,1)S(1)}, u32[]{:S(2)}, u32[]{:S(2)}) collective-permute-start(bf16[96,1024]{1,0:T(8,128)(2,1)S(1)} %get-tuple-element.180), channel_id=1, source_target_pairs={{0,16},{4,20},{8,24},{12,28},{16,0},{20,4},{24,8},{28,12},{1,17},{... | collective-permute-start | bytes 589832 | tf_op jit(solution)/shard_map/ppermute | solution.py:474
  85.6 2.4 %collective-permute-start.27 = (bf16[64,1024]{1,0:T(8,128)(2,1)S(1)}, bf16[64,1024]{1,0:T(8,128)(2,1)S(1)}, u32[]{:S(2)}, u32[]{:S(2)}) collective-permute-start(bf16[64,1024]{1,0:T(8,128)(2,1)S(1)} %get-tuple-element.177), channel_id=1, source_target_pairs={{0,1},{1,0},{2,3},{3,2},{4,5},{5,4},{6,7},{7,6},{8,9},{9,8},{10,11... | collective-permute-start | bytes 393224 | tf_op jit(solution)/shard_map/ppermute | solution.py:468
  85.7 2.4 %collective-permute-start.28 = (bf16[64,1024]{1,0:T(8,128)(2,1)S(1)}, bf16[64,1024]{1,0:T(8,128)(2,1)S(1)}, u32[]{:S(2)}, u32[]{:S(2)}) collective-permute-start(bf16[64,1024]{1,0:T(8,128)(2,1)S(1)} %get-tuple-element.178), channel_id=1, source_target_pairs={{0,1},{1,0},{2,3},{3,2},{4,5},{5,4},{6,7},{7,6},{8,9},{9,8},{10,11... | collective-permute-start | bytes 393224 | tf_op jit(solution)/shard_map/ppermute | solution.py:468
  89.0 10.9 %collective-permute-start.36 = (bf16[4,128,256]{2,1,0:T(8,128)(2,1)S(1)}, bf16[4,128,256]{2,1,0:T(8,128)(2,1)S(1)}, u32[]{:S(2)}, u32[]{:S(2)}) collective-permute-start(bf16[4,128,256]{2,1,0:T(8,128)(2,1)S(1)} %get-tuple-element.200), channel_id=1, source_target_pairs={{0,4},{4,0},{8,12},{12,8},{16,20},{20,16},{24,28},{28,24},{1,5},{5... | collective-permute-start | bytes 786440 | tf_op jit(solution)/shard_map/ppermute | solution.py:474
  89.8 15.1 %collective-permute-start.30 = (bf16[4,128,256]{2,1,0:T(8,128)(2,1)S(1)}, bf16[4,128,256]{2,1,0:T(8,128)(2,1)S(1)}, u32[]{:S(2)}, u32[]{:S(2)}) collective-permute-start(bf16[4,128,256]{2,1,0:T(8,128)(2,1)S(1)} %get-tuple-element.186), channel_id=1, source_target_pairs={{0,16},{4,20},{8,24},{12,28},{16,0},{20,4},{24,8},{28,12},{1,17},{... | collective-permute-start | bytes 786440 | tf_op jit(solution)/shard_map/ppermute | solution.py:474
  91.3 10.5 %collective-permute-start.31 = (bf16[48,1024]{1,0:T(8,128)(2,1)S(1)}, bf16[48,1024]{1,0:T(8,128)(2,1)S(1)}, u32[]{:S(2)}, u32[]{:S(2)}) collective-permute-start(bf16[48,1024]{1,0:T(8,128)(2,1)S(1)} %get-tuple-element.190), channel_id=1, source_target_pairs={{0,4},{4,0},{8,12},{12,8},{16,20},{20,16},{24,28},{28,24},{1,5},{5... | collective-permute-start | bytes 294920 | tf_op jit(solution)/shard_map/ppermute | solution.py:474
  93.4 10.1 %collective-permute-start.32 = (bf16[48,1024]{1,0:T(8,128)(2,1)S(1)}, bf16[48,1024]{1,0:T(8,128)(2,1)S(1)}, u32[]{:S(2)}, u32[]{:S(2)}) collective-permute-start(bf16[48,1024]{1,0:T(8,128)(2,1)S(1)} %get-tuple-element.191), channel_id=1, source_target_pairs={{0,8},{4,12},{8,0},{12,4},{16,24},{20,28},{24,16},{28,20},{1,9},{5... | collective-permute-start | bytes 294920 | tf_op jit(solution)/shard_map/ppermute | solution.py:474
  94.7 10.2 %collective-permute-start.33 = (bf16[48,1024]{1,0:T(8,128)(2,1)S(1)}, bf16[48,1024]{1,0:T(8,128)(2,1)S(1)}, u32[]{:S(2)}, u32[]{:S(2)}) collective-permute-start(bf16[48,1024]{1,0:T(8,128)(2,1)S(1)} %get-tuple-element.192), channel_id=1, source_target_pairs={{0,12},{4,8},{8,4},{12,0},{16,28},{20,24},{24,20},{28,16},{1,13},{... | collective-permute-start | bytes 294920 | tf_op jit(solution)/shard_map/ppermute | solution.py:474
  99.9 13.3 %collective-permute-start.39 = (bf16[128,1024]{1,0:T(8,128)(2,1)S(1)}, bf16[128,1024]{1,0:T(8,128)(2,1)S(1)}, u32[]{:S(2)}, u32[]{:S(2)}) collective-permute-start(bf16[128,1024]{1,0:T(8,128)(2,1)S(1)} %ffn_out_far.1), channel_id=1, source_target_pairs={{0,2},{1,3},{2,0},{3,1},{4,6},{5,7},{6,4},{7,5},{8,10},{9,11},{10,... | collective-permute-start | bytes 786440 | tf_op jit(solution)/shard_map/ppermute | solution.py:471
  101.8 5.0 %collective-permute-start.37 = (bf16[2,128,256]{2,1,0:T(8,128)(2,1)S(1)}, bf16[2,128,256]{2,1,0:T(8,128)(2,1)S(1)}, u32[]{:S(2)}, u32[]{:S(2)}) collective-permute-start(bf16[2,128,256]{2,1,0:T(8,128)(2,1)S(1)} %get-tuple-element.204), channel_id=1, source_target_pairs={{0,16},{4,20},{8,24},{12,28},{16,0},{20,4},{24,8},{28,12},{1,17},{... | collective-permute-start | bytes 393224 | tf_op jit(solution)/shard_map/ppermute | solution.py:474
  104.9 5.0 %collective-permute-start.34 = (bf16[2,128,256]{2,1,0:T(8,128)(2,1)S(1)}, bf16[2,128,256]{2,1,0:T(8,128)(2,1)S(1)}, u32[]{:S(2)}, u32[]{:S(2)}) collective-permute-start(bf16[2,128,256]{2,1,0:T(8,128)(2,1)S(1)} %get-tuple-element.195), channel_id=1, source_target_pairs={{0,4},{4,0},{8,12},{12,8},{16,20},{20,16},{24,28},{28,24},{1,5},{5... | collective-permute-start | bytes 393224 | tf_op jit(solution)/shard_map/ppermute | solution.py:474
  106.9 7.5 %collective-permute-start.38 = (bf16[1,128,256]{2,1,0:T(8,128)(2,1)S(1)}, bf16[1,128,256]{2,1,0:T(8,128)(2,1)S(1)}, u32[]{:S(2)}, u32[]{:S(2)}) collective-permute-start(bf16[1,128,256]{2,1,0:T(8,128)(2,1)S(1)} %get-tuple-element.205), channel_id=1, source_target_pairs={{0,8},{4,12},{8,0},{12,4},{16,24},{20,28},{24,16},{28,20},{1,9},{5... | collective-permute-start | bytes 196616 | tf_op jit(solution)/shard_map/ppermute | solution.py:474
  110.0 5.5 %collective-permute-start.35 = (bf16[1,128,256]{2,1,0:T(8,128)(2,1)S(1)}, bf16[1,128,256]{2,1,0:T(8,128)(2,1)S(1)}, u32[]{:S(2)}, u32[]{:S(2)}) collective-permute-start(bf16[1,128,256]{2,1,0:T(8,128)(2,1)S(1)} %get-tuple-element.196), channel_id=1, source_target_pairs={{0,8},{4,12},{8,0},{12,4},{16,24},{20,28},{24,16},{28,20},{1,9},{5... | collective-permute-start | bytes 196616 | tf_op jit(solution)/shard_map/ppermute | solution.py:474

commit v8 on v6

--- a/solution.py
+++ b/solution.py
@@ -39,6 +39,10 @@
 
 def norm_back(grad, normed, factor):
     return factor * (grad - normed * jnp.mean(grad * normed, axis=-1, keepdims=True))
+
+
+def joined(refs):
+    return jnp.concatenate([r[...] for r in refs], axis=0)
 
 
 def turned(row, rows):
@@ -86,8 +90,8 @@
     j = lax.broadcasted_iota(jnp.int32, (rows, rows), 1)
     earlier = jnp.where((o_col == o_row.astype(F32)) & (i < j), 1.0, 0.0)
     rank = jnp.sum(earlier, axis=0, keepdims=True).astype(jnp.int32)
-    place_ref[...] = o_row * capacity + rank
     place = (o_row ^ group_index()) * capacity + rank
+    place_ref[...] = place
     spots = lax.broadcasted_iota(jnp.int32, (groups * capacity, rows), 0)
     hot = jnp.where(spots == place, 1.0, 0.0).astype(BF16)
     big = dot(hot, features[...])
@@ -108,21 +112,34 @@
     rows_ref[...] = bf16(dot(hot, bf16(got[:, :width]), TN))
 
 
-def back_send(order, hot, d_packed, out):
-    capacity = out.shape[1]
+def back_send(order, hot, d_packed, keep, send):
+    groups = len(order)
+    capacity = hot.shape[0] // groups
     big = dot(hot[...], d_packed[...])
-    for n, k in enumerate(order):
-        out[group_index() ^ k] = bf16(big[n * capacity : (n + 1) * capacity])
-
-
-def back_recv(place, got_ref, out):
-    got = jnp.concatenate([got_ref[k].astype(F32) for k in range(got_ref.shape[0])], axis=0)
+    at = {k: n * capacity for n, k in enumerate(order)}
+    for target, first in ((keep, 0), (send, groups // 2)):
+        parts = [big[at[first + k] : at[first + k] + capacity] for k in range(groups // 2)]
+        target[...] = bf16(jnp.concatenate(parts, axis=0))
+
+
+def picked(places, capacity, refs):
+    wide = [r[...].astype(F32) for r in refs]
+    parts = [wide[n][p * capacity : (p + 1) * capacity] for n, p in places]
+    return bf16(jnp.concatenate(parts, axis=0))
+
+
+def back_pick(places, capacity, *refs):
+    refs[-1][...] = picked(places, capacity, refs[:-1])
+
+
+def back_recv(places, capacity, place, *refs):
+    got, out = picked(places, capacity, refs[:-1]), refs[-1]
     spots = lax.broadcasted_iota(jnp.int32, (got.shape[0], out.shape[0]), 0)
     hot = jnp.where(spots == place[...], 1.0, 0.0).astype(BF16)
-    out[...] = bf16(dot(hot, bf16(got), TN))
-
-
-def encode(rows, enc, w_in, pre_all, pre_ref, act_ref, packed_ref, store):
+    out[...] = bf16(dot(hot, got, TN))
+
+
+def encode(rows, enc, w_in, pre_all, pre_ref, act_ref, store):
     width = rows.shape[1]
     cols = pre_ref.shape[1]
     for n in range(width // CHUNK):
@@ -132,22 +149,24 @@
         act_ref[:, part] = bf16(pre * jax.nn.sigmoid(pre))
     pre_ref[...] = pre_all[:, pl.ds(pl.multiple_of(tensor_index() * cols, cols), cols)]
     packed = bf16(dot(act_ref[...], enc[1]))
-    packed_ref[...] = packed[: packed_ref.shape[0]]
     wide = packed.astype(F32)
     normed = bf16(wide * norm_factor(wide))
     for c in range(w_in.shape[0]):
         store(c, bf16(dot(normed, w_in[c])))
-
-
-def encode_first(first, second, enc, w_in, pre_ref, act_ref, packed_ref, proj_ref, pre_all):
-    rows = jnp.concatenate([first[...], second[...]], axis=0)
-    half = first.shape[0]
+    return packed
+
+
+def encode_blocks(*refs):
+    blocks, (enc, w_in, pre_ref, act_ref, packed_ref, proj_ref, pre_all) = refs[:-7], refs[-7:]
+    rows = joined(blocks)
+    size = blocks[0].shape[0]
 
     def store(c, value):
-        proj_ref[c, 0] = value[:half]
-        proj_ref[c, 1] = value[half:]
-
-    encode(rows, enc, w_in, pre_all, pre_ref, act_ref, packed_ref, store)
+        for n in range(len(blocks)):
+            proj_ref[c, n] = value[n * size : (n + 1) * size]
+
+    packed = encode(rows, enc, w_in, pre_all, pre_ref, act_ref, store)
+    packed_ref[...] = packed[:size]
 
 
 def window(docs, r, rows):
@@ -185,19 +204,22 @@
 
 
 def attend_first(
-    docs, third, fourth, proj_a, enc, w_in,
-    pre_ref, act_ref, packed_ref, proj_ref, att_ref, give_ref, keep_ref, pre_all,
+    docs, fourth, pre_c, act_c, proj_a, proj_c, enc, w_in,
+    pre_ref, act_ref, proj_ref, att_ref, give_ref, keep_ref, pre_all,
 ):
-    rows = jnp.concatenate([third[...], fourth[...]], axis=0)
-    half = third.shape[0]
+    half = fourth.shape[0]
     cols = proj_a.shape[-1]
     proj_ref[:, 0:2] = proj_a[...]
+    proj_ref[:, 2:3] = proj_c[...]
+    pre_ref[:half, :] = pre_c[...]
+    act_ref[:half, :] = act_c[...]
 
     def store(c, value):
-        proj_ref[c, 2] = value[:half]
-        proj_ref[c, 3] = value[half:]
-
-    encode(rows, enc, w_in, pre_all, pre_ref, act_ref, packed_ref, store)
+        proj_ref[c, 3] = value
+
+    encode(
+        fourth[...], enc, w_in, pre_all, pre_ref.at[half : 2 * half], act_ref.at[half : 2 * half], store
+    )
     masks = head_masks(cols)
     for r, (target, place) in enumerate(((keep_ref, 1), (give_ref, 1), (keep_ref, 0), (give_ref, 0))):
         ahead, allowed, root_inv = window(docs, r, half)
@@ -299,10 +321,6 @@
     d_v[r] += d_values[half:]
 
 
-def joined(refs):
-    return jnp.concatenate([r[...] for r in refs], axis=0)
-
-
 def attn_back_first(docs, third, fourth_a, fourth_b, proj, att, w_out, d_q, d_k, d_v, d_g):
     masks = head_masks(w_out.shape[0])
     d_k[...] = jnp.zeros_like(d_k)
@@ -320,17 +338,25 @@
     return total
 
 
+def attn_back_own(docs, first, proj, att, w_out, d_k_far, d_v_far, d_q, d_k, d_v, d_g):
+    masks = head_masks(w_out.shape[0])
+    d_k[...] = d_k_far[...]
+    d_v[...] = d_v_far[...]
+    attend_back(docs, first[...], 0, proj, att, w_out[...], masks, d_q, d_k, d_v, d_g)
+
+
 def attn_back_second(
-    docs, first, second, proj, att, w_out, d_q_far, d_k_far, d_v_far, d_g_far, w_in,
+    docs, second, proj, att, w_out, d_q_far, d_g_far, d_q_own, d_k_own, d_v_own, d_g_own, w_in,
     give_ref, d_q, d_k, d_v, d_g, sum_k, sum_v,
 ):
     masks = head_masks(w_out.shape[0])
     d_q[2:4] = d_q_far[2:4]
     d_g[2:4] = d_g_far[2:4]
-    sum_k[...] = d_k_far[...]
-    sum_v[...] = d_v_far[...]
-    for r, rows in ((0, first), (1, second)):
-        attend_back(docs, rows[...], r, proj, att, w_out[...], masks, d_q, sum_k, sum_v, d_g)
+    d_q[0] = d_q_own[0]
+    d_g[0] = d_g_own[0]
+    sum_k[...] = d_k_own[...]
+    sum_v[...] = d_v_own[...]
+    attend_back(docs, second[...], 1, proj, att, w_out[...], masks, d_q, sum_k, sum_v, d_g)
     d_k[...] = bf16(sum_k[...])
     d_v[...] = bf16(sum_v[...])
     give_ref[...] = bf16(back_norm((d_q, d_k, d_v, d_g), w_in, 3, 1))
@@ -485,7 +511,7 @@
 
     pair = 2 * rows_dev
     pre_a, act_a, packed, proj_a = run(
-        encode_first,
+        encode_blocks,
         [
             like((pair, cols), F32),
             like((pair, width), BF16),
@@ -501,23 +527,28 @@
     mine_both = near(mine_far)
     attn_out_near = near(attn_out_late)
     d_out_far = far(d_out_late)
-    pre_b, act_b, packed_far, proj, attended, give, keep = run(
+    pre_c, act_c, packed_far, proj_c = run(
+        encode_blocks,
+        [like((rows_dev, cols), F32), row_b, row_b, like((comps, 1, rows_dev, cols), BF16)],
+        [mine_far, enc_weight, attn_in],
+        [pltpu.VMEM((rows_dev, width), F32)],
+        name="encode_third",
+    )
+    pre_b, act_b, proj, attended, give, keep = run(
         attend_first,
         [
             like((pair, cols), F32),
             like((pair, width), BF16),
-            row_b,
             like((comps, tensors, rows_dev, cols), BF16),
             like((tensors, rows_dev, cols), F32),
             like((pair, cols), BF16),
             like((pair, cols), BF16),
         ],
-        [docs, mine_far, mine_both, proj_a, enc_weight, attn_in],
-        [pltpu.VMEM((pair, width), F32)],
+        [docs, mine_both, pre_c, act_c, proj_a, proj_c, enc_weight, attn_in],
+        [pltpu.VMEM((rows_dev, width), F32)],
         name="attend_first",
     )
     take = near(give)
-    take, d_out_far = tie(take, d_out_far)
 
 
     def out_part(index, name):
@@ -531,6 +562,7 @@
     part_far = out_part(0, "attn_out_far")
     got_own = far(part_far)
     part_own = out_part(1, "attn_out_own")
+    part_own, d_out_far = tie(part_own, d_out_far)
     got_far = far(part_own)
 
     def feed(rows, cotangent, name):
@@ -571,10 +603,16 @@
     got_back_own, d_q = tie(got_back_own, d_q)
     (d_resid,) = run(resid_back, [row_b], [back_own, got_back_own, resid, d_out], name="resid_back")
     d_resid_near = near(d_resid)
+    own_grads = run(
+        attn_back_own,
+        [block_b, block_f, block_f, block_b],
+        [docs, d_resid, proj, attended, attn_out, d_k, d_v],
+        name="attn_back_own",
+    )
     give, *d_projected = run(
         attn_back_second,
         [like((pair, width), BF16)] + [block_b] * 4,
-        [docs, d_resid, d_resid_near, proj, attended, attn_out, d_q, d_k, d_v, d_g, attn_in],
+        [docs, d_resid_near, proj, attended, attn_out, d_q, d_g, *own_grads, attn_in],
         [pltpu.VMEM((tensors, rows_dev, cols), F32)] * 2,
         name="attn_back_second",
     )
@@ -596,13 +634,11 @@
     )
 
     cot_near = [near(h) for h in halves]
-    (backs,) = run(
-        functools.partial(back_send, order),
-        [like((groups, capacity, width), BF16)],
-        [hot, d_packed],
-        name="back_send",
-    )
-    returned = lax.all_to_all(backs, group_axes, split_axis=0, concat_axis=0, tiled=True)
+    half_rows = like((groups * capacity // 2, width), BF16)
+    kept, back = run(
+        functools.partial(back_send, order), [half_rows] * 2, [hot, d_packed], name="back_send"
+    )
+    back_got = crossed(back, groups // 2)
 
     part_f = like((width, cols), F32)
     part1, part0 = run(
@@ -612,10 +648,33 @@
         name="enc_grads_first",
     )
     got_far, part1, part0 = tie(got_far, part1, part0)
-    (cot_far,) = run(
-        packed_back, [row_b], [sum_far, got_far, packed_far, d_resid_far], name="packed_back_far"
-    )
-    cot_both = near(cot_far)
+    cot_far, *cot_pieces = run(
+        packed_back,
+        [row_b] + [piece_b] * pieces,
+        [sum_far, got_far, packed_far, d_resid_far],
+        name="packed_back_far",
+    )
+    cot_both = [near(piece) for piece in cot_pieces]
+    *cot_both, back_got = tie(*cot_both, back_got)
+    arrays = [kept, back_got]
+    held = {k: divmod(k, groups // 2) for k in range(groups)}
+
+    def send_back(bit):
+        moved = [k for k in range(groups) if k & bit]
+        (back,) = run(
+            functools.partial(back_pick, [held[k] for k in moved], capacity),
+            [half_rows],
+            arrays,
+            name="back_pick",
+        )
+        held.update({k: (len(arrays), n) for n, k in enumerate(moved)})
+        arrays.append(crossed(back, bit))
+
+    bit = groups // 4
+    while bit > 1:
+        send_back(bit)
+        bit //= 2
+
     cot_far, hidden_far = tie(cot_far, hidden_far)
     (out_far,) = run(
         ffn_out_far, [row_b], [hidden_far, ffn_out, ffn_out_near], name="ffn_out_far"
@@ -630,11 +689,10 @@
         shape = (2 ** (len(remaining) - 1), size, cols)
         return [like(shape, F32), like(shape, BF16)]
 
-    def reduce_over(stages, start, held, name):
+    def reduce_over(stages, start, name, beside=None):
         remaining = list(bits)
         kept, send = start((tuple(remaining), stages[0]))
         got = crossed(send, 1 << stages[0])
-        got, held = tie(got, held)
         remaining.remove(stages[0])
         for bit in stages[1:]:
             kept, send = run(
@@ -645,13 +703,15 @@
             )
             got = crossed(send, 1 << bit)
             remaining.remove(bit)
-        return kept, got, held
+            if beside is not None and bit == stages[1]:
+                got, beside[-1] = tie(got, beside[-1])
+        return kept, got
 
     def start1(setting):
         return run(
             functools.partial(enc_grad1_second, *setting),
             halves(bits),
-            [cot_far, cot_both, act_b, part1],
+            [cot_far, *cot_both, act_b, part1],
             total,
             name="enc_grad1_second",
         )
@@ -660,23 +720,23 @@
         return run(
             functools.partial(enc_grad0_second, *setting),
             halves(bits),
-            [cot_far, cot_both, mine_far, mine_both, pre_b, enc_weight, part0],
+            [cot_far, *cot_both, mine_far, mine_both, pre_b, enc_weight, part0],
             total,
             name="enc_grad0_second",
         )
 
-    kept1, got1, returned = reduce_over(event_bits + pack_bits, start1, returned, "halve1_")
-    kept0, got0, out_far = reduce_over(
-        pack_bits[:1] + event_bits + pack_bits[1:], start0, out_far, "halve0_"
-    )
+    kept1, got1 = reduce_over(event_bits + pack_bits, start1, "halve1_", arrays)
+    kept0, got0 = reduce_over(pack_bits[:1] + event_bits + pack_bits[1:], start0, "halve0_")
+    send_back(1)
+    back_places = [held[k] for k in range(groups)]
     got_out = far(out_far)
     (packed_out,) = run(
         ffn_out_own, [row_b], [hidden_own, ffn_out, ffn_out_near, resid, got_out], name="ffn_out_own"
     )
     (row_grad,) = run(
-        back_recv,
+        functools.partial(back_recv, back_places, capacity),
         [row_b],
-        [place, returned],
+        [place, *arrays],
         name="back_recv",
     )
     got1, got0, packed_out, row_grad = tie(got1, got0, packed_out, row_grad)

time: 132 us -> 117 us (0.89)
  local copies, waits for them, and re-layouts: 15.8 us -> 0.99 us
  waiting for transfers between devices: 40.1 us -> 51.8 us
  Pallas kernels: 33.7 us -> 26.7 us
  starting transfers between devices: 40.1 us -> 35.3 us
    unnamed x72 -> x16, local copies, waits for them, and re-layouts: 15.8 us -> 0.99 us
    ppermute x13 -> x16, waiting for transfers between devices: 11.5 us -> 22.5 us  [crossed(): return lax.ppermute(value, group_axes, [(i, i ^ k) for i in range(groups)])]
    pallas_call x30 -> x34, Pallas kernels: 33.7 us -> 26.7 us  [run(): pl.pallas_call(body, out_shape=list(outs), in_specs=[pl.BlockSpec(memory_...]
    all_to_all x1 -> x0, starting transfers between devices: 4.74 us -> none  [shards(): lax.all_to_all(backs, group_axes, split_axis=0, concat_axis=0, tiled=True)]
    ppermute x9, waiting for transfers between devices: 23.2 us -> 25.8 us  [far(): return lax.ppermute(value, 'tensor', [(i, i ^ 2) for i in range(tensors)])]
    ppermute x13 -> x14, waiting for transfers between devices: 5.37 us -> 3.49 us  [near(): return lax.ppermute(value, 'tensor', [(i, i ^ 1) for i in range(tensors)])]
    ppermute x13 -> x14, starting transfers between devices: 2.74 us -> 3.68 us  [near(): return lax.ppermute(value, 'tensor', [(i, i ^ 1) for i in range(tensors)])]
    ppermute x13 -> x16, starting transfers between devices: 21.8 us -> 21.7 us  [crossed(): return lax.ppermute(value, group_axes, [(i, i ^ k) for i in range(groups)])]
  transfers between devices with their start and end apart: 36 -> 39, of which waited for: 19 -> 22; matrix products, arithmetic and copies ran while one was open for 1% -> 1% of each run, Pallas kernels for 22% -> 20%
where the time goes in v8:
time: 117 us; the launch traced here: 116 us
  waiting for transfers between devices  51.8 us (44%)
  starting transfers between devices  35.3 us (30%)
  Pallas kernels  26.7 us (23%)
    pallas_call x34, Pallas kernels, run(): pl.pallas_call(body, out_shape=list(outs), in_specs=[pl.BlockSpec(memory_...  26.7 us
    ppermute x9, waiting for transfers between devices, far(): return lax.ppermute(value, 'tensor', [(i, i ^ 2) for i in range(tensors)])  25.8 us
    ppermute x16, waiting for transfers between devices, crossed(): return lax.ppermute(value, group_axes, [(i, i ^ k) for i in range(groups)])  22.5 us
    ppermute x16, starting transfers between devices, crossed(): return lax.ppermute(value, group_axes, [(i, i ^ k) for i in range(groups)])  21.7 us
    ppermute x9, starting transfers between devices, far(): return lax.ppermute(value, 'tensor', [(i, i ^ 2) for i in range(tensors)])  9.95 us
    ppermute x14, starting transfers between devices, near(): return lax.ppermute(value, 'tensor', [(i, i ^ 1) for i in range(tensors)])  3.68 us
    ppermute x14, waiting for transfers between devices, near(): return lax.ppermute(value, 'tensor', [(i, i ^ 1) for i in range(tensors)])  3.49 us
  transfers between devices with their start and end apart: 39, of which 22 were waited for; matrix products, arithmetic and copies ran while one was open for 1% of the time, Pallas kernels for 20%

profile of v8, /device:TPU:0, one launch (start us, length us, event | category | flops | bytes accessed | tf_op | source)
XLA Modules:
  0.0 116.4 jit_solution(13167326554959567215)
XLA Ops:
  0.6 0.5 collective-permute-start
  1.2 0.7 add_bitcast_fusion.code
  1.9 0.9 copy-done.7
  3.2 4.1 %collective-permute-start.2 = (bf16[24,1152]{1,0:T(8,128)(2,1)S(1)}, bf16[24,1152]{1,0:T(8,128)(2,1)S(1)}, u32[]{:S(2)}, u32[]{:S(2)}) collective-permute-start(bf16[24,1152]{1,0:T(8,128)(2,1)S(1)} %get-tuple-element.110), channel_id=1, source_target_pairs={{0,8},{4,12},{8,0},{12,4},{16,24},{20,28},{24,16},{28,20},{1,9},{5... | collective-permute-start | bytes 165896 | tf_op jit(solution)/shard_map/ppermute | solution.py:480
  7.3 1.3 %collective-permute-start.3 = (bf16[24,1152]{1,0:T(8,128)(2,1)S(1)}, bf16[24,1152]{1,0:T(8,128)(2,1)S(1)}, u32[]{:S(2)}, u32[]{:S(2)}) collective-permute-start(bf16[24,1152]{1,0:T(8,128)(2,1)S(1)} %get-tuple-element.111), channel_id=1, source_target_pairs={{0,24},{4,28},{8,16},{12,20},{16,8},{20,12},{24,0},{28,4},{1,25},{... | collective-permute-start | bytes 165896 | tf_op jit(solution)/shard_map/ppermute | solution.py:480
  8.6 3.6 %collective-permute-start.4 = (bf16[24,1152]{1,0:T(8,128)(2,1)S(1)}, bf16[24,1152]{1,0:T(8,128)(2,1)S(1)}, u32[]{:S(2)}, u32[]{:S(2)}) collective-permute-start(bf16[24,1152]{1,0:T(8,128)(2,1)S(1)} %get-tuple-element.118), channel_id=1, source_target_pairs={{0,12},{4,8},{8,4},{12,0},{16,28},{20,24},{24,20},{28,16},{1,13},{... | collective-permute-start | bytes 165896 | tf_op jit(solution)/shard_map/ppermute | solution.py:480
  12.2 0.6 collective-permute-start.5
  12.8 1.1 collective-permute-start.6
  13.9 2.2 %collective-permute-done.3.refs_2_ = bf16[24,1152]{1,0:T(8,128)(2,1)S(1)} collective-permute-done((bf16[24,1152]{1,0:T(8,128)(2,1)S(1)}, bf16[24,1152]{1,0:T(8,128)(2,1)S(1)}, u32[]{:S(2)}, u32[]{:S(2)}) %collective-permute-start.3) | collective-permute-done | bytes 55328 | tf_op jit(solution)/shard_map/ppermute | solution.py:480
  16.4 2.8 %collective-permute-done.5.refs_4_ = bf16[24,1152]{1,0:T(8,128)(2,1)S(1)} collective-permute-done((bf16[24,1152]{1,0:T(8,128)(2,1)S(1)}, bf16[24,1152]{1,0:T(8,128)(2,1)S(1)}, u32[]{:S(2)}, u32[]{:S(2)}) %collective-permute-start.5) | collective-permute-done | bytes 55328 | tf_op jit(solution)/shard_map/ppermute | solution.py:480
  19.2 1.9 %collective-permute-done.8.refs_7_ = bf16[24,1152]{1,0:T(8,128)(2,1)S(1)} collective-permute-done((bf16[24,1152]{1,0:T(8,128)(2,1)S(1)}, bf16[24,1152]{1,0:T(8,128)(2,1)S(1)}, u32[]{:S(2)}, u32[]{:S(2)}) %collective-permute-start.8) | collective-permute-done | bytes 55328 | tf_op jit(solution)/shard_map/ppermute | solution.py:480
  21.5 1.6 %collective-permute-start.9 = (bf16[128,1024]{1,0:T(8,128)(2,1)S(1)}, bf16[128,1024]{1,0:T(8,128)(2,1)S(1)}, u32[]{:S(2)}, u32[]{:S(2)}) collective-permute-start(bf16[128,1024]{1,0:T(8,128)(2,1)S(1)} %get-tuple-element.123.refs_0_.refs_3_), channel_id=1, source_target_pairs={{0,2},{1,3},{2,0},{3,1},{4,6},{5,7},{6,4},{7,5},{8,10},{9,11},{10,... | collective-permute-start | bytes 786440 | tf_op jit(solution)/shard_map/ppermute | solution.py:477
  23.1 2.2 %encode_first.1 = (f32[256,256]{1,0:T(8,128)S(1)}, bf16[256,1024]{1,0:T(8,128)(2,1)S(1)}, bf16[128,1024]{1,0:T(8,128)(2,1)S(1)}, bf16[4,2,128,256]{3,2,1,0:T(8,128)(2,1)S(1)}) custom-call(bf16[128,1024]{1,0:T(8,128)(2,1)S(1)} %get-tuple-element.123.refs_0_.refs_3_, bf16[128,1024]{1,0:T(8,128)(2,1)S(1)} %collective-permute-done.10.refs_1_.refs_4_, ...), custom_call_target="tpu_custom_call" | custom-call | tf_op jit(solution)/shard_map/encode_first/pallas_call | solution.py:57
  25.3 4.9 %collective-permute-done.9.refs_0_.refs_3_ = bf16[128,1024]{1,0:T(8,128)(2,1)S(1)} collective-permute-done((bf16[128,1024]{1,0:T(8,128)(2,1)S(1)}, bf16[128,1024]{1,0:T(8,128)(2,1)S(1)}, u32[]{:S(2)}, u32[]{:S(2)}) %collective-permute-start.9) | collective-permute-done | bytes 262176 | tf_op jit(solution)/shard_map/ppermute | solution.py:477
  30.2 0.5 collective-permute-start.11
  30.7 1.5 %collective-permute-start.14 = (bf16[128,1024]{1,0:T(8,128)(2,1)S(1)}, bf16[128,1024]{1,0:T(8,128)(2,1)S(1)}, u32[]{:S(2)}, u32[]{:S(2)}) collective-permute-start(bf16[128,1024]{1,0:T(8,128)(2,1)S(1)} %bitcast.5), channel_id=1, source_target_pairs={{0,2},{1,3},{2,0},{3,1},{4,6},{5,7},{6,4},{7,5},{8,10},{9,11},{10,... | collective-permute-start | bytes 786440 | tf_op jit(solution)/shard_map/ppermute | solution.py:477
  32.2 1.4 %encode_third.1 = (f32[128,256]{1,0:T(8,128)S(1)}, bf16[128,1024]{1,0:T(8,128)(2,1)S(1)}, bf16[128,1024]{1,0:T(8,128)(2,1)S(1)}, bf16[4,1,128,256]{3,2,1,0:T(8,128)(2,1)S(1)}) custom-call(bf16[128,1024]{1,0:T(8,128)(2,1)S(1)} %collective-permute-done.9.refs_0_.refs_3_, bf16[2,1024,1024]{2,1,0:T(8,128)(2,1)S(1)} %copy-done, bf16[4,1024,256]{2,1,0:T(8,128)(2,1)S(1)} %copy-done.1), custom_call_target="tpu_custom_call" | custom-call | tf_op jit(solution)/shard_map/encode_third/pallas_call | solution.py:57
  33.6 2.5 %attend_first.1 = (f32[256,256]{1,0:T(8,128)S(1)}, bf16[256,1024]{1,0:T(8,128)(2,1)S(1)}, bf16[4,4,128,256]{3,2,1,0:T(8,128)(2,1)S(1)}, f32[4,128,256]{2,1,0:T(8...) custom-call(s32[4,1,128]{2,1,0:T(1,128)S(1)} %bitcast.8, ...), custom_call_target="tpu_custom_call" | custom-call | tf_op jit(solution)/shard_map/attend_first/pallas_call | solution.py:57
  36.3 1.3 %collective-permute-done.12.take = bf16[256,256]{1,0:T(8,128)(2,1)S(1)} collective-permute-done((bf16[256,256]{1,0:T(8,128)(2,1)S(1)}, bf16[256,256]{1,0:T(8,128)(2,1)S(1)}, u32[]{:S(2)}, u32[]{:S(2)}) %collective-permute-start.12) | collective-permute-done | bytes 131104 | tf_op jit(solution)/shard_map/ppermute | solution.py:474
  37.9 0.6 collective-permute-start.16
  39.0 1.5 %collective-permute-start.15 = (bf16[128,1024]{1,0:T(8,128)(2,1)S(1)}, bf16[128,1024]{1,0:T(8,128)(2,1)S(1)}, u32[]{:S(2)}, u32[]{:S(2)}) collective-permute-start(bf16[128,1024]{1,0:T(8,128)(2,1)S(1)} %attn_out_own.1.part), channel_id=1, source_target_pairs={{0,2},{1,3},{2,0},{3,1},{4,6},{5,7},{6,4},{7,5},{8,10},{9,11},{10,... | collective-permute-start | bytes 786440 | tf_op jit(solution)/shard_map/ppermute | solution.py:477
  40.5 6.6 %collective-permute-done.16.got = bf16[128,1024]{1,0:T(8,128)(2,1)S(1)} collective-permute-done((bf16[128,1024]{1,0:T(8,128)(2,1)S(1)}, bf16[128,1024]{1,0:T(8,128)(2,1)S(1)}, u32[]{:S(2)}, u32[]{:S(2)}) %collective-permute-start.16) | collective-permute-done | bytes 262176 | tf_op jit(solution)/shard_map/ppermute | solution.py:477
  47.4 2.9 %ffn_own.1 = (bf16[128,1024]{1,0:T(8,128)(2,1)S(1)}, bf16[128,1024]{1,0:T(8,128)(2,1)S(1)}) custom-call(bf16[128,1024]{1,0:T(8,128)(2,1)S(1)} %get-tuple-element.137.rows_ref, bf16[128,1024]{1,0:T(8,128)(2,1)S(1)} %bitcast.6, bf16[2,1024,512]{2,1,0:T(8,128)(2,1)S(1)} %copy-done.4, bf16[2,1024,512]{2,1,0:T(8,128)(2,1)S(1)} %collective-permute-done.in_b, ...), custom_call_target="tpu_custom_call" | custom-call | tf_op jit(solution)/shard_map/ffn_own/pallas_call | solution.py:57
  50.3 1.7 %collective-permute-done.15.got = bf16[128,1024]{1,0:T(8,128)(2,1)S(1)} collective-permute-done((bf16[128,1024]{1,0:T(8,128)(2,1)S(1)}, bf16[128,1024]{1,0:T(8,128)(2,1)S(1)}, u32[]{:S(2)}, u32[]{:S(2)}) %collective-permute-start.15) | collective-permute-done | bytes 262176 | tf_op jit(solution)/shard_map/ppermute | solution.py:477
  52.0 0.5 collective-permute-start.18
  52.7 2.9 %ffn_far.1 = (bf16[128,1024]{1,0:T(8,128)(2,1)S(1)}, bf16[128,1024]{1,0:T(8,128)(2,1)S(1)}) custom-call(bf16[128,1024]{1,0:T(8,128)(2,1)S(1)} %get-tuple-element.144.rows_ref, bf16[128,1024]{1,0:T(8,128)(2,1)S(1)} %collective-permute-done.14.d_out_ref.d_out, bf16[2,1024,512]{2,1,0:T(8,128)(2,1)S(1)} %copy-done.4, ...), custom_call_target="tpu_custom_call" | custom-call | tf_op jit(solution)/shard_map/ffn_far/pallas_call | solution.py:57
  55.6 1.6 %collective-permute-start.17 = (bf16[128,1024]{1,0:T(8,128)(2,1)S(1)}, bf16[128,1024]{1,0:T(8,128)(2,1)S(1)}, u32[]{:S(2)}, u32[]{:S(2)}) collective-permute-start(bf16[128,1024]{1,0:T(8,128)(2,1)S(1)} %get-tuple-element.146.back), channel_id=1, source_target_pairs={{0,2},{1,3},{2,0},{3,1},{4,6},{5,7},{6,4},{7,5},{8,10},{9,11},{10,... | collective-permute-start | bytes 786440 | tf_op jit(solution)/shard_map/ppermute | solution.py:477
  57.2 4.1 %collective-permute-done.18.got = bf16[128,1024]{1,0:T(8,128)(2,1)S(1)} collective-permute-done((bf16[128,1024]{1,0:T(8,128)(2,1)S(1)}, bf16[128,1024]{1,0:T(8,128)(2,1)S(1)}, u32[]{:S(2)}, u32[]{:S(2)}) %collective-permute-start.18) | collective-permute-done | bytes 262176 | tf_op jit(solution)/shard_map/ppermute | solution.py:477
  61.6 0.5 collective-permute-start.20
  62.1 0.8 collective-permute-done.19.fourth_a
  63.1 2.0 %attn_back_first.1 = (bf16[4,128,256]{2,1,0:T(8,128)(2,1)S(1)}, f32[4,128,256]{2,1,0:T(8,128)S(1)}, f32[4,128,256]{2,1,0:T(8,128)S(1)}, bf16[4,128,256]{2,1,0:T(8,128)(2,1)S(1)}) custom-call(s32[4,1,128]{2,1,0:T(1,128)S(1)} %bitcast.9, bf16[128,1024]{1,0:T(8,128)(2,1)S(1)} %get-tuple-element.148.third.d_resid, ...), custom_call_target="tpu_custom_call" | custom-call | tf_op jit(solution)/shard_map/attn_back_first/pallas_call | solution.py:57
  65.4 0.4 collective-permute-start.21
  65.8 1.0 attn_back_own.1
  67.0 2.0 %attn_back_second.1 = (bf16[256,1024]{1,0:T(8,128)(2,1)S(1)}, bf16[4,128,256]{2,1,0:T(8,128)(2,1)S(1)}, bf16[4,128,256]{2,1,0:T(8,128)(2,1)S(1)}, bf16[4,128,256...) custom-call(s32[4,1,128]{2,1,0:T(1,128)S(1)} %bitcast.11, bf16[128,1024]{1,0:T(8,128)(2,1)S(1)} %collective-permute-done.21.second, ...), custom_call_target="tpu_custom_call" | custom-call | tf_op jit(solution)/shard_map/attn_back_second/pallas_call | solution.py:57
  69.0 0.4 collective-permute-start.22
  69.4 0.7 attn_back_keep.1.keep
  70.1 0.9 collective-permute-done.22.take
  71.1 0.6 collective-permute-start.24
  71.7 1.5 %collective-permute-start.23 = (bf16[128,1024]{1,0:T(8,128)(2,1)S(1)}, bf16[128,1024]{1,0:T(8,128)(2,1)S(1)}, u32[]{:S(2)}, u32[]{:S(2)}) collective-permute-start(bf16[128,1024]{1,0:T(8,128)(2,1)S(1)} %get-tuple-element.170.part), channel_id=1, source_target_pairs={{0,2},{1,3},{2,0},{3,1},{4,6},{5,7},{6,4},{7,5},{8,10},{9,11},{10,... | collective-permute-start | bytes 786440 | tf_op jit(solution)/shard_map/ppermute | solution.py:477
  73.2 7.1 %collective-permute-done.24.got = bf16[128,1024]{1,0:T(8,128)(2,1)S(1)} collective-permute-done((bf16[128,1024]{1,0:T(8,128)(2,1)S(1)}, bf16[128,1024]{1,0:T(8,128)(2,1)S(1)}, u32[]{:S(2)}, u32[]{:S(2)}) %collective-permute-start.24) | collective-permute-done | bytes 262176 | tf_op jit(solution)/shard_map/ppermute | solution.py:477
  80.7 0.5 collective-permute-start.26
  81.5 1.7 %collective-permute-start.29 = (bf16[96,1024]{1,0:T(8,128)(2,1)S(1)}, bf16[96,1024]{1,0:T(8,128)(2,1)S(1)}, u32[]{:S(2)}, u32[]{:S(2)}) collective-permute-start(bf16[96,1024]{1,0:T(8,128)(2,1)S(1)} %get-tuple-element.185), channel_id=1, source_target_pairs={{0,16},{4,20},{8,24},{12,28},{16,0},{20,4},{24,8},{28,12},{1,17},{... | collective-permute-start | bytes 589832 | tf_op jit(solution)/shard_map/ppermute | solution.py:480
  83.1 1.0 enc_grads_first.1
  84.1 1.2 %collective-permute-done.23.got = bf16[128,1024]{1,0:T(8,128)(2,1)S(1)} collective-permute-done((bf16[128,1024]{1,0:T(8,128)(2,1)S(1)}, bf16[128,1024]{1,0:T(8,128)(2,1)S(1)}, u32[]{:S(2)}, u32[]{:S(2)}) %collective-permute-start.23) | collective-permute-done | bytes 262176 | tf_op jit(solution)/shard_map/ppermute | solution.py:477
  85.7 0.5 collective-permute-start.28
  86.2 2.2 %collective-permute-done.29.refs_1_ = bf16[96,1024]{1,0:T(8,128)(2,1)S(1)} collective-permute-done((bf16[96,1024]{1,0:T(8,128)(2,1)S(1)}, bf16[96,1024]{1,0:T(8,128)(2,1)S(1)}, u32[]{:S(2)}, u32[]{:S(2)}) %collective-permute-start.29) | collective-permute-done | bytes 196640 | tf_op jit(solution)/shard_map/ppermute | solution.py:480
  88.4 0.5 enc_grad1_second.1
  89.0 1.7 %collective-permute-start.30 = (bf16[4,128,256]{2,1,0:T(8,128)(2,1)S(1)}, bf16[4,128,256]{2,1,0:T(8,128)(2,1)S(1)}, u32[]{:S(2)}, u32[]{:S(2)}) collective-permute-start(bf16[4,128,256]{2,1,0:T(8,128)(2,1)S(1)} %get-tuple-element.191), channel_id=1, source_target_pairs={{0,16},{4,20},{8,24},{12,28},{16,0},{20,4},{24,8},{28,12},{1,17},{... | collective-permute-start | bytes 786440 | tf_op jit(solution)/shard_map/ppermute | solution.py:480
  90.6 0.9 enc_grad0_second.1
  91.7 2.9 %collective-permute-start.32 = (bf16[96,1024]{1,0:T(8,128)(2,1)S(1)}, bf16[96,1024]{1,0:T(8,128)(2,1)S(1)}, u32[]{:S(2)}, u32[]{:S(2)}) collective-permute-start(bf16[96,1024]{1,0:T(8,128)(2,1)S(1)} %back_pick.2), channel_id=1, source_target_pairs={{0,8},{4,12},{8,0},{12,4},{16,24},{20,28},{24,16},{28,20},{1,9},{5... | collective-permute-start | bytes 589832 | tf_op jit(solution)/shard_map/ppermute | solution.py:480
  94.6 1.9 %collective-permute-done.30.got = bf16[4,128,256]{2,1,0:T(8,128)(2,1)S(1)} collective-permute-done((bf16[4,128,256]{2,1,0:T(8,128)(2,1)S(1)}, bf16[4,128,256]{2,1,0:T(8,128)(2,1)S(1)}, u32[]{:S(2)}, u32[]{:S(2)}) %collective-permute-start.30) | collective-permute-done | bytes 262176 | tf_op jit(solution)/shard_map/ppermute | solution.py:480
  96.8 0.4 ffn_out_far.1
  97.2 0.6 collective-permute-start.37
  97.8 6.4 %collective-permute-done.34.got = bf16[4,128,256]{2,1,0:T(8,128)(2,1)S(1)} collective-permute-done((bf16[4,128,256]{2,1,0:T(8,128)(2,1)S(1)}, bf16[4,128,256]{2,1,0:T(8,128)(2,1)S(1)}, u32[]{:S(2)}, u32[]{:S(2)}) %collective-permute-start.34) | collective-permute-done | bytes 262176 | tf_op jit(solution)/shard_map/ppermute | solution.py:480
  104.3 0.7 collective-permute-start.35
  105.0 0.9 collective-permute-done.31.got
  106.2 3.1 %collective-permute-done.35.got = bf16[2,128,256]{2,1,0:T(8,128)(2,1)S(1)} collective-permute-done((bf16[2,128,256]{2,1,0:T(8,128)(2,1)S(1)}, bf16[2,128,256]{2,1,0:T(8,128)(2,1)S(1)}, u32[]{:S(2)}, u32[]{:S(2)}) %collective-permute-start.35) | collective-permute-done | bytes 131104 | tf_op jit(solution)/shard_map/ppermute | solution.py:480
  109.3 0.6 collective-permute-start.36
  110.0 2.4 %collective-permute-start.33 = (bf16[1,128,256]{2,1,0:T(8,128)(2,1)S(1)}, bf16[1,128,256]{2,1,0:T(8,128)(2,1)S(1)}, u32[]{:S(2)}, u32[]{:S(2)}) collective-permute-start(bf16[1,128,256]{2,1,0:T(8,128)(2,1)S(1)} %get-tuple-element.197), channel_id=1, source_target_pairs={{0,8},{4,12},{8,0},{12,4},{16,24},{20,28},{24,16},{28,20},{1,9},{5... | collective-permute-start | bytes 196616 | tf_op jit(solution)/shard_map/ppermute | solution.py:480
  112.4 1.2 ffn_out_own.1
  113.6 1.0 back_recv.1
  114.5 0.4 collective-permute-done.36.got0
  115.0 0.7 collective-permute-done.33.got1
  115.7 0.7 finish.1
  (65 shorter events, 5.5 us)
Async XLA Ops:
  0.6 7.9 %collective-permute-start = (bf16[2,1024,512]{2,1,0:T(8,128)(2,1)}, bf16[2,1024,512]{2,1,0:T(8,128)(2,1)S(1)}, u32[]{:S(2)}, u32[]{:S(2)}) collective-permute-start(bf16[2,1024,512]{2,1,0:T(8,128)(2,1)} %in_a.3), channel_id=1, source_target_pairs={{0,1},{1,0},{2,3},{3,2},{4,5},{5,4},{6,7},{7,6},{8,9},{9,8},{10,11... | collective-permute-start | bytes 6291464 | tf_op jit(solution)/shard_map/ppermute | solution.py:474
  1.1 7.4 %collective-permute-start.1 = (bf16[512,1024]{1,0:T(8,128)(2,1)}, bf16[512,1024]{1,0:T(8,128)(2,1)S(1)}, u32[]{:S(2)}, u32[]{:S(2)}) collective-permute-start(bf16[512,1024]{1,0:T(8,128)(2,1)} %w_a.3), channel_id=1, source_target_pairs={{0,1},{1,0},{2,3},{3,2},{4,5},{5,4},{6,7},{7,6},{8,9},{9,8},{10,11... | collective-permute-start | bytes 3145736 | tf_op jit(solution)/shard_map/ppermute | solution.py:474
  1.9 0.9 copy-start.7
  2.9 20.2 %copy-start = (bf16[2,1024,1024]{2,1,0:T(8,128)(2,1)S(1)}, bf16[2,1024,1024]{2,1,0:T(8,128)(2,1)}, u32[]{:S(2)}) copy-start(bf16[2,1024,1024]{2,1,0:T(8,128)(2,1)} %refs_6_.1) | copy-start | bytes 12582916
  2.9 20.2 %copy-start.1 = (bf16[4,1024,256]{2,1,0:T(8,128)(2,1)S(1)}, bf16[4,1024,256]{2,1,0:T(8,128)(2,1)}, u32[]{:S(2)}) copy-start(bf16[4,1024,256]{2,1,0:T(8,128)(2,1)} %w_in.5) | copy-start | bytes 6291460
  3.2 10.6 %collective-permute-start.2 = (bf16[24,1152]{1,0:T(8,128)(2,1)S(1)}, bf16[24,1152]{1,0:T(8,128)(2,1)S(1)}, u32[]{:S(2)}, u32[]{:S(2)}) collective-permute-start(bf16[24,1152]{1,0:T(8,128)(2,1)S(1)} %get-tuple-element.110), channel_id=1, source_target_pairs={{0,8},{4,12},{8,0},{12,4},{16,24},{20,28},{24,16},{28,20},{1,9},{5... | collective-permute-start | bytes 165896 | tf_op jit(solution)/shard_map/ppermute | solution.py:480
  7.3 8.8 %collective-permute-start.3 = (bf16[24,1152]{1,0:T(8,128)(2,1)S(1)}, bf16[24,1152]{1,0:T(8,128)(2,1)S(1)}, u32[]{:S(2)}, u32[]{:S(2)}) collective-permute-start(bf16[24,1152]{1,0:T(8,128)(2,1)S(1)} %get-tuple-element.111), channel_id=1, source_target_pairs={{0,24},{4,28},{8,16},{12,20},{16,8},{20,12},{24,0},{28,4},{1,25},{... | collective-permute-start | bytes 165896 | tf_op jit(solution)/shard_map/ppermute | solution.py:480
  8.6 7.8 %collective-permute-start.4 = (bf16[24,1152]{1,0:T(8,128)(2,1)S(1)}, bf16[24,1152]{1,0:T(8,128)(2,1)S(1)}, u32[]{:S(2)}, u32[]{:S(2)}) collective-permute-start(bf16[24,1152]{1,0:T(8,128)(2,1)S(1)} %get-tuple-element.118), channel_id=1, source_target_pairs={{0,12},{4,8},{8,4},{12,0},{16,28},{20,24},{24,20},{28,16},{1,13},{... | collective-permute-start | bytes 165896 | tf_op jit(solution)/shard_map/ppermute | solution.py:480
  12.2 7.0 %collective-permute-start.5 = (bf16[24,1152]{1,0:T(8,128)(2,1)S(1)}, bf16[24,1152]{1,0:T(8,128)(2,1)S(1)}, u32[]{:S(2)}, u32[]{:S(2)}) collective-permute-start(bf16[24,1152]{1,0:T(8,128)(2,1)S(1)} %get-tuple-element.119), channel_id=1, source_target_pairs={{0,28},{4,24},{8,20},{12,16},{16,12},{20,8},{24,4},{28,0},{1,29},{... | collective-permute-start | bytes 165896 | tf_op jit(solution)/shard_map/ppermute | solution.py:480
  12.8 6.4 %collective-permute-start.6 = (bf16[24,1152]{1,0:T(8,128)(2,1)S(1)}, bf16[24,1152]{1,0:T(8,128)(2,1)S(1)}, u32[]{:S(2)}, u32[]{:S(2)}) collective-permute-start(bf16[24,1152]{1,0:T(8,128)(2,1)S(1)} %get-tuple-element.120), channel_id=1, source_target_pairs={{0,16},{4,20},{8,24},{12,28},{16,0},{20,4},{24,8},{28,12},{1,17},{... | collective-permute-start | bytes 165896 | tf_op jit(solution)/shard_map/ppermute | solution.py:480
  13.9 5.3 %collective-permute-start.7 = (bf16[24,1152]{1,0:T(8,128)(2,1)S(1)}, bf16[24,1152]{1,0:T(8,128)(2,1)S(1)}, u32[]{:S(2)}, u32[]{:S(2)}) collective-permute-start(bf16[24,1152]{1,0:T(8,128)(2,1)S(1)} %get-tuple-element.121), channel_id=1, source_target_pairs={{0,4},{4,0},{8,12},{12,8},{16,20},{20,16},{24,28},{28,24},{1,5},{5... | collective-permute-start | bytes 165896 | tf_op jit(solution)/shard_map/ppermute | solution.py:480
  16.1 5.1 %collective-permute-start.8 = (bf16[24,1152]{1,0:T(8,128)(2,1)S(1)}, bf16[24,1152]{1,0:T(8,128)(2,1)S(1)}, u32[]{:S(2)}, u32[]{:S(2)}) collective-permute-start(bf16[24,1152]{1,0:T(8,128)(2,1)S(1)} %get-tuple-element.122), channel_id=1, source_target_pairs={{0,20},{4,16},{8,28},{12,24},{16,4},{20,0},{24,12},{28,8},{1,21},{... | collective-permute-start | bytes 165896 | tf_op jit(solution)/shard_map/ppermute | solution.py:480
  21.4 8.8 %copy-start.3 = (bf16[256,1024]{1,0:T(8,128)(2,1)S(1)}, bf16[256,1024]{1,0:T(8,128)(2,1)}, u32[]{:S(2)}) copy-start(bf16[256,1024]{1,0:T(8,128)(2,1)} %w_out.5) | copy-start | bytes 1572868
  21.4 9.3 %copy-start.5 = (bf16[1,128,1024]{2,1,0:T(8,128)(2,1)S(1)}, bf16[1,128,1024]{2,1,0:T(8,128)(2,1)}, u32[]{:S(2)}) copy-start(bf16[1,128,1024]{2,1,0:T(8,128)(2,1)} %param.19) | copy-start | bytes 786436
  21.4 1.7 %collective-permute-start.10 = (bf16[128,1024]{1,0:T(8,128)(2,1)S(1)}, bf16[128,1024]{1,0:T(8,128)(2,1)S(1)}, u32[]{:S(2)}, u32[]{:S(2)}) collective-permute-start(bf16[128,1024]{1,0:T(8,128)(2,1)S(1)} %get-tuple-element.123.refs_0_.refs_3_), channel_id=1, source_target_pairs={{0,1},{1,0},{2,3},{3,2},{4,5},{5,4},{6,7},{7,6},{8,9},{9,8},{10,11... | collective-permute-start | bytes 786440 | tf_op jit(solution)/shard_map/ppermute | solution.py:474
  21.5 8.7 %collective-permute-start.9 = (bf16[128,1024]{1,0:T(8,128)(2,1)S(1)}, bf16[128,1024]{1,0:T(8,128)(2,1)S(1)}, u32[]{:S(2)}, u32[]{:S(2)}) collective-permute-start(bf16[128,1024]{1,0:T(8,128)(2,1)S(1)} %get-tuple-element.123.refs_0_.refs_3_), channel_id=1, source_target_pairs={{0,2},{1,3},{2,0},{3,1},{4,6},{5,7},{6,4},{7,5},{8,10},{9,11},{10,... | collective-permute-start | bytes 786440 | tf_op jit(solution)/shard_map/ppermute | solution.py:477
  30.2 3.4 %copy-start.6 = (s32[1,512]{1,0:T(1,128)S(1)}, s32[1,512]{1,0:T(1,128)}, u32[]{:S(2)}) copy-start(s32[1,512]{1,0:T(1,128)} %param.13) | copy-start | bytes 6148
  30.2 7.4 %collective-permute-start.13 = (bf16[256,1024]{1,0:T(8,128)(2,1)S(1)}, bf16[256,1024]{1,0:T(8,128)(2,1)S(1)}, u32[]{:S(2)}, u32[]{:S(2)}) collective-permute-start(bf16[256,1024]{1,0:T(8,128)(2,1)S(1)} %copy-done.3), channel_id=1, source_target_pairs={{0,1},{1,0},{2,3},{3,2},{4,5},{5,4},{6,7},{7,6},{8,9},{9,8},{10,11... | collective-permute-start | bytes 1572872 | tf_op jit(solution)/shard_map/ppermute | solution.py:474
  30.2 3.4 %collective-permute-start.11 = (bf16[128,1024]{1,0:T(8,128)(2,1)S(1)}, bf16[128,1024]{1,0:T(8,128)(2,1)S(1)}, u32[]{:S(2)}, u32[]{:S(2)}) collective-permute-start(bf16[128,1024]{1,0:T(8,128)(2,1)S(1)} %collective-permute-done.9.refs_0_.refs_3_), channel_id=1, source_target_pairs={{0,1},{1,0},{2,3},{3,2},{4,5},{5,4},{6,7},{7,6},{8,9},{9,8},{10,11... | collective-permute-start | bytes 786440 | tf_op jit(solution)/shard_map/ppermute | solution.py:474
  30.7 8.3 %collective-permute-start.14 = (bf16[128,1024]{1,0:T(8,128)(2,1)S(1)}, bf16[128,1024]{1,0:T(8,128)(2,1)S(1)}, u32[]{:S(2)}, u32[]{:S(2)}) collective-permute-start(bf16[128,1024]{1,0:T(8,128)(2,1)S(1)} %bitcast.5), channel_id=1, source_target_pairs={{0,2},{1,3},{2,0},{3,1},{4,6},{5,7},{6,4},{7,5},{8,10},{9,11},{10,... | collective-permute-start | bytes 786440 | tf_op jit(solution)/shard_map/ppermute | solution.py:477
  36.2 11.2 %copy-start.2 = (bf16[512,1024]{1,0:T(8,128)(2,1)S(1)}, bf16[512,1024]{1,0:T(8,128)(2,1)}, u32[]{:S(2)}) copy-start(bf16[512,1024]{1,0:T(8,128)(2,1)} %w_a.3) | copy-start | bytes 3145732
  36.2 11.2 %copy-start.4 = (bf16[2,1024,512]{2,1,0:T(8,128)(2,1)S(1)}, bf16[2,1024,512]{2,1,0:T(8,128)(2,1)}, u32[]{:S(2)}) copy-start(bf16[2,1024,512]{2,1,0:T(8,128)(2,1)} %in_a.3) | copy-start | bytes 6291460
  36.2 1.4 %collective-permute-start.12 = (bf16[256,256]{1,0:T(8,128)(2,1)S(1)}, bf16[256,256]{1,0:T(8,128)(2,1)S(1)}, u32[]{:S(2)}, u32[]{:S(2)}) collective-permute-start(bf16[256,256]{1,0:T(8,128)(2,1)S(1)} %get-tuple-element.132), channel_id=1, source_target_pairs={{0,1},{1,0},{2,3},{3,2},{4,5},{5,4},{6,7},{7,6},{8,9},{9,8},{10,11... | collective-permute-start | bytes 393224 | tf_op jit(solution)/shard_map/ppermute | solution.py:474
  37.9 9.2 %collective-permute-start.16 = (bf16[128,1024]{1,0:T(8,128)(2,1)S(1)}, bf16[128,1024]{1,0:T(8,128)(2,1)S(1)}, u32[]{:S(2)}, u32[]{:S(2)}) collective-permute-start(bf16[128,1024]{1,0:T(8,128)(2,1)S(1)} %attn_out_far.1.part), channel_id=1, source_target_pairs={{0,2},{1,3},{2,0},{3,1},{4,6},{5,7},{6,4},{7,5},{8,10},{9,11},{10,... | collective-permute-start | bytes 786440 | tf_op jit(solution)/shard_map/ppermute | solution.py:477
  39.0 13.0 %collective-permute-start.15 = (bf16[128,1024]{1,0:T(8,128)(2,1)S(1)}, bf16[128,1024]{1,0:T(8,128)(2,1)S(1)}, u32[]{:S(2)}, u32[]{:S(2)}) collective-permute-start(bf16[128,1024]{1,0:T(8,128)(2,1)S(1)} %attn_out_own.1.part), channel_id=1, source_target_pairs={{0,2},{1,3},{2,0},{3,1},{4,6},{5,7},{6,4},{7,5},{8,10},{9,11},{10,... | collective-permute-start | bytes 786440 | tf_op jit(solution)/shard_map/ppermute | solution.py:477
  52.0 9.2 %collective-permute-start.18 = (bf16[128,1024]{1,0:T(8,128)(2,1)S(1)}, bf16[128,1024]{1,0:T(8,128)(2,1)S(1)}, u32[]{:S(2)}, u32[]{:S(2)}) collective-permute-start(bf16[128,1024]{1,0:T(8,128)(2,1)S(1)} %get-tuple-element.141.back), channel_id=1, source_target_pairs={{0,2},{1,3},{2,0},{3,1},{4,6},{5,7},{6,4},{7,5},{8,10},{9,11},{10,... | collective-permute-start | bytes 786440 | tf_op jit(solution)/shard_map/ppermute | solution.py:477
  55.6 9.6 %collective-permute-start.17 = (bf16[128,1024]{1,0:T(8,128)(2,1)S(1)}, bf16[128,1024]{1,0:T(8,128)(2,1)S(1)}, u32[]{:S(2)}, u32[]{:S(2)}) collective-permute-start(bf16[128,1024]{1,0:T(8,128)(2,1)S(1)} %get-tuple-element.146.back), channel_id=1, source_target_pairs={{0,2},{1,3},{2,0},{3,1},{4,6},{5,7},{6,4},{7,5},{8,10},{9,11},{10,... | collective-permute-start | bytes 786440 | tf_op jit(solution)/shard_map/ppermute | solution.py:477
  61.5 1.4 %collective-permute-start.19 = (bf16[64,1024]{1,0:T(8,128)(2,1)S(1)}, bf16[64,1024]{1,0:T(8,128)(2,1)S(1)}, u32[]{:S(2)}, u32[]{:S(2)}) collective-permute-start(bf16[64,1024]{1,0:T(8,128)(2,1)S(1)} %get-tuple-element.149), channel_id=1, source_target_pairs={{0,1},{1,0},{2,3},{3,2},{4,5},{5,4},{6,7},{7,6},{8,9},{9,8},{10,11... | collective-permute-start | bytes 393224 | tf_op jit(solution)/shard_map/ppermute | solution.py:474
  61.6 1.5 %collective-permute-start.20 = (bf16[64,1024]{1,0:T(8,128)(2,1)S(1)}, bf16[64,1024]{1,0:T(8,128)(2,1)S(1)}, u32[]{:S(2)}, u32[]{:S(2)}) collective-permute-start(bf16[64,1024]{1,0:T(8,128)(2,1)S(1)} %get-tuple-element.150), channel_id=1, source_target_pairs={{0,1},{1,0},{2,3},{3,2},{4,5},{5,4},{6,7},{7,6},{8,9},{9,8},{10,11... | collective-permute-start | bytes 393224 | tf_op jit(solution)/shard_map/ppermute | solution.py:474
  65.4 1.6 %collective-permute-start.21 = (bf16[128,1024]{1,0:T(8,128)(2,1)S(1)}, bf16[128,1024]{1,0:T(8,128)(2,1)S(1)}, u32[]{:S(2)}, u32[]{:S(2)}) collective-permute-start(bf16[128,1024]{1,0:T(8,128)(2,1)S(1)} %resid_back.1.first.d_resid), channel_id=1, source_target_pairs={{0,1},{1,0},{2,3},{3,2},{4,5},{5,4},{6,7},{7,6},{8,9},{9,8},{10,11... | collective-permute-start | bytes 786440 | tf_op jit(solution)/shard_map/ppermute | solution.py:474
  69.0 2.0 %collective-permute-start.22 = (bf16[256,1024]{1,0:T(8,128)(2,1)S(1)}, bf16[256,1024]{1,0:T(8,128)(2,1)S(1)}, u32[]{:S(2)}, u32[]{:S(2)}) collective-permute-start(bf16[256,1024]{1,0:T(8,128)(2,1)S(1)} %get-tuple-element.168), channel_id=1, source_target_pairs={{0,1},{1,0},{2,3},{3,2},{4,5},{5,4},{6,7},{7,6},{8,9},{9,8},{10,11... | collective-permute-start | bytes 1572872 | tf_op jit(solution)/shard_map/ppermute | solution.py:474
  71.1 9.2 %collective-permute-start.24 = (bf16[128,1024]{1,0:T(8,128)(2,1)S(1)}, bf16[128,1024]{1,0:T(8,128)(2,1)S(1)}, u32[]{:S(2)}, u32[]{:S(2)}) collective-permute-start(bf16[128,1024]{1,0:T(8,128)(2,1)S(1)} %get-tuple-element.169.part), channel_id=1, source_target_pairs={{0,2},{1,3},{2,0},{3,1},{4,6},{5,7},{6,4},{7,5},{8,10},{9,11},{10,... | collective-permute-start | bytes 786440 | tf_op jit(solution)/shard_map/ppermute | solution.py:477
  71.7 13.6 %collective-permute-start.23 = (bf16[128,1024]{1,0:T(8,128)(2,1)S(1)}, bf16[128,1024]{1,0:T(8,128)(2,1)S(1)}, u32[]{:S(2)}, u32[]{:S(2)}) collective-permute-start(bf16[128,1024]{1,0:T(8,128)(2,1)S(1)} %get-tuple-element.170.part), channel_id=1, source_target_pairs={{0,2},{1,3},{2,0},{3,1},{4,6},{5,7},{6,4},{7,5},{8,10},{9,11},{10,... | collective-permute-start | bytes 786440 | tf_op jit(solution)/shard_map/ppermute | solution.py:477
  80.6 2.5 %collective-permute-start.25 = (bf16[64,1024]{1,0:T(8,128)(2,1)S(1)}, bf16[64,1024]{1,0:T(8,128)(2,1)S(1)}, u32[]{:S(2)}, u32[]{:S(2)}) collective-permute-start(bf16[64,1024]{1,0:T(8,128)(2,1)S(1)} %get-tuple-element.172), channel_id=1, source_target_pairs={{0,1},{1,0},{2,3},{3,2},{4,5},{5,4},{6,7},{7,6},{8,9},{9,8},{10,11... | collective-permute-start | bytes 393224 | tf_op jit(solution)/shard_map/ppermute | solution.py:474
  80.7 2.4 %collective-permute-start.26 = (bf16[64,1024]{1,0:T(8,128)(2,1)S(1)}, bf16[64,1024]{1,0:T(8,128)(2,1)S(1)}, u32[]{:S(2)}, u32[]{:S(2)}) collective-permute-start(bf16[64,1024]{1,0:T(8,128)(2,1)S(1)} %get-tuple-element.173), channel_id=1, source_target_pairs={{0,1},{1,0},{2,3},{3,2},{4,5},{5,4},{6,7},{7,6},{8,9},{9,8},{10,11... | collective-permute-start | bytes 393224 | tf_op jit(solution)/shard_map/ppermute | solution.py:474
  81.5 7.0 %collective-permute-start.29 = (bf16[96,1024]{1,0:T(8,128)(2,1)S(1)}, bf16[96,1024]{1,0:T(8,128)(2,1)S(1)}, u32[]{:S(2)}, u32[]{:S(2)}) collective-permute-start(bf16[96,1024]{1,0:T(8,128)(2,1)S(1)} %get-tuple-element.185), channel_id=1, source_target_pairs={{0,16},{4,20},{8,24},{12,28},{16,0},{20,4},{24,8},{28,12},{1,17},{... | collective-permute-start | bytes 589832 | tf_op jit(solution)/shard_map/ppermute | solution.py:480
  85.6 2.8 %collective-permute-start.27 = (bf16[64,1024]{1,0:T(8,128)(2,1)S(1)}, bf16[64,1024]{1,0:T(8,128)(2,1)S(1)}, u32[]{:S(2)}, u32[]{:S(2)}) collective-permute-start(bf16[64,1024]{1,0:T(8,128)(2,1)S(1)} %get-tuple-element.182), channel_id=1, source_target_pairs={{0,1},{1,0},{2,3},{3,2},{4,5},{5,4},{6,7},{7,6},{8,9},{9,8},{10,11... | collective-permute-start | bytes 393224 | tf_op jit(solution)/shard_map/ppermute | solution.py:474
  85.7 2.7 %collective-permute-start.28 = (bf16[64,1024]{1,0:T(8,128)(2,1)S(1)}, bf16[64,1024]{1,0:T(8,128)(2,1)S(1)}, u32[]{:S(2)}, u32[]{:S(2)}) collective-permute-start(bf16[64,1024]{1,0:T(8,128)(2,1)S(1)} %get-tuple-element.183), channel_id=1, source_target_pairs={{0,1},{1,0},{2,3},{3,2},{4,5},{5,4},{6,7},{7,6},{8,9},{9,8},{10,11... | collective-permute-start | bytes 393224 | tf_op jit(solution)/shard_map/ppermute | solution.py:474
  89.0 7.5 %collective-permute-start.30 = (bf16[4,128,256]{2,1,0:T(8,128)(2,1)S(1)}, bf16[4,128,256]{2,1,0:T(8,128)(2,1)S(1)}, u32[]{:S(2)}, u32[]{:S(2)}) collective-permute-start(bf16[4,128,256]{2,1,0:T(8,128)(2,1)S(1)} %get-tuple-element.191), channel_id=1, source_target_pairs={{0,16},{4,20},{8,24},{12,28},{16,0},{20,4},{24,8},{28,12},{1,17},{... | collective-permute-start | bytes 786440 | tf_op jit(solution)/shard_map/ppermute | solution.py:480
  91.6 12.6 %collective-permute-start.34 = (bf16[4,128,256]{2,1,0:T(8,128)(2,1)S(1)}, bf16[4,128,256]{2,1,0:T(8,128)(2,1)S(1)}, u32[]{:S(2)}, u32[]{:S(2)}) collective-permute-start(bf16[4,128,256]{2,1,0:T(8,128)(2,1)S(1)} %get-tuple-element.201), channel_id=1, source_target_pairs={{0,4},{4,0},{8,12},{12,8},{16,20},{20,16},{24,28},{28,24},{1,5},{5... | collective-permute-start | bytes 786440 | tf_op jit(solution)/shard_map/ppermute | solution.py:480
  91.7 13.3 %collective-permute-start.32 = (bf16[96,1024]{1,0:T(8,128)(2,1)S(1)}, bf16[96,1024]{1,0:T(8,128)(2,1)S(1)}, u32[]{:S(2)}, u32[]{:S(2)}) collective-permute-start(bf16[96,1024]{1,0:T(8,128)(2,1)S(1)} %back_pick.2), channel_id=1, source_target_pairs={{0,8},{4,12},{8,0},{12,4},{16,24},{20,28},{24,16},{28,20},{1,9},{5... | collective-permute-start | bytes 589832 | tf_op jit(solution)/shard_map/ppermute | solution.py:480
  96.5 9.3 %collective-permute-start.31 = (bf16[2,128,256]{2,1,0:T(8,128)(2,1)S(1)}, bf16[2,128,256]{2,1,0:T(8,128)(2,1)S(1)}, u32[]{:S(2)}, u32[]{:S(2)}) collective-permute-start(bf16[2,128,256]{2,1,0:T(8,128)(2,1)S(1)} %get-tuple-element.193), channel_id=1, source_target_pairs={{0,4},{4,0},{8,12},{12,8},{16,20},{20,16},{24,28},{28,24},{1,5},{5... | collective-permute-start | bytes 393224 | tf_op jit(solution)/shard_map/ppermute | solution.py:480
  97.2 15.2 %collective-permute-start.37 = (bf16[128,1024]{1,0:T(8,128)(2,1)S(1)}, bf16[128,1024]{1,0:T(8,128)(2,1)S(1)}, u32[]{:S(2)}, u32[]{:S(2)}) collective-permute-start(bf16[128,1024]{1,0:T(8,128)(2,1)S(1)} %ffn_out_far.1), channel_id=1, source_target_pairs={{0,2},{1,3},{2,0},{3,1},{4,6},{5,7},{6,4},{7,5},{8,10},{9,11},{10,... | collective-permute-start | bytes 786440 | tf_op jit(solution)/shard_map/ppermute | solution.py:477
  104.3 5.0 %collective-permute-start.35 = (bf16[2,128,256]{2,1,0:T(8,128)(2,1)S(1)}, bf16[2,128,256]{2,1,0:T(8,128)(2,1)S(1)}, u32[]{:S(2)}, u32[]{:S(2)}) collective-permute-start(bf16[2,128,256]{2,1,0:T(8,128)(2,1)S(1)} %get-tuple-element.203), channel_id=1, source_target_pairs={{0,16},{4,20},{8,24},{12,28},{16,0},{20,4},{24,8},{28,12},{1,17},{... | collective-permute-start | bytes 393224 | tf_op jit(solution)/shard_map/ppermute | solution.py:480
  105.9 7.7 %collective-permute-start.38 = (bf16[96,1024]{1,0:T(8,128)(2,1)S(1)}, bf16[96,1024]{1,0:T(8,128)(2,1)S(1)}, u32[]{:S(2)}, u32[]{:S(2)}) collective-permute-start(bf16[96,1024]{1,0:T(8,128)(2,1)S(1)} %back_pick.3), channel_id=1, source_target_pairs={{0,4},{4,0},{8,12},{12,8},{16,20},{20,16},{24,28},{28,24},{1,5},{5... | collective-permute-start | bytes 589832 | tf_op jit(solution)/shard_map/ppermute | solution.py:480
  109.3 5.6 %collective-permute-start.36 = (bf16[1,128,256]{2,1,0:T(8,128)(2,1)S(1)}, bf16[1,128,256]{2,1,0:T(8,128)(2,1)S(1)}, u32[]{:S(2)}, u32[]{:S(2)}) collective-permute-start(bf16[1,128,256]{2,1,0:T(8,128)(2,1)S(1)} %get-tuple-element.204), channel_id=1, source_target_pairs={{0,8},{4,12},{8,0},{12,4},{16,24},{20,28},{24,16},{28,20},{1,9},{5... | collective-permute-start | bytes 196616 | tf_op jit(solution)/shard_map/ppermute | solution.py:480
  110.0 5.7 %collective-permute-start.33 = (bf16[1,128,256]{2,1,0:T(8,128)(2,1)S(1)}, bf16[1,128,256]{2,1,0:T(8,128)(2,1)S(1)}, u32[]{:S(2)}, u32[]{:S(2)}) collective-permute-start(bf16[1,128,256]{2,1,0:T(8,128)(2,1)S(1)} %get-tuple-element.197), channel_id=1, source_target_pairs={{0,8},{4,12},{8,0},{12,4},{16,24},{20,28},{24,16},{28,20},{1,9},{5... | collective-permute-start | bytes 196616 | tf_op jit(solution)/shard_map/ppermute | solution.py:480

commit v9 on v8

--- a/solution.py
+++ b/solution.py
@@ -43,6 +43,13 @@
 
 def joined(refs):
     return jnp.concatenate([r[...] for r in refs], axis=0)
+
+
+def store_halves(value, out, halves):
+    out[...] = value
+    rows = value.shape[0] // max(len(halves), 1)
+    for n, target in enumerate(halves):
+        target[...] = value[n * rows : (n + 1) * rows]
 
 
 def turned(row, rows):
@@ -103,22 +110,23 @@
 
 
 def route_recv(*refs):
-    gots, (rows_ref, hot_ref) = refs[:-2], refs[-2:]
+    gots, (rows_ref, hot_ref, *halves) = refs[:-4], refs[-4:]
     rows, width = rows_ref.shape
     got = jnp.concatenate([g[...].astype(F32) for g in gots], axis=0)
     lanes = lax.broadcasted_iota(jnp.int32, (got.shape[0], rows), 1) + 1
     hot = jnp.where(got[:, width:] == lanes.astype(F32), 1.0, 0.0).astype(BF16)
     hot_ref[...] = hot
-    rows_ref[...] = bf16(dot(hot, bf16(got[:, :width]), TN))
-
-
-def back_send(order, hot, d_packed, keep, send):
+    store_halves(bf16(dot(hot, bf16(got[:, :width]), TN)), rows_ref, halves)
+
+
+def back_send(order, bit, hot, d_packed, keep, send):
     groups = len(order)
     capacity = hot.shape[0] // groups
     big = dot(hot[...], d_packed[...])
     at = {k: n * capacity for n, k in enumerate(order)}
-    for target, first in ((keep, 0), (send, groups // 2)):
-        parts = [big[at[first + k] : at[first + k] + capacity] for k in range(groups // 2)]
+    for target, value in ((keep, 0), (send, bit)):
+        chosen = [k for k in range(groups) if k & bit == value]
+        parts = [big[at[k] : at[k] + capacity] for k in chosen]
         target[...] = bf16(jnp.concatenate(parts, axis=0))
 
 
@@ -159,10 +167,10 @@
 def encode_blocks(*refs):
     blocks, (enc, w_in, pre_ref, act_ref, packed_ref, proj_ref, pre_all) = refs[:-7], refs[-7:]
     rows = joined(blocks)
-    size = blocks[0].shape[0]
+    count, size = proj_ref.shape[1:3]
 
     def store(c, value):
-        for n in range(len(blocks)):
+        for n in range(count):
             proj_ref[c, n] = value[n * size : (n + 1) * size]
 
     packed = encode(rows, enc, w_in, pre_all, pre_ref, act_ref, store)
@@ -277,13 +285,6 @@
     units = w_a.shape[0]
     total = dot(hidden[:, :units], w_a[...]) + dot(hidden[:, units:], w_b[...])
     out[...] = bf16(resid[...].astype(F32) + total + got[...].astype(F32))
-
-
-def store_halves(value, out, halves):
-    out[...] = value
-    rows = value.shape[0] // max(len(halves), 1)
-    for n, target in enumerate(halves):
-        target[...] = value[n * rows : (n + 1) * rows]
 
 
 def resid_back(back, got, resid, d_out, out, *halves):
@@ -400,10 +401,11 @@
 
 
 def enc_grads_first(*refs):
-    cots, (act0_a, act0_b, act1, pre, enc, part1, part0) = refs[:-7], refs[-7:]
+    rows, (act1, pre, enc, part1, part0) = refs[:-5], refs[-5:]
+    cots, act0 = rows[: len(rows) // 2], rows[len(rows) // 2 :]
     cols = pre.shape[1]
     part1[...] = rows_term([act1], cot_columns(cots, cols))
-    part0[...] = rows_term([act0_a, act0_b], first_cot(cots, pre, enc))
+    part0[...] = rows_term(act0, first_cot(cots, pre, enc))
 
 
 def halve(bits, bit, total, keep, send):
@@ -499,15 +501,17 @@
     early = [crossed(sends[n], order[n]) for n in (1, 2)]
     ffn_in_near, ffn_out_near, *sends = tie(ffn_in_near, ffn_out_near, *sends)
     gots = [sends[0], *early] + [crossed(sends[n], order[n]) for n in range(3, groups)]
-    mine, hot = run(
+    pieces = 2
+    piece_b = like((rows_dev // pieces, width), BF16)
+    mine, hot, *halves = run(
         route_recv,
-        [row_b, like((groups * capacity, rows_dev), BF16)],
+        [row_b, like((groups * capacity, rows_dev), BF16)] + [piece_b] * pieces,
         gots,
         name="route_recv",
     )
 
     mine_far = far(mine)
-    mine_near = near(mine)
+    mine_near = [near(h) for h in halves]
 
     pair = 2 * rows_dev
     pre_a, act_a, packed, proj_a = run(
@@ -518,7 +522,7 @@
             row_b,
             like((comps, 2, rows_dev, cols), BF16),
         ],
-        [mine, mine_near, enc_weight, attn_in],
+        [mine, *mine_near, enc_weight, attn_in],
         [pltpu.VMEM((pair, width), F32)],
         name="encode_first",
     )
@@ -583,8 +587,6 @@
     hidden_far, back_far = feed(normed2_far, d_out_far, "ffn_far")
     got_back_own = far(back_far)
 
-    pieces = 2
-    piece_b = like((rows_dev // pieces, width), BF16)
     d_resid_far, *halves = run(
         resid_back,
         [row_b] + [piece_b] * pieces,
@@ -635,46 +637,29 @@
 
     cot_near = [near(h) for h in halves]
     half_rows = like((groups * capacity // 2, width), BF16)
+    group_bits = [1 << b for b in range(groups.bit_length() - 1)]
+    near_bit, pack_far, event_far = group_bits[0], group_bits[1 : packs.bit_length() - 1], group_bits[packs.bit_length() - 1 :]
+    back_bits = pack_far[::-1] + event_far[::-1] + [near_bit]
     kept, back = run(
-        functools.partial(back_send, order), [half_rows] * 2, [hot, d_packed], name="back_send"
-    )
-    back_got = crossed(back, groups // 2)
+        functools.partial(back_send, order, back_bits[0]), [half_rows] * 2, [hot, d_packed], name="back_send"
+    )
+    back_got = crossed(back, back_bits[0])
 
     part_f = like((width, cols), F32)
     part1, part0 = run(
         enc_grads_first,
         [part_f, part_f],
-        [d_packed, *cot_near, mine, mine_near, act_a, pre_a, enc_weight],
+        [d_packed, *cot_near, mine, *mine_near, act_a, pre_a, enc_weight],
         name="enc_grads_first",
     )
     got_far, part1, part0 = tie(got_far, part1, part0)
     cot_far, *cot_pieces = run(
         packed_back,
-        [row_b] + [piece_b] * pieces,
+        [row_b] + [like((rows_dev // 4, width), BF16)] * 4,
         [sum_far, got_far, packed_far, d_resid_far],
         name="packed_back_far",
     )
     cot_both = [near(piece) for piece in cot_pieces]
-    *cot_both, back_got = tie(*cot_both, back_got)
-    arrays = [kept, back_got]
-    held = {k: divmod(k, groups // 2) for k in range(groups)}
-
-    def send_back(bit):
-        moved = [k for k in range(groups) if k & bit]
-        (back,) = run(
-            functools.partial(back_pick, [held[k] for k in moved], capacity),
-            [half_rows],
-            arrays,
-            name="back_pick",
-        )
-        held.update({k: (len(arrays), n) for n, k in enumerate(moved)})
-        arrays.append(crossed(back, bit))
-
-    bit = groups // 4
-    while bit > 1:
-        send_back(bit)
-        bit //= 2
-
     cot_far, hidden_far = tie(cot_far, hidden_far)
     (out_far,) = run(
         ffn_out_far, [row_b], [hidden_far, ffn_out, ffn_out_near], name="ffn_out_far"
@@ -689,9 +674,8 @@
         shape = (2 ** (len(remaining) - 1), size, cols)
         return [like(shape, F32), like(shape, BF16)]
 
-    def reduce_over(stages, start, name, beside=None):
+    def reduce_over(stages, kept, send, name, beside=False):
         remaining = list(bits)
-        kept, send = start((tuple(remaining), stages[0]))
         got = crossed(send, 1 << stages[0])
         remaining.remove(stages[0])
         for bit in stages[1:]:
@@ -703,8 +687,8 @@
             )
             got = crossed(send, 1 << bit)
             remaining.remove(bit)
-            if beside is not None and bit == stages[1]:
-                got, beside[-1] = tie(got, beside[-1])
+            if beside and bit == stages[1]:
+                got, arrays[-1] = tie(got, arrays[-1])
         return kept, got
 
     def start1(setting):
@@ -725,9 +709,34 @@
             name="enc_grad0_second",
         )
 
-    kept1, got1 = reduce_over(event_bits + pack_bits, start1, "halve1_", arrays)
-    kept0, got0 = reduce_over(pack_bits[:1] + event_bits + pack_bits[1:], start0, "halve0_")
-    send_back(1)
+    kept1, send1 = start1((tuple(bits), event_bits[0]))
+    send1, part0 = tie(send1, part0)
+    part0, back_got = tie(part0, back_got)
+    kept0, send0 = start0((tuple(bits), pack_bits[0]))
+    arrays = [kept, back_got]
+    held = {}
+    for n, value in enumerate((0, back_bits[0])):
+        chosen = [k for k in range(groups) if k & back_bits[0] == value]
+        held.update({k: (n, at) for at, k in enumerate(chosen)})
+
+    def send_back(bit):
+        moved = [k for k in range(groups) if k & bit]
+        (back,) = run(
+            functools.partial(back_pick, [held[k] for k in moved], capacity),
+            [half_rows],
+            arrays,
+            name="back_pick",
+        )
+        held.update({k: (len(arrays), n) for n, k in enumerate(moved)})
+        arrays.append(crossed(back, bit))
+
+    for bit in back_bits[1:-1]:
+        send_back(bit)
+    kept1, got1 = reduce_over(event_bits + pack_bits, kept1, send1, "halve1_", True)
+    kept0, got0 = reduce_over(
+        pack_bits[:1] + event_bits + pack_bits[1:], kept0, send0, "halve0_"
+    )
+    send_back(back_bits[-1])
     back_places = [held[k] for k in range(groups)]
     got_out = far(out_far)
     (packed_out,) = run(

time: 117 us -> 115 us (0.983)
  waiting for transfers between devices: 51.8 us -> 47 us
  starting transfers between devices: 35.3 us -> 38.3 us
    ppermute x9, waiting for transfers between devices: 25.8 us -> 21.3 us  [far(): return lax.ppermute(value, 'tensor', [(i, i ^ 2) for i in range(tensors)])]
    ppermute x16, waiting for transfers between devices: 22.5 us -> 20.2 us  [crossed(): return lax.ppermute(value, group_axes, [(i, i ^ k) for i in range(groups)])]
    ppermute x16, starting transfers between devices: 21.7 us -> 23.8 us  [crossed(): return lax.ppermute(value, group_axes, [(i, i ^ k) for i in range(groups)])]
    ppermute x14 -> x17, waiting for transfers between devices: 3.49 us -> 5.39 us  [near(): return lax.ppermute(value, 'tensor', [(i, i ^ 1) for i in range(tensors)])]
    ppermute x14 -> x17, starting transfers between devices: 3.68 us -> 4.63 us  [near(): return lax.ppermute(value, 'tensor', [(i, i ^ 1) for i in range(tensors)])]
  transfers between devices with their start and end apart: 39 -> 42, of which waited for: 22 -> 27; matrix products, arithmetic and copies ran while one was open for 1% -> 1% of each run, Pallas kernels for 20% -> 20%
where the time goes in v9:
time: 115 us
  waiting for transfers between devices  47 us (41%)
  starting transfers between devices  38.3 us (33%)
  Pallas kernels  26.7 us (23%)
    pallas_call x34, Pallas kernels, run(): pl.pallas_call(body, out_shape=list(outs), in_specs=[pl.BlockSpec(memory_...  26.7 us
    ppermute x16, starting transfers between devices, crossed(): return lax.ppermute(value, group_axes, [(i, i ^ k) for i in range(groups)])  23.8 us
    ppermute x9, waiting for transfers between devices, far(): return lax.ppermute(value, 'tensor', [(i, i ^ 2) for i in range(tensors)])  21.3 us
    ppermute x16, waiting for transfers between devices, crossed(): return lax.ppermute(value, group_axes, [(i, i ^ k) for i in range(groups)])  20.2 us
    ppermute x9, starting transfers between devices, far(): return lax.ppermute(value, 'tensor', [(i, i ^ 2) for i in range(tensors)])  9.9 us
    ppermute x17, waiting for transfers between devices, near(): return lax.ppermute(value, 'tensor', [(i, i ^ 1) for i in range(tensors)])  5.39 us
    ppermute x17, starting transfers between devices, near(): return lax.ppermute(value, 'tensor', [(i, i ^ 1) for i in range(tensors)])  4.63 us
  transfers between devices with their start and end apart: 42, of which 27 were waited for; matrix products, arithmetic and copies ran while one was open for 1% of the time, Pallas kernels for 20%

profile of v9, /device:TPU:0, one launch (start us, length us, event | category | flops | bytes accessed | tf_op | source)
XLA Modules:
  0.0 114.6 jit_solution(6479011034192507577)
XLA Ops:
  0.6 0.5 collective-permute-start
  1.2 0.7 add_bitcast_fusion.code
  1.9 0.9 copy-done.7
  3.2 4.1 %collective-permute-start.2 = (bf16[24,1152]{1,0:T(8,128)(2,1)S(1)}, bf16[24,1152]{1,0:T(8,128)(2,1)S(1)}, u32[]{:S(2)}, u32[]{:S(2)}) collective-permute-start(bf16[24,1152]{1,0:T(8,128)(2,1)S(1)} %get-tuple-element.115), channel_id=1, source_target_pairs={{0,8},{4,12},{8,0},{12,4},{16,24},{20,28},{24,16},{28,20},{1,9},{5... | collective-permute-start | bytes 165896 | tf_op jit(solution)/shard_map/ppermute | solution.py:482
  7.3 1.3 %collective-permute-start.3 = (bf16[24,1152]{1,0:T(8,128)(2,1)S(1)}, bf16[24,1152]{1,0:T(8,128)(2,1)S(1)}, u32[]{:S(2)}, u32[]{:S(2)}) collective-permute-start(bf16[24,1152]{1,0:T(8,128)(2,1)S(1)} %get-tuple-element.116), channel_id=1, source_target_pairs={{0,24},{4,28},{8,16},{12,20},{16,8},{20,12},{24,0},{28,4},{1,25},{... | collective-permute-start | bytes 165896 | tf_op jit(solution)/shard_map/ppermute | solution.py:482
  8.6 3.6 %collective-permute-start.4 = (bf16[24,1152]{1,0:T(8,128)(2,1)S(1)}, bf16[24,1152]{1,0:T(8,128)(2,1)S(1)}, u32[]{:S(2)}, u32[]{:S(2)}) collective-permute-start(bf16[24,1152]{1,0:T(8,128)(2,1)S(1)} %get-tuple-element.123), channel_id=1, source_target_pairs={{0,12},{4,8},{8,4},{12,0},{16,28},{20,24},{24,20},{28,16},{1,13},{... | collective-permute-start | bytes 165896 | tf_op jit(solution)/shard_map/ppermute | solution.py:482
  12.2 0.6 collective-permute-start.5
  12.8 1.1 collective-permute-start.6
  13.9 2.2 %collective-permute-done.3.refs_2_ = bf16[24,1152]{1,0:T(8,128)(2,1)S(1)} collective-permute-done((bf16[24,1152]{1,0:T(8,128)(2,1)S(1)}, bf16[24,1152]{1,0:T(8,128)(2,1)S(1)}, u32[]{:S(2)}, u32[]{:S(2)}) %collective-permute-start.3) | collective-permute-done | bytes 55328 | tf_op jit(solution)/shard_map/ppermute | solution.py:482
  16.4 2.8 %collective-permute-done.5.refs_4_ = bf16[24,1152]{1,0:T(8,128)(2,1)S(1)} collective-permute-done((bf16[24,1152]{1,0:T(8,128)(2,1)S(1)}, bf16[24,1152]{1,0:T(8,128)(2,1)S(1)}, u32[]{:S(2)}, u32[]{:S(2)}) %collective-permute-start.5) | collective-permute-done | bytes 55328 | tf_op jit(solution)/shard_map/ppermute | solution.py:482
  19.2 1.9 %collective-permute-done.8.refs_7_ = bf16[24,1152]{1,0:T(8,128)(2,1)S(1)} collective-permute-done((bf16[24,1152]{1,0:T(8,128)(2,1)S(1)}, bf16[24,1152]{1,0:T(8,128)(2,1)S(1)}, u32[]{:S(2)}, u32[]{:S(2)}) %collective-permute-start.8) | collective-permute-done | bytes 55328 | tf_op jit(solution)/shard_map/ppermute | solution.py:482
  21.4 1.6 %collective-permute-start.9 = (bf16[128,1024]{1,0:T(8,128)(2,1)S(1)}, bf16[128,1024]{1,0:T(8,128)(2,1)S(1)}, u32[]{:S(2)}, u32[]{:S(2)}) collective-permute-start(bf16[128,1024]{1,0:T(8,128)(2,1)S(1)} %get-tuple-element.128.refs_0_.refs_3_), channel_id=1, source_target_pairs={{0,2},{1,3},{2,0},{3,1},{4,6},{5,7},{6,4},{7,5},{8,10},{9,11},{10,... | collective-permute-start | bytes 786440 | tf_op jit(solution)/shard_map/ppermute | solution.py:479
  23.0 0.5 collective-permute-start.11
  23.5 0.8 collective-permute-done.10.refs_1_.refs_4_
  24.5 2.2 %encode_first.1 = (f32[256,256]{1,0:T(8,128)S(1)}, bf16[256,1024]{1,0:T(8,128)(2,1)S(1)}, bf16[128,1024]{1,0:T(8,128)(2,1)S(1)}, bf16[4,2,128,256]{3,2,1,0:T(8,128)(2,1)S(1)}) custom-call(bf16[128,1024]{1,0:T(8,128)(2,1)S(1)} %get-tuple-element.128.refs_0_.refs_3_, bf16[64,1024]{1,0:T(8,128)(2,1)S(1)} %collective-permute-done.10.refs_1_.refs_4_, ...), custom_call_target="tpu_custom_call" | custom-call | tf_op jit(solution)/shard_map/encode_first/pallas_call | solution.py:64
  26.8 1.1 collective-permute-done.9.refs_0_.refs_5_
  27.8 0.5 collective-permute-start.12
  28.3 1.5 %collective-permute-start.15 = (bf16[128,1024]{1,0:T(8,128)(2,1)S(1)}, bf16[128,1024]{1,0:T(8,128)(2,1)S(1)}, u32[]{:S(2)}, u32[]{:S(2)}) collective-permute-start(bf16[128,1024]{1,0:T(8,128)(2,1)S(1)} %bitcast.5), channel_id=1, source_target_pairs={{0,2},{1,3},{2,0},{3,1},{4,6},{5,7},{6,4},{7,5},{8,10},{9,11},{10,... | collective-permute-start | bytes 786440 | tf_op jit(solution)/shard_map/ppermute | solution.py:479
  29.8 1.4 %encode_third.1 = (f32[128,256]{1,0:T(8,128)S(1)}, bf16[128,1024]{1,0:T(8,128)(2,1)S(1)}, bf16[128,1024]{1,0:T(8,128)(2,1)S(1)}, bf16[4,1,128,256]{3,2,1,0:T(8,128)(2,1)S(1)}) custom-call(bf16[128,1024]{1,0:T(8,128)(2,1)S(1)} %collective-permute-done.9.refs_0_.refs_5_, bf16[2,1024,1024]{2,1,0:T(8,128)(2,1)S(1)} %copy-done, bf16[4,1024,256]{2,1,0:T(8,128)(2,1)S(1)} %copy-done.1), custom_call_target="tpu_custom_call" | custom-call | tf_op jit(solution)/shard_map/encode_third/pallas_call | solution.py:64
  31.3 2.5 %attend_first.1 = (f32[256,256]{1,0:T(8,128)S(1)}, bf16[256,1024]{1,0:T(8,128)(2,1)S(1)}, bf16[4,4,128,256]{3,2,1,0:T(8,128)(2,1)S(1)}, f32[4,128,256]{2,1,0:T(8...) custom-call(s32[4,1,128]{2,1,0:T(1,128)S(1)} %bitcast.8, ...), custom_call_target="tpu_custom_call" | custom-call | tf_op jit(solution)/shard_map/attend_first/pallas_call | solution.py:64
  33.9 1.3 %collective-permute-done.13.take = bf16[256,256]{1,0:T(8,128)(2,1)S(1)} collective-permute-done((bf16[256,256]{1,0:T(8,128)(2,1)S(1)}, bf16[256,256]{1,0:T(8,128)(2,1)S(1)}, u32[]{:S(2)}, u32[]{:S(2)}) %collective-permute-start.13) | collective-permute-done | bytes 131104 | tf_op jit(solution)/shard_map/ppermute | solution.py:476
  35.6 0.5 collective-permute-start.17
  36.6 1.5 %collective-permute-start.16 = (bf16[128,1024]{1,0:T(8,128)(2,1)S(1)}, bf16[128,1024]{1,0:T(8,128)(2,1)S(1)}, u32[]{:S(2)}, u32[]{:S(2)}) collective-permute-start(bf16[128,1024]{1,0:T(8,128)(2,1)S(1)} %attn_out_own.1.part), channel_id=1, source_target_pairs={{0,2},{1,3},{2,0},{3,1},{4,6},{5,7},{6,4},{7,5},{8,10},{9,11},{10,... | collective-permute-start | bytes 786440 | tf_op jit(solution)/shard_map/ppermute | solution.py:479
  38.1 6.6 %collective-permute-done.17.got = bf16[128,1024]{1,0:T(8,128)(2,1)S(1)} collective-permute-done((bf16[128,1024]{1,0:T(8,128)(2,1)S(1)}, bf16[128,1024]{1,0:T(8,128)(2,1)S(1)}, u32[]{:S(2)}, u32[]{:S(2)}) %collective-permute-start.17) | collective-permute-done | bytes 262176 | tf_op jit(solution)/shard_map/ppermute | solution.py:479
  45.0 2.9 %ffn_own.1 = (bf16[128,1024]{1,0:T(8,128)(2,1)S(1)}, bf16[128,1024]{1,0:T(8,128)(2,1)S(1)}) custom-call(bf16[128,1024]{1,0:T(8,128)(2,1)S(1)} %get-tuple-element.144.rows_ref, bf16[128,1024]{1,0:T(8,128)(2,1)S(1)} %bitcast.6, bf16[2,1024,512]{2,1,0:T(8,128)(2,1)S(1)} %copy-done.4, bf16[2,1024,512]{2,1,0:T(8,128)(2,1)S(1)} %collective-permute-done.in_b, ...), custom_call_target="tpu_custom_call" | custom-call | tf_op jit(solution)/shard_map/ffn_own/pallas_call | solution.py:64
  47.9 1.7 %collective-permute-done.16.got = bf16[128,1024]{1,0:T(8,128)(2,1)S(1)} collective-permute-done((bf16[128,1024]{1,0:T(8,128)(2,1)S(1)}, bf16[128,1024]{1,0:T(8,128)(2,1)S(1)}, u32[]{:S(2)}, u32[]{:S(2)}) %collective-permute-start.16) | collective-permute-done | bytes 262176 | tf_op jit(solution)/shard_map/ppermute | solution.py:479
  49.6 0.5 collective-permute-start.19
  50.3 2.9 %ffn_far.1 = (bf16[128,1024]{1,0:T(8,128)(2,1)S(1)}, bf16[128,1024]{1,0:T(8,128)(2,1)S(1)}) custom-call(bf16[128,1024]{1,0:T(8,128)(2,1)S(1)} %get-tuple-element.151.rows_ref, bf16[128,1024]{1,0:T(8,128)(2,1)S(1)} %collective-permute-done.15.d_out_ref.d_out, bf16[2,1024,512]{2,1,0:T(8,128)(2,1)S(1)} %copy-done.4, ...), custom_call_target="tpu_custom_call" | custom-call | tf_op jit(solution)/shard_map/ffn_far/pallas_call | solution.py:64
  53.2 1.6 %collective-permute-start.18 = (bf16[128,1024]{1,0:T(8,128)(2,1)S(1)}, bf16[128,1024]{1,0:T(8,128)(2,1)S(1)}, u32[]{:S(2)}, u32[]{:S(2)}) collective-permute-start(bf16[128,1024]{1,0:T(8,128)(2,1)S(1)} %get-tuple-element.153.back), channel_id=1, source_target_pairs={{0,2},{1,3},{2,0},{3,1},{4,6},{5,7},{6,4},{7,5},{8,10},{9,11},{10,... | collective-permute-start | bytes 786440 | tf_op jit(solution)/shard_map/ppermute | solution.py:479
  54.8 4.1 %collective-permute-done.19.got = bf16[128,1024]{1,0:T(8,128)(2,1)S(1)} collective-permute-done((bf16[128,1024]{1,0:T(8,128)(2,1)S(1)}, bf16[128,1024]{1,0:T(8,128)(2,1)S(1)}, u32[]{:S(2)}, u32[]{:S(2)}) %collective-permute-start.19) | collective-permute-done | bytes 262176 | tf_op jit(solution)/shard_map/ppermute | solution.py:479
  59.2 0.5 collective-permute-start.21
  59.7 0.8 collective-permute-done.20.fourth_a
  60.7 2.0 %attn_back_first.1 = (bf16[4,128,256]{2,1,0:T(8,128)(2,1)S(1)}, f32[4,128,256]{2,1,0:T(8,128)S(1)}, f32[4,128,256]{2,1,0:T(8,128)S(1)}, bf16[4,128,256]{2,1,0:T(8,128)(2,1)S(1)}) custom-call(s32[4,1,128]{2,1,0:T(1,128)S(1)} %bitcast.9, bf16[128,1024]{1,0:T(8,128)(2,1)S(1)} %get-tuple-element.155.third.d_resid, ...), custom_call_target="tpu_custom_call" | custom-call | tf_op jit(solution)/shard_map/attn_back_first/pallas_call | solution.py:64
  63.4 1.0 attn_back_own.1
  64.6 2.0 %attn_back_second.1 = (bf16[256,1024]{1,0:T(8,128)(2,1)S(1)}, bf16[4,128,256]{2,1,0:T(8,128)(2,1)S(1)}, bf16[4,128,256]{2,1,0:T(8,128)(2,1)S(1)}, bf16[4,128,256...) custom-call(s32[4,1,128]{2,1,0:T(1,128)S(1)} %bitcast.11, bf16[128,1024]{1,0:T(8,128)(2,1)S(1)} %collective-permute-done.22.second, ...), custom_call_target="tpu_custom_call" | custom-call | tf_op jit(solution)/shard_map/attn_back_second/pallas_call | solution.py:64
  67.0 0.7 attn_back_keep.1.keep
  67.7 0.9 collective-permute-done.23.take
  68.8 0.5 collective-permute-start.25
  69.3 1.6 %collective-permute-start.24 = (bf16[128,1024]{1,0:T(8,128)(2,1)S(1)}, bf16[128,1024]{1,0:T(8,128)(2,1)S(1)}, u32[]{:S(2)}, u32[]{:S(2)}) collective-permute-start(bf16[128,1024]{1,0:T(8,128)(2,1)S(1)} %get-tuple-element.177.part), channel_id=1, source_target_pairs={{0,2},{1,3},{2,0},{3,1},{4,6},{5,7},{6,4},{7,5},{8,10},{9,11},{10,... | collective-permute-start | bytes 786440 | tf_op jit(solution)/shard_map/ppermute | solution.py:479
  70.9 7.1 %collective-permute-done.25.got = bf16[128,1024]{1,0:T(8,128)(2,1)S(1)} collective-permute-done((bf16[128,1024]{1,0:T(8,128)(2,1)S(1)}, bf16[128,1024]{1,0:T(8,128)(2,1)S(1)}, u32[]{:S(2)}, u32[]{:S(2)}) %collective-permute-start.25) | collective-permute-done | bytes 262176 | tf_op jit(solution)/shard_map/ppermute | solution.py:479
  78.3 0.5 collective-permute-start.27
  79.1 2.3 %collective-permute-start.34 = (bf16[96,1024]{1,0:T(8,128)(2,1)S(1)}, bf16[96,1024]{1,0:T(8,128)(2,1)S(1)}, u32[]{:S(2)}, u32[]{:S(2)}) collective-permute-start(bf16[96,1024]{1,0:T(8,128)(2,1)S(1)} %get-tuple-element.204), channel_id=1, source_target_pairs={{0,8},{4,12},{8,0},{12,4},{16,24},{20,28},{24,16},{28,20},{1,9},{5... | collective-permute-start | bytes 589832 | tf_op jit(solution)/shard_map/ppermute | solution.py:482
  81.4 1.0 enc_grads_first.1
  82.4 0.6 collective-permute-done.24.got
  83.3 0.5 collective-permute-start.29
  85.2 0.5 enc_grad1_second.1
  85.8 1.7 %collective-permute-start.32 = (bf16[4,128,256]{2,1,0:T(8,128)(2,1)S(1)}, bf16[4,128,256]{2,1,0:T(8,128)(2,1)S(1)}, u32[]{:S(2)}, u32[]{:S(2)}) collective-permute-start(bf16[4,128,256]{2,1,0:T(8,128)(2,1)S(1)} %get-tuple-element.198), channel_id=1, source_target_pairs={{0,16},{4,20},{8,24},{12,28},{16,0},{20,4},{24,8},{28,12},{1,17},{... | collective-permute-start | bytes 786440 | tf_op jit(solution)/shard_map/ppermute | solution.py:482
  87.5 3.7 %collective-permute-done.34.refs_1_ = bf16[96,1024]{1,0:T(8,128)(2,1)S(1)} collective-permute-done((bf16[96,1024]{1,0:T(8,128)(2,1)S(1)}, bf16[96,1024]{1,0:T(8,128)(2,1)S(1)}, u32[]{:S(2)}, u32[]{:S(2)}) %collective-permute-start.34) | collective-permute-done | bytes 196640 | tf_op jit(solution)/shard_map/ppermute | solution.py:482
  91.2 0.9 enc_grad0_second.1
  92.5 1.0 collective-permute-start.35
  93.6 0.8 collective-permute-done.32.got
  94.4 1.7 %collective-permute-start.33 = (bf16[2,128,256]{2,1,0:T(8,128)(2,1)S(1)}, bf16[2,128,256]{2,1,0:T(8,128)(2,1)S(1)}, u32[]{:S(2)}, u32[]{:S(2)}) collective-permute-start(bf16[2,128,256]{2,1,0:T(8,128)(2,1)S(1)} %get-tuple-element.200), channel_id=1, source_target_pairs={{0,4},{4,0},{8,12},{12,8},{16,20},{20,16},{24,28},{28,24},{1,5},{5... | collective-permute-start | bytes 393224 | tf_op jit(solution)/shard_map/ppermute | solution.py:482
  96.6 0.5 collective-permute-start.40
  97.2 3.8 %collective-permute-done.37.got = bf16[4,128,256]{2,1,0:T(8,128)(2,1)S(1)} collective-permute-done((bf16[4,128,256]{2,1,0:T(8,128)(2,1)S(1)}, bf16[4,128,256]{2,1,0:T(8,128)(2,1)S(1)}, u32[]{:S(2)}, u32[]{:S(2)}) %collective-permute-start.37) | collective-permute-done | bytes 262176 | tf_op jit(solution)/shard_map/ppermute | solution.py:482
  101.1 1.7 %collective-permute-start.38 = (bf16[2,128,256]{2,1,0:T(8,128)(2,1)S(1)}, bf16[2,128,256]{2,1,0:T(8,128)(2,1)S(1)}, u32[]{:S(2)}, u32[]{:S(2)}) collective-permute-start(bf16[2,128,256]{2,1,0:T(8,128)(2,1)S(1)} %get-tuple-element.213), channel_id=1, source_target_pairs={{0,16},{4,20},{8,24},{12,28},{16,0},{20,4},{24,8},{28,12},{1,17},{... | collective-permute-start | bytes 393224 | tf_op jit(solution)/shard_map/ppermute | solution.py:482
  102.8 0.9 collective-permute-start.41
  103.6 2.5 %collective-permute-done.38.got = bf16[2,128,256]{2,1,0:T(8,128)(2,1)S(1)} collective-permute-done((bf16[2,128,256]{2,1,0:T(8,128)(2,1)S(1)}, bf16[2,128,256]{2,1,0:T(8,128)(2,1)S(1)}, u32[]{:S(2)}, u32[]{:S(2)}) %collective-permute-start.38) | collective-permute-done | bytes 131104 | tf_op jit(solution)/shard_map/ppermute | solution.py:482
  106.1 2.0 %collective-permute-start.39 = (bf16[1,128,256]{2,1,0:T(8,128)(2,1)S(1)}, bf16[1,128,256]{2,1,0:T(8,128)(2,1)S(1)}, u32[]{:S(2)}, u32[]{:S(2)}) collective-permute-start(bf16[1,128,256]{2,1,0:T(8,128)(2,1)S(1)} %get-tuple-element.214), channel_id=1, source_target_pairs={{0,8},{4,12},{8,0},{12,4},{16,24},{20,28},{24,16},{28,20},{1,9},{5... | collective-permute-start | bytes 196616 | tf_op jit(solution)/shard_map/ppermute | solution.py:482
  108.2 1.0 collective-permute-start.36
  109.2 1.2 %ffn_out_own.1 = bf16[128,1024]{1,0:T(8,128)(2,1)} custom-call(bf16[128,1024]{1,0:T(8,128)(2,1)S(1)} %get-tuple-element.215.hidden, bf16[512,1024]{1,0:T(8,128)(2,1)S(1)} %copy-done.2, bf16[512,1024]{1,0:T(8,128)(2,1)S(1)} %collective-permute-done.1.out_b.w_b, bf16[128,1024]{1,0:T(8,128)(2,1)S(1)} %get-tuple-element.162.resid, ...), custom_call_target="tpu_custom_call" | custom-call | tf_op jit(solution)/shard_map/ffn_out_own/pallas_call | solution.py:64
  110.4 1.0 back_recv.1
  111.3 1.0 collective-permute-done.39.got0
  112.3 1.5 %collective-permute-done.36.got1 = bf16[1,128,256]{2,1,0:T(8,128)(2,1)S(1)} collective-permute-done((bf16[1,128,256]{2,1,0:T(8,128)(2,1)S(1)}, bf16[1,128,256]{2,1,0:T(8,128)(2,1)S(1)}, u32[]{:S(2)}, u32[]{:S(2)}) %collective-permute-start.36) | collective-permute-done | bytes 65568 | tf_op jit(solution)/shard_map/ppermute | solution.py:482
  113.8 0.7 finish.1
  (71 shorter events, 7.9 us)
Async XLA Ops:
  0.6 7.9 %collective-permute-start = (bf16[2,1024,512]{2,1,0:T(8,128)(2,1)}, bf16[2,1024,512]{2,1,0:T(8,128)(2,1)S(1)}, u32[]{:S(2)}, u32[]{:S(2)}) collective-permute-start(bf16[2,1024,512]{2,1,0:T(8,128)(2,1)} %in_a.3), channel_id=1, source_target_pairs={{0,1},{1,0},{2,3},{3,2},{4,5},{5,4},{6,7},{7,6},{8,9},{9,8},{10,11... | collective-permute-start | bytes 6291464 | tf_op jit(solution)/shard_map/ppermute | solution.py:476
  1.1 7.4 %collective-permute-start.1 = (bf16[512,1024]{1,0:T(8,128)(2,1)}, bf16[512,1024]{1,0:T(8,128)(2,1)S(1)}, u32[]{:S(2)}, u32[]{:S(2)}) collective-permute-start(bf16[512,1024]{1,0:T(8,128)(2,1)} %w_a.3), channel_id=1, source_target_pairs={{0,1},{1,0},{2,3},{3,2},{4,5},{5,4},{6,7},{7,6},{8,9},{9,8},{10,11... | collective-permute-start | bytes 3145736 | tf_op jit(solution)/shard_map/ppermute | solution.py:476
  1.9 0.9 copy-start.7
  2.9 21.6 %copy-start = (bf16[2,1024,1024]{2,1,0:T(8,128)(2,1)S(1)}, bf16[2,1024,1024]{2,1,0:T(8,128)(2,1)}, u32[]{:S(2)}) copy-start(bf16[2,1024,1024]{2,1,0:T(8,128)(2,1)} %refs_8_.3) | copy-start | bytes 12582916
  2.9 21.6 %copy-start.1 = (bf16[4,1024,256]{2,1,0:T(8,128)(2,1)S(1)}, bf16[4,1024,256]{2,1,0:T(8,128)(2,1)}, u32[]{:S(2)}) copy-start(bf16[4,1024,256]{2,1,0:T(8,128)(2,1)} %w_in.5) | copy-start | bytes 6291460
  3.2 10.6 %collective-permute-start.2 = (bf16[24,1152]{1,0:T(8,128)(2,1)S(1)}, bf16[24,1152]{1,0:T(8,128)(2,1)S(1)}, u32[]{:S(2)}, u32[]{:S(2)}) collective-permute-start(bf16[24,1152]{1,0:T(8,128)(2,1)S(1)} %get-tuple-element.115), channel_id=1, source_target_pairs={{0,8},{4,12},{8,0},{12,4},{16,24},{20,28},{24,16},{28,20},{1,9},{5... | collective-permute-start | bytes 165896 | tf_op jit(solution)/shard_map/ppermute | solution.py:482
  7.3 8.8 %collective-permute-start.3 = (bf16[24,1152]{1,0:T(8,128)(2,1)S(1)}, bf16[24,1152]{1,0:T(8,128)(2,1)S(1)}, u32[]{:S(2)}, u32[]{:S(2)}) collective-permute-start(bf16[24,1152]{1,0:T(8,128)(2,1)S(1)} %get-tuple-element.116), channel_id=1, source_target_pairs={{0,24},{4,28},{8,16},{12,20},{16,8},{20,12},{24,0},{28,4},{1,25},{... | collective-permute-start | bytes 165896 | tf_op jit(solution)/shard_map/ppermute | solution.py:482
  8.6 7.8 %collective-permute-start.4 = (bf16[24,1152]{1,0:T(8,128)(2,1)S(1)}, bf16[24,1152]{1,0:T(8,128)(2,1)S(1)}, u32[]{:S(2)}, u32[]{:S(2)}) collective-permute-start(bf16[24,1152]{1,0:T(8,128)(2,1)S(1)} %get-tuple-element.123), channel_id=1, source_target_pairs={{0,12},{4,8},{8,4},{12,0},{16,28},{20,24},{24,20},{28,16},{1,13},{... | collective-permute-start | bytes 165896 | tf_op jit(solution)/shard_map/ppermute | solution.py:482
  12.2 7.0 %collective-permute-start.5 = (bf16[24,1152]{1,0:T(8,128)(2,1)S(1)}, bf16[24,1152]{1,0:T(8,128)(2,1)S(1)}, u32[]{:S(2)}, u32[]{:S(2)}) collective-permute-start(bf16[24,1152]{1,0:T(8,128)(2,1)S(1)} %get-tuple-element.124), channel_id=1, source_target_pairs={{0,28},{4,24},{8,20},{12,16},{16,12},{20,8},{24,4},{28,0},{1,29},{... | collective-permute-start | bytes 165896 | tf_op jit(solution)/shard_map/ppermute | solution.py:482
  12.8 6.4 %collective-permute-start.6 = (bf16[24,1152]{1,0:T(8,128)(2,1)S(1)}, bf16[24,1152]{1,0:T(8,128)(2,1)S(1)}, u32[]{:S(2)}, u32[]{:S(2)}) collective-permute-start(bf16[24,1152]{1,0:T(8,128)(2,1)S(1)} %get-tuple-element.125), channel_id=1, source_target_pairs={{0,16},{4,20},{8,24},{12,28},{16,0},{20,4},{24,8},{28,12},{1,17},{... | collective-permute-start | bytes 165896 | tf_op jit(solution)/shard_map/ppermute | solution.py:482
  13.9 5.3 %collective-permute-start.7 = (bf16[24,1152]{1,0:T(8,128)(2,1)S(1)}, bf16[24,1152]{1,0:T(8,128)(2,1)S(1)}, u32[]{:S(2)}, u32[]{:S(2)}) collective-permute-start(bf16[24,1152]{1,0:T(8,128)(2,1)S(1)} %get-tuple-element.126), channel_id=1, source_target_pairs={{0,4},{4,0},{8,12},{12,8},{16,20},{20,16},{24,28},{28,24},{1,5},{5... | collective-permute-start | bytes 165896 | tf_op jit(solution)/shard_map/ppermute | solution.py:482
  16.1 5.1 %collective-permute-start.8 = (bf16[24,1152]{1,0:T(8,128)(2,1)S(1)}, bf16[24,1152]{1,0:T(8,128)(2,1)S(1)}, u32[]{:S(2)}, u32[]{:S(2)}) collective-permute-start(bf16[24,1152]{1,0:T(8,128)(2,1)S(1)} %get-tuple-element.127), channel_id=1, source_target_pairs={{0,20},{4,16},{8,28},{12,24},{16,4},{20,0},{24,12},{28,8},{1,21},{... | collective-permute-start | bytes 165896 | tf_op jit(solution)/shard_map/ppermute | solution.py:482
  21.4 6.4 %collective-permute-start.9 = (bf16[128,1024]{1,0:T(8,128)(2,1)S(1)}, bf16[128,1024]{1,0:T(8,128)(2,1)S(1)}, u32[]{:S(2)}, u32[]{:S(2)}) collective-permute-start(bf16[128,1024]{1,0:T(8,128)(2,1)S(1)} %get-tuple-element.128.refs_0_.refs_3_), channel_id=1, source_target_pairs={{0,2},{1,3},{2,0},{3,1},{4,6},{5,7},{6,4},{7,5},{8,10},{9,11},{10,... | collective-permute-start | bytes 786440 | tf_op jit(solution)/shard_map/ppermute | solution.py:479
  23.0 1.3 %collective-permute-start.10 = (bf16[64,1024]{1,0:T(8,128)(2,1)S(1)}, bf16[64,1024]{1,0:T(8,128)(2,1)S(1)}, u32[]{:S(2)}, u32[]{:S(2)}) collective-permute-start(bf16[64,1024]{1,0:T(8,128)(2,1)S(1)} %get-tuple-element.129), channel_id=1, source_target_pairs={{0,1},{1,0},{2,3},{3,2},{4,5},{5,4},{6,7},{7,6},{8,9},{9,8},{10,11... | collective-permute-start | bytes 393224 | tf_op jit(solution)/shard_map/ppermute | solution.py:476
  23.0 4.9 %copy-start.3 = (bf16[256,1024]{1,0:T(8,128)(2,1)S(1)}, bf16[256,1024]{1,0:T(8,128)(2,1)}, u32[]{:S(2)}) copy-start(bf16[256,1024]{1,0:T(8,128)(2,1)} %w_out.5) | copy-start | bytes 1572868
  23.0 5.4 %copy-start.5 = (bf16[1,128,1024]{2,1,0:T(8,128)(2,1)S(1)}, bf16[1,128,1024]{2,1,0:T(8,128)(2,1)}, u32[]{:S(2)}) copy-start(bf16[1,128,1024]{2,1,0:T(8,128)(2,1)} %param.19) | copy-start | bytes 786436
  23.0 1.5 %collective-permute-start.11 = (bf16[64,1024]{1,0:T(8,128)(2,1)S(1)}, bf16[64,1024]{1,0:T(8,128)(2,1)S(1)}, u32[]{:S(2)}, u32[]{:S(2)}) collective-permute-start(bf16[64,1024]{1,0:T(8,128)(2,1)S(1)} %get-tuple-element.130), channel_id=1, source_target_pairs={{0,1},{1,0},{2,3},{3,2},{4,5},{5,4},{6,7},{7,6},{8,9},{9,8},{10,11... | collective-permute-start | bytes 393224 | tf_op jit(solution)/shard_map/ppermute | solution.py:476
  27.8 3.4 %copy-start.6 = (s32[1,512]{1,0:T(1,128)S(1)}, s32[1,512]{1,0:T(1,128)}, u32[]{:S(2)}) copy-start(s32[1,512]{1,0:T(1,128)} %param.13) | copy-start | bytes 6148
  27.8 7.4 %collective-permute-start.14 = (bf16[256,1024]{1,0:T(8,128)(2,1)S(1)}, bf16[256,1024]{1,0:T(8,128)(2,1)S(1)}, u32[]{:S(2)}, u32[]{:S(2)}) collective-permute-start(bf16[256,1024]{1,0:T(8,128)(2,1)S(1)} %copy-done.3), channel_id=1, source_target_pairs={{0,1},{1,0},{2,3},{3,2},{4,5},{5,4},{6,7},{7,6},{8,9},{9,8},{10,11... | collective-permute-start | bytes 1572872 | tf_op jit(solution)/shard_map/ppermute | solution.py:476
  27.8 3.4 %collective-permute-start.12 = (bf16[128,1024]{1,0:T(8,128)(2,1)S(1)}, bf16[128,1024]{1,0:T(8,128)(2,1)S(1)}, u32[]{:S(2)}, u32[]{:S(2)}) collective-permute-start(bf16[128,1024]{1,0:T(8,128)(2,1)S(1)} %collective-permute-done.9.refs_0_.refs_5_), channel_id=1, source_target_pairs={{0,1},{1,0},{2,3},{3,2},{4,5},{5,4},{6,7},{7,6},{8,9},{9,8},{10,11... | collective-permute-start | bytes 786440 | tf_op jit(solution)/shard_map/ppermute | solution.py:476
  28.3 8.3 %collective-permute-start.15 = (bf16[128,1024]{1,0:T(8,128)(2,1)S(1)}, bf16[128,1024]{1,0:T(8,128)(2,1)S(1)}, u32[]{:S(2)}, u32[]{:S(2)}) collective-permute-start(bf16[128,1024]{1,0:T(8,128)(2,1)S(1)} %bitcast.5), channel_id=1, source_target_pairs={{0,2},{1,3},{2,0},{3,1},{4,6},{5,7},{6,4},{7,5},{8,10},{9,11},{10,... | collective-permute-start | bytes 786440 | tf_op jit(solution)/shard_map/ppermute | solution.py:479
  33.8 11.2 %copy-start.2 = (bf16[512,1024]{1,0:T(8,128)(2,1)S(1)}, bf16[512,1024]{1,0:T(8,128)(2,1)}, u32[]{:S(2)}) copy-start(bf16[512,1024]{1,0:T(8,128)(2,1)} %w_a.3) | copy-start | bytes 3145732
  33.8 11.2 %copy-start.4 = (bf16[2,1024,512]{2,1,0:T(8,128)(2,1)S(1)}, bf16[2,1024,512]{2,1,0:T(8,128)(2,1)}, u32[]{:S(2)}) copy-start(bf16[2,1024,512]{2,1,0:T(8,128)(2,1)} %in_a.3) | copy-start | bytes 6291460
  33.8 1.4 %collective-permute-start.13 = (bf16[256,256]{1,0:T(8,128)(2,1)S(1)}, bf16[256,256]{1,0:T(8,128)(2,1)S(1)}, u32[]{:S(2)}, u32[]{:S(2)}) collective-permute-start(bf16[256,256]{1,0:T(8,128)(2,1)S(1)} %get-tuple-element.139), channel_id=1, source_target_pairs={{0,1},{1,0},{2,3},{3,2},{4,5},{5,4},{6,7},{7,6},{8,9},{9,8},{10,11... | collective-permute-start | bytes 393224 | tf_op jit(solution)/shard_map/ppermute | solution.py:476
  35.6 9.2 %collective-permute-start.17 = (bf16[128,1024]{1,0:T(8,128)(2,1)S(1)}, bf16[128,1024]{1,0:T(8,128)(2,1)S(1)}, u32[]{:S(2)}, u32[]{:S(2)}) collective-permute-start(bf16[128,1024]{1,0:T(8,128)(2,1)S(1)} %attn_out_far.1.part), channel_id=1, source_target_pairs={{0,2},{1,3},{2,0},{3,1},{4,6},{5,7},{6,4},{7,5},{8,10},{9,11},{10,... | collective-permute-start | bytes 786440 | tf_op jit(solution)/shard_map/ppermute | solution.py:479
  36.6 13.0 %collective-permute-start.16 = (bf16[128,1024]{1,0:T(8,128)(2,1)S(1)}, bf16[128,1024]{1,0:T(8,128)(2,1)S(1)}, u32[]{:S(2)}, u32[]{:S(2)}) collective-permute-start(bf16[128,1024]{1,0:T(8,128)(2,1)S(1)} %attn_out_own.1.part), channel_id=1, source_target_pairs={{0,2},{1,3},{2,0},{3,1},{4,6},{5,7},{6,4},{7,5},{8,10},{9,11},{10,... | collective-permute-start | bytes 786440 | tf_op jit(solution)/shard_map/ppermute | solution.py:479
  49.6 9.2 %collective-permute-start.19 = (bf16[128,1024]{1,0:T(8,128)(2,1)S(1)}, bf16[128,1024]{1,0:T(8,128)(2,1)S(1)}, u32[]{:S(2)}, u32[]{:S(2)}) collective-permute-start(bf16[128,1024]{1,0:T(8,128)(2,1)S(1)} %get-tuple-element.148.back), channel_id=1, source_target_pairs={{0,2},{1,3},{2,0},{3,1},{4,6},{5,7},{6,4},{7,5},{8,10},{9,11},{10,... | collective-permute-start | bytes 786440 | tf_op jit(solution)/shard_map/ppermute | solution.py:479
  53.2 9.6 %collective-permute-start.18 = (bf16[128,1024]{1,0:T(8,128)(2,1)S(1)}, bf16[128,1024]{1,0:T(8,128)(2,1)S(1)}, u32[]{:S(2)}, u32[]{:S(2)}) collective-permute-start(bf16[128,1024]{1,0:T(8,128)(2,1)S(1)} %get-tuple-element.153.back), channel_id=1, source_target_pairs={{0,2},{1,3},{2,0},{3,1},{4,6},{5,7},{6,4},{7,5},{8,10},{9,11},{10,... | collective-permute-start | bytes 786440 | tf_op jit(solution)/shard_map/ppermute | solution.py:479
  59.1 1.4 %collective-permute-start.20 = (bf16[64,1024]{1,0:T(8,128)(2,1)S(1)}, bf16[64,1024]{1,0:T(8,128)(2,1)S(1)}, u32[]{:S(2)}, u32[]{:S(2)}) collective-permute-start(bf16[64,1024]{1,0:T(8,128)(2,1)S(1)} %get-tuple-element.156), channel_id=1, source_target_pairs={{0,1},{1,0},{2,3},{3,2},{4,5},{5,4},{6,7},{7,6},{8,9},{9,8},{10,11... | collective-permute-start | bytes 393224 | tf_op jit(solution)/shard_map/ppermute | solution.py:476
  59.2 1.5 %collective-permute-start.21 = (bf16[64,1024]{1,0:T(8,128)(2,1)S(1)}, bf16[64,1024]{1,0:T(8,128)(2,1)S(1)}, u32[]{:S(2)}, u32[]{:S(2)}) collective-permute-start(bf16[64,1024]{1,0:T(8,128)(2,1)S(1)} %get-tuple-element.157), channel_id=1, source_target_pairs={{0,1},{1,0},{2,3},{3,2},{4,5},{5,4},{6,7},{7,6},{8,9},{9,8},{10,11... | collective-permute-start | bytes 393224 | tf_op jit(solution)/shard_map/ppermute | solution.py:476
  63.0 1.6 %collective-permute-start.22 = (bf16[128,1024]{1,0:T(8,128)(2,1)S(1)}, bf16[128,1024]{1,0:T(8,128)(2,1)S(1)}, u32[]{:S(2)}, u32[]{:S(2)}) collective-permute-start(bf16[128,1024]{1,0:T(8,128)(2,1)S(1)} %resid_back.1.first.d_resid), channel_id=1, source_target_pairs={{0,1},{1,0},{2,3},{3,2},{4,5},{5,4},{6,7},{7,6},{8,9},{9,8},{10,11... | collective-permute-start | bytes 786440 | tf_op jit(solution)/shard_map/ppermute | solution.py:476
  66.6 2.0 %collective-permute-start.23 = (bf16[256,1024]{1,0:T(8,128)(2,1)S(1)}, bf16[256,1024]{1,0:T(8,128)(2,1)S(1)}, u32[]{:S(2)}, u32[]{:S(2)}) collective-permute-start(bf16[256,1024]{1,0:T(8,128)(2,1)S(1)} %get-tuple-element.175), channel_id=1, source_target_pairs={{0,1},{1,0},{2,3},{3,2},{4,5},{5,4},{6,7},{7,6},{8,9},{9,8},{10,11... | collective-permute-start | bytes 1572872 | tf_op jit(solution)/shard_map/ppermute | solution.py:476
  68.8 9.2 %collective-permute-start.25 = (bf16[128,1024]{1,0:T(8,128)(2,1)S(1)}, bf16[128,1024]{1,0:T(8,128)(2,1)S(1)}, u32[]{:S(2)}, u32[]{:S(2)}) collective-permute-start(bf16[128,1024]{1,0:T(8,128)(2,1)S(1)} %get-tuple-element.176.part), channel_id=1, source_target_pairs={{0,2},{1,3},{2,0},{3,1},{4,6},{5,7},{6,4},{7,5},{8,10},{9,11},{10,... | collective-permute-start | bytes 786440 | tf_op jit(solution)/shard_map/ppermute | solution.py:479
  69.3 13.6 %collective-permute-start.24 = (bf16[128,1024]{1,0:T(8,128)(2,1)S(1)}, bf16[128,1024]{1,0:T(8,128)(2,1)S(1)}, u32[]{:S(2)}, u32[]{:S(2)}) collective-permute-start(bf16[128,1024]{1,0:T(8,128)(2,1)S(1)} %get-tuple-element.177.part), channel_id=1, source_target_pairs={{0,2},{1,3},{2,0},{3,1},{4,6},{5,7},{6,4},{7,5},{8,10},{9,11},{10,... | collective-permute-start | bytes 786440 | tf_op jit(solution)/shard_map/ppermute | solution.py:479
  78.3 3.1 %collective-permute-start.26 = (bf16[64,1024]{1,0:T(8,128)(2,1)S(1)}, bf16[64,1024]{1,0:T(8,128)(2,1)S(1)}, u32[]{:S(2)}, u32[]{:S(2)}) collective-permute-start(bf16[64,1024]{1,0:T(8,128)(2,1)S(1)} %get-tuple-element.179), channel_id=1, source_target_pairs={{0,1},{1,0},{2,3},{3,2},{4,5},{5,4},{6,7},{7,6},{8,9},{9,8},{10,11... | collective-permute-start | bytes 393224 | tf_op jit(solution)/shard_map/ppermute | solution.py:476
  78.3 3.1 %collective-permute-start.27 = (bf16[64,1024]{1,0:T(8,128)(2,1)S(1)}, bf16[64,1024]{1,0:T(8,128)(2,1)S(1)}, u32[]{:S(2)}, u32[]{:S(2)}) collective-permute-start(bf16[64,1024]{1,0:T(8,128)(2,1)S(1)} %get-tuple-element.180), channel_id=1, source_target_pairs={{0,1},{1,0},{2,3},{3,2},{4,5},{5,4},{6,7},{7,6},{8,9},{9,8},{10,11... | collective-permute-start | bytes 393224 | tf_op jit(solution)/shard_map/ppermute | solution.py:476
  79.1 12.1 %collective-permute-start.34 = (bf16[96,1024]{1,0:T(8,128)(2,1)S(1)}, bf16[96,1024]{1,0:T(8,128)(2,1)S(1)}, u32[]{:S(2)}, u32[]{:S(2)}) collective-permute-start(bf16[96,1024]{1,0:T(8,128)(2,1)S(1)} %get-tuple-element.204), channel_id=1, source_target_pairs={{0,8},{4,12},{8,0},{12,4},{16,24},{20,28},{24,16},{28,20},{1,9},{5... | collective-permute-start | bytes 589832 | tf_op jit(solution)/shard_map/ppermute | solution.py:482
  83.2 1.3 %collective-permute-start.28 = (bf16[32,1024]{1,0:T(8,128)(2,1)S(1)}, bf16[32,1024]{1,0:T(8,128)(2,1)S(1)}, u32[]{:S(2)}, u32[]{:S(2)}) collective-permute-start(bf16[32,1024]{1,0:T(8,128)(2,1)S(1)} %get-tuple-element.189), channel_id=1, source_target_pairs={{0,1},{1,0},{2,3},{3,2},{4,5},{5,4},{6,7},{7,6},{8,9},{9,8},{10,11... | collective-permute-start | bytes 196616 | tf_op jit(solution)/shard_map/ppermute | solution.py:476
  83.3 1.4 %collective-permute-start.29 = (bf16[32,1024]{1,0:T(8,128)(2,1)S(1)}, bf16[32,1024]{1,0:T(8,128)(2,1)S(1)}, u32[]{:S(2)}, u32[]{:S(2)}) collective-permute-start(bf16[32,1024]{1,0:T(8,128)(2,1)S(1)} %get-tuple-element.190), channel_id=1, source_target_pairs={{0,1},{1,0},{2,3},{3,2},{4,5},{5,4},{6,7},{7,6},{8,9},{9,8},{10,11... | collective-permute-start | bytes 196616 | tf_op jit(solution)/shard_map/ppermute | solution.py:476
  83.8 1.3 %collective-permute-start.30 = (bf16[32,1024]{1,0:T(8,128)(2,1)S(1)}, bf16[32,1024]{1,0:T(8,128)(2,1)S(1)}, u32[]{:S(2)}, u32[]{:S(2)}) collective-permute-start(bf16[32,1024]{1,0:T(8,128)(2,1)S(1)} %get-tuple-element.191), channel_id=1, source_target_pairs={{0,1},{1,0},{2,3},{3,2},{4,5},{5,4},{6,7},{7,6},{8,9},{9,8},{10,11... | collective-permute-start | bytes 196616 | tf_op jit(solution)/shard_map/ppermute | solution.py:476
  83.9 1.3 %collective-permute-start.31 = (bf16[32,1024]{1,0:T(8,128)(2,1)S(1)}, bf16[32,1024]{1,0:T(8,128)(2,1)S(1)}, u32[]{:S(2)}, u32[]{:S(2)}) collective-permute-start(bf16[32,1024]{1,0:T(8,128)(2,1)S(1)} %get-tuple-element.192), channel_id=1, source_target_pairs={{0,1},{1,0},{2,3},{3,2},{4,5},{5,4},{6,7},{7,6},{8,9},{9,8},{10,11... | collective-permute-start | bytes 196616 | tf_op jit(solution)/shard_map/ppermute | solution.py:476
  85.8 8.6 %collective-permute-start.32 = (bf16[4,128,256]{2,1,0:T(8,128)(2,1)S(1)}, bf16[4,128,256]{2,1,0:T(8,128)(2,1)S(1)}, u32[]{:S(2)}, u32[]{:S(2)}) collective-permute-start(bf16[4,128,256]{2,1,0:T(8,128)(2,1)S(1)} %get-tuple-element.198), channel_id=1, source_target_pairs={{0,16},{4,20},{8,24},{12,28},{16,0},{20,4},{24,8},{28,12},{1,17},{... | collective-permute-start | bytes 786440 | tf_op jit(solution)/shard_map/ppermute | solution.py:482
  92.1 8.9 %collective-permute-start.37 = (bf16[4,128,256]{2,1,0:T(8,128)(2,1)S(1)}, bf16[4,128,256]{2,1,0:T(8,128)(2,1)S(1)}, u32[]{:S(2)}, u32[]{:S(2)}) collective-permute-start(bf16[4,128,256]{2,1,0:T(8,128)(2,1)S(1)} %get-tuple-element.211), channel_id=1, source_target_pairs={{0,4},{4,0},{8,12},{12,8},{16,20},{20,16},{24,28},{28,24},{1,5},{5... | collective-permute-start | bytes 786440 | tf_op jit(solution)/shard_map/ppermute | solution.py:482
  92.5 10.2 %collective-permute-start.35 = (bf16[96,1024]{1,0:T(8,128)(2,1)S(1)}, bf16[96,1024]{1,0:T(8,128)(2,1)S(1)}, u32[]{:S(2)}, u32[]{:S(2)}) collective-permute-start(bf16[96,1024]{1,0:T(8,128)(2,1)S(1)} %back_pick.2), channel_id=1, source_target_pairs={{0,16},{4,20},{8,24},{12,28},{16,0},{20,4},{24,8},{28,12},{1,17},{... | collective-permute-start | bytes 589832 | tf_op jit(solution)/shard_map/ppermute | solution.py:482
  94.4 8.3 %collective-permute-start.33 = (bf16[2,128,256]{2,1,0:T(8,128)(2,1)S(1)}, bf16[2,128,256]{2,1,0:T(8,128)(2,1)S(1)}, u32[]{:S(2)}, u32[]{:S(2)}) collective-permute-start(bf16[2,128,256]{2,1,0:T(8,128)(2,1)S(1)} %get-tuple-element.200), channel_id=1, source_target_pairs={{0,4},{4,0},{8,12},{12,8},{16,20},{20,16},{24,28},{28,24},{1,5},{5... | collective-permute-start | bytes 393224 | tf_op jit(solution)/shard_map/ppermute | solution.py:482
  96.6 12.6 %collective-permute-start.40 = (bf16[128,1024]{1,0:T(8,128)(2,1)S(1)}, bf16[128,1024]{1,0:T(8,128)(2,1)S(1)}, u32[]{:S(2)}, u32[]{:S(2)}) collective-permute-start(bf16[128,1024]{1,0:T(8,128)(2,1)S(1)} %ffn_out_far.1), channel_id=1, source_target_pairs={{0,2},{1,3},{2,0},{3,1},{4,6},{5,7},{6,4},{7,5},{8,10},{9,11},{10,... | collective-permute-start | bytes 786440 | tf_op jit(solution)/shard_map/ppermute | solution.py:479
  101.1 5.0 %collective-permute-start.38 = (bf16[2,128,256]{2,1,0:T(8,128)(2,1)S(1)}, bf16[2,128,256]{2,1,0:T(8,128)(2,1)S(1)}, u32[]{:S(2)}, u32[]{:S(2)}) collective-permute-start(bf16[2,128,256]{2,1,0:T(8,128)(2,1)S(1)} %get-tuple-element.213), channel_id=1, source_target_pairs={{0,16},{4,20},{8,24},{12,28},{16,0},{20,4},{24,8},{28,12},{1,17},{... | collective-permute-start | bytes 393224 | tf_op jit(solution)/shard_map/ppermute | solution.py:482
  102.8 7.6 %collective-permute-start.41 = (bf16[96,1024]{1,0:T(8,128)(2,1)S(1)}, bf16[96,1024]{1,0:T(8,128)(2,1)S(1)}, u32[]{:S(2)}, u32[]{:S(2)}) collective-permute-start(bf16[96,1024]{1,0:T(8,128)(2,1)S(1)} %back_pick.3), channel_id=1, source_target_pairs={{0,4},{4,0},{8,12},{12,8},{16,20},{20,16},{24,28},{28,24},{1,5},{5... | collective-permute-start | bytes 589832 | tf_op jit(solution)/shard_map/ppermute | solution.py:482
  106.1 6.2 %collective-permute-start.39 = (bf16[1,128,256]{2,1,0:T(8,128)(2,1)S(1)}, bf16[1,128,256]{2,1,0:T(8,128)(2,1)S(1)}, u32[]{:S(2)}, u32[]{:S(2)}) collective-permute-start(bf16[1,128,256]{2,1,0:T(8,128)(2,1)S(1)} %get-tuple-element.214), channel_id=1, source_target_pairs={{0,8},{4,12},{8,0},{12,4},{16,24},{20,28},{24,16},{28,20},{1,9},{5... | collective-permute-start | bytes 196616 | tf_op jit(solution)/shard_map/ppermute | solution.py:482
  108.2 5.6 %collective-permute-start.36 = (bf16[1,128,256]{2,1,0:T(8,128)(2,1)S(1)}, bf16[1,128,256]{2,1,0:T(8,128)(2,1)S(1)}, u32[]{:S(2)}, u32[]{:S(2)}) collective-permute-start(bf16[1,128,256]{2,1,0:T(8,128)(2,1)S(1)} %get-tuple-element.207), channel_id=1, source_target_pairs={{0,8},{4,12},{8,0},{12,4},{16,24},{20,28},{24,16},{28,20},{1,9},{5... | collective-permute-start | bytes 196616 | tf_op jit(solution)/shard_map/ppermute | solution.py:482

commit v10 on v9

--- a/solution.py
+++ b/solution.py
@@ -330,47 +330,45 @@
         attend_back(docs, joined(rows), r, proj, att, w_out[...], masks, d_q, d_k, d_v, d_g)
 
 
-def back_norm(grads, w_in, first, second):
-    total = None
-    for c, grad in enumerate(grads):
-        left = jnp.concatenate([grad[first], grad[second]], axis=0)
-        term = dot(left, w_in[c], NT)
-        total = term if total is None else total + term
-    return total
-
-
-def attn_back_own(docs, first, proj, att, w_out, d_k_far, d_v_far, d_q, d_k, d_v, d_g):
+def attn_back_own(
+    docs, first, proj, att, w_out, d_q_far, d_k_far, d_v_far, d_g_far, w_in, give_ref, d_q, d_k, d_v, d_g
+):
     masks = head_masks(w_out.shape[0])
+    d_q[...] = d_q_far[...]
+    d_g[...] = d_g_far[...]
     d_k[...] = d_k_far[...]
     d_v[...] = d_v_far[...]
     attend_back(docs, first[...], 0, proj, att, w_out[...], masks, d_q, d_k, d_v, d_g)
+    give_ref[...] = bf16(back_norm((d_q, d_k, d_v, d_g), w_in, 3))
 
 
 def attn_back_second(
-    docs, second, proj, att, w_out, d_q_far, d_g_far, d_q_own, d_k_own, d_v_own, d_g_own, w_in,
-    give_ref, d_q, d_k, d_v, d_g, sum_k, sum_v,
+    docs, second, proj, att, w_out, d_q_own, d_k_own, d_v_own, d_g_own, d_q, d_k, d_v, d_g, sum_k, sum_v
 ):
     masks = head_masks(w_out.shape[0])
-    d_q[2:4] = d_q_far[2:4]
-    d_g[2:4] = d_g_far[2:4]
-    d_q[0] = d_q_own[0]
-    d_g[0] = d_g_own[0]
+    d_q[...] = d_q_own[...]
+    d_g[...] = d_g_own[...]
     sum_k[...] = d_k_own[...]
     sum_v[...] = d_v_own[...]
     attend_back(docs, second[...], 1, proj, att, w_out[...], masks, d_q, sum_k, sum_v, d_g)
     d_k[...] = bf16(sum_k[...])
     d_v[...] = bf16(sum_v[...])
-    give_ref[...] = bf16(back_norm((d_q, d_k, d_v, d_g), w_in, 3, 1))
-
-
-def attn_back_keep(d_q, d_k, d_v, d_g, w_in, keep_ref):
-    keep_ref[...] = back_norm((d_q, d_k, d_v, d_g), w_in, 2, 0)
-
-
-def add_near(keep, take, out_far, out_own):
-    half = out_far.shape[0]
-    out_far[...] = bf16(keep[:half, :] + take[:half, :].astype(F32))
-    out_own[...] = bf16(keep[half:, :] + take[half:, :].astype(F32))
+
+
+def back_norm(grads, w_in, block):
+    total = None
+    for c, grad in enumerate(grads):
+        term = dot(bf16(grad[block]), w_in[c], NT)
+        total = term if total is None else total + term
+    return total
+
+
+def back_give(block, d_q, d_k, d_v, d_g, w_in, out):
+    out[...] = bf16(back_norm((d_q, d_k, d_v, d_g), w_in, block))
+
+
+def back_sum(block, d_q, d_k, d_v, d_g, w_in, take, out):
+    out[...] = bf16(back_norm((d_q, d_k, d_v, d_g), w_in, block) + take[...].astype(F32))
 
 
 def packed_back(part, got, packed, d_resid, out, *halves):
@@ -605,27 +603,27 @@
     got_back_own, d_q = tie(got_back_own, d_q)
     (d_resid,) = run(resid_back, [row_b], [back_own, got_back_own, resid, d_out], name="resid_back")
     d_resid_near = near(d_resid)
-    own_grads = run(
+    give, *own_grads = run(
         attn_back_own,
-        [block_b, block_f, block_f, block_b],
-        [docs, d_resid, proj, attended, attn_out, d_k, d_v],
+        [row_b, block_b, block_f, block_f, block_b],
+        [docs, d_resid, proj, attended, attn_out, d_q, d_k, d_v, d_g, attn_in],
         name="attn_back_own",
     )
-    give, *d_projected = run(
+    take = near(give)
+    d_projected = run(
         attn_back_second,
-        [like((pair, width), BF16)] + [block_b] * 4,
-        [docs, d_resid_near, proj, attended, attn_out, d_q, d_g, *own_grads, attn_in],
+        [block_b] * 4,
+        [docs, d_resid_near, proj, attended, attn_out, *own_grads],
         [pltpu.VMEM((tensors, rows_dev, cols), F32)] * 2,
         name="attn_back_second",
     )
-    take = near(give)
-    (keep,) = run(
-        attn_back_keep,
-        [like((pair, width), F32)],
-        [*d_projected, attn_in],
-        name="attn_back_keep",
-    )
-    sum_far, sum_own = run(add_near, [row_b, row_b], [keep, take], name="add_near")
+
+    def back_part(body, block, more, name):
+        return run(functools.partial(body, block), [row_b], [*d_projected, attn_in, *more], name=name)[0]
+
+    sum_far = back_part(back_sum, 2, [take], "back_sum_far")
+    take = near(back_part(back_give, 1, [], "back_give"))
+    sum_own = back_part(back_sum, 0, [take], "back_sum_own")
     got_own = far(sum_far)
     got_far = far(sum_own)
     d_packed, *halves = run(
@@ -639,7 +637,7 @@
     half_rows = like((groups * capacity // 2, width), BF16)
     group_bits = [1 << b for b in range(groups.bit_length() - 1)]
     near_bit, pack_far, event_far = group_bits[0], group_bits[1 : packs.bit_length() - 1], group_bits[packs.bit_length() - 1 :]
-    back_bits = pack_far[::-1] + event_far[::-1] + [near_bit]
+    back_bits = pack_far[::-1] + [near_bit] + event_far[::-1]
     kept, back = run(
         functools.partial(back_send, order, back_bits[0]), [half_rows] * 2, [hot, d_packed], name="back_send"
     )
@@ -712,7 +710,7 @@
     kept1, send1 = start1((tuple(bits), event_bits[0]))
     send1, part0 = tie(send1, part0)
     part0, back_got = tie(part0, back_got)
-    kept0, send0 = start0((tuple(bits), pack_bits[0]))
+    kept0, send0 = start0((tuple(bits), event_bits[0]))
     arrays = [kept, back_got]
     held = {}
     for n, value in enumerate((0, back_bits[0])):
@@ -733,9 +731,8 @@
     for bit in back_bits[1:-1]:
         send_back(bit)
     kept1, got1 = reduce_over(event_bits + pack_bits, kept1, send1, "halve1_", True)
-    kept0, got0 = reduce_over(
-        pack_bits[:1] + event_bits + pack_bits[1:], kept0, send0, "halve0_"
-    )
+    kept0, got0 = reduce_over(event_bits + pack_bits, kept0, send0, "halve0_")
+    got1, hidden_own, place = tie(got1, hidden_own, place)
     send_back(back_bits[-1])
     back_places = [held[k] for k in range(groups)]
     got_out = far(out_far)

time: 115 us -> 114 us (level)
  waiting for transfers between devices: 47 us -> 43.6 us
  Pallas kernels: 26.7 us -> 28.3 us
    pallas_call x34 -> x35, Pallas kernels: 26.7 us -> 28.3 us  [run(): pl.pallas_call(body, out_shape=list(outs), in_specs=[pl.BlockSpec(memory_...]
    ppermute x16, waiting for transfers between devices: 20.2 us -> 18.8 us  [crossed(): return lax.ppermute(value, group_axes, [(i, i ^ k) for i in range(groups)])]
    ppermute x17 -> x18, waiting for transfers between devices: 5.39 us -> 4.45 us  [near(): return lax.ppermute(value, 'tensor', [(i, i ^ 1) for i in range(tensors)])]
    ppermute x17 -> x18, starting transfers between devices: 4.63 us -> 4.91 us  [near(): return lax.ppermute(value, 'tensor', [(i, i ^ 1) for i in range(tensors)])]
  transfers between devices with their start and end apart: 42 -> 43, of which waited for: 27 -> 26; matrix products, arithmetic and copies ran while one was open for 1% -> 1% of each run, Pallas kernels for 20% -> 24%
where the time goes in v10:
time: 114 us
  waiting for transfers between devices  43.6 us (38%)
  starting transfers between devices  39.1 us (34%)
  Pallas kernels  28.3 us (25%)
    pallas_call x35, Pallas kernels, run(): pl.pallas_call(body, out_shape=list(outs), in_specs=[pl.BlockSpec(memory_...  28.3 us
    ppermute x16, starting transfers between devices, crossed(): return lax.ppermute(value, group_axes, [(i, i ^ k) for i in range(groups)])  24.7 us
    ppermute x9, waiting for transfers between devices, far(): return lax.ppermute(value, 'tensor', [(i, i ^ 2) for i in range(tensors)])  20.4 us
    ppermute x16, waiting for transfers between devices, crossed(): return lax.ppermute(value, group_axes, [(i, i ^ k) for i in range(groups)])  18.8 us
    ppermute x9, starting transfers between devices, far(): return lax.ppermute(value, 'tensor', [(i, i ^ 2) for i in range(tensors)])  9.49 us
    ppermute x18, starting transfers between devices, near(): return lax.ppermute(value, 'tensor', [(i, i ^ 1) for i in range(tensors)])  4.91 us
    ppermute x18, waiting for transfers between devices, near(): return lax.ppermute(value, 'tensor', [(i, i ^ 1) for i in range(tensors)])  4.45 us
  transfers between devices with their start and end apart: 43, of which 26 were waited for; matrix products, arithmetic and copies ran while one was open for 1% of the time, Pallas kernels for 24%

profile of v10, /device:TPU:0, one launch (start us, length us, event | category | flops | bytes accessed | tf_op | source)
XLA Modules:
  0.0 113.7 jit_solution(14340692683810842812)
XLA Ops:
  0.6 0.5 collective-permute-start
  1.2 0.7 add_bitcast_fusion.code
  1.9 0.9 copy-done.7
  3.2 4.1 %collective-permute-start.2 = (bf16[24,1152]{1,0:T(8,128)(2,1)S(1)}, bf16[24,1152]{1,0:T(8,128)(2,1)S(1)}, u32[]{:S(2)}, u32[]{:S(2)}) collective-permute-start(bf16[24,1152]{1,0:T(8,128)(2,1)S(1)} %get-tuple-element.116), channel_id=1, source_target_pairs={{0,8},{4,12},{8,0},{12,4},{16,24},{20,28},{24,16},{28,20},{1,9},{5... | collective-permute-start | bytes 165896 | tf_op jit(solution)/shard_map/ppermute | solution.py:480
  7.3 1.3 %collective-permute-start.3 = (bf16[24,1152]{1,0:T(8,128)(2,1)S(1)}, bf16[24,1152]{1,0:T(8,128)(2,1)S(1)}, u32[]{:S(2)}, u32[]{:S(2)}) collective-permute-start(bf16[24,1152]{1,0:T(8,128)(2,1)S(1)} %get-tuple-element.117), channel_id=1, source_target_pairs={{0,24},{4,28},{8,16},{12,20},{16,8},{20,12},{24,0},{28,4},{1,25},{... | collective-permute-start | bytes 165896 | tf_op jit(solution)/shard_map/ppermute | solution.py:480
  8.6 3.6 %collective-permute-start.4 = (bf16[24,1152]{1,0:T(8,128)(2,1)S(1)}, bf16[24,1152]{1,0:T(8,128)(2,1)S(1)}, u32[]{:S(2)}, u32[]{:S(2)}) collective-permute-start(bf16[24,1152]{1,0:T(8,128)(2,1)S(1)} %get-tuple-element.124), channel_id=1, source_target_pairs={{0,12},{4,8},{8,4},{12,0},{16,28},{20,24},{24,20},{28,16},{1,13},{... | collective-permute-start | bytes 165896 | tf_op jit(solution)/shard_map/ppermute | solution.py:480
  12.2 0.6 collective-permute-start.5
  12.8 1.1 collective-permute-start.6
  13.9 2.2 %collective-permute-done.3.refs_2_ = bf16[24,1152]{1,0:T(8,128)(2,1)S(1)} collective-permute-done((bf16[24,1152]{1,0:T(8,128)(2,1)S(1)}, bf16[24,1152]{1,0:T(8,128)(2,1)S(1)}, u32[]{:S(2)}, u32[]{:S(2)}) %collective-permute-start.3) | collective-permute-done | bytes 55328 | tf_op jit(solution)/shard_map/ppermute | solution.py:480
  16.4 2.8 %collective-permute-done.5.refs_4_ = bf16[24,1152]{1,0:T(8,128)(2,1)S(1)} collective-permute-done((bf16[24,1152]{1,0:T(8,128)(2,1)S(1)}, bf16[24,1152]{1,0:T(8,128)(2,1)S(1)}, u32[]{:S(2)}, u32[]{:S(2)}) %collective-permute-start.5) | collective-permute-done | bytes 55328 | tf_op jit(solution)/shard_map/ppermute | solution.py:480
  19.2 1.9 %collective-permute-done.8.refs_7_ = bf16[24,1152]{1,0:T(8,128)(2,1)S(1)} collective-permute-done((bf16[24,1152]{1,0:T(8,128)(2,1)S(1)}, bf16[24,1152]{1,0:T(8,128)(2,1)S(1)}, u32[]{:S(2)}, u32[]{:S(2)}) %collective-permute-start.8) | collective-permute-done | bytes 55328 | tf_op jit(solution)/shard_map/ppermute | solution.py:480
  21.4 1.6 %collective-permute-start.9 = (bf16[128,1024]{1,0:T(8,128)(2,1)S(1)}, bf16[128,1024]{1,0:T(8,128)(2,1)S(1)}, u32[]{:S(2)}, u32[]{:S(2)}) collective-permute-start(bf16[128,1024]{1,0:T(8,128)(2,1)S(1)} %get-tuple-element.129.refs_0_.refs_3_), channel_id=1, source_target_pairs={{0,2},{1,3},{2,0},{3,1},{4,6},{5,7},{6,4},{7,5},{8,10},{9,11},{10,... | collective-permute-start | bytes 786440 | tf_op jit(solution)/shard_map/ppermute | solution.py:477
  23.0 0.5 collective-permute-start.11
  23.5 0.8 collective-permute-done.10.refs_1_.refs_4_
  24.5 2.2 %encode_first.1 = (f32[256,256]{1,0:T(8,128)S(1)}, bf16[256,1024]{1,0:T(8,128)(2,1)S(1)}, bf16[128,1024]{1,0:T(8,128)(2,1)S(1)}, bf16[4,2,128,256]{3,2,1,0:T(8,128)(2,1)S(1)}) custom-call(bf16[128,1024]{1,0:T(8,128)(2,1)S(1)} %get-tuple-element.129.refs_0_.refs_3_, bf16[64,1024]{1,0:T(8,128)(2,1)S(1)} %collective-permute-done.10.refs_1_.refs_4_, ...), custom_call_target="tpu_custom_call" | custom-call | tf_op jit(solution)/shard_map/encode_first/pallas_call | solution.py:64
  26.8 1.1 collective-permute-done.9.refs_0_.refs_5_
  27.8 0.5 collective-permute-start.12
  28.3 1.5 %collective-permute-start.15 = (bf16[128,1024]{1,0:T(8,128)(2,1)S(1)}, bf16[128,1024]{1,0:T(8,128)(2,1)S(1)}, u32[]{:S(2)}, u32[]{:S(2)}) collective-permute-start(bf16[128,1024]{1,0:T(8,128)(2,1)S(1)} %bitcast.5), channel_id=1, source_target_pairs={{0,2},{1,3},{2,0},{3,1},{4,6},{5,7},{6,4},{7,5},{8,10},{9,11},{10,... | collective-permute-start | bytes 786440 | tf_op jit(solution)/shard_map/ppermute | solution.py:477
  29.8 1.4 %encode_third.1 = (f32[128,256]{1,0:T(8,128)S(1)}, bf16[128,1024]{1,0:T(8,128)(2,1)S(1)}, bf16[128,1024]{1,0:T(8,128)(2,1)S(1)}, bf16[4,1,128,256]{3,2,1,0:T(8,128)(2,1)S(1)}) custom-call(bf16[128,1024]{1,0:T(8,128)(2,1)S(1)} %collective-permute-done.9.refs_0_.refs_5_, bf16[2,1024,1024]{2,1,0:T(8,128)(2,1)S(1)} %copy-done, bf16[4,1024,256]{2,1,0:T(8,128)(2,1)S(1)} %copy-done.1), custom_call_target="tpu_custom_call" | custom-call | tf_op jit(solution)/shard_map/encode_third/pallas_call | solution.py:64
  31.3 2.5 %attend_first.1 = (f32[256,256]{1,0:T(8,128)S(1)}, bf16[256,1024]{1,0:T(8,128)(2,1)S(1)}, bf16[4,4,128,256]{3,2,1,0:T(8,128)(2,1)S(1)}, f32[4,128,256]{2,1,0:T(8...) custom-call(s32[4,1,128]{2,1,0:T(1,128)S(1)} %bitcast.8, ...), custom_call_target="tpu_custom_call" | custom-call | tf_op jit(solution)/shard_map/attend_first/pallas_call | solution.py:64
  33.9 1.3 %collective-permute-done.13.take = bf16[256,256]{1,0:T(8,128)(2,1)S(1)} collective-permute-done((bf16[256,256]{1,0:T(8,128)(2,1)S(1)}, bf16[256,256]{1,0:T(8,128)(2,1)S(1)}, u32[]{:S(2)}, u32[]{:S(2)}) %collective-permute-start.13) | collective-permute-done | bytes 131104 | tf_op jit(solution)/shard_map/ppermute | solution.py:474
  35.6 0.5 collective-permute-start.17
  36.6 1.5 %collective-permute-start.16 = (bf16[128,1024]{1,0:T(8,128)(2,1)S(1)}, bf16[128,1024]{1,0:T(8,128)(2,1)S(1)}, u32[]{:S(2)}, u32[]{:S(2)}) collective-permute-start(bf16[128,1024]{1,0:T(8,128)(2,1)S(1)} %attn_out_own.1.part), channel_id=1, source_target_pairs={{0,2},{1,3},{2,0},{3,1},{4,6},{5,7},{6,4},{7,5},{8,10},{9,11},{10,... | collective-permute-start | bytes 786440 | tf_op jit(solution)/shard_map/ppermute | solution.py:477
  38.1 6.6 %collective-permute-done.17.got = bf16[128,1024]{1,0:T(8,128)(2,1)S(1)} collective-permute-done((bf16[128,1024]{1,0:T(8,128)(2,1)S(1)}, bf16[128,1024]{1,0:T(8,128)(2,1)S(1)}, u32[]{:S(2)}, u32[]{:S(2)}) %collective-permute-start.17) | collective-permute-done | bytes 262176 | tf_op jit(solution)/shard_map/ppermute | solution.py:477
  45.0 2.9 %ffn_own.1 = (bf16[128,1024]{1,0:T(8,128)(2,1)S(1)}, bf16[128,1024]{1,0:T(8,128)(2,1)S(1)}) custom-call(bf16[128,1024]{1,0:T(8,128)(2,1)S(1)} %get-tuple-element.145.rows_ref, bf16[128,1024]{1,0:T(8,128)(2,1)S(1)} %bitcast.6, bf16[2,1024,512]{2,1,0:T(8,128)(2,1)S(1)} %copy-done.4, bf16[2,1024,512]{2,1,0:T(8,128)(2,1)S(1)} %collective-permute-done.in_b, ...), custom_call_target="tpu_custom_call" | custom-call | tf_op jit(solution)/shard_map/ffn_own/pallas_call | solution.py:64
  47.9 1.7 %collective-permute-done.16.got = bf16[128,1024]{1,0:T(8,128)(2,1)S(1)} collective-permute-done((bf16[128,1024]{1,0:T(8,128)(2,1)S(1)}, bf16[128,1024]{1,0:T(8,128)(2,1)S(1)}, u32[]{:S(2)}, u32[]{:S(2)}) %collective-permute-start.16) | collective-permute-done | bytes 262176 | tf_op jit(solution)/shard_map/ppermute | solution.py:477
  49.6 0.5 collective-permute-start.19
  50.3 2.9 %ffn_far.1 = (bf16[128,1024]{1,0:T(8,128)(2,1)S(1)}, bf16[128,1024]{1,0:T(8,128)(2,1)S(1)}) custom-call(bf16[128,1024]{1,0:T(8,128)(2,1)S(1)} %get-tuple-element.152.rows_ref, bf16[128,1024]{1,0:T(8,128)(2,1)S(1)} %collective-permute-done.15.d_out_ref.d_out, bf16[2,1024,512]{2,1,0:T(8,128)(2,1)S(1)} %copy-done.4, ...), custom_call_target="tpu_custom_call" | custom-call | tf_op jit(solution)/shard_map/ffn_far/pallas_call | solution.py:64
  53.2 1.6 %collective-permute-start.18 = (bf16[128,1024]{1,0:T(8,128)(2,1)S(1)}, bf16[128,1024]{1,0:T(8,128)(2,1)S(1)}, u32[]{:S(2)}, u32[]{:S(2)}) collective-permute-start(bf16[128,1024]{1,0:T(8,128)(2,1)S(1)} %get-tuple-element.154.back), channel_id=1, source_target_pairs={{0,2},{1,3},{2,0},{3,1},{4,6},{5,7},{6,4},{7,5},{8,10},{9,11},{10,... | collective-permute-start | bytes 786440 | tf_op jit(solution)/shard_map/ppermute | solution.py:477
  54.8 4.0 %collective-permute-done.19.got = bf16[128,1024]{1,0:T(8,128)(2,1)S(1)} collective-permute-done((bf16[128,1024]{1,0:T(8,128)(2,1)S(1)}, bf16[128,1024]{1,0:T(8,128)(2,1)S(1)}, u32[]{:S(2)}, u32[]{:S(2)}) %collective-permute-start.19) | collective-permute-done | bytes 262176 | tf_op jit(solution)/shard_map/ppermute | solution.py:477
  59.2 0.5 collective-permute-start.21
  59.7 0.8 collective-permute-done.20.fourth_a
  60.7 2.0 %attn_back_first.1 = (bf16[4,128,256]{2,1,0:T(8,128)(2,1)S(1)}, f32[4,128,256]{2,1,0:T(8,128)S(1)}, f32[4,128,256]{2,1,0:T(8,128)S(1)}, bf16[4,128,256]{2,1,0:T(8,128)(2,1)S(1)}) custom-call(s32[4,1,128]{2,1,0:T(1,128)S(1)} %bitcast.9, bf16[128,1024]{1,0:T(8,128)(2,1)S(1)} %get-tuple-element.156.third.d_resid, ...), custom_call_target="tpu_custom_call" | custom-call | tf_op jit(solution)/shard_map/attn_back_first/pallas_call | solution.py:64
  63.4 2.0 %attn_back_own.1 = (bf16[128,1024]{1,0:T(8,128)(2,1)S(1)}, bf16[4,128,256]{2,1,0:T(8,128)(2,1)S(1)}, f32[4,128,256]{2,1,0:T(8,128)S(1)}, f32[4,128,256]{2,1,0:T(8,128)S(1)}, bf16[4,128,256]{2,1,0:T(8,128)(2,1)S(1)}) custom-call(s32[4,1,128]{2,1,0:T(1,128)S(1)} %bitcast.10, bf16[128,1024]{1,0:T(8,128)(2,1)S(1)} %resid_back.1.first.d_resid, ...), custom_call_target="tpu_custom_call" | custom-call | tf_op jit(solution)/shard_map/attn_back_own/pallas_call | solution.py:64
  65.7 1.0 attn_back_second.1
  66.7 0.8 back_give.1
  67.9 0.8 back_sum_far.1.part
  69.1 0.8 back_sum_own.1.part
  69.9 1.7 %collective-permute-start.25 = (bf16[128,1024]{1,0:T(8,128)(2,1)S(1)}, bf16[128,1024]{1,0:T(8,128)(2,1)S(1)}, u32[]{:S(2)}, u32[]{:S(2)}) collective-permute-start(bf16[128,1024]{1,0:T(8,128)(2,1)S(1)} %back_sum_own.1.part), channel_id=1, source_target_pairs={{0,2},{1,3},{2,0},{3,1},{4,6},{5,7},{6,4},{7,5},{8,10},{9,11},{10,... | collective-permute-start | bytes 786440 | tf_op jit(solution)/shard_map/ppermute | solution.py:477
  71.6 6.2 %collective-permute-done.26.got = bf16[128,1024]{1,0:T(8,128)(2,1)S(1)} collective-permute-done((bf16[128,1024]{1,0:T(8,128)(2,1)S(1)}, bf16[128,1024]{1,0:T(8,128)(2,1)S(1)}, u32[]{:S(2)}, u32[]{:S(2)}) %collective-permute-start.26) | collective-permute-done | bytes 262176 | tf_op jit(solution)/shard_map/ppermute | solution.py:477
  78.2 0.5 collective-permute-start.28
  79.0 2.3 %collective-permute-start.35 = (bf16[96,1024]{1,0:T(8,128)(2,1)S(1)}, bf16[96,1024]{1,0:T(8,128)(2,1)S(1)}, u32[]{:S(2)}, u32[]{:S(2)}) collective-permute-start(bf16[96,1024]{1,0:T(8,128)(2,1)S(1)} %get-tuple-element.203), channel_id=1, source_target_pairs={{0,8},{4,12},{8,0},{12,4},{16,24},{20,28},{24,16},{28,20},{1,9},{5... | collective-permute-start | bytes 589832 | tf_op jit(solution)/shard_map/ppermute | solution.py:480
  81.3 1.0 enc_grads_first.1
  82.3 0.5 collective-permute-done.25.got
  83.1 0.5 collective-permute-start.30
  83.7 0.4 collective-permute-start.32
  85.1 0.5 enc_grad1_second.1
  85.6 1.7 %collective-permute-start.33 = (bf16[4,128,256]{2,1,0:T(8,128)(2,1)S(1)}, bf16[4,128,256]{2,1,0:T(8,128)(2,1)S(1)}, u32[]{:S(2)}, u32[]{:S(2)}) collective-permute-start(bf16[4,128,256]{2,1,0:T(8,128)(2,1)S(1)} %get-tuple-element.197), channel_id=1, source_target_pairs={{0,16},{4,20},{8,24},{12,28},{16,0},{20,4},{24,8},{28,12},{1,17},{... | collective-permute-start | bytes 786440 | tf_op jit(solution)/shard_map/ppermute | solution.py:480
  87.3 3.8 %collective-permute-done.35.refs_1_ = bf16[96,1024]{1,0:T(8,128)(2,1)S(1)} collective-permute-done((bf16[96,1024]{1,0:T(8,128)(2,1)S(1)}, bf16[96,1024]{1,0:T(8,128)(2,1)S(1)}, u32[]{:S(2)}, u32[]{:S(2)}) %collective-permute-start.35) | collective-permute-done | bytes 196640 | tf_op jit(solution)/shard_map/ppermute | solution.py:480
  91.0 1.0 enc_grad0_second.1
  92.1 1.4 %collective-permute-start.38 = (bf16[4,128,256]{2,1,0:T(8,128)(2,1)S(1)}, bf16[4,128,256]{2,1,0:T(8,128)(2,1)S(1)}, u32[]{:S(2)}, u32[]{:S(2)}) collective-permute-start(bf16[4,128,256]{2,1,0:T(8,128)(2,1)S(1)} %get-tuple-element.213), channel_id=1, source_target_pairs={{0,16},{4,20},{8,24},{12,28},{16,0},{20,4},{24,8},{28,12},{1,17},{... | collective-permute-start | bytes 786440 | tf_op jit(solution)/shard_map/ppermute | solution.py:480
  93.5 0.7 collective-permute-done.33.got
  94.3 2.4 %collective-permute-start.34 = (bf16[2,128,256]{2,1,0:T(8,128)(2,1)S(1)}, bf16[2,128,256]{2,1,0:T(8,128)(2,1)S(1)}, u32[]{:S(2)}, u32[]{:S(2)}) collective-permute-start(bf16[2,128,256]{2,1,0:T(8,128)(2,1)S(1)} %get-tuple-element.199), channel_id=1, source_target_pairs={{0,4},{4,0},{8,12},{12,8},{16,20},{20,16},{24,28},{28,24},{1,5},{5... | collective-permute-start | bytes 393224 | tf_op jit(solution)/shard_map/ppermute | solution.py:480
  96.7 0.5 ffn_out_far.1
  97.3 2.6 %collective-permute-done.38.got = bf16[4,128,256]{2,1,0:T(8,128)(2,1)S(1)} collective-permute-done((bf16[4,128,256]{2,1,0:T(8,128)(2,1)S(1)}, bf16[4,128,256]{2,1,0:T(8,128)(2,1)S(1)}, u32[]{:S(2)}, u32[]{:S(2)}) %collective-permute-start.38) | collective-permute-done | bytes 262176 | tf_op jit(solution)/shard_map/ppermute | solution.py:480
  100.0 1.7 %collective-permute-start.39 = (bf16[2,128,256]{2,1,0:T(8,128)(2,1)S(1)}, bf16[2,128,256]{2,1,0:T(8,128)(2,1)S(1)}, u32[]{:S(2)}, u32[]{:S(2)}) collective-permute-start(bf16[2,128,256]{2,1,0:T(8,128)(2,1)S(1)} %get-tuple-element.215), channel_id=1, source_target_pairs={{0,4},{4,0},{8,12},{12,8},{16,20},{20,16},{24,28},{28,24},{1,5},{5... | collective-permute-start | bytes 393224 | tf_op jit(solution)/shard_map/ppermute | solution.py:480
  101.7 1.9 %collective-permute-done.34.got = bf16[2,128,256]{2,1,0:T(8,128)(2,1)S(1)} collective-permute-done((bf16[2,128,256]{2,1,0:T(8,128)(2,1)S(1)}, bf16[2,128,256]{2,1,0:T(8,128)(2,1)S(1)}, u32[]{:S(2)}, u32[]{:S(2)}) %collective-permute-start.34) | collective-permute-done | bytes 131104 | tf_op jit(solution)/shard_map/ppermute | solution.py:480
  103.7 2.3 %collective-permute-start.37 = (bf16[1,128,256]{2,1,0:T(8,128)(2,1)S(1)}, bf16[1,128,256]{2,1,0:T(8,128)(2,1)S(1)}, u32[]{:S(2)}, u32[]{:S(2)}) collective-permute-start(bf16[1,128,256]{2,1,0:T(8,128)(2,1)S(1)} %get-tuple-element.206), channel_id=1, source_target_pairs={{0,8},{4,12},{8,0},{12,4},{16,24},{20,28},{24,16},{28,20},{1,9},{5... | collective-permute-start | bytes 196616 | tf_op jit(solution)/shard_map/ppermute | solution.py:480
  106.0 0.4 collective-permute-done.39.got
  106.4 1.9 %collective-permute-start.40 = (bf16[1,128,256]{2,1,0:T(8,128)(2,1)S(1)}, bf16[1,128,256]{2,1,0:T(8,128)(2,1)S(1)}, u32[]{:S(2)}, u32[]{:S(2)}) collective-permute-start(bf16[1,128,256]{2,1,0:T(8,128)(2,1)S(1)} %get-tuple-element.216), channel_id=1, source_target_pairs={{0,8},{4,12},{8,0},{12,4},{16,24},{20,28},{24,16},{28,20},{1,9},{5... | collective-permute-start | bytes 196616 | tf_op jit(solution)/shard_map/ppermute | solution.py:480
  108.3 2.5 %collective-permute-done.37.got1 = bf16[1,128,256]{2,1,0:T(8,128)(2,1)S(1)} collective-permute-done((bf16[1,128,256]{2,1,0:T(8,128)(2,1)S(1)}, bf16[1,128,256]{2,1,0:T(8,128)(2,1)S(1)}, u32[]{:S(2)}, u32[]{:S(2)}) %collective-permute-start.37) | collective-permute-done | bytes 65568 | tf_op jit(solution)/shard_map/ppermute | solution.py:480
  110.8 1.2 %ffn_out_own.1 = bf16[128,1024]{1,0:T(8,128)(2,1)} custom-call(bf16[128,1024]{1,0:T(8,128)(2,1)S(1)} %get-tuple-element.217.hidden, bf16[512,1024]{1,0:T(8,128)(2,1)S(1)} %copy-done.2, bf16[512,1024]{1,0:T(8,128)(2,1)S(1)} %collective-permute-done.1.out_b.w_b, bf16[128,1024]{1,0:T(8,128)(2,1)S(1)} %get-tuple-element.163.resid, ...), custom_call_target="tpu_custom_call" | custom-call | tf_op jit(solution)/shard_map/ffn_out_own/pallas_call | solution.py:64
  112.0 1.0 back_recv.1
  112.9 0.7 finish.1
  (74 shorter events, 7.3 us)
Async XLA Ops:
  0.6 7.9 %collective-permute-start = (bf16[2,1024,512]{2,1,0:T(8,128)(2,1)}, bf16[2,1024,512]{2,1,0:T(8,128)(2,1)S(1)}, u32[]{:S(2)}, u32[]{:S(2)}) collective-permute-start(bf16[2,1024,512]{2,1,0:T(8,128)(2,1)} %in_a.3), channel_id=1, source_target_pairs={{0,1},{1,0},{2,3},{3,2},{4,5},{5,4},{6,7},{7,6},{8,9},{9,8},{10,11... | collective-permute-start | bytes 6291464 | tf_op jit(solution)/shard_map/ppermute | solution.py:474
  1.1 7.4 %collective-permute-start.1 = (bf16[512,1024]{1,0:T(8,128)(2,1)}, bf16[512,1024]{1,0:T(8,128)(2,1)S(1)}, u32[]{:S(2)}, u32[]{:S(2)}) collective-permute-start(bf16[512,1024]{1,0:T(8,128)(2,1)} %w_a.3), channel_id=1, source_target_pairs={{0,1},{1,0},{2,3},{3,2},{4,5},{5,4},{6,7},{7,6},{8,9},{9,8},{10,11... | collective-permute-start | bytes 3145736 | tf_op jit(solution)/shard_map/ppermute | solution.py:474
  1.9 0.9 copy-start.7
  2.9 21.6 %copy-start = (bf16[2,1024,1024]{2,1,0:T(8,128)(2,1)S(1)}, bf16[2,1024,1024]{2,1,0:T(8,128)(2,1)}, u32[]{:S(2)}) copy-start(bf16[2,1024,1024]{2,1,0:T(8,128)(2,1)} %refs_8_.3) | copy-start | bytes 12582916
  2.9 21.6 %copy-start.1 = (bf16[4,1024,256]{2,1,0:T(8,128)(2,1)S(1)}, bf16[4,1024,256]{2,1,0:T(8,128)(2,1)}, u32[]{:S(2)}) copy-start(bf16[4,1024,256]{2,1,0:T(8,128)(2,1)} %w_in.9) | copy-start | bytes 6291460
  3.2 10.6 %collective-permute-start.2 = (bf16[24,1152]{1,0:T(8,128)(2,1)S(1)}, bf16[24,1152]{1,0:T(8,128)(2,1)S(1)}, u32[]{:S(2)}, u32[]{:S(2)}) collective-permute-start(bf16[24,1152]{1,0:T(8,128)(2,1)S(1)} %get-tuple-element.116), channel_id=1, source_target_pairs={{0,8},{4,12},{8,0},{12,4},{16,24},{20,28},{24,16},{28,20},{1,9},{5... | collective-permute-start | bytes 165896 | tf_op jit(solution)/shard_map/ppermute | solution.py:480
  7.3 8.8 %collective-permute-start.3 = (bf16[24,1152]{1,0:T(8,128)(2,1)S(1)}, bf16[24,1152]{1,0:T(8,128)(2,1)S(1)}, u32[]{:S(2)}, u32[]{:S(2)}) collective-permute-start(bf16[24,1152]{1,0:T(8,128)(2,1)S(1)} %get-tuple-element.117), channel_id=1, source_target_pairs={{0,24},{4,28},{8,16},{12,20},{16,8},{20,12},{24,0},{28,4},{1,25},{... | collective-permute-start | bytes 165896 | tf_op jit(solution)/shard_map/ppermute | solution.py:480
  8.6 7.8 %collective-permute-start.4 = (bf16[24,1152]{1,0:T(8,128)(2,1)S(1)}, bf16[24,1152]{1,0:T(8,128)(2,1)S(1)}, u32[]{:S(2)}, u32[]{:S(2)}) collective-permute-start(bf16[24,1152]{1,0:T(8,128)(2,1)S(1)} %get-tuple-element.124), channel_id=1, source_target_pairs={{0,12},{4,8},{8,4},{12,0},{16,28},{20,24},{24,20},{28,16},{1,13},{... | collective-permute-start | bytes 165896 | tf_op jit(solution)/shard_map/ppermute | solution.py:480
  12.2 7.0 %collective-permute-start.5 = (bf16[24,1152]{1,0:T(8,128)(2,1)S(1)}, bf16[24,1152]{1,0:T(8,128)(2,1)S(1)}, u32[]{:S(2)}, u32[]{:S(2)}) collective-permute-start(bf16[24,1152]{1,0:T(8,128)(2,1)S(1)} %get-tuple-element.125), channel_id=1, source_target_pairs={{0,28},{4,24},{8,20},{12,16},{16,12},{20,8},{24,4},{28,0},{1,29},{... | collective-permute-start | bytes 165896 | tf_op jit(solution)/shard_map/ppermute | solution.py:480
  12.8 6.4 %collective-permute-start.6 = (bf16[24,1152]{1,0:T(8,128)(2,1)S(1)}, bf16[24,1152]{1,0:T(8,128)(2,1)S(1)}, u32[]{:S(2)}, u32[]{:S(2)}) collective-permute-start(bf16[24,1152]{1,0:T(8,128)(2,1)S(1)} %get-tuple-element.126), channel_id=1, source_target_pairs={{0,16},{4,20},{8,24},{12,28},{16,0},{20,4},{24,8},{28,12},{1,17},{... | collective-permute-start | bytes 165896 | tf_op jit(solution)/shard_map/ppermute | solution.py:480
  13.9 5.3 %collective-permute-start.7 = (bf16[24,1152]{1,0:T(8,128)(2,1)S(1)}, bf16[24,1152]{1,0:T(8,128)(2,1)S(1)}, u32[]{:S(2)}, u32[]{:S(2)}) collective-permute-start(bf16[24,1152]{1,0:T(8,128)(2,1)S(1)} %get-tuple-element.127), channel_id=1, source_target_pairs={{0,4},{4,0},{8,12},{12,8},{16,20},{20,16},{24,28},{28,24},{1,5},{5... | collective-permute-start | bytes 165896 | tf_op jit(solution)/shard_map/ppermute | solution.py:480
  16.1 5.1 %collective-permute-start.8 = (bf16[24,1152]{1,0:T(8,128)(2,1)S(1)}, bf16[24,1152]{1,0:T(8,128)(2,1)S(1)}, u32[]{:S(2)}, u32[]{:S(2)}) collective-permute-start(bf16[24,1152]{1,0:T(8,128)(2,1)S(1)} %get-tuple-element.128), channel_id=1, source_target_pairs={{0,20},{4,16},{8,28},{12,24},{16,4},{20,0},{24,12},{28,8},{1,21},{... | collective-permute-start | bytes 165896 | tf_op jit(solution)/shard_map/ppermute | solution.py:480
  21.4 6.4 %collective-permute-start.9 = (bf16[128,1024]{1,0:T(8,128)(2,1)S(1)}, bf16[128,1024]{1,0:T(8,128)(2,1)S(1)}, u32[]{:S(2)}, u32[]{:S(2)}) collective-permute-start(bf16[128,1024]{1,0:T(8,128)(2,1)S(1)} %get-tuple-element.129.refs_0_.refs_3_), channel_id=1, source_target_pairs={{0,2},{1,3},{2,0},{3,1},{4,6},{5,7},{6,4},{7,5},{8,10},{9,11},{10,... | collective-permute-start | bytes 786440 | tf_op jit(solution)/shard_map/ppermute | solution.py:477
  23.0 1.3 %collective-permute-start.10 = (bf16[64,1024]{1,0:T(8,128)(2,1)S(1)}, bf16[64,1024]{1,0:T(8,128)(2,1)S(1)}, u32[]{:S(2)}, u32[]{:S(2)}) collective-permute-start(bf16[64,1024]{1,0:T(8,128)(2,1)S(1)} %get-tuple-element.130), channel_id=1, source_target_pairs={{0,1},{1,0},{2,3},{3,2},{4,5},{5,4},{6,7},{7,6},{8,9},{9,8},{10,11... | collective-permute-start | bytes 393224 | tf_op jit(solution)/shard_map/ppermute | solution.py:474
  23.0 4.9 %copy-start.3 = (bf16[256,1024]{1,0:T(8,128)(2,1)S(1)}, bf16[256,1024]{1,0:T(8,128)(2,1)}, u32[]{:S(2)}) copy-start(bf16[256,1024]{1,0:T(8,128)(2,1)} %w_out.5) | copy-start | bytes 1572868
  23.0 5.4 %copy-start.5 = (bf16[1,128,1024]{2,1,0:T(8,128)(2,1)S(1)}, bf16[1,128,1024]{2,1,0:T(8,128)(2,1)}, u32[]{:S(2)}) copy-start(bf16[1,128,1024]{2,1,0:T(8,128)(2,1)} %param.19) | copy-start | bytes 786436
  23.0 1.5 %collective-permute-start.11 = (bf16[64,1024]{1,0:T(8,128)(2,1)S(1)}, bf16[64,1024]{1,0:T(8,128)(2,1)S(1)}, u32[]{:S(2)}, u32[]{:S(2)}) collective-permute-start(bf16[64,1024]{1,0:T(8,128)(2,1)S(1)} %get-tuple-element.131), channel_id=1, source_target_pairs={{0,1},{1,0},{2,3},{3,2},{4,5},{5,4},{6,7},{7,6},{8,9},{9,8},{10,11... | collective-permute-start | bytes 393224 | tf_op jit(solution)/shard_map/ppermute | solution.py:474
  27.8 3.4 %copy-start.6 = (s32[1,512]{1,0:T(1,128)S(1)}, s32[1,512]{1,0:T(1,128)}, u32[]{:S(2)}) copy-start(s32[1,512]{1,0:T(1,128)} %param.13) | copy-start | bytes 6148
  27.8 7.4 %collective-permute-start.14 = (bf16[256,1024]{1,0:T(8,128)(2,1)S(1)}, bf16[256,1024]{1,0:T(8,128)(2,1)S(1)}, u32[]{:S(2)}, u32[]{:S(2)}) collective-permute-start(bf16[256,1024]{1,0:T(8,128)(2,1)S(1)} %copy-done.3), channel_id=1, source_target_pairs={{0,1},{1,0},{2,3},{3,2},{4,5},{5,4},{6,7},{7,6},{8,9},{9,8},{10,11... | collective-permute-start | bytes 1572872 | tf_op jit(solution)/shard_map/ppermute | solution.py:474
  27.8 3.4 %collective-permute-start.12 = (bf16[128,1024]{1,0:T(8,128)(2,1)S(1)}, bf16[128,1024]{1,0:T(8,128)(2,1)S(1)}, u32[]{:S(2)}, u32[]{:S(2)}) collective-permute-start(bf16[128,1024]{1,0:T(8,128)(2,1)S(1)} %collective-permute-done.9.refs_0_.refs_5_), channel_id=1, source_target_pairs={{0,1},{1,0},{2,3},{3,2},{4,5},{5,4},{6,7},{7,6},{8,9},{9,8},{10,11... | collective-permute-start | bytes 786440 | tf_op jit(solution)/shard_map/ppermute | solution.py:474
  28.3 8.3 %collective-permute-start.15 = (bf16[128,1024]{1,0:T(8,128)(2,1)S(1)}, bf16[128,1024]{1,0:T(8,128)(2,1)S(1)}, u32[]{:S(2)}, u32[]{:S(2)}) collective-permute-start(bf16[128,1024]{1,0:T(8,128)(2,1)S(1)} %bitcast.5), channel_id=1, source_target_pairs={{0,2},{1,3},{2,0},{3,1},{4,6},{5,7},{6,4},{7,5},{8,10},{9,11},{10,... | collective-permute-start | bytes 786440 | tf_op jit(solution)/shard_map/ppermute | solution.py:477
  33.8 11.2 %copy-start.2 = (bf16[512,1024]{1,0:T(8,128)(2,1)S(1)}, bf16[512,1024]{1,0:T(8,128)(2,1)}, u32[]{:S(2)}) copy-start(bf16[512,1024]{1,0:T(8,128)(2,1)} %w_a.3) | copy-start | bytes 3145732
  33.8 11.2 %copy-start.4 = (bf16[2,1024,512]{2,1,0:T(8,128)(2,1)S(1)}, bf16[2,1024,512]{2,1,0:T(8,128)(2,1)}, u32[]{:S(2)}) copy-start(bf16[2,1024,512]{2,1,0:T(8,128)(2,1)} %in_a.3) | copy-start | bytes 6291460
  33.8 1.4 %collective-permute-start.13 = (bf16[256,256]{1,0:T(8,128)(2,1)S(1)}, bf16[256,256]{1,0:T(8,128)(2,1)S(1)}, u32[]{:S(2)}, u32[]{:S(2)}) collective-permute-start(bf16[256,256]{1,0:T(8,128)(2,1)S(1)} %get-tuple-element.140), channel_id=1, source_target_pairs={{0,1},{1,0},{2,3},{3,2},{4,5},{5,4},{6,7},{7,6},{8,9},{9,8},{10,11... | collective-permute-start | bytes 393224 | tf_op jit(solution)/shard_map/ppermute | solution.py:474
  35.6 9.2 %collective-permute-start.17 = (bf16[128,1024]{1,0:T(8,128)(2,1)S(1)}, bf16[128,1024]{1,0:T(8,128)(2,1)S(1)}, u32[]{:S(2)}, u32[]{:S(2)}) collective-permute-start(bf16[128,1024]{1,0:T(8,128)(2,1)S(1)} %attn_out_far.1.part), channel_id=1, source_target_pairs={{0,2},{1,3},{2,0},{3,1},{4,6},{5,7},{6,4},{7,5},{8,10},{9,11},{10,... | collective-permute-start | bytes 786440 | tf_op jit(solution)/shard_map/ppermute | solution.py:477
  36.6 13.0 %collective-permute-start.16 = (bf16[128,1024]{1,0:T(8,128)(2,1)S(1)}, bf16[128,1024]{1,0:T(8,128)(2,1)S(1)}, u32[]{:S(2)}, u32[]{:S(2)}) collective-permute-start(bf16[128,1024]{1,0:T(8,128)(2,1)S(1)} %attn_out_own.1.part), channel_id=1, source_target_pairs={{0,2},{1,3},{2,0},{3,1},{4,6},{5,7},{6,4},{7,5},{8,10},{9,11},{10,... | collective-permute-start | bytes 786440 | tf_op jit(solution)/shard_map/ppermute | solution.py:477
  49.6 9.2 %collective-permute-start.19 = (bf16[128,1024]{1,0:T(8,128)(2,1)S(1)}, bf16[128,1024]{1,0:T(8,128)(2,1)S(1)}, u32[]{:S(2)}, u32[]{:S(2)}) collective-permute-start(bf16[128,1024]{1,0:T(8,128)(2,1)S(1)} %get-tuple-element.149.back), channel_id=1, source_target_pairs={{0,2},{1,3},{2,0},{3,1},{4,6},{5,7},{6,4},{7,5},{8,10},{9,11},{10,... | collective-permute-start | bytes 786440 | tf_op jit(solution)/shard_map/ppermute | solution.py:477
  53.2 9.6 %collective-permute-start.18 = (bf16[128,1024]{1,0:T(8,128)(2,1)S(1)}, bf16[128,1024]{1,0:T(8,128)(2,1)S(1)}, u32[]{:S(2)}, u32[]{:S(2)}) collective-permute-start(bf16[128,1024]{1,0:T(8,128)(2,1)S(1)} %get-tuple-element.154.back), channel_id=1, source_target_pairs={{0,2},{1,3},{2,0},{3,1},{4,6},{5,7},{6,4},{7,5},{8,10},{9,11},{10,... | collective-permute-start | bytes 786440 | tf_op jit(solution)/shard_map/ppermute | solution.py:477
  59.1 1.4 %collective-permute-start.20 = (bf16[64,1024]{1,0:T(8,128)(2,1)S(1)}, bf16[64,1024]{1,0:T(8,128)(2,1)S(1)}, u32[]{:S(2)}, u32[]{:S(2)}) collective-permute-start(bf16[64,1024]{1,0:T(8,128)(2,1)S(1)} %get-tuple-element.157), channel_id=1, source_target_pairs={{0,1},{1,0},{2,3},{3,2},{4,5},{5,4},{6,7},{7,6},{8,9},{9,8},{10,11... | collective-permute-start | bytes 393224 | tf_op jit(solution)/shard_map/ppermute | solution.py:474
  59.2 1.5 %collective-permute-start.21 = (bf16[64,1024]{1,0:T(8,128)(2,1)S(1)}, bf16[64,1024]{1,0:T(8,128)(2,1)S(1)}, u32[]{:S(2)}, u32[]{:S(2)}) collective-permute-start(bf16[64,1024]{1,0:T(8,128)(2,1)S(1)} %get-tuple-element.158), channel_id=1, source_target_pairs={{0,1},{1,0},{2,3},{3,2},{4,5},{5,4},{6,7},{7,6},{8,9},{9,8},{10,11... | collective-permute-start | bytes 393224 | tf_op jit(solution)/shard_map/ppermute | solution.py:474
  63.0 2.6 %collective-permute-start.22 = (bf16[128,1024]{1,0:T(8,128)(2,1)S(1)}, bf16[128,1024]{1,0:T(8,128)(2,1)S(1)}, u32[]{:S(2)}, u32[]{:S(2)}) collective-permute-start(bf16[128,1024]{1,0:T(8,128)(2,1)S(1)} %resid_back.1.first.d_resid), channel_id=1, source_target_pairs={{0,1},{1,0},{2,3},{3,2},{4,5},{5,4},{6,7},{7,6},{8,9},{9,8},{10,11... | collective-permute-start | bytes 786440 | tf_op jit(solution)/shard_map/ppermute | solution.py:474
  65.4 2.5 %collective-permute-start.23 = (bf16[128,1024]{1,0:T(8,128)(2,1)S(1)}, bf16[128,1024]{1,0:T(8,128)(2,1)S(1)}, u32[]{:S(2)}, u32[]{:S(2)}) collective-permute-start(bf16[128,1024]{1,0:T(8,128)(2,1)S(1)} %get-tuple-element.176), channel_id=1, source_target_pairs={{0,1},{1,0},{2,3},{3,2},{4,5},{5,4},{6,7},{7,6},{8,9},{9,8},{10,11... | collective-permute-start | bytes 786440 | tf_op jit(solution)/shard_map/ppermute | solution.py:474
  67.5 1.6 %collective-permute-start.24 = (bf16[128,1024]{1,0:T(8,128)(2,1)S(1)}, bf16[128,1024]{1,0:T(8,128)(2,1)S(1)}, u32[]{:S(2)}, u32[]{:S(2)}) collective-permute-start(bf16[128,1024]{1,0:T(8,128)(2,1)S(1)} %back_give.1), channel_id=1, source_target_pairs={{0,1},{1,0},{2,3},{3,2},{4,5},{5,4},{6,7},{7,6},{8,9},{9,8},{10,11... | collective-permute-start | bytes 786440 | tf_op jit(solution)/shard_map/ppermute | solution.py:474
  68.7 9.2 %collective-permute-start.26 = (bf16[128,1024]{1,0:T(8,128)(2,1)S(1)}, bf16[128,1024]{1,0:T(8,128)(2,1)S(1)}, u32[]{:S(2)}, u32[]{:S(2)}) collective-permute-start(bf16[128,1024]{1,0:T(8,128)(2,1)S(1)} %back_sum_far.1.part), channel_id=1, source_target_pairs={{0,2},{1,3},{2,0},{3,1},{4,6},{5,7},{6,4},{7,5},{8,10},{9,11},{10,... | collective-permute-start | bytes 786440 | tf_op jit(solution)/shard_map/ppermute | solution.py:477
  69.9 12.9 %collective-permute-start.25 = (bf16[128,1024]{1,0:T(8,128)(2,1)S(1)}, bf16[128,1024]{1,0:T(8,128)(2,1)S(1)}, u32[]{:S(2)}, u32[]{:S(2)}) collective-permute-start(bf16[128,1024]{1,0:T(8,128)(2,1)S(1)} %back_sum_own.1.part), channel_id=1, source_target_pairs={{0,2},{1,3},{2,0},{3,1},{4,6},{5,7},{6,4},{7,5},{8,10},{9,11},{10,... | collective-permute-start | bytes 786440 | tf_op jit(solution)/shard_map/ppermute | solution.py:477
  78.2 3.1 %collective-permute-start.27 = (bf16[64,1024]{1,0:T(8,128)(2,1)S(1)}, bf16[64,1024]{1,0:T(8,128)(2,1)S(1)}, u32[]{:S(2)}, u32[]{:S(2)}) collective-permute-start(bf16[64,1024]{1,0:T(8,128)(2,1)S(1)} %get-tuple-element.178), channel_id=1, source_target_pairs={{0,1},{1,0},{2,3},{3,2},{4,5},{5,4},{6,7},{7,6},{8,9},{9,8},{10,11... | collective-permute-start | bytes 393224 | tf_op jit(solution)/shard_map/ppermute | solution.py:474
  78.2 3.1 %collective-permute-start.28 = (bf16[64,1024]{1,0:T(8,128)(2,1)S(1)}, bf16[64,1024]{1,0:T(8,128)(2,1)S(1)}, u32[]{:S(2)}, u32[]{:S(2)}) collective-permute-start(bf16[64,1024]{1,0:T(8,128)(2,1)S(1)} %get-tuple-element.179), channel_id=1, source_target_pairs={{0,1},{1,0},{2,3},{3,2},{4,5},{5,4},{6,7},{7,6},{8,9},{9,8},{10,11... | collective-permute-start | bytes 393224 | tf_op jit(solution)/shard_map/ppermute | solution.py:474
  79.0 12.1 %collective-permute-start.35 = (bf16[96,1024]{1,0:T(8,128)(2,1)S(1)}, bf16[96,1024]{1,0:T(8,128)(2,1)S(1)}, u32[]{:S(2)}, u32[]{:S(2)}) collective-permute-start(bf16[96,1024]{1,0:T(8,128)(2,1)S(1)} %get-tuple-element.203), channel_id=1, source_target_pairs={{0,8},{4,12},{8,0},{12,4},{16,24},{20,28},{24,16},{28,20},{1,9},{5... | collective-permute-start | bytes 589832 | tf_op jit(solution)/shard_map/ppermute | solution.py:480
  83.1 1.3 %collective-permute-start.29 = (bf16[32,1024]{1,0:T(8,128)(2,1)S(1)}, bf16[32,1024]{1,0:T(8,128)(2,1)S(1)}, u32[]{:S(2)}, u32[]{:S(2)}) collective-permute-start(bf16[32,1024]{1,0:T(8,128)(2,1)S(1)} %get-tuple-element.188), channel_id=1, source_target_pairs={{0,1},{1,0},{2,3},{3,2},{4,5},{5,4},{6,7},{7,6},{8,9},{9,8},{10,11... | collective-permute-start | bytes 196616 | tf_op jit(solution)/shard_map/ppermute | solution.py:474
  83.1 1.4 %collective-permute-start.30 = (bf16[32,1024]{1,0:T(8,128)(2,1)S(1)}, bf16[32,1024]{1,0:T(8,128)(2,1)S(1)}, u32[]{:S(2)}, u32[]{:S(2)}) collective-permute-start(bf16[32,1024]{1,0:T(8,128)(2,1)S(1)} %get-tuple-element.189), channel_id=1, source_target_pairs={{0,1},{1,0},{2,3},{3,2},{4,5},{5,4},{6,7},{7,6},{8,9},{9,8},{10,11... | collective-permute-start | bytes 196616 | tf_op jit(solution)/shard_map/ppermute | solution.py:474
  83.6 1.3 %collective-permute-start.31 = (bf16[32,1024]{1,0:T(8,128)(2,1)S(1)}, bf16[32,1024]{1,0:T(8,128)(2,1)S(1)}, u32[]{:S(2)}, u32[]{:S(2)}) collective-permute-start(bf16[32,1024]{1,0:T(8,128)(2,1)S(1)} %get-tuple-element.190), channel_id=1, source_target_pairs={{0,1},{1,0},{2,3},{3,2},{4,5},{5,4},{6,7},{7,6},{8,9},{9,8},{10,11... | collective-permute-start | bytes 196616 | tf_op jit(solution)/shard_map/ppermute | solution.py:474
  83.7 1.3 %collective-permute-start.32 = (bf16[32,1024]{1,0:T(8,128)(2,1)S(1)}, bf16[32,1024]{1,0:T(8,128)(2,1)S(1)}, u32[]{:S(2)}, u32[]{:S(2)}) collective-permute-start(bf16[32,1024]{1,0:T(8,128)(2,1)S(1)} %get-tuple-element.191), channel_id=1, source_target_pairs={{0,1},{1,0},{2,3},{3,2},{4,5},{5,4},{6,7},{7,6},{8,9},{9,8},{10,11... | collective-permute-start | bytes 196616 | tf_op jit(solution)/shard_map/ppermute | solution.py:474
  85.6 8.6 %collective-permute-start.33 = (bf16[4,128,256]{2,1,0:T(8,128)(2,1)S(1)}, bf16[4,128,256]{2,1,0:T(8,128)(2,1)S(1)}, u32[]{:S(2)}, u32[]{:S(2)}) collective-permute-start(bf16[4,128,256]{2,1,0:T(8,128)(2,1)S(1)} %get-tuple-element.197), channel_id=1, source_target_pairs={{0,16},{4,20},{8,24},{12,28},{16,0},{20,4},{24,8},{28,12},{1,17},{... | collective-permute-start | bytes 786440 | tf_op jit(solution)/shard_map/ppermute | solution.py:480
  92.1 7.9 %collective-permute-start.38 = (bf16[4,128,256]{2,1,0:T(8,128)(2,1)S(1)}, bf16[4,128,256]{2,1,0:T(8,128)(2,1)S(1)}, u32[]{:S(2)}, u32[]{:S(2)}) collective-permute-start(bf16[4,128,256]{2,1,0:T(8,128)(2,1)S(1)} %get-tuple-element.213), channel_id=1, source_target_pairs={{0,16},{4,20},{8,24},{12,28},{16,0},{20,4},{24,8},{28,12},{1,17},{... | collective-permute-start | bytes 786440 | tf_op jit(solution)/shard_map/ppermute | solution.py:480
  93.4 8.3 %collective-permute-start.36 = (bf16[96,1024]{1,0:T(8,128)(2,1)S(1)}, bf16[96,1024]{1,0:T(8,128)(2,1)S(1)}, u32[]{:S(2)}, u32[]{:S(2)}) collective-permute-start(bf16[96,1024]{1,0:T(8,128)(2,1)S(1)} %back_pick.2), channel_id=1, source_target_pairs={{0,4},{4,0},{8,12},{12,8},{16,20},{20,16},{24,28},{28,24},{1,5},{5... | collective-permute-start | bytes 589832 | tf_op jit(solution)/shard_map/ppermute | solution.py:480
  94.3 9.3 %collective-permute-start.34 = (bf16[2,128,256]{2,1,0:T(8,128)(2,1)S(1)}, bf16[2,128,256]{2,1,0:T(8,128)(2,1)S(1)}, u32[]{:S(2)}, u32[]{:S(2)}) collective-permute-start(bf16[2,128,256]{2,1,0:T(8,128)(2,1)S(1)} %get-tuple-element.199), channel_id=1, source_target_pairs={{0,4},{4,0},{8,12},{12,8},{16,20},{20,16},{24,28},{28,24},{1,5},{5... | collective-permute-start | bytes 393224 | tf_op jit(solution)/shard_map/ppermute | solution.py:480
  97.1 13.7 %collective-permute-start.41 = (bf16[128,1024]{1,0:T(8,128)(2,1)S(1)}, bf16[128,1024]{1,0:T(8,128)(2,1)S(1)}, u32[]{:S(2)}, u32[]{:S(2)}) collective-permute-start(bf16[128,1024]{1,0:T(8,128)(2,1)S(1)} %ffn_out_far.1), channel_id=1, source_target_pairs={{0,2},{1,3},{2,0},{3,1},{4,6},{5,7},{6,4},{7,5},{8,10},{9,11},{10,... | collective-permute-start | bytes 786440 | tf_op jit(solution)/shard_map/ppermute | solution.py:477
  100.0 6.4 %collective-permute-start.39 = (bf16[2,128,256]{2,1,0:T(8,128)(2,1)S(1)}, bf16[2,128,256]{2,1,0:T(8,128)(2,1)S(1)}, u32[]{:S(2)}, u32[]{:S(2)}) collective-permute-start(bf16[2,128,256]{2,1,0:T(8,128)(2,1)S(1)} %get-tuple-element.215), channel_id=1, source_target_pairs={{0,4},{4,0},{8,12},{12,8},{16,20},{20,16},{24,28},{28,24},{1,5},{5... | collective-permute-start | bytes 393224 | tf_op jit(solution)/shard_map/ppermute | solution.py:480
  103.6 8.4 %collective-permute-start.42 = (bf16[96,1024]{1,0:T(8,128)(2,1)S(1)}, bf16[96,1024]{1,0:T(8,128)(2,1)S(1)}, u32[]{:S(2)}, u32[]{:S(2)}) collective-permute-start(bf16[96,1024]{1,0:T(8,128)(2,1)S(1)} %back_pick.3), channel_id=1, source_target_pairs={{0,16},{4,20},{8,24},{12,28},{16,0},{20,4},{24,8},{28,12},{1,17},{... | collective-permute-start | bytes 589832 | tf_op jit(solution)/shard_map/ppermute | solution.py:480
  103.7 7.1 %collective-permute-start.37 = (bf16[1,128,256]{2,1,0:T(8,128)(2,1)S(1)}, bf16[1,128,256]{2,1,0:T(8,128)(2,1)S(1)}, u32[]{:S(2)}, u32[]{:S(2)}) collective-permute-start(bf16[1,128,256]{2,1,0:T(8,128)(2,1)S(1)} %get-tuple-element.206), channel_id=1, source_target_pairs={{0,8},{4,12},{8,0},{12,4},{16,24},{20,28},{24,16},{28,20},{1,9},{5... | collective-permute-start | bytes 196616 | tf_op jit(solution)/shard_map/ppermute | solution.py:480
  106.4 6.5 %collective-permute-start.40 = (bf16[1,128,256]{2,1,0:T(8,128)(2,1)S(1)}, bf16[1,128,256]{2,1,0:T(8,128)(2,1)S(1)}, u32[]{:S(2)}, u32[]{:S(2)}) collective-permute-start(bf16[1,128,256]{2,1,0:T(8,128)(2,1)S(1)} %get-tuple-element.216), channel_id=1, source_target_pairs={{0,8},{4,12},{8,0},{12,4},{16,24},{20,28},{24,16},{28,20},{1,9},{5... | collective-permute-start | bytes 196616 | tf_op jit(solution)/shard_map/ppermute | solution.py:480

commit v11 on v10

--- a/solution.py
+++ b/solution.py
@@ -60,13 +60,14 @@
     return jax.ShapeDtypeStruct(shape, dtype)
 
 
-def run(body, outs, args, scratch=(), flops=0, name=None):
+def run(body, outs, args, scratch=(), flops=0, name=None, aliases=None):
     return pl.pallas_call(
         body,
         out_shape=list(outs),
         in_specs=[pl.BlockSpec(memory_space=pltpu.VMEM)] * len(args),
         out_specs=[pl.BlockSpec(memory_space=pltpu.VMEM)] * len(outs),
         scratch_shapes=list(scratch),
+        input_output_aliases=aliases or {},
         compiler_params=pltpu.CompilerParams(vmem_limit_bytes=16 * MIB),
         cost_estimate=pl.CostEstimate(flops=flops, bytes_accessed=0, transcendentals=0),
         name=name,
@@ -177,6 +178,12 @@
     packed_ref[...] = packed[:size]
 
 
+def turn(attn_in, attn_out, in_ref, out_ref):
+    for c in range(attn_in.shape[0]):
+        in_ref[c] = attn_in[c].T
+    out_ref[...] = attn_out[...].T
+
+
 def window(docs, r, rows):
     t = tensor_index()
     b = t ^ r
@@ -300,7 +307,7 @@
     ahead, allowed, root_inv = window(docs, r, half)
     gate = proj_ref[3, r].astype(F32)
     sigma_g = jax.nn.sigmoid(gate)
-    d_gated = dot(d_resid, w_out, NT)
+    d_gated = dot(d_resid, w_out)
     d_att = bf16(d_gated * (gate * sigma_g) * root_inv)
     d_g[r] = bf16(d_gated * att_ref[r] * silu_grad(gate, sigma_g))
     keys = jnp.concatenate([proj_ref[1, ahead], proj_ref[1, r]], axis=0)
@@ -323,7 +330,7 @@
 
 
 def attn_back_first(docs, third, fourth_a, fourth_b, proj, att, w_out, d_q, d_k, d_v, d_g):
-    masks = head_masks(w_out.shape[0])
+    masks = head_masks(w_out.shape[1])
     d_k[...] = jnp.zeros_like(d_k)
     d_v[...] = jnp.zeros_like(d_v)
     for r, rows in ((2, [third]), (3, [fourth_a, fourth_b])):
@@ -331,44 +338,38 @@
 
 
 def attn_back_own(
-    docs, first, proj, att, w_out, d_q_far, d_k_far, d_v_far, d_g_far, w_in, give_ref, d_q, d_k, d_v, d_g
+    docs, first, proj, att, w_out, _q, _k, _v, _g, w_in, give_ref, d_q, d_k, d_v, d_g
 ):
-    masks = head_masks(w_out.shape[0])
-    d_q[...] = d_q_far[...]
-    d_g[...] = d_g_far[...]
-    d_k[...] = d_k_far[...]
-    d_v[...] = d_v_far[...]
+    masks = head_masks(w_out.shape[1])
     attend_back(docs, first[...], 0, proj, att, w_out[...], masks, d_q, d_k, d_v, d_g)
     give_ref[...] = bf16(back_norm((d_q, d_k, d_v, d_g), w_in, 3))
 
 
 def attn_back_second(
-    docs, second, proj, att, w_out, d_q_own, d_k_own, d_v_own, d_g_own, d_q, d_k, d_v, d_g, sum_k, sum_v
+    docs, second, proj, att, w_out, _q, _k, _v, _g, d_q, d_k, d_v, d_g
 ):
-    masks = head_masks(w_out.shape[0])
-    d_q[...] = d_q_own[...]
-    d_g[...] = d_g_own[...]
-    sum_k[...] = d_k_own[...]
-    sum_v[...] = d_v_own[...]
-    attend_back(docs, second[...], 1, proj, att, w_out[...], masks, d_q, sum_k, sum_v, d_g)
-    d_k[...] = bf16(sum_k[...])
-    d_v[...] = bf16(sum_v[...])
+    masks = head_masks(w_out.shape[1])
+    attend_back(docs, second[...], 1, proj, att, w_out[...], masks, d_q, d_k, d_v, d_g)
 
 
 def back_norm(grads, w_in, block):
     total = None
     for c, grad in enumerate(grads):
-        term = dot(bf16(grad[block]), w_in[c], NT)
+        term = dot(bf16(grad[block]), w_in[c])
         total = term if total is None else total + term
     return total
 
 
-def back_give(block, d_q, d_k, d_v, d_g, w_in, out):
-    out[...] = bf16(back_norm((d_q, d_k, d_v, d_g), w_in, block))
-
-
-def back_sum(block, d_q, d_k, d_v, d_g, w_in, take, out):
-    out[...] = bf16(back_norm((d_q, d_k, d_v, d_g), w_in, block) + take[...].astype(F32))
+def back_give(block, d_q, d_k, d_v, d_g, w_in, *outs):
+    value = bf16(back_norm((d_q, d_k, d_v, d_g), w_in, block))
+    rows = value.shape[0] // len(outs)
+    for n, out in enumerate(outs):
+        out[...] = value[n * rows : (n + 1) * rows]
+
+
+def back_sum(block, d_q, d_k, d_v, d_g, w_in, *refs):
+    takes, out = refs[:-1], refs[-1]
+    out[...] = bf16(back_norm((d_q, d_k, d_v, d_g), w_in, block) + joined(takes).astype(F32))
 
 
 def packed_back(part, got, packed, d_resid, out, *halves):
@@ -442,7 +443,7 @@
             target[j] = (kept[index] + got[index].astype(F32)).astype(target.dtype)
 
 
-def finish(kept0, got0, kept1, got1, out):
+def finish(kept1, got1, kept0, got0, out):
     out[0] = kept0[0] + got0[0].astype(F32)
     out[1] = kept1[0] + got1[0].astype(F32)
 
@@ -501,6 +502,13 @@
     gots = [sends[0], *early] + [crossed(sends[n], order[n]) for n in range(3, groups)]
     pieces = 2
     piece_b = like((rows_dev // pieces, width), BF16)
+    in_turned, out_turned = run(
+        turn,
+        [like((comps, cols, width), BF16), like((width, cols), BF16)],
+        [attn_in, attn_out],
+        name="turn",
+    )
+    in_turned, *gots = tie(in_turned, *gots)
     mine, hot, *halves = run(
         route_recv,
         [row_b, like((groups * capacity, rows_dev), BF16)] + [piece_b] * pieces,
@@ -597,7 +605,7 @@
     d_q, d_k, d_v, d_g = run(
         attn_back_first,
         [block_b, block_f, block_f, block_b],
-        [docs, d_resid_far, *d_resid_both, proj, attended, attn_out],
+        [docs, d_resid_far, *d_resid_both, proj, attended, out_turned],
         name="attn_back_first",
     )
     got_back_own, d_q = tie(got_back_own, d_q)
@@ -606,24 +614,26 @@
     give, *own_grads = run(
         attn_back_own,
         [row_b, block_b, block_f, block_f, block_b],
-        [docs, d_resid, proj, attended, attn_out, d_q, d_k, d_v, d_g, attn_in],
+        [docs, d_resid, proj, attended, out_turned, d_q, d_k, d_v, d_g, in_turned],
+        aliases={5: 1, 6: 2, 7: 3, 8: 4},
         name="attn_back_own",
     )
     take = near(give)
     d_projected = run(
         attn_back_second,
-        [block_b] * 4,
-        [docs, d_resid_near, proj, attended, attn_out, *own_grads],
-        [pltpu.VMEM((tensors, rows_dev, cols), F32)] * 2,
+        [block_b, block_f, block_f, block_b],
+        [docs, d_resid_near, proj, attended, out_turned, *own_grads],
+        aliases={5: 0, 6: 1, 7: 2, 8: 3},
         name="attn_back_second",
     )
 
-    def back_part(body, block, more, name):
-        return run(functools.partial(body, block), [row_b], [*d_projected, attn_in, *more], name=name)[0]
-
-    sum_far = back_part(back_sum, 2, [take], "back_sum_far")
-    take = near(back_part(back_give, 1, [], "back_give"))
-    sum_own = back_part(back_sum, 0, [take], "back_sum_own")
+    def back_part(body, block, outs, more, name):
+        return run(functools.partial(body, block), outs, [*d_projected, in_turned, *more], name=name)
+
+    (sum_far,) = back_part(back_sum, 2, [row_b], [take], "back_sum_far")
+    sum_far, *d_projected = tie(sum_far, *d_projected)
+    takes = [near(h) for h in back_part(back_give, 1, [piece_b] * pieces, [], "back_give")]
+    (sum_own,) = back_part(back_sum, 0, [row_b], takes, "back_sum_own")
     got_own = far(sum_far)
     got_far = far(sum_own)
     d_packed, *halves = run(
@@ -637,7 +647,7 @@
     half_rows = like((groups * capacity // 2, width), BF16)
     group_bits = [1 << b for b in range(groups.bit_length() - 1)]
     near_bit, pack_far, event_far = group_bits[0], group_bits[1 : packs.bit_length() - 1], group_bits[packs.bit_length() - 1 :]
-    back_bits = pack_far[::-1] + [near_bit] + event_far[::-1]
+    back_bits = event_far[::-1] + pack_far[::-1] + [near_bit]
     kept, back = run(
         functools.partial(back_send, order, back_bits[0]), [half_rows] * 2, [hot, d_packed], name="back_send"
     )
@@ -732,7 +742,7 @@
         send_back(bit)
     kept1, got1 = reduce_over(event_bits + pack_bits, kept1, send1, "halve1_", True)
     kept0, got0 = reduce_over(event_bits + pack_bits, kept0, send0, "halve0_")
-    got1, hidden_own, place = tie(got1, hidden_own, place)
+    got1, place = tie(got1, place)
     send_back(back_bits[-1])
     back_places = [held[k] for k in range(groups)]
     got_out = far(out_far)
@@ -746,7 +756,7 @@
         name="back_recv",
     )
     got1, got0, packed_out, row_grad = tie(got1, got0, packed_out, row_grad)
-    (enc_grad,) = run(finish, [like((2, size, cols), F32)], [kept0, got0, kept1, got1], name="finish")
+    (enc_grad,) = run(finish, [like((2, size, cols), F32)], [kept1, got1, kept0, got0], name="finish")
     return (packed_out[None], row_grad, enc_grad)
 
 

time: 114 us -> 114 us (level)
  waiting for transfers between devices: 43.6 us -> 45.9 us
  Pallas kernels: 28.3 us -> 26.8 us
    ppermute x16, waiting for transfers between devices: 18.8 us -> 20.6 us  [crossed(): return lax.ppermute(value, group_axes, [(i, i ^ k) for i in range(groups)])]
    ppermute x16, starting transfers between devices: 24.7 us -> 23 us  [crossed(): return lax.ppermute(value, group_axes, [(i, i ^ k) for i in range(groups)])]
    pallas_call x35 -> x36, Pallas kernels: 28.3 us -> 26.8 us  [run(): pl.pallas_call(body, out_shape=list(outs), in_specs=[pl.BlockSpec(memory_...]
    ppermute x18 -> x19, waiting for transfers between devices: 4.45 us -> 5.64 us  [near(): return lax.ppermute(value, 'tensor', [(i, i ^ 1) for i in range(tensors)])]
    ppermute x18 -> x19, starting transfers between devices: 4.91 us -> 5.12 us  [near(): return lax.ppermute(value, 'tensor', [(i, i ^ 1) for i in range(tensors)])]
  transfers between devices with their start and end apart: 43 -> 44, of which waited for: 26 -> 30; matrix products, arithmetic and copies ran while one was open for 1% -> 1% of each run, Pallas kernels for 24% -> 22%
where the time goes in v11:
time: 114 us
  waiting for transfers between devices  45.9 us (40%)
  starting transfers between devices  38.2 us (34%)
  Pallas kernels  26.8 us (24%)
    pallas_call x36, Pallas kernels, run(): pl.pallas_call(body, out_shape=list(outs), in_specs=[pl.BlockSpec(memory_...  26.8 us
    ppermute x16, starting transfers between devices, crossed(): return lax.ppermute(value, group_axes, [(i, i ^ k) for i in range(groups)])  23 us
    ppermute x16, waiting for transfers between devices, crossed(): return lax.ppermute(value, group_axes, [(i, i ^ k) for i in range(groups)])  20.6 us
    ppermute x9, waiting for transfers between devices, far(): return lax.ppermute(value, 'tensor', [(i, i ^ 2) for i in range(tensors)])  19.7 us
    ppermute x9, starting transfers between devices, far(): return lax.ppermute(value, 'tensor', [(i, i ^ 2) for i in range(tensors)])  10 us
    ppermute x19, waiting for transfers between devices, near(): return lax.ppermute(value, 'tensor', [(i, i ^ 1) for i in range(tensors)])  5.64 us
    ppermute x19, starting transfers between devices, near(): return lax.ppermute(value, 'tensor', [(i, i ^ 1) for i in range(tensors)])  5.12 us
  transfers between devices with their start and end apart: 44, of which 30 were waited for; matrix products, arithmetic and copies ran while one was open for 1% of the time, Pallas kernels for 22%

profile of v11, /device:TPU:0, one launch (start us, length us, event | category | flops | bytes accessed | tf_op | source)
XLA Modules:
  0.0 113.5 jit_solution(3225440108612005330)
XLA Ops:
  0.6 0.5 collective-permute-start
  1.2 0.7 add_bitcast_fusion.code
  1.9 0.9 copy-done.7
  3.2 4.1 %collective-permute-start.2 = (bf16[24,1152]{1,0:T(8,128)(2,1)S(1)}, bf16[24,1152]{1,0:T(8,128)(2,1)S(1)}, u32[]{:S(2)}, u32[]{:S(2)}) collective-permute-start(bf16[24,1152]{1,0:T(8,128)(2,1)S(1)} %get-tuple-element.134), channel_id=1, source_target_pairs={{0,8},{4,12},{8,0},{12,4},{16,24},{20,28},{24,16},{28,20},{1,9},{5... | collective-permute-start | bytes 165896 | tf_op jit(solution)/shard_map/ppermute | solution.py:481
  7.3 1.3 %collective-permute-start.3 = (bf16[24,1152]{1,0:T(8,128)(2,1)S(1)}, bf16[24,1152]{1,0:T(8,128)(2,1)S(1)}, u32[]{:S(2)}, u32[]{:S(2)}) collective-permute-start(bf16[24,1152]{1,0:T(8,128)(2,1)S(1)} %get-tuple-element.135), channel_id=1, source_target_pairs={{0,24},{4,28},{8,16},{12,20},{16,8},{20,12},{24,0},{28,4},{1,25},{... | collective-permute-start | bytes 165896 | tf_op jit(solution)/shard_map/ppermute | solution.py:481
  8.6 3.6 %collective-permute-start.4 = (bf16[24,1152]{1,0:T(8,128)(2,1)S(1)}, bf16[24,1152]{1,0:T(8,128)(2,1)S(1)}, u32[]{:S(2)}, u32[]{:S(2)}) collective-permute-start(bf16[24,1152]{1,0:T(8,128)(2,1)S(1)} %get-tuple-element.142), channel_id=1, source_target_pairs={{0,12},{4,8},{8,4},{12,0},{16,28},{20,24},{24,20},{28,16},{1,13},{... | collective-permute-start | bytes 165896 | tf_op jit(solution)/shard_map/ppermute | solution.py:481
  12.2 0.6 collective-permute-start.5
  12.8 1.1 collective-permute-start.6
  13.9 2.2 %collective-permute-done.3.refs_2_ = bf16[24,1152]{1,0:T(8,128)(2,1)S(1)} collective-permute-done((bf16[24,1152]{1,0:T(8,128)(2,1)S(1)}, bf16[24,1152]{1,0:T(8,128)(2,1)S(1)}, u32[]{:S(2)}, u32[]{:S(2)}) %collective-permute-start.3) | collective-permute-done | bytes 55328 | tf_op jit(solution)/shard_map/ppermute | solution.py:481
  16.4 0.8 turn.1
  17.2 2.0 %collective-permute-done.5.refs_4_ = bf16[24,1152]{1,0:T(8,128)(2,1)S(1)} collective-permute-done((bf16[24,1152]{1,0:T(8,128)(2,1)S(1)}, bf16[24,1152]{1,0:T(8,128)(2,1)S(1)}, u32[]{:S(2)}, u32[]{:S(2)}) %collective-permute-start.5) | collective-permute-done | bytes 55328 | tf_op jit(solution)/shard_map/ppermute | solution.py:481
  19.2 1.9 %collective-permute-done.8.refs_7_ = bf16[24,1152]{1,0:T(8,128)(2,1)S(1)} collective-permute-done((bf16[24,1152]{1,0:T(8,128)(2,1)S(1)}, bf16[24,1152]{1,0:T(8,128)(2,1)S(1)}, u32[]{:S(2)}, u32[]{:S(2)}) %collective-permute-start.8) | collective-permute-done | bytes 55328 | tf_op jit(solution)/shard_map/ppermute | solution.py:481
  21.4 1.6 %collective-permute-start.9 = (bf16[128,1024]{1,0:T(8,128)(2,1)S(1)}, bf16[128,1024]{1,0:T(8,128)(2,1)S(1)}, u32[]{:S(2)}, u32[]{:S(2)}) collective-permute-start(bf16[128,1024]{1,0:T(8,128)(2,1)S(1)} %get-tuple-element.155.refs_0_.refs_3_), channel_id=1, source_target_pairs={{0,2},{1,3},{2,0},{3,1},{4,6},{5,7},{6,4},{7,5},{8,10},{9,11},{10,... | collective-permute-start | bytes 786440 | tf_op jit(solution)/shard_map/ppermute | solution.py:478
  23.0 0.5 collective-permute-start.11
  23.5 0.8 collective-permute-done.10.refs_1_.refs_4_
  24.5 2.2 %encode_first.1 = (f32[256,256]{1,0:T(8,128)S(1)}, bf16[256,1024]{1,0:T(8,128)(2,1)S(1)}, bf16[128,1024]{1,0:T(8,128)(2,1)S(1)}, bf16[4,2,128,256]{3,2,1,0:T(8,128)(2,1)S(1)}) custom-call(bf16[128,1024]{1,0:T(8,128)(2,1)S(1)} %get-tuple-element.155.refs_0_.refs_3_, bf16[64,1024]{1,0:T(8,128)(2,1)S(1)} %collective-permute-done.10.refs_1_.refs_4_, ...), custom_call_target="tpu_custom_call" | custom-call | tf_op jit(solution)/shard_map/encode_first/pallas_call | solution.py:64
  26.8 1.1 collective-permute-done.9.refs_0_.refs_5_
  27.8 0.5 collective-permute-start.12
  28.3 1.5 %collective-permute-start.15 = (bf16[128,1024]{1,0:T(8,128)(2,1)S(1)}, bf16[128,1024]{1,0:T(8,128)(2,1)S(1)}, u32[]{:S(2)}, u32[]{:S(2)}) collective-permute-start(bf16[128,1024]{1,0:T(8,128)(2,1)S(1)} %bitcast.5), channel_id=1, source_target_pairs={{0,2},{1,3},{2,0},{3,1},{4,6},{5,7},{6,4},{7,5},{8,10},{9,11},{10,... | collective-permute-start | bytes 786440 | tf_op jit(solution)/shard_map/ppermute | solution.py:478
  29.9 1.4 %encode_third.1 = (f32[128,256]{1,0:T(8,128)S(1)}, bf16[128,1024]{1,0:T(8,128)(2,1)S(1)}, bf16[128,1024]{1,0:T(8,128)(2,1)S(1)}, bf16[4,1,128,256]{3,2,1,0:T(8,128)(2,1)S(1)}) custom-call(bf16[128,1024]{1,0:T(8,128)(2,1)S(1)} %collective-permute-done.9.refs_0_.refs_5_, bf16[2,1024,1024]{2,1,0:T(8,128)(2,1)S(1)} %copy-done, bf16[4,1024,256]{2,1,0:T(8,128)(2,1)S(1)} %copy-done.1), custom_call_target="tpu_custom_call" | custom-call | tf_op jit(solution)/shard_map/encode_third/pallas_call | solution.py:64
  31.3 2.5 %attend_first.1 = (f32[256,256]{1,0:T(8,128)S(1)}, bf16[256,1024]{1,0:T(8,128)(2,1)S(1)}, bf16[4,4,128,256]{3,2,1,0:T(8,128)(2,1)S(1)}, f32[4,128,256]{2,1,0:T(8...) custom-call(s32[4,1,128]{2,1,0:T(1,128)S(1)} %bitcast.8, ...), custom_call_target="tpu_custom_call" | custom-call | tf_op jit(solution)/shard_map/attend_first/pallas_call | solution.py:64
  33.9 1.3 %collective-permute-done.13.take = bf16[256,256]{1,0:T(8,128)(2,1)S(1)} collective-permute-done((bf16[256,256]{1,0:T(8,128)(2,1)S(1)}, bf16[256,256]{1,0:T(8,128)(2,1)S(1)}, u32[]{:S(2)}, u32[]{:S(2)}) %collective-permute-start.13) | collective-permute-done | bytes 131104 | tf_op jit(solution)/shard_map/ppermute | solution.py:475
  35.5 0.6 collective-permute-start.17
  36.5 1.5 %collective-permute-start.16 = (bf16[128,1024]{1,0:T(8,128)(2,1)S(1)}, bf16[128,1024]{1,0:T(8,128)(2,1)S(1)}, u32[]{:S(2)}, u32[]{:S(2)}) collective-permute-start(bf16[128,1024]{1,0:T(8,128)(2,1)S(1)} %attn_out_own.1.part), channel_id=1, source_target_pairs={{0,2},{1,3},{2,0},{3,1},{4,6},{5,7},{6,4},{7,5},{8,10},{9,11},{10,... | collective-permute-start | bytes 786440 | tf_op jit(solution)/shard_map/ppermute | solution.py:478
  38.1 6.7 %collective-permute-done.17.got = bf16[128,1024]{1,0:T(8,128)(2,1)S(1)} collective-permute-done((bf16[128,1024]{1,0:T(8,128)(2,1)S(1)}, bf16[128,1024]{1,0:T(8,128)(2,1)S(1)}, u32[]{:S(2)}, u32[]{:S(2)}) %collective-permute-start.17) | collective-permute-done | bytes 262176 | tf_op jit(solution)/shard_map/ppermute | solution.py:478
  45.0 2.9 %ffn_own.1 = (bf16[128,1024]{1,0:T(8,128)(2,1)S(1)}, bf16[128,1024]{1,0:T(8,128)(2,1)S(1)}) custom-call(bf16[128,1024]{1,0:T(8,128)(2,1)S(1)} %get-tuple-element.171.rows_ref, bf16[128,1024]{1,0:T(8,128)(2,1)S(1)} %bitcast.6, bf16[2,1024,512]{2,1,0:T(8,128)(2,1)S(1)} %copy-done.3, bf16[2,1024,512]{2,1,0:T(8,128)(2,1)S(1)} %collective-permute-done.in_b, ...), custom_call_target="tpu_custom_call" | custom-call | tf_op jit(solution)/shard_map/ffn_own/pallas_call | solution.py:64
  47.9 1.7 %collective-permute-done.16.got = bf16[128,1024]{1,0:T(8,128)(2,1)S(1)} collective-permute-done((bf16[128,1024]{1,0:T(8,128)(2,1)S(1)}, bf16[128,1024]{1,0:T(8,128)(2,1)S(1)}, u32[]{:S(2)}, u32[]{:S(2)}) %collective-permute-start.16) | collective-permute-done | bytes 262176 | tf_op jit(solution)/shard_map/ppermute | solution.py:478
  49.6 0.5 collective-permute-start.19
  50.3 2.9 %ffn_far.1 = (bf16[128,1024]{1,0:T(8,128)(2,1)S(1)}, bf16[128,1024]{1,0:T(8,128)(2,1)S(1)}) custom-call(bf16[128,1024]{1,0:T(8,128)(2,1)S(1)} %get-tuple-element.178.rows_ref, bf16[128,1024]{1,0:T(8,128)(2,1)S(1)} %collective-permute-done.15.d_out_ref.d_out, bf16[2,1024,512]{2,1,0:T(8,128)(2,1)S(1)} %copy-done.3, ...), custom_call_target="tpu_custom_call" | custom-call | tf_op jit(solution)/shard_map/ffn_far/pallas_call | solution.py:64
  53.2 1.6 %collective-permute-start.18 = (bf16[128,1024]{1,0:T(8,128)(2,1)S(1)}, bf16[128,1024]{1,0:T(8,128)(2,1)S(1)}, u32[]{:S(2)}, u32[]{:S(2)}) collective-permute-start(bf16[128,1024]{1,0:T(8,128)(2,1)S(1)} %get-tuple-element.180.back), channel_id=1, source_target_pairs={{0,2},{1,3},{2,0},{3,1},{4,6},{5,7},{6,4},{7,5},{8,10},{9,11},{10,... | collective-permute-start | bytes 786440 | tf_op jit(solution)/shard_map/ppermute | solution.py:478
  54.8 4.1 %collective-permute-done.19.got = bf16[128,1024]{1,0:T(8,128)(2,1)S(1)} collective-permute-done((bf16[128,1024]{1,0:T(8,128)(2,1)S(1)}, bf16[128,1024]{1,0:T(8,128)(2,1)S(1)}, u32[]{:S(2)}, u32[]{:S(2)}) %collective-permute-start.19) | collective-permute-done | bytes 262176 | tf_op jit(solution)/shard_map/ppermute | solution.py:478
  58.8 0.5 resid_back_far.1
  59.4 0.5 collective-permute-start.21
  59.9 0.8 collective-permute-done.20.fourth_a
  60.9 1.6 %attn_back_first.1 = (bf16[4,128,256]{2,1,0:T(8,128)(2,1)S(1)}, f32[4,128,256]{2,1,0:T(8,128)S(1)}, f32[4,128,256]{2,1,0:T(8,128)S(1)}, bf16[4,128,256]{2,1,0:T(8,128)(2,1)S(1)}) custom-call(s32[4,1,128]{2,1,0:T(1,128)S(1)} %bitcast.9, bf16[128,1024]{1,0:T(8,128)(2,1)S(1)} %get-tuple-element.182.third.d_resid, ...), custom_call_target="tpu_custom_call" | custom-call | tf_op jit(solution)/shard_map/attn_back_first/pallas_call | solution.py:64
  63.2 1.2 %attn_back_own.1 = (bf16[128,1024]{1,0:T(8,128)(2,1)S(1)}, bf16[4,128,256]{2,1,0:T(8,128)(2,1)S(1)}, f32[4,128,256]{2,1,0:T(8,128)S(1)}, f32[4,128,256]{2,1,0:T(8,128)S(1)}, bf16[4,128,256]{2,1,0:T(8,128)(2,1)S(1)}) custom-call(s32[4,1,128]{2,1,0:T(1,128)S(1)} %bitcast.10, ...), custom_call_target="tpu_custom_call", output_to_operand_aliasing={{1}: (5, {}), {2}: (6, {}), {3}: (7, {}), {4}: (8, {})} | custom-call | tf_op jit(solution)/shard_map/attn_back_own/pallas_call | solution.py:64
  64.4 0.5 collective-permute-start.23
  64.8 0.8 attn_back_second.1
  66.4 0.6 collective-permute-start.27
  68.0 0.8 collective-permute-done.24.refs_0_
  69.5 1.6 %collective-permute-start.26 = (bf16[128,1024]{1,0:T(8,128)(2,1)S(1)}, bf16[128,1024]{1,0:T(8,128)(2,1)S(1)}, u32[]{:S(2)}, u32[]{:S(2)}) collective-permute-start(bf16[128,1024]{1,0:T(8,128)(2,1)S(1)} %back_sum_own.1.part), channel_id=1, source_target_pairs={{0,2},{1,3},{2,0},{3,1},{4,6},{5,7},{6,4},{7,5},{8,10},{9,11},{10,... | collective-permute-start | bytes 786440 | tf_op jit(solution)/shard_map/ppermute | solution.py:478
  71.1 4.5 %collective-permute-done.27.got = bf16[128,1024]{1,0:T(8,128)(2,1)S(1)} collective-permute-done((bf16[128,1024]{1,0:T(8,128)(2,1)S(1)}, bf16[128,1024]{1,0:T(8,128)(2,1)S(1)}, u32[]{:S(2)}, u32[]{:S(2)}) %collective-permute-start.27) | collective-permute-done | bytes 262176 | tf_op jit(solution)/shard_map/ppermute | solution.py:478
  76.0 0.5 collective-permute-start.29
  76.8 1.7 %collective-permute-start.36 = (bf16[96,1024]{1,0:T(8,128)(2,1)S(1)}, bf16[96,1024]{1,0:T(8,128)(2,1)S(1)}, u32[]{:S(2)}, u32[]{:S(2)}) collective-permute-start(bf16[96,1024]{1,0:T(8,128)(2,1)S(1)} %get-tuple-element.238), channel_id=1, source_target_pairs={{0,16},{4,20},{8,24},{12,28},{16,0},{20,4},{24,8},{28,12},{1,17},{... | collective-permute-start | bytes 589832 | tf_op jit(solution)/shard_map/ppermute | solution.py:481
  78.5 1.0 enc_grads_first.1
  79.4 1.3 %collective-permute-done.26.got = bf16[128,1024]{1,0:T(8,128)(2,1)S(1)} collective-permute-done((bf16[128,1024]{1,0:T(8,128)(2,1)S(1)}, bf16[128,1024]{1,0:T(8,128)(2,1)S(1)}, u32[]{:S(2)}, u32[]{:S(2)}) %collective-permute-start.26) | collective-permute-done | bytes 262176 | tf_op jit(solution)/shard_map/ppermute | solution.py:478
  81.1 0.5 collective-permute-start.31
  83.0 0.5 enc_grad1_second.1
  83.5 1.7 %collective-permute-start.34 = (bf16[4,128,256]{2,1,0:T(8,128)(2,1)S(1)}, bf16[4,128,256]{2,1,0:T(8,128)(2,1)S(1)}, u32[]{:S(2)}, u32[]{:S(2)}) collective-permute-start(bf16[4,128,256]{2,1,0:T(8,128)(2,1)S(1)} %get-tuple-element.232), channel_id=1, source_target_pairs={{0,16},{4,20},{8,24},{12,28},{16,0},{20,4},{24,8},{28,12},{1,17},{... | collective-permute-start | bytes 786440 | tf_op jit(solution)/shard_map/ppermute | solution.py:481
  85.2 1.0 enc_grad0_second.1
  86.2 0.5 collective-permute-start.39
  86.7 2.3 %collective-permute-start.37 = (bf16[96,1024]{1,0:T(8,128)(2,1)S(1)}, bf16[96,1024]{1,0:T(8,128)(2,1)S(1)}, u32[]{:S(2)}, u32[]{:S(2)}) collective-permute-start(bf16[96,1024]{1,0:T(8,128)(2,1)S(1)} %back_pick.2), channel_id=1, source_target_pairs={{0,8},{4,12},{8,0},{12,4},{16,24},{20,28},{24,16},{28,20},{1,9},{5... | collective-permute-start | bytes 589832 | tf_op jit(solution)/shard_map/ppermute | solution.py:481
  89.0 3.7 %collective-permute-done.34.got = bf16[4,128,256]{2,1,0:T(8,128)(2,1)S(1)} collective-permute-done((bf16[4,128,256]{2,1,0:T(8,128)(2,1)S(1)}, bf16[4,128,256]{2,1,0:T(8,128)(2,1)S(1)}, u32[]{:S(2)}, u32[]{:S(2)}) %collective-permute-start.34) | collective-permute-done | bytes 262176 | tf_op jit(solution)/shard_map/ppermute | solution.py:481
  93.5 0.6 collective-permute-start.42
  94.0 3.8 %collective-permute-done.39.got = bf16[4,128,256]{2,1,0:T(8,128)(2,1)S(1)} collective-permute-done((bf16[4,128,256]{2,1,0:T(8,128)(2,1)S(1)}, bf16[4,128,256]{2,1,0:T(8,128)(2,1)S(1)}, u32[]{:S(2)}, u32[]{:S(2)}) %collective-permute-start.39) | collective-permute-done | bytes 262176 | tf_op jit(solution)/shard_map/ppermute | solution.py:481
  98.0 0.6 collective-permute-done.37.refs_2_
  98.6 1.5 %collective-permute-done.35.got = bf16[2,128,256]{2,1,0:T(8,128)(2,1)S(1)} collective-permute-done((bf16[2,128,256]{2,1,0:T(8,128)(2,1)S(1)}, bf16[2,128,256]{2,1,0:T(8,128)(2,1)S(1)}, u32[]{:S(2)}, u32[]{:S(2)}) %collective-permute-start.35) | collective-permute-done | bytes 131104 | tf_op jit(solution)/shard_map/ppermute | solution.py:481
  100.2 5.1 %collective-permute-start.38 = (bf16[1,128,256]{2,1,0:T(8,128)(2,1)S(1)}, bf16[1,128,256]{2,1,0:T(8,128)(2,1)S(1)}, u32[]{:S(2)}, u32[]{:S(2)}) collective-permute-start(bf16[1,128,256]{2,1,0:T(8,128)(2,1)S(1)} %get-tuple-element.241), channel_id=1, source_target_pairs={{0,8},{4,12},{8,0},{12,4},{16,24},{20,28},{24,16},{28,20},{1,9},{5... | collective-permute-start | bytes 196616 | tf_op jit(solution)/shard_map/ppermute | solution.py:481
  105.7 1.2 %ffn_out_own.1 = bf16[128,1024]{1,0:T(8,128)(2,1)} custom-call(bf16[128,1024]{1,0:T(8,128)(2,1)S(1)} %get-tuple-element.251.hidden, bf16[512,1024]{1,0:T(8,128)(2,1)S(1)} %copy-done.2, bf16[512,1024]{1,0:T(8,128)(2,1)S(1)} %collective-permute-done.1.out_b.w_b, bf16[128,1024]{1,0:T(8,128)(2,1)S(1)} %get-tuple-element.190.resid, ...), custom_call_target="tpu_custom_call" | custom-call | tf_op jit(solution)/shard_map/ffn_out_own/pallas_call | solution.py:64
  106.8 0.8 collective-permute-done.38.got1
  107.6 1.6 %collective-permute-done.43.refs_3_ = bf16[96,1024]{1,0:T(8,128)(2,1)S(1)} collective-permute-done((bf16[96,1024]{1,0:T(8,128)(2,1)S(1)}, bf16[96,1024]{1,0:T(8,128)(2,1)S(1)}, u32[]{:S(2)}, u32[]{:S(2)}) %collective-permute-start.43) | collective-permute-done | bytes 196640 | tf_op jit(solution)/shard_map/ppermute | solution.py:481
  109.2 1.0 back_recv.1
  110.2 2.7 %collective-permute-done.41.got0 = bf16[1,128,256]{2,1,0:T(8,128)(2,1)S(1)} collective-permute-done((bf16[1,128,256]{2,1,0:T(8,128)(2,1)S(1)}, bf16[1,128,256]{2,1,0:T(8,128)(2,1)S(1)}, u32[]{:S(2)}, u32[]{:S(2)}) %collective-permute-start.41) | collective-permute-done | bytes 65568 | tf_op jit(solution)/shard_map/ppermute | solution.py:481
  112.8 0.7 finish.1
  (77 shorter events, 9.7 us)
Async XLA Ops:
  0.6 7.9 %collective-permute-start = (bf16[2,1024,512]{2,1,0:T(8,128)(2,1)}, bf16[2,1024,512]{2,1,0:T(8,128)(2,1)S(1)}, u32[]{:S(2)}, u32[]{:S(2)}) collective-permute-start(bf16[2,1024,512]{2,1,0:T(8,128)(2,1)} %in_a.3), channel_id=1, source_target_pairs={{0,1},{1,0},{2,3},{3,2},{4,5},{5,4},{6,7},{7,6},{8,9},{9,8},{10,11... | collective-permute-start | bytes 6291464 | tf_op jit(solution)/shard_map/ppermute | solution.py:475
  1.1 7.4 %collective-permute-start.1 = (bf16[512,1024]{1,0:T(8,128)(2,1)}, bf16[512,1024]{1,0:T(8,128)(2,1)S(1)}, u32[]{:S(2)}, u32[]{:S(2)}) collective-permute-start(bf16[512,1024]{1,0:T(8,128)(2,1)} %w_a.3), channel_id=1, source_target_pairs={{0,1},{1,0},{2,3},{3,2},{4,5},{5,4},{6,7},{7,6},{8,9},{9,8},{10,11... | collective-permute-start | bytes 3145736 | tf_op jit(solution)/shard_map/ppermute | solution.py:475
  1.9 0.9 copy-start.7
  2.9 13.5 %copy-start.1 = (bf16[4,1024,256]{2,1,0:T(8,128)(2,1)S(1)}, bf16[4,1024,256]{2,1,0:T(8,128)(2,1)}, u32[]{:S(2)}) copy-start(bf16[4,1024,256]{2,1,0:T(8,128)(2,1)} %w_in.1) | copy-start | bytes 6291460
  2.9 13.5 %copy-start.4 = (bf16[256,1024]{1,0:T(8,128)(2,1)S(1)}, bf16[256,1024]{1,0:T(8,128)(2,1)}, u32[]{:S(2)}) copy-start(bf16[256,1024]{1,0:T(8,128)(2,1)} %w_own.3) | copy-start | bytes 1572868
  2.9 21.6 %copy-start = (bf16[2,1024,1024]{2,1,0:T(8,128)(2,1)S(1)}, bf16[2,1024,1024]{2,1,0:T(8,128)(2,1)}, u32[]{:S(2)}) copy-start(bf16[2,1024,1024]{2,1,0:T(8,128)(2,1)} %refs_8_.3) | copy-start | bytes 12582916
  3.2 10.6 %collective-permute-start.2 = (bf16[24,1152]{1,0:T(8,128)(2,1)S(1)}, bf16[24,1152]{1,0:T(8,128)(2,1)S(1)}, u32[]{:S(2)}, u32[]{:S(2)}) collective-permute-start(bf16[24,1152]{1,0:T(8,128)(2,1)S(1)} %get-tuple-element.134), channel_id=1, source_target_pairs={{0,8},{4,12},{8,0},{12,4},{16,24},{20,28},{24,16},{28,20},{1,9},{5... | collective-permute-start | bytes 165896 | tf_op jit(solution)/shard_map/ppermute | solution.py:481
  7.3 8.8 %collective-permute-start.3 = (bf16[24,1152]{1,0:T(8,128)(2,1)S(1)}, bf16[24,1152]{1,0:T(8,128)(2,1)S(1)}, u32[]{:S(2)}, u32[]{:S(2)}) collective-permute-start(bf16[24,1152]{1,0:T(8,128)(2,1)S(1)} %get-tuple-element.135), channel_id=1, source_target_pairs={{0,24},{4,28},{8,16},{12,20},{16,8},{20,12},{24,0},{28,4},{1,25},{... | collective-permute-start | bytes 165896 | tf_op jit(solution)/shard_map/ppermute | solution.py:481
  8.6 8.6 %collective-permute-start.4 = (bf16[24,1152]{1,0:T(8,128)(2,1)S(1)}, bf16[24,1152]{1,0:T(8,128)(2,1)S(1)}, u32[]{:S(2)}, u32[]{:S(2)}) collective-permute-start(bf16[24,1152]{1,0:T(8,128)(2,1)S(1)} %get-tuple-element.142), channel_id=1, source_target_pairs={{0,12},{4,8},{8,4},{12,0},{16,28},{20,24},{24,20},{28,16},{1,13},{... | collective-permute-start | bytes 165896 | tf_op jit(solution)/shard_map/ppermute | solution.py:481
  12.2 7.0 %collective-permute-start.5 = (bf16[24,1152]{1,0:T(8,128)(2,1)S(1)}, bf16[24,1152]{1,0:T(8,128)(2,1)S(1)}, u32[]{:S(2)}, u32[]{:S(2)}) collective-permute-start(bf16[24,1152]{1,0:T(8,128)(2,1)S(1)} %get-tuple-element.143), channel_id=1, source_target_pairs={{0,28},{4,24},{8,20},{12,16},{16,12},{20,8},{24,4},{28,0},{1,29},{... | collective-permute-start | bytes 165896 | tf_op jit(solution)/shard_map/ppermute | solution.py:481
  12.8 6.4 %collective-permute-start.6 = (bf16[24,1152]{1,0:T(8,128)(2,1)S(1)}, bf16[24,1152]{1,0:T(8,128)(2,1)S(1)}, u32[]{:S(2)}, u32[]{:S(2)}) collective-permute-start(bf16[24,1152]{1,0:T(8,128)(2,1)S(1)} %get-tuple-element.144), channel_id=1, source_target_pairs={{0,16},{4,20},{8,24},{12,28},{16,0},{20,4},{24,8},{28,12},{1,17},{... | collective-permute-start | bytes 165896 | tf_op jit(solution)/shard_map/ppermute | solution.py:481
  13.9 5.3 %collective-permute-start.7 = (bf16[24,1152]{1,0:T(8,128)(2,1)S(1)}, bf16[24,1152]{1,0:T(8,128)(2,1)S(1)}, u32[]{:S(2)}, u32[]{:S(2)}) collective-permute-start(bf16[24,1152]{1,0:T(8,128)(2,1)S(1)} %get-tuple-element.145), channel_id=1, source_target_pairs={{0,4},{4,0},{8,12},{12,8},{16,20},{20,16},{24,28},{28,24},{1,5},{5... | collective-permute-start | bytes 165896 | tf_op jit(solution)/shard_map/ppermute | solution.py:481
  16.1 5.1 %collective-permute-start.8 = (bf16[24,1152]{1,0:T(8,128)(2,1)S(1)}, bf16[24,1152]{1,0:T(8,128)(2,1)S(1)}, u32[]{:S(2)}, u32[]{:S(2)}) collective-permute-start(bf16[24,1152]{1,0:T(8,128)(2,1)S(1)} %get-tuple-element.146), channel_id=1, source_target_pairs={{0,20},{4,16},{8,28},{12,24},{16,4},{20,0},{24,12},{28,8},{1,21},{... | collective-permute-start | bytes 165896 | tf_op jit(solution)/shard_map/ppermute | solution.py:481
  21.4 6.4 %collective-permute-start.9 = (bf16[128,1024]{1,0:T(8,128)(2,1)S(1)}, bf16[128,1024]{1,0:T(8,128)(2,1)S(1)}, u32[]{:S(2)}, u32[]{:S(2)}) collective-permute-start(bf16[128,1024]{1,0:T(8,128)(2,1)S(1)} %get-tuple-element.155.refs_0_.refs_3_), channel_id=1, source_target_pairs={{0,2},{1,3},{2,0},{3,1},{4,6},{5,7},{6,4},{7,5},{8,10},{9,11},{10,... | collective-permute-start | bytes 786440 | tf_op jit(solution)/shard_map/ppermute | solution.py:478
  23.0 1.3 %collective-permute-start.10 = (bf16[64,1024]{1,0:T(8,128)(2,1)S(1)}, bf16[64,1024]{1,0:T(8,128)(2,1)S(1)}, u32[]{:S(2)}, u32[]{:S(2)}) collective-permute-start(bf16[64,1024]{1,0:T(8,128)(2,1)S(1)} %get-tuple-element.156), channel_id=1, source_target_pairs={{0,1},{1,0},{2,3},{3,2},{4,5},{5,4},{6,7},{7,6},{8,9},{9,8},{10,11... | collective-permute-start | bytes 393224 | tf_op jit(solution)/shard_map/ppermute | solution.py:475
  23.0 5.4 %copy-start.5 = (bf16[1,128,1024]{2,1,0:T(8,128)(2,1)S(1)}, bf16[1,128,1024]{2,1,0:T(8,128)(2,1)}, u32[]{:S(2)}) copy-start(bf16[1,128,1024]{2,1,0:T(8,128)(2,1)} %param.19) | copy-start | bytes 786436
  23.0 1.5 %collective-permute-start.11 = (bf16[64,1024]{1,0:T(8,128)(2,1)S(1)}, bf16[64,1024]{1,0:T(8,128)(2,1)S(1)}, u32[]{:S(2)}, u32[]{:S(2)}) collective-permute-start(bf16[64,1024]{1,0:T(8,128)(2,1)S(1)} %get-tuple-element.157), channel_id=1, source_target_pairs={{0,1},{1,0},{2,3},{3,2},{4,5},{5,4},{6,7},{7,6},{8,9},{9,8},{10,11... | collective-permute-start | bytes 393224 | tf_op jit(solution)/shard_map/ppermute | solution.py:475
  27.8 3.4 %copy-start.6 = (s32[1,512]{1,0:T(1,128)S(1)}, s32[1,512]{1,0:T(1,128)}, u32[]{:S(2)}) copy-start(s32[1,512]{1,0:T(1,128)} %param.13) | copy-start | bytes 6148
  27.8 7.4 %collective-permute-start.14 = (bf16[256,1024]{1,0:T(8,128)(2,1)S(1)}, bf16[256,1024]{1,0:T(8,128)(2,1)S(1)}, u32[]{:S(2)}, u32[]{:S(2)}) collective-permute-start(bf16[256,1024]{1,0:T(8,128)(2,1)S(1)} %copy-done.4), channel_id=1, source_target_pairs={{0,1},{1,0},{2,3},{3,2},{4,5},{5,4},{6,7},{7,6},{8,9},{9,8},{10,11... | collective-permute-start | bytes 1572872 | tf_op jit(solution)/shard_map/ppermute | solution.py:475
  27.8 3.4 %collective-permute-start.12 = (bf16[128,1024]{1,0:T(8,128)(2,1)S(1)}, bf16[128,1024]{1,0:T(8,128)(2,1)S(1)}, u32[]{:S(2)}, u32[]{:S(2)}) collective-permute-start(bf16[128,1024]{1,0:T(8,128)(2,1)S(1)} %collective-permute-done.9.refs_0_.refs_5_), channel_id=1, source_target_pairs={{0,1},{1,0},{2,3},{3,2},{4,5},{5,4},{6,7},{7,6},{8,9},{9,8},{10,11... | collective-permute-start | bytes 786440 | tf_op jit(solution)/shard_map/ppermute | solution.py:475
  28.3 8.2 %collective-permute-start.15 = (bf16[128,1024]{1,0:T(8,128)(2,1)S(1)}, bf16[128,1024]{1,0:T(8,128)(2,1)S(1)}, u32[]{:S(2)}, u32[]{:S(2)}) collective-permute-start(bf16[128,1024]{1,0:T(8,128)(2,1)S(1)} %bitcast.5), channel_id=1, source_target_pairs={{0,2},{1,3},{2,0},{3,1},{4,6},{5,7},{6,4},{7,5},{8,10},{9,11},{10,... | collective-permute-start | bytes 786440 | tf_op jit(solution)/shard_map/ppermute | solution.py:478
  33.8 11.2 %copy-start.2 = (bf16[512,1024]{1,0:T(8,128)(2,1)S(1)}, bf16[512,1024]{1,0:T(8,128)(2,1)}, u32[]{:S(2)}) copy-start(bf16[512,1024]{1,0:T(8,128)(2,1)} %w_a.3) | copy-start | bytes 3145732
  33.8 11.2 %copy-start.3 = (bf16[2,1024,512]{2,1,0:T(8,128)(2,1)S(1)}, bf16[2,1024,512]{2,1,0:T(8,128)(2,1)}, u32[]{:S(2)}) copy-start(bf16[2,1024,512]{2,1,0:T(8,128)(2,1)} %in_a.3) | copy-start | bytes 6291460
  33.8 1.4 %collective-permute-start.13 = (bf16[256,256]{1,0:T(8,128)(2,1)S(1)}, bf16[256,256]{1,0:T(8,128)(2,1)S(1)}, u32[]{:S(2)}, u32[]{:S(2)}) collective-permute-start(bf16[256,256]{1,0:T(8,128)(2,1)S(1)} %get-tuple-element.166), channel_id=1, source_target_pairs={{0,1},{1,0},{2,3},{3,2},{4,5},{5,4},{6,7},{7,6},{8,9},{9,8},{10,11... | collective-permute-start | bytes 393224 | tf_op jit(solution)/shard_map/ppermute | solution.py:475
  35.5 9.2 %collective-permute-start.17 = (bf16[128,1024]{1,0:T(8,128)(2,1)S(1)}, bf16[128,1024]{1,0:T(8,128)(2,1)S(1)}, u32[]{:S(2)}, u32[]{:S(2)}) collective-permute-start(bf16[128,1024]{1,0:T(8,128)(2,1)S(1)} %attn_out_far.1.part), channel_id=1, source_target_pairs={{0,2},{1,3},{2,0},{3,1},{4,6},{5,7},{6,4},{7,5},{8,10},{9,11},{10,... | collective-permute-start | bytes 786440 | tf_op jit(solution)/shard_map/ppermute | solution.py:478
  36.5 13.0 %collective-permute-start.16 = (bf16[128,1024]{1,0:T(8,128)(2,1)S(1)}, bf16[128,1024]{1,0:T(8,128)(2,1)S(1)}, u32[]{:S(2)}, u32[]{:S(2)}) collective-permute-start(bf16[128,1024]{1,0:T(8,128)(2,1)S(1)} %attn_out_own.1.part), channel_id=1, source_target_pairs={{0,2},{1,3},{2,0},{3,1},{4,6},{5,7},{6,4},{7,5},{8,10},{9,11},{10,... | collective-permute-start | bytes 786440 | tf_op jit(solution)/shard_map/ppermute | solution.py:478
  49.6 9.2 %collective-permute-start.19 = (bf16[128,1024]{1,0:T(8,128)(2,1)S(1)}, bf16[128,1024]{1,0:T(8,128)(2,1)S(1)}, u32[]{:S(2)}, u32[]{:S(2)}) collective-permute-start(bf16[128,1024]{1,0:T(8,128)(2,1)S(1)} %get-tuple-element.175.back), channel_id=1, source_target_pairs={{0,2},{1,3},{2,0},{3,1},{4,6},{5,7},{6,4},{7,5},{8,10},{9,11},{10,... | collective-permute-start | bytes 786440 | tf_op jit(solution)/shard_map/ppermute | solution.py:478
  53.2 9.6 %collective-permute-start.18 = (bf16[128,1024]{1,0:T(8,128)(2,1)S(1)}, bf16[128,1024]{1,0:T(8,128)(2,1)S(1)}, u32[]{:S(2)}, u32[]{:S(2)}) collective-permute-start(bf16[128,1024]{1,0:T(8,128)(2,1)S(1)} %get-tuple-element.180.back), channel_id=1, source_target_pairs={{0,2},{1,3},{2,0},{3,1},{4,6},{5,7},{6,4},{7,5},{8,10},{9,11},{10,... | collective-permute-start | bytes 786440 | tf_op jit(solution)/shard_map/ppermute | solution.py:478
  59.3 1.4 %collective-permute-start.20 = (bf16[64,1024]{1,0:T(8,128)(2,1)S(1)}, bf16[64,1024]{1,0:T(8,128)(2,1)S(1)}, u32[]{:S(2)}, u32[]{:S(2)}) collective-permute-start(bf16[64,1024]{1,0:T(8,128)(2,1)S(1)} %get-tuple-element.183), channel_id=1, source_target_pairs={{0,1},{1,0},{2,3},{3,2},{4,5},{5,4},{6,7},{7,6},{8,9},{9,8},{10,11... | collective-permute-start | bytes 393224 | tf_op jit(solution)/shard_map/ppermute | solution.py:475
  59.4 1.5 %collective-permute-start.21 = (bf16[64,1024]{1,0:T(8,128)(2,1)S(1)}, bf16[64,1024]{1,0:T(8,128)(2,1)S(1)}, u32[]{:S(2)}, u32[]{:S(2)}) collective-permute-start(bf16[64,1024]{1,0:T(8,128)(2,1)S(1)} %get-tuple-element.184), channel_id=1, source_target_pairs={{0,1},{1,0},{2,3},{3,2},{4,5},{5,4},{6,7},{7,6},{8,9},{9,8},{10,11... | collective-permute-start | bytes 393224 | tf_op jit(solution)/shard_map/ppermute | solution.py:475
  63.0 1.8 %collective-permute-start.22 = (bf16[128,1024]{1,0:T(8,128)(2,1)S(1)}, bf16[128,1024]{1,0:T(8,128)(2,1)S(1)}, u32[]{:S(2)}, u32[]{:S(2)}) collective-permute-start(bf16[128,1024]{1,0:T(8,128)(2,1)S(1)} %resid_back.1.first.d_resid), channel_id=1, source_target_pairs={{0,1},{1,0},{2,3},{3,2},{4,5},{5,4},{6,7},{7,6},{8,9},{9,8},{10,11... | collective-permute-start | bytes 786440 | tf_op jit(solution)/shard_map/ppermute | solution.py:475
  64.4 1.6 %collective-permute-start.23 = (bf16[128,1024]{1,0:T(8,128)(2,1)S(1)}, bf16[128,1024]{1,0:T(8,128)(2,1)S(1)}, u32[]{:S(2)}, u32[]{:S(2)}) collective-permute-start(bf16[128,1024]{1,0:T(8,128)(2,1)S(1)} %get-tuple-element.204), channel_id=1, source_target_pairs={{0,1},{1,0},{2,3},{3,2},{4,5},{5,4},{6,7},{7,6},{8,9},{9,8},{10,11... | collective-permute-start | bytes 786440 | tf_op jit(solution)/shard_map/ppermute | solution.py:475
  66.4 9.2 %collective-permute-start.27 = (bf16[128,1024]{1,0:T(8,128)(2,1)S(1)}, bf16[128,1024]{1,0:T(8,128)(2,1)S(1)}, u32[]{:S(2)}, u32[]{:S(2)}) collective-permute-start(bf16[128,1024]{1,0:T(8,128)(2,1)S(1)} %back_sum_far.1.part), channel_id=1, source_target_pairs={{0,2},{1,3},{2,0},{3,1},{4,6},{5,7},{6,4},{7,5},{8,10},{9,11},{10,... | collective-permute-start | bytes 786440 | tf_op jit(solution)/shard_map/ppermute | solution.py:478
  67.5 1.4 %collective-permute-start.24 = (bf16[64,1024]{1,0:T(8,128)(2,1)S(1)}, bf16[64,1024]{1,0:T(8,128)(2,1)S(1)}, u32[]{:S(2)}, u32[]{:S(2)}) collective-permute-start(bf16[64,1024]{1,0:T(8,128)(2,1)S(1)} %get-tuple-element.210), channel_id=1, source_target_pairs={{0,1},{1,0},{2,3},{3,2},{4,5},{5,4},{6,7},{7,6},{8,9},{9,8},{10,11... | collective-permute-start | bytes 393224 | tf_op jit(solution)/shard_map/ppermute | solution.py:475
  67.6 1.4 %collective-permute-start.25 = (bf16[64,1024]{1,0:T(8,128)(2,1)S(1)}, bf16[64,1024]{1,0:T(8,128)(2,1)S(1)}, u32[]{:S(2)}, u32[]{:S(2)}) collective-permute-start(bf16[64,1024]{1,0:T(8,128)(2,1)S(1)} %get-tuple-element.211), channel_id=1, source_target_pairs={{0,1},{1,0},{2,3},{3,2},{4,5},{5,4},{6,7},{7,6},{8,9},{9,8},{10,11... | collective-permute-start | bytes 393224 | tf_op jit(solution)/shard_map/ppermute | solution.py:475
  69.5 11.2 %collective-permute-start.26 = (bf16[128,1024]{1,0:T(8,128)(2,1)S(1)}, bf16[128,1024]{1,0:T(8,128)(2,1)S(1)}, u32[]{:S(2)}, u32[]{:S(2)}) collective-permute-start(bf16[128,1024]{1,0:T(8,128)(2,1)S(1)} %back_sum_own.1.part), channel_id=1, source_target_pairs={{0,2},{1,3},{2,0},{3,1},{4,6},{5,7},{6,4},{7,5},{8,10},{9,11},{10,... | collective-permute-start | bytes 786440 | tf_op jit(solution)/shard_map/ppermute | solution.py:478
  75.9 2.5 %collective-permute-start.28 = (bf16[64,1024]{1,0:T(8,128)(2,1)S(1)}, bf16[64,1024]{1,0:T(8,128)(2,1)S(1)}, u32[]{:S(2)}, u32[]{:S(2)}) collective-permute-start(bf16[64,1024]{1,0:T(8,128)(2,1)S(1)} %get-tuple-element.213), channel_id=1, source_target_pairs={{0,1},{1,0},{2,3},{3,2},{4,5},{5,4},{6,7},{7,6},{8,9},{9,8},{10,11... | collective-permute-start | bytes 393224 | tf_op jit(solution)/shard_map/ppermute | solution.py:475
  76.0 2.4 %collective-permute-start.29 = (bf16[64,1024]{1,0:T(8,128)(2,1)S(1)}, bf16[64,1024]{1,0:T(8,128)(2,1)S(1)}, u32[]{:S(2)}, u32[]{:S(2)}) collective-permute-start(bf16[64,1024]{1,0:T(8,128)(2,1)S(1)} %get-tuple-element.214), channel_id=1, source_target_pairs={{0,1},{1,0},{2,3},{3,2},{4,5},{5,4},{6,7},{7,6},{8,9},{9,8},{10,11... | collective-permute-start | bytes 393224 | tf_op jit(solution)/shard_map/ppermute | solution.py:475
  76.8 8.5 %collective-permute-start.36 = (bf16[96,1024]{1,0:T(8,128)(2,1)S(1)}, bf16[96,1024]{1,0:T(8,128)(2,1)S(1)}, u32[]{:S(2)}, u32[]{:S(2)}) collective-permute-start(bf16[96,1024]{1,0:T(8,128)(2,1)S(1)} %get-tuple-element.238), channel_id=1, source_target_pairs={{0,16},{4,20},{8,24},{12,28},{16,0},{20,4},{24,8},{28,12},{1,17},{... | collective-permute-start | bytes 589832 | tf_op jit(solution)/shard_map/ppermute | solution.py:481
  81.0 1.3 %collective-permute-start.30 = (bf16[32,1024]{1,0:T(8,128)(2,1)S(1)}, bf16[32,1024]{1,0:T(8,128)(2,1)S(1)}, u32[]{:S(2)}, u32[]{:S(2)}) collective-permute-start(bf16[32,1024]{1,0:T(8,128)(2,1)S(1)} %get-tuple-element.223), channel_id=1, source_target_pairs={{0,1},{1,0},{2,3},{3,2},{4,5},{5,4},{6,7},{7,6},{8,9},{9,8},{10,11... | collective-permute-start | bytes 196616 | tf_op jit(solution)/shard_map/ppermute | solution.py:475
  81.1 1.4 %collective-permute-start.31 = (bf16[32,1024]{1,0:T(8,128)(2,1)S(1)}, bf16[32,1024]{1,0:T(8,128)(2,1)S(1)}, u32[]{:S(2)}, u32[]{:S(2)}) collective-permute-start(bf16[32,1024]{1,0:T(8,128)(2,1)S(1)} %get-tuple-element.224), channel_id=1, source_target_pairs={{0,1},{1,0},{2,3},{3,2},{4,5},{5,4},{6,7},{7,6},{8,9},{9,8},{10,11... | collective-permute-start | bytes 196616 | tf_op jit(solution)/shard_map/ppermute | solution.py:475
  81.6 1.3 %collective-permute-start.32 = (bf16[32,1024]{1,0:T(8,128)(2,1)S(1)}, bf16[32,1024]{1,0:T(8,128)(2,1)S(1)}, u32[]{:S(2)}, u32[]{:S(2)}) collective-permute-start(bf16[32,1024]{1,0:T(8,128)(2,1)S(1)} %get-tuple-element.225), channel_id=1, source_target_pairs={{0,1},{1,0},{2,3},{3,2},{4,5},{5,4},{6,7},{7,6},{8,9},{9,8},{10,11... | collective-permute-start | bytes 196616 | tf_op jit(solution)/shard_map/ppermute | solution.py:475
  81.7 1.3 %collective-permute-start.33 = (bf16[32,1024]{1,0:T(8,128)(2,1)S(1)}, bf16[32,1024]{1,0:T(8,128)(2,1)S(1)}, u32[]{:S(2)}, u32[]{:S(2)}) collective-permute-start(bf16[32,1024]{1,0:T(8,128)(2,1)S(1)} %get-tuple-element.226), channel_id=1, source_target_pairs={{0,1},{1,0},{2,3},{3,2},{4,5},{5,4},{6,7},{7,6},{8,9},{9,8},{10,11... | collective-permute-start | bytes 196616 | tf_op jit(solution)/shard_map/ppermute | solution.py:475
  83.5 9.2 %collective-permute-start.34 = (bf16[4,128,256]{2,1,0:T(8,128)(2,1)S(1)}, bf16[4,128,256]{2,1,0:T(8,128)(2,1)S(1)}, u32[]{:S(2)}, u32[]{:S(2)}) collective-permute-start(bf16[4,128,256]{2,1,0:T(8,128)(2,1)S(1)} %get-tuple-element.232), channel_id=1, source_target_pairs={{0,16},{4,20},{8,24},{12,28},{16,0},{20,4},{24,8},{28,12},{1,17},{... | collective-permute-start | bytes 786440 | tf_op jit(solution)/shard_map/ppermute | solution.py:481
  86.2 11.6 %collective-permute-start.39 = (bf16[4,128,256]{2,1,0:T(8,128)(2,1)S(1)}, bf16[4,128,256]{2,1,0:T(8,128)(2,1)S(1)}, u32[]{:S(2)}, u32[]{:S(2)}) collective-permute-start(bf16[4,128,256]{2,1,0:T(8,128)(2,1)S(1)} %get-tuple-element.247), channel_id=1, source_target_pairs={{0,16},{4,20},{8,24},{12,28},{16,0},{20,4},{24,8},{28,12},{1,17},{... | collective-permute-start | bytes 786440 | tf_op jit(solution)/shard_map/ppermute | solution.py:481
  86.7 11.9 %collective-permute-start.37 = (bf16[96,1024]{1,0:T(8,128)(2,1)S(1)}, bf16[96,1024]{1,0:T(8,128)(2,1)S(1)}, u32[]{:S(2)}, u32[]{:S(2)}) collective-permute-start(bf16[96,1024]{1,0:T(8,128)(2,1)S(1)} %back_pick.2), channel_id=1, source_target_pairs={{0,8},{4,12},{8,0},{12,4},{16,24},{20,28},{24,16},{28,20},{1,9},{5... | collective-permute-start | bytes 589832 | tf_op jit(solution)/shard_map/ppermute | solution.py:481
  92.8 7.3 %collective-permute-start.35 = (bf16[2,128,256]{2,1,0:T(8,128)(2,1)S(1)}, bf16[2,128,256]{2,1,0:T(8,128)(2,1)S(1)}, u32[]{:S(2)}, u32[]{:S(2)}) collective-permute-start(bf16[2,128,256]{2,1,0:T(8,128)(2,1)S(1)} %get-tuple-element.234), channel_id=1, source_target_pairs={{0,4},{4,0},{8,12},{12,8},{16,20},{20,16},{24,28},{28,24},{1,5},{5... | collective-permute-start | bytes 393224 | tf_op jit(solution)/shard_map/ppermute | solution.py:481
  93.5 12.2 %collective-permute-start.42 = (bf16[128,1024]{1,0:T(8,128)(2,1)S(1)}, bf16[128,1024]{1,0:T(8,128)(2,1)S(1)}, u32[]{:S(2)}, u32[]{:S(2)}) collective-permute-start(bf16[128,1024]{1,0:T(8,128)(2,1)S(1)} %ffn_out_far.1), channel_id=1, source_target_pairs={{0,2},{1,3},{2,0},{3,1},{4,6},{5,7},{6,4},{7,5},{8,10},{9,11},{10,... | collective-permute-start | bytes 786440 | tf_op jit(solution)/shard_map/ppermute | solution.py:478
  97.8 7.5 %collective-permute-start.40 = (bf16[2,128,256]{2,1,0:T(8,128)(2,1)S(1)}, bf16[2,128,256]{2,1,0:T(8,128)(2,1)S(1)}, u32[]{:S(2)}, u32[]{:S(2)}) collective-permute-start(bf16[2,128,256]{2,1,0:T(8,128)(2,1)S(1)} %get-tuple-element.249), channel_id=1, source_target_pairs={{0,4},{4,0},{8,12},{12,8},{16,20},{20,16},{24,28},{28,24},{1,5},{5... | collective-permute-start | bytes 393224 | tf_op jit(solution)/shard_map/ppermute | solution.py:481
  100.1 9.1 %collective-permute-start.43 = (bf16[96,1024]{1,0:T(8,128)(2,1)S(1)}, bf16[96,1024]{1,0:T(8,128)(2,1)S(1)}, u32[]{:S(2)}, u32[]{:S(2)}) collective-permute-start(bf16[96,1024]{1,0:T(8,128)(2,1)S(1)} %back_pick.3), channel_id=1, source_target_pairs={{0,4},{4,0},{8,12},{12,8},{16,20},{20,16},{24,28},{28,24},{1,5},{5... | collective-permute-start | bytes 589832 | tf_op jit(solution)/shard_map/ppermute | solution.py:481
  100.2 7.4 %collective-permute-start.38 = (bf16[1,128,256]{2,1,0:T(8,128)(2,1)S(1)}, bf16[1,128,256]{2,1,0:T(8,128)(2,1)S(1)}, u32[]{:S(2)}, u32[]{:S(2)}) collective-permute-start(bf16[1,128,256]{2,1,0:T(8,128)(2,1)S(1)} %get-tuple-element.241), channel_id=1, source_target_pairs={{0,8},{4,12},{8,0},{12,4},{16,24},{20,28},{24,16},{28,20},{1,9},{5... | collective-permute-start | bytes 196616 | tf_op jit(solution)/shard_map/ppermute | solution.py:481
  105.3 7.5 %collective-permute-start.41 = (bf16[1,128,256]{2,1,0:T(8,128)(2,1)S(1)}, bf16[1,128,256]{2,1,0:T(8,128)(2,1)S(1)}, u32[]{:S(2)}, u32[]{:S(2)}) collective-permute-start(bf16[1,128,256]{2,1,0:T(8,128)(2,1)S(1)} %get-tuple-element.250), channel_id=1, source_target_pairs={{0,8},{4,12},{8,0},{12,4},{16,24},{20,28},{24,16},{28,20},{1,9},{5... | collective-permute-start | bytes 196616 | tf_op jit(solution)/shard_map/ppermute | solution.py:481

commit v12 on v11

--- a/solution.py
+++ b/solution.py
@@ -647,7 +647,7 @@
     half_rows = like((groups * capacity // 2, width), BF16)
     group_bits = [1 << b for b in range(groups.bit_length() - 1)]
     near_bit, pack_far, event_far = group_bits[0], group_bits[1 : packs.bit_length() - 1], group_bits[packs.bit_length() - 1 :]
-    back_bits = event_far[::-1] + pack_far[::-1] + [near_bit]
+    back_bits = event_far[::-1] + [near_bit] + pack_far[::-1]
     kept, back = run(
         functools.partial(back_send, order, back_bits[0]), [half_rows] * 2, [hot, d_packed], name="back_send"
     )
@@ -682,9 +682,11 @@
         shape = (2 ** (len(remaining) - 1), size, cols)
         return [like(shape, F32), like(shape, BF16)]
 
-    def reduce_over(stages, kept, send, name, beside=False):
+    def reduce_over(stages, kept, send, name, beside):
         remaining = list(bits)
         got = crossed(send, 1 << stages[0])
+        if beside == stages[0]:
+            got, arrays[-1] = tie(got, arrays[-1])
         remaining.remove(stages[0])
         for bit in stages[1:]:
             kept, send = run(
@@ -695,7 +697,7 @@
             )
             got = crossed(send, 1 << bit)
             remaining.remove(bit)
-            if beside and bit == stages[1]:
+            if bit == beside:
                 got, arrays[-1] = tie(got, arrays[-1])
         return kept, got
 
@@ -740,10 +742,10 @@
 
     for bit in back_bits[1:-1]:
         send_back(bit)
-    kept1, got1 = reduce_over(event_bits + pack_bits, kept1, send1, "halve1_", True)
-    kept0, got0 = reduce_over(event_bits + pack_bits, kept0, send0, "halve0_")
+    kept1, got1 = reduce_over(event_bits + pack_bits, kept1, send1, "halve1_", event_bits[0])
+    send_back(back_bits[-1])
+    kept0, got0 = reduce_over(event_bits + pack_bits, kept0, send0, "halve0_", pack_bits[0])
     got1, place = tie(got1, place)
-    send_back(back_bits[-1])
     back_places = [held[k] for k in range(groups)]
     got_out = far(out_far)
     (packed_out,) = run(

time: 114 us -> 114 us (level)
  no operation moved by 1% of the time
where the time goes in v12:
time: 114 us
  waiting for transfers between devices  46.5 us (41%)
  starting transfers between devices  38.1 us (33%)
  Pallas kernels  26.8 us (24%)
    pallas_call x36, Pallas kernels, run(): pl.pallas_call(body, out_shape=list(outs), in_specs=[pl.BlockSpec(memory_...  26.8 us
    ppermute x16, starting transfers between devices, crossed(): return lax.ppermute(value, group_axes, [(i, i ^ k) for i in range(groups)])  23 us
    ppermute x16, waiting for transfers between devices, crossed(): return lax.ppermute(value, group_axes, [(i, i ^ k) for i in range(groups)])  21.2 us
    ppermute x9, waiting for transfers between devices, far(): return lax.ppermute(value, 'tensor', [(i, i ^ 2) for i in range(tensors)])  19.6 us
    ppermute x9, starting transfers between devices, far(): return lax.ppermute(value, 'tensor', [(i, i ^ 2) for i in range(tensors)])  10 us
    ppermute x19, waiting for transfers between devices, near(): return lax.ppermute(value, 'tensor', [(i, i ^ 1) for i in range(tensors)])  5.63 us
    ppermute x19, starting transfers between devices, near(): return lax.ppermute(value, 'tensor', [(i, i ^ 1) for i in range(tensors)])  5.12 us
  transfers between devices with their start and end apart: 44, of which 30 were waited for; matrix products, arithmetic and copies ran while one was open for 1% of the time, Pallas kernels for 22%

profile of v12, /device:TPU:0, one launch (start us, length us, event | category | flops | bytes accessed | tf_op | source)
XLA Modules:
  0.0 114.1 jit_solution(8120044432475487747)
XLA Ops:
  0.6 0.5 collective-permute-start
  1.2 0.7 add_bitcast_fusion.code
  1.9 0.9 copy-done.7
  3.2 4.1 %collective-permute-start.2 = (bf16[24,1152]{1,0:T(8,128)(2,1)S(1)}, bf16[24,1152]{1,0:T(8,128)(2,1)S(1)}, u32[]{:S(2)}, u32[]{:S(2)}) collective-permute-start(bf16[24,1152]{1,0:T(8,128)(2,1)S(1)} %get-tuple-element.136), channel_id=1, source_target_pairs={{0,8},{4,12},{8,0},{12,4},{16,24},{20,28},{24,16},{28,20},{1,9},{5... | collective-permute-start | bytes 165896 | tf_op jit(solution)/shard_map/ppermute | solution.py:481
  7.3 1.3 %collective-permute-start.3 = (bf16[24,1152]{1,0:T(8,128)(2,1)S(1)}, bf16[24,1152]{1,0:T(8,128)(2,1)S(1)}, u32[]{:S(2)}, u32[]{:S(2)}) collective-permute-start(bf16[24,1152]{1,0:T(8,128)(2,1)S(1)} %get-tuple-element.137), channel_id=1, source_target_pairs={{0,24},{4,28},{8,16},{12,20},{16,8},{20,12},{24,0},{28,4},{1,25},{... | collective-permute-start | bytes 165896 | tf_op jit(solution)/shard_map/ppermute | solution.py:481
  8.6 3.6 %collective-permute-start.4 = (bf16[24,1152]{1,0:T(8,128)(2,1)S(1)}, bf16[24,1152]{1,0:T(8,128)(2,1)S(1)}, u32[]{:S(2)}, u32[]{:S(2)}) collective-permute-start(bf16[24,1152]{1,0:T(8,128)(2,1)S(1)} %get-tuple-element.144), channel_id=1, source_target_pairs={{0,12},{4,8},{8,4},{12,0},{16,28},{20,24},{24,20},{28,16},{1,13},{... | collective-permute-start | bytes 165896 | tf_op jit(solution)/shard_map/ppermute | solution.py:481
  12.2 0.6 collective-permute-start.5
  12.8 1.1 collective-permute-start.6
  13.9 2.2 %collective-permute-done.3.refs_2_ = bf16[24,1152]{1,0:T(8,128)(2,1)S(1)} collective-permute-done((bf16[24,1152]{1,0:T(8,128)(2,1)S(1)}, bf16[24,1152]{1,0:T(8,128)(2,1)S(1)}, u32[]{:S(2)}, u32[]{:S(2)}) %collective-permute-start.3) | collective-permute-done | bytes 55328 | tf_op jit(solution)/shard_map/ppermute | solution.py:481
  16.4 0.8 turn.1
  17.2 2.0 %collective-permute-done.5.refs_4_ = bf16[24,1152]{1,0:T(8,128)(2,1)S(1)} collective-permute-done((bf16[24,1152]{1,0:T(8,128)(2,1)S(1)}, bf16[24,1152]{1,0:T(8,128)(2,1)S(1)}, u32[]{:S(2)}, u32[]{:S(2)}) %collective-permute-start.5) | collective-permute-done | bytes 55328 | tf_op jit(solution)/shard_map/ppermute | solution.py:481
  19.2 1.9 %collective-permute-done.8.refs_7_ = bf16[24,1152]{1,0:T(8,128)(2,1)S(1)} collective-permute-done((bf16[24,1152]{1,0:T(8,128)(2,1)S(1)}, bf16[24,1152]{1,0:T(8,128)(2,1)S(1)}, u32[]{:S(2)}, u32[]{:S(2)}) %collective-permute-start.8) | collective-permute-done | bytes 55328 | tf_op jit(solution)/shard_map/ppermute | solution.py:481
  21.4 1.6 %collective-permute-start.9 = (bf16[128,1024]{1,0:T(8,128)(2,1)S(1)}, bf16[128,1024]{1,0:T(8,128)(2,1)S(1)}, u32[]{:S(2)}, u32[]{:S(2)}) collective-permute-start(bf16[128,1024]{1,0:T(8,128)(2,1)S(1)} %get-tuple-element.157.refs_0_.refs_3_), channel_id=1, source_target_pairs={{0,2},{1,3},{2,0},{3,1},{4,6},{5,7},{6,4},{7,5},{8,10},{9,11},{10,... | collective-permute-start | bytes 786440 | tf_op jit(solution)/shard_map/ppermute | solution.py:478
  23.0 0.5 collective-permute-start.11
  23.5 0.8 collective-permute-done.10.refs_1_.refs_4_
  24.5 2.2 %encode_first.1 = (f32[256,256]{1,0:T(8,128)S(1)}, bf16[256,1024]{1,0:T(8,128)(2,1)S(1)}, bf16[128,1024]{1,0:T(8,128)(2,1)S(1)}, bf16[4,2,128,256]{3,2,1,0:T(8,128)(2,1)S(1)}) custom-call(bf16[128,1024]{1,0:T(8,128)(2,1)S(1)} %get-tuple-element.157.refs_0_.refs_3_, bf16[64,1024]{1,0:T(8,128)(2,1)S(1)} %collective-permute-done.10.refs_1_.refs_4_, ...), custom_call_target="tpu_custom_call" | custom-call | tf_op jit(solution)/shard_map/encode_first/pallas_call | solution.py:64
  26.8 1.1 collective-permute-done.9.refs_0_.refs_5_
  27.8 0.5 collective-permute-start.12
  28.3 1.5 %collective-permute-start.15 = (bf16[128,1024]{1,0:T(8,128)(2,1)S(1)}, bf16[128,1024]{1,0:T(8,128)(2,1)S(1)}, u32[]{:S(2)}, u32[]{:S(2)}) collective-permute-start(bf16[128,1024]{1,0:T(8,128)(2,1)S(1)} %bitcast.5), channel_id=1, source_target_pairs={{0,2},{1,3},{2,0},{3,1},{4,6},{5,7},{6,4},{7,5},{8,10},{9,11},{10,... | collective-permute-start | bytes 786440 | tf_op jit(solution)/shard_map/ppermute | solution.py:478
  29.9 1.4 %encode_third.1 = (f32[128,256]{1,0:T(8,128)S(1)}, bf16[128,1024]{1,0:T(8,128)(2,1)S(1)}, bf16[128,1024]{1,0:T(8,128)(2,1)S(1)}, bf16[4,1,128,256]{3,2,1,0:T(8,128)(2,1)S(1)}) custom-call(bf16[128,1024]{1,0:T(8,128)(2,1)S(1)} %collective-permute-done.9.refs_0_.refs_5_, bf16[2,1024,1024]{2,1,0:T(8,128)(2,1)S(1)} %copy-done, bf16[4,1024,256]{2,1,0:T(8,128)(2,1)S(1)} %copy-done.1), custom_call_target="tpu_custom_call" | custom-call | tf_op jit(solution)/shard_map/encode_third/pallas_call | solution.py:64
  31.3 2.5 %attend_first.1 = (f32[256,256]{1,0:T(8,128)S(1)}, bf16[256,1024]{1,0:T(8,128)(2,1)S(1)}, bf16[4,4,128,256]{3,2,1,0:T(8,128)(2,1)S(1)}, f32[4,128,256]{2,1,0:T(8...) custom-call(s32[4,1,128]{2,1,0:T(1,128)S(1)} %bitcast.8, ...), custom_call_target="tpu_custom_call" | custom-call | tf_op jit(solution)/shard_map/attend_first/pallas_call | solution.py:64
  33.9 1.3 %collective-permute-done.13.take = bf16[256,256]{1,0:T(8,128)(2,1)S(1)} collective-permute-done((bf16[256,256]{1,0:T(8,128)(2,1)S(1)}, bf16[256,256]{1,0:T(8,128)(2,1)S(1)}, u32[]{:S(2)}, u32[]{:S(2)}) %collective-permute-start.13) | collective-permute-done | bytes 131104 | tf_op jit(solution)/shard_map/ppermute | solution.py:475
  35.5 0.6 collective-permute-start.17
  36.5 1.5 %collective-permute-start.16 = (bf16[128,1024]{1,0:T(8,128)(2,1)S(1)}, bf16[128,1024]{1,0:T(8,128)(2,1)S(1)}, u32[]{:S(2)}, u32[]{:S(2)}) collective-permute-start(bf16[128,1024]{1,0:T(8,128)(2,1)S(1)} %attn_out_own.1.part), channel_id=1, source_target_pairs={{0,2},{1,3},{2,0},{3,1},{4,6},{5,7},{6,4},{7,5},{8,10},{9,11},{10,... | collective-permute-start | bytes 786440 | tf_op jit(solution)/shard_map/ppermute | solution.py:478
  38.1 6.7 %collective-permute-done.17.got = bf16[128,1024]{1,0:T(8,128)(2,1)S(1)} collective-permute-done((bf16[128,1024]{1,0:T(8,128)(2,1)S(1)}, bf16[128,1024]{1,0:T(8,128)(2,1)S(1)}, u32[]{:S(2)}, u32[]{:S(2)}) %collective-permute-start.17) | collective-permute-done | bytes 262176 | tf_op jit(solution)/shard_map/ppermute | solution.py:478
  45.0 2.9 %ffn_own.1 = (bf16[128,1024]{1,0:T(8,128)(2,1)S(1)}, bf16[128,1024]{1,0:T(8,128)(2,1)S(1)}) custom-call(bf16[128,1024]{1,0:T(8,128)(2,1)S(1)} %get-tuple-element.173.rows_ref, bf16[128,1024]{1,0:T(8,128)(2,1)S(1)} %bitcast.6, bf16[2,1024,512]{2,1,0:T(8,128)(2,1)S(1)} %copy-done.3, bf16[2,1024,512]{2,1,0:T(8,128)(2,1)S(1)} %collective-permute-done.in_b, ...), custom_call_target="tpu_custom_call" | custom-call | tf_op jit(solution)/shard_map/ffn_own/pallas_call | solution.py:64
  47.9 1.7 %collective-permute-done.16.got = bf16[128,1024]{1,0:T(8,128)(2,1)S(1)} collective-permute-done((bf16[128,1024]{1,0:T(8,128)(2,1)S(1)}, bf16[128,1024]{1,0:T(8,128)(2,1)S(1)}, u32[]{:S(2)}, u32[]{:S(2)}) %collective-permute-start.16) | collective-permute-done | bytes 262176 | tf_op jit(solution)/shard_map/ppermute | solution.py:478
  49.6 0.5 collective-permute-start.19
  50.3 2.9 %ffn_far.1 = (bf16[128,1024]{1,0:T(8,128)(2,1)S(1)}, bf16[128,1024]{1,0:T(8,128)(2,1)S(1)}) custom-call(bf16[128,1024]{1,0:T(8,128)(2,1)S(1)} %get-tuple-element.180.rows_ref, bf16[128,1024]{1,0:T(8,128)(2,1)S(1)} %collective-permute-done.15.d_out_ref.d_out, bf16[2,1024,512]{2,1,0:T(8,128)(2,1)S(1)} %copy-done.3, ...), custom_call_target="tpu_custom_call" | custom-call | tf_op jit(solution)/shard_map/ffn_far/pallas_call | solution.py:64
  53.2 1.6 %collective-permute-start.18 = (bf16[128,1024]{1,0:T(8,128)(2,1)S(1)}, bf16[128,1024]{1,0:T(8,128)(2,1)S(1)}, u32[]{:S(2)}, u32[]{:S(2)}) collective-permute-start(bf16[128,1024]{1,0:T(8,128)(2,1)S(1)} %get-tuple-element.182.back), channel_id=1, source_target_pairs={{0,2},{1,3},{2,0},{3,1},{4,6},{5,7},{6,4},{7,5},{8,10},{9,11},{10,... | collective-permute-start | bytes 786440 | tf_op jit(solution)/shard_map/ppermute | solution.py:478
  54.8 4.0 %collective-permute-done.19.got = bf16[128,1024]{1,0:T(8,128)(2,1)S(1)} collective-permute-done((bf16[128,1024]{1,0:T(8,128)(2,1)S(1)}, bf16[128,1024]{1,0:T(8,128)(2,1)S(1)}, u32[]{:S(2)}, u32[]{:S(2)}) %collective-permute-start.19) | collective-permute-done | bytes 262176 | tf_op jit(solution)/shard_map/ppermute | solution.py:478
  59.4 0.5 collective-permute-start.21
  59.9 0.8 collective-permute-done.20.fourth_a
  60.9 1.6 %attn_back_first.1 = (bf16[4,128,256]{2,1,0:T(8,128)(2,1)S(1)}, f32[4,128,256]{2,1,0:T(8,128)S(1)}, f32[4,128,256]{2,1,0:T(8,128)S(1)}, bf16[4,128,256]{2,1,0:T(8,128)(2,1)S(1)}) custom-call(s32[4,1,128]{2,1,0:T(1,128)S(1)} %bitcast.9, bf16[128,1024]{1,0:T(8,128)(2,1)S(1)} %get-tuple-element.184.third.d_resid, ...), custom_call_target="tpu_custom_call" | custom-call | tf_op jit(solution)/shard_map/attn_back_first/pallas_call | solution.py:64
  63.2 1.2 %attn_back_own.1 = (bf16[128,1024]{1,0:T(8,128)(2,1)S(1)}, bf16[4,128,256]{2,1,0:T(8,128)(2,1)S(1)}, f32[4,128,256]{2,1,0:T(8,128)S(1)}, f32[4,128,256]{2,1,0:T(8,128)S(1)}, bf16[4,128,256]{2,1,0:T(8,128)(2,1)S(1)}) custom-call(s32[4,1,128]{2,1,0:T(1,128)S(1)} %bitcast.10, ...), custom_call_target="tpu_custom_call", output_to_operand_aliasing={{1}: (5, {}), {2}: (6, {}), {3}: (7, {}), {4}: (8, {})} | custom-call | tf_op jit(solution)/shard_map/attn_back_own/pallas_call | solution.py:64
  64.4 0.5 collective-permute-start.23
  64.8 0.8 attn_back_second.1
  66.4 0.6 collective-permute-start.27
  68.0 0.8 collective-permute-done.24.refs_0_
  69.5 1.6 %collective-permute-start.26 = (bf16[128,1024]{1,0:T(8,128)(2,1)S(1)}, bf16[128,1024]{1,0:T(8,128)(2,1)S(1)}, u32[]{:S(2)}, u32[]{:S(2)}) collective-permute-start(bf16[128,1024]{1,0:T(8,128)(2,1)S(1)} %back_sum_own.1.part), channel_id=1, source_target_pairs={{0,2},{1,3},{2,0},{3,1},{4,6},{5,7},{6,4},{7,5},{8,10},{9,11},{10,... | collective-permute-start | bytes 786440 | tf_op jit(solution)/shard_map/ppermute | solution.py:478
  71.1 4.5 %collective-permute-done.27.got = bf16[128,1024]{1,0:T(8,128)(2,1)S(1)} collective-permute-done((bf16[128,1024]{1,0:T(8,128)(2,1)S(1)}, bf16[128,1024]{1,0:T(8,128)(2,1)S(1)}, u32[]{:S(2)}, u32[]{:S(2)}) %collective-permute-start.27) | collective-permute-done | bytes 262176 | tf_op jit(solution)/shard_map/ppermute | solution.py:478
  76.0 0.5 collective-permute-start.29
  76.8 1.7 %collective-permute-start.35 = (bf16[96,1024]{1,0:T(8,128)(2,1)S(1)}, bf16[96,1024]{1,0:T(8,128)(2,1)S(1)}, u32[]{:S(2)}, u32[]{:S(2)}) collective-permute-start(bf16[96,1024]{1,0:T(8,128)(2,1)S(1)} %get-tuple-element.238), channel_id=1, source_target_pairs={{0,16},{4,20},{8,24},{12,28},{16,0},{20,4},{24,8},{28,12},{1,17},{... | collective-permute-start | bytes 589832 | tf_op jit(solution)/shard_map/ppermute | solution.py:481
  78.4 1.0 enc_grads_first.1
  79.4 1.3 %collective-permute-done.26.got = bf16[128,1024]{1,0:T(8,128)(2,1)S(1)} collective-permute-done((bf16[128,1024]{1,0:T(8,128)(2,1)S(1)}, bf16[128,1024]{1,0:T(8,128)(2,1)S(1)}, u32[]{:S(2)}, u32[]{:S(2)}) %collective-permute-start.26) | collective-permute-done | bytes 262176 | tf_op jit(solution)/shard_map/ppermute | solution.py:478
  81.1 0.5 collective-permute-start.31
  83.0 0.5 enc_grad1_second.1
  83.5 1.7 %collective-permute-start.34 = (bf16[4,128,256]{2,1,0:T(8,128)(2,1)S(1)}, bf16[4,128,256]{2,1,0:T(8,128)(2,1)S(1)}, u32[]{:S(2)}, u32[]{:S(2)}) collective-permute-start(bf16[4,128,256]{2,1,0:T(8,128)(2,1)S(1)} %get-tuple-element.234), channel_id=1, source_target_pairs={{0,16},{4,20},{8,24},{12,28},{16,0},{20,4},{24,8},{28,12},{1,17},{... | collective-permute-start | bytes 786440 | tf_op jit(solution)/shard_map/ppermute | solution.py:481
  85.3 1.0 enc_grad0_second.1
  86.3 0.6 collective-permute-start.39
  87.4 0.6 collective-permute-start.43
  88.0 4.2 %collective-permute-done.36.refs_2_ = bf16[96,1024]{1,0:T(8,128)(2,1)S(1)} collective-permute-done((bf16[96,1024]{1,0:T(8,128)(2,1)S(1)}, bf16[96,1024]{1,0:T(8,128)(2,1)S(1)}, u32[]{:S(2)}, u32[]{:S(2)}) %collective-permute-start.36) | collective-permute-done | bytes 196640 | tf_op jit(solution)/shard_map/ppermute | solution.py:481
  92.2 0.5 collective-permute-done.34.got
  92.7 2.3 %collective-permute-start.41 = (bf16[96,1024]{1,0:T(8,128)(2,1)S(1)}, bf16[96,1024]{1,0:T(8,128)(2,1)S(1)}, u32[]{:S(2)}, u32[]{:S(2)}) collective-permute-start(bf16[96,1024]{1,0:T(8,128)(2,1)S(1)} %back_pick.3), channel_id=1, source_target_pairs={{0,8},{4,12},{8,0},{12,4},{16,24},{20,28},{24,16},{28,20},{1,9},{5... | collective-permute-start | bytes 589832 | tf_op jit(solution)/shard_map/ppermute | solution.py:481
  95.1 2.3 %collective-permute-start.37 = (bf16[2,128,256]{2,1,0:T(8,128)(2,1)S(1)}, bf16[2,128,256]{2,1,0:T(8,128)(2,1)S(1)}, u32[]{:S(2)}, u32[]{:S(2)}) collective-permute-start(bf16[2,128,256]{2,1,0:T(8,128)(2,1)S(1)} %get-tuple-element.242), channel_id=1, source_target_pairs={{0,4},{4,0},{8,12},{12,8},{16,20},{20,16},{24,28},{28,24},{1,5},{5... | collective-permute-start | bytes 393224 | tf_op jit(solution)/shard_map/ppermute | solution.py:481
  98.0 6.5 %collective-permute-done.37.got = bf16[2,128,256]{2,1,0:T(8,128)(2,1)S(1)} collective-permute-done((bf16[2,128,256]{2,1,0:T(8,128)(2,1)S(1)}, bf16[2,128,256]{2,1,0:T(8,128)(2,1)S(1)}, u32[]{:S(2)}, u32[]{:S(2)}) %collective-permute-start.37) | collective-permute-done | bytes 131104 | tf_op jit(solution)/shard_map/ppermute | solution.py:481
  104.6 1.0 collective-permute-start.38
  105.6 1.1 collective-permute-done.40.got
  106.7 2.2 %collective-permute-start.42 = (bf16[1,128,256]{2,1,0:T(8,128)(2,1)S(1)}, bf16[1,128,256]{2,1,0:T(8,128)(2,1)S(1)}, u32[]{:S(2)}, u32[]{:S(2)}) collective-permute-start(bf16[1,128,256]{2,1,0:T(8,128)(2,1)S(1)} %get-tuple-element.254), channel_id=1, source_target_pairs={{0,8},{4,12},{8,0},{12,4},{16,24},{20,28},{24,16},{28,20},{1,9},{5... | collective-permute-start | bytes 196616 | tf_op jit(solution)/shard_map/ppermute | solution.py:481
  108.9 1.2 %ffn_out_own.1 = bf16[128,1024]{1,0:T(8,128)(2,1)} custom-call(bf16[128,1024]{1,0:T(8,128)(2,1)S(1)} %get-tuple-element.255.hidden, bf16[512,1024]{1,0:T(8,128)(2,1)S(1)} %copy-done.2, bf16[512,1024]{1,0:T(8,128)(2,1)S(1)} %collective-permute-done.1.out_b.w_b, bf16[128,1024]{1,0:T(8,128)(2,1)S(1)} %get-tuple-element.192.resid, ...), custom_call_target="tpu_custom_call" | custom-call | tf_op jit(solution)/shard_map/ffn_out_own/pallas_call | solution.py:64
  110.1 1.1 collective-permute-done.38.got1
  111.1 1.0 back_recv.1
  112.1 1.3 %collective-permute-done.42.got0 = bf16[1,128,256]{2,1,0:T(8,128)(2,1)S(1)} collective-permute-done((bf16[1,128,256]{2,1,0:T(8,128)(2,1)S(1)}, bf16[1,128,256]{2,1,0:T(8,128)(2,1)S(1)}, u32[]{:S(2)}, u32[]{:S(2)}) %collective-permute-start.42) | collective-permute-done | bytes 65568 | tf_op jit(solution)/shard_map/ppermute | solution.py:481
  113.3 0.7 finish.1
  (77 shorter events, 10.0 us)
Async XLA Ops:
  0.6 7.9 %collective-permute-start = (bf16[2,1024,512]{2,1,0:T(8,128)(2,1)}, bf16[2,1024,512]{2,1,0:T(8,128)(2,1)S(1)}, u32[]{:S(2)}, u32[]{:S(2)}) collective-permute-start(bf16[2,1024,512]{2,1,0:T(8,128)(2,1)} %in_a.3), channel_id=1, source_target_pairs={{0,1},{1,0},{2,3},{3,2},{4,5},{5,4},{6,7},{7,6},{8,9},{9,8},{10,11... | collective-permute-start | bytes 6291464 | tf_op jit(solution)/shard_map/ppermute | solution.py:475
  1.1 7.4 %collective-permute-start.1 = (bf16[512,1024]{1,0:T(8,128)(2,1)}, bf16[512,1024]{1,0:T(8,128)(2,1)S(1)}, u32[]{:S(2)}, u32[]{:S(2)}) collective-permute-start(bf16[512,1024]{1,0:T(8,128)(2,1)} %w_a.3), channel_id=1, source_target_pairs={{0,1},{1,0},{2,3},{3,2},{4,5},{5,4},{6,7},{7,6},{8,9},{9,8},{10,11... | collective-permute-start | bytes 3145736 | tf_op jit(solution)/shard_map/ppermute | solution.py:475
  1.9 0.9 copy-start.7
  2.9 13.5 %copy-start.1 = (bf16[4,1024,256]{2,1,0:T(8,128)(2,1)S(1)}, bf16[4,1024,256]{2,1,0:T(8,128)(2,1)}, u32[]{:S(2)}) copy-start(bf16[4,1024,256]{2,1,0:T(8,128)(2,1)} %w_in.1) | copy-start | bytes 6291460
  2.9 13.5 %copy-start.4 = (bf16[256,1024]{1,0:T(8,128)(2,1)S(1)}, bf16[256,1024]{1,0:T(8,128)(2,1)}, u32[]{:S(2)}) copy-start(bf16[256,1024]{1,0:T(8,128)(2,1)} %w_own.3) | copy-start | bytes 1572868
  2.9 21.6 %copy-start = (bf16[2,1024,1024]{2,1,0:T(8,128)(2,1)S(1)}, bf16[2,1024,1024]{2,1,0:T(8,128)(2,1)}, u32[]{:S(2)}) copy-start(bf16[2,1024,1024]{2,1,0:T(8,128)(2,1)} %refs_8_.3) | copy-start | bytes 12582916
  3.2 10.6 %collective-permute-start.2 = (bf16[24,1152]{1,0:T(8,128)(2,1)S(1)}, bf16[24,1152]{1,0:T(8,128)(2,1)S(1)}, u32[]{:S(2)}, u32[]{:S(2)}) collective-permute-start(bf16[24,1152]{1,0:T(8,128)(2,1)S(1)} %get-tuple-element.136), channel_id=1, source_target_pairs={{0,8},{4,12},{8,0},{12,4},{16,24},{20,28},{24,16},{28,20},{1,9},{5... | collective-permute-start | bytes 165896 | tf_op jit(solution)/shard_map/ppermute | solution.py:481
  7.3 8.8 %collective-permute-start.3 = (bf16[24,1152]{1,0:T(8,128)(2,1)S(1)}, bf16[24,1152]{1,0:T(8,128)(2,1)S(1)}, u32[]{:S(2)}, u32[]{:S(2)}) collective-permute-start(bf16[24,1152]{1,0:T(8,128)(2,1)S(1)} %get-tuple-element.137), channel_id=1, source_target_pairs={{0,24},{4,28},{8,16},{12,20},{16,8},{20,12},{24,0},{28,4},{1,25},{... | collective-permute-start | bytes 165896 | tf_op jit(solution)/shard_map/ppermute | solution.py:481
  8.6 8.6 %collective-permute-start.4 = (bf16[24,1152]{1,0:T(8,128)(2,1)S(1)}, bf16[24,1152]{1,0:T(8,128)(2,1)S(1)}, u32[]{:S(2)}, u32[]{:S(2)}) collective-permute-start(bf16[24,1152]{1,0:T(8,128)(2,1)S(1)} %get-tuple-element.144), channel_id=1, source_target_pairs={{0,12},{4,8},{8,4},{12,0},{16,28},{20,24},{24,20},{28,16},{1,13},{... | collective-permute-start | bytes 165896 | tf_op jit(solution)/shard_map/ppermute | solution.py:481
  12.2 7.0 %collective-permute-start.5 = (bf16[24,1152]{1,0:T(8,128)(2,1)S(1)}, bf16[24,1152]{1,0:T(8,128)(2,1)S(1)}, u32[]{:S(2)}, u32[]{:S(2)}) collective-permute-start(bf16[24,1152]{1,0:T(8,128)(2,1)S(1)} %get-tuple-element.145), channel_id=1, source_target_pairs={{0,28},{4,24},{8,20},{12,16},{16,12},{20,8},{24,4},{28,0},{1,29},{... | collective-permute-start | bytes 165896 | tf_op jit(solution)/shard_map/ppermute | solution.py:481
  12.8 6.4 %collective-permute-start.6 = (bf16[24,1152]{1,0:T(8,128)(2,1)S(1)}, bf16[24,1152]{1,0:T(8,128)(2,1)S(1)}, u32[]{:S(2)}, u32[]{:S(2)}) collective-permute-start(bf16[24,1152]{1,0:T(8,128)(2,1)S(1)} %get-tuple-element.146), channel_id=1, source_target_pairs={{0,16},{4,20},{8,24},{12,28},{16,0},{20,4},{24,8},{28,12},{1,17},{... | collective-permute-start | bytes 165896 | tf_op jit(solution)/shard_map/ppermute | solution.py:481
  13.9 5.3 %collective-permute-start.7 = (bf16[24,1152]{1,0:T(8,128)(2,1)S(1)}, bf16[24,1152]{1,0:T(8,128)(2,1)S(1)}, u32[]{:S(2)}, u32[]{:S(2)}) collective-permute-start(bf16[24,1152]{1,0:T(8,128)(2,1)S(1)} %get-tuple-element.147), channel_id=1, source_target_pairs={{0,4},{4,0},{8,12},{12,8},{16,20},{20,16},{24,28},{28,24},{1,5},{5... | collective-permute-start | bytes 165896 | tf_op jit(solution)/shard_map/ppermute | solution.py:481
  16.1 5.1 %collective-permute-start.8 = (bf16[24,1152]{1,0:T(8,128)(2,1)S(1)}, bf16[24,1152]{1,0:T(8,128)(2,1)S(1)}, u32[]{:S(2)}, u32[]{:S(2)}) collective-permute-start(bf16[24,1152]{1,0:T(8,128)(2,1)S(1)} %get-tuple-element.148), channel_id=1, source_target_pairs={{0,20},{4,16},{8,28},{12,24},{16,4},{20,0},{24,12},{28,8},{1,21},{... | collective-permute-start | bytes 165896 | tf_op jit(solution)/shard_map/ppermute | solution.py:481
  21.4 6.4 %collective-permute-start.9 = (bf16[128,1024]{1,0:T(8,128)(2,1)S(1)}, bf16[128,1024]{1,0:T(8,128)(2,1)S(1)}, u32[]{:S(2)}, u32[]{:S(2)}) collective-permute-start(bf16[128,1024]{1,0:T(8,128)(2,1)S(1)} %get-tuple-element.157.refs_0_.refs_3_), channel_id=1, source_target_pairs={{0,2},{1,3},{2,0},{3,1},{4,6},{5,7},{6,4},{7,5},{8,10},{9,11},{10,... | collective-permute-start | bytes 786440 | tf_op jit(solution)/shard_map/ppermute | solution.py:478
  23.0 1.3 %collective-permute-start.10 = (bf16[64,1024]{1,0:T(8,128)(2,1)S(1)}, bf16[64,1024]{1,0:T(8,128)(2,1)S(1)}, u32[]{:S(2)}, u32[]{:S(2)}) collective-permute-start(bf16[64,1024]{1,0:T(8,128)(2,1)S(1)} %get-tuple-element.158), channel_id=1, source_target_pairs={{0,1},{1,0},{2,3},{3,2},{4,5},{5,4},{6,7},{7,6},{8,9},{9,8},{10,11... | collective-permute-start | bytes 393224 | tf_op jit(solution)/shard_map/ppermute | solution.py:475
  23.0 5.4 %copy-start.5 = (bf16[1,128,1024]{2,1,0:T(8,128)(2,1)S(1)}, bf16[1,128,1024]{2,1,0:T(8,128)(2,1)}, u32[]{:S(2)}) copy-start(bf16[1,128,1024]{2,1,0:T(8,128)(2,1)} %param.19) | copy-start | bytes 786436
  23.0 1.5 %collective-permute-start.11 = (bf16[64,1024]{1,0:T(8,128)(2,1)S(1)}, bf16[64,1024]{1,0:T(8,128)(2,1)S(1)}, u32[]{:S(2)}, u32[]{:S(2)}) collective-permute-start(bf16[64,1024]{1,0:T(8,128)(2,1)S(1)} %get-tuple-element.159), channel_id=1, source_target_pairs={{0,1},{1,0},{2,3},{3,2},{4,5},{5,4},{6,7},{7,6},{8,9},{9,8},{10,11... | collective-permute-start | bytes 393224 | tf_op jit(solution)/shard_map/ppermute | solution.py:475
  27.8 3.4 %copy-start.6 = (s32[1,512]{1,0:T(1,128)S(1)}, s32[1,512]{1,0:T(1,128)}, u32[]{:S(2)}) copy-start(s32[1,512]{1,0:T(1,128)} %param.13) | copy-start | bytes 6148
  27.8 7.4 %collective-permute-start.14 = (bf16[256,1024]{1,0:T(8,128)(2,1)S(1)}, bf16[256,1024]{1,0:T(8,128)(2,1)S(1)}, u32[]{:S(2)}, u32[]{:S(2)}) collective-permute-start(bf16[256,1024]{1,0:T(8,128)(2,1)S(1)} %copy-done.4), channel_id=1, source_target_pairs={{0,1},{1,0},{2,3},{3,2},{4,5},{5,4},{6,7},{7,6},{8,9},{9,8},{10,11... | collective-permute-start | bytes 1572872 | tf_op jit(solution)/shard_map/ppermute | solution.py:475
  27.8 3.4 %collective-permute-start.12 = (bf16[128,1024]{1,0:T(8,128)(2,1)S(1)}, bf16[128,1024]{1,0:T(8,128)(2,1)S(1)}, u32[]{:S(2)}, u32[]{:S(2)}) collective-permute-start(bf16[128,1024]{1,0:T(8,128)(2,1)S(1)} %collective-permute-done.9.refs_0_.refs_5_), channel_id=1, source_target_pairs={{0,1},{1,0},{2,3},{3,2},{4,5},{5,4},{6,7},{7,6},{8,9},{9,8},{10,11... | collective-permute-start | bytes 786440 | tf_op jit(solution)/shard_map/ppermute | solution.py:475
  28.3 8.2 %collective-permute-start.15 = (bf16[128,1024]{1,0:T(8,128)(2,1)S(1)}, bf16[128,1024]{1,0:T(8,128)(2,1)S(1)}, u32[]{:S(2)}, u32[]{:S(2)}) collective-permute-start(bf16[128,1024]{1,0:T(8,128)(2,1)S(1)} %bitcast.5), channel_id=1, source_target_pairs={{0,2},{1,3},{2,0},{3,1},{4,6},{5,7},{6,4},{7,5},{8,10},{9,11},{10,... | collective-permute-start | bytes 786440 | tf_op jit(solution)/shard_map/ppermute | solution.py:478
  33.8 11.2 %copy-start.2 = (bf16[512,1024]{1,0:T(8,128)(2,1)S(1)}, bf16[512,1024]{1,0:T(8,128)(2,1)}, u32[]{:S(2)}) copy-start(bf16[512,1024]{1,0:T(8,128)(2,1)} %w_a.3) | copy-start | bytes 3145732
  33.8 11.2 %copy-start.3 = (bf16[2,1024,512]{2,1,0:T(8,128)(2,1)S(1)}, bf16[2,1024,512]{2,1,0:T(8,128)(2,1)}, u32[]{:S(2)}) copy-start(bf16[2,1024,512]{2,1,0:T(8,128)(2,1)} %in_a.3) | copy-start | bytes 6291460
  33.8 1.4 %collective-permute-start.13 = (bf16[256,256]{1,0:T(8,128)(2,1)S(1)}, bf16[256,256]{1,0:T(8,128)(2,1)S(1)}, u32[]{:S(2)}, u32[]{:S(2)}) collective-permute-start(bf16[256,256]{1,0:T(8,128)(2,1)S(1)} %get-tuple-element.168), channel_id=1, source_target_pairs={{0,1},{1,0},{2,3},{3,2},{4,5},{5,4},{6,7},{7,6},{8,9},{9,8},{10,11... | collective-permute-start | bytes 393224 | tf_op jit(solution)/shard_map/ppermute | solution.py:475
  35.5 9.2 %collective-permute-start.17 = (bf16[128,1024]{1,0:T(8,128)(2,1)S(1)}, bf16[128,1024]{1,0:T(8,128)(2,1)S(1)}, u32[]{:S(2)}, u32[]{:S(2)}) collective-permute-start(bf16[128,1024]{1,0:T(8,128)(2,1)S(1)} %attn_out_far.1.part), channel_id=1, source_target_pairs={{0,2},{1,3},{2,0},{3,1},{4,6},{5,7},{6,4},{7,5},{8,10},{9,11},{10,... | collective-permute-start | bytes 786440 | tf_op jit(solution)/shard_map/ppermute | solution.py:478
  36.5 13.0 %collective-permute-start.16 = (bf16[128,1024]{1,0:T(8,128)(2,1)S(1)}, bf16[128,1024]{1,0:T(8,128)(2,1)S(1)}, u32[]{:S(2)}, u32[]{:S(2)}) collective-permute-start(bf16[128,1024]{1,0:T(8,128)(2,1)S(1)} %attn_out_own.1.part), channel_id=1, source_target_pairs={{0,2},{1,3},{2,0},{3,1},{4,6},{5,7},{6,4},{7,5},{8,10},{9,11},{10,... | collective-permute-start | bytes 786440 | tf_op jit(solution)/shard_map/ppermute | solution.py:478
  49.6 9.2 %collective-permute-start.19 = (bf16[128,1024]{1,0:T(8,128)(2,1)S(1)}, bf16[128,1024]{1,0:T(8,128)(2,1)S(1)}, u32[]{:S(2)}, u32[]{:S(2)}) collective-permute-start(bf16[128,1024]{1,0:T(8,128)(2,1)S(1)} %get-tuple-element.177.back), channel_id=1, source_target_pairs={{0,2},{1,3},{2,0},{3,1},{4,6},{5,7},{6,4},{7,5},{8,10},{9,11},{10,... | collective-permute-start | bytes 786440 | tf_op jit(solution)/shard_map/ppermute | solution.py:478
  53.2 9.6 %collective-permute-start.18 = (bf16[128,1024]{1,0:T(8,128)(2,1)S(1)}, bf16[128,1024]{1,0:T(8,128)(2,1)S(1)}, u32[]{:S(2)}, u32[]{:S(2)}) collective-permute-start(bf16[128,1024]{1,0:T(8,128)(2,1)S(1)} %get-tuple-element.182.back), channel_id=1, source_target_pairs={{0,2},{1,3},{2,0},{3,1},{4,6},{5,7},{6,4},{7,5},{8,10},{9,11},{10,... | collective-permute-start | bytes 786440 | tf_op jit(solution)/shard_map/ppermute | solution.py:478
  59.3 1.4 %collective-permute-start.20 = (bf16[64,1024]{1,0:T(8,128)(2,1)S(1)}, bf16[64,1024]{1,0:T(8,128)(2,1)S(1)}, u32[]{:S(2)}, u32[]{:S(2)}) collective-permute-start(bf16[64,1024]{1,0:T(8,128)(2,1)S(1)} %get-tuple-element.185), channel_id=1, source_target_pairs={{0,1},{1,0},{2,3},{3,2},{4,5},{5,4},{6,7},{7,6},{8,9},{9,8},{10,11... | collective-permute-start | bytes 393224 | tf_op jit(solution)/shard_map/ppermute | solution.py:475
  59.4 1.5 %collective-permute-start.21 = (bf16[64,1024]{1,0:T(8,128)(2,1)S(1)}, bf16[64,1024]{1,0:T(8,128)(2,1)S(1)}, u32[]{:S(2)}, u32[]{:S(2)}) collective-permute-start(bf16[64,1024]{1,0:T(8,128)(2,1)S(1)} %get-tuple-element.186), channel_id=1, source_target_pairs={{0,1},{1,0},{2,3},{3,2},{4,5},{5,4},{6,7},{7,6},{8,9},{9,8},{10,11... | collective-permute-start | bytes 393224 | tf_op jit(solution)/shard_map/ppermute | solution.py:475
  63.0 1.8 %collective-permute-start.22 = (bf16[128,1024]{1,0:T(8,128)(2,1)S(1)}, bf16[128,1024]{1,0:T(8,128)(2,1)S(1)}, u32[]{:S(2)}, u32[]{:S(2)}) collective-permute-start(bf16[128,1024]{1,0:T(8,128)(2,1)S(1)} %resid_back.1.first.d_resid), channel_id=1, source_target_pairs={{0,1},{1,0},{2,3},{3,2},{4,5},{5,4},{6,7},{7,6},{8,9},{9,8},{10,11... | collective-permute-start | bytes 786440 | tf_op jit(solution)/shard_map/ppermute | solution.py:475
  64.4 1.6 %collective-permute-start.23 = (bf16[128,1024]{1,0:T(8,128)(2,1)S(1)}, bf16[128,1024]{1,0:T(8,128)(2,1)S(1)}, u32[]{:S(2)}, u32[]{:S(2)}) collective-permute-start(bf16[128,1024]{1,0:T(8,128)(2,1)S(1)} %get-tuple-element.206), channel_id=1, source_target_pairs={{0,1},{1,0},{2,3},{3,2},{4,5},{5,4},{6,7},{7,6},{8,9},{9,8},{10,11... | collective-permute-start | bytes 786440 | tf_op jit(solution)/shard_map/ppermute | solution.py:475
  66.4 9.2 %collective-permute-start.27 = (bf16[128,1024]{1,0:T(8,128)(2,1)S(1)}, bf16[128,1024]{1,0:T(8,128)(2,1)S(1)}, u32[]{:S(2)}, u32[]{:S(2)}) collective-permute-start(bf16[128,1024]{1,0:T(8,128)(2,1)S(1)} %back_sum_far.1.part), channel_id=1, source_target_pairs={{0,2},{1,3},{2,0},{3,1},{4,6},{5,7},{6,4},{7,5},{8,10},{9,11},{10,... | collective-permute-start | bytes 786440 | tf_op jit(solution)/shard_map/ppermute | solution.py:478
  67.5 1.4 %collective-permute-start.24 = (bf16[64,1024]{1,0:T(8,128)(2,1)S(1)}, bf16[64,1024]{1,0:T(8,128)(2,1)S(1)}, u32[]{:S(2)}, u32[]{:S(2)}) collective-permute-start(bf16[64,1024]{1,0:T(8,128)(2,1)S(1)} %get-tuple-element.212), channel_id=1, source_target_pairs={{0,1},{1,0},{2,3},{3,2},{4,5},{5,4},{6,7},{7,6},{8,9},{9,8},{10,11... | collective-permute-start | bytes 393224 | tf_op jit(solution)/shard_map/ppermute | solution.py:475
  67.6 1.4 %collective-permute-start.25 = (bf16[64,1024]{1,0:T(8,128)(2,1)S(1)}, bf16[64,1024]{1,0:T(8,128)(2,1)S(1)}, u32[]{:S(2)}, u32[]{:S(2)}) collective-permute-start(bf16[64,1024]{1,0:T(8,128)(2,1)S(1)} %get-tuple-element.213), channel_id=1, source_target_pairs={{0,1},{1,0},{2,3},{3,2},{4,5},{5,4},{6,7},{7,6},{8,9},{9,8},{10,11... | collective-permute-start | bytes 393224 | tf_op jit(solution)/shard_map/ppermute | solution.py:475
  69.5 11.2 %collective-permute-start.26 = (bf16[128,1024]{1,0:T(8,128)(2,1)S(1)}, bf16[128,1024]{1,0:T(8,128)(2,1)S(1)}, u32[]{:S(2)}, u32[]{:S(2)}) collective-permute-start(bf16[128,1024]{1,0:T(8,128)(2,1)S(1)} %back_sum_own.1.part), channel_id=1, source_target_pairs={{0,2},{1,3},{2,0},{3,1},{4,6},{5,7},{6,4},{7,5},{8,10},{9,11},{10,... | collective-permute-start | bytes 786440 | tf_op jit(solution)/shard_map/ppermute | solution.py:478
  75.9 2.5 %collective-permute-start.28 = (bf16[64,1024]{1,0:T(8,128)(2,1)S(1)}, bf16[64,1024]{1,0:T(8,128)(2,1)S(1)}, u32[]{:S(2)}, u32[]{:S(2)}) collective-permute-start(bf16[64,1024]{1,0:T(8,128)(2,1)S(1)} %get-tuple-element.215), channel_id=1, source_target_pairs={{0,1},{1,0},{2,3},{3,2},{4,5},{5,4},{6,7},{7,6},{8,9},{9,8},{10,11... | collective-permute-start | bytes 393224 | tf_op jit(solution)/shard_map/ppermute | solution.py:475
  76.0 2.4 %collective-permute-start.29 = (bf16[64,1024]{1,0:T(8,128)(2,1)S(1)}, bf16[64,1024]{1,0:T(8,128)(2,1)S(1)}, u32[]{:S(2)}, u32[]{:S(2)}) collective-permute-start(bf16[64,1024]{1,0:T(8,128)(2,1)S(1)} %get-tuple-element.216), channel_id=1, source_target_pairs={{0,1},{1,0},{2,3},{3,2},{4,5},{5,4},{6,7},{7,6},{8,9},{9,8},{10,11... | collective-permute-start | bytes 393224 | tf_op jit(solution)/shard_map/ppermute | solution.py:475
  76.8 8.5 %collective-permute-start.35 = (bf16[96,1024]{1,0:T(8,128)(2,1)S(1)}, bf16[96,1024]{1,0:T(8,128)(2,1)S(1)}, u32[]{:S(2)}, u32[]{:S(2)}) collective-permute-start(bf16[96,1024]{1,0:T(8,128)(2,1)S(1)} %get-tuple-element.238), channel_id=1, source_target_pairs={{0,16},{4,20},{8,24},{12,28},{16,0},{20,4},{24,8},{28,12},{1,17},{... | collective-permute-start | bytes 589832 | tf_op jit(solution)/shard_map/ppermute | solution.py:481
  81.0 1.3 %collective-permute-start.30 = (bf16[32,1024]{1,0:T(8,128)(2,1)S(1)}, bf16[32,1024]{1,0:T(8,128)(2,1)S(1)}, u32[]{:S(2)}, u32[]{:S(2)}) collective-permute-start(bf16[32,1024]{1,0:T(8,128)(2,1)S(1)} %get-tuple-element.225), channel_id=1, source_target_pairs={{0,1},{1,0},{2,3},{3,2},{4,5},{5,4},{6,7},{7,6},{8,9},{9,8},{10,11... | collective-permute-start | bytes 196616 | tf_op jit(solution)/shard_map/ppermute | solution.py:475
  81.1 1.4 %collective-permute-start.31 = (bf16[32,1024]{1,0:T(8,128)(2,1)S(1)}, bf16[32,1024]{1,0:T(8,128)(2,1)S(1)}, u32[]{:S(2)}, u32[]{:S(2)}) collective-permute-start(bf16[32,1024]{1,0:T(8,128)(2,1)S(1)} %get-tuple-element.226), channel_id=1, source_target_pairs={{0,1},{1,0},{2,3},{3,2},{4,5},{5,4},{6,7},{7,6},{8,9},{9,8},{10,11... | collective-permute-start | bytes 196616 | tf_op jit(solution)/shard_map/ppermute | solution.py:475
  81.6 1.3 %collective-permute-start.32 = (bf16[32,1024]{1,0:T(8,128)(2,1)S(1)}, bf16[32,1024]{1,0:T(8,128)(2,1)S(1)}, u32[]{:S(2)}, u32[]{:S(2)}) collective-permute-start(bf16[32,1024]{1,0:T(8,128)(2,1)S(1)} %get-tuple-element.227), channel_id=1, source_target_pairs={{0,1},{1,0},{2,3},{3,2},{4,5},{5,4},{6,7},{7,6},{8,9},{9,8},{10,11... | collective-permute-start | bytes 196616 | tf_op jit(solution)/shard_map/ppermute | solution.py:475
  81.7 1.3 %collective-permute-start.33 = (bf16[32,1024]{1,0:T(8,128)(2,1)S(1)}, bf16[32,1024]{1,0:T(8,128)(2,1)S(1)}, u32[]{:S(2)}, u32[]{:S(2)}) collective-permute-start(bf16[32,1024]{1,0:T(8,128)(2,1)S(1)} %get-tuple-element.228), channel_id=1, source_target_pairs={{0,1},{1,0},{2,3},{3,2},{4,5},{5,4},{6,7},{7,6},{8,9},{9,8},{10,11... | collective-permute-start | bytes 196616 | tf_op jit(solution)/shard_map/ppermute | solution.py:475
  83.5 9.2 %collective-permute-start.34 = (bf16[4,128,256]{2,1,0:T(8,128)(2,1)S(1)}, bf16[4,128,256]{2,1,0:T(8,128)(2,1)S(1)}, u32[]{:S(2)}, u32[]{:S(2)}) collective-permute-start(bf16[4,128,256]{2,1,0:T(8,128)(2,1)S(1)} %get-tuple-element.234), channel_id=1, source_target_pairs={{0,16},{4,20},{8,24},{12,28},{16,0},{20,4},{24,8},{28,12},{1,17},{... | collective-permute-start | bytes 786440 | tf_op jit(solution)/shard_map/ppermute | solution.py:481
  85.2 6.9 %collective-permute-start.36 = (bf16[96,1024]{1,0:T(8,128)(2,1)S(1)}, bf16[96,1024]{1,0:T(8,128)(2,1)S(1)}, u32[]{:S(2)}, u32[]{:S(2)}) collective-permute-start(bf16[96,1024]{1,0:T(8,128)(2,1)S(1)} %back_pick.2), channel_id=1, source_target_pairs={{0,4},{4,0},{8,12},{12,8},{16,20},{20,16},{24,28},{28,24},{1,5},{5... | collective-permute-start | bytes 589832 | tf_op jit(solution)/shard_map/ppermute | solution.py:481
  86.3 11.5 %collective-permute-start.39 = (bf16[4,128,256]{2,1,0:T(8,128)(2,1)S(1)}, bf16[4,128,256]{2,1,0:T(8,128)(2,1)S(1)}, u32[]{:S(2)}, u32[]{:S(2)}) collective-permute-start(bf16[4,128,256]{2,1,0:T(8,128)(2,1)S(1)} %get-tuple-element.249), channel_id=1, source_target_pairs={{0,16},{4,20},{8,24},{12,28},{16,0},{20,4},{24,8},{28,12},{1,17},{... | collective-permute-start | bytes 786440 | tf_op jit(solution)/shard_map/ppermute | solution.py:481
  87.4 21.5 %collective-permute-start.43 = (bf16[128,1024]{1,0:T(8,128)(2,1)S(1)}, bf16[128,1024]{1,0:T(8,128)(2,1)S(1)}, u32[]{:S(2)}, u32[]{:S(2)}) collective-permute-start(bf16[128,1024]{1,0:T(8,128)(2,1)S(1)} %ffn_out_far.1), channel_id=1, source_target_pairs={{0,2},{1,3},{2,0},{3,1},{4,6},{5,7},{6,4},{7,5},{8,10},{9,11},{10,... | collective-permute-start | bytes 786440 | tf_op jit(solution)/shard_map/ppermute | solution.py:478
  92.7 14.0 %collective-permute-start.41 = (bf16[96,1024]{1,0:T(8,128)(2,1)S(1)}, bf16[96,1024]{1,0:T(8,128)(2,1)S(1)}, u32[]{:S(2)}, u32[]{:S(2)}) collective-permute-start(bf16[96,1024]{1,0:T(8,128)(2,1)S(1)} %back_pick.3), channel_id=1, source_target_pairs={{0,8},{4,12},{8,0},{12,4},{16,24},{20,28},{24,16},{28,20},{1,9},{5... | collective-permute-start | bytes 589832 | tf_op jit(solution)/shard_map/ppermute | solution.py:481
  95.1 9.5 %collective-permute-start.37 = (bf16[2,128,256]{2,1,0:T(8,128)(2,1)S(1)}, bf16[2,128,256]{2,1,0:T(8,128)(2,1)S(1)}, u32[]{:S(2)}, u32[]{:S(2)}) collective-permute-start(bf16[2,128,256]{2,1,0:T(8,128)(2,1)S(1)} %get-tuple-element.242), channel_id=1, source_target_pairs={{0,4},{4,0},{8,12},{12,8},{16,20},{20,16},{24,28},{28,24},{1,5},{5... | collective-permute-start | bytes 393224 | tf_op jit(solution)/shard_map/ppermute | solution.py:481
  97.8 8.9 %collective-permute-start.40 = (bf16[2,128,256]{2,1,0:T(8,128)(2,1)S(1)}, bf16[2,128,256]{2,1,0:T(8,128)(2,1)S(1)}, u32[]{:S(2)}, u32[]{:S(2)}) collective-permute-start(bf16[2,128,256]{2,1,0:T(8,128)(2,1)S(1)} %get-tuple-element.251), channel_id=1, source_target_pairs={{0,4},{4,0},{8,12},{12,8},{16,20},{20,16},{24,28},{28,24},{1,5},{5... | collective-permute-start | bytes 393224 | tf_op jit(solution)/shard_map/ppermute | solution.py:481
  104.6 6.5 %collective-permute-start.38 = (bf16[1,128,256]{2,1,0:T(8,128)(2,1)S(1)}, bf16[1,128,256]{2,1,0:T(8,128)(2,1)S(1)}, u32[]{:S(2)}, u32[]{:S(2)}) collective-permute-start(bf16[1,128,256]{2,1,0:T(8,128)(2,1)S(1)} %get-tuple-element.243), channel_id=1, source_target_pairs={{0,8},{4,12},{8,0},{12,4},{16,24},{20,28},{24,16},{28,20},{1,9},{5... | collective-permute-start | bytes 196616 | tf_op jit(solution)/shard_map/ppermute | solution.py:481
  106.7 6.6 %collective-permute-start.42 = (bf16[1,128,256]{2,1,0:T(8,128)(2,1)S(1)}, bf16[1,128,256]{2,1,0:T(8,128)(2,1)S(1)}, u32[]{:S(2)}, u32[]{:S(2)}) collective-permute-start(bf16[1,128,256]{2,1,0:T(8,128)(2,1)S(1)} %get-tuple-element.254), channel_id=1, source_target_pairs={{0,8},{4,12},{8,0},{12,4},{16,24},{20,28},{24,16},{28,20},{1,9},{5... | collective-permute-start | bytes 196616 | tf_op jit(solution)/shard_map/ppermute | solution.py:481

commit v13 on v12

--- a/solution.py
+++ b/solution.py
@@ -420,16 +420,15 @@
             target[j] = rows.astype(target.dtype)
 
 
-def enc_grad1_second(bits, bit, *refs):
-    cots, (act1, part1, keep, send, total) = refs[:-5], refs[-5:]
-    total[...] = rows_term([act1], cot_columns(cots, part1.shape[1])) + part1[...]
-    halve(bits, bit, total, keep, send)
-
-
-def enc_grad0_second(bits, bit, *refs):
-    cots, (act0_a, act0_b, pre, enc, part0, keep, send, total) = refs[:-8], refs[-8:]
-    total[...] = rows_term([act0_a, act0_b], first_cot(cots, pre, enc)) + part0[...]
-    halve(bits, bit, total, keep, send)
+def enc_grads_second(bits, bit, *refs):
+    rows, refs = refs[:-11], refs[-11:]
+    act1, pre, enc, part1, part0, keep1, send1, keep0, send0 = refs[:9]
+    total1, total0 = refs[9:]
+    cots, act0 = rows[:-2], rows[-2:]
+    total1[...] = rows_term([act1], cot_columns(cots, part1.shape[1])) + part1[...]
+    halve(bits, bit, total1, keep1, send1)
+    total0[...] = rows_term(act0, first_cot(cots, pre, enc)) + part0[...]
+    halve(bits, bit, total0, keep0, send0)
 
 
 def halve_again(bits, bit, kept, got, keep, send):
@@ -647,7 +646,7 @@
     half_rows = like((groups * capacity // 2, width), BF16)
     group_bits = [1 << b for b in range(groups.bit_length() - 1)]
     near_bit, pack_far, event_far = group_bits[0], group_bits[1 : packs.bit_length() - 1], group_bits[packs.bit_length() - 1 :]
-    back_bits = event_far[::-1] + [near_bit] + pack_far[::-1]
+    back_bits = pack_far[::-1] + [near_bit] + event_far[::-1]
     kept, back = run(
         functools.partial(back_send, order, back_bits[0]), [half_rows] * 2, [hot, d_packed], name="back_send"
     )
@@ -701,28 +700,13 @@
                 got, arrays[-1] = tie(got, arrays[-1])
         return kept, got
 
-    def start1(setting):
-        return run(
-            functools.partial(enc_grad1_second, *setting),
-            halves(bits),
-            [cot_far, *cot_both, act_b, part1],
-            total,
-            name="enc_grad1_second",
-        )
-
-    def start0(setting):
-        return run(
-            functools.partial(enc_grad0_second, *setting),
-            halves(bits),
-            [cot_far, *cot_both, mine_far, mine_both, pre_b, enc_weight, part0],
-            total,
-            name="enc_grad0_second",
-        )
-
-    kept1, send1 = start1((tuple(bits), event_bits[0]))
-    send1, part0 = tie(send1, part0)
-    part0, back_got = tie(part0, back_got)
-    kept0, send0 = start0((tuple(bits), event_bits[0]))
+    kept1, send1, kept0, send0 = run(
+        functools.partial(enc_grads_second, tuple(bits), event_bits[0]),
+        halves(bits) * 2,
+        [cot_far, *cot_both, mine_far, mine_both, act_b, pre_b, enc_weight, part1, part0],
+        total * 2,
+        name="enc_grads_second",
+    )
     arrays = [kept, back_got]
     held = {}
     for n, value in enumerate((0, back_bits[0])):
@@ -742,9 +726,9 @@
 
     for bit in back_bits[1:-1]:
         send_back(bit)
-    kept1, got1 = reduce_over(event_bits + pack_bits, kept1, send1, "halve1_", event_bits[0])
+    kept1, got1 = reduce_over(event_bits + pack_bits, kept1, send1, "halve1_", None)
+    kept0, got0 = reduce_over(event_bits + pack_bits, kept0, send0, "halve0_", event_bits[0])
     send_back(back_bits[-1])
-    kept0, got0 = reduce_over(event_bits + pack_bits, kept0, send0, "halve0_", pack_bits[0])
     got1, place = tie(got1, place)
     back_places = [held[k] for k in range(groups)]
     got_out = far(out_far)

time: 114 us -> 110 us (0.965)
  waiting for transfers between devices: 46.5 us -> 40 us
  starting transfers between devices: 38.1 us -> 41 us
    ppermute x16, waiting for transfers between devices: 21.2 us -> 15.3 us  [crossed(): return lax.ppermute(value, group_axes, [(i, i ^ k) for i in range(groups)])]
    ppermute x16, starting transfers between devices: 23 us -> 25.8 us  [crossed(): return lax.ppermute(value, group_axes, [(i, i ^ k) for i in range(groups)])]
    pallas_call x36 -> x35, Pallas kernels: 26.8 us -> 26.6 us  [run(): pl.pallas_call(body, out_shape=list(outs), in_specs=[pl.BlockSpec(memory_...]
  transfers between devices with their start and end apart: 44 -> 44, of which waited for: 30 -> 27; matrix products, arithmetic and copies ran while one was open for 1% -> 1% of each run, Pallas kernels for 22% -> 23%
where the time goes in v13:
time: 110 us
  starting transfers between devices  41 us (37%)
  waiting for transfers between devices  40 us (36%)
  Pallas kernels  26.6 us (24%)
    pallas_call x35, Pallas kernels, run(): pl.pallas_call(body, out_shape=list(outs), in_specs=[pl.BlockSpec(memory_...  26.6 us
    ppermute x16, starting transfers between devices, crossed(): return lax.ppermute(value, group_axes, [(i, i ^ k) for i in range(groups)])  25.8 us
    ppermute x9, waiting for transfers between devices, far(): return lax.ppermute(value, 'tensor', [(i, i ^ 2) for i in range(tensors)])  19 us
    ppermute x16, waiting for transfers between devices, crossed(): return lax.ppermute(value, group_axes, [(i, i ^ k) for i in range(groups)])  15.3 us
    ppermute x9, starting transfers between devices, far(): return lax.ppermute(value, 'tensor', [(i, i ^ 2) for i in range(tensors)])  10 us
    ppermute x19, waiting for transfers between devices, near(): return lax.ppermute(value, 'tensor', [(i, i ^ 1) for i in range(tensors)])  5.63 us
    ppermute x19, starting transfers between devices, near(): return lax.ppermute(value, 'tensor', [(i, i ^ 1) for i in range(tensors)])  5.12 us
  transfers between devices with their start and end apart: 44, of which 27 were waited for; matrix products, arithmetic and copies ran while one was open for 1% of the time, Pallas kernels for 23%

profile of v13, /device:TPU:0, one launch (start us, length us, event | category | flops | bytes accessed | tf_op | source)
XLA Modules:
  0.0 110.1 jit_solution(11844610284852528175)
XLA Ops:
  0.6 0.5 collective-permute-start
  1.2 0.7 add_bitcast_fusion.code
  1.9 0.9 copy-done.7
  3.2 4.1 %collective-permute-start.2 = (bf16[24,1152]{1,0:T(8,128)(2,1)S(1)}, bf16[24,1152]{1,0:T(8,128)(2,1)S(1)}, u32[]{:S(2)}, u32[]{:S(2)}) collective-permute-start(bf16[24,1152]{1,0:T(8,128)(2,1)S(1)} %get-tuple-element.130), channel_id=1, source_target_pairs={{0,8},{4,12},{8,0},{12,4},{16,24},{20,28},{24,16},{28,20},{1,9},{5... | collective-permute-start | bytes 165896 | tf_op jit(solution)/shard_map/ppermute | solution.py:480
  7.3 1.3 %collective-permute-start.3 = (bf16[24,1152]{1,0:T(8,128)(2,1)S(1)}, bf16[24,1152]{1,0:T(8,128)(2,1)S(1)}, u32[]{:S(2)}, u32[]{:S(2)}) collective-permute-start(bf16[24,1152]{1,0:T(8,128)(2,1)S(1)} %get-tuple-element.131), channel_id=1, source_target_pairs={{0,24},{4,28},{8,16},{12,20},{16,8},{20,12},{24,0},{28,4},{1,25},{... | collective-permute-start | bytes 165896 | tf_op jit(solution)/shard_map/ppermute | solution.py:480
  8.6 3.6 %collective-permute-start.4 = (bf16[24,1152]{1,0:T(8,128)(2,1)S(1)}, bf16[24,1152]{1,0:T(8,128)(2,1)S(1)}, u32[]{:S(2)}, u32[]{:S(2)}) collective-permute-start(bf16[24,1152]{1,0:T(8,128)(2,1)S(1)} %get-tuple-element.138), channel_id=1, source_target_pairs={{0,12},{4,8},{8,4},{12,0},{16,28},{20,24},{24,20},{28,16},{1,13},{... | collective-permute-start | bytes 165896 | tf_op jit(solution)/shard_map/ppermute | solution.py:480
  12.2 0.6 collective-permute-start.5
  12.8 1.1 collective-permute-start.6
  13.9 2.2 %collective-permute-done.3.refs_2_ = bf16[24,1152]{1,0:T(8,128)(2,1)S(1)} collective-permute-done((bf16[24,1152]{1,0:T(8,128)(2,1)S(1)}, bf16[24,1152]{1,0:T(8,128)(2,1)S(1)}, u32[]{:S(2)}, u32[]{:S(2)}) %collective-permute-start.3) | collective-permute-done | bytes 55328 | tf_op jit(solution)/shard_map/ppermute | solution.py:480
  16.4 0.8 turn.1
  17.2 2.0 %collective-permute-done.5.refs_4_ = bf16[24,1152]{1,0:T(8,128)(2,1)S(1)} collective-permute-done((bf16[24,1152]{1,0:T(8,128)(2,1)S(1)}, bf16[24,1152]{1,0:T(8,128)(2,1)S(1)}, u32[]{:S(2)}, u32[]{:S(2)}) %collective-permute-start.5) | collective-permute-done | bytes 55328 | tf_op jit(solution)/shard_map/ppermute | solution.py:480
  19.2 1.9 %collective-permute-done.8.refs_7_ = bf16[24,1152]{1,0:T(8,128)(2,1)S(1)} collective-permute-done((bf16[24,1152]{1,0:T(8,128)(2,1)S(1)}, bf16[24,1152]{1,0:T(8,128)(2,1)S(1)}, u32[]{:S(2)}, u32[]{:S(2)}) %collective-permute-start.8) | collective-permute-done | bytes 55328 | tf_op jit(solution)/shard_map/ppermute | solution.py:480
  21.4 1.6 %collective-permute-start.9 = (bf16[128,1024]{1,0:T(8,128)(2,1)S(1)}, bf16[128,1024]{1,0:T(8,128)(2,1)S(1)}, u32[]{:S(2)}, u32[]{:S(2)}) collective-permute-start(bf16[128,1024]{1,0:T(8,128)(2,1)S(1)} %get-tuple-element.151.refs_0_.refs_3_), channel_id=1, source_target_pairs={{0,2},{1,3},{2,0},{3,1},{4,6},{5,7},{6,4},{7,5},{8,10},{9,11},{10,... | collective-permute-start | bytes 786440 | tf_op jit(solution)/shard_map/ppermute | solution.py:477
  23.0 0.5 collective-permute-start.11
  23.5 0.8 collective-permute-done.10.refs_1_.refs_4_
  24.5 2.2 %encode_first.1 = (f32[256,256]{1,0:T(8,128)S(1)}, bf16[256,1024]{1,0:T(8,128)(2,1)S(1)}, bf16[128,1024]{1,0:T(8,128)(2,1)S(1)}, bf16[4,2,128,256]{3,2,1,0:T(8,128)(2,1)S(1)}) custom-call(bf16[128,1024]{1,0:T(8,128)(2,1)S(1)} %get-tuple-element.151.refs_0_.refs_3_, bf16[64,1024]{1,0:T(8,128)(2,1)S(1)} %collective-permute-done.10.refs_1_.refs_4_, ...), custom_call_target="tpu_custom_call" | custom-call | tf_op jit(solution)/shard_map/encode_first/pallas_call | solution.py:64
  26.8 1.1 collective-permute-done.9.refs_0_.refs_5_
  27.8 0.5 collective-permute-start.12
  28.3 1.5 %collective-permute-start.15 = (bf16[128,1024]{1,0:T(8,128)(2,1)S(1)}, bf16[128,1024]{1,0:T(8,128)(2,1)S(1)}, u32[]{:S(2)}, u32[]{:S(2)}) collective-permute-start(bf16[128,1024]{1,0:T(8,128)(2,1)S(1)} %bitcast.5), channel_id=1, source_target_pairs={{0,2},{1,3},{2,0},{3,1},{4,6},{5,7},{6,4},{7,5},{8,10},{9,11},{10,... | collective-permute-start | bytes 786440 | tf_op jit(solution)/shard_map/ppermute | solution.py:477
  29.9 1.4 %encode_third.1 = (f32[128,256]{1,0:T(8,128)S(1)}, bf16[128,1024]{1,0:T(8,128)(2,1)S(1)}, bf16[128,1024]{1,0:T(8,128)(2,1)S(1)}, bf16[4,1,128,256]{3,2,1,0:T(8,128)(2,1)S(1)}) custom-call(bf16[128,1024]{1,0:T(8,128)(2,1)S(1)} %collective-permute-done.9.refs_0_.refs_5_, bf16[2,1024,1024]{2,1,0:T(8,128)(2,1)S(1)} %copy-done, bf16[4,1024,256]{2,1,0:T(8,128)(2,1)S(1)} %copy-done.1), custom_call_target="tpu_custom_call" | custom-call | tf_op jit(solution)/shard_map/encode_third/pallas_call | solution.py:64
  31.3 2.5 %attend_first.1 = (f32[256,256]{1,0:T(8,128)S(1)}, bf16[256,1024]{1,0:T(8,128)(2,1)S(1)}, bf16[4,4,128,256]{3,2,1,0:T(8,128)(2,1)S(1)}, f32[4,128,256]{2,1,0:T(8...) custom-call(s32[4,1,128]{2,1,0:T(1,128)S(1)} %bitcast.8, ...), custom_call_target="tpu_custom_call" | custom-call | tf_op jit(solution)/shard_map/attend_first/pallas_call | solution.py:64
  33.9 1.3 %collective-permute-done.13.take = bf16[256,256]{1,0:T(8,128)(2,1)S(1)} collective-permute-done((bf16[256,256]{1,0:T(8,128)(2,1)S(1)}, bf16[256,256]{1,0:T(8,128)(2,1)S(1)}, u32[]{:S(2)}, u32[]{:S(2)}) %collective-permute-start.13) | collective-permute-done | bytes 131104 | tf_op jit(solution)/shard_map/ppermute | solution.py:474
  35.6 0.6 collective-permute-start.17
  36.5 1.5 %collective-permute-start.16 = (bf16[128,1024]{1,0:T(8,128)(2,1)S(1)}, bf16[128,1024]{1,0:T(8,128)(2,1)S(1)}, u32[]{:S(2)}, u32[]{:S(2)}) collective-permute-start(bf16[128,1024]{1,0:T(8,128)(2,1)S(1)} %attn_out_own.1.part), channel_id=1, source_target_pairs={{0,2},{1,3},{2,0},{3,1},{4,6},{5,7},{6,4},{7,5},{8,10},{9,11},{10,... | collective-permute-start | bytes 786440 | tf_op jit(solution)/shard_map/ppermute | solution.py:477
  38.1 6.7 %collective-permute-done.17.got = bf16[128,1024]{1,0:T(8,128)(2,1)S(1)} collective-permute-done((bf16[128,1024]{1,0:T(8,128)(2,1)S(1)}, bf16[128,1024]{1,0:T(8,128)(2,1)S(1)}, u32[]{:S(2)}, u32[]{:S(2)}) %collective-permute-start.17) | collective-permute-done | bytes 262176 | tf_op jit(solution)/shard_map/ppermute | solution.py:477
  45.0 2.9 %ffn_own.1 = (bf16[128,1024]{1,0:T(8,128)(2,1)S(1)}, bf16[128,1024]{1,0:T(8,128)(2,1)S(1)}) custom-call(bf16[128,1024]{1,0:T(8,128)(2,1)S(1)} %get-tuple-element.167.rows_ref, bf16[128,1024]{1,0:T(8,128)(2,1)S(1)} %bitcast.6, bf16[2,1024,512]{2,1,0:T(8,128)(2,1)S(1)} %copy-done.3, bf16[2,1024,512]{2,1,0:T(8,128)(2,1)S(1)} %collective-permute-done.in_b, ...), custom_call_target="tpu_custom_call" | custom-call | tf_op jit(solution)/shard_map/ffn_own/pallas_call | solution.py:64
  47.9 1.7 %collective-permute-done.16.got = bf16[128,1024]{1,0:T(8,128)(2,1)S(1)} collective-permute-done((bf16[128,1024]{1,0:T(8,128)(2,1)S(1)}, bf16[128,1024]{1,0:T(8,128)(2,1)S(1)}, u32[]{:S(2)}, u32[]{:S(2)}) %collective-permute-start.16) | collective-permute-done | bytes 262176 | tf_op jit(solution)/shard_map/ppermute | solution.py:477
  49.6 0.5 collective-permute-start.19
  50.3 2.9 %ffn_far.1 = (bf16[128,1024]{1,0:T(8,128)(2,1)S(1)}, bf16[128,1024]{1,0:T(8,128)(2,1)S(1)}) custom-call(bf16[128,1024]{1,0:T(8,128)(2,1)S(1)} %get-tuple-element.174.rows_ref, bf16[128,1024]{1,0:T(8,128)(2,1)S(1)} %collective-permute-done.15.d_out_ref.d_out, bf16[2,1024,512]{2,1,0:T(8,128)(2,1)S(1)} %copy-done.3, ...), custom_call_target="tpu_custom_call" | custom-call | tf_op jit(solution)/shard_map/ffn_far/pallas_call | solution.py:64
  53.2 1.6 %collective-permute-start.18 = (bf16[128,1024]{1,0:T(8,128)(2,1)S(1)}, bf16[128,1024]{1,0:T(8,128)(2,1)S(1)}, u32[]{:S(2)}, u32[]{:S(2)}) collective-permute-start(bf16[128,1024]{1,0:T(8,128)(2,1)S(1)} %get-tuple-element.176.back), channel_id=1, source_target_pairs={{0,2},{1,3},{2,0},{3,1},{4,6},{5,7},{6,4},{7,5},{8,10},{9,11},{10,... | collective-permute-start | bytes 786440 | tf_op jit(solution)/shard_map/ppermute | solution.py:477
  54.8 4.0 %collective-permute-done.19.got = bf16[128,1024]{1,0:T(8,128)(2,1)S(1)} collective-permute-done((bf16[128,1024]{1,0:T(8,128)(2,1)S(1)}, bf16[128,1024]{1,0:T(8,128)(2,1)S(1)}, u32[]{:S(2)}, u32[]{:S(2)}) %collective-permute-start.19) | collective-permute-done | bytes 262176 | tf_op jit(solution)/shard_map/ppermute | solution.py:477
  58.8 0.5 resid_back_far.1
  59.4 0.5 collective-permute-start.21
  59.9 0.8 collective-permute-done.20.fourth_a
  60.9 1.6 %attn_back_first.1 = (bf16[4,128,256]{2,1,0:T(8,128)(2,1)S(1)}, f32[4,128,256]{2,1,0:T(8,128)S(1)}, f32[4,128,256]{2,1,0:T(8,128)S(1)}, bf16[4,128,256]{2,1,0:T(8,128)(2,1)S(1)}) custom-call(s32[4,1,128]{2,1,0:T(1,128)S(1)} %bitcast.9, bf16[128,1024]{1,0:T(8,128)(2,1)S(1)} %get-tuple-element.178.third.d_resid, ...), custom_call_target="tpu_custom_call" | custom-call | tf_op jit(solution)/shard_map/attn_back_first/pallas_call | solution.py:64
  63.2 1.2 %attn_back_own.1 = (bf16[128,1024]{1,0:T(8,128)(2,1)S(1)}, bf16[4,128,256]{2,1,0:T(8,128)(2,1)S(1)}, f32[4,128,256]{2,1,0:T(8,128)S(1)}, f32[4,128,256]{2,1,0:T(8,128)S(1)}, bf16[4,128,256]{2,1,0:T(8,128)(2,1)S(1)}) custom-call(s32[4,1,128]{2,1,0:T(1,128)S(1)} %bitcast.10, ...), custom_call_target="tpu_custom_call", output_to_operand_aliasing={{1}: (5, {}), {2}: (6, {}), {3}: (7, {}), {4}: (8, {})} | custom-call | tf_op jit(solution)/shard_map/attn_back_own/pallas_call | solution.py:64
  64.4 0.5 collective-permute-start.23
  64.8 0.8 attn_back_second.1
  66.0 0.4 back_sum_far.1.part
  66.5 0.6 collective-permute-start.27
  67.0 0.4 back_give.1
  68.1 0.8 collective-permute-done.24.refs_0_
  69.1 0.4 back_sum_own.1.part
  69.5 1.6 %collective-permute-start.26 = (bf16[128,1024]{1,0:T(8,128)(2,1)S(1)}, bf16[128,1024]{1,0:T(8,128)(2,1)S(1)}, u32[]{:S(2)}, u32[]{:S(2)}) collective-permute-start(bf16[128,1024]{1,0:T(8,128)(2,1)S(1)} %back_sum_own.1.part), channel_id=1, source_target_pairs={{0,2},{1,3},{2,0},{3,1},{4,6},{5,7},{6,4},{7,5},{8,10},{9,11},{10,... | collective-permute-start | bytes 786440 | tf_op jit(solution)/shard_map/ppermute | solution.py:477
  71.1 4.5 %collective-permute-done.27.got = bf16[128,1024]{1,0:T(8,128)(2,1)S(1)} collective-permute-done((bf16[128,1024]{1,0:T(8,128)(2,1)S(1)}, bf16[128,1024]{1,0:T(8,128)(2,1)S(1)}, u32[]{:S(2)}, u32[]{:S(2)}) %collective-permute-start.27) | collective-permute-done | bytes 262176 | tf_op jit(solution)/shard_map/ppermute | solution.py:477
  76.0 0.5 collective-permute-start.29
  76.8 2.3 %collective-permute-start.38 = (bf16[96,1024]{1,0:T(8,128)(2,1)S(1)}, bf16[96,1024]{1,0:T(8,128)(2,1)S(1)}, u32[]{:S(2)}, u32[]{:S(2)}) collective-permute-start(bf16[96,1024]{1,0:T(8,128)(2,1)S(1)} %get-tuple-element.238), channel_id=1, source_target_pairs={{0,8},{4,12},{8,0},{12,4},{16,24},{20,28},{24,16},{28,20},{1,9},{5... | collective-permute-start | bytes 589832 | tf_op jit(solution)/shard_map/ppermute | solution.py:480
  79.1 1.0 enc_grads_first.1
  80.1 0.7 collective-permute-done.26.got
  81.1 0.5 collective-permute-start.31
  83.0 1.3 %enc_grads_second.1 = (f32[4,128,256]{2,1,0:T(8,128)S(1)}, bf16[4,128,256]{2,1,0:T(8,128)(2,1)S(1)}, f32[4,128,256]{2,1,0:T(8,128)S(1)}, bf16[4,128,256]{2,1,0:T(8,128)(2,1)S(1)}) custom-call(bf16[128,1024]{1,0:T(8,128)(2,1)S(1)} %get-tuple-element.218.refs_0_, bf16[32,1024]{1,0:T(8,128)(2,1)S(1)} %collective-permute-done.30.refs_1_, ...), custom_call_target="tpu_custom_call" | custom-call | tf_op jit(solution)/shard_map/enc_grads_second/pallas_call | solution.py:64
  84.3 1.7 %collective-permute-start.34 = (bf16[4,128,256]{2,1,0:T(8,128)(2,1)S(1)}, bf16[4,128,256]{2,1,0:T(8,128)(2,1)S(1)}, u32[]{:S(2)}, u32[]{:S(2)}) collective-permute-start(bf16[4,128,256]{2,1,0:T(8,128)(2,1)S(1)} %get-tuple-element.228), channel_id=1, source_target_pairs={{0,16},{4,20},{8,24},{12,28},{16,0},{20,4},{24,8},{28,12},{1,17},{... | collective-permute-start | bytes 786440 | tf_op jit(solution)/shard_map/ppermute | solution.py:480
  86.4 2.4 %collective-permute-done.38.refs_1_ = bf16[96,1024]{1,0:T(8,128)(2,1)S(1)} collective-permute-done((bf16[96,1024]{1,0:T(8,128)(2,1)S(1)}, bf16[96,1024]{1,0:T(8,128)(2,1)S(1)}, u32[]{:S(2)}, u32[]{:S(2)}) %collective-permute-start.38) | collective-permute-done | bytes 196640 | tf_op jit(solution)/shard_map/ppermute | solution.py:480
  89.2 0.4 ffn_out_far.1
  89.7 0.6 collective-permute-start.42
  90.3 3.2 %collective-permute-done.34.got = bf16[4,128,256]{2,1,0:T(8,128)(2,1)S(1)} collective-permute-done((bf16[4,128,256]{2,1,0:T(8,128)(2,1)S(1)}, bf16[4,128,256]{2,1,0:T(8,128)(2,1)S(1)}, u32[]{:S(2)}, u32[]{:S(2)}) %collective-permute-start.34) | collective-permute-done | bytes 262176 | tf_op jit(solution)/shard_map/ppermute | solution.py:480
  93.5 1.7 %collective-permute-start.35 = (bf16[2,128,256]{2,1,0:T(8,128)(2,1)S(1)}, bf16[2,128,256]{2,1,0:T(8,128)(2,1)S(1)}, u32[]{:S(2)}, u32[]{:S(2)}) collective-permute-start(bf16[2,128,256]{2,1,0:T(8,128)(2,1)S(1)} %get-tuple-element.230), channel_id=1, source_target_pairs={{0,4},{4,0},{8,12},{12,8},{16,20},{20,16},{24,28},{28,24},{1,5},{5... | collective-permute-start | bytes 393224 | tf_op jit(solution)/shard_map/ppermute | solution.py:480
  95.2 3.3 %collective-permute-done.37.got = bf16[4,128,256]{2,1,0:T(8,128)(2,1)S(1)} collective-permute-done((bf16[4,128,256]{2,1,0:T(8,128)(2,1)S(1)}, bf16[4,128,256]{2,1,0:T(8,128)(2,1)S(1)}, u32[]{:S(2)}, u32[]{:S(2)}) %collective-permute-start.37) | collective-permute-done | bytes 262176 | tf_op jit(solution)/shard_map/ppermute | solution.py:480
  98.6 1.7 %collective-permute-start.40 = (bf16[2,128,256]{2,1,0:T(8,128)(2,1)S(1)}, bf16[2,128,256]{2,1,0:T(8,128)(2,1)S(1)}, u32[]{:S(2)}, u32[]{:S(2)}) collective-permute-start(bf16[2,128,256]{2,1,0:T(8,128)(2,1)S(1)} %get-tuple-element.241), channel_id=1, source_target_pairs={{0,4},{4,0},{8,12},{12,8},{16,20},{20,16},{24,28},{28,24},{1,5},{5... | collective-permute-start | bytes 393224 | tf_op jit(solution)/shard_map/ppermute | solution.py:480
  100.6 3.0 %collective-permute-start.36 = (bf16[1,128,256]{2,1,0:T(8,128)(2,1)S(1)}, bf16[1,128,256]{2,1,0:T(8,128)(2,1)S(1)}, u32[]{:S(2)}, u32[]{:S(2)}) collective-permute-start(bf16[1,128,256]{2,1,0:T(8,128)(2,1)S(1)} %get-tuple-element.231), channel_id=1, source_target_pairs={{0,8},{4,12},{8,0},{12,4},{16,24},{20,28},{24,16},{28,20},{1,9},{5... | collective-permute-start | bytes 196616 | tf_op jit(solution)/shard_map/ppermute | solution.py:480
  103.7 3.5 %collective-permute-start.41 = (bf16[1,128,256]{2,1,0:T(8,128)(2,1)S(1)}, bf16[1,128,256]{2,1,0:T(8,128)(2,1)S(1)}, u32[]{:S(2)}, u32[]{:S(2)}) collective-permute-start(bf16[1,128,256]{2,1,0:T(8,128)(2,1)S(1)} %get-tuple-element.242), channel_id=1, source_target_pairs={{0,8},{4,12},{8,0},{12,4},{16,24},{20,28},{24,16},{28,20},{1,9},{5... | collective-permute-start | bytes 196616 | tf_op jit(solution)/shard_map/ppermute | solution.py:480
  107.1 1.2 %ffn_out_own.1 = bf16[128,1024]{1,0:T(8,128)(2,1)} custom-call(bf16[128,1024]{1,0:T(8,128)(2,1)S(1)} %get-tuple-element.243.hidden, bf16[512,1024]{1,0:T(8,128)(2,1)S(1)} %copy-done.2, bf16[512,1024]{1,0:T(8,128)(2,1)S(1)} %collective-permute-done.1.out_b.w_b, bf16[128,1024]{1,0:T(8,128)(2,1)S(1)} %get-tuple-element.186.resid, ...), custom_call_target="tpu_custom_call" | custom-call | tf_op jit(solution)/shard_map/ffn_out_own/pallas_call | solution.py:64
  108.3 1.0 back_recv.1
  109.4 0.7 finish.1
  (76 shorter events, 8.4 us)
Async XLA Ops:
  0.6 7.9 %collective-permute-start = (bf16[2,1024,512]{2,1,0:T(8,128)(2,1)}, bf16[2,1024,512]{2,1,0:T(8,128)(2,1)S(1)}, u32[]{:S(2)}, u32[]{:S(2)}) collective-permute-start(bf16[2,1024,512]{2,1,0:T(8,128)(2,1)} %in_a.3), channel_id=1, source_target_pairs={{0,1},{1,0},{2,3},{3,2},{4,5},{5,4},{6,7},{7,6},{8,9},{9,8},{10,11... | collective-permute-start | bytes 6291464 | tf_op jit(solution)/shard_map/ppermute | solution.py:474
  1.1 7.4 %collective-permute-start.1 = (bf16[512,1024]{1,0:T(8,128)(2,1)}, bf16[512,1024]{1,0:T(8,128)(2,1)S(1)}, u32[]{:S(2)}, u32[]{:S(2)}) collective-permute-start(bf16[512,1024]{1,0:T(8,128)(2,1)} %w_a.3), channel_id=1, source_target_pairs={{0,1},{1,0},{2,3},{3,2},{4,5},{5,4},{6,7},{7,6},{8,9},{9,8},{10,11... | collective-permute-start | bytes 3145736 | tf_op jit(solution)/shard_map/ppermute | solution.py:474
  1.9 0.9 copy-start.7
  2.9 13.5 %copy-start.1 = (bf16[4,1024,256]{2,1,0:T(8,128)(2,1)S(1)}, bf16[4,1024,256]{2,1,0:T(8,128)(2,1)}, u32[]{:S(2)}) copy-start(bf16[4,1024,256]{2,1,0:T(8,128)(2,1)} %w_in.1) | copy-start | bytes 6291460
  2.9 13.5 %copy-start.4 = (bf16[256,1024]{1,0:T(8,128)(2,1)S(1)}, bf16[256,1024]{1,0:T(8,128)(2,1)}, u32[]{:S(2)}) copy-start(bf16[256,1024]{1,0:T(8,128)(2,1)} %w_own.3) | copy-start | bytes 1572868
  2.9 21.6 %copy-start = (bf16[2,1024,1024]{2,1,0:T(8,128)(2,1)S(1)}, bf16[2,1024,1024]{2,1,0:T(8,128)(2,1)}, u32[]{:S(2)}) copy-start(bf16[2,1024,1024]{2,1,0:T(8,128)(2,1)} %refs_9_.1) | copy-start | bytes 12582916
  3.2 10.6 %collective-permute-start.2 = (bf16[24,1152]{1,0:T(8,128)(2,1)S(1)}, bf16[24,1152]{1,0:T(8,128)(2,1)S(1)}, u32[]{:S(2)}, u32[]{:S(2)}) collective-permute-start(bf16[24,1152]{1,0:T(8,128)(2,1)S(1)} %get-tuple-element.130), channel_id=1, source_target_pairs={{0,8},{4,12},{8,0},{12,4},{16,24},{20,28},{24,16},{28,20},{1,9},{5... | collective-permute-start | bytes 165896 | tf_op jit(solution)/shard_map/ppermute | solution.py:480
  7.3 8.8 %collective-permute-start.3 = (bf16[24,1152]{1,0:T(8,128)(2,1)S(1)}, bf16[24,1152]{1,0:T(8,128)(2,1)S(1)}, u32[]{:S(2)}, u32[]{:S(2)}) collective-permute-start(bf16[24,1152]{1,0:T(8,128)(2,1)S(1)} %get-tuple-element.131), channel_id=1, source_target_pairs={{0,24},{4,28},{8,16},{12,20},{16,8},{20,12},{24,0},{28,4},{1,25},{... | collective-permute-start | bytes 165896 | tf_op jit(solution)/shard_map/ppermute | solution.py:480
  8.6 8.6 %collective-permute-start.4 = (bf16[24,1152]{1,0:T(8,128)(2,1)S(1)}, bf16[24,1152]{1,0:T(8,128)(2,1)S(1)}, u32[]{:S(2)}, u32[]{:S(2)}) collective-permute-start(bf16[24,1152]{1,0:T(8,128)(2,1)S(1)} %get-tuple-element.138), channel_id=1, source_target_pairs={{0,12},{4,8},{8,4},{12,0},{16,28},{20,24},{24,20},{28,16},{1,13},{... | collective-permute-start | bytes 165896 | tf_op jit(solution)/shard_map/ppermute | solution.py:480
  12.2 7.0 %collective-permute-start.5 = (bf16[24,1152]{1,0:T(8,128)(2,1)S(1)}, bf16[24,1152]{1,0:T(8,128)(2,1)S(1)}, u32[]{:S(2)}, u32[]{:S(2)}) collective-permute-start(bf16[24,1152]{1,0:T(8,128)(2,1)S(1)} %get-tuple-element.139), channel_id=1, source_target_pairs={{0,28},{4,24},{8,20},{12,16},{16,12},{20,8},{24,4},{28,0},{1,29},{... | collective-permute-start | bytes 165896 | tf_op jit(solution)/shard_map/ppermute | solution.py:480
  12.8 6.4 %collective-permute-start.6 = (bf16[24,1152]{1,0:T(8,128)(2,1)S(1)}, bf16[24,1152]{1,0:T(8,128)(2,1)S(1)}, u32[]{:S(2)}, u32[]{:S(2)}) collective-permute-start(bf16[24,1152]{1,0:T(8,128)(2,1)S(1)} %get-tuple-element.140), channel_id=1, source_target_pairs={{0,16},{4,20},{8,24},{12,28},{16,0},{20,4},{24,8},{28,12},{1,17},{... | collective-permute-start | bytes 165896 | tf_op jit(solution)/shard_map/ppermute | solution.py:480
  13.9 5.3 %collective-permute-start.7 = (bf16[24,1152]{1,0:T(8,128)(2,1)S(1)}, bf16[24,1152]{1,0:T(8,128)(2,1)S(1)}, u32[]{:S(2)}, u32[]{:S(2)}) collective-permute-start(bf16[24,1152]{1,0:T(8,128)(2,1)S(1)} %get-tuple-element.141), channel_id=1, source_target_pairs={{0,4},{4,0},{8,12},{12,8},{16,20},{20,16},{24,28},{28,24},{1,5},{5... | collective-permute-start | bytes 165896 | tf_op jit(solution)/shard_map/ppermute | solution.py:480
  16.1 5.1 %collective-permute-start.8 = (bf16[24,1152]{1,0:T(8,128)(2,1)S(1)}, bf16[24,1152]{1,0:T(8,128)(2,1)S(1)}, u32[]{:S(2)}, u32[]{:S(2)}) collective-permute-start(bf16[24,1152]{1,0:T(8,128)(2,1)S(1)} %get-tuple-element.142), channel_id=1, source_target_pairs={{0,20},{4,16},{8,28},{12,24},{16,4},{20,0},{24,12},{28,8},{1,21},{... | collective-permute-start | bytes 165896 | tf_op jit(solution)/shard_map/ppermute | solution.py:480
  21.4 6.4 %collective-permute-start.9 = (bf16[128,1024]{1,0:T(8,128)(2,1)S(1)}, bf16[128,1024]{1,0:T(8,128)(2,1)S(1)}, u32[]{:S(2)}, u32[]{:S(2)}) collective-permute-start(bf16[128,1024]{1,0:T(8,128)(2,1)S(1)} %get-tuple-element.151.refs_0_.refs_3_), channel_id=1, source_target_pairs={{0,2},{1,3},{2,0},{3,1},{4,6},{5,7},{6,4},{7,5},{8,10},{9,11},{10,... | collective-permute-start | bytes 786440 | tf_op jit(solution)/shard_map/ppermute | solution.py:477
  23.0 1.3 %collective-permute-start.10 = (bf16[64,1024]{1,0:T(8,128)(2,1)S(1)}, bf16[64,1024]{1,0:T(8,128)(2,1)S(1)}, u32[]{:S(2)}, u32[]{:S(2)}) collective-permute-start(bf16[64,1024]{1,0:T(8,128)(2,1)S(1)} %get-tuple-element.152), channel_id=1, source_target_pairs={{0,1},{1,0},{2,3},{3,2},{4,5},{5,4},{6,7},{7,6},{8,9},{9,8},{10,11... | collective-permute-start | bytes 393224 | tf_op jit(solution)/shard_map/ppermute | solution.py:474
  23.0 5.4 %copy-start.5 = (bf16[1,128,1024]{2,1,0:T(8,128)(2,1)S(1)}, bf16[1,128,1024]{2,1,0:T(8,128)(2,1)}, u32[]{:S(2)}) copy-start(bf16[1,128,1024]{2,1,0:T(8,128)(2,1)} %param.19) | copy-start | bytes 786436
  23.0 1.5 %collective-permute-start.11 = (bf16[64,1024]{1,0:T(8,128)(2,1)S(1)}, bf16[64,1024]{1,0:T(8,128)(2,1)S(1)}, u32[]{:S(2)}, u32[]{:S(2)}) collective-permute-start(bf16[64,1024]{1,0:T(8,128)(2,1)S(1)} %get-tuple-element.153), channel_id=1, source_target_pairs={{0,1},{1,0},{2,3},{3,2},{4,5},{5,4},{6,7},{7,6},{8,9},{9,8},{10,11... | collective-permute-start | bytes 393224 | tf_op jit(solution)/shard_map/ppermute | solution.py:474
  27.8 3.4 %copy-start.6 = (s32[1,512]{1,0:T(1,128)S(1)}, s32[1,512]{1,0:T(1,128)}, u32[]{:S(2)}) copy-start(s32[1,512]{1,0:T(1,128)} %param.13) | copy-start | bytes 6148
  27.8 7.4 %collective-permute-start.14 = (bf16[256,1024]{1,0:T(8,128)(2,1)S(1)}, bf16[256,1024]{1,0:T(8,128)(2,1)S(1)}, u32[]{:S(2)}, u32[]{:S(2)}) collective-permute-start(bf16[256,1024]{1,0:T(8,128)(2,1)S(1)} %copy-done.4), channel_id=1, source_target_pairs={{0,1},{1,0},{2,3},{3,2},{4,5},{5,4},{6,7},{7,6},{8,9},{9,8},{10,11... | collective-permute-start | bytes 1572872 | tf_op jit(solution)/shard_map/ppermute | solution.py:474
  27.8 3.4 %collective-permute-start.12 = (bf16[128,1024]{1,0:T(8,128)(2,1)S(1)}, bf16[128,1024]{1,0:T(8,128)(2,1)S(1)}, u32[]{:S(2)}, u32[]{:S(2)}) collective-permute-start(bf16[128,1024]{1,0:T(8,128)(2,1)S(1)} %collective-permute-done.9.refs_0_.refs_5_), channel_id=1, source_target_pairs={{0,1},{1,0},{2,3},{3,2},{4,5},{5,4},{6,7},{7,6},{8,9},{9,8},{10,11... | collective-permute-start | bytes 786440 | tf_op jit(solution)/shard_map/ppermute | solution.py:474
  28.3 8.2 %collective-permute-start.15 = (bf16[128,1024]{1,0:T(8,128)(2,1)S(1)}, bf16[128,1024]{1,0:T(8,128)(2,1)S(1)}, u32[]{:S(2)}, u32[]{:S(2)}) collective-permute-start(bf16[128,1024]{1,0:T(8,128)(2,1)S(1)} %bitcast.5), channel_id=1, source_target_pairs={{0,2},{1,3},{2,0},{3,1},{4,6},{5,7},{6,4},{7,5},{8,10},{9,11},{10,... | collective-permute-start | bytes 786440 | tf_op jit(solution)/shard_map/ppermute | solution.py:477
  33.8 11.2 %copy-start.2 = (bf16[512,1024]{1,0:T(8,128)(2,1)S(1)}, bf16[512,1024]{1,0:T(8,128)(2,1)}, u32[]{:S(2)}) copy-start(bf16[512,1024]{1,0:T(8,128)(2,1)} %w_a.3) | copy-start | bytes 3145732
  33.8 11.2 %copy-start.3 = (bf16[2,1024,512]{2,1,0:T(8,128)(2,1)S(1)}, bf16[2,1024,512]{2,1,0:T(8,128)(2,1)}, u32[]{:S(2)}) copy-start(bf16[2,1024,512]{2,1,0:T(8,128)(2,1)} %in_a.3) | copy-start | bytes 6291460
  33.8 1.4 %collective-permute-start.13 = (bf16[256,256]{1,0:T(8,128)(2,1)S(1)}, bf16[256,256]{1,0:T(8,128)(2,1)S(1)}, u32[]{:S(2)}, u32[]{:S(2)}) collective-permute-start(bf16[256,256]{1,0:T(8,128)(2,1)S(1)} %get-tuple-element.162), channel_id=1, source_target_pairs={{0,1},{1,0},{2,3},{3,2},{4,5},{5,4},{6,7},{7,6},{8,9},{9,8},{10,11... | collective-permute-start | bytes 393224 | tf_op jit(solution)/shard_map/ppermute | solution.py:474
  35.6 9.2 %collective-permute-start.17 = (bf16[128,1024]{1,0:T(8,128)(2,1)S(1)}, bf16[128,1024]{1,0:T(8,128)(2,1)S(1)}, u32[]{:S(2)}, u32[]{:S(2)}) collective-permute-start(bf16[128,1024]{1,0:T(8,128)(2,1)S(1)} %attn_out_far.1.part), channel_id=1, source_target_pairs={{0,2},{1,3},{2,0},{3,1},{4,6},{5,7},{6,4},{7,5},{8,10},{9,11},{10,... | collective-permute-start | bytes 786440 | tf_op jit(solution)/shard_map/ppermute | solution.py:477
  36.5 13.1 %collective-permute-start.16 = (bf16[128,1024]{1,0:T(8,128)(2,1)S(1)}, bf16[128,1024]{1,0:T(8,128)(2,1)S(1)}, u32[]{:S(2)}, u32[]{:S(2)}) collective-permute-start(bf16[128,1024]{1,0:T(8,128)(2,1)S(1)} %attn_out_own.1.part), channel_id=1, source_target_pairs={{0,2},{1,3},{2,0},{3,1},{4,6},{5,7},{6,4},{7,5},{8,10},{9,11},{10,... | collective-permute-start | bytes 786440 | tf_op jit(solution)/shard_map/ppermute | solution.py:477
  49.6 9.2 %collective-permute-start.19 = (bf16[128,1024]{1,0:T(8,128)(2,1)S(1)}, bf16[128,1024]{1,0:T(8,128)(2,1)S(1)}, u32[]{:S(2)}, u32[]{:S(2)}) collective-permute-start(bf16[128,1024]{1,0:T(8,128)(2,1)S(1)} %get-tuple-element.171.back), channel_id=1, source_target_pairs={{0,2},{1,3},{2,0},{3,1},{4,6},{5,7},{6,4},{7,5},{8,10},{9,11},{10,... | collective-permute-start | bytes 786440 | tf_op jit(solution)/shard_map/ppermute | solution.py:477
  53.2 9.6 %collective-permute-start.18 = (bf16[128,1024]{1,0:T(8,128)(2,1)S(1)}, bf16[128,1024]{1,0:T(8,128)(2,1)S(1)}, u32[]{:S(2)}, u32[]{:S(2)}) collective-permute-start(bf16[128,1024]{1,0:T(8,128)(2,1)S(1)} %get-tuple-element.176.back), channel_id=1, source_target_pairs={{0,2},{1,3},{2,0},{3,1},{4,6},{5,7},{6,4},{7,5},{8,10},{9,11},{10,... | collective-permute-start | bytes 786440 | tf_op jit(solution)/shard_map/ppermute | solution.py:477
  59.3 1.4 %collective-permute-start.20 = (bf16[64,1024]{1,0:T(8,128)(2,1)S(1)}, bf16[64,1024]{1,0:T(8,128)(2,1)S(1)}, u32[]{:S(2)}, u32[]{:S(2)}) collective-permute-start(bf16[64,1024]{1,0:T(8,128)(2,1)S(1)} %get-tuple-element.179), channel_id=1, source_target_pairs={{0,1},{1,0},{2,3},{3,2},{4,5},{5,4},{6,7},{7,6},{8,9},{9,8},{10,11... | collective-permute-start | bytes 393224 | tf_op jit(solution)/shard_map/ppermute | solution.py:474
  59.4 1.5 %collective-permute-start.21 = (bf16[64,1024]{1,0:T(8,128)(2,1)S(1)}, bf16[64,1024]{1,0:T(8,128)(2,1)S(1)}, u32[]{:S(2)}, u32[]{:S(2)}) collective-permute-start(bf16[64,1024]{1,0:T(8,128)(2,1)S(1)} %get-tuple-element.180), channel_id=1, source_target_pairs={{0,1},{1,0},{2,3},{3,2},{4,5},{5,4},{6,7},{7,6},{8,9},{9,8},{10,11... | collective-permute-start | bytes 393224 | tf_op jit(solution)/shard_map/ppermute | solution.py:474
  63.0 1.8 %collective-permute-start.22 = (bf16[128,1024]{1,0:T(8,128)(2,1)S(1)}, bf16[128,1024]{1,0:T(8,128)(2,1)S(1)}, u32[]{:S(2)}, u32[]{:S(2)}) collective-permute-start(bf16[128,1024]{1,0:T(8,128)(2,1)S(1)} %resid_back.1.first.d_resid), channel_id=1, source_target_pairs={{0,1},{1,0},{2,3},{3,2},{4,5},{5,4},{6,7},{7,6},{8,9},{9,8},{10,11... | collective-permute-start | bytes 786440 | tf_op jit(solution)/shard_map/ppermute | solution.py:474
  64.4 1.6 %collective-permute-start.23 = (bf16[128,1024]{1,0:T(8,128)(2,1)S(1)}, bf16[128,1024]{1,0:T(8,128)(2,1)S(1)}, u32[]{:S(2)}, u32[]{:S(2)}) collective-permute-start(bf16[128,1024]{1,0:T(8,128)(2,1)S(1)} %get-tuple-element.200), channel_id=1, source_target_pairs={{0,1},{1,0},{2,3},{3,2},{4,5},{5,4},{6,7},{7,6},{8,9},{9,8},{10,11... | collective-permute-start | bytes 786440 | tf_op jit(solution)/shard_map/ppermute | solution.py:474
  66.5 9.2 %collective-permute-start.27 = (bf16[128,1024]{1,0:T(8,128)(2,1)S(1)}, bf16[128,1024]{1,0:T(8,128)(2,1)S(1)}, u32[]{:S(2)}, u32[]{:S(2)}) collective-permute-start(bf16[128,1024]{1,0:T(8,128)(2,1)S(1)} %back_sum_far.1.part), channel_id=1, source_target_pairs={{0,2},{1,3},{2,0},{3,1},{4,6},{5,7},{6,4},{7,5},{8,10},{9,11},{10,... | collective-permute-start | bytes 786440 | tf_op jit(solution)/shard_map/ppermute | solution.py:477
  67.5 1.4 %collective-permute-start.24 = (bf16[64,1024]{1,0:T(8,128)(2,1)S(1)}, bf16[64,1024]{1,0:T(8,128)(2,1)S(1)}, u32[]{:S(2)}, u32[]{:S(2)}) collective-permute-start(bf16[64,1024]{1,0:T(8,128)(2,1)S(1)} %get-tuple-element.206), channel_id=1, source_target_pairs={{0,1},{1,0},{2,3},{3,2},{4,5},{5,4},{6,7},{7,6},{8,9},{9,8},{10,11... | collective-permute-start | bytes 393224 | tf_op jit(solution)/shard_map/ppermute | solution.py:474
  67.6 1.5 %collective-permute-start.25 = (bf16[64,1024]{1,0:T(8,128)(2,1)S(1)}, bf16[64,1024]{1,0:T(8,128)(2,1)S(1)}, u32[]{:S(2)}, u32[]{:S(2)}) collective-permute-start(bf16[64,1024]{1,0:T(8,128)(2,1)S(1)} %get-tuple-element.207), channel_id=1, source_target_pairs={{0,1},{1,0},{2,3},{3,2},{4,5},{5,4},{6,7},{7,6},{8,9},{9,8},{10,11... | collective-permute-start | bytes 393224 | tf_op jit(solution)/shard_map/ppermute | solution.py:474
  69.5 11.2 %collective-permute-start.26 = (bf16[128,1024]{1,0:T(8,128)(2,1)S(1)}, bf16[128,1024]{1,0:T(8,128)(2,1)S(1)}, u32[]{:S(2)}, u32[]{:S(2)}) collective-permute-start(bf16[128,1024]{1,0:T(8,128)(2,1)S(1)} %back_sum_own.1.part), channel_id=1, source_target_pairs={{0,2},{1,3},{2,0},{3,1},{4,6},{5,7},{6,4},{7,5},{8,10},{9,11},{10,... | collective-permute-start | bytes 786440 | tf_op jit(solution)/shard_map/ppermute | solution.py:477
  75.9 3.1 %collective-permute-start.28 = (bf16[64,1024]{1,0:T(8,128)(2,1)S(1)}, bf16[64,1024]{1,0:T(8,128)(2,1)S(1)}, u32[]{:S(2)}, u32[]{:S(2)}) collective-permute-start(bf16[64,1024]{1,0:T(8,128)(2,1)S(1)} %get-tuple-element.209), channel_id=1, source_target_pairs={{0,1},{1,0},{2,3},{3,2},{4,5},{5,4},{6,7},{7,6},{8,9},{9,8},{10,11... | collective-permute-start | bytes 393224 | tf_op jit(solution)/shard_map/ppermute | solution.py:474
  76.0 3.1 %collective-permute-start.29 = (bf16[64,1024]{1,0:T(8,128)(2,1)S(1)}, bf16[64,1024]{1,0:T(8,128)(2,1)S(1)}, u32[]{:S(2)}, u32[]{:S(2)}) collective-permute-start(bf16[64,1024]{1,0:T(8,128)(2,1)S(1)} %get-tuple-element.210), channel_id=1, source_target_pairs={{0,1},{1,0},{2,3},{3,2},{4,5},{5,4},{6,7},{7,6},{8,9},{9,8},{10,11... | collective-permute-start | bytes 393224 | tf_op jit(solution)/shard_map/ppermute | solution.py:474
  76.8 12.1 %collective-permute-start.38 = (bf16[96,1024]{1,0:T(8,128)(2,1)S(1)}, bf16[96,1024]{1,0:T(8,128)(2,1)S(1)}, u32[]{:S(2)}, u32[]{:S(2)}) collective-permute-start(bf16[96,1024]{1,0:T(8,128)(2,1)S(1)} %get-tuple-element.238), channel_id=1, source_target_pairs={{0,8},{4,12},{8,0},{12,4},{16,24},{20,28},{24,16},{28,20},{1,9},{5... | collective-permute-start | bytes 589832 | tf_op jit(solution)/shard_map/ppermute | solution.py:480
  81.0 1.3 %collective-permute-start.30 = (bf16[32,1024]{1,0:T(8,128)(2,1)S(1)}, bf16[32,1024]{1,0:T(8,128)(2,1)S(1)}, u32[]{:S(2)}, u32[]{:S(2)}) collective-permute-start(bf16[32,1024]{1,0:T(8,128)(2,1)S(1)} %get-tuple-element.219), channel_id=1, source_target_pairs={{0,1},{1,0},{2,3},{3,2},{4,5},{5,4},{6,7},{7,6},{8,9},{9,8},{10,11... | collective-permute-start | bytes 196616 | tf_op jit(solution)/shard_map/ppermute | solution.py:474
  81.1 1.4 %collective-permute-start.31 = (bf16[32,1024]{1,0:T(8,128)(2,1)S(1)}, bf16[32,1024]{1,0:T(8,128)(2,1)S(1)}, u32[]{:S(2)}, u32[]{:S(2)}) collective-permute-start(bf16[32,1024]{1,0:T(8,128)(2,1)S(1)} %get-tuple-element.220), channel_id=1, source_target_pairs={{0,1},{1,0},{2,3},{3,2},{4,5},{5,4},{6,7},{7,6},{8,9},{9,8},{10,11... | collective-permute-start | bytes 196616 | tf_op jit(solution)/shard_map/ppermute | solution.py:474
  81.6 1.3 %collective-permute-start.32 = (bf16[32,1024]{1,0:T(8,128)(2,1)S(1)}, bf16[32,1024]{1,0:T(8,128)(2,1)S(1)}, u32[]{:S(2)}, u32[]{:S(2)}) collective-permute-start(bf16[32,1024]{1,0:T(8,128)(2,1)S(1)} %get-tuple-element.221), channel_id=1, source_target_pairs={{0,1},{1,0},{2,3},{3,2},{4,5},{5,4},{6,7},{7,6},{8,9},{9,8},{10,11... | collective-permute-start | bytes 196616 | tf_op jit(solution)/shard_map/ppermute | solution.py:474
  81.7 1.3 %collective-permute-start.33 = (bf16[32,1024]{1,0:T(8,128)(2,1)S(1)}, bf16[32,1024]{1,0:T(8,128)(2,1)S(1)}, u32[]{:S(2)}, u32[]{:S(2)}) collective-permute-start(bf16[32,1024]{1,0:T(8,128)(2,1)S(1)} %get-tuple-element.222), channel_id=1, source_target_pairs={{0,1},{1,0},{2,3},{3,2},{4,5},{5,4},{6,7},{7,6},{8,9},{9,8},{10,11... | collective-permute-start | bytes 196616 | tf_op jit(solution)/shard_map/ppermute | solution.py:474
  84.3 9.2 %collective-permute-start.34 = (bf16[4,128,256]{2,1,0:T(8,128)(2,1)S(1)}, bf16[4,128,256]{2,1,0:T(8,128)(2,1)S(1)}, u32[]{:S(2)}, u32[]{:S(2)}) collective-permute-start(bf16[4,128,256]{2,1,0:T(8,128)(2,1)S(1)} %get-tuple-element.228), channel_id=1, source_target_pairs={{0,16},{4,20},{8,24},{12,28},{16,0},{20,4},{24,8},{28,12},{1,17},{... | collective-permute-start | bytes 786440 | tf_op jit(solution)/shard_map/ppermute | solution.py:480
  86.0 12.5 %collective-permute-start.37 = (bf16[4,128,256]{2,1,0:T(8,128)(2,1)S(1)}, bf16[4,128,256]{2,1,0:T(8,128)(2,1)S(1)}, u32[]{:S(2)}, u32[]{:S(2)}) collective-permute-start(bf16[4,128,256]{2,1,0:T(8,128)(2,1)S(1)} %get-tuple-element.235), channel_id=1, source_target_pairs={{0,16},{4,20},{8,24},{12,28},{16,0},{20,4},{24,8},{28,12},{1,17},{... | collective-permute-start | bytes 786440 | tf_op jit(solution)/shard_map/ppermute | solution.py:480
  88.9 6.3 %collective-permute-start.39 = (bf16[96,1024]{1,0:T(8,128)(2,1)S(1)}, bf16[96,1024]{1,0:T(8,128)(2,1)S(1)}, u32[]{:S(2)}, u32[]{:S(2)}) collective-permute-start(bf16[96,1024]{1,0:T(8,128)(2,1)S(1)} %back_pick.2), channel_id=1, source_target_pairs={{0,4},{4,0},{8,12},{12,8},{16,20},{20,16},{24,28},{28,24},{1,5},{5... | collective-permute-start | bytes 589832 | tf_op jit(solution)/shard_map/ppermute | solution.py:480
  89.7 17.4 %collective-permute-start.42 = (bf16[128,1024]{1,0:T(8,128)(2,1)S(1)}, bf16[128,1024]{1,0:T(8,128)(2,1)S(1)}, u32[]{:S(2)}, u32[]{:S(2)}) collective-permute-start(bf16[128,1024]{1,0:T(8,128)(2,1)S(1)} %ffn_out_far.1), channel_id=1, source_target_pairs={{0,2},{1,3},{2,0},{3,1},{4,6},{5,7},{6,4},{7,5},{8,10},{9,11},{10,... | collective-permute-start | bytes 786440 | tf_op jit(solution)/shard_map/ppermute | solution.py:477
  93.5 7.1 %collective-permute-start.35 = (bf16[2,128,256]{2,1,0:T(8,128)(2,1)S(1)}, bf16[2,128,256]{2,1,0:T(8,128)(2,1)S(1)}, u32[]{:S(2)}, u32[]{:S(2)}) collective-permute-start(bf16[2,128,256]{2,1,0:T(8,128)(2,1)S(1)} %get-tuple-element.230), channel_id=1, source_target_pairs={{0,4},{4,0},{8,12},{12,8},{16,20},{20,16},{24,28},{28,24},{1,5},{5... | collective-permute-start | bytes 393224 | tf_op jit(solution)/shard_map/ppermute | solution.py:480
  98.6 5.0 %collective-permute-start.40 = (bf16[2,128,256]{2,1,0:T(8,128)(2,1)S(1)}, bf16[2,128,256]{2,1,0:T(8,128)(2,1)S(1)}, u32[]{:S(2)}, u32[]{:S(2)}) collective-permute-start(bf16[2,128,256]{2,1,0:T(8,128)(2,1)S(1)} %get-tuple-element.241), channel_id=1, source_target_pairs={{0,4},{4,0},{8,12},{12,8},{16,20},{20,16},{24,28},{28,24},{1,5},{5... | collective-permute-start | bytes 393224 | tf_op jit(solution)/shard_map/ppermute | solution.py:480
  100.3 8.0 %collective-permute-start.43 = (bf16[96,1024]{1,0:T(8,128)(2,1)S(1)}, bf16[96,1024]{1,0:T(8,128)(2,1)S(1)}, u32[]{:S(2)}, u32[]{:S(2)}) collective-permute-start(bf16[96,1024]{1,0:T(8,128)(2,1)S(1)} %back_pick.3), channel_id=1, source_target_pairs={{0,16},{4,20},{8,24},{12,28},{16,0},{20,4},{24,8},{28,12},{1,17},{... | collective-permute-start | bytes 589832 | tf_op jit(solution)/shard_map/ppermute | solution.py:480
  100.6 7.6 %collective-permute-start.36 = (bf16[1,128,256]{2,1,0:T(8,128)(2,1)S(1)}, bf16[1,128,256]{2,1,0:T(8,128)(2,1)S(1)}, u32[]{:S(2)}, u32[]{:S(2)}) collective-permute-start(bf16[1,128,256]{2,1,0:T(8,128)(2,1)S(1)} %get-tuple-element.231), channel_id=1, source_target_pairs={{0,8},{4,12},{8,0},{12,4},{16,24},{20,28},{24,16},{28,20},{1,9},{5... | collective-permute-start | bytes 196616 | tf_op jit(solution)/shard_map/ppermute | solution.py:480
  103.7 5.7 %collective-permute-start.41 = (bf16[1,128,256]{2,1,0:T(8,128)(2,1)S(1)}, bf16[1,128,256]{2,1,0:T(8,128)(2,1)S(1)}, u32[]{:S(2)}, u32[]{:S(2)}) collective-permute-start(bf16[1,128,256]{2,1,0:T(8,128)(2,1)S(1)} %get-tuple-element.242), channel_id=1, source_target_pairs={{0,8},{4,12},{8,0},{12,4},{16,24},{20,28},{24,16},{28,20},{1,9},{5... | collective-permute-start | bytes 196616 | tf_op jit(solution)/shard_map/ppermute | solution.py:480

commit v14 on v13

--- a/solution.py
+++ b/solution.py
@@ -485,9 +485,11 @@
     mean_load = rows_dev // groups
     capacity = -(-(mean_load + mean_load // 2) // 8) * 8
     code = (dest_owner * rows_dev + dest_slot).reshape(1, rows_dev)
-    order = [0] + sorted(
-        range(1, groups), key=lambda k: (-((2 * (k % packs)) // packs), k % packs, k)
-    )
+    offsets = range(1, groups)
+    across = sorted((k for k in offsets if 2 * (k % packs) >= packs), key=lambda k: (k % packs, k))
+    short = [k for k in offsets if k not in across]
+    hops = [k for k in short if k & (k - 1)]
+    order = [0] + across[:2] + hops + across[2:] + [k for k in short if k not in hops]
     *sends, place = run(
         functools.partial(route_send, capacity, order),
         [like((capacity, width + rows_dev), BF16)] * groups + [like((1, rows_dev), jnp.int32)],

time: 110 us -> 110 us (level)
  waiting for transfers between devices: 40 us -> 37 us
  starting transfers between devices: 41 us -> 43.2 us
    ppermute x16, waiting for transfers between devices: 15.3 us -> 12.8 us  [crossed(): return lax.ppermute(value, group_axes, [(i, i ^ k) for i in range(groups)])]
    ppermute x16, starting transfers between devices: 25.8 us -> 28.1 us  [crossed(): return lax.ppermute(value, group_axes, [(i, i ^ k) for i in range(groups)])]
  transfers between devices with their start and end apart: 44 -> 44, of which waited for: 27 -> 26; matrix products, arithmetic and copies ran while one was open for 1% -> 1% of each run, Pallas kernels for 23% -> 23%
where the time goes in v14:
time: 110 us; the launch traced here: 109 us
  starting transfers between devices  43.2 us (39%)
  waiting for transfers between devices  37 us (34%)
  Pallas kernels  26.6 us (24%)
    ppermute x16, starting transfers between devices, crossed(): return lax.ppermute(value, group_axes, [(i, i ^ k) for i in range(groups)])  28.1 us
    pallas_call x35, Pallas kernels, run(): pl.pallas_call(body, out_shape=list(outs), in_specs=[pl.BlockSpec(memory_...  26.6 us
    ppermute x9, waiting for transfers between devices, far(): return lax.ppermute(value, 'tensor', [(i, i ^ 2) for i in range(tensors)])  18.6 us
    ppermute x16, waiting for transfers between devices, crossed(): return lax.ppermute(value, group_axes, [(i, i ^ k) for i in range(groups)])  12.8 us
    ppermute x9, starting transfers between devices, far(): return lax.ppermute(value, 'tensor', [(i, i ^ 2) for i in range(tensors)])  9.99 us
    ppermute x19, waiting for transfers between devices, near(): return lax.ppermute(value, 'tensor', [(i, i ^ 1) for i in range(tensors)])  5.63 us
    ppermute x19, starting transfers between devices, near(): return lax.ppermute(value, 'tensor', [(i, i ^ 1) for i in range(tensors)])  5.12 us
  transfers between devices with their start and end apart: 44, of which 26 were waited for; matrix products, arithmetic and copies ran while one was open for 1% of the time, Pallas kernels for 23%

profile of v14, /device:TPU:0, one launch (start us, length us, event | category | flops | bytes accessed | tf_op | source)
XLA Modules:
  0.0 109.5 jit_solution(7966502244697910583)
XLA Ops:
  0.6 0.5 collective-permute-start
  1.2 0.7 add_bitcast_fusion.code
  1.9 0.9 copy-done.7
  3.2 4.1 %collective-permute-start.2 = (bf16[24,1152]{1,0:T(8,128)(2,1)S(1)}, bf16[24,1152]{1,0:T(8,128)(2,1)S(1)}, u32[]{:S(2)}, u32[]{:S(2)}) collective-permute-start(bf16[24,1152]{1,0:T(8,128)(2,1)S(1)} %get-tuple-element.130), channel_id=1, source_target_pairs={{0,8},{4,12},{8,0},{12,4},{16,24},{20,28},{24,16},{28,20},{1,9},{5... | collective-permute-start | bytes 165896 | tf_op jit(solution)/shard_map/ppermute | solution.py:480
  7.3 1.3 %collective-permute-start.3 = (bf16[24,1152]{1,0:T(8,128)(2,1)S(1)}, bf16[24,1152]{1,0:T(8,128)(2,1)S(1)}, u32[]{:S(2)}, u32[]{:S(2)}) collective-permute-start(bf16[24,1152]{1,0:T(8,128)(2,1)S(1)} %get-tuple-element.131), channel_id=1, source_target_pairs={{0,24},{4,28},{8,16},{12,20},{16,8},{20,12},{24,0},{28,4},{1,25},{... | collective-permute-start | bytes 165896 | tf_op jit(solution)/shard_map/ppermute | solution.py:480
  8.6 2.0 %collective-permute-start.4 = (bf16[24,1152]{1,0:T(8,128)(2,1)S(1)}, bf16[24,1152]{1,0:T(8,128)(2,1)S(1)}, u32[]{:S(2)}, u32[]{:S(2)}) collective-permute-start(bf16[24,1152]{1,0:T(8,128)(2,1)S(1)} %get-tuple-element.138), channel_id=1, source_target_pairs={{0,20},{4,16},{8,28},{12,24},{16,4},{20,0},{24,12},{28,8},{1,21},{... | collective-permute-start | bytes 165896 | tf_op jit(solution)/shard_map/ppermute | solution.py:480
  10.5 2.5 %collective-permute-start.5 = (bf16[24,1152]{1,0:T(8,128)(2,1)S(1)}, bf16[24,1152]{1,0:T(8,128)(2,1)S(1)}, u32[]{:S(2)}, u32[]{:S(2)}) collective-permute-start(bf16[24,1152]{1,0:T(8,128)(2,1)S(1)} %get-tuple-element.139), channel_id=1, source_target_pairs={{0,12},{4,8},{8,4},{12,0},{16,28},{20,24},{24,20},{28,16},{1,13},{... | collective-permute-start | bytes 165896 | tf_op jit(solution)/shard_map/ppermute | solution.py:480
  13.0 1.9 %collective-permute-start.6 = (bf16[24,1152]{1,0:T(8,128)(2,1)S(1)}, bf16[24,1152]{1,0:T(8,128)(2,1)S(1)}, u32[]{:S(2)}, u32[]{:S(2)}) collective-permute-start(bf16[24,1152]{1,0:T(8,128)(2,1)S(1)} %get-tuple-element.140), channel_id=1, source_target_pairs={{0,28},{4,24},{8,20},{12,16},{16,12},{20,8},{24,4},{28,0},{1,29},{... | collective-permute-start | bytes 165896 | tf_op jit(solution)/shard_map/ppermute | solution.py:480
  14.9 1.0 collective-permute-start.8
  15.9 0.8 turn.1
  16.7 3.2 %collective-permute-done.6.refs_5_ = bf16[24,1152]{1,0:T(8,128)(2,1)S(1)} collective-permute-done((bf16[24,1152]{1,0:T(8,128)(2,1)S(1)}, bf16[24,1152]{1,0:T(8,128)(2,1)S(1)}, u32[]{:S(2)}, u32[]{:S(2)}) %collective-permute-start.6) | collective-permute-done | bytes 55328 | tf_op jit(solution)/shard_map/ppermute | solution.py:480
  20.2 1.6 %collective-permute-start.9 = (bf16[128,1024]{1,0:T(8,128)(2,1)S(1)}, bf16[128,1024]{1,0:T(8,128)(2,1)S(1)}, u32[]{:S(2)}, u32[]{:S(2)}) collective-permute-start(bf16[128,1024]{1,0:T(8,128)(2,1)S(1)} %get-tuple-element.151.refs_0_.refs_3_), channel_id=1, source_target_pairs={{0,2},{1,3},{2,0},{3,1},{4,6},{5,7},{6,4},{7,5},{8,10},{9,11},{10,... | collective-permute-start | bytes 786440 | tf_op jit(solution)/shard_map/ppermute | solution.py:477
  21.8 0.5 collective-permute-start.11
  22.3 0.8 collective-permute-done.10.refs_1_.refs_4_
  23.4 2.3 %encode_first.1 = (f32[256,256]{1,0:T(8,128)S(1)}, bf16[256,1024]{1,0:T(8,128)(2,1)S(1)}, bf16[128,1024]{1,0:T(8,128)(2,1)S(1)}, bf16[4,2,128,256]{3,2,1,0:T(8,128)(2,1)S(1)}) custom-call(bf16[128,1024]{1,0:T(8,128)(2,1)S(1)} %get-tuple-element.151.refs_0_.refs_3_, bf16[64,1024]{1,0:T(8,128)(2,1)S(1)} %collective-permute-done.10.refs_1_.refs_4_, ...), custom_call_target="tpu_custom_call" | custom-call | tf_op jit(solution)/shard_map/encode_first/pallas_call | solution.py:64
  25.6 1.3 %collective-permute-done.9.refs_0_.refs_5_ = bf16[128,1024]{1,0:T(8,128)(2,1)S(1)} collective-permute-done((bf16[128,1024]{1,0:T(8,128)(2,1)S(1)}, bf16[128,1024]{1,0:T(8,128)(2,1)S(1)}, u32[]{:S(2)}, u32[]{:S(2)}) %collective-permute-start.9) | collective-permute-done | bytes 262176 | tf_op jit(solution)/shard_map/ppermute | solution.py:477
  26.9 0.5 collective-permute-start.12
  27.4 1.5 %collective-permute-start.15 = (bf16[128,1024]{1,0:T(8,128)(2,1)S(1)}, bf16[128,1024]{1,0:T(8,128)(2,1)S(1)}, u32[]{:S(2)}, u32[]{:S(2)}) collective-permute-start(bf16[128,1024]{1,0:T(8,128)(2,1)S(1)} %bitcast.5), channel_id=1, source_target_pairs={{0,2},{1,3},{2,0},{3,1},{4,6},{5,7},{6,4},{7,5},{8,10},{9,11},{10,... | collective-permute-start | bytes 786440 | tf_op jit(solution)/shard_map/ppermute | solution.py:477
  29.0 1.4 %encode_third.1 = (f32[128,256]{1,0:T(8,128)S(1)}, bf16[128,1024]{1,0:T(8,128)(2,1)S(1)}, bf16[128,1024]{1,0:T(8,128)(2,1)S(1)}, bf16[4,1,128,256]{3,2,1,0:T(8,128)(2,1)S(1)}) custom-call(bf16[128,1024]{1,0:T(8,128)(2,1)S(1)} %collective-permute-done.9.refs_0_.refs_5_, bf16[2,1024,1024]{2,1,0:T(8,128)(2,1)S(1)} %copy-done, bf16[4,1024,256]{2,1,0:T(8,128)(2,1)S(1)} %copy-done.1), custom_call_target="tpu_custom_call" | custom-call | tf_op jit(solution)/shard_map/encode_third/pallas_call | solution.py:64
  30.4 2.5 %attend_first.1 = (f32[256,256]{1,0:T(8,128)S(1)}, bf16[256,1024]{1,0:T(8,128)(2,1)S(1)}, bf16[4,4,128,256]{3,2,1,0:T(8,128)(2,1)S(1)}, f32[4,128,256]{2,1,0:T(8...) custom-call(s32[4,1,128]{2,1,0:T(1,128)S(1)} %bitcast.8, ...), custom_call_target="tpu_custom_call" | custom-call | tf_op jit(solution)/shard_map/attend_first/pallas_call | solution.py:64
  33.0 1.3 %collective-permute-done.13.take = bf16[256,256]{1,0:T(8,128)(2,1)S(1)} collective-permute-done((bf16[256,256]{1,0:T(8,128)(2,1)S(1)}, bf16[256,256]{1,0:T(8,128)(2,1)S(1)}, u32[]{:S(2)}, u32[]{:S(2)}) %collective-permute-start.13) | collective-permute-done | bytes 131104 | tf_op jit(solution)/shard_map/ppermute | solution.py:474
  34.7 0.6 collective-permute-start.17
  35.7 1.5 %collective-permute-start.16 = (bf16[128,1024]{1,0:T(8,128)(2,1)S(1)}, bf16[128,1024]{1,0:T(8,128)(2,1)S(1)}, u32[]{:S(2)}, u32[]{:S(2)}) collective-permute-start(bf16[128,1024]{1,0:T(8,128)(2,1)S(1)} %attn_out_own.1.part), channel_id=1, source_target_pairs={{0,2},{1,3},{2,0},{3,1},{4,6},{5,7},{6,4},{7,5},{8,10},{9,11},{10,... | collective-permute-start | bytes 786440 | tf_op jit(solution)/shard_map/ppermute | solution.py:477
  37.2 6.7 %collective-permute-done.17.got = bf16[128,1024]{1,0:T(8,128)(2,1)S(1)} collective-permute-done((bf16[128,1024]{1,0:T(8,128)(2,1)S(1)}, bf16[128,1024]{1,0:T(8,128)(2,1)S(1)}, u32[]{:S(2)}, u32[]{:S(2)}) %collective-permute-start.17) | collective-permute-done | bytes 262176 | tf_op jit(solution)/shard_map/ppermute | solution.py:477
  44.1 2.9 %ffn_own.1 = (bf16[128,1024]{1,0:T(8,128)(2,1)S(1)}, bf16[128,1024]{1,0:T(8,128)(2,1)S(1)}) custom-call(bf16[128,1024]{1,0:T(8,128)(2,1)S(1)} %get-tuple-element.167.rows_ref, bf16[128,1024]{1,0:T(8,128)(2,1)S(1)} %bitcast.6, bf16[2,1024,512]{2,1,0:T(8,128)(2,1)S(1)} %copy-done.3, bf16[2,1024,512]{2,1,0:T(8,128)(2,1)S(1)} %collective-permute-done.in_b, ...), custom_call_target="tpu_custom_call" | custom-call | tf_op jit(solution)/shard_map/ffn_own/pallas_call | solution.py:64
  47.0 1.7 %collective-permute-done.16.got = bf16[128,1024]{1,0:T(8,128)(2,1)S(1)} collective-permute-done((bf16[128,1024]{1,0:T(8,128)(2,1)S(1)}, bf16[128,1024]{1,0:T(8,128)(2,1)S(1)}, u32[]{:S(2)}, u32[]{:S(2)}) %collective-permute-start.16) | collective-permute-done | bytes 262176 | tf_op jit(solution)/shard_map/ppermute | solution.py:477
  48.7 0.5 collective-permute-start.19
  49.4 2.9 %ffn_far.1 = (bf16[128,1024]{1,0:T(8,128)(2,1)S(1)}, bf16[128,1024]{1,0:T(8,128)(2,1)S(1)}) custom-call(bf16[128,1024]{1,0:T(8,128)(2,1)S(1)} %get-tuple-element.174.rows_ref, bf16[128,1024]{1,0:T(8,128)(2,1)S(1)} %collective-permute-done.15.d_out_ref.d_out, bf16[2,1024,512]{2,1,0:T(8,128)(2,1)S(1)} %copy-done.3, ...), custom_call_target="tpu_custom_call" | custom-call | tf_op jit(solution)/shard_map/ffn_far/pallas_call | solution.py:64
  52.3 1.6 %collective-permute-start.18 = (bf16[128,1024]{1,0:T(8,128)(2,1)S(1)}, bf16[128,1024]{1,0:T(8,128)(2,1)S(1)}, u32[]{:S(2)}, u32[]{:S(2)}) collective-permute-start(bf16[128,1024]{1,0:T(8,128)(2,1)S(1)} %get-tuple-element.176.back), channel_id=1, source_target_pairs={{0,2},{1,3},{2,0},{3,1},{4,6},{5,7},{6,4},{7,5},{8,10},{9,11},{10,... | collective-permute-start | bytes 786440 | tf_op jit(solution)/shard_map/ppermute | solution.py:477
  53.9 4.0 %collective-permute-done.19.got = bf16[128,1024]{1,0:T(8,128)(2,1)S(1)} collective-permute-done((bf16[128,1024]{1,0:T(8,128)(2,1)S(1)}, bf16[128,1024]{1,0:T(8,128)(2,1)S(1)}, u32[]{:S(2)}, u32[]{:S(2)}) %collective-permute-start.19) | collective-permute-done | bytes 262176 | tf_op jit(solution)/shard_map/ppermute | solution.py:477
  58.0 0.5 resid_back_far.1
  58.5 0.5 collective-permute-start.21
  59.0 0.8 collective-permute-done.20.fourth_a
  60.0 1.6 %attn_back_first.1 = (bf16[4,128,256]{2,1,0:T(8,128)(2,1)S(1)}, f32[4,128,256]{2,1,0:T(8,128)S(1)}, f32[4,128,256]{2,1,0:T(8,128)S(1)}, bf16[4,128,256]{2,1,0:T(8,128)(2,1)S(1)}) custom-call(s32[4,1,128]{2,1,0:T(1,128)S(1)} %bitcast.9, bf16[128,1024]{1,0:T(8,128)(2,1)S(1)} %get-tuple-element.178.third.d_resid, ...), custom_call_target="tpu_custom_call" | custom-call | tf_op jit(solution)/shard_map/attn_back_first/pallas_call | solution.py:64
  62.3 1.2 %attn_back_own.1 = (bf16[128,1024]{1,0:T(8,128)(2,1)S(1)}, bf16[4,128,256]{2,1,0:T(8,128)(2,1)S(1)}, f32[4,128,256]{2,1,0:T(8,128)S(1)}, f32[4,128,256]{2,1,0:T(8,128)S(1)}, bf16[4,128,256]{2,1,0:T(8,128)(2,1)S(1)}) custom-call(s32[4,1,128]{2,1,0:T(1,128)S(1)} %bitcast.10, ...), custom_call_target="tpu_custom_call", output_to_operand_aliasing={{1}: (5, {}), {2}: (6, {}), {3}: (7, {}), {4}: (8, {})} | custom-call | tf_op jit(solution)/shard_map/attn_back_own/pallas_call | solution.py:64
  63.5 0.5 collective-permute-start.23
  64.0 0.8 attn_back_second.1
  65.6 0.6 collective-permute-start.27
  67.2 0.8 collective-permute-done.24.refs_0_
  68.2 0.5 back_sum_own.1.part
  68.6 1.6 %collective-permute-start.26 = (bf16[128,1024]{1,0:T(8,128)(2,1)S(1)}, bf16[128,1024]{1,0:T(8,128)(2,1)S(1)}, u32[]{:S(2)}, u32[]{:S(2)}) collective-permute-start(bf16[128,1024]{1,0:T(8,128)(2,1)S(1)} %back_sum_own.1.part), channel_id=1, source_target_pairs={{0,2},{1,3},{2,0},{3,1},{4,6},{5,7},{6,4},{7,5},{8,10},{9,11},{10,... | collective-permute-start | bytes 786440 | tf_op jit(solution)/shard_map/ppermute | solution.py:477
  70.3 4.5 %collective-permute-done.27.got = bf16[128,1024]{1,0:T(8,128)(2,1)S(1)} collective-permute-done((bf16[128,1024]{1,0:T(8,128)(2,1)S(1)}, bf16[128,1024]{1,0:T(8,128)(2,1)S(1)}, u32[]{:S(2)}, u32[]{:S(2)}) %collective-permute-start.27) | collective-permute-done | bytes 262176 | tf_op jit(solution)/shard_map/ppermute | solution.py:477
  75.1 0.5 collective-permute-start.29
  75.9 3.0 %collective-permute-start.38 = (bf16[96,1024]{1,0:T(8,128)(2,1)S(1)}, bf16[96,1024]{1,0:T(8,128)(2,1)S(1)}, u32[]{:S(2)}, u32[]{:S(2)}) collective-permute-start(bf16[96,1024]{1,0:T(8,128)(2,1)S(1)} %get-tuple-element.238), channel_id=1, source_target_pairs={{0,8},{4,12},{8,0},{12,4},{16,24},{20,28},{24,16},{28,20},{1,9},{5... | collective-permute-start | bytes 589832 | tf_op jit(solution)/shard_map/ppermute | solution.py:480
  78.9 1.0 enc_grads_first.1
  80.3 0.5 collective-permute-start.31
  82.2 1.3 %enc_grads_second.1 = (f32[4,128,256]{2,1,0:T(8,128)S(1)}, bf16[4,128,256]{2,1,0:T(8,128)(2,1)S(1)}, f32[4,128,256]{2,1,0:T(8,128)S(1)}, bf16[4,128,256]{2,1,0:T(8,128)(2,1)S(1)}) custom-call(bf16[128,1024]{1,0:T(8,128)(2,1)S(1)} %get-tuple-element.218.refs_0_, bf16[32,1024]{1,0:T(8,128)(2,1)S(1)} %collective-permute-done.30.refs_1_, ...), custom_call_target="tpu_custom_call" | custom-call | tf_op jit(solution)/shard_map/enc_grads_second/pallas_call | solution.py:64
  83.5 0.8 collective-permute-start.34
  84.3 1.3 %collective-permute-start.37 = (bf16[4,128,256]{2,1,0:T(8,128)(2,1)S(1)}, bf16[4,128,256]{2,1,0:T(8,128)(2,1)S(1)}, u32[]{:S(2)}, u32[]{:S(2)}) collective-permute-start(bf16[4,128,256]{2,1,0:T(8,128)(2,1)S(1)} %get-tuple-element.235), channel_id=1, source_target_pairs={{0,16},{4,20},{8,24},{12,28},{16,0},{20,4},{24,8},{28,12},{1,17},{... | collective-permute-start | bytes 786440 | tf_op jit(solution)/shard_map/ppermute | solution.py:480
  85.6 2.7 %collective-permute-done.38.refs_1_ = bf16[96,1024]{1,0:T(8,128)(2,1)S(1)} collective-permute-done((bf16[96,1024]{1,0:T(8,128)(2,1)S(1)}, bf16[96,1024]{1,0:T(8,128)(2,1)S(1)}, u32[]{:S(2)}, u32[]{:S(2)}) %collective-permute-start.38) | collective-permute-done | bytes 196640 | tf_op jit(solution)/shard_map/ppermute | solution.py:480
  88.3 0.6 collective-permute-start.39
  88.9 0.5 ffn_out_far.1
  89.4 0.6 collective-permute-start.42
  90.0 2.7 %collective-permute-done.34.got = bf16[4,128,256]{2,1,0:T(8,128)(2,1)S(1)} collective-permute-done((bf16[4,128,256]{2,1,0:T(8,128)(2,1)S(1)}, bf16[4,128,256]{2,1,0:T(8,128)(2,1)S(1)}, u32[]{:S(2)}, u32[]{:S(2)}) %collective-permute-start.34) | collective-permute-done | bytes 262176 | tf_op jit(solution)/shard_map/ppermute | solution.py:480
  92.7 1.4 %collective-permute-start.35 = (bf16[2,128,256]{2,1,0:T(8,128)(2,1)S(1)}, bf16[2,128,256]{2,1,0:T(8,128)(2,1)S(1)}, u32[]{:S(2)}, u32[]{:S(2)}) collective-permute-start(bf16[2,128,256]{2,1,0:T(8,128)(2,1)S(1)} %get-tuple-element.230), channel_id=1, source_target_pairs={{0,4},{4,0},{8,12},{12,8},{16,20},{20,16},{24,28},{28,24},{1,5},{5... | collective-permute-start | bytes 393224 | tf_op jit(solution)/shard_map/ppermute | solution.py:480
  94.1 0.9 collective-permute-done.39.refs_2_
  95.0 2.7 %collective-permute-done.37.got = bf16[4,128,256]{2,1,0:T(8,128)(2,1)S(1)} collective-permute-done((bf16[4,128,256]{2,1,0:T(8,128)(2,1)S(1)}, bf16[4,128,256]{2,1,0:T(8,128)(2,1)S(1)}, u32[]{:S(2)}, u32[]{:S(2)}) %collective-permute-start.37) | collective-permute-done | bytes 262176 | tf_op jit(solution)/shard_map/ppermute | solution.py:480
  97.8 1.4 %collective-permute-start.40 = (bf16[2,128,256]{2,1,0:T(8,128)(2,1)S(1)}, bf16[2,128,256]{2,1,0:T(8,128)(2,1)S(1)}, u32[]{:S(2)}, u32[]{:S(2)}) collective-permute-start(bf16[2,128,256]{2,1,0:T(8,128)(2,1)S(1)} %get-tuple-element.241), channel_id=1, source_target_pairs={{0,4},{4,0},{8,12},{12,8},{16,20},{20,16},{24,28},{28,24},{1,5},{5... | collective-permute-start | bytes 393224 | tf_op jit(solution)/shard_map/ppermute | solution.py:480
  99.2 1.1 collective-permute-start.43
  100.3 2.2 %collective-permute-start.36 = (bf16[1,128,256]{2,1,0:T(8,128)(2,1)S(1)}, bf16[1,128,256]{2,1,0:T(8,128)(2,1)S(1)}, u32[]{:S(2)}, u32[]{:S(2)}) collective-permute-start(bf16[1,128,256]{2,1,0:T(8,128)(2,1)S(1)} %get-tuple-element.231), channel_id=1, source_target_pairs={{0,8},{4,12},{8,0},{12,4},{16,24},{20,28},{24,16},{28,20},{1,9},{5... | collective-permute-start | bytes 196616 | tf_op jit(solution)/shard_map/ppermute | solution.py:480
  102.9 3.6 %collective-permute-start.41 = (bf16[1,128,256]{2,1,0:T(8,128)(2,1)S(1)}, bf16[1,128,256]{2,1,0:T(8,128)(2,1)S(1)}, u32[]{:S(2)}, u32[]{:S(2)}) collective-permute-start(bf16[1,128,256]{2,1,0:T(8,128)(2,1)S(1)} %get-tuple-element.242), channel_id=1, source_target_pairs={{0,8},{4,12},{8,0},{12,4},{16,24},{20,28},{24,16},{28,20},{1,9},{5... | collective-permute-start | bytes 196616 | tf_op jit(solution)/shard_map/ppermute | solution.py:480
  106.5 1.2 %ffn_out_own.1 = bf16[128,1024]{1,0:T(8,128)(2,1)} custom-call(bf16[128,1024]{1,0:T(8,128)(2,1)S(1)} %get-tuple-element.243.hidden, bf16[512,1024]{1,0:T(8,128)(2,1)S(1)} %copy-done.2, bf16[512,1024]{1,0:T(8,128)(2,1)S(1)} %collective-permute-done.1.out_b.w_b, bf16[128,1024]{1,0:T(8,128)(2,1)S(1)} %get-tuple-element.186.resid, ...), custom_call_target="tpu_custom_call" | custom-call | tf_op jit(solution)/shard_map/ffn_out_own/pallas_call | solution.py:64
  107.7 1.0 back_recv.1
  108.7 0.7 finish.1
  (76 shorter events, 8.1 us)
Async XLA Ops:
  0.6 7.9 %collective-permute-start = (bf16[2,1024,512]{2,1,0:T(8,128)(2,1)}, bf16[2,1024,512]{2,1,0:T(8,128)(2,1)S(1)}, u32[]{:S(2)}, u32[]{:S(2)}) collective-permute-start(bf16[2,1024,512]{2,1,0:T(8,128)(2,1)} %in_a.3), channel_id=1, source_target_pairs={{0,1},{1,0},{2,3},{3,2},{4,5},{5,4},{6,7},{7,6},{8,9},{9,8},{10,11... | collective-permute-start | bytes 6291464 | tf_op jit(solution)/shard_map/ppermute | solution.py:474
  1.1 7.4 %collective-permute-start.1 = (bf16[512,1024]{1,0:T(8,128)(2,1)}, bf16[512,1024]{1,0:T(8,128)(2,1)S(1)}, u32[]{:S(2)}, u32[]{:S(2)}) collective-permute-start(bf16[512,1024]{1,0:T(8,128)(2,1)} %w_a.3), channel_id=1, source_target_pairs={{0,1},{1,0},{2,3},{3,2},{4,5},{5,4},{6,7},{7,6},{8,9},{9,8},{10,11... | collective-permute-start | bytes 3145736 | tf_op jit(solution)/shard_map/ppermute | solution.py:474
  1.9 0.9 copy-start.7
  2.9 13.0 %copy-start.1 = (bf16[4,1024,256]{2,1,0:T(8,128)(2,1)S(1)}, bf16[4,1024,256]{2,1,0:T(8,128)(2,1)}, u32[]{:S(2)}) copy-start(bf16[4,1024,256]{2,1,0:T(8,128)(2,1)} %w_in.1) | copy-start | bytes 6291460
  2.9 13.0 %copy-start.4 = (bf16[256,1024]{1,0:T(8,128)(2,1)S(1)}, bf16[256,1024]{1,0:T(8,128)(2,1)}, u32[]{:S(2)}) copy-start(bf16[256,1024]{1,0:T(8,128)(2,1)} %w_own.3) | copy-start | bytes 1572868
  2.9 20.5 %copy-start = (bf16[2,1024,1024]{2,1,0:T(8,128)(2,1)S(1)}, bf16[2,1024,1024]{2,1,0:T(8,128)(2,1)}, u32[]{:S(2)}) copy-start(bf16[2,1024,1024]{2,1,0:T(8,128)(2,1)} %refs_9_.1) | copy-start | bytes 12582916
  3.2 11.7 %collective-permute-start.2 = (bf16[24,1152]{1,0:T(8,128)(2,1)S(1)}, bf16[24,1152]{1,0:T(8,128)(2,1)S(1)}, u32[]{:S(2)}, u32[]{:S(2)}) collective-permute-start(bf16[24,1152]{1,0:T(8,128)(2,1)S(1)} %get-tuple-element.130), channel_id=1, source_target_pairs={{0,8},{4,12},{8,0},{12,4},{16,24},{20,28},{24,16},{28,20},{1,9},{5... | collective-permute-start | bytes 165896 | tf_op jit(solution)/shard_map/ppermute | solution.py:480
  7.3 7.6 %collective-permute-start.3 = (bf16[24,1152]{1,0:T(8,128)(2,1)S(1)}, bf16[24,1152]{1,0:T(8,128)(2,1)S(1)}, u32[]{:S(2)}, u32[]{:S(2)}) collective-permute-start(bf16[24,1152]{1,0:T(8,128)(2,1)S(1)} %get-tuple-element.131), channel_id=1, source_target_pairs={{0,24},{4,28},{8,16},{12,20},{16,8},{20,12},{24,0},{28,4},{1,25},{... | collective-permute-start | bytes 165896 | tf_op jit(solution)/shard_map/ppermute | solution.py:480
  8.6 8.1 %collective-permute-start.4 = (bf16[24,1152]{1,0:T(8,128)(2,1)S(1)}, bf16[24,1152]{1,0:T(8,128)(2,1)S(1)}, u32[]{:S(2)}, u32[]{:S(2)}) collective-permute-start(bf16[24,1152]{1,0:T(8,128)(2,1)S(1)} %get-tuple-element.138), channel_id=1, source_target_pairs={{0,20},{4,16},{8,28},{12,24},{16,4},{20,0},{24,12},{28,8},{1,21},{... | collective-permute-start | bytes 165896 | tf_op jit(solution)/shard_map/ppermute | solution.py:480
  10.5 6.2 %collective-permute-start.5 = (bf16[24,1152]{1,0:T(8,128)(2,1)S(1)}, bf16[24,1152]{1,0:T(8,128)(2,1)S(1)}, u32[]{:S(2)}, u32[]{:S(2)}) collective-permute-start(bf16[24,1152]{1,0:T(8,128)(2,1)S(1)} %get-tuple-element.139), channel_id=1, source_target_pairs={{0,12},{4,8},{8,4},{12,0},{16,28},{20,24},{24,20},{28,16},{1,13},{... | collective-permute-start | bytes 165896 | tf_op jit(solution)/shard_map/ppermute | solution.py:480
  13.0 7.0 %collective-permute-start.6 = (bf16[24,1152]{1,0:T(8,128)(2,1)S(1)}, bf16[24,1152]{1,0:T(8,128)(2,1)S(1)}, u32[]{:S(2)}, u32[]{:S(2)}) collective-permute-start(bf16[24,1152]{1,0:T(8,128)(2,1)S(1)} %get-tuple-element.140), channel_id=1, source_target_pairs={{0,28},{4,24},{8,20},{12,16},{16,12},{20,8},{24,4},{28,0},{1,29},{... | collective-permute-start | bytes 165896 | tf_op jit(solution)/shard_map/ppermute | solution.py:480
  14.9 5.1 %collective-permute-start.7 = (bf16[24,1152]{1,0:T(8,128)(2,1)S(1)}, bf16[24,1152]{1,0:T(8,128)(2,1)S(1)}, u32[]{:S(2)}, u32[]{:S(2)}) collective-permute-start(bf16[24,1152]{1,0:T(8,128)(2,1)S(1)} %get-tuple-element.141), channel_id=1, source_target_pairs={{0,4},{4,0},{8,12},{12,8},{16,20},{20,16},{24,28},{28,24},{1,5},{5... | collective-permute-start | bytes 165896 | tf_op jit(solution)/shard_map/ppermute | solution.py:480
  14.9 5.1 %collective-permute-start.8 = (bf16[24,1152]{1,0:T(8,128)(2,1)S(1)}, bf16[24,1152]{1,0:T(8,128)(2,1)S(1)}, u32[]{:S(2)}, u32[]{:S(2)}) collective-permute-start(bf16[24,1152]{1,0:T(8,128)(2,1)S(1)} %get-tuple-element.142), channel_id=1, source_target_pairs={{0,16},{4,20},{8,24},{12,28},{16,0},{20,4},{24,8},{28,12},{1,17},{... | collective-permute-start | bytes 165896 | tf_op jit(solution)/shard_map/ppermute | solution.py:480
  20.2 6.7 %collective-permute-start.9 = (bf16[128,1024]{1,0:T(8,128)(2,1)S(1)}, bf16[128,1024]{1,0:T(8,128)(2,1)S(1)}, u32[]{:S(2)}, u32[]{:S(2)}) collective-permute-start(bf16[128,1024]{1,0:T(8,128)(2,1)S(1)} %get-tuple-element.151.refs_0_.refs_3_), channel_id=1, source_target_pairs={{0,2},{1,3},{2,0},{3,1},{4,6},{5,7},{6,4},{7,5},{8,10},{9,11},{10,... | collective-permute-start | bytes 786440 | tf_op jit(solution)/shard_map/ppermute | solution.py:477
  21.8 1.3 %collective-permute-start.10 = (bf16[64,1024]{1,0:T(8,128)(2,1)S(1)}, bf16[64,1024]{1,0:T(8,128)(2,1)S(1)}, u32[]{:S(2)}, u32[]{:S(2)}) collective-permute-start(bf16[64,1024]{1,0:T(8,128)(2,1)S(1)} %get-tuple-element.152), channel_id=1, source_target_pairs={{0,1},{1,0},{2,3},{3,2},{4,5},{5,4},{6,7},{7,6},{8,9},{9,8},{10,11... | collective-permute-start | bytes 393224 | tf_op jit(solution)/shard_map/ppermute | solution.py:474
  21.8 5.6 %copy-start.5 = (bf16[1,128,1024]{2,1,0:T(8,128)(2,1)S(1)}, bf16[1,128,1024]{2,1,0:T(8,128)(2,1)}, u32[]{:S(2)}) copy-start(bf16[1,128,1024]{2,1,0:T(8,128)(2,1)} %param.19) | copy-start | bytes 786436
  21.8 1.5 %collective-permute-start.11 = (bf16[64,1024]{1,0:T(8,128)(2,1)S(1)}, bf16[64,1024]{1,0:T(8,128)(2,1)S(1)}, u32[]{:S(2)}, u32[]{:S(2)}) collective-permute-start(bf16[64,1024]{1,0:T(8,128)(2,1)S(1)} %get-tuple-element.153), channel_id=1, source_target_pairs={{0,1},{1,0},{2,3},{3,2},{4,5},{5,4},{6,7},{7,6},{8,9},{9,8},{10,11... | collective-permute-start | bytes 393224 | tf_op jit(solution)/shard_map/ppermute | solution.py:474
  26.9 3.4 %copy-start.6 = (s32[1,512]{1,0:T(1,128)S(1)}, s32[1,512]{1,0:T(1,128)}, u32[]{:S(2)}) copy-start(s32[1,512]{1,0:T(1,128)} %param.13) | copy-start | bytes 6148
  26.9 7.4 %collective-permute-start.14 = (bf16[256,1024]{1,0:T(8,128)(2,1)S(1)}, bf16[256,1024]{1,0:T(8,128)(2,1)S(1)}, u32[]{:S(2)}, u32[]{:S(2)}) collective-permute-start(bf16[256,1024]{1,0:T(8,128)(2,1)S(1)} %copy-done.4), channel_id=1, source_target_pairs={{0,1},{1,0},{2,3},{3,2},{4,5},{5,4},{6,7},{7,6},{8,9},{9,8},{10,11... | collective-permute-start | bytes 1572872 | tf_op jit(solution)/shard_map/ppermute | solution.py:474
  26.9 3.4 %collective-permute-start.12 = (bf16[128,1024]{1,0:T(8,128)(2,1)S(1)}, bf16[128,1024]{1,0:T(8,128)(2,1)S(1)}, u32[]{:S(2)}, u32[]{:S(2)}) collective-permute-start(bf16[128,1024]{1,0:T(8,128)(2,1)S(1)} %collective-permute-done.9.refs_0_.refs_5_), channel_id=1, source_target_pairs={{0,1},{1,0},{2,3},{3,2},{4,5},{5,4},{6,7},{7,6},{8,9},{9,8},{10,11... | collective-permute-start | bytes 786440 | tf_op jit(solution)/shard_map/ppermute | solution.py:474
  27.4 8.2 %collective-permute-start.15 = (bf16[128,1024]{1,0:T(8,128)(2,1)S(1)}, bf16[128,1024]{1,0:T(8,128)(2,1)S(1)}, u32[]{:S(2)}, u32[]{:S(2)}) collective-permute-start(bf16[128,1024]{1,0:T(8,128)(2,1)S(1)} %bitcast.5), channel_id=1, source_target_pairs={{0,2},{1,3},{2,0},{3,1},{4,6},{5,7},{6,4},{7,5},{8,10},{9,11},{10,... | collective-permute-start | bytes 786440 | tf_op jit(solution)/shard_map/ppermute | solution.py:477
  32.9 11.2 %copy-start.2 = (bf16[512,1024]{1,0:T(8,128)(2,1)S(1)}, bf16[512,1024]{1,0:T(8,128)(2,1)}, u32[]{:S(2)}) copy-start(bf16[512,1024]{1,0:T(8,128)(2,1)} %w_a.3) | copy-start | bytes 3145732
  32.9 11.2 %copy-start.3 = (bf16[2,1024,512]{2,1,0:T(8,128)(2,1)S(1)}, bf16[2,1024,512]{2,1,0:T(8,128)(2,1)}, u32[]{:S(2)}) copy-start(bf16[2,1024,512]{2,1,0:T(8,128)(2,1)} %in_a.3) | copy-start | bytes 6291460
  32.9 1.4 %collective-permute-start.13 = (bf16[256,256]{1,0:T(8,128)(2,1)S(1)}, bf16[256,256]{1,0:T(8,128)(2,1)S(1)}, u32[]{:S(2)}, u32[]{:S(2)}) collective-permute-start(bf16[256,256]{1,0:T(8,128)(2,1)S(1)} %get-tuple-element.162), channel_id=1, source_target_pairs={{0,1},{1,0},{2,3},{3,2},{4,5},{5,4},{6,7},{7,6},{8,9},{9,8},{10,11... | collective-permute-start | bytes 393224 | tf_op jit(solution)/shard_map/ppermute | solution.py:474
  34.7 9.2 %collective-permute-start.17 = (bf16[128,1024]{1,0:T(8,128)(2,1)S(1)}, bf16[128,1024]{1,0:T(8,128)(2,1)S(1)}, u32[]{:S(2)}, u32[]{:S(2)}) collective-permute-start(bf16[128,1024]{1,0:T(8,128)(2,1)S(1)} %attn_out_far.1.part), channel_id=1, source_target_pairs={{0,2},{1,3},{2,0},{3,1},{4,6},{5,7},{6,4},{7,5},{8,10},{9,11},{10,... | collective-permute-start | bytes 786440 | tf_op jit(solution)/shard_map/ppermute | solution.py:477
  35.7 13.0 %collective-permute-start.16 = (bf16[128,1024]{1,0:T(8,128)(2,1)S(1)}, bf16[128,1024]{1,0:T(8,128)(2,1)S(1)}, u32[]{:S(2)}, u32[]{:S(2)}) collective-permute-start(bf16[128,1024]{1,0:T(8,128)(2,1)S(1)} %attn_out_own.1.part), channel_id=1, source_target_pairs={{0,2},{1,3},{2,0},{3,1},{4,6},{5,7},{6,4},{7,5},{8,10},{9,11},{10,... | collective-permute-start | bytes 786440 | tf_op jit(solution)/shard_map/ppermute | solution.py:477
  48.7 9.2 %collective-permute-start.19 = (bf16[128,1024]{1,0:T(8,128)(2,1)S(1)}, bf16[128,1024]{1,0:T(8,128)(2,1)S(1)}, u32[]{:S(2)}, u32[]{:S(2)}) collective-permute-start(bf16[128,1024]{1,0:T(8,128)(2,1)S(1)} %get-tuple-element.171.back), channel_id=1, source_target_pairs={{0,2},{1,3},{2,0},{3,1},{4,6},{5,7},{6,4},{7,5},{8,10},{9,11},{10,... | collective-permute-start | bytes 786440 | tf_op jit(solution)/shard_map/ppermute | solution.py:477
  52.3 9.6 %collective-permute-start.18 = (bf16[128,1024]{1,0:T(8,128)(2,1)S(1)}, bf16[128,1024]{1,0:T(8,128)(2,1)S(1)}, u32[]{:S(2)}, u32[]{:S(2)}) collective-permute-start(bf16[128,1024]{1,0:T(8,128)(2,1)S(1)} %get-tuple-element.176.back), channel_id=1, source_target_pairs={{0,2},{1,3},{2,0},{3,1},{4,6},{5,7},{6,4},{7,5},{8,10},{9,11},{10,... | collective-permute-start | bytes 786440 | tf_op jit(solution)/shard_map/ppermute | solution.py:477
  58.4 1.4 %collective-permute-start.20 = (bf16[64,1024]{1,0:T(8,128)(2,1)S(1)}, bf16[64,1024]{1,0:T(8,128)(2,1)S(1)}, u32[]{:S(2)}, u32[]{:S(2)}) collective-permute-start(bf16[64,1024]{1,0:T(8,128)(2,1)S(1)} %get-tuple-element.179), channel_id=1, source_target_pairs={{0,1},{1,0},{2,3},{3,2},{4,5},{5,4},{6,7},{7,6},{8,9},{9,8},{10,11... | collective-permute-start | bytes 393224 | tf_op jit(solution)/shard_map/ppermute | solution.py:474
  58.5 1.5 %collective-permute-start.21 = (bf16[64,1024]{1,0:T(8,128)(2,1)S(1)}, bf16[64,1024]{1,0:T(8,128)(2,1)S(1)}, u32[]{:S(2)}, u32[]{:S(2)}) collective-permute-start(bf16[64,1024]{1,0:T(8,128)(2,1)S(1)} %get-tuple-element.180), channel_id=1, source_target_pairs={{0,1},{1,0},{2,3},{3,2},{4,5},{5,4},{6,7},{7,6},{8,9},{9,8},{10,11... | collective-permute-start | bytes 393224 | tf_op jit(solution)/shard_map/ppermute | solution.py:474
  62.1 1.8 %collective-permute-start.22 = (bf16[128,1024]{1,0:T(8,128)(2,1)S(1)}, bf16[128,1024]{1,0:T(8,128)(2,1)S(1)}, u32[]{:S(2)}, u32[]{:S(2)}) collective-permute-start(bf16[128,1024]{1,0:T(8,128)(2,1)S(1)} %resid_back.1.first.d_resid), channel_id=1, source_target_pairs={{0,1},{1,0},{2,3},{3,2},{4,5},{5,4},{6,7},{7,6},{8,9},{9,8},{10,11... | collective-permute-start | bytes 786440 | tf_op jit(solution)/shard_map/ppermute | solution.py:474
  63.5 1.6 %collective-permute-start.23 = (bf16[128,1024]{1,0:T(8,128)(2,1)S(1)}, bf16[128,1024]{1,0:T(8,128)(2,1)S(1)}, u32[]{:S(2)}, u32[]{:S(2)}) collective-permute-start(bf16[128,1024]{1,0:T(8,128)(2,1)S(1)} %get-tuple-element.200), channel_id=1, source_target_pairs={{0,1},{1,0},{2,3},{3,2},{4,5},{5,4},{6,7},{7,6},{8,9},{9,8},{10,11... | collective-permute-start | bytes 786440 | tf_op jit(solution)/shard_map/ppermute | solution.py:474
  65.6 9.2 %collective-permute-start.27 = (bf16[128,1024]{1,0:T(8,128)(2,1)S(1)}, bf16[128,1024]{1,0:T(8,128)(2,1)S(1)}, u32[]{:S(2)}, u32[]{:S(2)}) collective-permute-start(bf16[128,1024]{1,0:T(8,128)(2,1)S(1)} %back_sum_far.1.part), channel_id=1, source_target_pairs={{0,2},{1,3},{2,0},{3,1},{4,6},{5,7},{6,4},{7,5},{8,10},{9,11},{10,... | collective-permute-start | bytes 786440 | tf_op jit(solution)/shard_map/ppermute | solution.py:477
  66.6 1.4 %collective-permute-start.24 = (bf16[64,1024]{1,0:T(8,128)(2,1)S(1)}, bf16[64,1024]{1,0:T(8,128)(2,1)S(1)}, u32[]{:S(2)}, u32[]{:S(2)}) collective-permute-start(bf16[64,1024]{1,0:T(8,128)(2,1)S(1)} %get-tuple-element.206), channel_id=1, source_target_pairs={{0,1},{1,0},{2,3},{3,2},{4,5},{5,4},{6,7},{7,6},{8,9},{9,8},{10,11... | collective-permute-start | bytes 393224 | tf_op jit(solution)/shard_map/ppermute | solution.py:474
  66.7 1.5 %collective-permute-start.25 = (bf16[64,1024]{1,0:T(8,128)(2,1)S(1)}, bf16[64,1024]{1,0:T(8,128)(2,1)S(1)}, u32[]{:S(2)}, u32[]{:S(2)}) collective-permute-start(bf16[64,1024]{1,0:T(8,128)(2,1)S(1)} %get-tuple-element.207), channel_id=1, source_target_pairs={{0,1},{1,0},{2,3},{3,2},{4,5},{5,4},{6,7},{7,6},{8,9},{9,8},{10,11... | collective-permute-start | bytes 393224 | tf_op jit(solution)/shard_map/ppermute | solution.py:474
  68.6 11.3 %collective-permute-start.26 = (bf16[128,1024]{1,0:T(8,128)(2,1)S(1)}, bf16[128,1024]{1,0:T(8,128)(2,1)S(1)}, u32[]{:S(2)}, u32[]{:S(2)}) collective-permute-start(bf16[128,1024]{1,0:T(8,128)(2,1)S(1)} %back_sum_own.1.part), channel_id=1, source_target_pairs={{0,2},{1,3},{2,0},{3,1},{4,6},{5,7},{6,4},{7,5},{8,10},{9,11},{10,... | collective-permute-start | bytes 786440 | tf_op jit(solution)/shard_map/ppermute | solution.py:477
  75.1 3.9 %collective-permute-start.28 = (bf16[64,1024]{1,0:T(8,128)(2,1)S(1)}, bf16[64,1024]{1,0:T(8,128)(2,1)S(1)}, u32[]{:S(2)}, u32[]{:S(2)}) collective-permute-start(bf16[64,1024]{1,0:T(8,128)(2,1)S(1)} %get-tuple-element.209), channel_id=1, source_target_pairs={{0,1},{1,0},{2,3},{3,2},{4,5},{5,4},{6,7},{7,6},{8,9},{9,8},{10,11... | collective-permute-start | bytes 393224 | tf_op jit(solution)/shard_map/ppermute | solution.py:474
  75.1 3.8 %collective-permute-start.29 = (bf16[64,1024]{1,0:T(8,128)(2,1)S(1)}, bf16[64,1024]{1,0:T(8,128)(2,1)S(1)}, u32[]{:S(2)}, u32[]{:S(2)}) collective-permute-start(bf16[64,1024]{1,0:T(8,128)(2,1)S(1)} %get-tuple-element.210), channel_id=1, source_target_pairs={{0,1},{1,0},{2,3},{3,2},{4,5},{5,4},{6,7},{7,6},{8,9},{9,8},{10,11... | collective-permute-start | bytes 393224 | tf_op jit(solution)/shard_map/ppermute | solution.py:474
  75.9 12.4 %collective-permute-start.38 = (bf16[96,1024]{1,0:T(8,128)(2,1)S(1)}, bf16[96,1024]{1,0:T(8,128)(2,1)S(1)}, u32[]{:S(2)}, u32[]{:S(2)}) collective-permute-start(bf16[96,1024]{1,0:T(8,128)(2,1)S(1)} %get-tuple-element.238), channel_id=1, source_target_pairs={{0,8},{4,12},{8,0},{12,4},{16,24},{20,28},{24,16},{28,20},{1,9},{5... | collective-permute-start | bytes 589832 | tf_op jit(solution)/shard_map/ppermute | solution.py:480
  80.2 1.3 %collective-permute-start.30 = (bf16[32,1024]{1,0:T(8,128)(2,1)S(1)}, bf16[32,1024]{1,0:T(8,128)(2,1)S(1)}, u32[]{:S(2)}, u32[]{:S(2)}) collective-permute-start(bf16[32,1024]{1,0:T(8,128)(2,1)S(1)} %get-tuple-element.219), channel_id=1, source_target_pairs={{0,1},{1,0},{2,3},{3,2},{4,5},{5,4},{6,7},{7,6},{8,9},{9,8},{10,11... | collective-permute-start | bytes 196616 | tf_op jit(solution)/shard_map/ppermute | solution.py:474
  80.3 1.4 %collective-permute-start.31 = (bf16[32,1024]{1,0:T(8,128)(2,1)S(1)}, bf16[32,1024]{1,0:T(8,128)(2,1)S(1)}, u32[]{:S(2)}, u32[]{:S(2)}) collective-permute-start(bf16[32,1024]{1,0:T(8,128)(2,1)S(1)} %get-tuple-element.220), channel_id=1, source_target_pairs={{0,1},{1,0},{2,3},{3,2},{4,5},{5,4},{6,7},{7,6},{8,9},{9,8},{10,11... | collective-permute-start | bytes 196616 | tf_op jit(solution)/shard_map/ppermute | solution.py:474
  80.8 1.3 %collective-permute-start.32 = (bf16[32,1024]{1,0:T(8,128)(2,1)S(1)}, bf16[32,1024]{1,0:T(8,128)(2,1)S(1)}, u32[]{:S(2)}, u32[]{:S(2)}) collective-permute-start(bf16[32,1024]{1,0:T(8,128)(2,1)S(1)} %get-tuple-element.221), channel_id=1, source_target_pairs={{0,1},{1,0},{2,3},{3,2},{4,5},{5,4},{6,7},{7,6},{8,9},{9,8},{10,11... | collective-permute-start | bytes 196616 | tf_op jit(solution)/shard_map/ppermute | solution.py:474
  80.9 1.3 %collective-permute-start.33 = (bf16[32,1024]{1,0:T(8,128)(2,1)S(1)}, bf16[32,1024]{1,0:T(8,128)(2,1)S(1)}, u32[]{:S(2)}, u32[]{:S(2)}) collective-permute-start(bf16[32,1024]{1,0:T(8,128)(2,1)S(1)} %get-tuple-element.222), channel_id=1, source_target_pairs={{0,1},{1,0},{2,3},{3,2},{4,5},{5,4},{6,7},{7,6},{8,9},{9,8},{10,11... | collective-permute-start | bytes 196616 | tf_op jit(solution)/shard_map/ppermute | solution.py:474
  83.5 9.2 %collective-permute-start.34 = (bf16[4,128,256]{2,1,0:T(8,128)(2,1)S(1)}, bf16[4,128,256]{2,1,0:T(8,128)(2,1)S(1)}, u32[]{:S(2)}, u32[]{:S(2)}) collective-permute-start(bf16[4,128,256]{2,1,0:T(8,128)(2,1)S(1)} %get-tuple-element.228), channel_id=1, source_target_pairs={{0,16},{4,20},{8,24},{12,28},{16,0},{20,4},{24,8},{28,12},{1,17},{... | collective-permute-start | bytes 786440 | tf_op jit(solution)/shard_map/ppermute | solution.py:480
  84.3 13.4 %collective-permute-start.37 = (bf16[4,128,256]{2,1,0:T(8,128)(2,1)S(1)}, bf16[4,128,256]{2,1,0:T(8,128)(2,1)S(1)}, u32[]{:S(2)}, u32[]{:S(2)}) collective-permute-start(bf16[4,128,256]{2,1,0:T(8,128)(2,1)S(1)} %get-tuple-element.235), channel_id=1, source_target_pairs={{0,16},{4,20},{8,24},{12,28},{16,0},{20,4},{24,8},{28,12},{1,17},{... | collective-permute-start | bytes 786440 | tf_op jit(solution)/shard_map/ppermute | solution.py:480
  88.3 6.7 %collective-permute-start.39 = (bf16[96,1024]{1,0:T(8,128)(2,1)S(1)}, bf16[96,1024]{1,0:T(8,128)(2,1)S(1)}, u32[]{:S(2)}, u32[]{:S(2)}) collective-permute-start(bf16[96,1024]{1,0:T(8,128)(2,1)S(1)} %back_pick.2), channel_id=1, source_target_pairs={{0,4},{4,0},{8,12},{12,8},{16,20},{20,16},{24,28},{28,24},{1,5},{5... | collective-permute-start | bytes 589832 | tf_op jit(solution)/shard_map/ppermute | solution.py:480
  89.4 17.1 %collective-permute-start.42 = (bf16[128,1024]{1,0:T(8,128)(2,1)S(1)}, bf16[128,1024]{1,0:T(8,128)(2,1)S(1)}, u32[]{:S(2)}, u32[]{:S(2)}) collective-permute-start(bf16[128,1024]{1,0:T(8,128)(2,1)S(1)} %ffn_out_far.1), channel_id=1, source_target_pairs={{0,2},{1,3},{2,0},{3,1},{4,6},{5,7},{6,4},{7,5},{8,10},{9,11},{10,... | collective-permute-start | bytes 786440 | tf_op jit(solution)/shard_map/ppermute | solution.py:477
  92.7 7.5 %collective-permute-start.35 = (bf16[2,128,256]{2,1,0:T(8,128)(2,1)S(1)}, bf16[2,128,256]{2,1,0:T(8,128)(2,1)S(1)}, u32[]{:S(2)}, u32[]{:S(2)}) collective-permute-start(bf16[2,128,256]{2,1,0:T(8,128)(2,1)S(1)} %get-tuple-element.230), channel_id=1, source_target_pairs={{0,4},{4,0},{8,12},{12,8},{16,20},{20,16},{24,28},{28,24},{1,5},{5... | collective-permute-start | bytes 393224 | tf_op jit(solution)/shard_map/ppermute | solution.py:480
  97.8 5.0 %collective-permute-start.40 = (bf16[2,128,256]{2,1,0:T(8,128)(2,1)S(1)}, bf16[2,128,256]{2,1,0:T(8,128)(2,1)S(1)}, u32[]{:S(2)}, u32[]{:S(2)}) collective-permute-start(bf16[2,128,256]{2,1,0:T(8,128)(2,1)S(1)} %get-tuple-element.241), channel_id=1, source_target_pairs={{0,4},{4,0},{8,12},{12,8},{16,20},{20,16},{24,28},{28,24},{1,5},{5... | collective-permute-start | bytes 393224 | tf_op jit(solution)/shard_map/ppermute | solution.py:480
  99.2 8.5 %collective-permute-start.43 = (bf16[96,1024]{1,0:T(8,128)(2,1)S(1)}, bf16[96,1024]{1,0:T(8,128)(2,1)S(1)}, u32[]{:S(2)}, u32[]{:S(2)}) collective-permute-start(bf16[96,1024]{1,0:T(8,128)(2,1)S(1)} %back_pick.3), channel_id=1, source_target_pairs={{0,16},{4,20},{8,24},{12,28},{16,0},{20,4},{24,8},{28,12},{1,17},{... | collective-permute-start | bytes 589832 | tf_op jit(solution)/shard_map/ppermute | solution.py:480
  100.3 7.4 %collective-permute-start.36 = (bf16[1,128,256]{2,1,0:T(8,128)(2,1)S(1)}, bf16[1,128,256]{2,1,0:T(8,128)(2,1)S(1)}, u32[]{:S(2)}, u32[]{:S(2)}) collective-permute-start(bf16[1,128,256]{2,1,0:T(8,128)(2,1)S(1)} %get-tuple-element.231), channel_id=1, source_target_pairs={{0,8},{4,12},{8,0},{12,4},{16,24},{20,28},{24,16},{28,20},{1,9},{5... | collective-permute-start | bytes 196616 | tf_op jit(solution)/shard_map/ppermute | solution.py:480
  102.9 5.9 %collective-permute-start.41 = (bf16[1,128,256]{2,1,0:T(8,128)(2,1)S(1)}, bf16[1,128,256]{2,1,0:T(8,128)(2,1)S(1)}, u32[]{:S(2)}, u32[]{:S(2)}) collective-permute-start(bf16[1,128,256]{2,1,0:T(8,128)(2,1)S(1)} %get-tuple-element.242), channel_id=1, source_target_pairs={{0,8},{4,12},{8,0},{12,4},{16,24},{20,28},{24,16},{28,20},{1,9},{5... | collective-permute-start | bytes 196616 | tf_op jit(solution)/shard_map/ppermute | solution.py:480

commit v15 on v14

--- a/solution.py
+++ b/solution.py
@@ -220,7 +220,7 @@
 
 def attend_first(
     docs, fourth, pre_c, act_c, proj_a, proj_c, enc, w_in,
-    pre_ref, act_ref, proj_ref, att_ref, give_ref, keep_ref, pre_all,
+    pre_ref, act_ref, proj_ref, att_ref, give_ref, pre_all,
 ):
     half = fourth.shape[0]
     cols = proj_a.shape[-1]
@@ -235,8 +235,17 @@
     encode(
         fourth[...], enc, w_in, pre_all, pre_ref.at[half : 2 * half], act_ref.at[half : 2 * half], store
     )
+    attend((1, 3), docs, proj_ref, att_ref, give_ref)
+
+
+def attend_second(docs, proj_ref, _att, att_ref, keep_ref):
+    attend((0, 2), docs, proj_ref, att_ref, keep_ref)
+
+
+def attend(blocks, docs, proj_ref, att_ref, target):
+    half, cols = proj_ref.shape[2:]
     masks = head_masks(cols)
-    for r, (target, place) in enumerate(((keep_ref, 1), (give_ref, 1), (keep_ref, 0), (give_ref, 0))):
+    for place, r in enumerate(blocks[::-1]):
         ahead, allowed, root_inv = window(docs, r, half)
         keys = jnp.concatenate([proj_ref[1, ahead], proj_ref[1, r]], axis=0)
         values = jnp.concatenate([proj_ref[2, ahead], proj_ref[2, r]], axis=0)
@@ -545,7 +554,7 @@
         [pltpu.VMEM((rows_dev, width), F32)],
         name="encode_third",
     )
-    pre_b, act_b, proj, attended, give, keep = run(
+    pre_b, act_b, proj, attended, give = run(
         attend_first,
         [
             like((pair, cols), F32),
@@ -553,13 +562,19 @@
             like((comps, tensors, rows_dev, cols), BF16),
             like((tensors, rows_dev, cols), F32),
             like((pair, cols), BF16),
-            like((pair, cols), BF16),
         ],
         [docs, mine_both, pre_c, act_c, proj_a, proj_c, enc_weight, attn_in],
         [pltpu.VMEM((rows_dev, width), F32)],
         name="attend_first",
     )
     take = near(give)
+    attended, keep = run(
+        attend_second,
+        [like((tensors, rows_dev, cols), F32), like((pair, cols), BF16)],
+        [docs, proj, attended],
+        name="attend_second",
+        aliases={2: 0},
+    )
 
 
     def out_part(index, name):

time: 110 us -> 109 us (level)
    pallas_call x35 -> x36, Pallas kernels: 26.6 us -> 26.7 us  [run(): pl.pallas_call(body, out_shape=list(outs), in_specs=[pl.BlockSpec(memory_...]
where the time goes in v15:
time: 109 us
  starting transfers between devices  43.4 us (40%)
  waiting for transfers between devices  36.3 us (33%)
  Pallas kernels  26.7 us (24%)
    ppermute x16, starting transfers between devices, crossed(): return lax.ppermute(value, group_axes, [(i, i ^ k) for i in range(groups)])  28.1 us
    pallas_call x36, Pallas kernels, run(): pl.pallas_call(body, out_shape=list(outs), in_specs=[pl.BlockSpec(memory_...  26.7 us
    ppermute x9, waiting for transfers between devices, far(): return lax.ppermute(value, 'tensor', [(i, i ^ 2) for i in range(tensors)])  18.6 us
    ppermute x16, waiting for transfers between devices, crossed(): return lax.ppermute(value, group_axes, [(i, i ^ k) for i in range(groups)])  12.8 us
    ppermute x9, starting transfers between devices, far(): return lax.ppermute(value, 'tensor', [(i, i ^ 2) for i in range(tensors)])  10.2 us
    ppermute x19, starting transfers between devices, near(): return lax.ppermute(value, 'tensor', [(i, i ^ 1) for i in range(tensors)])  5.11 us
    ppermute x19, waiting for transfers between devices, near(): return lax.ppermute(value, 'tensor', [(i, i ^ 1) for i in range(tensors)])  4.88 us
  transfers between devices with their start and end apart: 44, of which 26 were waited for; matrix products, arithmetic and copies ran while one was open for 1% of the time, Pallas kernels for 23%

profile of v15, /device:TPU:0, one launch (start us, length us, event | category | flops | bytes accessed | tf_op | source)
XLA Modules:
  0.0 109.0 jit_solution(9838225345738582664)
XLA Ops:
  0.6 0.5 collective-permute-start
  1.2 0.7 add_bitcast_fusion.code
  1.9 0.9 copy-done.7
  3.2 4.1 %collective-permute-start.2 = (bf16[24,1152]{1,0:T(8,128)(2,1)S(1)}, bf16[24,1152]{1,0:T(8,128)(2,1)S(1)}, u32[]{:S(2)}, u32[]{:S(2)}) collective-permute-start(bf16[24,1152]{1,0:T(8,128)(2,1)S(1)} %get-tuple-element.131), channel_id=1, source_target_pairs={{0,8},{4,12},{8,0},{12,4},{16,24},{20,28},{24,16},{28,20},{1,9},{5... | collective-permute-start | bytes 165896 | tf_op jit(solution)/shard_map/ppermute | solution.py:489
  7.3 1.3 %collective-permute-start.3 = (bf16[24,1152]{1,0:T(8,128)(2,1)S(1)}, bf16[24,1152]{1,0:T(8,128)(2,1)S(1)}, u32[]{:S(2)}, u32[]{:S(2)}) collective-permute-start(bf16[24,1152]{1,0:T(8,128)(2,1)S(1)} %get-tuple-element.132), channel_id=1, source_target_pairs={{0,24},{4,28},{8,16},{12,20},{16,8},{20,12},{24,0},{28,4},{1,25},{... | collective-permute-start | bytes 165896 | tf_op jit(solution)/shard_map/ppermute | solution.py:489
  8.6 2.0 %collective-permute-start.4 = (bf16[24,1152]{1,0:T(8,128)(2,1)S(1)}, bf16[24,1152]{1,0:T(8,128)(2,1)S(1)}, u32[]{:S(2)}, u32[]{:S(2)}) collective-permute-start(bf16[24,1152]{1,0:T(8,128)(2,1)S(1)} %get-tuple-element.139), channel_id=1, source_target_pairs={{0,20},{4,16},{8,28},{12,24},{16,4},{20,0},{24,12},{28,8},{1,21},{... | collective-permute-start | bytes 165896 | tf_op jit(solution)/shard_map/ppermute | solution.py:489
  10.5 2.5 %collective-permute-start.5 = (bf16[24,1152]{1,0:T(8,128)(2,1)S(1)}, bf16[24,1152]{1,0:T(8,128)(2,1)S(1)}, u32[]{:S(2)}, u32[]{:S(2)}) collective-permute-start(bf16[24,1152]{1,0:T(8,128)(2,1)S(1)} %get-tuple-element.140), channel_id=1, source_target_pairs={{0,12},{4,8},{8,4},{12,0},{16,28},{20,24},{24,20},{28,16},{1,13},{... | collective-permute-start | bytes 165896 | tf_op jit(solution)/shard_map/ppermute | solution.py:489
  13.0 1.9 %collective-permute-start.6 = (bf16[24,1152]{1,0:T(8,128)(2,1)S(1)}, bf16[24,1152]{1,0:T(8,128)(2,1)S(1)}, u32[]{:S(2)}, u32[]{:S(2)}) collective-permute-start(bf16[24,1152]{1,0:T(8,128)(2,1)S(1)} %get-tuple-element.141), channel_id=1, source_target_pairs={{0,28},{4,24},{8,20},{12,16},{16,12},{20,8},{24,4},{28,0},{1,29},{... | collective-permute-start | bytes 165896 | tf_op jit(solution)/shard_map/ppermute | solution.py:489
  14.9 1.0 collective-permute-start.8
  15.9 0.8 turn.1
  16.7 3.2 %collective-permute-done.6.refs_5_ = bf16[24,1152]{1,0:T(8,128)(2,1)S(1)} collective-permute-done((bf16[24,1152]{1,0:T(8,128)(2,1)S(1)}, bf16[24,1152]{1,0:T(8,128)(2,1)S(1)}, u32[]{:S(2)}, u32[]{:S(2)}) %collective-permute-start.6) | collective-permute-done | bytes 55328 | tf_op jit(solution)/shard_map/ppermute | solution.py:489
  20.2 1.6 %collective-permute-start.9 = (bf16[128,1024]{1,0:T(8,128)(2,1)S(1)}, bf16[128,1024]{1,0:T(8,128)(2,1)S(1)}, u32[]{:S(2)}, u32[]{:S(2)}) collective-permute-start(bf16[128,1024]{1,0:T(8,128)(2,1)S(1)} %get-tuple-element.152.refs_0_.refs_3_), channel_id=1, source_target_pairs={{0,2},{1,3},{2,0},{3,1},{4,6},{5,7},{6,4},{7,5},{8,10},{9,11},{10,... | collective-permute-start | bytes 786440 | tf_op jit(solution)/shard_map/ppermute | solution.py:486
  21.8 0.5 collective-permute-start.11
  22.3 0.8 collective-permute-done.10.refs_1_.refs_4_
  23.4 2.3 %encode_first.1 = (f32[256,256]{1,0:T(8,128)S(1)}, bf16[256,1024]{1,0:T(8,128)(2,1)S(1)}, bf16[128,1024]{1,0:T(8,128)(2,1)S(1)}, bf16[4,2,128,256]{3,2,1,0:T(8,128)(2,1)S(1)}) custom-call(bf16[128,1024]{1,0:T(8,128)(2,1)S(1)} %get-tuple-element.152.refs_0_.refs_3_, bf16[64,1024]{1,0:T(8,128)(2,1)S(1)} %collective-permute-done.10.refs_1_.refs_4_, ...), custom_call_target="tpu_custom_call" | custom-call | tf_op jit(solution)/shard_map/encode_first/pallas_call | solution.py:64
  25.6 1.3 %collective-permute-done.9.refs_0_.refs_5_ = bf16[128,1024]{1,0:T(8,128)(2,1)S(1)} collective-permute-done((bf16[128,1024]{1,0:T(8,128)(2,1)S(1)}, bf16[128,1024]{1,0:T(8,128)(2,1)S(1)}, u32[]{:S(2)}, u32[]{:S(2)}) %collective-permute-start.9) | collective-permute-done | bytes 262176 | tf_op jit(solution)/shard_map/ppermute | solution.py:486
  26.9 0.5 collective-permute-start.12
  27.4 1.5 %collective-permute-start.15 = (bf16[128,1024]{1,0:T(8,128)(2,1)S(1)}, bf16[128,1024]{1,0:T(8,128)(2,1)S(1)}, u32[]{:S(2)}, u32[]{:S(2)}) collective-permute-start(bf16[128,1024]{1,0:T(8,128)(2,1)S(1)} %bitcast.5), channel_id=1, source_target_pairs={{0,2},{1,3},{2,0},{3,1},{4,6},{5,7},{6,4},{7,5},{8,10},{9,11},{10,... | collective-permute-start | bytes 786440 | tf_op jit(solution)/shard_map/ppermute | solution.py:486
  29.0 1.4 %encode_third.1 = (f32[128,256]{1,0:T(8,128)S(1)}, bf16[128,1024]{1,0:T(8,128)(2,1)S(1)}, bf16[128,1024]{1,0:T(8,128)(2,1)S(1)}, bf16[4,1,128,256]{3,2,1,0:T(8,128)(2,1)S(1)}) custom-call(bf16[128,1024]{1,0:T(8,128)(2,1)S(1)} %collective-permute-done.9.refs_0_.refs_5_, bf16[2,1024,1024]{2,1,0:T(8,128)(2,1)S(1)} %copy-done, bf16[4,1024,256]{2,1,0:T(8,128)(2,1)S(1)} %copy-done.1), custom_call_target="tpu_custom_call" | custom-call | tf_op jit(solution)/shard_map/encode_third/pallas_call | solution.py:64
  30.4 2.1 %attend_first.1 = (f32[256,256]{1,0:T(8,128)S(1)}, bf16[256,1024]{1,0:T(8,128)(2,1)S(1)}, bf16[4,4,128,256]{3,2,1,0:T(8,128)(2,1)S(1)}, f32[4,128,256]{2,1,0:T(8,128)S(1)}, bf16[256,256]{1,0:T(8,128)(2,1)S(1)}) custom-call(s32[4,1,128]{2,1,0:T(1,128)S(1)} %bitcast.8, bf16[128,1024]{1,0:T(8,128)(2,1)S(1)} %collective-permute-done.12.fourth.refs_6_, ...), custom_call_target="tpu_custom_call" | custom-call | tf_op jit(solution)/shard_map/attend_first/pallas_call | solution.py:64
  32.6 0.7 attend_second.1
  33.4 0.6 collective-permute-done.13.take
  34.3 0.6 collective-permute-start.17
  35.1 0.5 collective-permute-done.15.d_out_ref.d_out
  35.7 1.5 %collective-permute-start.16 = (bf16[128,1024]{1,0:T(8,128)(2,1)S(1)}, bf16[128,1024]{1,0:T(8,128)(2,1)S(1)}, u32[]{:S(2)}, u32[]{:S(2)}) collective-permute-start(bf16[128,1024]{1,0:T(8,128)(2,1)S(1)} %attn_out_own.1.part), channel_id=1, source_target_pairs={{0,2},{1,3},{2,0},{3,1},{4,6},{5,7},{6,4},{7,5},{8,10},{9,11},{10,... | collective-permute-start | bytes 786440 | tf_op jit(solution)/shard_map/ppermute | solution.py:486
  37.2 6.3 %collective-permute-done.17.got = bf16[128,1024]{1,0:T(8,128)(2,1)S(1)} collective-permute-done((bf16[128,1024]{1,0:T(8,128)(2,1)S(1)}, bf16[128,1024]{1,0:T(8,128)(2,1)S(1)}, u32[]{:S(2)}, u32[]{:S(2)}) %collective-permute-start.17) | collective-permute-done | bytes 262176 | tf_op jit(solution)/shard_map/ppermute | solution.py:486
  43.7 2.9 %ffn_own.1 = (bf16[128,1024]{1,0:T(8,128)(2,1)S(1)}, bf16[128,1024]{1,0:T(8,128)(2,1)S(1)}) custom-call(bf16[128,1024]{1,0:T(8,128)(2,1)S(1)} %get-tuple-element.170.rows_ref, bf16[128,1024]{1,0:T(8,128)(2,1)S(1)} %bitcast.6, bf16[2,1024,512]{2,1,0:T(8,128)(2,1)S(1)} %copy-done.3, bf16[2,1024,512]{2,1,0:T(8,128)(2,1)S(1)} %collective-permute-done.in_b, ...), custom_call_target="tpu_custom_call" | custom-call | tf_op jit(solution)/shard_map/ffn_own/pallas_call | solution.py:64
  46.6 1.7 %collective-permute-done.16.got = bf16[128,1024]{1,0:T(8,128)(2,1)S(1)} collective-permute-done((bf16[128,1024]{1,0:T(8,128)(2,1)S(1)}, bf16[128,1024]{1,0:T(8,128)(2,1)S(1)}, u32[]{:S(2)}, u32[]{:S(2)}) %collective-permute-start.16) | collective-permute-done | bytes 262176 | tf_op jit(solution)/shard_map/ppermute | solution.py:486
  48.3 0.5 collective-permute-start.19
  49.0 2.9 %ffn_far.1 = (bf16[128,1024]{1,0:T(8,128)(2,1)S(1)}, bf16[128,1024]{1,0:T(8,128)(2,1)S(1)}) custom-call(bf16[128,1024]{1,0:T(8,128)(2,1)S(1)} %get-tuple-element.177.rows_ref, bf16[128,1024]{1,0:T(8,128)(2,1)S(1)} %collective-permute-done.15.d_out_ref.d_out, bf16[2,1024,512]{2,1,0:T(8,128)(2,1)S(1)} %copy-done.3, ...), custom_call_target="tpu_custom_call" | custom-call | tf_op jit(solution)/shard_map/ffn_far/pallas_call | solution.py:64
  51.9 1.8 %collective-permute-start.18 = (bf16[128,1024]{1,0:T(8,128)(2,1)S(1)}, bf16[128,1024]{1,0:T(8,128)(2,1)S(1)}, u32[]{:S(2)}, u32[]{:S(2)}) collective-permute-start(bf16[128,1024]{1,0:T(8,128)(2,1)S(1)} %get-tuple-element.179.back), channel_id=1, source_target_pairs={{0,2},{1,3},{2,0},{3,1},{4,6},{5,7},{6,4},{7,5},{8,10},{9,11},{10,... | collective-permute-start | bytes 786440 | tf_op jit(solution)/shard_map/ppermute | solution.py:486
  53.7 3.9 %collective-permute-done.19.got = bf16[128,1024]{1,0:T(8,128)(2,1)S(1)} collective-permute-done((bf16[128,1024]{1,0:T(8,128)(2,1)S(1)}, bf16[128,1024]{1,0:T(8,128)(2,1)S(1)}, u32[]{:S(2)}, u32[]{:S(2)}) %collective-permute-start.19) | collective-permute-done | bytes 262176 | tf_op jit(solution)/shard_map/ppermute | solution.py:486
  57.9 0.5 collective-permute-start.21
  58.4 0.8 collective-permute-done.20.fourth_a
  59.4 1.6 %attn_back_first.1 = (bf16[4,128,256]{2,1,0:T(8,128)(2,1)S(1)}, f32[4,128,256]{2,1,0:T(8,128)S(1)}, f32[4,128,256]{2,1,0:T(8,128)S(1)}, bf16[4,128,256]{2,1,0:T(8,128)(2,1)S(1)}) custom-call(s32[4,1,128]{2,1,0:T(1,128)S(1)} %bitcast.10, bf16[128,1024]{1,0:T(8,128)(2,1)S(1)} %get-tuple-element.181.third.d_resid, ...), custom_call_target="tpu_custom_call" | custom-call | tf_op jit(solution)/shard_map/attn_back_first/pallas_call | solution.py:64
  61.8 1.2 %attn_back_own.1 = (bf16[128,1024]{1,0:T(8,128)(2,1)S(1)}, bf16[4,128,256]{2,1,0:T(8,128)(2,1)S(1)}, f32[4,128,256]{2,1,0:T(8,128)S(1)}, f32[4,128,256]{2,1,0:T(8,128)S(1)}, bf16[4,128,256]{2,1,0:T(8,128)(2,1)S(1)}) custom-call(s32[4,1,128]{2,1,0:T(1,128)S(1)} %bitcast.11, ...), custom_call_target="tpu_custom_call", output_to_operand_aliasing={{1}: (5, {}), {2}: (6, {}), {3}: (7, {}), {4}: (8, {})} | custom-call | tf_op jit(solution)/shard_map/attn_back_own/pallas_call | solution.py:64
  63.0 0.6 collective-permute-start.23
  63.5 0.8 attn_back_second.1
  65.2 0.6 collective-permute-start.27
  66.8 0.8 collective-permute-done.24.refs_0_
  68.2 1.6 %collective-permute-start.26 = (bf16[128,1024]{1,0:T(8,128)(2,1)S(1)}, bf16[128,1024]{1,0:T(8,128)(2,1)S(1)}, u32[]{:S(2)}, u32[]{:S(2)}) collective-permute-start(bf16[128,1024]{1,0:T(8,128)(2,1)S(1)} %back_sum_own.1.part), channel_id=1, source_target_pairs={{0,2},{1,3},{2,0},{3,1},{4,6},{5,7},{6,4},{7,5},{8,10},{9,11},{10,... | collective-permute-start | bytes 786440 | tf_op jit(solution)/shard_map/ppermute | solution.py:486
  69.8 4.5 %collective-permute-done.27.got = bf16[128,1024]{1,0:T(8,128)(2,1)S(1)} collective-permute-done((bf16[128,1024]{1,0:T(8,128)(2,1)S(1)}, bf16[128,1024]{1,0:T(8,128)(2,1)S(1)}, u32[]{:S(2)}, u32[]{:S(2)}) %collective-permute-start.27) | collective-permute-done | bytes 262176 | tf_op jit(solution)/shard_map/ppermute | solution.py:486
  74.7 0.5 collective-permute-start.29
  75.5 3.0 %collective-permute-start.38 = (bf16[96,1024]{1,0:T(8,128)(2,1)S(1)}, bf16[96,1024]{1,0:T(8,128)(2,1)S(1)}, u32[]{:S(2)}, u32[]{:S(2)}) collective-permute-start(bf16[96,1024]{1,0:T(8,128)(2,1)S(1)} %get-tuple-element.240), channel_id=1, source_target_pairs={{0,8},{4,12},{8,0},{12,4},{16,24},{20,28},{24,16},{28,20},{1,9},{5... | collective-permute-start | bytes 589832 | tf_op jit(solution)/shard_map/ppermute | solution.py:489
  78.5 1.0 enc_grads_first.1
  79.9 0.5 collective-permute-start.31
  81.8 1.3 %enc_grads_second.1 = (f32[4,128,256]{2,1,0:T(8,128)S(1)}, bf16[4,128,256]{2,1,0:T(8,128)(2,1)S(1)}, f32[4,128,256]{2,1,0:T(8,128)S(1)}, bf16[4,128,256]{2,1,0:T(8,128)(2,1)S(1)}) custom-call(bf16[128,1024]{1,0:T(8,128)(2,1)S(1)} %get-tuple-element.220.refs_0_, bf16[32,1024]{1,0:T(8,128)(2,1)S(1)} %collective-permute-done.30.refs_1_, ...), custom_call_target="tpu_custom_call" | custom-call | tf_op jit(solution)/shard_map/enc_grads_second/pallas_call | solution.py:64
  83.1 0.8 collective-permute-start.34
  83.9 1.3 %collective-permute-start.37 = (bf16[4,128,256]{2,1,0:T(8,128)(2,1)S(1)}, bf16[4,128,256]{2,1,0:T(8,128)(2,1)S(1)}, u32[]{:S(2)}, u32[]{:S(2)}) collective-permute-start(bf16[4,128,256]{2,1,0:T(8,128)(2,1)S(1)} %get-tuple-element.237), channel_id=1, source_target_pairs={{0,16},{4,20},{8,24},{12,28},{16,0},{20,4},{24,8},{28,12},{1,17},{... | collective-permute-start | bytes 786440 | tf_op jit(solution)/shard_map/ppermute | solution.py:489
  85.2 2.7 %collective-permute-done.38.refs_1_ = bf16[96,1024]{1,0:T(8,128)(2,1)S(1)} collective-permute-done((bf16[96,1024]{1,0:T(8,128)(2,1)S(1)}, bf16[96,1024]{1,0:T(8,128)(2,1)S(1)}, u32[]{:S(2)}, u32[]{:S(2)}) %collective-permute-start.38) | collective-permute-done | bytes 196640 | tf_op jit(solution)/shard_map/ppermute | solution.py:489
  87.9 0.6 collective-permute-start.39
  88.5 0.5 ffn_out_far.1
  89.0 0.6 collective-permute-start.42
  89.6 2.7 %collective-permute-done.34.got = bf16[4,128,256]{2,1,0:T(8,128)(2,1)S(1)} collective-permute-done((bf16[4,128,256]{2,1,0:T(8,128)(2,1)S(1)}, bf16[4,128,256]{2,1,0:T(8,128)(2,1)S(1)}, u32[]{:S(2)}, u32[]{:S(2)}) %collective-permute-start.34) | collective-permute-done | bytes 262176 | tf_op jit(solution)/shard_map/ppermute | solution.py:489
  92.3 1.4 %collective-permute-start.35 = (bf16[2,128,256]{2,1,0:T(8,128)(2,1)S(1)}, bf16[2,128,256]{2,1,0:T(8,128)(2,1)S(1)}, u32[]{:S(2)}, u32[]{:S(2)}) collective-permute-start(bf16[2,128,256]{2,1,0:T(8,128)(2,1)S(1)} %get-tuple-element.232), channel_id=1, source_target_pairs={{0,4},{4,0},{8,12},{12,8},{16,20},{20,16},{24,28},{28,24},{1,5},{5... | collective-permute-start | bytes 393224 | tf_op jit(solution)/shard_map/ppermute | solution.py:489
  93.7 0.9 collective-permute-done.39.refs_2_
  94.6 2.7 %collective-permute-done.37.got = bf16[4,128,256]{2,1,0:T(8,128)(2,1)S(1)} collective-permute-done((bf16[4,128,256]{2,1,0:T(8,128)(2,1)S(1)}, bf16[4,128,256]{2,1,0:T(8,128)(2,1)S(1)}, u32[]{:S(2)}, u32[]{:S(2)}) %collective-permute-start.37) | collective-permute-done | bytes 262176 | tf_op jit(solution)/shard_map/ppermute | solution.py:489
  97.4 1.4 %collective-permute-start.40 = (bf16[2,128,256]{2,1,0:T(8,128)(2,1)S(1)}, bf16[2,128,256]{2,1,0:T(8,128)(2,1)S(1)}, u32[]{:S(2)}, u32[]{:S(2)}) collective-permute-start(bf16[2,128,256]{2,1,0:T(8,128)(2,1)S(1)} %get-tuple-element.243), channel_id=1, source_target_pairs={{0,4},{4,0},{8,12},{12,8},{16,20},{20,16},{24,28},{28,24},{1,5},{5... | collective-permute-start | bytes 393224 | tf_op jit(solution)/shard_map/ppermute | solution.py:489
  98.8 1.1 collective-permute-start.43
  99.9 2.2 %collective-permute-start.36 = (bf16[1,128,256]{2,1,0:T(8,128)(2,1)S(1)}, bf16[1,128,256]{2,1,0:T(8,128)(2,1)S(1)}, u32[]{:S(2)}, u32[]{:S(2)}) collective-permute-start(bf16[1,128,256]{2,1,0:T(8,128)(2,1)S(1)} %get-tuple-element.233), channel_id=1, source_target_pairs={{0,8},{4,12},{8,0},{12,4},{16,24},{20,28},{24,16},{28,20},{1,9},{5... | collective-permute-start | bytes 196616 | tf_op jit(solution)/shard_map/ppermute | solution.py:489
  102.4 3.6 %collective-permute-start.41 = (bf16[1,128,256]{2,1,0:T(8,128)(2,1)S(1)}, bf16[1,128,256]{2,1,0:T(8,128)(2,1)S(1)}, u32[]{:S(2)}, u32[]{:S(2)}) collective-permute-start(bf16[1,128,256]{2,1,0:T(8,128)(2,1)S(1)} %get-tuple-element.244), channel_id=1, source_target_pairs={{0,8},{4,12},{8,0},{12,4},{16,24},{20,28},{24,16},{28,20},{1,9},{5... | collective-permute-start | bytes 196616 | tf_op jit(solution)/shard_map/ppermute | solution.py:489
  106.1 1.2 %ffn_out_own.1 = bf16[128,1024]{1,0:T(8,128)(2,1)} custom-call(bf16[128,1024]{1,0:T(8,128)(2,1)S(1)} %get-tuple-element.245.hidden, bf16[512,1024]{1,0:T(8,128)(2,1)S(1)} %copy-done.2, bf16[512,1024]{1,0:T(8,128)(2,1)S(1)} %collective-permute-done.1.out_b.w_b, bf16[128,1024]{1,0:T(8,128)(2,1)S(1)} %get-tuple-element.188.resid, ...), custom_call_target="tpu_custom_call" | custom-call | tf_op jit(solution)/shard_map/ffn_out_own/pallas_call | solution.py:64
  107.2 1.0 back_recv.1
  108.3 0.7 finish.1
  (77 shorter events, 8.8 us)
Async XLA Ops:
  0.6 7.9 %collective-permute-start = (bf16[2,1024,512]{2,1,0:T(8,128)(2,1)}, bf16[2,1024,512]{2,1,0:T(8,128)(2,1)S(1)}, u32[]{:S(2)}, u32[]{:S(2)}) collective-permute-start(bf16[2,1024,512]{2,1,0:T(8,128)(2,1)} %in_a.3), channel_id=1, source_target_pairs={{0,1},{1,0},{2,3},{3,2},{4,5},{5,4},{6,7},{7,6},{8,9},{9,8},{10,11... | collective-permute-start | bytes 6291464 | tf_op jit(solution)/shard_map/ppermute | solution.py:483
  1.1 7.4 %collective-permute-start.1 = (bf16[512,1024]{1,0:T(8,128)(2,1)}, bf16[512,1024]{1,0:T(8,128)(2,1)S(1)}, u32[]{:S(2)}, u32[]{:S(2)}) collective-permute-start(bf16[512,1024]{1,0:T(8,128)(2,1)} %w_a.3), channel_id=1, source_target_pairs={{0,1},{1,0},{2,3},{3,2},{4,5},{5,4},{6,7},{7,6},{8,9},{9,8},{10,11... | collective-permute-start | bytes 3145736 | tf_op jit(solution)/shard_map/ppermute | solution.py:483
  1.9 0.9 copy-start.7
  2.9 13.0 %copy-start.1 = (bf16[4,1024,256]{2,1,0:T(8,128)(2,1)S(1)}, bf16[4,1024,256]{2,1,0:T(8,128)(2,1)}, u32[]{:S(2)}) copy-start(bf16[4,1024,256]{2,1,0:T(8,128)(2,1)} %w_in.1) | copy-start | bytes 6291460
  2.9 13.0 %copy-start.4 = (bf16[256,1024]{1,0:T(8,128)(2,1)S(1)}, bf16[256,1024]{1,0:T(8,128)(2,1)}, u32[]{:S(2)}) copy-start(bf16[256,1024]{1,0:T(8,128)(2,1)} %w_own.3) | copy-start | bytes 1572868
  2.9 20.5 %copy-start = (bf16[2,1024,1024]{2,1,0:T(8,128)(2,1)S(1)}, bf16[2,1024,1024]{2,1,0:T(8,128)(2,1)}, u32[]{:S(2)}) copy-start(bf16[2,1024,1024]{2,1,0:T(8,128)(2,1)} %refs_9_.1) | copy-start | bytes 12582916
  3.2 11.7 %collective-permute-start.2 = (bf16[24,1152]{1,0:T(8,128)(2,1)S(1)}, bf16[24,1152]{1,0:T(8,128)(2,1)S(1)}, u32[]{:S(2)}, u32[]{:S(2)}) collective-permute-start(bf16[24,1152]{1,0:T(8,128)(2,1)S(1)} %get-tuple-element.131), channel_id=1, source_target_pairs={{0,8},{4,12},{8,0},{12,4},{16,24},{20,28},{24,16},{28,20},{1,9},{5... | collective-permute-start | bytes 165896 | tf_op jit(solution)/shard_map/ppermute | solution.py:489
  7.3 7.6 %collective-permute-start.3 = (bf16[24,1152]{1,0:T(8,128)(2,1)S(1)}, bf16[24,1152]{1,0:T(8,128)(2,1)S(1)}, u32[]{:S(2)}, u32[]{:S(2)}) collective-permute-start(bf16[24,1152]{1,0:T(8,128)(2,1)S(1)} %get-tuple-element.132), channel_id=1, source_target_pairs={{0,24},{4,28},{8,16},{12,20},{16,8},{20,12},{24,0},{28,4},{1,25},{... | collective-permute-start | bytes 165896 | tf_op jit(solution)/shard_map/ppermute | solution.py:489
  8.6 8.1 %collective-permute-start.4 = (bf16[24,1152]{1,0:T(8,128)(2,1)S(1)}, bf16[24,1152]{1,0:T(8,128)(2,1)S(1)}, u32[]{:S(2)}, u32[]{:S(2)}) collective-permute-start(bf16[24,1152]{1,0:T(8,128)(2,1)S(1)} %get-tuple-element.139), channel_id=1, source_target_pairs={{0,20},{4,16},{8,28},{12,24},{16,4},{20,0},{24,12},{28,8},{1,21},{... | collective-permute-start | bytes 165896 | tf_op jit(solution)/shard_map/ppermute | solution.py:489
  10.5 6.2 %collective-permute-start.5 = (bf16[24,1152]{1,0:T(8,128)(2,1)S(1)}, bf16[24,1152]{1,0:T(8,128)(2,1)S(1)}, u32[]{:S(2)}, u32[]{:S(2)}) collective-permute-start(bf16[24,1152]{1,0:T(8,128)(2,1)S(1)} %get-tuple-element.140), channel_id=1, source_target_pairs={{0,12},{4,8},{8,4},{12,0},{16,28},{20,24},{24,20},{28,16},{1,13},{... | collective-permute-start | bytes 165896 | tf_op jit(solution)/shard_map/ppermute | solution.py:489
  13.0 7.0 %collective-permute-start.6 = (bf16[24,1152]{1,0:T(8,128)(2,1)S(1)}, bf16[24,1152]{1,0:T(8,128)(2,1)S(1)}, u32[]{:S(2)}, u32[]{:S(2)}) collective-permute-start(bf16[24,1152]{1,0:T(8,128)(2,1)S(1)} %get-tuple-element.141), channel_id=1, source_target_pairs={{0,28},{4,24},{8,20},{12,16},{16,12},{20,8},{24,4},{28,0},{1,29},{... | collective-permute-start | bytes 165896 | tf_op jit(solution)/shard_map/ppermute | solution.py:489
  14.9 5.1 %collective-permute-start.7 = (bf16[24,1152]{1,0:T(8,128)(2,1)S(1)}, bf16[24,1152]{1,0:T(8,128)(2,1)S(1)}, u32[]{:S(2)}, u32[]{:S(2)}) collective-permute-start(bf16[24,1152]{1,0:T(8,128)(2,1)S(1)} %get-tuple-element.142), channel_id=1, source_target_pairs={{0,4},{4,0},{8,12},{12,8},{16,20},{20,16},{24,28},{28,24},{1,5},{5... | collective-permute-start | bytes 165896 | tf_op jit(solution)/shard_map/ppermute | solution.py:489
  14.9 5.1 %collective-permute-start.8 = (bf16[24,1152]{1,0:T(8,128)(2,1)S(1)}, bf16[24,1152]{1,0:T(8,128)(2,1)S(1)}, u32[]{:S(2)}, u32[]{:S(2)}) collective-permute-start(bf16[24,1152]{1,0:T(8,128)(2,1)S(1)} %get-tuple-element.143), channel_id=1, source_target_pairs={{0,16},{4,20},{8,24},{12,28},{16,0},{20,4},{24,8},{28,12},{1,17},{... | collective-permute-start | bytes 165896 | tf_op jit(solution)/shard_map/ppermute | solution.py:489
  20.2 6.7 %collective-permute-start.9 = (bf16[128,1024]{1,0:T(8,128)(2,1)S(1)}, bf16[128,1024]{1,0:T(8,128)(2,1)S(1)}, u32[]{:S(2)}, u32[]{:S(2)}) collective-permute-start(bf16[128,1024]{1,0:T(8,128)(2,1)S(1)} %get-tuple-element.152.refs_0_.refs_3_), channel_id=1, source_target_pairs={{0,2},{1,3},{2,0},{3,1},{4,6},{5,7},{6,4},{7,5},{8,10},{9,11},{10,... | collective-permute-start | bytes 786440 | tf_op jit(solution)/shard_map/ppermute | solution.py:486
  21.8 1.3 %collective-permute-start.10 = (bf16[64,1024]{1,0:T(8,128)(2,1)S(1)}, bf16[64,1024]{1,0:T(8,128)(2,1)S(1)}, u32[]{:S(2)}, u32[]{:S(2)}) collective-permute-start(bf16[64,1024]{1,0:T(8,128)(2,1)S(1)} %get-tuple-element.153), channel_id=1, source_target_pairs={{0,1},{1,0},{2,3},{3,2},{4,5},{5,4},{6,7},{7,6},{8,9},{9,8},{10,11... | collective-permute-start | bytes 393224 | tf_op jit(solution)/shard_map/ppermute | solution.py:483
  21.8 5.6 %copy-start.5 = (bf16[1,128,1024]{2,1,0:T(8,128)(2,1)S(1)}, bf16[1,128,1024]{2,1,0:T(8,128)(2,1)}, u32[]{:S(2)}) copy-start(bf16[1,128,1024]{2,1,0:T(8,128)(2,1)} %param.19) | copy-start | bytes 786436
  21.8 1.5 %collective-permute-start.11 = (bf16[64,1024]{1,0:T(8,128)(2,1)S(1)}, bf16[64,1024]{1,0:T(8,128)(2,1)S(1)}, u32[]{:S(2)}, u32[]{:S(2)}) collective-permute-start(bf16[64,1024]{1,0:T(8,128)(2,1)S(1)} %get-tuple-element.154), channel_id=1, source_target_pairs={{0,1},{1,0},{2,3},{3,2},{4,5},{5,4},{6,7},{7,6},{8,9},{9,8},{10,11... | collective-permute-start | bytes 393224 | tf_op jit(solution)/shard_map/ppermute | solution.py:483
  26.9 3.4 %copy-start.6 = (s32[1,512]{1,0:T(1,128)S(1)}, s32[1,512]{1,0:T(1,128)}, u32[]{:S(2)}) copy-start(s32[1,512]{1,0:T(1,128)} %param.13) | copy-start | bytes 6148
  26.9 7.0 %collective-permute-start.14 = (bf16[256,1024]{1,0:T(8,128)(2,1)S(1)}, bf16[256,1024]{1,0:T(8,128)(2,1)S(1)}, u32[]{:S(2)}, u32[]{:S(2)}) collective-permute-start(bf16[256,1024]{1,0:T(8,128)(2,1)S(1)} %copy-done.4), channel_id=1, source_target_pairs={{0,1},{1,0},{2,3},{3,2},{4,5},{5,4},{6,7},{7,6},{8,9},{9,8},{10,11... | collective-permute-start | bytes 1572872 | tf_op jit(solution)/shard_map/ppermute | solution.py:483
  26.9 3.4 %collective-permute-start.12 = (bf16[128,1024]{1,0:T(8,128)(2,1)S(1)}, bf16[128,1024]{1,0:T(8,128)(2,1)S(1)}, u32[]{:S(2)}, u32[]{:S(2)}) collective-permute-start(bf16[128,1024]{1,0:T(8,128)(2,1)S(1)} %collective-permute-done.9.refs_0_.refs_5_), channel_id=1, source_target_pairs={{0,1},{1,0},{2,3},{3,2},{4,5},{5,4},{6,7},{7,6},{8,9},{9,8},{10,11... | collective-permute-start | bytes 786440 | tf_op jit(solution)/shard_map/ppermute | solution.py:483
  27.4 8.2 %collective-permute-start.15 = (bf16[128,1024]{1,0:T(8,128)(2,1)S(1)}, bf16[128,1024]{1,0:T(8,128)(2,1)S(1)}, u32[]{:S(2)}, u32[]{:S(2)}) collective-permute-start(bf16[128,1024]{1,0:T(8,128)(2,1)S(1)} %bitcast.5), channel_id=1, source_target_pairs={{0,2},{1,3},{2,0},{3,1},{4,6},{5,7},{6,4},{7,5},{8,10},{9,11},{10,... | collective-permute-start | bytes 786440 | tf_op jit(solution)/shard_map/ppermute | solution.py:486
  32.5 1.4 %collective-permute-start.13 = (bf16[256,256]{1,0:T(8,128)(2,1)S(1)}, bf16[256,256]{1,0:T(8,128)(2,1)S(1)}, u32[]{:S(2)}, u32[]{:S(2)}) collective-permute-start(bf16[256,256]{1,0:T(8,128)(2,1)S(1)} %get-tuple-element.165), channel_id=1, source_target_pairs={{0,1},{1,0},{2,3},{3,2},{4,5},{5,4},{6,7},{7,6},{8,9},{9,8},{10,11... | collective-permute-start | bytes 393224 | tf_op jit(solution)/shard_map/ppermute | solution.py:483
  33.3 10.4 %copy-start.2 = (bf16[512,1024]{1,0:T(8,128)(2,1)S(1)}, bf16[512,1024]{1,0:T(8,128)(2,1)}, u32[]{:S(2)}) copy-start(bf16[512,1024]{1,0:T(8,128)(2,1)} %w_a.3) | copy-start | bytes 3145732
  33.3 10.4 %copy-start.3 = (bf16[2,1024,512]{2,1,0:T(8,128)(2,1)S(1)}, bf16[2,1024,512]{2,1,0:T(8,128)(2,1)}, u32[]{:S(2)}) copy-start(bf16[2,1024,512]{2,1,0:T(8,128)(2,1)} %in_a.3) | copy-start | bytes 6291460
  34.3 9.2 %collective-permute-start.17 = (bf16[128,1024]{1,0:T(8,128)(2,1)S(1)}, bf16[128,1024]{1,0:T(8,128)(2,1)S(1)}, u32[]{:S(2)}, u32[]{:S(2)}) collective-permute-start(bf16[128,1024]{1,0:T(8,128)(2,1)S(1)} %attn_out_far.1.part), channel_id=1, source_target_pairs={{0,2},{1,3},{2,0},{3,1},{4,6},{5,7},{6,4},{7,5},{8,10},{9,11},{10,... | collective-permute-start | bytes 786440 | tf_op jit(solution)/shard_map/ppermute | solution.py:486
  35.7 12.6 %collective-permute-start.16 = (bf16[128,1024]{1,0:T(8,128)(2,1)S(1)}, bf16[128,1024]{1,0:T(8,128)(2,1)S(1)}, u32[]{:S(2)}, u32[]{:S(2)}) collective-permute-start(bf16[128,1024]{1,0:T(8,128)(2,1)S(1)} %attn_out_own.1.part), channel_id=1, source_target_pairs={{0,2},{1,3},{2,0},{3,1},{4,6},{5,7},{6,4},{7,5},{8,10},{9,11},{10,... | collective-permute-start | bytes 786440 | tf_op jit(solution)/shard_map/ppermute | solution.py:486
  48.3 9.2 %collective-permute-start.19 = (bf16[128,1024]{1,0:T(8,128)(2,1)S(1)}, bf16[128,1024]{1,0:T(8,128)(2,1)S(1)}, u32[]{:S(2)}, u32[]{:S(2)}) collective-permute-start(bf16[128,1024]{1,0:T(8,128)(2,1)S(1)} %get-tuple-element.174.back), channel_id=1, source_target_pairs={{0,2},{1,3},{2,0},{3,1},{4,6},{5,7},{6,4},{7,5},{8,10},{9,11},{10,... | collective-permute-start | bytes 786440 | tf_op jit(solution)/shard_map/ppermute | solution.py:486
  51.9 9.6 %collective-permute-start.18 = (bf16[128,1024]{1,0:T(8,128)(2,1)S(1)}, bf16[128,1024]{1,0:T(8,128)(2,1)S(1)}, u32[]{:S(2)}, u32[]{:S(2)}) collective-permute-start(bf16[128,1024]{1,0:T(8,128)(2,1)S(1)} %get-tuple-element.179.back), channel_id=1, source_target_pairs={{0,2},{1,3},{2,0},{3,1},{4,6},{5,7},{6,4},{7,5},{8,10},{9,11},{10,... | collective-permute-start | bytes 786440 | tf_op jit(solution)/shard_map/ppermute | solution.py:486
  57.8 1.4 %collective-permute-start.20 = (bf16[64,1024]{1,0:T(8,128)(2,1)S(1)}, bf16[64,1024]{1,0:T(8,128)(2,1)S(1)}, u32[]{:S(2)}, u32[]{:S(2)}) collective-permute-start(bf16[64,1024]{1,0:T(8,128)(2,1)S(1)} %get-tuple-element.182), channel_id=1, source_target_pairs={{0,1},{1,0},{2,3},{3,2},{4,5},{5,4},{6,7},{7,6},{8,9},{9,8},{10,11... | collective-permute-start | bytes 393224 | tf_op jit(solution)/shard_map/ppermute | solution.py:483
  57.9 1.5 %collective-permute-start.21 = (bf16[64,1024]{1,0:T(8,128)(2,1)S(1)}, bf16[64,1024]{1,0:T(8,128)(2,1)S(1)}, u32[]{:S(2)}, u32[]{:S(2)}) collective-permute-start(bf16[64,1024]{1,0:T(8,128)(2,1)S(1)} %get-tuple-element.183), channel_id=1, source_target_pairs={{0,1},{1,0},{2,3},{3,2},{4,5},{5,4},{6,7},{7,6},{8,9},{9,8},{10,11... | collective-permute-start | bytes 393224 | tf_op jit(solution)/shard_map/ppermute | solution.py:483
  61.7 1.8 %collective-permute-start.22 = (bf16[128,1024]{1,0:T(8,128)(2,1)S(1)}, bf16[128,1024]{1,0:T(8,128)(2,1)S(1)}, u32[]{:S(2)}, u32[]{:S(2)}) collective-permute-start(bf16[128,1024]{1,0:T(8,128)(2,1)S(1)} %resid_back.1.first.d_resid), channel_id=1, source_target_pairs={{0,1},{1,0},{2,3},{3,2},{4,5},{5,4},{6,7},{7,6},{8,9},{9,8},{10,11... | collective-permute-start | bytes 786440 | tf_op jit(solution)/shard_map/ppermute | solution.py:483
  63.0 1.7 %collective-permute-start.23 = (bf16[128,1024]{1,0:T(8,128)(2,1)S(1)}, bf16[128,1024]{1,0:T(8,128)(2,1)S(1)}, u32[]{:S(2)}, u32[]{:S(2)}) collective-permute-start(bf16[128,1024]{1,0:T(8,128)(2,1)S(1)} %get-tuple-element.202), channel_id=1, source_target_pairs={{0,1},{1,0},{2,3},{3,2},{4,5},{5,4},{6,7},{7,6},{8,9},{9,8},{10,11... | collective-permute-start | bytes 786440 | tf_op jit(solution)/shard_map/ppermute | solution.py:483
  65.2 9.2 %collective-permute-start.27 = (bf16[128,1024]{1,0:T(8,128)(2,1)S(1)}, bf16[128,1024]{1,0:T(8,128)(2,1)S(1)}, u32[]{:S(2)}, u32[]{:S(2)}) collective-permute-start(bf16[128,1024]{1,0:T(8,128)(2,1)S(1)} %back_sum_far.1.part), channel_id=1, source_target_pairs={{0,2},{1,3},{2,0},{3,1},{4,6},{5,7},{6,4},{7,5},{8,10},{9,11},{10,... | collective-permute-start | bytes 786440 | tf_op jit(solution)/shard_map/ppermute | solution.py:486
  66.2 1.4 %collective-permute-start.24 = (bf16[64,1024]{1,0:T(8,128)(2,1)S(1)}, bf16[64,1024]{1,0:T(8,128)(2,1)S(1)}, u32[]{:S(2)}, u32[]{:S(2)}) collective-permute-start(bf16[64,1024]{1,0:T(8,128)(2,1)S(1)} %get-tuple-element.208), channel_id=1, source_target_pairs={{0,1},{1,0},{2,3},{3,2},{4,5},{5,4},{6,7},{7,6},{8,9},{9,8},{10,11... | collective-permute-start | bytes 393224 | tf_op jit(solution)/shard_map/ppermute | solution.py:483
  66.3 1.5 %collective-permute-start.25 = (bf16[64,1024]{1,0:T(8,128)(2,1)S(1)}, bf16[64,1024]{1,0:T(8,128)(2,1)S(1)}, u32[]{:S(2)}, u32[]{:S(2)}) collective-permute-start(bf16[64,1024]{1,0:T(8,128)(2,1)S(1)} %get-tuple-element.209), channel_id=1, source_target_pairs={{0,1},{1,0},{2,3},{3,2},{4,5},{5,4},{6,7},{7,6},{8,9},{9,8},{10,11... | collective-permute-start | bytes 393224 | tf_op jit(solution)/shard_map/ppermute | solution.py:483
  68.2 11.3 %collective-permute-start.26 = (bf16[128,1024]{1,0:T(8,128)(2,1)S(1)}, bf16[128,1024]{1,0:T(8,128)(2,1)S(1)}, u32[]{:S(2)}, u32[]{:S(2)}) collective-permute-start(bf16[128,1024]{1,0:T(8,128)(2,1)S(1)} %back_sum_own.1.part), channel_id=1, source_target_pairs={{0,2},{1,3},{2,0},{3,1},{4,6},{5,7},{6,4},{7,5},{8,10},{9,11},{10,... | collective-permute-start | bytes 786440 | tf_op jit(solution)/shard_map/ppermute | solution.py:486
  74.6 3.9 %collective-permute-start.28 = (bf16[64,1024]{1,0:T(8,128)(2,1)S(1)}, bf16[64,1024]{1,0:T(8,128)(2,1)S(1)}, u32[]{:S(2)}, u32[]{:S(2)}) collective-permute-start(bf16[64,1024]{1,0:T(8,128)(2,1)S(1)} %get-tuple-element.211), channel_id=1, source_target_pairs={{0,1},{1,0},{2,3},{3,2},{4,5},{5,4},{6,7},{7,6},{8,9},{9,8},{10,11... | collective-permute-start | bytes 393224 | tf_op jit(solution)/shard_map/ppermute | solution.py:483
  74.7 3.8 %collective-permute-start.29 = (bf16[64,1024]{1,0:T(8,128)(2,1)S(1)}, bf16[64,1024]{1,0:T(8,128)(2,1)S(1)}, u32[]{:S(2)}, u32[]{:S(2)}) collective-permute-start(bf16[64,1024]{1,0:T(8,128)(2,1)S(1)} %get-tuple-element.212), channel_id=1, source_target_pairs={{0,1},{1,0},{2,3},{3,2},{4,5},{5,4},{6,7},{7,6},{8,9},{9,8},{10,11... | collective-permute-start | bytes 393224 | tf_op jit(solution)/shard_map/ppermute | solution.py:483
  75.5 12.4 %collective-permute-start.38 = (bf16[96,1024]{1,0:T(8,128)(2,1)S(1)}, bf16[96,1024]{1,0:T(8,128)(2,1)S(1)}, u32[]{:S(2)}, u32[]{:S(2)}) collective-permute-start(bf16[96,1024]{1,0:T(8,128)(2,1)S(1)} %get-tuple-element.240), channel_id=1, source_target_pairs={{0,8},{4,12},{8,0},{12,4},{16,24},{20,28},{24,16},{28,20},{1,9},{5... | collective-permute-start | bytes 589832 | tf_op jit(solution)/shard_map/ppermute | solution.py:489
  79.8 1.3 %collective-permute-start.30 = (bf16[32,1024]{1,0:T(8,128)(2,1)S(1)}, bf16[32,1024]{1,0:T(8,128)(2,1)S(1)}, u32[]{:S(2)}, u32[]{:S(2)}) collective-permute-start(bf16[32,1024]{1,0:T(8,128)(2,1)S(1)} %get-tuple-element.221), channel_id=1, source_target_pairs={{0,1},{1,0},{2,3},{3,2},{4,5},{5,4},{6,7},{7,6},{8,9},{9,8},{10,11... | collective-permute-start | bytes 196616 | tf_op jit(solution)/shard_map/ppermute | solution.py:483
  79.9 1.4 %collective-permute-start.31 = (bf16[32,1024]{1,0:T(8,128)(2,1)S(1)}, bf16[32,1024]{1,0:T(8,128)(2,1)S(1)}, u32[]{:S(2)}, u32[]{:S(2)}) collective-permute-start(bf16[32,1024]{1,0:T(8,128)(2,1)S(1)} %get-tuple-element.222), channel_id=1, source_target_pairs={{0,1},{1,0},{2,3},{3,2},{4,5},{5,4},{6,7},{7,6},{8,9},{9,8},{10,11... | collective-permute-start | bytes 196616 | tf_op jit(solution)/shard_map/ppermute | solution.py:483
  80.4 1.3 %collective-permute-start.32 = (bf16[32,1024]{1,0:T(8,128)(2,1)S(1)}, bf16[32,1024]{1,0:T(8,128)(2,1)S(1)}, u32[]{:S(2)}, u32[]{:S(2)}) collective-permute-start(bf16[32,1024]{1,0:T(8,128)(2,1)S(1)} %get-tuple-element.223), channel_id=1, source_target_pairs={{0,1},{1,0},{2,3},{3,2},{4,5},{5,4},{6,7},{7,6},{8,9},{9,8},{10,11... | collective-permute-start | bytes 196616 | tf_op jit(solution)/shard_map/ppermute | solution.py:483
  80.5 1.3 %collective-permute-start.33 = (bf16[32,1024]{1,0:T(8,128)(2,1)S(1)}, bf16[32,1024]{1,0:T(8,128)(2,1)S(1)}, u32[]{:S(2)}, u32[]{:S(2)}) collective-permute-start(bf16[32,1024]{1,0:T(8,128)(2,1)S(1)} %get-tuple-element.224), channel_id=1, source_target_pairs={{0,1},{1,0},{2,3},{3,2},{4,5},{5,4},{6,7},{7,6},{8,9},{9,8},{10,11... | collective-permute-start | bytes 196616 | tf_op jit(solution)/shard_map/ppermute | solution.py:483
  83.1 9.2 %collective-permute-start.34 = (bf16[4,128,256]{2,1,0:T(8,128)(2,1)S(1)}, bf16[4,128,256]{2,1,0:T(8,128)(2,1)S(1)}, u32[]{:S(2)}, u32[]{:S(2)}) collective-permute-start(bf16[4,128,256]{2,1,0:T(8,128)(2,1)S(1)} %get-tuple-element.230), channel_id=1, source_target_pairs={{0,16},{4,20},{8,24},{12,28},{16,0},{20,4},{24,8},{28,12},{1,17},{... | collective-permute-start | bytes 786440 | tf_op jit(solution)/shard_map/ppermute | solution.py:489
  83.9 13.4 %collective-permute-start.37 = (bf16[4,128,256]{2,1,0:T(8,128)(2,1)S(1)}, bf16[4,128,256]{2,1,0:T(8,128)(2,1)S(1)}, u32[]{:S(2)}, u32[]{:S(2)}) collective-permute-start(bf16[4,128,256]{2,1,0:T(8,128)(2,1)S(1)} %get-tuple-element.237), channel_id=1, source_target_pairs={{0,16},{4,20},{8,24},{12,28},{16,0},{20,4},{24,8},{28,12},{1,17},{... | collective-permute-start | bytes 786440 | tf_op jit(solution)/shard_map/ppermute | solution.py:489
  87.9 6.7 %collective-permute-start.39 = (bf16[96,1024]{1,0:T(8,128)(2,1)S(1)}, bf16[96,1024]{1,0:T(8,128)(2,1)S(1)}, u32[]{:S(2)}, u32[]{:S(2)}) collective-permute-start(bf16[96,1024]{1,0:T(8,128)(2,1)S(1)} %back_pick.2), channel_id=1, source_target_pairs={{0,4},{4,0},{8,12},{12,8},{16,20},{20,16},{24,28},{28,24},{1,5},{5... | collective-permute-start | bytes 589832 | tf_op jit(solution)/shard_map/ppermute | solution.py:489
  89.0 17.1 %collective-permute-start.42 = (bf16[128,1024]{1,0:T(8,128)(2,1)S(1)}, bf16[128,1024]{1,0:T(8,128)(2,1)S(1)}, u32[]{:S(2)}, u32[]{:S(2)}) collective-permute-start(bf16[128,1024]{1,0:T(8,128)(2,1)S(1)} %ffn_out_far.1), channel_id=1, source_target_pairs={{0,2},{1,3},{2,0},{3,1},{4,6},{5,7},{6,4},{7,5},{8,10},{9,11},{10,... | collective-permute-start | bytes 786440 | tf_op jit(solution)/shard_map/ppermute | solution.py:486
  92.3 7.5 %collective-permute-start.35 = (bf16[2,128,256]{2,1,0:T(8,128)(2,1)S(1)}, bf16[2,128,256]{2,1,0:T(8,128)(2,1)S(1)}, u32[]{:S(2)}, u32[]{:S(2)}) collective-permute-start(bf16[2,128,256]{2,1,0:T(8,128)(2,1)S(1)} %get-tuple-element.232), channel_id=1, source_target_pairs={{0,4},{4,0},{8,12},{12,8},{16,20},{20,16},{24,28},{28,24},{1,5},{5... | collective-permute-start | bytes 393224 | tf_op jit(solution)/shard_map/ppermute | solution.py:489
  97.4 5.0 %collective-permute-start.40 = (bf16[2,128,256]{2,1,0:T(8,128)(2,1)S(1)}, bf16[2,128,256]{2,1,0:T(8,128)(2,1)S(1)}, u32[]{:S(2)}, u32[]{:S(2)}) collective-permute-start(bf16[2,128,256]{2,1,0:T(8,128)(2,1)S(1)} %get-tuple-element.243), channel_id=1, source_target_pairs={{0,4},{4,0},{8,12},{12,8},{16,20},{20,16},{24,28},{28,24},{1,5},{5... | collective-permute-start | bytes 393224 | tf_op jit(solution)/shard_map/ppermute | solution.py:489
  98.8 8.5 %collective-permute-start.43 = (bf16[96,1024]{1,0:T(8,128)(2,1)S(1)}, bf16[96,1024]{1,0:T(8,128)(2,1)S(1)}, u32[]{:S(2)}, u32[]{:S(2)}) collective-permute-start(bf16[96,1024]{1,0:T(8,128)(2,1)S(1)} %back_pick.3), channel_id=1, source_target_pairs={{0,16},{4,20},{8,24},{12,28},{16,0},{20,4},{24,8},{28,12},{1,17},{... | collective-permute-start | bytes 589832 | tf_op jit(solution)/shard_map/ppermute | solution.py:489
  99.9 7.4 %collective-permute-start.36 = (bf16[1,128,256]{2,1,0:T(8,128)(2,1)S(1)}, bf16[1,128,256]{2,1,0:T(8,128)(2,1)S(1)}, u32[]{:S(2)}, u32[]{:S(2)}) collective-permute-start(bf16[1,128,256]{2,1,0:T(8,128)(2,1)S(1)} %get-tuple-element.233), channel_id=1, source_target_pairs={{0,8},{4,12},{8,0},{12,4},{16,24},{20,28},{24,16},{28,20},{1,9},{5... | collective-permute-start | bytes 196616 | tf_op jit(solution)/shard_map/ppermute | solution.py:489
  102.4 5.9 %collective-permute-start.41 = (bf16[1,128,256]{2,1,0:T(8,128)(2,1)S(1)}, bf16[1,128,256]{2,1,0:T(8,128)(2,1)S(1)}, u32[]{:S(2)}, u32[]{:S(2)}) collective-permute-start(bf16[1,128,256]{2,1,0:T(8,128)(2,1)S(1)} %get-tuple-element.244), channel_id=1, source_target_pairs={{0,8},{4,12},{8,0},{12,4},{16,24},{20,28},{24,16},{28,20},{1,9},{5... | collective-permute-start | bytes 196616 | tf_op jit(solution)/shard_map/ppermute | solution.py:489

commit v16 on v15

--- a/solution.py
+++ b/solution.py
@@ -429,15 +429,15 @@
             target[j] = rows.astype(target.dtype)
 
 
-def enc_grads_second(bits, bit, *refs):
+def enc_grads_second(bits, bit1, bit0, *refs):
     rows, refs = refs[:-11], refs[-11:]
     act1, pre, enc, part1, part0, keep1, send1, keep0, send0 = refs[:9]
     total1, total0 = refs[9:]
     cots, act0 = rows[:-2], rows[-2:]
     total1[...] = rows_term([act1], cot_columns(cots, part1.shape[1])) + part1[...]
-    halve(bits, bit, total1, keep1, send1)
+    halve(bits, bit1, total1, keep1, send1)
     total0[...] = rows_term(act0, first_cot(cots, pre, enc)) + part0[...]
-    halve(bits, bit, total0, keep0, send0)
+    halve(bits, bit0, total0, keep0, send0)
 
 
 def halve_again(bits, bit, kept, got, keep, send):
@@ -718,7 +718,7 @@
         return kept, got
 
     kept1, send1, kept0, send0 = run(
-        functools.partial(enc_grads_second, tuple(bits), event_bits[0]),
+        functools.partial(enc_grads_second, tuple(bits), event_bits[0], pack_bits[0]),
         halves(bits) * 2,
         [cot_far, *cot_both, mine_far, mine_both, act_b, pre_b, enc_weight, part1, part0],
         total * 2,
@@ -744,7 +744,9 @@
     for bit in back_bits[1:-1]:
         send_back(bit)
     kept1, got1 = reduce_over(event_bits + pack_bits, kept1, send1, "halve1_", None)
-    kept0, got0 = reduce_over(event_bits + pack_bits, kept0, send0, "halve0_", event_bits[0])
+    kept0, got0 = reduce_over(
+        pack_bits[:1] + event_bits + pack_bits[1:], kept0, send0, "halve0_", pack_bits[0]
+    )
     send_back(back_bits[-1])
     got1, place = tie(got1, place)
     back_places = [held[k] for k in range(groups)]

time: 109 us -> 111 us (1.018)
  waiting for transfers between devices: 36.3 us -> 40.9 us
  starting transfers between devices: 43.4 us -> 40.7 us
    ppermute x16, waiting for transfers between devices: 12.8 us -> 17.4 us  [crossed(): return lax.ppermute(value, group_axes, [(i, i ^ k) for i in range(groups)])]
    ppermute x16, starting transfers between devices: 28.1 us -> 25.4 us  [crossed(): return lax.ppermute(value, group_axes, [(i, i ^ k) for i in range(groups)])]
  transfers between devices with their start and end apart: 44 -> 44, of which waited for: 26 -> 27; matrix products, arithmetic and copies ran while one was open for 1% -> 1% of each run, Pallas kernels for 23% -> 22%
where the time goes in v16:
time: 111 us
  waiting for transfers between devices  40.9 us (37%)
  starting transfers between devices  40.7 us (37%)
  Pallas kernels  26.7 us (24%)
    pallas_call x36, Pallas kernels, run(): pl.pallas_call(body, out_shape=list(outs), in_specs=[pl.BlockSpec(memory_...  26.7 us
    ppermute x16, starting transfers between devices, crossed(): return lax.ppermute(value, group_axes, [(i, i ^ k) for i in range(groups)])  25.4 us
    ppermute x9, waiting for transfers between devices, far(): return lax.ppermute(value, 'tensor', [(i, i ^ 2) for i in range(tensors)])  18.6 us
    ppermute x16, waiting for transfers between devices, crossed(): return lax.ppermute(value, group_axes, [(i, i ^ k) for i in range(groups)])  17.4 us
    ppermute x9, starting transfers between devices, far(): return lax.ppermute(value, 'tensor', [(i, i ^ 2) for i in range(tensors)])  10.2 us
    ppermute x19, starting transfers between devices, near(): return lax.ppermute(value, 'tensor', [(i, i ^ 1) for i in range(tensors)])  5.11 us
    ppermute x19, waiting for transfers between devices, near(): return lax.ppermute(value, 'tensor', [(i, i ^ 1) for i in range(tensors)])  4.88 us
  transfers between devices with their start and end apart: 44, of which 27 were waited for; matrix products, arithmetic and copies ran while one was open for 1% of the time, Pallas kernels for 22%

profile of v16, /device:TPU:0, one launch (start us, length us, event | category | flops | bytes accessed | tf_op | source)
XLA Modules:
  0.0 111.0 jit_solution(5615167896505115726)
XLA Ops:
  0.6 0.5 collective-permute-start
  1.2 0.7 add_bitcast_fusion.code
  1.9 0.9 copy-done.7
  3.2 4.1 %collective-permute-start.2 = (bf16[24,1152]{1,0:T(8,128)(2,1)S(1)}, bf16[24,1152]{1,0:T(8,128)(2,1)S(1)}, u32[]{:S(2)}, u32[]{:S(2)}) collective-permute-start(bf16[24,1152]{1,0:T(8,128)(2,1)S(1)} %get-tuple-element.131), channel_id=1, source_target_pairs={{0,8},{4,12},{8,0},{12,4},{16,24},{20,28},{24,16},{28,20},{1,9},{5... | collective-permute-start | bytes 165896 | tf_op jit(solution)/shard_map/ppermute | solution.py:489
  7.3 1.3 %collective-permute-start.3 = (bf16[24,1152]{1,0:T(8,128)(2,1)S(1)}, bf16[24,1152]{1,0:T(8,128)(2,1)S(1)}, u32[]{:S(2)}, u32[]{:S(2)}) collective-permute-start(bf16[24,1152]{1,0:T(8,128)(2,1)S(1)} %get-tuple-element.132), channel_id=1, source_target_pairs={{0,24},{4,28},{8,16},{12,20},{16,8},{20,12},{24,0},{28,4},{1,25},{... | collective-permute-start | bytes 165896 | tf_op jit(solution)/shard_map/ppermute | solution.py:489
  8.6 2.0 %collective-permute-start.4 = (bf16[24,1152]{1,0:T(8,128)(2,1)S(1)}, bf16[24,1152]{1,0:T(8,128)(2,1)S(1)}, u32[]{:S(2)}, u32[]{:S(2)}) collective-permute-start(bf16[24,1152]{1,0:T(8,128)(2,1)S(1)} %get-tuple-element.139), channel_id=1, source_target_pairs={{0,20},{4,16},{8,28},{12,24},{16,4},{20,0},{24,12},{28,8},{1,21},{... | collective-permute-start | bytes 165896 | tf_op jit(solution)/shard_map/ppermute | solution.py:489
  10.5 2.5 %collective-permute-start.5 = (bf16[24,1152]{1,0:T(8,128)(2,1)S(1)}, bf16[24,1152]{1,0:T(8,128)(2,1)S(1)}, u32[]{:S(2)}, u32[]{:S(2)}) collective-permute-start(bf16[24,1152]{1,0:T(8,128)(2,1)S(1)} %get-tuple-element.140), channel_id=1, source_target_pairs={{0,12},{4,8},{8,4},{12,0},{16,28},{20,24},{24,20},{28,16},{1,13},{... | collective-permute-start | bytes 165896 | tf_op jit(solution)/shard_map/ppermute | solution.py:489
  13.0 1.9 %collective-permute-start.6 = (bf16[24,1152]{1,0:T(8,128)(2,1)S(1)}, bf16[24,1152]{1,0:T(8,128)(2,1)S(1)}, u32[]{:S(2)}, u32[]{:S(2)}) collective-permute-start(bf16[24,1152]{1,0:T(8,128)(2,1)S(1)} %get-tuple-element.141), channel_id=1, source_target_pairs={{0,28},{4,24},{8,20},{12,16},{16,12},{20,8},{24,4},{28,0},{1,29},{... | collective-permute-start | bytes 165896 | tf_op jit(solution)/shard_map/ppermute | solution.py:489
  14.9 1.0 collective-permute-start.8
  15.9 0.8 turn.1
  16.7 3.2 %collective-permute-done.6.refs_5_ = bf16[24,1152]{1,0:T(8,128)(2,1)S(1)} collective-permute-done((bf16[24,1152]{1,0:T(8,128)(2,1)S(1)}, bf16[24,1152]{1,0:T(8,128)(2,1)S(1)}, u32[]{:S(2)}, u32[]{:S(2)}) %collective-permute-start.6) | collective-permute-done | bytes 55328 | tf_op jit(solution)/shard_map/ppermute | solution.py:489
  20.2 1.6 %collective-permute-start.9 = (bf16[128,1024]{1,0:T(8,128)(2,1)S(1)}, bf16[128,1024]{1,0:T(8,128)(2,1)S(1)}, u32[]{:S(2)}, u32[]{:S(2)}) collective-permute-start(bf16[128,1024]{1,0:T(8,128)(2,1)S(1)} %get-tuple-element.152.refs_0_.refs_3_), channel_id=1, source_target_pairs={{0,2},{1,3},{2,0},{3,1},{4,6},{5,7},{6,4},{7,5},{8,10},{9,11},{10,... | collective-permute-start | bytes 786440 | tf_op jit(solution)/shard_map/ppermute | solution.py:486
  21.8 0.5 collective-permute-start.11
  22.3 0.8 collective-permute-done.10.refs_1_.refs_4_
  23.4 2.3 %encode_first.1 = (f32[256,256]{1,0:T(8,128)S(1)}, bf16[256,1024]{1,0:T(8,128)(2,1)S(1)}, bf16[128,1024]{1,0:T(8,128)(2,1)S(1)}, bf16[4,2,128,256]{3,2,1,0:T(8,128)(2,1)S(1)}) custom-call(bf16[128,1024]{1,0:T(8,128)(2,1)S(1)} %get-tuple-element.152.refs_0_.refs_3_, bf16[64,1024]{1,0:T(8,128)(2,1)S(1)} %collective-permute-done.10.refs_1_.refs_4_, ...), custom_call_target="tpu_custom_call" | custom-call | tf_op jit(solution)/shard_map/encode_first/pallas_call | solution.py:64
  25.6 1.3 %collective-permute-done.9.refs_0_.refs_5_ = bf16[128,1024]{1,0:T(8,128)(2,1)S(1)} collective-permute-done((bf16[128,1024]{1,0:T(8,128)(2,1)S(1)}, bf16[128,1024]{1,0:T(8,128)(2,1)S(1)}, u32[]{:S(2)}, u32[]{:S(2)}) %collective-permute-start.9) | collective-permute-done | bytes 262176 | tf_op jit(solution)/shard_map/ppermute | solution.py:486
  26.9 0.5 collective-permute-start.12
  27.4 1.5 %collective-permute-start.15 = (bf16[128,1024]{1,0:T(8,128)(2,1)S(1)}, bf16[128,1024]{1,0:T(8,128)(2,1)S(1)}, u32[]{:S(2)}, u32[]{:S(2)}) collective-permute-start(bf16[128,1024]{1,0:T(8,128)(2,1)S(1)} %bitcast.5), channel_id=1, source_target_pairs={{0,2},{1,3},{2,0},{3,1},{4,6},{5,7},{6,4},{7,5},{8,10},{9,11},{10,... | collective-permute-start | bytes 786440 | tf_op jit(solution)/shard_map/ppermute | solution.py:486
  29.0 1.4 %encode_third.1 = (f32[128,256]{1,0:T(8,128)S(1)}, bf16[128,1024]{1,0:T(8,128)(2,1)S(1)}, bf16[128,1024]{1,0:T(8,128)(2,1)S(1)}, bf16[4,1,128,256]{3,2,1,0:T(8,128)(2,1)S(1)}) custom-call(bf16[128,1024]{1,0:T(8,128)(2,1)S(1)} %collective-permute-done.9.refs_0_.refs_5_, bf16[2,1024,1024]{2,1,0:T(8,128)(2,1)S(1)} %copy-done, bf16[4,1024,256]{2,1,0:T(8,128)(2,1)S(1)} %copy-done.1), custom_call_target="tpu_custom_call" | custom-call | tf_op jit(solution)/shard_map/encode_third/pallas_call | solution.py:64
  30.4 2.1 %attend_first.1 = (f32[256,256]{1,0:T(8,128)S(1)}, bf16[256,1024]{1,0:T(8,128)(2,1)S(1)}, bf16[4,4,128,256]{3,2,1,0:T(8,128)(2,1)S(1)}, f32[4,128,256]{2,1,0:T(8,128)S(1)}, bf16[256,256]{1,0:T(8,128)(2,1)S(1)}) custom-call(s32[4,1,128]{2,1,0:T(1,128)S(1)} %bitcast.8, bf16[128,1024]{1,0:T(8,128)(2,1)S(1)} %collective-permute-done.12.fourth.refs_6_, ...), custom_call_target="tpu_custom_call" | custom-call | tf_op jit(solution)/shard_map/attend_first/pallas_call | solution.py:64
  32.6 0.7 attend_second.1
  33.4 0.6 collective-permute-done.13.take
  34.3 0.6 collective-permute-start.17
  35.1 0.5 collective-permute-done.15.d_out_ref.d_out
  35.7 1.5 %collective-permute-start.16 = (bf16[128,1024]{1,0:T(8,128)(2,1)S(1)}, bf16[128,1024]{1,0:T(8,128)(2,1)S(1)}, u32[]{:S(2)}, u32[]{:S(2)}) collective-permute-start(bf16[128,1024]{1,0:T(8,128)(2,1)S(1)} %attn_out_own.1.part), channel_id=1, source_target_pairs={{0,2},{1,3},{2,0},{3,1},{4,6},{5,7},{6,4},{7,5},{8,10},{9,11},{10,... | collective-permute-start | bytes 786440 | tf_op jit(solution)/shard_map/ppermute | solution.py:486
  37.2 6.3 %collective-permute-done.17.got = bf16[128,1024]{1,0:T(8,128)(2,1)S(1)} collective-permute-done((bf16[128,1024]{1,0:T(8,128)(2,1)S(1)}, bf16[128,1024]{1,0:T(8,128)(2,1)S(1)}, u32[]{:S(2)}, u32[]{:S(2)}) %collective-permute-start.17) | collective-permute-done | bytes 262176 | tf_op jit(solution)/shard_map/ppermute | solution.py:486
  43.7 2.9 %ffn_own.1 = (bf16[128,1024]{1,0:T(8,128)(2,1)S(1)}, bf16[128,1024]{1,0:T(8,128)(2,1)S(1)}) custom-call(bf16[128,1024]{1,0:T(8,128)(2,1)S(1)} %get-tuple-element.170.rows_ref, bf16[128,1024]{1,0:T(8,128)(2,1)S(1)} %bitcast.6, bf16[2,1024,512]{2,1,0:T(8,128)(2,1)S(1)} %copy-done.3, bf16[2,1024,512]{2,1,0:T(8,128)(2,1)S(1)} %collective-permute-done.in_b, ...), custom_call_target="tpu_custom_call" | custom-call | tf_op jit(solution)/shard_map/ffn_own/pallas_call | solution.py:64
  46.6 1.7 %collective-permute-done.16.got = bf16[128,1024]{1,0:T(8,128)(2,1)S(1)} collective-permute-done((bf16[128,1024]{1,0:T(8,128)(2,1)S(1)}, bf16[128,1024]{1,0:T(8,128)(2,1)S(1)}, u32[]{:S(2)}, u32[]{:S(2)}) %collective-permute-start.16) | collective-permute-done | bytes 262176 | tf_op jit(solution)/shard_map/ppermute | solution.py:486
  48.3 0.5 collective-permute-start.19
  49.0 2.9 %ffn_far.1 = (bf16[128,1024]{1,0:T(8,128)(2,1)S(1)}, bf16[128,1024]{1,0:T(8,128)(2,1)S(1)}) custom-call(bf16[128,1024]{1,0:T(8,128)(2,1)S(1)} %get-tuple-element.177.rows_ref, bf16[128,1024]{1,0:T(8,128)(2,1)S(1)} %collective-permute-done.15.d_out_ref.d_out, bf16[2,1024,512]{2,1,0:T(8,128)(2,1)S(1)} %copy-done.3, ...), custom_call_target="tpu_custom_call" | custom-call | tf_op jit(solution)/shard_map/ffn_far/pallas_call | solution.py:64
  51.9 1.8 %collective-permute-start.18 = (bf16[128,1024]{1,0:T(8,128)(2,1)S(1)}, bf16[128,1024]{1,0:T(8,128)(2,1)S(1)}, u32[]{:S(2)}, u32[]{:S(2)}) collective-permute-start(bf16[128,1024]{1,0:T(8,128)(2,1)S(1)} %get-tuple-element.179.back), channel_id=1, source_target_pairs={{0,2},{1,3},{2,0},{3,1},{4,6},{5,7},{6,4},{7,5},{8,10},{9,11},{10,... | collective-permute-start | bytes 786440 | tf_op jit(solution)/shard_map/ppermute | solution.py:486
  53.7 3.9 %collective-permute-done.19.got = bf16[128,1024]{1,0:T(8,128)(2,1)S(1)} collective-permute-done((bf16[128,1024]{1,0:T(8,128)(2,1)S(1)}, bf16[128,1024]{1,0:T(8,128)(2,1)S(1)}, u32[]{:S(2)}, u32[]{:S(2)}) %collective-permute-start.19) | collective-permute-done | bytes 262176 | tf_op jit(solution)/shard_map/ppermute | solution.py:486
  57.9 0.5 collective-permute-start.21
  58.4 0.8 collective-permute-done.20.fourth_a
  59.4 1.6 %attn_back_first.1 = (bf16[4,128,256]{2,1,0:T(8,128)(2,1)S(1)}, f32[4,128,256]{2,1,0:T(8,128)S(1)}, f32[4,128,256]{2,1,0:T(8,128)S(1)}, bf16[4,128,256]{2,1,0:T(8,128)(2,1)S(1)}) custom-call(s32[4,1,128]{2,1,0:T(1,128)S(1)} %bitcast.10, bf16[128,1024]{1,0:T(8,128)(2,1)S(1)} %get-tuple-element.181.third.d_resid, ...), custom_call_target="tpu_custom_call" | custom-call | tf_op jit(solution)/shard_map/attn_back_first/pallas_call | solution.py:64
  61.8 1.2 %attn_back_own.1 = (bf16[128,1024]{1,0:T(8,128)(2,1)S(1)}, bf16[4,128,256]{2,1,0:T(8,128)(2,1)S(1)}, f32[4,128,256]{2,1,0:T(8,128)S(1)}, f32[4,128,256]{2,1,0:T(8,128)S(1)}, bf16[4,128,256]{2,1,0:T(8,128)(2,1)S(1)}) custom-call(s32[4,1,128]{2,1,0:T(1,128)S(1)} %bitcast.11, ...), custom_call_target="tpu_custom_call", output_to_operand_aliasing={{1}: (5, {}), {2}: (6, {}), {3}: (7, {}), {4}: (8, {})} | custom-call | tf_op jit(solution)/shard_map/attn_back_own/pallas_call | solution.py:64
  63.0 0.6 collective-permute-start.23
  63.5 0.8 attn_back_second.1
  65.2 0.6 collective-permute-start.27
  66.8 0.8 collective-permute-done.24.refs_0_
  68.2 1.6 %collective-permute-start.26 = (bf16[128,1024]{1,0:T(8,128)(2,1)S(1)}, bf16[128,1024]{1,0:T(8,128)(2,1)S(1)}, u32[]{:S(2)}, u32[]{:S(2)}) collective-permute-start(bf16[128,1024]{1,0:T(8,128)(2,1)S(1)} %back_sum_own.1.part), channel_id=1, source_target_pairs={{0,2},{1,3},{2,0},{3,1},{4,6},{5,7},{6,4},{7,5},{8,10},{9,11},{10,... | collective-permute-start | bytes 786440 | tf_op jit(solution)/shard_map/ppermute | solution.py:486
  69.8 4.5 %collective-permute-done.27.got = bf16[128,1024]{1,0:T(8,128)(2,1)S(1)} collective-permute-done((bf16[128,1024]{1,0:T(8,128)(2,1)S(1)}, bf16[128,1024]{1,0:T(8,128)(2,1)S(1)}, u32[]{:S(2)}, u32[]{:S(2)}) %collective-permute-start.27) | collective-permute-done | bytes 262176 | tf_op jit(solution)/shard_map/ppermute | solution.py:486
  75.5 3.0 %collective-permute-start.38 = (bf16[96,1024]{1,0:T(8,128)(2,1)S(1)}, bf16[96,1024]{1,0:T(8,128)(2,1)S(1)}, u32[]{:S(2)}, u32[]{:S(2)}) collective-permute-start(bf16[96,1024]{1,0:T(8,128)(2,1)S(1)} %get-tuple-element.240), channel_id=1, source_target_pairs={{0,8},{4,12},{8,0},{12,4},{16,24},{20,28},{24,16},{28,20},{1,9},{5... | collective-permute-start | bytes 589832 | tf_op jit(solution)/shard_map/ppermute | solution.py:489
  78.5 1.0 enc_grads_first.1
  81.8 1.2 %enc_grads_second.1 = (f32[4,128,256]{2,1,0:T(8,128)S(1)}, bf16[4,128,256]{2,1,0:T(8,128)(2,1)S(1)}, f32[4,128,256]{2,1,0:T(8,128)S(1)}, bf16[4,128,256]{2,1,0:T(8,128)(2,1)S(1)}) custom-call(bf16[128,1024]{1,0:T(8,128)(2,1)S(1)} %get-tuple-element.220.refs_0_, bf16[32,1024]{1,0:T(8,128)(2,1)S(1)} %collective-permute-done.30.refs_1_, ...), custom_call_target="tpu_custom_call" | custom-call | tf_op jit(solution)/shard_map/enc_grads_second/pallas_call | solution.py:64
  83.0 0.8 collective-permute-start.34
  83.8 1.6 %collective-permute-start.37 = (bf16[4,128,256]{2,1,0:T(8,128)(2,1)S(1)}, bf16[4,128,256]{2,1,0:T(8,128)(2,1)S(1)}, u32[]{:S(2)}, u32[]{:S(2)}) collective-permute-start(bf16[4,128,256]{2,1,0:T(8,128)(2,1)S(1)} %get-tuple-element.237), channel_id=1, source_target_pairs={{0,4},{4,0},{8,12},{12,8},{16,20},{20,16},{24,28},{28,24},{1,5},{5... | collective-permute-start | bytes 786440 | tf_op jit(solution)/shard_map/ppermute | solution.py:489
  85.4 2.6 %collective-permute-done.38.refs_1_ = bf16[96,1024]{1,0:T(8,128)(2,1)S(1)} collective-permute-done((bf16[96,1024]{1,0:T(8,128)(2,1)S(1)}, bf16[96,1024]{1,0:T(8,128)(2,1)S(1)}, u32[]{:S(2)}, u32[]{:S(2)}) %collective-permute-start.38) | collective-permute-done | bytes 196640 | tf_op jit(solution)/shard_map/ppermute | solution.py:489
  88.0 0.5 collective-permute-start.39
  89.0 0.6 collective-permute-start.42
  89.6 2.1 %collective-permute-done.34.got = bf16[4,128,256]{2,1,0:T(8,128)(2,1)S(1)} collective-permute-done((bf16[4,128,256]{2,1,0:T(8,128)(2,1)S(1)}, bf16[4,128,256]{2,1,0:T(8,128)(2,1)S(1)}, u32[]{:S(2)}, u32[]{:S(2)}) %collective-permute-start.34) | collective-permute-done | bytes 262176 | tf_op jit(solution)/shard_map/ppermute | solution.py:489
  91.7 1.4 %collective-permute-start.35 = (bf16[2,128,256]{2,1,0:T(8,128)(2,1)S(1)}, bf16[2,128,256]{2,1,0:T(8,128)(2,1)S(1)}, u32[]{:S(2)}, u32[]{:S(2)}) collective-permute-start(bf16[2,128,256]{2,1,0:T(8,128)(2,1)S(1)} %get-tuple-element.232), channel_id=1, source_target_pairs={{0,4},{4,0},{8,12},{12,8},{16,20},{20,16},{24,28},{28,24},{1,5},{5... | collective-permute-start | bytes 393224 | tf_op jit(solution)/shard_map/ppermute | solution.py:489
  93.1 4.7 %collective-permute-done.39.refs_2_ = bf16[96,1024]{1,0:T(8,128)(2,1)S(1)} collective-permute-done((bf16[96,1024]{1,0:T(8,128)(2,1)S(1)}, bf16[96,1024]{1,0:T(8,128)(2,1)S(1)}, u32[]{:S(2)}, u32[]{:S(2)}) %collective-permute-start.39) | collective-permute-done | bytes 196640 | tf_op jit(solution)/shard_map/ppermute | solution.py:489
  97.8 0.8 collective-permute-start.40
  98.7 1.4 %collective-permute-start.43 = (bf16[96,1024]{1,0:T(8,128)(2,1)S(1)}, bf16[96,1024]{1,0:T(8,128)(2,1)S(1)}, u32[]{:S(2)}, u32[]{:S(2)}) collective-permute-start(bf16[96,1024]{1,0:T(8,128)(2,1)S(1)} %back_pick.3), channel_id=1, source_target_pairs={{0,16},{4,20},{8,24},{12,28},{16,0},{20,4},{24,8},{28,12},{1,17},{... | collective-permute-start | bytes 589832 | tf_op jit(solution)/shard_map/ppermute | solution.py:489
  100.0 0.5 collective-permute-done.35.got
  100.5 1.6 %collective-permute-start.36 = (bf16[1,128,256]{2,1,0:T(8,128)(2,1)S(1)}, bf16[1,128,256]{2,1,0:T(8,128)(2,1)S(1)}, u32[]{:S(2)}, u32[]{:S(2)}) collective-permute-start(bf16[1,128,256]{2,1,0:T(8,128)(2,1)S(1)} %get-tuple-element.233), channel_id=1, source_target_pairs={{0,8},{4,12},{8,0},{12,4},{16,24},{20,28},{24,16},{28,20},{1,9},{5... | collective-permute-start | bytes 196616 | tf_op jit(solution)/shard_map/ppermute | solution.py:489
  102.1 2.2 %collective-permute-done.40.got = bf16[2,128,256]{2,1,0:T(8,128)(2,1)S(1)} collective-permute-done((bf16[2,128,256]{2,1,0:T(8,128)(2,1)S(1)}, bf16[2,128,256]{2,1,0:T(8,128)(2,1)S(1)}, u32[]{:S(2)}, u32[]{:S(2)}) %collective-permute-start.40) | collective-permute-done | bytes 131104 | tf_op jit(solution)/shard_map/ppermute | solution.py:489
  104.3 1.7 %collective-permute-start.41 = (bf16[1,128,256]{2,1,0:T(8,128)(2,1)S(1)}, bf16[1,128,256]{2,1,0:T(8,128)(2,1)S(1)}, u32[]{:S(2)}, u32[]{:S(2)}) collective-permute-start(bf16[1,128,256]{2,1,0:T(8,128)(2,1)S(1)} %get-tuple-element.244), channel_id=1, source_target_pairs={{0,8},{4,12},{8,0},{12,4},{16,24},{20,28},{24,16},{28,20},{1,9},{5... | collective-permute-start | bytes 196616 | tf_op jit(solution)/shard_map/ppermute | solution.py:489
  106.0 1.2 %ffn_out_own.1 = bf16[128,1024]{1,0:T(8,128)(2,1)} custom-call(bf16[128,1024]{1,0:T(8,128)(2,1)S(1)} %get-tuple-element.245.hidden, bf16[512,1024]{1,0:T(8,128)(2,1)S(1)} %copy-done.2, bf16[512,1024]{1,0:T(8,128)(2,1)S(1)} %collective-permute-done.1.out_b.w_b, bf16[128,1024]{1,0:T(8,128)(2,1)S(1)} %get-tuple-element.188.resid, ...), custom_call_target="tpu_custom_call" | custom-call | tf_op jit(solution)/shard_map/ffn_out_own/pallas_call | solution.py:64
  107.2 1.1 %collective-permute-done.36.got1 = bf16[1,128,256]{2,1,0:T(8,128)(2,1)S(1)} collective-permute-done((bf16[1,128,256]{2,1,0:T(8,128)(2,1)S(1)}, bf16[1,128,256]{2,1,0:T(8,128)(2,1)S(1)}, u32[]{:S(2)}, u32[]{:S(2)}) %collective-permute-start.36) | collective-permute-done | bytes 65568 | tf_op jit(solution)/shard_map/ppermute | solution.py:489
  108.3 1.0 back_recv.1
  109.3 1.0 collective-permute-done.41.got0
  110.2 0.7 finish.1
  (77 shorter events, 9.8 us)
Async XLA Ops:
  0.6 7.9 %collective-permute-start = (bf16[2,1024,512]{2,1,0:T(8,128)(2,1)}, bf16[2,1024,512]{2,1,0:T(8,128)(2,1)S(1)}, u32[]{:S(2)}, u32[]{:S(2)}) collective-permute-start(bf16[2,1024,512]{2,1,0:T(8,128)(2,1)} %in_a.3), channel_id=1, source_target_pairs={{0,1},{1,0},{2,3},{3,2},{4,5},{5,4},{6,7},{7,6},{8,9},{9,8},{10,11... | collective-permute-start | bytes 6291464 | tf_op jit(solution)/shard_map/ppermute | solution.py:483
  1.1 7.4 %collective-permute-start.1 = (bf16[512,1024]{1,0:T(8,128)(2,1)}, bf16[512,1024]{1,0:T(8,128)(2,1)S(1)}, u32[]{:S(2)}, u32[]{:S(2)}) collective-permute-start(bf16[512,1024]{1,0:T(8,128)(2,1)} %w_a.3), channel_id=1, source_target_pairs={{0,1},{1,0},{2,3},{3,2},{4,5},{5,4},{6,7},{7,6},{8,9},{9,8},{10,11... | collective-permute-start | bytes 3145736 | tf_op jit(solution)/shard_map/ppermute | solution.py:483
  1.9 0.9 copy-start.7
  2.9 13.0 %copy-start.1 = (bf16[4,1024,256]{2,1,0:T(8,128)(2,1)S(1)}, bf16[4,1024,256]{2,1,0:T(8,128)(2,1)}, u32[]{:S(2)}) copy-start(bf16[4,1024,256]{2,1,0:T(8,128)(2,1)} %w_in.1) | copy-start | bytes 6291460
  2.9 13.0 %copy-start.4 = (bf16[256,1024]{1,0:T(8,128)(2,1)S(1)}, bf16[256,1024]{1,0:T(8,128)(2,1)}, u32[]{:S(2)}) copy-start(bf16[256,1024]{1,0:T(8,128)(2,1)} %w_own.3) | copy-start | bytes 1572868
  2.9 20.5 %copy-start = (bf16[2,1024,1024]{2,1,0:T(8,128)(2,1)S(1)}, bf16[2,1024,1024]{2,1,0:T(8,128)(2,1)}, u32[]{:S(2)}) copy-start(bf16[2,1024,1024]{2,1,0:T(8,128)(2,1)} %refs_9_.1) | copy-start | bytes 12582916
  3.2 11.7 %collective-permute-start.2 = (bf16[24,1152]{1,0:T(8,128)(2,1)S(1)}, bf16[24,1152]{1,0:T(8,128)(2,1)S(1)}, u32[]{:S(2)}, u32[]{:S(2)}) collective-permute-start(bf16[24,1152]{1,0:T(8,128)(2,1)S(1)} %get-tuple-element.131), channel_id=1, source_target_pairs={{0,8},{4,12},{8,0},{12,4},{16,24},{20,28},{24,16},{28,20},{1,9},{5... | collective-permute-start | bytes 165896 | tf_op jit(solution)/shard_map/ppermute | solution.py:489
  7.3 7.6 %collective-permute-start.3 = (bf16[24,1152]{1,0:T(8,128)(2,1)S(1)}, bf16[24,1152]{1,0:T(8,128)(2,1)S(1)}, u32[]{:S(2)}, u32[]{:S(2)}) collective-permute-start(bf16[24,1152]{1,0:T(8,128)(2,1)S(1)} %get-tuple-element.132), channel_id=1, source_target_pairs={{0,24},{4,28},{8,16},{12,20},{16,8},{20,12},{24,0},{28,4},{1,25},{... | collective-permute-start | bytes 165896 | tf_op jit(solution)/shard_map/ppermute | solution.py:489
  8.6 8.1 %collective-permute-start.4 = (bf16[24,1152]{1,0:T(8,128)(2,1)S(1)}, bf16[24,1152]{1,0:T(8,128)(2,1)S(1)}, u32[]{:S(2)}, u32[]{:S(2)}) collective-permute-start(bf16[24,1152]{1,0:T(8,128)(2,1)S(1)} %get-tuple-element.139), channel_id=1, source_target_pairs={{0,20},{4,16},{8,28},{12,24},{16,4},{20,0},{24,12},{28,8},{1,21},{... | collective-permute-start | bytes 165896 | tf_op jit(solution)/shard_map/ppermute | solution.py:489
  10.5 6.2 %collective-permute-start.5 = (bf16[24,1152]{1,0:T(8,128)(2,1)S(1)}, bf16[24,1152]{1,0:T(8,128)(2,1)S(1)}, u32[]{:S(2)}, u32[]{:S(2)}) collective-permute-start(bf16[24,1152]{1,0:T(8,128)(2,1)S(1)} %get-tuple-element.140), channel_id=1, source_target_pairs={{0,12},{4,8},{8,4},{12,0},{16,28},{20,24},{24,20},{28,16},{1,13},{... | collective-permute-start | bytes 165896 | tf_op jit(solution)/shard_map/ppermute | solution.py:489
  13.0 7.0 %collective-permute-start.6 = (bf16[24,1152]{1,0:T(8,128)(2,1)S(1)}, bf16[24,1152]{1,0:T(8,128)(2,1)S(1)}, u32[]{:S(2)}, u32[]{:S(2)}) collective-permute-start(bf16[24,1152]{1,0:T(8,128)(2,1)S(1)} %get-tuple-element.141), channel_id=1, source_target_pairs={{0,28},{4,24},{8,20},{12,16},{16,12},{20,8},{24,4},{28,0},{1,29},{... | collective-permute-start | bytes 165896 | tf_op jit(solution)/shard_map/ppermute | solution.py:489
  14.9 5.1 %collective-permute-start.7 = (bf16[24,1152]{1,0:T(8,128)(2,1)S(1)}, bf16[24,1152]{1,0:T(8,128)(2,1)S(1)}, u32[]{:S(2)}, u32[]{:S(2)}) collective-permute-start(bf16[24,1152]{1,0:T(8,128)(2,1)S(1)} %get-tuple-element.142), channel_id=1, source_target_pairs={{0,4},{4,0},{8,12},{12,8},{16,20},{20,16},{24,28},{28,24},{1,5},{5... | collective-permute-start | bytes 165896 | tf_op jit(solution)/shard_map/ppermute | solution.py:489
  14.9 5.1 %collective-permute-start.8 = (bf16[24,1152]{1,0:T(8,128)(2,1)S(1)}, bf16[24,1152]{1,0:T(8,128)(2,1)S(1)}, u32[]{:S(2)}, u32[]{:S(2)}) collective-permute-start(bf16[24,1152]{1,0:T(8,128)(2,1)S(1)} %get-tuple-element.143), channel_id=1, source_target_pairs={{0,16},{4,20},{8,24},{12,28},{16,0},{20,4},{24,8},{28,12},{1,17},{... | collective-permute-start | bytes 165896 | tf_op jit(solution)/shard_map/ppermute | solution.py:489
  20.2 6.7 %collective-permute-start.9 = (bf16[128,1024]{1,0:T(8,128)(2,1)S(1)}, bf16[128,1024]{1,0:T(8,128)(2,1)S(1)}, u32[]{:S(2)}, u32[]{:S(2)}) collective-permute-start(bf16[128,1024]{1,0:T(8,128)(2,1)S(1)} %get-tuple-element.152.refs_0_.refs_3_), channel_id=1, source_target_pairs={{0,2},{1,3},{2,0},{3,1},{4,6},{5,7},{6,4},{7,5},{8,10},{9,11},{10,... | collective-permute-start | bytes 786440 | tf_op jit(solution)/shard_map/ppermute | solution.py:486
  21.8 1.3 %collective-permute-start.10 = (bf16[64,1024]{1,0:T(8,128)(2,1)S(1)}, bf16[64,1024]{1,0:T(8,128)(2,1)S(1)}, u32[]{:S(2)}, u32[]{:S(2)}) collective-permute-start(bf16[64,1024]{1,0:T(8,128)(2,1)S(1)} %get-tuple-element.153), channel_id=1, source_target_pairs={{0,1},{1,0},{2,3},{3,2},{4,5},{5,4},{6,7},{7,6},{8,9},{9,8},{10,11... | collective-permute-start | bytes 393224 | tf_op jit(solution)/shard_map/ppermute | solution.py:483
  21.8 5.6 %copy-start.5 = (bf16[1,128,1024]{2,1,0:T(8,128)(2,1)S(1)}, bf16[1,128,1024]{2,1,0:T(8,128)(2,1)}, u32[]{:S(2)}) copy-start(bf16[1,128,1024]{2,1,0:T(8,128)(2,1)} %param.19) | copy-start | bytes 786436
  21.8 1.5 %collective-permute-start.11 = (bf16[64,1024]{1,0:T(8,128)(2,1)S(1)}, bf16[64,1024]{1,0:T(8,128)(2,1)S(1)}, u32[]{:S(2)}, u32[]{:S(2)}) collective-permute-start(bf16[64,1024]{1,0:T(8,128)(2,1)S(1)} %get-tuple-element.154), channel_id=1, source_target_pairs={{0,1},{1,0},{2,3},{3,2},{4,5},{5,4},{6,7},{7,6},{8,9},{9,8},{10,11... | collective-permute-start | bytes 393224 | tf_op jit(solution)/shard_map/ppermute | solution.py:483
  26.9 3.4 %copy-start.6 = (s32[1,512]{1,0:T(1,128)S(1)}, s32[1,512]{1,0:T(1,128)}, u32[]{:S(2)}) copy-start(s32[1,512]{1,0:T(1,128)} %param.13) | copy-start | bytes 6148
  26.9 7.0 %collective-permute-start.14 = (bf16[256,1024]{1,0:T(8,128)(2,1)S(1)}, bf16[256,1024]{1,0:T(8,128)(2,1)S(1)}, u32[]{:S(2)}, u32[]{:S(2)}) collective-permute-start(bf16[256,1024]{1,0:T(8,128)(2,1)S(1)} %copy-done.4), channel_id=1, source_target_pairs={{0,1},{1,0},{2,3},{3,2},{4,5},{5,4},{6,7},{7,6},{8,9},{9,8},{10,11... | collective-permute-start | bytes 1572872 | tf_op jit(solution)/shard_map/ppermute | solution.py:483
  26.9 3.4 %collective-permute-start.12 = (bf16[128,1024]{1,0:T(8,128)(2,1)S(1)}, bf16[128,1024]{1,0:T(8,128)(2,1)S(1)}, u32[]{:S(2)}, u32[]{:S(2)}) collective-permute-start(bf16[128,1024]{1,0:T(8,128)(2,1)S(1)} %collective-permute-done.9.refs_0_.refs_5_), channel_id=1, source_target_pairs={{0,1},{1,0},{2,3},{3,2},{4,5},{5,4},{6,7},{7,6},{8,9},{9,8},{10,11... | collective-permute-start | bytes 786440 | tf_op jit(solution)/shard_map/ppermute | solution.py:483
  27.4 8.2 %collective-permute-start.15 = (bf16[128,1024]{1,0:T(8,128)(2,1)S(1)}, bf16[128,1024]{1,0:T(8,128)(2,1)S(1)}, u32[]{:S(2)}, u32[]{:S(2)}) collective-permute-start(bf16[128,1024]{1,0:T(8,128)(2,1)S(1)} %bitcast.5), channel_id=1, source_target_pairs={{0,2},{1,3},{2,0},{3,1},{4,6},{5,7},{6,4},{7,5},{8,10},{9,11},{10,... | collective-permute-start | bytes 786440 | tf_op jit(solution)/shard_map/ppermute | solution.py:486
  32.5 1.4 %collective-permute-start.13 = (bf16[256,256]{1,0:T(8,128)(2,1)S(1)}, bf16[256,256]{1,0:T(8,128)(2,1)S(1)}, u32[]{:S(2)}, u32[]{:S(2)}) collective-permute-start(bf16[256,256]{1,0:T(8,128)(2,1)S(1)} %get-tuple-element.165), channel_id=1, source_target_pairs={{0,1},{1,0},{2,3},{3,2},{4,5},{5,4},{6,7},{7,6},{8,9},{9,8},{10,11... | collective-permute-start | bytes 393224 | tf_op jit(solution)/shard_map/ppermute | solution.py:483
  33.3 10.4 %copy-start.2 = (bf16[512,1024]{1,0:T(8,128)(2,1)S(1)}, bf16[512,1024]{1,0:T(8,128)(2,1)}, u32[]{:S(2)}) copy-start(bf16[512,1024]{1,0:T(8,128)(2,1)} %w_a.3) | copy-start | bytes 3145732
  33.3 10.4 %copy-start.3 = (bf16[2,1024,512]{2,1,0:T(8,128)(2,1)S(1)}, bf16[2,1024,512]{2,1,0:T(8,128)(2,1)}, u32[]{:S(2)}) copy-start(bf16[2,1024,512]{2,1,0:T(8,128)(2,1)} %in_a.3) | copy-start | bytes 6291460
  34.3 9.2 %collective-permute-start.17 = (bf16[128,1024]{1,0:T(8,128)(2,1)S(1)}, bf16[128,1024]{1,0:T(8,128)(2,1)S(1)}, u32[]{:S(2)}, u32[]{:S(2)}) collective-permute-start(bf16[128,1024]{1,0:T(8,128)(2,1)S(1)} %attn_out_far.1.part), channel_id=1, source_target_pairs={{0,2},{1,3},{2,0},{3,1},{4,6},{5,7},{6,4},{7,5},{8,10},{9,11},{10,... | collective-permute-start | bytes 786440 | tf_op jit(solution)/shard_map/ppermute | solution.py:486
  35.7 12.6 %collective-permute-start.16 = (bf16[128,1024]{1,0:T(8,128)(2,1)S(1)}, bf16[128,1024]{1,0:T(8,128)(2,1)S(1)}, u32[]{:S(2)}, u32[]{:S(2)}) collective-permute-start(bf16[128,1024]{1,0:T(8,128)(2,1)S(1)} %attn_out_own.1.part), channel_id=1, source_target_pairs={{0,2},{1,3},{2,0},{3,1},{4,6},{5,7},{6,4},{7,5},{8,10},{9,11},{10,... | collective-permute-start | bytes 786440 | tf_op jit(solution)/shard_map/ppermute | solution.py:486
  48.3 9.2 %collective-permute-start.19 = (bf16[128,1024]{1,0:T(8,128)(2,1)S(1)}, bf16[128,1024]{1,0:T(8,128)(2,1)S(1)}, u32[]{:S(2)}, u32[]{:S(2)}) collective-permute-start(bf16[128,1024]{1,0:T(8,128)(2,1)S(1)} %get-tuple-element.174.back), channel_id=1, source_target_pairs={{0,2},{1,3},{2,0},{3,1},{4,6},{5,7},{6,4},{7,5},{8,10},{9,11},{10,... | collective-permute-start | bytes 786440 | tf_op jit(solution)/shard_map/ppermute | solution.py:486
  51.9 9.6 %collective-permute-start.18 = (bf16[128,1024]{1,0:T(8,128)(2,1)S(1)}, bf16[128,1024]{1,0:T(8,128)(2,1)S(1)}, u32[]{:S(2)}, u32[]{:S(2)}) collective-permute-start(bf16[128,1024]{1,0:T(8,128)(2,1)S(1)} %get-tuple-element.179.back), channel_id=1, source_target_pairs={{0,2},{1,3},{2,0},{3,1},{4,6},{5,7},{6,4},{7,5},{8,10},{9,11},{10,... | collective-permute-start | bytes 786440 | tf_op jit(solution)/shard_map/ppermute | solution.py:486
  57.8 1.4 %collective-permute-start.20 = (bf16[64,1024]{1,0:T(8,128)(2,1)S(1)}, bf16[64,1024]{1,0:T(8,128)(2,1)S(1)}, u32[]{:S(2)}, u32[]{:S(2)}) collective-permute-start(bf16[64,1024]{1,0:T(8,128)(2,1)S(1)} %get-tuple-element.182), channel_id=1, source_target_pairs={{0,1},{1,0},{2,3},{3,2},{4,5},{5,4},{6,7},{7,6},{8,9},{9,8},{10,11... | collective-permute-start | bytes 393224 | tf_op jit(solution)/shard_map/ppermute | solution.py:483
  57.9 1.5 %collective-permute-start.21 = (bf16[64,1024]{1,0:T(8,128)(2,1)S(1)}, bf16[64,1024]{1,0:T(8,128)(2,1)S(1)}, u32[]{:S(2)}, u32[]{:S(2)}) collective-permute-start(bf16[64,1024]{1,0:T(8,128)(2,1)S(1)} %get-tuple-element.183), channel_id=1, source_target_pairs={{0,1},{1,0},{2,3},{3,2},{4,5},{5,4},{6,7},{7,6},{8,9},{9,8},{10,11... | collective-permute-start | bytes 393224 | tf_op jit(solution)/shard_map/ppermute | solution.py:483
  61.7 1.8 %collective-permute-start.22 = (bf16[128,1024]{1,0:T(8,128)(2,1)S(1)}, bf16[128,1024]{1,0:T(8,128)(2,1)S(1)}, u32[]{:S(2)}, u32[]{:S(2)}) collective-permute-start(bf16[128,1024]{1,0:T(8,128)(2,1)S(1)} %resid_back.1.first.d_resid), channel_id=1, source_target_pairs={{0,1},{1,0},{2,3},{3,2},{4,5},{5,4},{6,7},{7,6},{8,9},{9,8},{10,11... | collective-permute-start | bytes 786440 | tf_op jit(solution)/shard_map/ppermute | solution.py:483
  63.0 1.7 %collective-permute-start.23 = (bf16[128,1024]{1,0:T(8,128)(2,1)S(1)}, bf16[128,1024]{1,0:T(8,128)(2,1)S(1)}, u32[]{:S(2)}, u32[]{:S(2)}) collective-permute-start(bf16[128,1024]{1,0:T(8,128)(2,1)S(1)} %get-tuple-element.202), channel_id=1, source_target_pairs={{0,1},{1,0},{2,3},{3,2},{4,5},{5,4},{6,7},{7,6},{8,9},{9,8},{10,11... | collective-permute-start | bytes 786440 | tf_op jit(solution)/shard_map/ppermute | solution.py:483
  65.2 9.2 %collective-permute-start.27 = (bf16[128,1024]{1,0:T(8,128)(2,1)S(1)}, bf16[128,1024]{1,0:T(8,128)(2,1)S(1)}, u32[]{:S(2)}, u32[]{:S(2)}) collective-permute-start(bf16[128,1024]{1,0:T(8,128)(2,1)S(1)} %back_sum_far.1.part), channel_id=1, source_target_pairs={{0,2},{1,3},{2,0},{3,1},{4,6},{5,7},{6,4},{7,5},{8,10},{9,11},{10,... | collective-permute-start | bytes 786440 | tf_op jit(solution)/shard_map/ppermute | solution.py:486
  66.2 1.4 %collective-permute-start.24 = (bf16[64,1024]{1,0:T(8,128)(2,1)S(1)}, bf16[64,1024]{1,0:T(8,128)(2,1)S(1)}, u32[]{:S(2)}, u32[]{:S(2)}) collective-permute-start(bf16[64,1024]{1,0:T(8,128)(2,1)S(1)} %get-tuple-element.208), channel_id=1, source_target_pairs={{0,1},{1,0},{2,3},{3,2},{4,5},{5,4},{6,7},{7,6},{8,9},{9,8},{10,11... | collective-permute-start | bytes 393224 | tf_op jit(solution)/shard_map/ppermute | solution.py:483
  66.3 1.5 %collective-permute-start.25 = (bf16[64,1024]{1,0:T(8,128)(2,1)S(1)}, bf16[64,1024]{1,0:T(8,128)(2,1)S(1)}, u32[]{:S(2)}, u32[]{:S(2)}) collective-permute-start(bf16[64,1024]{1,0:T(8,128)(2,1)S(1)} %get-tuple-element.209), channel_id=1, source_target_pairs={{0,1},{1,0},{2,3},{3,2},{4,5},{5,4},{6,7},{7,6},{8,9},{9,8},{10,11... | collective-permute-start | bytes 393224 | tf_op jit(solution)/shard_map/ppermute | solution.py:483
  68.2 11.3 %collective-permute-start.26 = (bf16[128,1024]{1,0:T(8,128)(2,1)S(1)}, bf16[128,1024]{1,0:T(8,128)(2,1)S(1)}, u32[]{:S(2)}, u32[]{:S(2)}) collective-permute-start(bf16[128,1024]{1,0:T(8,128)(2,1)S(1)} %back_sum_own.1.part), channel_id=1, source_target_pairs={{0,2},{1,3},{2,0},{3,1},{4,6},{5,7},{6,4},{7,5},{8,10},{9,11},{10,... | collective-permute-start | bytes 786440 | tf_op jit(solution)/shard_map/ppermute | solution.py:486
  74.6 3.9 %collective-permute-start.28 = (bf16[64,1024]{1,0:T(8,128)(2,1)S(1)}, bf16[64,1024]{1,0:T(8,128)(2,1)S(1)}, u32[]{:S(2)}, u32[]{:S(2)}) collective-permute-start(bf16[64,1024]{1,0:T(8,128)(2,1)S(1)} %get-tuple-element.211), channel_id=1, source_target_pairs={{0,1},{1,0},{2,3},{3,2},{4,5},{5,4},{6,7},{7,6},{8,9},{9,8},{10,11... | collective-permute-start | bytes 393224 | tf_op jit(solution)/shard_map/ppermute | solution.py:483
  74.7 3.8 %collective-permute-start.29 = (bf16[64,1024]{1,0:T(8,128)(2,1)S(1)}, bf16[64,1024]{1,0:T(8,128)(2,1)S(1)}, u32[]{:S(2)}, u32[]{:S(2)}) collective-permute-start(bf16[64,1024]{1,0:T(8,128)(2,1)S(1)} %get-tuple-element.212), channel_id=1, source_target_pairs={{0,1},{1,0},{2,3},{3,2},{4,5},{5,4},{6,7},{7,6},{8,9},{9,8},{10,11... | collective-permute-start | bytes 393224 | tf_op jit(solution)/shard_map/ppermute | solution.py:483
  75.5 12.5 %collective-permute-start.38 = (bf16[96,1024]{1,0:T(8,128)(2,1)S(1)}, bf16[96,1024]{1,0:T(8,128)(2,1)S(1)}, u32[]{:S(2)}, u32[]{:S(2)}) collective-permute-start(bf16[96,1024]{1,0:T(8,128)(2,1)S(1)} %get-tuple-element.240), channel_id=1, source_target_pairs={{0,8},{4,12},{8,0},{12,4},{16,24},{20,28},{24,16},{28,20},{1,9},{5... | collective-permute-start | bytes 589832 | tf_op jit(solution)/shard_map/ppermute | solution.py:489
  79.8 1.3 %collective-permute-start.30 = (bf16[32,1024]{1,0:T(8,128)(2,1)S(1)}, bf16[32,1024]{1,0:T(8,128)(2,1)S(1)}, u32[]{:S(2)}, u32[]{:S(2)}) collective-permute-start(bf16[32,1024]{1,0:T(8,128)(2,1)S(1)} %get-tuple-element.221), channel_id=1, source_target_pairs={{0,1},{1,0},{2,3},{3,2},{4,5},{5,4},{6,7},{7,6},{8,9},{9,8},{10,11... | collective-permute-start | bytes 196616 | tf_op jit(solution)/shard_map/ppermute | solution.py:483
  79.9 1.4 %collective-permute-start.31 = (bf16[32,1024]{1,0:T(8,128)(2,1)S(1)}, bf16[32,1024]{1,0:T(8,128)(2,1)S(1)}, u32[]{:S(2)}, u32[]{:S(2)}) collective-permute-start(bf16[32,1024]{1,0:T(8,128)(2,1)S(1)} %get-tuple-element.222), channel_id=1, source_target_pairs={{0,1},{1,0},{2,3},{3,2},{4,5},{5,4},{6,7},{7,6},{8,9},{9,8},{10,11... | collective-permute-start | bytes 196616 | tf_op jit(solution)/shard_map/ppermute | solution.py:483
  80.4 1.3 %collective-permute-start.32 = (bf16[32,1024]{1,0:T(8,128)(2,1)S(1)}, bf16[32,1024]{1,0:T(8,128)(2,1)S(1)}, u32[]{:S(2)}, u32[]{:S(2)}) collective-permute-start(bf16[32,1024]{1,0:T(8,128)(2,1)S(1)} %get-tuple-element.223), channel_id=1, source_target_pairs={{0,1},{1,0},{2,3},{3,2},{4,5},{5,4},{6,7},{7,6},{8,9},{9,8},{10,11... | collective-permute-start | bytes 196616 | tf_op jit(solution)/shard_map/ppermute | solution.py:483
  80.5 1.3 %collective-permute-start.33 = (bf16[32,1024]{1,0:T(8,128)(2,1)S(1)}, bf16[32,1024]{1,0:T(8,128)(2,1)S(1)}, u32[]{:S(2)}, u32[]{:S(2)}) collective-permute-start(bf16[32,1024]{1,0:T(8,128)(2,1)S(1)} %get-tuple-element.224), channel_id=1, source_target_pairs={{0,1},{1,0},{2,3},{3,2},{4,5},{5,4},{6,7},{7,6},{8,9},{9,8},{10,11... | collective-permute-start | bytes 196616 | tf_op jit(solution)/shard_map/ppermute | solution.py:483
  83.0 8.6 %collective-permute-start.34 = (bf16[4,128,256]{2,1,0:T(8,128)(2,1)S(1)}, bf16[4,128,256]{2,1,0:T(8,128)(2,1)S(1)}, u32[]{:S(2)}, u32[]{:S(2)}) collective-permute-start(bf16[4,128,256]{2,1,0:T(8,128)(2,1)S(1)} %get-tuple-element.230), channel_id=1, source_target_pairs={{0,16},{4,20},{8,24},{12,28},{16,0},{20,4},{24,8},{28,12},{1,17},{... | collective-permute-start | bytes 786440 | tf_op jit(solution)/shard_map/ppermute | solution.py:489
  83.8 14.0 %collective-permute-start.37 = (bf16[4,128,256]{2,1,0:T(8,128)(2,1)S(1)}, bf16[4,128,256]{2,1,0:T(8,128)(2,1)S(1)}, u32[]{:S(2)}, u32[]{:S(2)}) collective-permute-start(bf16[4,128,256]{2,1,0:T(8,128)(2,1)S(1)} %get-tuple-element.237), channel_id=1, source_target_pairs={{0,4},{4,0},{8,12},{12,8},{16,20},{20,16},{24,28},{28,24},{1,5},{5... | collective-permute-start | bytes 786440 | tf_op jit(solution)/shard_map/ppermute | solution.py:489
  88.0 9.8 %collective-permute-start.39 = (bf16[96,1024]{1,0:T(8,128)(2,1)S(1)}, bf16[96,1024]{1,0:T(8,128)(2,1)S(1)}, u32[]{:S(2)}, u32[]{:S(2)}) collective-permute-start(bf16[96,1024]{1,0:T(8,128)(2,1)S(1)} %back_pick.2), channel_id=1, source_target_pairs={{0,4},{4,0},{8,12},{12,8},{16,20},{20,16},{24,28},{28,24},{1,5},{5... | collective-permute-start | bytes 589832 | tf_op jit(solution)/shard_map/ppermute | solution.py:489
  89.0 17.0 %collective-permute-start.42 = (bf16[128,1024]{1,0:T(8,128)(2,1)S(1)}, bf16[128,1024]{1,0:T(8,128)(2,1)S(1)}, u32[]{:S(2)}, u32[]{:S(2)}) collective-permute-start(bf16[128,1024]{1,0:T(8,128)(2,1)S(1)} %ffn_out_far.1), channel_id=1, source_target_pairs={{0,2},{1,3},{2,0},{3,1},{4,6},{5,7},{6,4},{7,5},{8,10},{9,11},{10,... | collective-permute-start | bytes 786440 | tf_op jit(solution)/shard_map/ppermute | solution.py:486
  91.7 8.8 %collective-permute-start.35 = (bf16[2,128,256]{2,1,0:T(8,128)(2,1)S(1)}, bf16[2,128,256]{2,1,0:T(8,128)(2,1)S(1)}, u32[]{:S(2)}, u32[]{:S(2)}) collective-permute-start(bf16[2,128,256]{2,1,0:T(8,128)(2,1)S(1)} %get-tuple-element.232), channel_id=1, source_target_pairs={{0,4},{4,0},{8,12},{12,8},{16,20},{20,16},{24,28},{28,24},{1,5},{5... | collective-permute-start | bytes 393224 | tf_op jit(solution)/shard_map/ppermute | solution.py:489
  97.8 6.4 %collective-permute-start.40 = (bf16[2,128,256]{2,1,0:T(8,128)(2,1)S(1)}, bf16[2,128,256]{2,1,0:T(8,128)(2,1)S(1)}, u32[]{:S(2)}, u32[]{:S(2)}) collective-permute-start(bf16[2,128,256]{2,1,0:T(8,128)(2,1)S(1)} %get-tuple-element.243), channel_id=1, source_target_pairs={{0,16},{4,20},{8,24},{12,28},{16,0},{20,4},{24,8},{28,12},{1,17},{... | collective-permute-start | bytes 393224 | tf_op jit(solution)/shard_map/ppermute | solution.py:489
  98.7 9.7 %collective-permute-start.43 = (bf16[96,1024]{1,0:T(8,128)(2,1)S(1)}, bf16[96,1024]{1,0:T(8,128)(2,1)S(1)}, u32[]{:S(2)}, u32[]{:S(2)}) collective-permute-start(bf16[96,1024]{1,0:T(8,128)(2,1)S(1)} %back_pick.3), channel_id=1, source_target_pairs={{0,16},{4,20},{8,24},{12,28},{16,0},{20,4},{24,8},{28,12},{1,17},{... | collective-permute-start | bytes 589832 | tf_op jit(solution)/shard_map/ppermute | solution.py:489
  100.5 7.8 %collective-permute-start.36 = (bf16[1,128,256]{2,1,0:T(8,128)(2,1)S(1)}, bf16[1,128,256]{2,1,0:T(8,128)(2,1)S(1)}, u32[]{:S(2)}, u32[]{:S(2)}) collective-permute-start(bf16[1,128,256]{2,1,0:T(8,128)(2,1)S(1)} %get-tuple-element.233), channel_id=1, source_target_pairs={{0,8},{4,12},{8,0},{12,4},{16,24},{20,28},{24,16},{28,20},{1,9},{5... | collective-permute-start | bytes 196616 | tf_op jit(solution)/shard_map/ppermute | solution.py:489
  104.3 5.9 %collective-permute-start.41 = (bf16[1,128,256]{2,1,0:T(8,128)(2,1)S(1)}, bf16[1,128,256]{2,1,0:T(8,128)(2,1)S(1)}, u32[]{:S(2)}, u32[]{:S(2)}) collective-permute-start(bf16[1,128,256]{2,1,0:T(8,128)(2,1)S(1)} %get-tuple-element.244), channel_id=1, source_target_pairs={{0,8},{4,12},{8,0},{12,4},{16,24},{20,28},{24,16},{28,20},{1,9},{5... | collective-permute-start | bytes 196616 | tf_op jit(solution)/shard_map/ppermute | solution.py:489

commit v17 on v15

--- a/solution.py
+++ b/solution.py
@@ -47,9 +47,10 @@
 
 def store_halves(value, out, halves):
     out[...] = value
-    rows = value.shape[0] // max(len(halves), 1)
-    for n, target in enumerate(halves):
-        target[...] = value[n * rows : (n + 1) * rows]
+    first = 0
+    for target in halves:
+        target[...] = value[first : first + target.shape[0]]
+        first += target.shape[0]
 
 
 def turned(row, rows):
@@ -679,7 +680,7 @@
     got_far, part1, part0 = tie(got_far, part1, part0)
     cot_far, *cot_pieces = run(
         packed_back,
-        [row_b] + [like((rows_dev // 4, width), BF16)] * 4,
+        [row_b] + [like((rows_dev * part // 8, width), BF16) for part in (3, 3, 2)],
         [sum_far, got_far, packed_far, d_resid_far],
         name="packed_back_far",
     )

time: 109 us -> 109 us (level)
  starting transfers between devices: 43.4 us -> 42.1 us
    ppermute x19 -> x18, starting transfers between devices: 5.11 us -> 4.67 us  [near(): return lax.ppermute(value, 'tensor', [(i, i ^ 1) for i in range(tensors)])]
    ppermute x19 -> x18, waiting for transfers between devices: 4.88 us -> 5.16 us  [near(): return lax.ppermute(value, 'tensor', [(i, i ^ 1) for i in range(tensors)])]
  transfers between devices with their start and end apart: 44 -> 43, of which waited for: 26 -> 24; matrix products, arithmetic and copies ran while one was open for 1% -> 1% of each run, Pallas kernels for 23% -> 23%
where the time goes in v17:
time: 109 us
  starting transfers between devices  42.1 us (39%)
  waiting for transfers between devices  37.3 us (34%)
  Pallas kernels  26.7 us (24%)
    ppermute x16, starting transfers between devices, crossed(): return lax.ppermute(value, group_axes, [(i, i ^ k) for i in range(groups)])  27.2 us
    pallas_call x36, Pallas kernels, run(): pl.pallas_call(body, out_shape=list(outs), in_specs=[pl.BlockSpec(memory_...  26.7 us
    ppermute x9, waiting for transfers between devices, far(): return lax.ppermute(value, 'tensor', [(i, i ^ 2) for i in range(tensors)])  18.6 us
    ppermute x16, waiting for transfers between devices, crossed(): return lax.ppermute(value, group_axes, [(i, i ^ k) for i in range(groups)])  13.5 us
    ppermute x9, starting transfers between devices, far(): return lax.ppermute(value, 'tensor', [(i, i ^ 2) for i in range(tensors)])  10.2 us
    ppermute x18, waiting for transfers between devices, near(): return lax.ppermute(value, 'tensor', [(i, i ^ 1) for i in range(tensors)])  5.16 us
    ppermute x18, starting transfers between devices, near(): return lax.ppermute(value, 'tensor', [(i, i ^ 1) for i in range(tensors)])  4.67 us
  transfers between devices with their start and end apart: 43, of which 24 were waited for; matrix products, arithmetic and copies ran while one was open for 1% of the time, Pallas kernels for 23%

profile of v17, /device:TPU:0, one launch (start us, length us, event | category | flops | bytes accessed | tf_op | source)
XLA Modules:
  0.0 108.8 jit_solution(17365704634506048351)
XLA Ops:
  0.6 0.5 collective-permute-start
  1.2 0.7 add_bitcast_fusion.code
  1.9 0.9 copy-done.7
  3.2 4.1 %collective-permute-start.2 = (bf16[24,1152]{1,0:T(8,128)(2,1)S(1)}, bf16[24,1152]{1,0:T(8,128)(2,1)S(1)}, u32[]{:S(2)}, u32[]{:S(2)}) collective-permute-start(bf16[24,1152]{1,0:T(8,128)(2,1)S(1)} %get-tuple-element.130), channel_id=1, source_target_pairs={{0,8},{4,12},{8,0},{12,4},{16,24},{20,28},{24,16},{28,20},{1,9},{5... | collective-permute-start | bytes 165896 | tf_op jit(solution)/shard_map/ppermute | solution.py:490
  7.3 1.3 %collective-permute-start.3 = (bf16[24,1152]{1,0:T(8,128)(2,1)S(1)}, bf16[24,1152]{1,0:T(8,128)(2,1)S(1)}, u32[]{:S(2)}, u32[]{:S(2)}) collective-permute-start(bf16[24,1152]{1,0:T(8,128)(2,1)S(1)} %get-tuple-element.131), channel_id=1, source_target_pairs={{0,24},{4,28},{8,16},{12,20},{16,8},{20,12},{24,0},{28,4},{1,25},{... | collective-permute-start | bytes 165896 | tf_op jit(solution)/shard_map/ppermute | solution.py:490
  8.6 2.0 %collective-permute-start.4 = (bf16[24,1152]{1,0:T(8,128)(2,1)S(1)}, bf16[24,1152]{1,0:T(8,128)(2,1)S(1)}, u32[]{:S(2)}, u32[]{:S(2)}) collective-permute-start(bf16[24,1152]{1,0:T(8,128)(2,1)S(1)} %get-tuple-element.138), channel_id=1, source_target_pairs={{0,20},{4,16},{8,28},{12,24},{16,4},{20,0},{24,12},{28,8},{1,21},{... | collective-permute-start | bytes 165896 | tf_op jit(solution)/shard_map/ppermute | solution.py:490
  10.5 2.5 %collective-permute-start.5 = (bf16[24,1152]{1,0:T(8,128)(2,1)S(1)}, bf16[24,1152]{1,0:T(8,128)(2,1)S(1)}, u32[]{:S(2)}, u32[]{:S(2)}) collective-permute-start(bf16[24,1152]{1,0:T(8,128)(2,1)S(1)} %get-tuple-element.139), channel_id=1, source_target_pairs={{0,12},{4,8},{8,4},{12,0},{16,28},{20,24},{24,20},{28,16},{1,13},{... | collective-permute-start | bytes 165896 | tf_op jit(solution)/shard_map/ppermute | solution.py:490
  13.0 1.9 %collective-permute-start.6 = (bf16[24,1152]{1,0:T(8,128)(2,1)S(1)}, bf16[24,1152]{1,0:T(8,128)(2,1)S(1)}, u32[]{:S(2)}, u32[]{:S(2)}) collective-permute-start(bf16[24,1152]{1,0:T(8,128)(2,1)S(1)} %get-tuple-element.140), channel_id=1, source_target_pairs={{0,28},{4,24},{8,20},{12,16},{16,12},{20,8},{24,4},{28,0},{1,29},{... | collective-permute-start | bytes 165896 | tf_op jit(solution)/shard_map/ppermute | solution.py:490
  14.9 1.0 collective-permute-start.8
  15.9 0.8 turn.1
  16.7 3.2 %collective-permute-done.6.refs_5_ = bf16[24,1152]{1,0:T(8,128)(2,1)S(1)} collective-permute-done((bf16[24,1152]{1,0:T(8,128)(2,1)S(1)}, bf16[24,1152]{1,0:T(8,128)(2,1)S(1)}, u32[]{:S(2)}, u32[]{:S(2)}) %collective-permute-start.6) | collective-permute-done | bytes 55328 | tf_op jit(solution)/shard_map/ppermute | solution.py:490
  20.2 1.6 %collective-permute-start.9 = (bf16[128,1024]{1,0:T(8,128)(2,1)S(1)}, bf16[128,1024]{1,0:T(8,128)(2,1)S(1)}, u32[]{:S(2)}, u32[]{:S(2)}) collective-permute-start(bf16[128,1024]{1,0:T(8,128)(2,1)S(1)} %get-tuple-element.151.refs_0_.refs_3_), channel_id=1, source_target_pairs={{0,2},{1,3},{2,0},{3,1},{4,6},{5,7},{6,4},{7,5},{8,10},{9,11},{10,... | collective-permute-start | bytes 786440 | tf_op jit(solution)/shard_map/ppermute | solution.py:487
  21.8 0.5 collective-permute-start.11
  22.3 0.8 collective-permute-done.10.refs_1_.refs_4_
  23.4 2.3 %encode_first.1 = (f32[256,256]{1,0:T(8,128)S(1)}, bf16[256,1024]{1,0:T(8,128)(2,1)S(1)}, bf16[128,1024]{1,0:T(8,128)(2,1)S(1)}, bf16[4,2,128,256]{3,2,1,0:T(8,128)(2,1)S(1)}) custom-call(bf16[128,1024]{1,0:T(8,128)(2,1)S(1)} %get-tuple-element.151.refs_0_.refs_3_, bf16[64,1024]{1,0:T(8,128)(2,1)S(1)} %collective-permute-done.10.refs_1_.refs_4_, ...), custom_call_target="tpu_custom_call" | custom-call | tf_op jit(solution)/shard_map/encode_first/pallas_call | solution.py:65
  25.6 1.3 %collective-permute-done.9.refs_0_.refs_4_ = bf16[128,1024]{1,0:T(8,128)(2,1)S(1)} collective-permute-done((bf16[128,1024]{1,0:T(8,128)(2,1)S(1)}, bf16[128,1024]{1,0:T(8,128)(2,1)S(1)}, u32[]{:S(2)}, u32[]{:S(2)}) %collective-permute-start.9) | collective-permute-done | bytes 262176 | tf_op jit(solution)/shard_map/ppermute | solution.py:487
  26.9 0.5 collective-permute-start.12
  27.4 1.5 %collective-permute-start.15 = (bf16[128,1024]{1,0:T(8,128)(2,1)S(1)}, bf16[128,1024]{1,0:T(8,128)(2,1)S(1)}, u32[]{:S(2)}, u32[]{:S(2)}) collective-permute-start(bf16[128,1024]{1,0:T(8,128)(2,1)S(1)} %bitcast.5), channel_id=1, source_target_pairs={{0,2},{1,3},{2,0},{3,1},{4,6},{5,7},{6,4},{7,5},{8,10},{9,11},{10,... | collective-permute-start | bytes 786440 | tf_op jit(solution)/shard_map/ppermute | solution.py:487
  29.0 1.4 %encode_third.1 = (f32[128,256]{1,0:T(8,128)S(1)}, bf16[128,1024]{1,0:T(8,128)(2,1)S(1)}, bf16[128,1024]{1,0:T(8,128)(2,1)S(1)}, bf16[4,1,128,256]{3,2,1,0:T(8,128)(2,1)S(1)}) custom-call(bf16[128,1024]{1,0:T(8,128)(2,1)S(1)} %collective-permute-done.9.refs_0_.refs_4_, bf16[2,1024,1024]{2,1,0:T(8,128)(2,1)S(1)} %copy-done, bf16[4,1024,256]{2,1,0:T(8,128)(2,1)S(1)} %copy-done.1), custom_call_target="tpu_custom_call" | custom-call | tf_op jit(solution)/shard_map/encode_third/pallas_call | solution.py:65
  30.4 2.1 %attend_first.1 = (f32[256,256]{1,0:T(8,128)S(1)}, bf16[256,1024]{1,0:T(8,128)(2,1)S(1)}, bf16[4,4,128,256]{3,2,1,0:T(8,128)(2,1)S(1)}, f32[4,128,256]{2,1,0:T(8,128)S(1)}, bf16[256,256]{1,0:T(8,128)(2,1)S(1)}) custom-call(s32[4,1,128]{2,1,0:T(1,128)S(1)} %bitcast.8, bf16[128,1024]{1,0:T(8,128)(2,1)S(1)} %collective-permute-done.12.fourth.refs_5_, ...), custom_call_target="tpu_custom_call" | custom-call | tf_op jit(solution)/shard_map/attend_first/pallas_call | solution.py:65
  32.6 0.7 attend_second.1
  33.4 0.6 collective-permute-done.13.take
  34.3 0.6 collective-permute-start.17
  35.1 0.5 collective-permute-done.15.d_out_ref.d_out
  35.7 1.5 %collective-permute-start.16 = (bf16[128,1024]{1,0:T(8,128)(2,1)S(1)}, bf16[128,1024]{1,0:T(8,128)(2,1)S(1)}, u32[]{:S(2)}, u32[]{:S(2)}) collective-permute-start(bf16[128,1024]{1,0:T(8,128)(2,1)S(1)} %attn_out_own.1.part), channel_id=1, source_target_pairs={{0,2},{1,3},{2,0},{3,1},{4,6},{5,7},{6,4},{7,5},{8,10},{9,11},{10,... | collective-permute-start | bytes 786440 | tf_op jit(solution)/shard_map/ppermute | solution.py:487
  37.2 6.3 %collective-permute-done.17.got = bf16[128,1024]{1,0:T(8,128)(2,1)S(1)} collective-permute-done((bf16[128,1024]{1,0:T(8,128)(2,1)S(1)}, bf16[128,1024]{1,0:T(8,128)(2,1)S(1)}, u32[]{:S(2)}, u32[]{:S(2)}) %collective-permute-start.17) | collective-permute-done | bytes 262176 | tf_op jit(solution)/shard_map/ppermute | solution.py:487
  43.7 2.9 %ffn_own.1 = (bf16[128,1024]{1,0:T(8,128)(2,1)S(1)}, bf16[128,1024]{1,0:T(8,128)(2,1)S(1)}) custom-call(bf16[128,1024]{1,0:T(8,128)(2,1)S(1)} %get-tuple-element.169.rows_ref, bf16[128,1024]{1,0:T(8,128)(2,1)S(1)} %bitcast.6, bf16[2,1024,512]{2,1,0:T(8,128)(2,1)S(1)} %copy-done.3, bf16[2,1024,512]{2,1,0:T(8,128)(2,1)S(1)} %collective-permute-done.in_b, ...), custom_call_target="tpu_custom_call" | custom-call | tf_op jit(solution)/shard_map/ffn_own/pallas_call | solution.py:65
  46.6 1.7 %collective-permute-done.16.got = bf16[128,1024]{1,0:T(8,128)(2,1)S(1)} collective-permute-done((bf16[128,1024]{1,0:T(8,128)(2,1)S(1)}, bf16[128,1024]{1,0:T(8,128)(2,1)S(1)}, u32[]{:S(2)}, u32[]{:S(2)}) %collective-permute-start.16) | collective-permute-done | bytes 262176 | tf_op jit(solution)/shard_map/ppermute | solution.py:487
  48.3 0.5 collective-permute-start.19
  49.0 2.9 %ffn_far.1 = (bf16[128,1024]{1,0:T(8,128)(2,1)S(1)}, bf16[128,1024]{1,0:T(8,128)(2,1)S(1)}) custom-call(bf16[128,1024]{1,0:T(8,128)(2,1)S(1)} %get-tuple-element.176.rows_ref, bf16[128,1024]{1,0:T(8,128)(2,1)S(1)} %collective-permute-done.15.d_out_ref.d_out, bf16[2,1024,512]{2,1,0:T(8,128)(2,1)S(1)} %copy-done.3, ...), custom_call_target="tpu_custom_call" | custom-call | tf_op jit(solution)/shard_map/ffn_far/pallas_call | solution.py:65
  51.9 1.8 %collective-permute-start.18 = (bf16[128,1024]{1,0:T(8,128)(2,1)S(1)}, bf16[128,1024]{1,0:T(8,128)(2,1)S(1)}, u32[]{:S(2)}, u32[]{:S(2)}) collective-permute-start(bf16[128,1024]{1,0:T(8,128)(2,1)S(1)} %get-tuple-element.178.back), channel_id=1, source_target_pairs={{0,2},{1,3},{2,0},{3,1},{4,6},{5,7},{6,4},{7,5},{8,10},{9,11},{10,... | collective-permute-start | bytes 786440 | tf_op jit(solution)/shard_map/ppermute | solution.py:487
  53.7 3.9 %collective-permute-done.19.got = bf16[128,1024]{1,0:T(8,128)(2,1)S(1)} collective-permute-done((bf16[128,1024]{1,0:T(8,128)(2,1)S(1)}, bf16[128,1024]{1,0:T(8,128)(2,1)S(1)}, u32[]{:S(2)}, u32[]{:S(2)}) %collective-permute-start.19) | collective-permute-done | bytes 262176 | tf_op jit(solution)/shard_map/ppermute | solution.py:487
  57.9 0.5 collective-permute-start.21
  58.4 0.8 collective-permute-done.20.fourth_a
  59.4 1.6 %attn_back_first.1 = (bf16[4,128,256]{2,1,0:T(8,128)(2,1)S(1)}, f32[4,128,256]{2,1,0:T(8,128)S(1)}, f32[4,128,256]{2,1,0:T(8,128)S(1)}, bf16[4,128,256]{2,1,0:T(8,128)(2,1)S(1)}) custom-call(s32[4,1,128]{2,1,0:T(1,128)S(1)} %bitcast.10, bf16[128,1024]{1,0:T(8,128)(2,1)S(1)} %get-tuple-element.180.third.d_resid, ...), custom_call_target="tpu_custom_call" | custom-call | tf_op jit(solution)/shard_map/attn_back_first/pallas_call | solution.py:65
  61.8 1.2 %attn_back_own.1 = (bf16[128,1024]{1,0:T(8,128)(2,1)S(1)}, bf16[4,128,256]{2,1,0:T(8,128)(2,1)S(1)}, f32[4,128,256]{2,1,0:T(8,128)S(1)}, f32[4,128,256]{2,1,0:T(8,128)S(1)}, bf16[4,128,256]{2,1,0:T(8,128)(2,1)S(1)}) custom-call(s32[4,1,128]{2,1,0:T(1,128)S(1)} %bitcast.11, ...), custom_call_target="tpu_custom_call", output_to_operand_aliasing={{1}: (5, {}), {2}: (6, {}), {3}: (7, {}), {4}: (8, {})} | custom-call | tf_op jit(solution)/shard_map/attn_back_own/pallas_call | solution.py:65
  63.0 0.6 collective-permute-start.23
  63.5 0.8 attn_back_second.1
  65.2 0.6 collective-permute-start.27
  66.8 0.8 collective-permute-done.24.refs_0_
  68.2 1.6 %collective-permute-start.26 = (bf16[128,1024]{1,0:T(8,128)(2,1)S(1)}, bf16[128,1024]{1,0:T(8,128)(2,1)S(1)}, u32[]{:S(2)}, u32[]{:S(2)}) collective-permute-start(bf16[128,1024]{1,0:T(8,128)(2,1)S(1)} %back_sum_own.1.part), channel_id=1, source_target_pairs={{0,2},{1,3},{2,0},{3,1},{4,6},{5,7},{6,4},{7,5},{8,10},{9,11},{10,... | collective-permute-start | bytes 786440 | tf_op jit(solution)/shard_map/ppermute | solution.py:487
  69.8 4.5 %collective-permute-done.27.got = bf16[128,1024]{1,0:T(8,128)(2,1)S(1)} collective-permute-done((bf16[128,1024]{1,0:T(8,128)(2,1)S(1)}, bf16[128,1024]{1,0:T(8,128)(2,1)S(1)}, u32[]{:S(2)}, u32[]{:S(2)}) %collective-permute-start.27) | collective-permute-done | bytes 262176 | tf_op jit(solution)/shard_map/ppermute | solution.py:487
  74.7 0.5 collective-permute-start.29
  75.5 3.0 %collective-permute-start.37 = (bf16[96,1024]{1,0:T(8,128)(2,1)S(1)}, bf16[96,1024]{1,0:T(8,128)(2,1)S(1)}, u32[]{:S(2)}, u32[]{:S(2)}) collective-permute-start(bf16[96,1024]{1,0:T(8,128)(2,1)S(1)} %get-tuple-element.238), channel_id=1, source_target_pairs={{0,8},{4,12},{8,0},{12,4},{16,24},{20,28},{24,16},{28,20},{1,9},{5... | collective-permute-start | bytes 589832 | tf_op jit(solution)/shard_map/ppermute | solution.py:490
  78.5 1.0 enc_grads_first.1
  80.5 1.2 %collective-permute-done.32.refs_3_ = bf16[32,1024]{1,0:T(8,128)(2,1)S(1)} collective-permute-done((bf16[32,1024]{1,0:T(8,128)(2,1)S(1)}, bf16[32,1024]{1,0:T(8,128)(2,1)S(1)}, u32[]{:S(2)}, u32[]{:S(2)}) %collective-permute-start.32) | collective-permute-done | bytes 65568 | tf_op jit(solution)/shard_map/ppermute | solution.py:484
  81.6 1.3 %enc_grads_second.1 = (f32[4,128,256]{2,1,0:T(8,128)S(1)}, bf16[4,128,256]{2,1,0:T(8,128)(2,1)S(1)}, f32[4,128,256]{2,1,0:T(8,128)S(1)}, bf16[4,128,256]{2,1,0:T(8,128)(2,1)S(1)}) custom-call(bf16[128,1024]{1,0:T(8,128)(2,1)S(1)} %get-tuple-element.219.refs_0_, bf16[48,1024]{1,0:T(8,128)(2,1)S(1)} %collective-permute-done.30.refs_1_, ...), custom_call_target="tpu_custom_call" | custom-call | tf_op jit(solution)/shard_map/enc_grads_second/pallas_call | solution.py:65
  82.9 0.8 collective-permute-start.33
  83.8 1.3 %collective-permute-start.36 = (bf16[4,128,256]{2,1,0:T(8,128)(2,1)S(1)}, bf16[4,128,256]{2,1,0:T(8,128)(2,1)S(1)}, u32[]{:S(2)}, u32[]{:S(2)}) collective-permute-start(bf16[4,128,256]{2,1,0:T(8,128)(2,1)S(1)} %get-tuple-element.235), channel_id=1, source_target_pairs={{0,16},{4,20},{8,24},{12,28},{16,0},{20,4},{24,8},{28,12},{1,17},{... | collective-permute-start | bytes 786440 | tf_op jit(solution)/shard_map/ppermute | solution.py:490
  85.0 2.8 %collective-permute-done.37.refs_1_ = bf16[96,1024]{1,0:T(8,128)(2,1)S(1)} collective-permute-done((bf16[96,1024]{1,0:T(8,128)(2,1)S(1)}, bf16[96,1024]{1,0:T(8,128)(2,1)S(1)}, u32[]{:S(2)}, u32[]{:S(2)}) %collective-permute-start.37) | collective-permute-done | bytes 196640 | tf_op jit(solution)/shard_map/ppermute | solution.py:490
  87.9 0.6 collective-permute-start.38
  89.0 0.6 collective-permute-start.41
  89.6 2.6 %collective-permute-done.33.got = bf16[4,128,256]{2,1,0:T(8,128)(2,1)S(1)} collective-permute-done((bf16[4,128,256]{2,1,0:T(8,128)(2,1)S(1)}, bf16[4,128,256]{2,1,0:T(8,128)(2,1)S(1)}, u32[]{:S(2)}, u32[]{:S(2)}) %collective-permute-start.33) | collective-permute-done | bytes 262176 | tf_op jit(solution)/shard_map/ppermute | solution.py:490
  92.2 1.4 %collective-permute-start.34 = (bf16[2,128,256]{2,1,0:T(8,128)(2,1)S(1)}, bf16[2,128,256]{2,1,0:T(8,128)(2,1)S(1)}, u32[]{:S(2)}, u32[]{:S(2)}) collective-permute-start(bf16[2,128,256]{2,1,0:T(8,128)(2,1)S(1)} %get-tuple-element.230), channel_id=1, source_target_pairs={{0,4},{4,0},{8,12},{12,8},{16,20},{20,16},{24,28},{28,24},{1,5},{5... | collective-permute-start | bytes 393224 | tf_op jit(solution)/shard_map/ppermute | solution.py:490
  93.6 1.6 %collective-permute-done.38.refs_2_ = bf16[96,1024]{1,0:T(8,128)(2,1)S(1)} collective-permute-done((bf16[96,1024]{1,0:T(8,128)(2,1)S(1)}, bf16[96,1024]{1,0:T(8,128)(2,1)S(1)}, u32[]{:S(2)}, u32[]{:S(2)}) %collective-permute-start.38) | collective-permute-done | bytes 196640 | tf_op jit(solution)/shard_map/ppermute | solution.py:490
  95.2 1.8 %collective-permute-done.36.got = bf16[4,128,256]{2,1,0:T(8,128)(2,1)S(1)} collective-permute-done((bf16[4,128,256]{2,1,0:T(8,128)(2,1)S(1)}, bf16[4,128,256]{2,1,0:T(8,128)(2,1)S(1)}, u32[]{:S(2)}, u32[]{:S(2)}) %collective-permute-start.36) | collective-permute-done | bytes 262176 | tf_op jit(solution)/shard_map/ppermute | solution.py:490
  97.0 1.4 %collective-permute-start.39 = (bf16[2,128,256]{2,1,0:T(8,128)(2,1)S(1)}, bf16[2,128,256]{2,1,0:T(8,128)(2,1)S(1)}, u32[]{:S(2)}, u32[]{:S(2)}) collective-permute-start(bf16[2,128,256]{2,1,0:T(8,128)(2,1)S(1)} %get-tuple-element.241), channel_id=1, source_target_pairs={{0,4},{4,0},{8,12},{12,8},{16,20},{20,16},{24,28},{28,24},{1,5},{5... | collective-permute-start | bytes 393224 | tf_op jit(solution)/shard_map/ppermute | solution.py:490
  98.4 1.1 collective-permute-start.42
  99.5 2.2 %collective-permute-start.35 = (bf16[1,128,256]{2,1,0:T(8,128)(2,1)S(1)}, bf16[1,128,256]{2,1,0:T(8,128)(2,1)S(1)}, u32[]{:S(2)}, u32[]{:S(2)}) collective-permute-start(bf16[1,128,256]{2,1,0:T(8,128)(2,1)S(1)} %get-tuple-element.231), channel_id=1, source_target_pairs={{0,8},{4,12},{8,0},{12,4},{16,24},{20,28},{24,16},{28,20},{1,9},{5... | collective-permute-start | bytes 196616 | tf_op jit(solution)/shard_map/ppermute | solution.py:490
  101.8 1.0 collective-permute-done.39.got
  102.8 2.7 %collective-permute-start.40 = (bf16[1,128,256]{2,1,0:T(8,128)(2,1)S(1)}, bf16[1,128,256]{2,1,0:T(8,128)(2,1)S(1)}, u32[]{:S(2)}, u32[]{:S(2)}) collective-permute-start(bf16[1,128,256]{2,1,0:T(8,128)(2,1)S(1)} %get-tuple-element.242), channel_id=1, source_target_pairs={{0,8},{4,12},{8,0},{12,4},{16,24},{20,28},{24,16},{28,20},{1,9},{5... | collective-permute-start | bytes 196616 | tf_op jit(solution)/shard_map/ppermute | solution.py:490
  105.5 1.2 %ffn_out_own.1 = bf16[128,1024]{1,0:T(8,128)(2,1)} custom-call(bf16[128,1024]{1,0:T(8,128)(2,1)S(1)} %get-tuple-element.243.hidden, bf16[512,1024]{1,0:T(8,128)(2,1)S(1)} %copy-done.2, bf16[512,1024]{1,0:T(8,128)(2,1)S(1)} %collective-permute-done.1.out_b.w_b, bf16[128,1024]{1,0:T(8,128)(2,1)S(1)} %get-tuple-element.187.resid, ...), custom_call_target="tpu_custom_call" | custom-call | tf_op jit(solution)/shard_map/ffn_out_own/pallas_call | solution.py:65
  106.9 1.0 back_recv.1
  108.0 0.7 finish.1
  (75 shorter events, 8.4 us)
Async XLA Ops:
  0.6 7.9 %collective-permute-start = (bf16[2,1024,512]{2,1,0:T(8,128)(2,1)}, bf16[2,1024,512]{2,1,0:T(8,128)(2,1)S(1)}, u32[]{:S(2)}, u32[]{:S(2)}) collective-permute-start(bf16[2,1024,512]{2,1,0:T(8,128)(2,1)} %in_a.3), channel_id=1, source_target_pairs={{0,1},{1,0},{2,3},{3,2},{4,5},{5,4},{6,7},{7,6},{8,9},{9,8},{10,11... | collective-permute-start | bytes 6291464 | tf_op jit(solution)/shard_map/ppermute | solution.py:484
  1.1 7.4 %collective-permute-start.1 = (bf16[512,1024]{1,0:T(8,128)(2,1)}, bf16[512,1024]{1,0:T(8,128)(2,1)S(1)}, u32[]{:S(2)}, u32[]{:S(2)}) collective-permute-start(bf16[512,1024]{1,0:T(8,128)(2,1)} %w_a.3), channel_id=1, source_target_pairs={{0,1},{1,0},{2,3},{3,2},{4,5},{5,4},{6,7},{7,6},{8,9},{9,8},{10,11... | collective-permute-start | bytes 3145736 | tf_op jit(solution)/shard_map/ppermute | solution.py:484
  1.9 0.9 copy-start.7
  2.9 13.0 %copy-start.1 = (bf16[4,1024,256]{2,1,0:T(8,128)(2,1)S(1)}, bf16[4,1024,256]{2,1,0:T(8,128)(2,1)}, u32[]{:S(2)}) copy-start(bf16[4,1024,256]{2,1,0:T(8,128)(2,1)} %w_in.1) | copy-start | bytes 6291460
  2.9 13.0 %copy-start.4 = (bf16[256,1024]{1,0:T(8,128)(2,1)S(1)}, bf16[256,1024]{1,0:T(8,128)(2,1)}, u32[]{:S(2)}) copy-start(bf16[256,1024]{1,0:T(8,128)(2,1)} %w_own.3) | copy-start | bytes 1572868
  2.9 20.5 %copy-start = (bf16[2,1024,1024]{2,1,0:T(8,128)(2,1)S(1)}, bf16[2,1024,1024]{2,1,0:T(8,128)(2,1)}, u32[]{:S(2)}) copy-start(bf16[2,1024,1024]{2,1,0:T(8,128)(2,1)} %refs_8_.3) | copy-start | bytes 12582916
  3.2 11.7 %collective-permute-start.2 = (bf16[24,1152]{1,0:T(8,128)(2,1)S(1)}, bf16[24,1152]{1,0:T(8,128)(2,1)S(1)}, u32[]{:S(2)}, u32[]{:S(2)}) collective-permute-start(bf16[24,1152]{1,0:T(8,128)(2,1)S(1)} %get-tuple-element.130), channel_id=1, source_target_pairs={{0,8},{4,12},{8,0},{12,4},{16,24},{20,28},{24,16},{28,20},{1,9},{5... | collective-permute-start | bytes 165896 | tf_op jit(solution)/shard_map/ppermute | solution.py:490
  7.3 7.6 %collective-permute-start.3 = (bf16[24,1152]{1,0:T(8,128)(2,1)S(1)}, bf16[24,1152]{1,0:T(8,128)(2,1)S(1)}, u32[]{:S(2)}, u32[]{:S(2)}) collective-permute-start(bf16[24,1152]{1,0:T(8,128)(2,1)S(1)} %get-tuple-element.131), channel_id=1, source_target_pairs={{0,24},{4,28},{8,16},{12,20},{16,8},{20,12},{24,0},{28,4},{1,25},{... | collective-permute-start | bytes 165896 | tf_op jit(solution)/shard_map/ppermute | solution.py:490
  8.6 8.1 %collective-permute-start.4 = (bf16[24,1152]{1,0:T(8,128)(2,1)S(1)}, bf16[24,1152]{1,0:T(8,128)(2,1)S(1)}, u32[]{:S(2)}, u32[]{:S(2)}) collective-permute-start(bf16[24,1152]{1,0:T(8,128)(2,1)S(1)} %get-tuple-element.138), channel_id=1, source_target_pairs={{0,20},{4,16},{8,28},{12,24},{16,4},{20,0},{24,12},{28,8},{1,21},{... | collective-permute-start | bytes 165896 | tf_op jit(solution)/shard_map/ppermute | solution.py:490
  10.5 6.2 %collective-permute-start.5 = (bf16[24,1152]{1,0:T(8,128)(2,1)S(1)}, bf16[24,1152]{1,0:T(8,128)(2,1)S(1)}, u32[]{:S(2)}, u32[]{:S(2)}) collective-permute-start(bf16[24,1152]{1,0:T(8,128)(2,1)S(1)} %get-tuple-element.139), channel_id=1, source_target_pairs={{0,12},{4,8},{8,4},{12,0},{16,28},{20,24},{24,20},{28,16},{1,13},{... | collective-permute-start | bytes 165896 | tf_op jit(solution)/shard_map/ppermute | solution.py:490
  13.0 7.0 %collective-permute-start.6 = (bf16[24,1152]{1,0:T(8,128)(2,1)S(1)}, bf16[24,1152]{1,0:T(8,128)(2,1)S(1)}, u32[]{:S(2)}, u32[]{:S(2)}) collective-permute-start(bf16[24,1152]{1,0:T(8,128)(2,1)S(1)} %get-tuple-element.140), channel_id=1, source_target_pairs={{0,28},{4,24},{8,20},{12,16},{16,12},{20,8},{24,4},{28,0},{1,29},{... | collective-permute-start | bytes 165896 | tf_op jit(solution)/shard_map/ppermute | solution.py:490
  14.9 5.1 %collective-permute-start.7 = (bf16[24,1152]{1,0:T(8,128)(2,1)S(1)}, bf16[24,1152]{1,0:T(8,128)(2,1)S(1)}, u32[]{:S(2)}, u32[]{:S(2)}) collective-permute-start(bf16[24,1152]{1,0:T(8,128)(2,1)S(1)} %get-tuple-element.141), channel_id=1, source_target_pairs={{0,4},{4,0},{8,12},{12,8},{16,20},{20,16},{24,28},{28,24},{1,5},{5... | collective-permute-start | bytes 165896 | tf_op jit(solution)/shard_map/ppermute | solution.py:490
  14.9 5.1 %collective-permute-start.8 = (bf16[24,1152]{1,0:T(8,128)(2,1)S(1)}, bf16[24,1152]{1,0:T(8,128)(2,1)S(1)}, u32[]{:S(2)}, u32[]{:S(2)}) collective-permute-start(bf16[24,1152]{1,0:T(8,128)(2,1)S(1)} %get-tuple-element.142), channel_id=1, source_target_pairs={{0,16},{4,20},{8,24},{12,28},{16,0},{20,4},{24,8},{28,12},{1,17},{... | collective-permute-start | bytes 165896 | tf_op jit(solution)/shard_map/ppermute | solution.py:490
  20.2 6.7 %collective-permute-start.9 = (bf16[128,1024]{1,0:T(8,128)(2,1)S(1)}, bf16[128,1024]{1,0:T(8,128)(2,1)S(1)}, u32[]{:S(2)}, u32[]{:S(2)}) collective-permute-start(bf16[128,1024]{1,0:T(8,128)(2,1)S(1)} %get-tuple-element.151.refs_0_.refs_3_), channel_id=1, source_target_pairs={{0,2},{1,3},{2,0},{3,1},{4,6},{5,7},{6,4},{7,5},{8,10},{9,11},{10,... | collective-permute-start | bytes 786440 | tf_op jit(solution)/shard_map/ppermute | solution.py:487
  21.8 1.3 %collective-permute-start.10 = (bf16[64,1024]{1,0:T(8,128)(2,1)S(1)}, bf16[64,1024]{1,0:T(8,128)(2,1)S(1)}, u32[]{:S(2)}, u32[]{:S(2)}) collective-permute-start(bf16[64,1024]{1,0:T(8,128)(2,1)S(1)} %get-tuple-element.152), channel_id=1, source_target_pairs={{0,1},{1,0},{2,3},{3,2},{4,5},{5,4},{6,7},{7,6},{8,9},{9,8},{10,11... | collective-permute-start | bytes 393224 | tf_op jit(solution)/shard_map/ppermute | solution.py:484
  21.8 5.6 %copy-start.5 = (bf16[1,128,1024]{2,1,0:T(8,128)(2,1)S(1)}, bf16[1,128,1024]{2,1,0:T(8,128)(2,1)}, u32[]{:S(2)}) copy-start(bf16[1,128,1024]{2,1,0:T(8,128)(2,1)} %param.19) | copy-start | bytes 786436
  21.8 1.5 %collective-permute-start.11 = (bf16[64,1024]{1,0:T(8,128)(2,1)S(1)}, bf16[64,1024]{1,0:T(8,128)(2,1)S(1)}, u32[]{:S(2)}, u32[]{:S(2)}) collective-permute-start(bf16[64,1024]{1,0:T(8,128)(2,1)S(1)} %get-tuple-element.153), channel_id=1, source_target_pairs={{0,1},{1,0},{2,3},{3,2},{4,5},{5,4},{6,7},{7,6},{8,9},{9,8},{10,11... | collective-permute-start | bytes 393224 | tf_op jit(solution)/shard_map/ppermute | solution.py:484
  26.9 3.4 %copy-start.6 = (s32[1,512]{1,0:T(1,128)S(1)}, s32[1,512]{1,0:T(1,128)}, u32[]{:S(2)}) copy-start(s32[1,512]{1,0:T(1,128)} %param.13) | copy-start | bytes 6148
  26.9 7.0 %collective-permute-start.14 = (bf16[256,1024]{1,0:T(8,128)(2,1)S(1)}, bf16[256,1024]{1,0:T(8,128)(2,1)S(1)}, u32[]{:S(2)}, u32[]{:S(2)}) collective-permute-start(bf16[256,1024]{1,0:T(8,128)(2,1)S(1)} %copy-done.4), channel_id=1, source_target_pairs={{0,1},{1,0},{2,3},{3,2},{4,5},{5,4},{6,7},{7,6},{8,9},{9,8},{10,11... | collective-permute-start | bytes 1572872 | tf_op jit(solution)/shard_map/ppermute | solution.py:484
  26.9 3.4 %collective-permute-start.12 = (bf16[128,1024]{1,0:T(8,128)(2,1)S(1)}, bf16[128,1024]{1,0:T(8,128)(2,1)S(1)}, u32[]{:S(2)}, u32[]{:S(2)}) collective-permute-start(bf16[128,1024]{1,0:T(8,128)(2,1)S(1)} %collective-permute-done.9.refs_0_.refs_4_), channel_id=1, source_target_pairs={{0,1},{1,0},{2,3},{3,2},{4,5},{5,4},{6,7},{7,6},{8,9},{9,8},{10,11... | collective-permute-start | bytes 786440 | tf_op jit(solution)/shard_map/ppermute | solution.py:484
  27.4 8.2 %collective-permute-start.15 = (bf16[128,1024]{1,0:T(8,128)(2,1)S(1)}, bf16[128,1024]{1,0:T(8,128)(2,1)S(1)}, u32[]{:S(2)}, u32[]{:S(2)}) collective-permute-start(bf16[128,1024]{1,0:T(8,128)(2,1)S(1)} %bitcast.5), channel_id=1, source_target_pairs={{0,2},{1,3},{2,0},{3,1},{4,6},{5,7},{6,4},{7,5},{8,10},{9,11},{10,... | collective-permute-start | bytes 786440 | tf_op jit(solution)/shard_map/ppermute | solution.py:487
  32.5 1.4 %collective-permute-start.13 = (bf16[256,256]{1,0:T(8,128)(2,1)S(1)}, bf16[256,256]{1,0:T(8,128)(2,1)S(1)}, u32[]{:S(2)}, u32[]{:S(2)}) collective-permute-start(bf16[256,256]{1,0:T(8,128)(2,1)S(1)} %get-tuple-element.164), channel_id=1, source_target_pairs={{0,1},{1,0},{2,3},{3,2},{4,5},{5,4},{6,7},{7,6},{8,9},{9,8},{10,11... | collective-permute-start | bytes 393224 | tf_op jit(solution)/shard_map/ppermute | solution.py:484
  33.3 10.4 %copy-start.2 = (bf16[512,1024]{1,0:T(8,128)(2,1)S(1)}, bf16[512,1024]{1,0:T(8,128)(2,1)}, u32[]{:S(2)}) copy-start(bf16[512,1024]{1,0:T(8,128)(2,1)} %w_a.3) | copy-start | bytes 3145732
  33.3 10.4 %copy-start.3 = (bf16[2,1024,512]{2,1,0:T(8,128)(2,1)S(1)}, bf16[2,1024,512]{2,1,0:T(8,128)(2,1)}, u32[]{:S(2)}) copy-start(bf16[2,1024,512]{2,1,0:T(8,128)(2,1)} %in_a.3) | copy-start | bytes 6291460
  34.3 9.2 %collective-permute-start.17 = (bf16[128,1024]{1,0:T(8,128)(2,1)S(1)}, bf16[128,1024]{1,0:T(8,128)(2,1)S(1)}, u32[]{:S(2)}, u32[]{:S(2)}) collective-permute-start(bf16[128,1024]{1,0:T(8,128)(2,1)S(1)} %attn_out_far.1.part), channel_id=1, source_target_pairs={{0,2},{1,3},{2,0},{3,1},{4,6},{5,7},{6,4},{7,5},{8,10},{9,11},{10,... | collective-permute-start | bytes 786440 | tf_op jit(solution)/shard_map/ppermute | solution.py:487
  35.7 12.6 %collective-permute-start.16 = (bf16[128,1024]{1,0:T(8,128)(2,1)S(1)}, bf16[128,1024]{1,0:T(8,128)(2,1)S(1)}, u32[]{:S(2)}, u32[]{:S(2)}) collective-permute-start(bf16[128,1024]{1,0:T(8,128)(2,1)S(1)} %attn_out_own.1.part), channel_id=1, source_target_pairs={{0,2},{1,3},{2,0},{3,1},{4,6},{5,7},{6,4},{7,5},{8,10},{9,11},{10,... | collective-permute-start | bytes 786440 | tf_op jit(solution)/shard_map/ppermute | solution.py:487
  48.3 9.2 %collective-permute-start.19 = (bf16[128,1024]{1,0:T(8,128)(2,1)S(1)}, bf16[128,1024]{1,0:T(8,128)(2,1)S(1)}, u32[]{:S(2)}, u32[]{:S(2)}) collective-permute-start(bf16[128,1024]{1,0:T(8,128)(2,1)S(1)} %get-tuple-element.173.back), channel_id=1, source_target_pairs={{0,2},{1,3},{2,0},{3,1},{4,6},{5,7},{6,4},{7,5},{8,10},{9,11},{10,... | collective-permute-start | bytes 786440 | tf_op jit(solution)/shard_map/ppermute | solution.py:487
  51.9 9.6 %collective-permute-start.18 = (bf16[128,1024]{1,0:T(8,128)(2,1)S(1)}, bf16[128,1024]{1,0:T(8,128)(2,1)S(1)}, u32[]{:S(2)}, u32[]{:S(2)}) collective-permute-start(bf16[128,1024]{1,0:T(8,128)(2,1)S(1)} %get-tuple-element.178.back), channel_id=1, source_target_pairs={{0,2},{1,3},{2,0},{3,1},{4,6},{5,7},{6,4},{7,5},{8,10},{9,11},{10,... | collective-permute-start | bytes 786440 | tf_op jit(solution)/shard_map/ppermute | solution.py:487
  57.8 1.4 %collective-permute-start.20 = (bf16[64,1024]{1,0:T(8,128)(2,1)S(1)}, bf16[64,1024]{1,0:T(8,128)(2,1)S(1)}, u32[]{:S(2)}, u32[]{:S(2)}) collective-permute-start(bf16[64,1024]{1,0:T(8,128)(2,1)S(1)} %get-tuple-element.181), channel_id=1, source_target_pairs={{0,1},{1,0},{2,3},{3,2},{4,5},{5,4},{6,7},{7,6},{8,9},{9,8},{10,11... | collective-permute-start | bytes 393224 | tf_op jit(solution)/shard_map/ppermute | solution.py:484
  57.9 1.5 %collective-permute-start.21 = (bf16[64,1024]{1,0:T(8,128)(2,1)S(1)}, bf16[64,1024]{1,0:T(8,128)(2,1)S(1)}, u32[]{:S(2)}, u32[]{:S(2)}) collective-permute-start(bf16[64,1024]{1,0:T(8,128)(2,1)S(1)} %get-tuple-element.182), channel_id=1, source_target_pairs={{0,1},{1,0},{2,3},{3,2},{4,5},{5,4},{6,7},{7,6},{8,9},{9,8},{10,11... | collective-permute-start | bytes 393224 | tf_op jit(solution)/shard_map/ppermute | solution.py:484
  61.7 1.8 %collective-permute-start.22 = (bf16[128,1024]{1,0:T(8,128)(2,1)S(1)}, bf16[128,1024]{1,0:T(8,128)(2,1)S(1)}, u32[]{:S(2)}, u32[]{:S(2)}) collective-permute-start(bf16[128,1024]{1,0:T(8,128)(2,1)S(1)} %resid_back.1.first.d_resid), channel_id=1, source_target_pairs={{0,1},{1,0},{2,3},{3,2},{4,5},{5,4},{6,7},{7,6},{8,9},{9,8},{10,11... | collective-permute-start | bytes 786440 | tf_op jit(solution)/shard_map/ppermute | solution.py:484
  63.0 1.7 %collective-permute-start.23 = (bf16[128,1024]{1,0:T(8,128)(2,1)S(1)}, bf16[128,1024]{1,0:T(8,128)(2,1)S(1)}, u32[]{:S(2)}, u32[]{:S(2)}) collective-permute-start(bf16[128,1024]{1,0:T(8,128)(2,1)S(1)} %get-tuple-element.201), channel_id=1, source_target_pairs={{0,1},{1,0},{2,3},{3,2},{4,5},{5,4},{6,7},{7,6},{8,9},{9,8},{10,11... | collective-permute-start | bytes 786440 | tf_op jit(solution)/shard_map/ppermute | solution.py:484
  65.2 9.2 %collective-permute-start.27 = (bf16[128,1024]{1,0:T(8,128)(2,1)S(1)}, bf16[128,1024]{1,0:T(8,128)(2,1)S(1)}, u32[]{:S(2)}, u32[]{:S(2)}) collective-permute-start(bf16[128,1024]{1,0:T(8,128)(2,1)S(1)} %back_sum_far.1.part), channel_id=1, source_target_pairs={{0,2},{1,3},{2,0},{3,1},{4,6},{5,7},{6,4},{7,5},{8,10},{9,11},{10,... | collective-permute-start | bytes 786440 | tf_op jit(solution)/shard_map/ppermute | solution.py:487
  66.2 1.4 %collective-permute-start.24 = (bf16[64,1024]{1,0:T(8,128)(2,1)S(1)}, bf16[64,1024]{1,0:T(8,128)(2,1)S(1)}, u32[]{:S(2)}, u32[]{:S(2)}) collective-permute-start(bf16[64,1024]{1,0:T(8,128)(2,1)S(1)} %get-tuple-element.207), channel_id=1, source_target_pairs={{0,1},{1,0},{2,3},{3,2},{4,5},{5,4},{6,7},{7,6},{8,9},{9,8},{10,11... | collective-permute-start | bytes 393224 | tf_op jit(solution)/shard_map/ppermute | solution.py:484
  66.3 1.5 %collective-permute-start.25 = (bf16[64,1024]{1,0:T(8,128)(2,1)S(1)}, bf16[64,1024]{1,0:T(8,128)(2,1)S(1)}, u32[]{:S(2)}, u32[]{:S(2)}) collective-permute-start(bf16[64,1024]{1,0:T(8,128)(2,1)S(1)} %get-tuple-element.208), channel_id=1, source_target_pairs={{0,1},{1,0},{2,3},{3,2},{4,5},{5,4},{6,7},{7,6},{8,9},{9,8},{10,11... | collective-permute-start | bytes 393224 | tf_op jit(solution)/shard_map/ppermute | solution.py:484
  68.2 11.3 %collective-permute-start.26 = (bf16[128,1024]{1,0:T(8,128)(2,1)S(1)}, bf16[128,1024]{1,0:T(8,128)(2,1)S(1)}, u32[]{:S(2)}, u32[]{:S(2)}) collective-permute-start(bf16[128,1024]{1,0:T(8,128)(2,1)S(1)} %back_sum_own.1.part), channel_id=1, source_target_pairs={{0,2},{1,3},{2,0},{3,1},{4,6},{5,7},{6,4},{7,5},{8,10},{9,11},{10,... | collective-permute-start | bytes 786440 | tf_op jit(solution)/shard_map/ppermute | solution.py:487
  74.6 3.9 %collective-permute-start.28 = (bf16[64,1024]{1,0:T(8,128)(2,1)S(1)}, bf16[64,1024]{1,0:T(8,128)(2,1)S(1)}, u32[]{:S(2)}, u32[]{:S(2)}) collective-permute-start(bf16[64,1024]{1,0:T(8,128)(2,1)S(1)} %get-tuple-element.210), channel_id=1, source_target_pairs={{0,1},{1,0},{2,3},{3,2},{4,5},{5,4},{6,7},{7,6},{8,9},{9,8},{10,11... | collective-permute-start | bytes 393224 | tf_op jit(solution)/shard_map/ppermute | solution.py:484
  74.7 3.8 %collective-permute-start.29 = (bf16[64,1024]{1,0:T(8,128)(2,1)S(1)}, bf16[64,1024]{1,0:T(8,128)(2,1)S(1)}, u32[]{:S(2)}, u32[]{:S(2)}) collective-permute-start(bf16[64,1024]{1,0:T(8,128)(2,1)S(1)} %get-tuple-element.211), channel_id=1, source_target_pairs={{0,1},{1,0},{2,3},{3,2},{4,5},{5,4},{6,7},{7,6},{8,9},{9,8},{10,11... | collective-permute-start | bytes 393224 | tf_op jit(solution)/shard_map/ppermute | solution.py:484
  75.5 12.4 %collective-permute-start.37 = (bf16[96,1024]{1,0:T(8,128)(2,1)S(1)}, bf16[96,1024]{1,0:T(8,128)(2,1)S(1)}, u32[]{:S(2)}, u32[]{:S(2)}) collective-permute-start(bf16[96,1024]{1,0:T(8,128)(2,1)S(1)} %get-tuple-element.238), channel_id=1, source_target_pairs={{0,8},{4,12},{8,0},{12,4},{16,24},{20,28},{24,16},{28,20},{1,9},{5... | collective-permute-start | bytes 589832 | tf_op jit(solution)/shard_map/ppermute | solution.py:490
  79.8 1.8 %collective-permute-start.30 = (bf16[48,1024]{1,0:T(8,128)(2,1)S(1)}, bf16[48,1024]{1,0:T(8,128)(2,1)S(1)}, u32[]{:S(2)}, u32[]{:S(2)}) collective-permute-start(bf16[48,1024]{1,0:T(8,128)(2,1)S(1)} %get-tuple-element.220), channel_id=1, source_target_pairs={{0,1},{1,0},{2,3},{3,2},{4,5},{5,4},{6,7},{7,6},{8,9},{9,8},{10,11... | collective-permute-start | bytes 294920 | tf_op jit(solution)/shard_map/ppermute | solution.py:484
  79.9 1.8 %collective-permute-start.31 = (bf16[48,1024]{1,0:T(8,128)(2,1)S(1)}, bf16[48,1024]{1,0:T(8,128)(2,1)S(1)}, u32[]{:S(2)}, u32[]{:S(2)}) collective-permute-start(bf16[48,1024]{1,0:T(8,128)(2,1)S(1)} %get-tuple-element.221), channel_id=1, source_target_pairs={{0,1},{1,0},{2,3},{3,2},{4,5},{5,4},{6,7},{7,6},{8,9},{9,8},{10,11... | collective-permute-start | bytes 294920 | tf_op jit(solution)/shard_map/ppermute | solution.py:484
  80.4 1.3 %collective-permute-start.32 = (bf16[32,1024]{1,0:T(8,128)(2,1)S(1)}, bf16[32,1024]{1,0:T(8,128)(2,1)S(1)}, u32[]{:S(2)}, u32[]{:S(2)}) collective-permute-start(bf16[32,1024]{1,0:T(8,128)(2,1)S(1)} %get-tuple-element.222), channel_id=1, source_target_pairs={{0,1},{1,0},{2,3},{3,2},{4,5},{5,4},{6,7},{7,6},{8,9},{9,8},{10,11... | collective-permute-start | bytes 196616 | tf_op jit(solution)/shard_map/ppermute | solution.py:484
  82.9 9.2 %collective-permute-start.33 = (bf16[4,128,256]{2,1,0:T(8,128)(2,1)S(1)}, bf16[4,128,256]{2,1,0:T(8,128)(2,1)S(1)}, u32[]{:S(2)}, u32[]{:S(2)}) collective-permute-start(bf16[4,128,256]{2,1,0:T(8,128)(2,1)S(1)} %get-tuple-element.228), channel_id=1, source_target_pairs={{0,16},{4,20},{8,24},{12,28},{16,0},{20,4},{24,8},{28,12},{1,17},{... | collective-permute-start | bytes 786440 | tf_op jit(solution)/shard_map/ppermute | solution.py:490
  83.8 13.2 %collective-permute-start.36 = (bf16[4,128,256]{2,1,0:T(8,128)(2,1)S(1)}, bf16[4,128,256]{2,1,0:T(8,128)(2,1)S(1)}, u32[]{:S(2)}, u32[]{:S(2)}) collective-permute-start(bf16[4,128,256]{2,1,0:T(8,128)(2,1)S(1)} %get-tuple-element.235), channel_id=1, source_target_pairs={{0,16},{4,20},{8,24},{12,28},{16,0},{20,4},{24,8},{28,12},{1,17},{... | collective-permute-start | bytes 786440 | tf_op jit(solution)/shard_map/ppermute | solution.py:490
  87.9 7.3 %collective-permute-start.38 = (bf16[96,1024]{1,0:T(8,128)(2,1)S(1)}, bf16[96,1024]{1,0:T(8,128)(2,1)S(1)}, u32[]{:S(2)}, u32[]{:S(2)}) collective-permute-start(bf16[96,1024]{1,0:T(8,128)(2,1)S(1)} %back_pick.2), channel_id=1, source_target_pairs={{0,4},{4,0},{8,12},{12,8},{16,20},{20,16},{24,28},{28,24},{1,5},{5... | collective-permute-start | bytes 589832 | tf_op jit(solution)/shard_map/ppermute | solution.py:490
  89.0 16.5 %collective-permute-start.41 = (bf16[128,1024]{1,0:T(8,128)(2,1)S(1)}, bf16[128,1024]{1,0:T(8,128)(2,1)S(1)}, u32[]{:S(2)}, u32[]{:S(2)}) collective-permute-start(bf16[128,1024]{1,0:T(8,128)(2,1)S(1)} %ffn_out_far.1), channel_id=1, source_target_pairs={{0,2},{1,3},{2,0},{3,1},{4,6},{5,7},{6,4},{7,5},{8,10},{9,11},{10,... | collective-permute-start | bytes 786440 | tf_op jit(solution)/shard_map/ppermute | solution.py:487
  92.2 7.3 %collective-permute-start.34 = (bf16[2,128,256]{2,1,0:T(8,128)(2,1)S(1)}, bf16[2,128,256]{2,1,0:T(8,128)(2,1)S(1)}, u32[]{:S(2)}, u32[]{:S(2)}) collective-permute-start(bf16[2,128,256]{2,1,0:T(8,128)(2,1)S(1)} %get-tuple-element.230), channel_id=1, source_target_pairs={{0,4},{4,0},{8,12},{12,8},{16,20},{20,16},{24,28},{28,24},{1,5},{5... | collective-permute-start | bytes 393224 | tf_op jit(solution)/shard_map/ppermute | solution.py:490
  97.0 5.7 %collective-permute-start.39 = (bf16[2,128,256]{2,1,0:T(8,128)(2,1)S(1)}, bf16[2,128,256]{2,1,0:T(8,128)(2,1)S(1)}, u32[]{:S(2)}, u32[]{:S(2)}) collective-permute-start(bf16[2,128,256]{2,1,0:T(8,128)(2,1)S(1)} %get-tuple-element.241), channel_id=1, source_target_pairs={{0,4},{4,0},{8,12},{12,8},{16,20},{20,16},{24,28},{28,24},{1,5},{5... | collective-permute-start | bytes 393224 | tf_op jit(solution)/shard_map/ppermute | solution.py:490
  98.4 8.4 %collective-permute-start.42 = (bf16[96,1024]{1,0:T(8,128)(2,1)S(1)}, bf16[96,1024]{1,0:T(8,128)(2,1)S(1)}, u32[]{:S(2)}, u32[]{:S(2)}) collective-permute-start(bf16[96,1024]{1,0:T(8,128)(2,1)S(1)} %back_pick.3), channel_id=1, source_target_pairs={{0,16},{4,20},{8,24},{12,28},{16,0},{20,4},{24,8},{28,12},{1,17},{... | collective-permute-start | bytes 589832 | tf_op jit(solution)/shard_map/ppermute | solution.py:490
  99.5 7.3 %collective-permute-start.35 = (bf16[1,128,256]{2,1,0:T(8,128)(2,1)S(1)}, bf16[1,128,256]{2,1,0:T(8,128)(2,1)S(1)}, u32[]{:S(2)}, u32[]{:S(2)}) collective-permute-start(bf16[1,128,256]{2,1,0:T(8,128)(2,1)S(1)} %get-tuple-element.231), channel_id=1, source_target_pairs={{0,8},{4,12},{8,0},{12,4},{16,24},{20,28},{24,16},{28,20},{1,9},{5... | collective-permute-start | bytes 196616 | tf_op jit(solution)/shard_map/ppermute | solution.py:490
  102.8 5.2 %collective-permute-start.40 = (bf16[1,128,256]{2,1,0:T(8,128)(2,1)S(1)}, bf16[1,128,256]{2,1,0:T(8,128)(2,1)S(1)}, u32[]{:S(2)}, u32[]{:S(2)}) collective-permute-start(bf16[1,128,256]{2,1,0:T(8,128)(2,1)S(1)} %get-tuple-element.242), channel_id=1, source_target_pairs={{0,8},{4,12},{8,0},{12,4},{16,24},{20,28},{24,16},{28,20},{1,9},{5... | collective-permute-start | bytes 196616 | tf_op jit(solution)/shard_map/ppermute | solution.py:490
